TPU v7x, 32 devices: a whole 2x2x4 slice. The times are simulated.
32 devices in a mesh: seq: 8 (over z, y), head: 4 (over x, core).
Axes of the slice: x: 2, y: 2, z: 4, core: 2. Of those that a mesh axis runs over, the one named last changes fastest.
Arguments:
- tokens: bfloat16 [8192, 2048], P('seq', 'head'), may hold values from -20 to 20
- w_query: bfloat16 [2048, 2048], P(None, 'head'), may hold values from -1 to 1
- w_key: bfloat16 [2048, 2048], P(None, 'head'), may hold values from -1 to 1
- w_value: bfloat16 [2048, 2048], P(None, 'head'), may hold values from -0.125 to 0.125
- w_out: bfloat16 [2048, 2048], P('head'), may hold values from -0.125 to 0.125
Outputs:
- attended: bfloat16 [8192, 2048], P(('seq', 'head'))
All inputs are finite; a program needn't handle non-finite values.
Results may differ from a plain program's by a relative error of at most 0.04.
Values may be sent and summed in bfloat16 or wider, within the bound.
No kernel may reach another device: no remote copies, remote signals or barrier semaphores. Data moves between devices by JAX's collectives and lax.ppermute only.
A program may use at most 128 MiB of HBM per device.

v0:
```python
import jax
import jax.numpy as jnp
from jax import lax
from jax.sharding import PartitionSpec as P

DH = 128
STRIDE = 256


def from_behind(value, axis, by):
    peers = lax.axis_size(axis)
    pairs = [(i, i + by) for i in range(peers) if 0 <= i + by < peers]
    return lax.ppermute(value, axis, pairs)


def shards(tokens, w_query, w_key, w_value, w_out):
    tok_rows = tokens.shape[0]
    head_width = w_query.shape[1]
    head_count = head_width // DH
    score_scale = DH ** (-0.5)
    shard_piece = lax.all_gather(tokens, "head", axis=1, tiled=True)
    query_full, key_full, value_full = tuple(
        (
            jnp.dot(shard_piece, weight, preferred_element_type=jnp.float32)
            for weight in (w_query, w_key, w_value)
        )
    )
    query = query_full.astype(jnp.bfloat16).reshape(tok_rows, head_count, DH)
    key_heads = key_full.astype(jnp.bfloat16).reshape(tok_rows, head_count, DH)
    value_heads = value_full.astype(jnp.bfloat16).reshape(tok_rows, head_count, DH)
    prev_keys, prev_values = from_behind((key_heads[-STRIDE:], value_heads[-STRIDE:]), "seq", 1)
    blocks = tok_rows // STRIDE
    extended_keys = jnp.concatenate([prev_keys, key_heads], 0)
    extended_values = jnp.concatenate([prev_values, value_heads], 0)
    window_keys = jnp.concatenate(
        [
            extended_keys[:tok_rows].reshape(blocks, STRIDE, head_count, DH),
            extended_keys[STRIDE:].reshape(blocks, STRIDE, head_count, DH),
        ],
        1,
    )
    window_values = jnp.concatenate(
        [
            extended_values[:tok_rows].reshape(blocks, STRIDE, head_count, DH),
            extended_values[STRIDE:].reshape(blocks, STRIDE, head_count, DH),
        ],
        1,
    )
    query_blocks = query.reshape(blocks, STRIDE, head_count, DH)
    scores = (
        jnp.einsum("bthd,buhd->bhtu", query_blocks, window_keys, preferred_element_type=jnp.float32)
        * score_scale
    )
    first_position = lax.axis_index("seq") * tok_rows
    block_index = jnp.arange(blocks)[:, None, None, None]
    query_index = jnp.arange(STRIDE)[None, None, :, None]
    key_index = jnp.arange(2 * STRIDE)[None, None, None, :]
    allowed = (
        (key_index > query_index)
        & (key_index <= query_index + STRIDE)
        & (first_position + block_index * STRIDE + key_index - STRIDE >= 0)
    )
    local_top = jnp.max(jnp.where(allowed, scores, -1e30), axis=-1)
    local_weights = jnp.where(allowed, jnp.exp(scores - local_top[..., None]), 0.0)
    local_total = jnp.sum(local_weights, axis=-1)
    local_out = jnp.einsum(
        "bhtu,buhd->bthd",
        local_weights.astype(jnp.bfloat16),
        window_values,
        preferred_element_type=jnp.float32,
    )
    local_out = local_out.reshape(tok_rows, head_count, DH)
    local_top = local_top.transpose(0, 2, 1).reshape(tok_rows, head_count)
    local_total = local_total.transpose(0, 2, 1).reshape(tok_rows, head_count)
    row_count = tok_rows // STRIDE
    query_class = lax.all_to_all(
        query.reshape(row_count, STRIDE, head_count, DH),
        "seq",
        split_axis=1,
        concat_axis=0,
        tiled=True,
    )
    key_class = lax.all_to_all(
        key_heads.reshape(row_count, STRIDE, head_count, DH),
        "seq",
        split_axis=1,
        concat_axis=0,
        tiled=True,
    )
    value_class = lax.all_to_all(
        value_heads.reshape(row_count, STRIDE, head_count, DH),
        "seq",
        split_axis=1,
        concat_axis=0,
        tiled=True,
    )
    row_total = query_class.shape[0]
    class_scores = (
        jnp.einsum("rchd,schd->chrs", query_class, key_class, preferred_element_type=jnp.float32)
        * score_scale
    )
    earlier = (
        jnp.arange(row_total)[None, None, :, None] > jnp.arange(row_total)[None, None, None, :]
    )
    class_top = jnp.max(jnp.where(earlier, class_scores, -1e30), axis=-1)
    class_weights = jnp.where(earlier, jnp.exp(class_scores - class_top[..., None]), 0.0)
    class_total = jnp.sum(class_weights, axis=-1)
    summed = jnp.einsum(
        "chrs,schd->rchd",
        class_weights.astype(jnp.bfloat16),
        value_class,
        preferred_element_type=jnp.float32,
    )
    floor_total = jnp.maximum(class_total, 1.0).transpose(2, 0, 1)
    class_out = (summed / floor_total[..., None]).astype(jnp.bfloat16)
    class_top_rows = class_top.transpose(2, 0, 1)
    class_total_rows = class_total.transpose(2, 0, 1)
    column_out = class_out
    column_top = class_top_rows
    column_total = class_total_rows
    column_out, column_top, column_total = (
        lax.all_to_all(column_out, "seq", split_axis=0, concat_axis=1, tiled=True),
        lax.all_to_all(
            column_top.astype(jnp.bfloat16), "seq", split_axis=0, concat_axis=1, tiled=True
        ).astype(column_top.dtype),
        lax.all_to_all(
            column_total.astype(jnp.bfloat16), "seq", split_axis=0, concat_axis=1, tiled=True
        ).astype(column_total.dtype),
    )
    column_out = column_out.reshape(tok_rows, head_count, DH)
    column_top = column_top.reshape(tok_rows, head_count)
    column_total = column_total.reshape(tok_rows, head_count)
    top_score = jnp.maximum(local_top, column_top)
    local_weight = jnp.exp(local_top - top_score)
    column_weight = column_total * jnp.exp(column_top - top_score)
    denominator = local_total * local_weight + column_weight
    mixed = (
        local_out * local_weight[..., None]
        + column_out.astype(jnp.float32) * column_weight[..., None]
    ) / denominator[..., None]
    mixed = mixed.astype(jnp.bfloat16).reshape(tok_rows, head_width)
    return lax.psum_scatter(
        jnp.dot(mixed, w_out, preferred_element_type=jnp.float32).astype(jnp.bfloat16),
        "head",
        scatter_dimension=0,
        tiled=True,
    )


def solution(mesh):
    in_specs = (
        P("seq", "head"),
        P(None, "head"),
        P(None, "head"),
        P(None, "head"),
        P("head", None),
    )
    out_specs = P(("seq", "head"), None)
    return jax.shard_map(shards, mesh=mesh, in_specs=in_specs, out_specs=out_specs, check_vma=False)
```

profile of v0, /device:TPU:0, one launch (start us, length us, event | category | flops | bytes accessed | tf_op | source)
XLA Modules:
  0.0 262.5 jit_solution(13467066051989401508)
XLA Ops:
  7.3 38.9 %all-gather.2.cloned.1.call-done = bf16[1024,2048]{1,0:T(8,128)(2,1)} async-done(((bf16[1024,512]{1,0:T(8,128)(2,1)}), bf16[1024,2048]{1,0:T(8,128)(2,1)}) %all-gather.2.cloned.1.call-update) | async-done | bytes 4194320 | tf_op jit(solution)/shard_map/all_gather | solution.py:21
  46.1 6.2 %convolution_convert_fusion.1 = bf16[1024,512]{0,1:T(8,128)(2,1)} fusion(bf16[1024,2048]{1,0:T(8,128)(2,1)} %all-gather.2.cloned.1.call-done, bf16[2048,512]{1,0:T(8,128)(2,1)} %param.7), kind=kOutput, calls=%fused_computation.29 | convolution fusion | flops 2148007936 | bytes 7340032 | tf_op jit(solution)/shard_map/dot_general | solution.py:24
  56.4 5.5 %all-to-all-start.1 = ((bf16[4,256,4,128]{3,2,0,1:T(4,128)(2,1)}), bf16[4,256,4,128]{3,2,0,1:T(4,128)(2,1)}, u32[]{:S(2)}, u32[]{:S(2)}) async-start(bf16[4,256,4,128]{3,2,0,1:T(4,128)(2,1)} %copy.49), calls=%async_computation.1 | async-start | bytes 2097152 | tf_op jit(solution)/shard_map/all_to_all | solution.py:83
  61.9 6.2 %convolution_convert_fusion.2 = bf16[1024,512]{1,0:T(8,128)(2,1)} fusion(bf16[1024,2048]{1,0:T(8,128)(2,1)} %all-gather.2.cloned.1.call-done, bf16[2048,512]{1,0:T(8,128)(2,1)} %param.6), kind=kOutput, calls=%fused_computation.30 | convolution fusion | flops 2148007936 | bytes 7340032 | tf_op jit(solution)/shard_map/dot_general | solution.py:24
  72.8 15.4 %all-to-all-done.1 = bf16[4,256,4,128]{3,2,0,1:T(4,128)(2,1)} async-done(((bf16[4,256,4,128]{3,2,0,1:T(4,128)(2,1)}), bf16[4,256,4,128]{3,2,0,1:T(4,128)(2,1)}, u32[]{:S(2)}, u32[]{:S(2)}) %all-to-all-start.1) | async-done | bytes 1048608 | tf_op jit(solution)/shard_map/all_to_all | solution.py:83
  88.2 4.2 %all-to-all-start = ((bf16[4,256,4,128]{3,2,0,1:T(4,128)(2,1)}), bf16[4,256,4,128]{3,2,0,1:T(4,128)(2,1)}, u32[]{:S(2)}, u32[]{:S(2)}) async-start(bf16[4,256,4,128]{3,2,0,1:T(4,128)(2,1)} %copy.47), calls=%async_computation | async-start | bytes 2097152 | tf_op jit(solution)/shard_map/all_to_all | solution.py:76
  92.7 5.2 %convolution_convert_fusion.3 = bf16[1024,512]{0,1:T(8,128)(2,1)S(1)} fusion(bf16[1024,2048]{1,0:T(8,128)(2,1)} %all-gather.2.cloned.1.call-done, bf16[2048,512]{1,0:T(8,128)(2,1)} %param.8), kind=kOutput, calls=%fused_computation.31 | convolution fusion | flops 2148007936 | bytes 7340032 | tf_op jit(solution)/shard_map/dot_general | solution.py:24
  99.7 2.7 %reshape_reshape.12 = bf16[4,256,4,128]{1,0,3,2:T(4,128)(2,1)} reshape(bf16[1024,512]{0,1:T(8,128)(2,1)} %copy-done.2) | data formatting | bytes 2097152 | tf_op jit(solution)/shard_map/reshape;reshape | solution.py:45
  103.2 3.8 %collective-permute-start.1 = (bf16[256,4,128]{2,0,1:T(8,128)(2,1)}, bf16[256,4,128]{2,0,1:T(8,128)(2,1)S(1)}, u32[]{:S(2)}, u32[]{:S(2)}) collective-permute-start(bf16[256,4,128]{2,0,1:T(8,128)(2,1)} %copy.41), channel_id=1, source_target_pairs={{0,4},{4,8},{8,12},{12,16},{16,20},{20,24},{24,28},{1,5},{5,9},{9,... | collective-permute-start | bytes 786440 | tf_op jit(solution)/shard_map/ppermute | solution.py:13
  108.7 4.0 %collective-permute-start = (bf16[256,4,128]{2,0,1:T(8,128)(2,1)}, bf16[256,4,128]{2,0,1:T(8,128)(2,1)}, u32[]{:S(2)}, u32[]{:S(2)}) collective-permute-start(bf16[256,4,128]{2,0,1:T(8,128)(2,1)} %copy.37), channel_id=1, source_target_pairs={{0,4},{4,8},{8,12},{12,16},{16,20},{20,24},{24,28},{1,5},{5,9},{9,... | collective-permute-start | bytes 786440 | tf_op jit(solution)/shard_map/ppermute | solution.py:13
  112.8 2.8 %copy.56 = bf16[4,256,4,128]{3,2,0,1:T(4,128)(2,1)} copy(bf16[4,256,4,128]{1,0,3,2:T(4,128)(2,1)} %reshape_reshape.12) | data formatting | bytes 2097152 | tf_op jit(solution)/shard_map/reshape;reshape | solution.py:45
  118.1 4.4 %all-to-all-start.3 = ((bf16[4,256,4,128]{3,2,0,1:T(4,128)(2,1)}), bf16[4,256,4,128]{3,2,0,1:T(4,128)(2,1)}, u32[]{:S(2)}, u32[]{:S(2)}) async-start(bf16[4,256,4,128]{3,2,0,1:T(4,128)(2,1)} %copy.56), calls=%async_computation.3 | async-start | bytes 2097152 | tf_op jit(solution)/shard_map/all_to_all | solution.py:90
  137.4 4.2 %select_reduce_fusion = (f32[4,4,256]{2,1,0:T(4,128)S(1)}, f32[4,4,256,512]{3,2,1,0:T(8,128)}) fusion(pred[4,256,512]{2,1,0:T(8,128)(4,1)S(1)} %copy-done.4, bf16[4,256,4,128]{3,1,2,0:T(8,128)(2,1)S(1)} %copy-done.9, bf16[4,256,4,128]{3,2,1,0:T(4,128)(2,1)S(1)} %copy-done.3, bf16[4,256,4,128]{3,1,0,2:T(8,128)(2,1)S(1)} %bitcast.118), kind=kOutput, calls=%fused_computation.1 | convolution fusion | flops 547352576 | bytes 12075008 | tf_op jit(solution)/shard_map/bthd,buhd->bhtu/dot_general | solution.py:51
  150.8 8.7 %all-to-all-start.2 = ((bf16[8,2,256]{2,1,0:T(2,128)(2,1)}), bf16[8,2,256]{2,1,0:T(2,128)(2,1)S(1)}, u32[]{:S(2)}, u32[]{:S(2)}) async-start(bf16[8,2,256]{2,1,0:T(2,128)(2,1)} %reshape.210), calls=%async_computation.2 | async-start | bytes 16384 | tf_op jit(solution)/shard_map/all_to_all | solution.py:123
  162.6 3.4 %all-to-all-done.2 = bf16[8,2,256]{2,1,0:T(2,128)(2,1)S(1)} async-done(((bf16[8,2,256]{2,1,0:T(2,128)(2,1)}), bf16[8,2,256]{2,1,0:T(2,128)(2,1)S(1)}, u32[]{:S(2)}, u32[]{:S(2)}) %all-to-all-start.2) | async-done | bytes 8224 | tf_op jit(solution)/shard_map/all_to_all | solution.py:123
  166.0 3.3 %all-to-all-start.5 = ((bf16[8,2,256]{2,1,0:T(2,128)(2,1)}), bf16[8,2,256]{2,1,0:T(2,128)(2,1)S(1)}, u32[]{:S(2)}, u32[]{:S(2)}) async-start(bf16[8,2,256]{2,1,0:T(2,128)(2,1)} %reshape.208), calls=%async_computation.5 | async-start | bytes 16384 | tf_op jit(solution)/shard_map/all_to_all | solution.py:126
  169.4 2.7 %fusion.17 = bf16[32,32,4,128]{3,0,2,1:T(8,128)(2,1)S(1)} fusion(bf16[32,32,4,128]{3,0,2,1:T(8,128)(2,1)S(1)} %bitcast.117, f32[32,4,32,32]{2,3,1,0:T(8,128)} %get-tuple-element.13, f32[32,32,4]{0,2,1:T(4,128)S(1)} %get-tuple-element.8, f32[32,4,32]{2,1,0:T(4,128)S(1)} %get-tuple-element.12, pred[32,32]{0,1:T(8,128)(4,1)S(1)} %iota_compare_fusion.2), kind=kOutput, calls=%fused_computation.23 | convolution fusion | flops 35127296 | bytes 2655232 | tf_op jit(solution)/shard_map/chrs,schd->rchd/dot_general | solution.py:108
  175.8 3.7 %all-to-all-start.4 = ((bf16[32,32,4,128]{3,2,1,0:T(4,128)(2,1)}), bf16[32,32,4,128]{3,2,1,0:T(4,128)(2,1)S(1)}, u32[]{:S(2)}, u32[]{:S(2)}) async-start(bf16[32,32,4,128]{3,2,1,0:T(4,128)(2,1)} %copy.60), calls=%async_computation.4 | async-start | bytes 2097152 | tf_op jit(solution)/shard_map/all_to_all | solution.py:122
  179.8 7.5 %fusion.18 = f32[4,256,4,128]{1,3,2,0:T(8,128)} fusion(f32[4,4,256,512]{3,2,1,0:T(8,128)} %get-tuple-element.11, f32[4,4,256]{2,1,0:T(4,128)S(1)} %get-tuple-element.10, pred[4,256,512]{2,1,0:T(8,128)(4,1)} %broadcast_and_fusion, bf16[4,256,4,128]{1,3,2,0:T(8,128)(2,1)} %copy.40, bf16[4,256,4,128]{1,3,2,0:T(8,128)(2,1)} %copy.39), kind=kOutput, calls=%fused_computation.26 | convolution fusion | flops 549453824 | bytes 13123584 | tf_op jit(solution)/shard_map/bhtu,buhd->bthd/dot_general | solution.py:66
  187.2 3.0 %copy.46 = f32[4,256,4,128]{3,2,1,0:T(4,128)} copy(f32[4,256,4,128]{1,3,2,0:T(8,128)} %fusion.18) | data formatting | bytes 4194304 | tf_op jit(solution)/shard_map/bhtu,buhd->bthd/transpose | solution.py:66
  190.2 5.1 %fusion = f32[4,4,256]{2,1,0:T(4,128)S(1)} fusion(f32[4,4,256,512]{3,2,1,0:T(8,128)} %get-tuple-element.11, f32[4,4,256]{2,1,0:T(4,128)S(1)} %get-tuple-element.10, pred[4,256,512]{2,1,0:T(8,128)(4,1)} %broadcast_and_fusion), kind=kLoop, calls=%fused_computation.2 | loop fusion | flops 8384512 | bytes 8945664 | tf_op jit(solution)/shard_map/reduce_sum | solution.py:65
  198.8 4.8 %all-to-all-done.4 = bf16[32,32,4,128]{3,2,1,0:T(4,128)(2,1)S(1)} async-done(((bf16[32,32,4,128]{3,2,1,0:T(4,128)(2,1)}), bf16[32,32,4,128]{3,2,1,0:T(4,128)(2,1)S(1)}, u32[]{:S(2)}, u32[]{:S(2)}) %all-to-all-start.4) | async-done | bytes 1048608 | tf_op jit(solution)/shard_map/all_to_all | solution.py:122
  208.5 4.6 %convolution_convert_fusion = bf16[1024,2048]{1,0:T(8,128)(2,1)} fusion(bf16[512,2048]{1,0:T(8,128)(2,1)S(1)} %copy-done, f32[128,8,4,128]{3,2,1,0:T(4,128)S(1)} %bitcast.114, f32[128,8,4,128]{3,2,1,0:T(4,128)S(1)} %bitcast.112, f32[128,8,4,128]{3,2,1,0:T(4,128)S(1)} %bitcast.115, f32[128,8,4,128]{3,2,1,0:T(4,128)S(1)} %bitcast.113, ...), kind=kOutput, calls=%fused_computation.9 | convolution fusion | flops 2152202240 | bytes 16777216 | tf_op jit(solution)/shard_map/dot_general | solution.py:143
  213.1 42.6 %reduce-scatter.2.cloned.1.call-done = bf16[256,2048]{1,0:T(8,128)(2,1)} async-done(((bf16[1024,2048]{1,0:T(8,128)(2,1)}), bf16[256,2048]{1,0:T(8,128)(2,1)}) %reduce-scatter.2.cloned.1.call-update) | async-done | bytes 1048592 | tf_op jit(solution)/shard_map/reduce_scatter | solution.py:142
  (83 shorter events, 55.9 us)
Async XLA Ops:
  6.5 201.9 %copy-start = (bf16[512,2048]{1,0:T(8,128)(2,1)S(1)}, bf16[512,2048]{1,0:T(8,128)(2,1)}, u32[]{:S(2)}) copy-start(bf16[512,2048]{1,0:T(8,128)(2,1)} %param.9) | copy-start | bytes 6291460
  6.5 39.6 %all-gather.2.cloned.1.call-start = ((), (), s32[]{:S(2)}) async-start(), calls=%async_computation.7 | async-start | bytes 5242880 | tf_op jit(solution)/shard_map/all_gather | solution.py:21
  56.4 31.8 %all-to-all-start.1 = ((bf16[4,256,4,128]{3,2,0,1:T(4,128)(2,1)}), bf16[4,256,4,128]{3,2,0,1:T(4,128)(2,1)}, u32[]{:S(2)}, u32[]{:S(2)}) async-start(bf16[4,256,4,128]{3,2,0,1:T(4,128)(2,1)} %copy.49), calls=%async_computation.1 | async-start | bytes 2097152 | tf_op jit(solution)/shard_map/all_to_all | solution.py:83
  88.2 29.9 %all-to-all-start = ((bf16[4,256,4,128]{3,2,0,1:T(4,128)(2,1)}), bf16[4,256,4,128]{3,2,0,1:T(4,128)(2,1)}, u32[]{:S(2)}, u32[]{:S(2)}) async-start(bf16[4,256,4,128]{3,2,0,1:T(4,128)(2,1)} %copy.47), calls=%async_computation | async-start | bytes 2097152 | tf_op jit(solution)/shard_map/all_to_all | solution.py:76
  97.9 1.0 copy-start.2
  98.9 3.4 %slice-start = ((bf16[1024,512]{0,1:T(8,128)(2,1)}), bf16[256,512]{0,1:T(8,128)(2,1)S(1)}, s32[]{:S(2)}) async-start(bf16[1024,512]{0,1:T(8,128)(2,1)} %convolution_convert_fusion.1), calls=%async_computation.9 | async-start | bytes 524288 | tf_op jit(solution)/shard_map/slice | solution.py:31
  103.2 32.6 %collective-permute-start.1 = (bf16[256,4,128]{2,0,1:T(8,128)(2,1)}, bf16[256,4,128]{2,0,1:T(8,128)(2,1)S(1)}, u32[]{:S(2)}, u32[]{:S(2)}) collective-permute-start(bf16[256,4,128]{2,0,1:T(8,128)(2,1)} %copy.41), channel_id=1, source_target_pairs={{0,4},{4,8},{8,12},{12,16},{16,20},{20,24},{24,28},{1,5},{5,9},{9,... | collective-permute-start | bytes 786440 | tf_op jit(solution)/shard_map/ppermute | solution.py:13
  108.7 22.4 %collective-permute-start = (bf16[256,4,128]{2,0,1:T(8,128)(2,1)}, bf16[256,4,128]{2,0,1:T(8,128)(2,1)}, u32[]{:S(2)}, u32[]{:S(2)}) collective-permute-start(bf16[256,4,128]{2,0,1:T(8,128)(2,1)} %copy.37), channel_id=1, source_target_pairs={{0,4},{4,8},{8,12},{12,16},{16,20},{20,24},{24,28},{1,5},{5,9},{9,... | collective-permute-start | bytes 786440 | tf_op jit(solution)/shard_map/ppermute | solution.py:13
  118.1 32.8 %all-to-all-start.3 = ((bf16[4,256,4,128]{3,2,0,1:T(4,128)(2,1)}), bf16[4,256,4,128]{3,2,0,1:T(4,128)(2,1)}, u32[]{:S(2)}, u32[]{:S(2)}) async-start(bf16[4,256,4,128]{3,2,0,1:T(4,128)(2,1)} %copy.56), calls=%async_computation.3 | async-start | bytes 2097152 | tf_op jit(solution)/shard_map/all_to_all | solution.py:90
  125.0 4.8 %copy-start.1 = (bf16[1024,512]{0,1:T(8,128)(2,1)S(1)}, bf16[1024,512]{0,1:T(8,128)(2,1)}, u32[]{:S(2)}) copy-start(bf16[1024,512]{0,1:T(8,128)(2,1)} %convolution_convert_fusion.1) | copy-start | bytes 3145732
  133.4 3.7 %copy-start.3 = (bf16[4,256,4,128]{3,2,1,0:T(4,128)(2,1)S(1)}, bf16[4,256,4,128]{3,2,1,0:T(4,128)(2,1)}, u32[]{:S(2)}) copy-start(bf16[4,256,4,128]{3,2,1,0:T(4,128)(2,1)} %reshape_reshape.13) | copy-start | bytes 3145732
  135.7 1.3 copy-start.4
  135.7 1.6 copy-start.9
  150.8 15.2 %all-to-all-start.2 = ((bf16[8,2,256]{2,1,0:T(2,128)(2,1)}), bf16[8,2,256]{2,1,0:T(2,128)(2,1)S(1)}, u32[]{:S(2)}, u32[]{:S(2)}) async-start(bf16[8,2,256]{2,1,0:T(2,128)(2,1)} %reshape.210), calls=%async_computation.2 | async-start | bytes 16384 | tf_op jit(solution)/shard_map/all_to_all | solution.py:123
  166.0 9.8 %all-to-all-start.5 = ((bf16[8,2,256]{2,1,0:T(2,128)(2,1)}), bf16[8,2,256]{2,1,0:T(2,128)(2,1)S(1)}, u32[]{:S(2)}, u32[]{:S(2)}) async-start(bf16[8,2,256]{2,1,0:T(2,128)(2,1)} %reshape.208), calls=%async_computation.5 | async-start | bytes 16384 | tf_op jit(solution)/shard_map/all_to_all | solution.py:126
  175.8 27.9 %all-to-all-start.4 = ((bf16[32,32,4,128]{3,2,1,0:T(4,128)(2,1)}), bf16[32,32,4,128]{3,2,1,0:T(4,128)(2,1)S(1)}, u32[]{:S(2)}, u32[]{:S(2)}) async-start(bf16[32,32,4,128]{3,2,1,0:T(4,128)(2,1)} %copy.60), calls=%async_computation.4 | async-start | bytes 2097152 | tf_op jit(solution)/shard_map/all_to_all | solution.py:122
  179.5 76.1 %reduce-scatter.2.cloned.1.call-start = ((), (), s32[]{:S(2)}) async-start(), calls=%async_computation.8 | async-start | bytes 5242880 | tf_op jit(solution)/shard_map/reduce_scatter | solution.py:142
  203.7 1.0 copy-start.7
  203.9 2.0 copy-start.6
  204.7 2.5 copy-start.5
  205.9 2.5 copy-start.8
Sparse Core Ops, SparseCore 0:
  8.9 37.1 all-gather.1
  213.2 42.3 reduce-scatter.1
where the time goes:
time: 263 us; the launch traced here: 262 us
  waiting for transfers between devices  110 us (42%)
  local copies, waits for them, and re-layouts  49.5 us (19%)
  matrix products  38.6 us (15%)
  starting transfers between devices  38 us (14%)
  between operations  13.7 us (5%)
  other arithmetic  12.2 us (5%)
    reduce_scatter x1, waiting for transfers between devices, shards(): lax.psum_scatter(jnp.dot(mixed, w_out, preferred_element_type=jnp.float32...  42.6 us
    all_gather x1, waiting for transfers between devices, shards(): shard_piece = lax.all_gather(tokens, 'head', axis=1, tiled=True)  38.9 us
    dot_general x3, matrix products, shards(): jnp.dot(shard_piece, weight, preferred_element_type=jnp.float32)  17.6 us
    all_to_all x1, waiting for transfers between devices, shards(): lax.all_to_all(key_heads.reshape(row_count, STRIDE, head_count, DH), 'seq...  15.4 us
    all_to_all x1, starting transfers between devices, shards(): lax.all_to_all(column_top.astype(jnp.bfloat16), 'seq', split_axis=0, conc...  8.67 us
    another operation x3, local copies, waits for them, and re-layouts, shards(): extended_values[STRIDE:].reshape(blocks, STRIDE, head_count, DH)  8.04 us
    ppermute x2, starting transfers between devices, from_behind(): return lax.ppermute(value, axis, pairs)  7.83 us
    dot_general x1, matrix products, shards(): jnp.einsum('bhtu,buhd->bthd', local_weights.astype(jnp.bfloat16), window_...  7.46 us
  transfers between devices with their start and end apart: 10, of which 7 were waited for; matrix products, arithmetic and copies ran while one was open for 30% of the time, Pallas kernels for 0%

commit v1 on v0

--- a/solution.py
+++ b/solution.py
@@ -1,10 +1,389 @@
+import functools
+
 import jax
 import jax.numpy as jnp
 from jax import lax
+from jax.experimental import pallas as pl
+from jax.experimental.pallas import tpu as pltpu
 from jax.sharding import PartitionSpec as P
 
 DH = 128
 STRIDE = 256
+HEADS = 4
+ROWS = 4
+SUB = 8
+CHUNKS = 2
+SCALE2 = DH ** (-0.5) * 1.4426950408889634
+FLOOR = -1e29
+MIB = 1024 * 1024
+F32 = jnp.float32
+BF16 = jnp.bfloat16
+
+
+def params(mib, **kw):
+    return pltpu.CompilerParams(vmem_limit_bytes=mib * MIB, **kw)
+
+
+def cost(flops, moved, exps=0):
+    return pl.CostEstimate(flops=flops, bytes_accessed=moved, transcendentals=exps)
+
+
+def dot(a, b):
+    return jnp.dot(a, b, preferred_element_type=F32)
+
+
+def dot_t(a, b):
+    return lax.dot_general(a, b, (((1,), (1,)), ((), ())), preferred_element_type=F32)
+
+
+def pack_kernel(tok_ref, *out_refs):
+    owners = out_refs[0].shape[0]
+    per_owner = STRIDE // owners
+    groups = per_owner // SUB
+    per_chunk = groups // len(out_refs)
+    for d in range(owners):
+        rows = [
+            tok_ref[r * STRIDE + d * per_owner : r * STRIDE + (d + 1) * per_owner, :].astype(F32)
+            for r in range(ROWS)
+        ]
+        for g in range(groups):
+            piece = jnp.concatenate([x[g * SUB : (g + 1) * SUB] for x in rows], 0)
+            at = (g % per_chunk) * ROWS * SUB
+            out_refs[g // per_chunk][d, at : at + ROWS * SUB, :] = piece.astype(BF16)
+
+
+def pack(tokens, owners):
+    width = tokens.shape[1]
+    message = tokens.shape[0] // owners // CHUNKS
+    return pl.pallas_call(
+        pack_kernel,
+        out_shape=[jax.ShapeDtypeStruct((owners, message, width), BF16)] * CHUNKS,
+        compiler_params=params(16),
+        cost_estimate=cost(0, 2 * tokens.size * 2),
+        name="pack_tokens",
+    )(tokens)
+
+
+def project_kernel(order_ref, x0, x1, x2, x3, wq, wk, wv, q_ref, k_ref, v_ref, halo_ref):
+    for n, (w_ref, out_ref) in enumerate(((wq, q_ref), (wk, k_ref), (wv, v_ref))):
+        total = None
+        for p, x_ref in enumerate((x0, x1, x2, x3)):
+            rows = pl.ds(pl.multiple_of(order_ref[p] * 512, 512), 512)
+            term = dot(x_ref[...], w_ref[rows, :])
+            total = term if total is None else total + term
+        total = total.astype(BF16)
+        out_ref[...] = total
+        if n:
+            halo_ref[(n - 1) * STRIDE : n * STRIDE, :] = total[-STRIDE:]
+
+
+def project(order, pieces, weights):
+    rows, width = pieces[0].shape
+    tile = 512
+    full = lambda m, s: (0, 0)
+    tiled = lambda m, s: (m, 0)
+    return pl.pallas_call(
+        project_kernel,
+        grid_spec=pltpu.PrefetchScalarGridSpec(
+            num_scalar_prefetch=1,
+            grid=(rows // tile,),
+            in_specs=[pl.BlockSpec((tile, width), tiled)] * 4
+            + [pl.BlockSpec(weights[0].shape, full)] * 3,
+            out_specs=[pl.BlockSpec((tile, width), tiled)] * 3
+            + [pl.BlockSpec((2 * STRIDE, width), full)],
+        ),
+        out_shape=[jax.ShapeDtypeStruct((rows, width), BF16)] * 3
+        + [jax.ShapeDtypeStruct((2 * STRIDE, width), BF16)],
+        compiler_params=params(32),
+        cost_estimate=cost(2 * rows * 2048 * 3 * width, 14 * MIB),
+        name="project_block",
+    )(order, *pieces, *weights)
+
+
+def local_kernel(pos_ref, q_ref, k_ref, v_ref, kp_ref, vp_ref, halo_ref, out_ref, lse_ref):
+    r = pl.program_id(0)
+    first = r == 0
+    no_prev = jnp.logical_and(first, pos_ref[0] == 0)
+    t = lax.broadcasted_iota(jnp.int32, (STRIDE, STRIDE), 0)
+    u = lax.broadcasted_iota(jnp.int32, (STRIDE, STRIDE), 1)
+    current = u <= t
+    lane = lax.broadcasted_iota(jnp.int32, (STRIDE, 128), 1)
+    low = jnp.where(no_prev, -1e30, 0.0).astype(F32)
+    lses = jnp.zeros((STRIDE, 128), F32)
+    for h in range(HEADS):
+        cols = slice(h * DH, (h + 1) * DH)
+        q = q_ref[:, cols]
+        k_prev = jnp.where(first, halo_ref[:STRIDE, cols], kp_ref[:, cols])
+        v_prev = jnp.where(first, halo_ref[STRIDE:, cols], vp_ref[:, cols])
+        s = jnp.where(current, dot_t(q, k_ref[:, cols]), dot_t(q, k_prev) + low)
+        m = jnp.max(s, -1, keepdims=True)
+        p = jnp.exp2((s - m) * SCALE2)
+        total = jnp.sum(p, -1, keepdims=True)
+        p_now = jnp.where(current, p, 0.0).astype(BF16)
+        p_prev = jnp.where(current, 0.0, p).astype(BF16)
+        o = dot(p_now, v_ref[:, cols]) + dot(p_prev, v_prev)
+        out_ref[:, cols] = o / total
+        lses = jnp.where(lane == h, m * SCALE2 + jnp.log2(total), lses)
+    lse_ref[...] = lses
+
+
+def local_part(pos, q, k, v, halo):
+    rows, width = q.shape
+    tile = lambda r, s: (r, 0)
+    back = lambda r, s: (jnp.maximum(r - 1, 0), 0)
+    block = (STRIDE, width)
+    return pl.pallas_call(
+        local_kernel,
+        grid_spec=pltpu.PrefetchScalarGridSpec(
+            num_scalar_prefetch=1,
+            grid=(rows // STRIDE,),
+            in_specs=[pl.BlockSpec(block, tile)] * 3
+            + [pl.BlockSpec(block, back)] * 2
+            + [pl.BlockSpec((2 * STRIDE, width), lambda r, s: (0, 0))],
+            out_specs=[pl.BlockSpec(block, tile), pl.BlockSpec((STRIDE, 128), tile)],
+        ),
+        out_shape=[
+            jax.ShapeDtypeStruct((rows, width), F32),
+            jax.ShapeDtypeStruct((rows, 128), F32),
+        ],
+        compiler_params=params(24),
+        cost_estimate=cost(8 * rows * STRIDE * width, 8 * MIB, rows * STRIDE * HEADS),
+        name="local_part",
+    )(pos, q, k, v, k, v, halo)
+
+
+def column_kernel(order_ref, x0, x1, x2, x3, wq, wk, wv, out_ref, aq, ak, av):
+    step = pl.program_id(0)
+    owners, message, width = x0.shape
+    groups = message // (ROWS * SUB)
+    for p, x_ref in enumerate((x0, x1, x2, x3)):
+
+        @pl.when(step == p)
+        def _(p=p, x_ref=x_ref):
+            x = x_ref[...].reshape(owners * message, width)
+            for w_ref, acc in ((wq, aq), (wk, ak), (wv, av)):
+                term = dot(x, w_ref[...]).reshape(acc.shape)
+                acc[...] = term if p == 0 else acc[...] + term
+
+    @pl.when(step == 3)
+    def _():
+        size = owners * ROWS * SUB
+        i = lax.broadcasted_iota(jnp.int32, (size, size), 0)
+        j = lax.broadcasted_iota(jnp.int32, (size, size), 1)
+        earlier = jnp.logical_and(i % SUB == j % SUB, i > j)
+        part = ROWS * SUB
+        lane = lax.broadcasted_iota(jnp.int32, (part, 128), 1)
+        stats = []
+        for g in range(groups):
+            at = slice(g * part, (g + 1) * part)
+            stat = jnp.zeros((part, 128), F32)
+            for h in range(HEADS):
+                cols = slice(h * DH, (h + 1) * DH)
+                q, k, v = (a[:, at, cols].reshape(size, DH).astype(BF16) for a in (aq, ak, av))
+                s = jnp.where(earlier, dot_t(q, k), -1e30)
+                m = jnp.maximum(jnp.max(s, -1, keepdims=True), FLOOR)
+                e = jnp.exp2((s - m) * SCALE2)
+                total = jnp.maximum(jnp.sum(e, -1, keepdims=True), 1.0)
+                o = dot(e.astype(BF16), v) / total
+                rows = slice(h * message + g * part, h * message + (g + 1) * part)
+                out_ref[:, rows, :] = o.astype(BF16).reshape(owners, part, DH)
+                lse = (m * SCALE2 + jnp.log2(total)).reshape(owners, part, 1)
+                for d in range(owners):
+                    mine = jnp.logical_and(lane // 8 == d, lane % 4 == h)
+                    stat = jnp.where(mine, lse[d], stat)
+            stats.append(stat)
+        if message < 128:
+            stats.append(jnp.zeros((128 - message, 128), F32))
+        turned = jnp.concatenate(stats, 0).T
+        upper = lax.broadcasted_iota(jnp.int32, (8, 128), 0) < 4
+        for d in range(owners):
+            x = turned[8 * d : 8 * d + 8]
+            hi = x.astype(BF16).astype(F32)
+            mid = (x - hi).astype(BF16).astype(F32)
+            lo = x - hi - mid
+            tail = jnp.concatenate([jnp.where(upper, hi, lo), jnp.where(upper, mid, 0.0)], 0)
+            out_ref[d, HEADS * message : HEADS * message + 16, :] = tail.astype(BF16)
+
+
+def column_part(order, pieces, weights):
+    owners, message, width = pieces[0].shape
+    rows_out = HEADS * message + 16
+    whole = lambda p, s: (0, 0, 0)
+    tokens = owners * message
+    return pl.pallas_call(
+        column_kernel,
+        grid_spec=pltpu.PrefetchScalarGridSpec(
+            num_scalar_prefetch=1,
+            grid=(4,),
+            in_specs=[pl.BlockSpec(pieces[0].shape, whole)] * 4
+            + [pl.BlockSpec((512, width), lambda p, s: (s[p], 0))] * 3,
+            out_specs=pl.BlockSpec((owners, rows_out, DH), whole),
+            scratch_shapes=[pltpu.VMEM((owners, message, width), F32)] * 3,
+        ),
+        out_shape=jax.ShapeDtypeStruct((owners, rows_out, DH), BF16),
+        compiler_params=params(32),
+        cost_estimate=cost(2 * tokens * 2048 * 3 * width, 10 * MIB, tokens * 256 * HEADS),
+        name="column_part",
+    )(order, *pieces, *weights)
+
+
+def mix_kernel(chunk, pos_ref, col_ref, loc_ref, lse_ref, own_ref, send_ref, mixed):
+    owners = col_ref.shape[0]
+    message = (col_ref.shape[1] - 16) // HEADS
+    groups = message // (ROWS * SUB)
+    per_owner = STRIDE // owners
+    base = HEADS * message
+    tiles = []
+    for d in range(owners):
+        tail = col_ref[d, base : base + 16, :].astype(F32)
+        tiles.append(tail[:8] + tail[8:])
+    tiles.append(jnp.zeros((128 - 8 * owners, 128), F32))
+    turned = jnp.concatenate(tiles, 0).T[:message]
+    for d in range(owners):
+        spots = [
+            r * STRIDE + d * per_owner + (chunk * groups + g) * SUB
+            for g in range(groups)
+            for r in range(ROWS)
+        ]
+        local_lse = jnp.concatenate([lse_ref[s : s + SUB, :] for s in spots], 0)
+        for h in range(HEADS):
+            cols = slice(h * DH, (h + 1) * DH)
+            col = col_ref[d, h * message : (h + 1) * message, :].astype(F32)
+            loc = jnp.concatenate([loc_ref[s : s + SUB, cols] for s in spots], 0)
+            at = 8 * d + h
+            col_lse = turned[:, at : at + 1] + turned[:, at + 4 : at + 5]
+            loc_lse = local_lse[:, h : h + 1]
+            top = jnp.maximum(col_lse, loc_lse)
+            w_col = jnp.exp2(col_lse - top)
+            w_loc = jnp.exp2(loc_lse - top)
+            both = (loc * w_loc + col * w_col) / (w_loc + w_col)
+            for r in range(ROWS):
+                piece = jnp.concatenate(
+                    [both[(g * ROWS + r) * SUB : (g * ROWS + r + 1) * SUB] for g in range(groups)], 0
+                )
+                span = groups * SUB
+                mixed[r, d * span : (d + 1) * span, cols] = piece.astype(BF16)
+    core = pos_ref[1]
+    for x in range(2):
+        own_ref[x] = mixed[2 * x + core]
+        send_ref[x] = mixed[2 * x + 1 - core]
+
+
+def mix(pos, chunk, column, local, lse):
+    owners = column.shape[0]
+    message = (column.shape[1] - 16) // HEADS
+    tokens = owners * message // ROWS
+    width = local.shape[1]
+    vmem = pl.BlockSpec(memory_space=pltpu.VMEM)
+    return pl.pallas_call(
+        functools.partial(mix_kernel, chunk),
+        in_specs=[pl.BlockSpec(memory_space=pltpu.SMEM), vmem, vmem, vmem],
+        out_specs=[vmem, vmem],
+        out_shape=[jax.ShapeDtypeStruct((2, tokens, width), BF16)] * 2,
+        scratch_shapes=[pltpu.VMEM((ROWS, tokens, width), BF16)],
+        compiler_params=params(16),
+        cost_estimate=cost(8 * tokens * ROWS * width, 4 * MIB),
+        name="mix",
+    )(pos, column, local, lse)
+
+
+def out_kernel(which_ref, a_ref, b_ref, wa_ref, wb_ref, out_ref):
+    total = dot(a_ref[0], wa_ref[...]) + dot(b_ref[0], wb_ref[...])
+    out_ref[...] = total.astype(out_ref.dtype)
+
+
+def out_project(which, own, other, w_own, w_other, dtype):
+    _, tokens, width = own.shape
+    columns = w_own.shape[1]
+    tile = 512
+    rows = pl.BlockSpec((1, tokens, width), lambda n, s: (s[0], 0, 0))
+    cols = pl.BlockSpec((width, tile), lambda n, s: (0, n))
+    return pl.pallas_call(
+        out_kernel,
+        grid_spec=pltpu.PrefetchScalarGridSpec(
+            num_scalar_prefetch=1,
+            grid=(columns // tile,),
+            in_specs=[rows, rows, cols, cols],
+            out_specs=pl.BlockSpec((tokens, tile), lambda n, s: (0, n)),
+        ),
+        out_shape=jax.ShapeDtypeStruct((tokens, columns), dtype),
+        compiler_params=params(16),
+        cost_estimate=cost(4 * tokens * width * columns, 5 * MIB),
+        name="out_project",
+    )(which, own, other, w_own, w_other)
+
+
+def join_kernel(*refs):
+    out_ref = refs[-1]
+    chunks = (len(refs) - 1) // 2
+    tokens = refs[0].shape[0]
+    owners = STRIDE // 32
+    span = tokens // owners
+    for i in range(chunks):
+        keep, got = refs[2 * i], refs[2 * i + 1]
+        for d in range(owners):
+            rows = slice(d * span, (d + 1) * span)
+            at = (d * chunks + i) * span
+            total = keep[rows, :] + got[rows, :].astype(F32)
+            out_ref[at : at + span, :] = total.astype(BF16)
+
+
+def join(pairs):
+    tokens, columns = pairs[0][0].shape
+    tile = 512
+    spec = pl.BlockSpec((tokens, tile), lambda n: (0, n))
+    return pl.pallas_call(
+        join_kernel,
+        grid=(columns // tile,),
+        in_specs=[spec] * (2 * len(pairs)),
+        out_specs=pl.BlockSpec((STRIDE, tile), lambda n: (0, n)),
+        out_shape=jax.ShapeDtypeStruct((STRIDE, columns), BF16),
+        compiler_params=params(16),
+        cost_estimate=cost(STRIDE * columns, 4 * MIB),
+        name="join",
+    )(*[x for pair in pairs for x in pair])
+
+
+def swap(value, distance):
+    return lax.ppermute(value, "head", [(i, i ^ distance) for i in range(4)])
+
+
+def exchange(value):
+    return lax.all_to_all(value, "seq", split_axis=0, concat_axis=0, tiled=True)
+
+
+def gather(own):
+    far = swap(own, 2)
+    return own, swap(own, 1), far, swap(far, 1)
+
+
+def chunked(tokens, w_query, w_key, w_value, w_out):
+    owners = lax.axis_size("seq")
+    head = lax.axis_index("head")
+    block = lax.axis_index("seq")
+    weights = (w_query, w_key, w_value)
+    order = jnp.bitwise_xor(jnp.arange(4, dtype=jnp.int32), head.astype(jnp.int32))
+    pos = jnp.stack([block, head % 2]).astype(jnp.int32)
+    side = (head // 2).astype(jnp.int32).reshape(1)
+
+    messages = pack(tokens, owners)
+    block_pieces = gather(tokens)
+    w_other = swap(w_out, 1)
+    classes = [exchange(m) for m in messages]
+    q, k, v, halo = project(order, block_pieces, weights)
+    peers = owners
+    halo = lax.ppermute(halo, "seq", [(i, i + 1) for i in range(peers - 1)])
+    local, lse = local_part(pos, q, k, v, halo)
+    columns = [exchange(column_part(order, gather(c), weights)) for c in classes]
+    pairs = []
+    for i, column in enumerate(columns):
+        own, send = mix(pos, i, column, local, lse)
+        other = swap(send, 1)
+        out = out_project(1 - side, own, other, w_out, w_other, BF16)
+        got = swap(out, 2)
+        keep = out_project(side, own, other, w_out, w_other, F32)
+        pairs.append((keep, got))
+    return join(pairs)
 
 
 def from_behind(value, axis, by):
@@ -13,7 +392,7 @@
     return lax.ppermute(value, axis, pairs)
 
 
-def shards(tokens, w_query, w_key, w_value, w_out):
+def general(tokens, w_query, w_key, w_value, w_out):
     tok_rows = tokens.shape[0]
     head_width = w_query.shape[1]
     head_count = head_width // DH
@@ -147,6 +526,18 @@
     )
 
 
+def shards(tokens, w_query, w_key, w_value, w_out):
+    rows, width = w_query.shape
+    fits = (
+        lax.axis_size("seq") == STRIDE // 32
+        and lax.axis_size("head") == 4
+        and tokens.shape == (ROWS * STRIDE, HEADS * DH)
+        and (rows, width) == (4 * HEADS * DH, HEADS * DH)
+    )
+    plan = chunked if fits else general
+    return plan(tokens, w_query, w_key, w_value, w_out)
+
+
 def solution(mesh):
     in_specs = (
         P("seq", "head"),

time: 263 us -> 174 us (0.66)
  Pallas kernels: 0 us -> 57.5 us
  waiting for transfers between devices: 110 us -> 56.3 us
  matrix products: 38.6 us -> 0 us
  local copies, waits for them, and re-layouts: 49.5 us -> 22.8 us
  between operations: 13.7 us -> 0.19 us
  other arithmetic: 12.2 us -> 0.08 us
    pallas_call x0 -> x12, Pallas kernels: none -> 57.5 us  [the longest x2 15.4 us: column_part(): pl.pallas_call(column_kernel, grid_spec=pltpu.PrefetchScalarGridSpec(num_...]
    ppermute x2 -> x15, waiting for transfers between devices: 0.01 us -> 43.3 us  [the longest x14 33 us: swap(): return lax.ppermute(value, 'head', [(i, i ^ distance) for i in range(4)])]
    reduce_scatter x1 -> x0, waiting for transfers between devices: 42.6 us -> none  [shards(): lax.psum_scatter(jnp.dot(mixed, w_out, preferred_element_type=jnp.float32...]
    all_gather x1 -> x0, waiting for transfers between devices: 38.9 us -> none  [shards(): shard_piece = lax.all_gather(tokens, 'head', axis=1, tiled=True)]
    dot_general x8 -> x0, matrix products: 38.6 us -> none  [the longest x3 17.6 us: shards(): jnp.dot(shard_piece, weight, preferred_element_type=jnp.float32)]
    unnamed x24 -> x40, local copies, waits for them, and re-layouts: 3.63 us -> 22.8 us
    another operation x8 -> x0, local copies, waits for them, and re-layouts: 18.2 us -> none  [the longest x3 8.04 us: shards(): extended_values[STRIDE:].reshape(blocks, STRIDE, head_count, DH)]
    all_to_all x6 -> x4, waiting for transfers between devices: 28.3 us -> 13 us  [exchange(): return lax.all_to_all(value, 'seq', split_axis=0, concat_axis=0, tiled=True)]
  transfers between devices with their start and end apart: 10 -> 19, of which waited for: 7 -> 8; matrix products, arithmetic and copies ran while one was open for 30% -> 0% of each run, Pallas kernels for 0% -> 31%
where the time goes in v1:
time: 174 us; the launch traced here: 172 us
  Pallas kernels  57.5 us (33%)
  waiting for transfers between devices  56.3 us (32%)
  starting transfers between devices  35.6 us (20%)
  local copies, waits for them, and re-layouts  22.8 us (13%)
    ppermute x14, waiting for transfers between devices, swap(): return lax.ppermute(value, 'head', [(i, i ^ distance) for i in range(4)])  33 us
    unnamed x40, local copies, waits for them, and re-layouts  22.8 us
    all_to_all x4, starting transfers between devices, exchange(): return lax.all_to_all(value, 'seq', split_axis=0, concat_axis=0, tiled=True)  22.6 us
    pallas_call x2, Pallas kernels, column_part(): pl.pallas_call(column_kernel, grid_spec=pltpu.PrefetchScalarGridSpec(num_...  15.4 us
    all_to_all x4, waiting for transfers between devices, exchange(): return lax.all_to_all(value, 'seq', split_axis=0, concat_axis=0, tiled=True)  13 us
    pallas_call x4, Pallas kernels, out_project(): pl.pallas_call(out_kernel, grid_spec=pltpu.PrefetchScalarGridSpec(num_sca...  13 us
    ppermute x1, waiting for transfers between devices, chunked(): halo = lax.ppermute(halo, 'seq', [(i, i + 1) for i in range(peers - 1)])  10.4 us
    pallas_call x1, Pallas kernels, project(): pl.pallas_call(project_kernel, grid_spec=pltpu.PrefetchScalarGridSpec(num...  9.75 us
  transfers between devices with their start and end apart: 19, of which 8 were waited for; matrix products, arithmetic and copies ran while one was open for 0% of the time, Pallas kernels for 31%

profile of v1, /device:TPU:0, one launch (start us, length us, event | category | flops | bytes accessed | tf_op | source)
XLA Modules:
  0.0 172.5 jit_solution(9904474417228228898)
XLA Ops:
  0.0 2.3 %pack_tokens.1 = (bf16[8,64,512]{2,1,0:T(8,128)(2,1)}, bf16[8,64,512]{2,1,0:T(8,128)(2,1)}) custom-call(bf16[1024,512]{1,0:T(8,128)(2,1)} %x0.1), custom_call_target="tpu_custom_call" | custom-call | bytes 2097152 | tf_op jit(solution)/shard_map/pack_tokens/pallas_call | solution.py:58
  2.3 7.3 %all-to-all-start = ((bf16[8,64,512]{2,1,0:T(8,128)(2,1)}), bf16[8,64,512]{2,1,0:T(8,128)(2,1)S(1)}, u32[]{:S(2)}, u32[]{:S(2)}) async-start(bf16[8,64,512]{2,1,0:T(8,128)(2,1)} %get-tuple-element.17), calls=%async_computation | async-start | bytes 1048576 | tf_op jit(solution)/shard_map/all_to_all | solution.py:352
  11.0 13.0 %all-to-all-done.x0 = bf16[8,64,512]{2,1,0:T(8,128)(2,1)S(1)} async-done(((bf16[8,64,512]{2,1,0:T(8,128)(2,1)}), bf16[8,64,512]{2,1,0:T(8,128)(2,1)S(1)}, u32[]{:S(2)}, u32[]{:S(2)}) %all-to-all-start) | async-done | bytes 524320 | tf_op jit(solution)/shard_map/all_to_all | solution.py:352
  25.5 3.6 %all-to-all-start.2 = ((bf16[8,64,512]{2,1,0:T(8,128)(2,1)}), bf16[8,64,512]{2,1,0:T(8,128)(2,1)S(1)}, u32[]{:S(2)}, u32[]{:S(2)}) async-start(bf16[8,64,512]{2,1,0:T(8,128)(2,1)} %get-tuple-element.26), calls=%async_computation.2 | async-start | bytes 1048576 | tf_op jit(solution)/shard_map/all_to_all | solution.py:352
  29.2 16.5 %collective-permute-done.1.x2 = bf16[8,64,512]{2,1,0:T(8,128)(2,1)} collective-permute-done((bf16[8,64,512]{2,1,0:T(8,128)(2,1)S(1)}, bf16[8,64,512]{2,1,0:T(8,128)(2,1)}, u32[]{:S(2)}, u32[]{:S(2)}) %collective-permute-start.1) | collective-permute-done | bytes 524320 | tf_op jit(solution)/shard_map/ppermute | solution.py:348
  48.0 1.7 copy-done.11
  52.9 7.8 %column_part.2 = bf16[8,272,128]{2,1,0:T(8,128)(2,1)} custom-call(s32[4]{0:T(128)S(1)} %iota_xor_fusion.order_ref, bf16[8,64,512]{2,1,0:T(8,128)(2,1)S(1)} %all-to-all-done.x0, bf16[8,64,512]{2,1,0:T(8,128)(2,1)} %collective-permute-done.x1, bf16[8,64,512]{2,1,0:T(8,128)(2,1)} %collective-permute-done.1.x2, bf16[8,64,512]{2,1,0:T(8,128)(2,1)} %collective-permute-done.2.x3, ...), custom_call_target="tpu_custom_call" | custom-call | flops 3221225472 | bytes 10485760 | tf_op jit(solution)/shard_map/column_part/pallas_call | solution.py:213
  60.7 5.7 %all-to-all-start.1 = ((bf16[8,272,128]{2,1,0:T(8,128)(2,1)}), bf16[8,272,128]{2,1,0:T(8,128)(2,1)S(1)}, u32[]{:S(2)}, u32[]{:S(2)}) async-start(bf16[8,272,128]{2,1,0:T(8,128)(2,1)} %column_part.2), calls=%async_computation.1 | async-start | bytes 1114112 | tf_op jit(solution)/shard_map/all_to_all | solution.py:352
  68.4 1.7 collective-permute-done.12.x3
  74.8 7.6 %column_part.3 = bf16[8,272,128]{2,1,0:T(8,128)(2,1)} custom-call(s32[4]{0:T(128)S(1)} %iota_xor_fusion.order_ref, bf16[8,64,512]{2,1,0:T(8,128)(2,1)S(1)} %all-to-all-done.2.x0, bf16[8,64,512]{2,1,0:T(8,128)(2,1)S(1)} %collective-permute-done.10.x1, bf16[8,64,512]{2,1,0:T(8,128)(2,1)} %collective-permute-done.11.x2, ...), custom_call_target="tpu_custom_call" | custom-call | flops 3221225472 | bytes 10485760 | tf_op jit(solution)/shard_map/column_part/pallas_call | solution.py:213
  82.4 6.0 %all-to-all-start.3 = ((bf16[8,272,128]{2,1,0:T(8,128)(2,1)}), bf16[8,272,128]{2,1,0:T(8,128)(2,1)}, u32[]{:S(2)}, u32[]{:S(2)}) async-start(bf16[8,272,128]{2,1,0:T(8,128)(2,1)} %column_part.3), calls=%async_computation.3 | async-start | bytes 1114112 | tf_op jit(solution)/shard_map/all_to_all | solution.py:352
  93.2 9.7 %project_block.1 = (bf16[1024,512]{1,0:T(8,128)(2,1)S(1)}, bf16[1024,512]{1,0:T(8,128)(2,1)S(1)}, bf16[1024,512]{1,0:T(8,128)(2,1)S(1)}, bf16[512,512]{1,0:T(8,128)(2,1)}) custom-call(s32[4]{0:T(128)S(1)} %iota_xor_fusion.order_ref, bf16[1024,512]{1,0:T(8,128)(2,1)} %x0.1, bf16[1024,512]{1,0:T(8,128)(2,1)} %collective-permute-done.3.x1, ...), custom_call_target="tpu_custom_call" | custom-call | flops 6442450944 | bytes 14680064 | tf_op jit(solution)/shard_map/project_block/pallas_call | solution.py:85
  104.9 4.7 %collective-permute-start.6 = (bf16[512,512]{1,0:T(8,128)(2,1)}, bf16[512,512]{1,0:T(8,128)(2,1)}, u32[]{:S(2)}, u32[]{:S(2)}) collective-permute-start(bf16[512,512]{1,0:T(8,128)(2,1)} %get-tuple-element.21), channel_id=1, source_target_pairs={{0,4},{4,8},{8,12},{12,16},{16,20},{20,24},{24,28},{1,5},{5,9},{9,... | collective-permute-start | bytes 1572872 | tf_op jit(solution)/shard_map/ppermute | solution.py:375
  109.7 10.4 %collective-permute-done.6.halo_ref = bf16[512,512]{1,0:T(8,128)(2,1)} collective-permute-done((bf16[512,512]{1,0:T(8,128)(2,1)}, bf16[512,512]{1,0:T(8,128)(2,1)}, u32[]{:S(2)}, u32[]{:S(2)}) %collective-permute-start.6) | collective-permute-done | bytes 524320 | tf_op jit(solution)/shard_map/ppermute | solution.py:375
  122.5 7.1 %local_part.1 = (f32[1024,512]{1,0:T(8,128)S(1)}, f32[1024,128]{1,0:T(8,128)S(1)}) custom-call(s32[2]{0:T(128)S(1)} %pad_add_fusion.pos_ref, bf16[1024,512]{1,0:T(8,128)(2,1)S(1)} %copy-done.10, bf16[1024,512]{1,0:T(8,128)(2,1)S(1)} %get-tuple-element.19.k_ref.kp_ref, bf16[1024,512]{1,0:T(8,128)(2,1)S(1)} %copy-done.4, ...), custom_call_target="tpu_custom_call" | custom-call | flops 1073741824 | bytes 8388608 | tf_op jit(solution)/shard_map/local_part/pallas_call | solution.py:135
  129.6 3.5 %mix.2 = (bf16[2,128,512]{2,1,0:T(8,128)(2,1)S(1)}, bf16[2,128,512]{2,1,0:T(8,128)(2,1)S(1)}) custom-call(s32[2]{0:T(128)S(1)} %pad_add_fusion.pos_ref, bf16[8,272,128]{2,1,0:T(8,128)(2,1)S(1)} %copy-done.6, f32[1024,512]{1,0:T(8,128)S(1)} %get-tuple-element.22.loc_ref, f32[1024,128]{1,0:T(8,128)S(1)} %get-tuple-element.23.lse_ref), custom_call_target="tpu_custom_call" | custom-call | flops 2097152 | bytes 4194304 | tf_op jit(solution)/shard_map/mix/pallas_call | solution.py:278
  137.1 4.7 %mix.3 = (bf16[2,128,512]{2,1,0:T(8,128)(2,1)S(1)}, bf16[2,128,512]{2,1,0:T(8,128)(2,1)}) custom-call(s32[2]{0:T(128)S(1)} %pad_add_fusion.pos_ref, bf16[8,272,128]{2,1,0:T(8,128)(2,1)} %all-to-all-done.3.col_ref, f32[1024,512]{1,0:T(8,128)S(1)} %copy-done.2, f32[1024,128]{1,0:T(8,128)S(1)} %copy-done.8), custom_call_target="tpu_custom_call" | custom-call | flops 2097152 | bytes 4194304 | tf_op jit(solution)/shard_map/mix/pallas_call | solution.py:278
  142.3 3.2 %out_project.5 = bf16[128,2048]{1,0:T(8,128)(2,1)S(1)} custom-call(s32[1]{0:T(128)S(6)} %sub.9.which_ref, bf16[2,128,512]{2,1,0:T(8,128)(2,1)S(1)} %get-tuple-element.24.a_ref, bf16[2,128,512]{2,1,0:T(8,128)(2,1)S(1)} %collective-permute-done.7.b_ref, bf16[512,2048]{1,0:T(8,128)(2,1)S(1)} %copy-done, bf16[512,2048]{1,0:T(8,128)(2,1)} %collective-permute-done.8.wb_ref), custom_call_target="tpu_custom_call" | custom-call | flops 536870912 | bytes 5242880 | tf_op jit(solution)/shard_map/out_project/pallas_call | solution.py:301
  147.0 3.2 %out_project.7 = bf16[128,2048]{1,0:T(8,128)(2,1)S(1)} custom-call(s32[1]{0:T(128)S(6)} %sub.9.which_ref, bf16[2,128,512]{2,1,0:T(8,128)(2,1)S(1)} %get-tuple-element.27.a_ref, bf16[2,128,512]{2,1,0:T(8,128)(2,1)S(1)} %collective-permute-done.13.b_ref, bf16[512,2048]{1,0:T(8,128)(2,1)S(1)} %copy-done, bf16[512,2048]{1,0:T(8,128)(2,1)} %collective-permute-done.8.wb_ref), custom_call_target="tpu_custom_call" | custom-call | flops 536870912 | bytes 5242880 | tf_op jit(solution)/shard_map/out_project/pallas_call | solution.py:301
  151.0 3.2 %out_project.4.refs_0_ = f32[128,2048]{1,0:T(8,128)S(1)} custom-call(s32[1]{0:T(128)} %bitcast.which_ref, bf16[2,128,512]{2,1,0:T(8,128)(2,1)S(1)} %get-tuple-element.24.a_ref, bf16[2,128,512]{2,1,0:T(8,128)(2,1)S(1)} %collective-permute-done.7.b_ref, bf16[512,2048]{1,0:T(8,128)(2,1)S(1)} %copy-done, bf16[512,2048]{1,0:T(8,128)(2,1)} %collective-permute-done.8.wb_ref), custom_call_target="tpu_custom_call" | custom-call | flops 536870912 | bytes 5242880 | tf_op jit(solution)/shard_map/out_project/pallas_call | solution.py:301
  154.2 3.2 %out_project.6.refs_2_ = f32[128,2048]{1,0:T(8,128)S(1)} custom-call(s32[1]{0:T(128)} %bitcast.which_ref, bf16[2,128,512]{2,1,0:T(8,128)(2,1)S(1)} %get-tuple-element.27.a_ref, bf16[2,128,512]{2,1,0:T(8,128)(2,1)S(1)} %collective-permute-done.13.b_ref, bf16[512,2048]{1,0:T(8,128)(2,1)S(1)} %copy-done, bf16[512,2048]{1,0:T(8,128)(2,1)} %collective-permute-done.8.wb_ref), custom_call_target="tpu_custom_call" | custom-call | flops 536870912 | bytes 5242880 | tf_op jit(solution)/shard_map/out_project/pallas_call | solution.py:301
  157.5 2.9 %collective-permute-done.9.refs_1_ = bf16[128,2048]{1,0:T(8,128)(2,1)S(1)} collective-permute-done((bf16[128,2048]{1,0:T(8,128)(2,1)S(1)}, bf16[128,2048]{1,0:T(8,128)(2,1)S(1)}, u32[]{:S(2)}, u32[]{:S(2)}) %collective-permute-start.9) | collective-permute-done | bytes 524320 | tf_op jit(solution)/shard_map/ppermute | solution.py:348
  160.4 10.3 %collective-permute-done.14.refs_3_ = bf16[128,2048]{1,0:T(8,128)(2,1)S(1)} collective-permute-done((bf16[128,2048]{1,0:T(8,128)(2,1)S(1)}, bf16[128,2048]{1,0:T(8,128)(2,1)S(1)}, u32[]{:S(2)}, u32[]{:S(2)}) %collective-permute-start.14) | collective-permute-done | bytes 524320 | tf_op jit(solution)/shard_map/ppermute | solution.py:348
  170.7 1.8 %join.1 = bf16[256,2048]{1,0:T(8,128)(2,1)} custom-call(f32[128,2048]{1,0:T(8,128)S(1)} %out_project.4.refs_0_, bf16[128,2048]{1,0:T(8,128)(2,1)S(1)} %collective-permute-done.9.refs_1_, f32[128,2048]{1,0:T(8,128)S(1)} %out_project.6.refs_2_, bf16[128,2048]{1,0:T(8,128)(2,1)S(1)} %collective-permute-done.14.refs_3_), custom_call_target="tpu_custom_call" | custom-call | flops 524288 | bytes 4194304 | tf_op jit(solution)/shard_map/join/pallas_call | solution.py:335
  (68 shorter events, 31.0 us)
Async XLA Ops:
  2.3 21.8 %all-to-all-start = ((bf16[8,64,512]{2,1,0:T(8,128)(2,1)}), bf16[8,64,512]{2,1,0:T(8,128)(2,1)S(1)}, u32[]{:S(2)}, u32[]{:S(2)}) async-start(bf16[8,64,512]{2,1,0:T(8,128)(2,1)} %get-tuple-element.17), calls=%async_computation | async-start | bytes 1048576 | tf_op jit(solution)/shard_map/all_to_all | solution.py:352
  9.5 38.2 %collective-permute-start.4 = (bf16[1024,512]{1,0:T(8,128)(2,1)}, bf16[1024,512]{1,0:T(8,128)(2,1)}, u32[]{:S(2)}, u32[]{:S(2)}) collective-permute-start(bf16[1024,512]{1,0:T(8,128)(2,1)} %x0.1), channel_id=1, source_target_pairs={{0,2},{1,3},{2,0},{3,1},{4,6},{5,7},{6,4},{7,5},{8,10},{9,11},{10,... | collective-permute-start | bytes 3145736 | tf_op jit(solution)/shard_map/ppermute | solution.py:348
  24.0 21.7 %collective-permute-start.1 = (bf16[8,64,512]{2,1,0:T(8,128)(2,1)S(1)}, bf16[8,64,512]{2,1,0:T(8,128)(2,1)}, u32[]{:S(2)}, u32[]{:S(2)}) collective-permute-start(bf16[8,64,512]{2,1,0:T(8,128)(2,1)S(1)} %all-to-all-done.x0), channel_id=1, source_target_pairs={{0,2},{1,3},{2,0},{3,1},{4,6},{5,7},{6,4},{7,5},{8,10},{9,11},{10,... | collective-permute-start | bytes 1572872 | tf_op jit(solution)/shard_map/ppermute | solution.py:348
  25.5 20.7 %all-to-all-start.2 = ((bf16[8,64,512]{2,1,0:T(8,128)(2,1)}), bf16[8,64,512]{2,1,0:T(8,128)(2,1)S(1)}, u32[]{:S(2)}, u32[]{:S(2)}) async-start(bf16[8,64,512]{2,1,0:T(8,128)(2,1)} %get-tuple-element.26), calls=%async_computation.2 | async-start | bytes 1048576 | tf_op jit(solution)/shard_map/all_to_all | solution.py:352
  29.2 18.7 %collective-permute-start = (bf16[8,64,512]{2,1,0:T(8,128)(2,1)S(1)}, bf16[8,64,512]{2,1,0:T(8,128)(2,1)}, u32[]{:S(2)}, u32[]{:S(2)}) collective-permute-start(bf16[8,64,512]{2,1,0:T(8,128)(2,1)S(1)} %all-to-all-done.x0), channel_id=1, source_target_pairs={{0,1},{1,0},{2,3},{3,2},{4,5},{5,4},{6,7},{7,6},{8,9},{9,8},{10,11... | collective-permute-start | bytes 1572872 | tf_op jit(solution)/shard_map/ppermute | solution.py:348
  45.7 2.3 %collective-permute-start.2 = (bf16[8,64,512]{2,1,0:T(8,128)(2,1)}, bf16[8,64,512]{2,1,0:T(8,128)(2,1)}, u32[]{:S(2)}, u32[]{:S(2)}) collective-permute-start(bf16[8,64,512]{2,1,0:T(8,128)(2,1)} %collective-permute-done.1.x2), channel_id=1, source_target_pairs={{0,1},{1,0},{2,3},{3,2},{4,5},{5,4},{6,7},{7,6},{8,9},{9,8},{10,11... | collective-permute-start | bytes 1572872 | tf_op jit(solution)/shard_map/ppermute | solution.py:348
  45.7 42.7 %collective-permute-start.3 = (bf16[1024,512]{1,0:T(8,128)(2,1)}, bf16[1024,512]{1,0:T(8,128)(2,1)}, u32[]{:S(2)}, u32[]{:S(2)}) collective-permute-start(bf16[1024,512]{1,0:T(8,128)(2,1)} %x0.1), channel_id=1, source_target_pairs={{0,1},{1,0},{2,3},{3,2},{4,5},{5,4},{6,7},{7,6},{8,9},{9,8},{10,11... | collective-permute-start | bytes 3145736 | tf_op jit(solution)/shard_map/ppermute | solution.py:348
  46.2 20.2 %collective-permute-start.11 = (bf16[8,64,512]{2,1,0:T(8,128)(2,1)S(1)}, bf16[8,64,512]{2,1,0:T(8,128)(2,1)}, u32[]{:S(2)}, u32[]{:S(2)}) collective-permute-start(bf16[8,64,512]{2,1,0:T(8,128)(2,1)S(1)} %all-to-all-done.2.x0), channel_id=1, source_target_pairs={{0,2},{1,3},{2,0},{3,1},{4,6},{5,7},{6,4},{7,5},{8,10},{9,11},{10,... | collective-permute-start | bytes 1572872 | tf_op jit(solution)/shard_map/ppermute | solution.py:348
  47.7 19.2 %copy-start = (bf16[512,2048]{1,0:T(8,128)(2,1)S(1)}, bf16[512,2048]{1,0:T(8,128)(2,1)}, u32[]{:S(2)}) copy-start(bf16[512,2048]{1,0:T(8,128)(2,1)} %wa_ref.7) | copy-start | bytes 6291460
  47.7 40.7 %collective-permute-start.5 = (bf16[1024,512]{1,0:T(8,128)(2,1)}, bf16[1024,512]{1,0:T(8,128)(2,1)}, u32[]{:S(2)}, u32[]{:S(2)}) collective-permute-start(bf16[1024,512]{1,0:T(8,128)(2,1)} %collective-permute-done.4.x2), channel_id=1, source_target_pairs={{0,1},{1,0},{2,3},{3,2},{4,5},{5,4},{6,7},{7,6},{8,9},{9,8},{10,11... | collective-permute-start | bytes 3145736 | tf_op jit(solution)/shard_map/ppermute | solution.py:348
  48.0 1.7 copy-start.11
  60.7 21.7 %all-to-all-start.1 = ((bf16[8,272,128]{2,1,0:T(8,128)(2,1)}), bf16[8,272,128]{2,1,0:T(8,128)(2,1)S(1)}, u32[]{:S(2)}, u32[]{:S(2)}) async-start(bf16[8,272,128]{2,1,0:T(8,128)(2,1)} %column_part.2), calls=%async_computation.1 | async-start | bytes 1114112 | tf_op jit(solution)/shard_map/all_to_all | solution.py:352
  66.4 1.9 %collective-permute-start.10 = (bf16[8,64,512]{2,1,0:T(8,128)(2,1)S(1)}, bf16[8,64,512]{2,1,0:T(8,128)(2,1)S(1)}, u32[]{:S(2)}, u32[]{:S(2)}) collective-permute-start(bf16[8,64,512]{2,1,0:T(8,128)(2,1)S(1)} %all-to-all-done.2.x0), channel_id=1, source_target_pairs={{0,1},{1,0},{2,3},{3,2},{4,5},{5,4},{6,7},{7,6},{8,9},{9,8},{10,11... | collective-permute-start | bytes 1572872 | tf_op jit(solution)/shard_map/ppermute | solution.py:348
  66.5 3.6 %collective-permute-start.12 = (bf16[8,64,512]{2,1,0:T(8,128)(2,1)}, bf16[8,64,512]{2,1,0:T(8,128)(2,1)S(1)}, u32[]{:S(2)}, u32[]{:S(2)}) collective-permute-start(bf16[8,64,512]{2,1,0:T(8,128)(2,1)} %collective-permute-done.11.x2), channel_id=1, source_target_pairs={{0,1},{1,0},{2,3},{3,2},{4,5},{5,4},{6,7},{7,6},{8,9},{9,8},{10,11... | collective-permute-start | bytes 1572872 | tf_op jit(solution)/shard_map/ppermute | solution.py:348
  67.0 75.4 %collective-permute-start.8 = (bf16[512,2048]{1,0:T(8,128)(2,1)S(1)}, bf16[512,2048]{1,0:T(8,128)(2,1)}, u32[]{:S(2)}, u32[]{:S(2)}) collective-permute-start(bf16[512,2048]{1,0:T(8,128)(2,1)S(1)} %copy-done), channel_id=1, source_target_pairs={{0,1},{1,0},{2,3},{3,2},{4,5},{5,4},{6,7},{7,6},{8,9},{9,8},{10,11... | collective-permute-start | bytes 6291464 | tf_op jit(solution)/shard_map/ppermute | solution.py:348
  82.4 6.0 %copy-start.5 = (bf16[8,272,128]{2,1,0:T(8,128)(2,1)}, bf16[8,272,128]{2,1,0:T(8,128)(2,1)S(1)}, u32[]{:S(2)}) copy-start(bf16[8,272,128]{2,1,0:T(8,128)(2,1)S(1)} %all-to-all-done.1.col_ref) | copy-start | bytes 1671172
  82.4 52.1 %all-to-all-start.3 = ((bf16[8,272,128]{2,1,0:T(8,128)(2,1)}), bf16[8,272,128]{2,1,0:T(8,128)(2,1)}, u32[]{:S(2)}, u32[]{:S(2)}) async-start(bf16[8,272,128]{2,1,0:T(8,128)(2,1)} %column_part.3), calls=%async_computation.3 | async-start | bytes 1114112 | tf_op jit(solution)/shard_map/all_to_all | solution.py:352
  104.9 15.1 %collective-permute-start.6 = (bf16[512,512]{1,0:T(8,128)(2,1)}, bf16[512,512]{1,0:T(8,128)(2,1)}, u32[]{:S(2)}, u32[]{:S(2)}) collective-permute-start(bf16[512,512]{1,0:T(8,128)(2,1)} %get-tuple-element.21), channel_id=1, source_target_pairs={{0,4},{4,8},{8,12},{12,16},{16,20},{20,24},{24,28},{1,5},{5,9},{9,... | collective-permute-start | bytes 1572872 | tf_op jit(solution)/shard_map/ppermute | solution.py:375
  122.5 7.1 %copy-start.6 = (bf16[8,272,128]{2,1,0:T(8,128)(2,1)S(1)}, bf16[8,272,128]{2,1,0:T(8,128)(2,1)}, u32[]{:S(2)}) copy-start(bf16[8,272,128]{2,1,0:T(8,128)(2,1)} %copy-done.5) | copy-start | bytes 1671172
  129.6 3.5 %copy-start.7 = (f32[1024,128]{1,0:T(8,128)}, f32[1024,128]{1,0:T(8,128)S(1)}, u32[]{:S(2)}) copy-start(f32[1024,128]{1,0:T(8,128)S(1)} %get-tuple-element.23.lse_ref) | copy-start | bytes 1572868
  134.5 7.9 %collective-permute-start.7 = (bf16[2,128,512]{2,1,0:T(8,128)(2,1)S(1)}, bf16[2,128,512]{2,1,0:T(8,128)(2,1)S(1)}, u32[]{:S(2)}, u32[]{:S(2)}) collective-permute-start(bf16[2,128,512]{2,1,0:T(8,128)(2,1)S(1)} %get-tuple-element.25), channel_id=1, source_target_pairs={{0,1},{1,0},{2,3},{3,2},{4,5},{5,4},{6,7},{7,6},{8,9},{9,8},{10,11... | collective-permute-start | bytes 786440 | tf_op jit(solution)/shard_map/ppermute | solution.py:348
  141.8 5.2 %collective-permute-start.13 = (bf16[2,128,512]{2,1,0:T(8,128)(2,1)}, bf16[2,128,512]{2,1,0:T(8,128)(2,1)S(1)}, u32[]{:S(2)}, u32[]{:S(2)}) collective-permute-start(bf16[2,128,512]{2,1,0:T(8,128)(2,1)} %get-tuple-element.28), channel_id=1, source_target_pairs={{0,1},{1,0},{2,3},{3,2},{4,5},{5,4},{6,7},{7,6},{8,9},{9,8},{10,11... | collective-permute-start | bytes 786440 | tf_op jit(solution)/shard_map/ppermute | solution.py:348
  145.6 14.8 %collective-permute-start.9 = (bf16[128,2048]{1,0:T(8,128)(2,1)S(1)}, bf16[128,2048]{1,0:T(8,128)(2,1)S(1)}, u32[]{:S(2)}, u32[]{:S(2)}) collective-permute-start(bf16[128,2048]{1,0:T(8,128)(2,1)S(1)} %out_project.5), channel_id=1, source_target_pairs={{0,2},{1,3},{2,0},{3,1},{4,6},{5,7},{6,4},{7,5},{8,10},{9,11},{10,... | collective-permute-start | bytes 1572872 | tf_op jit(solution)/shard_map/ppermute | solution.py:348
  150.3 20.5 %collective-permute-start.14 = (bf16[128,2048]{1,0:T(8,128)(2,1)S(1)}, bf16[128,2048]{1,0:T(8,128)(2,1)S(1)}, u32[]{:S(2)}, u32[]{:S(2)}) collective-permute-start(bf16[128,2048]{1,0:T(8,128)(2,1)S(1)} %out_project.7), channel_id=1, source_target_pairs={{0,2},{1,3},{2,0},{3,1},{4,6},{5,7},{6,4},{7,5},{8,10},{9,11},{10,... | collective-permute-start | bytes 1572872 | tf_op jit(solution)/shard_map/ppermute | solution.py:348
  (15 other events, 21.1 us)

commit v2 on v1

--- a/solution.py
+++ b/solution.py
@@ -20,12 +20,15 @@
 BF16 = jnp.bfloat16
 
 
-def params(mib, **kw):
-    return pltpu.CompilerParams(vmem_limit_bytes=mib * MIB, **kw)
-
-
-def cost(flops, moved, exps=0):
-    return pl.CostEstimate(flops=flops, bytes_accessed=moved, transcendentals=exps)
+ANYWHERE = pl.BlockSpec(memory_space=pl.ANY)
+
+
+def params():
+    return pltpu.CompilerParams(vmem_limit_bytes=56 * MIB)
+
+
+def cost():
+    return pl.CostEstimate(flops=0, bytes_accessed=MIB, transcendentals=0)
 
 
 def dot(a, b):
@@ -34,6 +37,10 @@
 
 def dot_t(a, b):
     return lax.dot_general(a, b, (((1,), (1,)), ((), ())), preferred_element_type=F32)
+
+
+def dot_l(a, b):
+    return lax.dot_general(a, b, (((0,), (0,)), ((), ())), preferred_element_type=F32)
 
 
 def pack_kernel(tok_ref, *out_refs):
@@ -58,13 +65,13 @@
     return pl.pallas_call(
         pack_kernel,
         out_shape=[jax.ShapeDtypeStruct((owners, message, width), BF16)] * CHUNKS,
-        compiler_params=params(16),
-        cost_estimate=cost(0, 2 * tokens.size * 2),
+        compiler_params=params(),
+        cost_estimate=cost(),
         name="pack_tokens",
     )(tokens)
 
 
-def project_kernel(order_ref, x0, x1, x2, x3, wq, wk, wv, q_ref, k_ref, v_ref, halo_ref):
+def project_kernel(order_ref, x0, x1, x2, x3, wq, wk, wv, after, q_ref, k_ref, v_ref, halo_ref):
     for n, (w_ref, out_ref) in enumerate(((wq, q_ref), (wk, k_ref), (wv, v_ref))):
         total = None
         for p, x_ref in enumerate((x0, x1, x2, x3)):
@@ -77,82 +84,103 @@
             halo_ref[(n - 1) * STRIDE : n * STRIDE, :] = total[-STRIDE:]
 
 
-def project(order, pieces, weights):
+def project(order, pieces, weights, after):
     rows, width = pieces[0].shape
-    tile = 512
-    full = lambda m, s: (0, 0)
-    tiled = lambda m, s: (m, 0)
+    tile = 256
+    full = lambda n, s: (0, 0)
+    tiled = lambda n, s: (0, n)
     return pl.pallas_call(
         project_kernel,
         grid_spec=pltpu.PrefetchScalarGridSpec(
             num_scalar_prefetch=1,
-            grid=(rows // tile,),
-            in_specs=[pl.BlockSpec((tile, width), tiled)] * 4
-            + [pl.BlockSpec(weights[0].shape, full)] * 3,
-            out_specs=[pl.BlockSpec((tile, width), tiled)] * 3
-            + [pl.BlockSpec((2 * STRIDE, width), full)],
+            grid=(width // tile,),
+            in_specs=[pl.BlockSpec((rows, width), full)] * 4
+            + [pl.BlockSpec((weights[0].shape[0], tile), tiled)] * 3
+            + [ANYWHERE],
+            out_specs=[pl.BlockSpec((rows, tile), tiled)] * 3
+            + [pl.BlockSpec((2 * STRIDE, tile), tiled)],
         ),
         out_shape=[jax.ShapeDtypeStruct((rows, width), BF16)] * 3
         + [jax.ShapeDtypeStruct((2 * STRIDE, width), BF16)],
-        compiler_params=params(32),
-        cost_estimate=cost(2 * rows * 2048 * 3 * width, 14 * MIB),
+        compiler_params=params(),
+        cost_estimate=cost(),
         name="project_block",
-    )(order, *pieces, *weights)
-
-
-def local_kernel(pos_ref, q_ref, k_ref, v_ref, kp_ref, vp_ref, halo_ref, out_ref, lse_ref):
+    )(order, *pieces, *weights, after)
+
+
+def softmax_columns(s):
+    m = jnp.maximum(jnp.max(s, 0, keepdims=True), FLOOR)
+    p = jnp.exp2((s - m) * SCALE2)
+    total = jnp.maximum(jnp.sum(p, 0, keepdims=True), 1.0)
+    return p, total, m * SCALE2 + jnp.log2(total)
+
+
+def local_kernel(pos_ref, q_ref, k_ref, v_ref, kp_ref, vp_ref, halo_ref, after, *outs):
+    out_refs, lse_refs = outs[:CHUNKS], outs[CHUNKS:]
+    owners, groups = out_refs[0].shape[:2]
     r = pl.program_id(0)
     first = r == 0
     no_prev = jnp.logical_and(first, pos_ref[0] == 0)
-    t = lax.broadcasted_iota(jnp.int32, (STRIDE, STRIDE), 0)
-    u = lax.broadcasted_iota(jnp.int32, (STRIDE, STRIDE), 1)
+    u = lax.broadcasted_iota(jnp.int32, (STRIDE, STRIDE), 0)
+    t = lax.broadcasted_iota(jnp.int32, (STRIDE, STRIDE), 1)
     current = u <= t
-    lane = lax.broadcasted_iota(jnp.int32, (STRIDE, 128), 1)
     low = jnp.where(no_prev, -1e30, 0.0).astype(F32)
-    lses = jnp.zeros((STRIDE, 128), F32)
+
+    def spots():
+        for d in range(owners):
+            for i in range(CHUNKS):
+                for g in range(groups):
+                    at = ((d * CHUNKS + i) * groups + g) * SUB
+                    yield d, i, g, slice(at, at + SUB)
+
+    lses = []
     for h in range(HEADS):
         cols = slice(h * DH, (h + 1) * DH)
         q = q_ref[:, cols]
         k_prev = jnp.where(first, halo_ref[:STRIDE, cols], kp_ref[:, cols])
         v_prev = jnp.where(first, halo_ref[STRIDE:, cols], vp_ref[:, cols])
-        s = jnp.where(current, dot_t(q, k_ref[:, cols]), dot_t(q, k_prev) + low)
-        m = jnp.max(s, -1, keepdims=True)
-        p = jnp.exp2((s - m) * SCALE2)
-        total = jnp.sum(p, -1, keepdims=True)
+        s = jnp.where(current, dot_t(k_ref[:, cols], q), dot_t(k_prev, q) + low)
+        p, total, lse = softmax_columns(s)
         p_now = jnp.where(current, p, 0.0).astype(BF16)
         p_prev = jnp.where(current, 0.0, p).astype(BF16)
-        o = dot(p_now, v_ref[:, cols]) + dot(p_prev, v_prev)
-        out_ref[:, cols] = o / total
-        lses = jnp.where(lane == h, m * SCALE2 + jnp.log2(total), lses)
-    lse_ref[...] = lses
-
-
-def local_part(pos, q, k, v, halo):
+        o = dot_l(v_ref[:, cols], p_now) + dot_l(v_prev, p_prev)
+        o = (o / total).T
+        lses.append(lse)
+        for d, i, g, at in spots():
+            out_refs[i][d, g, r, :, cols] = o[at]
+    lses.append(jnp.zeros((128 - HEADS, STRIDE), F32))
+    turned = jnp.concatenate(lses, 0).T
+    for d, i, g, at in spots():
+        lse_refs[i][d, g, r] = turned[at]
+
+
+def local_part(pos, q, k, v, halo, owners, after):
     rows, width = q.shape
     tile = lambda r, s: (r, 0)
     back = lambda r, s: (jnp.maximum(r - 1, 0), 0)
     block = (STRIDE, width)
-    return pl.pallas_call(
+    lead = (owners, STRIDE // owners // SUB // CHUNKS, ROWS, SUB)
+    shapes = [lead + (width,)] * CHUNKS + [lead + (128,)] * CHUNKS
+    outs = pl.pallas_call(
         local_kernel,
         grid_spec=pltpu.PrefetchScalarGridSpec(
             num_scalar_prefetch=1,
             grid=(rows // STRIDE,),
             in_specs=[pl.BlockSpec(block, tile)] * 3
             + [pl.BlockSpec(block, back)] * 2
-            + [pl.BlockSpec((2 * STRIDE, width), lambda r, s: (0, 0))],
-            out_specs=[pl.BlockSpec(block, tile), pl.BlockSpec((STRIDE, 128), tile)],
+            + [pl.BlockSpec((2 * STRIDE, width), lambda r, s: (0, 0)), ANYWHERE],
+            out_specs=[pl.BlockSpec(shape, lambda r, s: (0, 0, 0, 0, 0)) for shape in shapes],
         ),
-        out_shape=[
-            jax.ShapeDtypeStruct((rows, width), F32),
-            jax.ShapeDtypeStruct((rows, 128), F32),
-        ],
-        compiler_params=params(24),
-        cost_estimate=cost(8 * rows * STRIDE * width, 8 * MIB, rows * STRIDE * HEADS),
+        out_shape=[jax.ShapeDtypeStruct(shape, F32) for shape in shapes],
+        compiler_params=params(),
+        cost_estimate=cost(),
         name="local_part",
-    )(pos, q, k, v, k, v, halo)
-
-
-def column_kernel(order_ref, x0, x1, x2, x3, wq, wk, wv, out_ref, aq, ak, av):
+    )(pos, q, k, v, k, v, halo, after)
+    outs = [x.reshape(owners, -1, x.shape[-1]) for x in outs]
+    return list(zip(outs[:CHUNKS], outs[CHUNKS:]))
+
+
+def column_kernel(order_ref, x0, x1, x2, x3, wq, wk, wv, after, out_ref, aq, ak, av):
     step = pl.program_id(0)
     owners, message, width = x0.shape
     groups = message // (ROWS * SUB)
@@ -167,37 +195,28 @@
 
     @pl.when(step == 3)
     def _():
-        size = owners * ROWS * SUB
-        i = lax.broadcasted_iota(jnp.int32, (size, size), 0)
-        j = lax.broadcasted_iota(jnp.int32, (size, size), 1)
+        part = ROWS * SUB
+        size = owners * part
+        j = lax.broadcasted_iota(jnp.int32, (size, size), 0)
+        i = lax.broadcasted_iota(jnp.int32, (size, size), 1)
         earlier = jnp.logical_and(i % SUB == j % SUB, i > j)
-        part = ROWS * SUB
-        lane = lax.broadcasted_iota(jnp.int32, (part, 128), 1)
         stats = []
         for g in range(groups):
             at = slice(g * part, (g + 1) * part)
-            stat = jnp.zeros((part, 128), F32)
+            lses = []
             for h in range(HEADS):
                 cols = slice(h * DH, (h + 1) * DH)
                 q, k, v = (a[:, at, cols].reshape(size, DH).astype(BF16) for a in (aq, ak, av))
-                s = jnp.where(earlier, dot_t(q, k), -1e30)
-                m = jnp.maximum(jnp.max(s, -1, keepdims=True), FLOOR)
-                e = jnp.exp2((s - m) * SCALE2)
-                total = jnp.maximum(jnp.sum(e, -1, keepdims=True), 1.0)
-                o = dot(e.astype(BF16), v) / total
+                p, total, lse = softmax_columns(jnp.where(earlier, dot_t(k, q), -1e30))
+                o = (dot_l(v, p.astype(BF16)) / total).T
                 rows = slice(h * message + g * part, h * message + (g + 1) * part)
                 out_ref[:, rows, :] = o.astype(BF16).reshape(owners, part, DH)
-                lse = (m * SCALE2 + jnp.log2(total)).reshape(owners, part, 1)
-                for d in range(owners):
-                    mine = jnp.logical_and(lane // 8 == d, lane % 4 == h)
-                    stat = jnp.where(mine, lse[d], stat)
-            stats.append(stat)
-        if message < 128:
-            stats.append(jnp.zeros((128 - message, 128), F32))
-        turned = jnp.concatenate(stats, 0).T
-        upper = lax.broadcasted_iota(jnp.int32, (8, 128), 0) < 4
+                lses.append(lse)
+            stats.append(jnp.concatenate(lses + lses, 0))
+        upper = lax.broadcasted_iota(jnp.int32, (8, 128), 0) < HEADS
+        blank = [jnp.zeros((8, 128 - message), F32)] if message < 128 else []
         for d in range(owners):
-            x = turned[8 * d : 8 * d + 8]
+            x = jnp.concatenate([s[:, d * part : (d + 1) * part] for s in stats] + blank, 1)
             hi = x.astype(BF16).astype(F32)
             mid = (x - hi).astype(BF16).astype(F32)
             lo = x - hi - mid
@@ -205,33 +224,31 @@
             out_ref[d, HEADS * message : HEADS * message + 16, :] = tail.astype(BF16)
 
 
-def column_part(order, pieces, weights):
+def column_part(order, pieces, weights, after):
     owners, message, width = pieces[0].shape
     rows_out = HEADS * message + 16
     whole = lambda p, s: (0, 0, 0)
-    tokens = owners * message
     return pl.pallas_call(
         column_kernel,
         grid_spec=pltpu.PrefetchScalarGridSpec(
             num_scalar_prefetch=1,
             grid=(4,),
             in_specs=[pl.BlockSpec(pieces[0].shape, whole)] * 4
-            + [pl.BlockSpec((512, width), lambda p, s: (s[p], 0))] * 3,
+            + [pl.BlockSpec((512, width), lambda p, s: (s[p], 0))] * 3
+            + [ANYWHERE],
             out_specs=pl.BlockSpec((owners, rows_out, DH), whole),
             scratch_shapes=[pltpu.VMEM((owners, message, width), F32)] * 3,
         ),
         out_shape=jax.ShapeDtypeStruct((owners, rows_out, DH), BF16),
-        compiler_params=params(32),
-        cost_estimate=cost(2 * tokens * 2048 * 3 * width, 10 * MIB, tokens * 256 * HEADS),
+        compiler_params=params(),
+        cost_estimate=cost(),
         name="column_part",
-    )(order, *pieces, *weights)
-
-
-def mix_kernel(chunk, pos_ref, col_ref, loc_ref, lse_ref, own_ref, send_ref, mixed):
-    owners = col_ref.shape[0]
-    message = (col_ref.shape[1] - 16) // HEADS
+    )(order, *pieces, *weights, after)
+
+
+def mix_kernel(pos_ref, col_ref, loc_ref, lse_ref, after, own_ref, send_ref, mixed):
+    owners, message, _ = loc_ref.shape
     groups = message // (ROWS * SUB)
-    per_owner = STRIDE // owners
     base = HEADS * message
     tiles = []
     for d in range(owners):
@@ -239,29 +256,21 @@
         tiles.append(tail[:8] + tail[8:])
     tiles.append(jnp.zeros((128 - 8 * owners, 128), F32))
     turned = jnp.concatenate(tiles, 0).T[:message]
+    span = groups * SUB
     for d in range(owners):
-        spots = [
-            r * STRIDE + d * per_owner + (chunk * groups + g) * SUB
-            for g in range(groups)
-            for r in range(ROWS)
-        ]
-        local_lse = jnp.concatenate([lse_ref[s : s + SUB, :] for s in spots], 0)
         for h in range(HEADS):
             cols = slice(h * DH, (h + 1) * DH)
             col = col_ref[d, h * message : (h + 1) * message, :].astype(F32)
-            loc = jnp.concatenate([loc_ref[s : s + SUB, cols] for s in spots], 0)
             at = 8 * d + h
             col_lse = turned[:, at : at + 1] + turned[:, at + 4 : at + 5]
-            loc_lse = local_lse[:, h : h + 1]
+            loc_lse = lse_ref[d, :, h : h + 1]
             top = jnp.maximum(col_lse, loc_lse)
             w_col = jnp.exp2(col_lse - top)
             w_loc = jnp.exp2(loc_lse - top)
-            both = (loc * w_loc + col * w_col) / (w_loc + w_col)
+            both = (loc_ref[d, :, cols] * w_loc + col * w_col) / (w_loc + w_col)
             for r in range(ROWS):
-                piece = jnp.concatenate(
-                    [both[(g * ROWS + r) * SUB : (g * ROWS + r + 1) * SUB] for g in range(groups)], 0
-                )
-                span = groups * SUB
+                starts = [(g * ROWS + r) * SUB for g in range(groups)]
+                piece = jnp.concatenate([both[s : s + SUB] for s in starts], 0)
                 mixed[r, d * span : (d + 1) * span, cols] = piece.astype(BF16)
     core = pos_ref[1]
     for x in range(2):
@@ -269,34 +278,37 @@
         send_ref[x] = mixed[2 * x + 1 - core]
 
 
-def mix(pos, chunk, column, local, lse):
-    owners = column.shape[0]
-    message = (column.shape[1] - 16) // HEADS
+def mix(pos, column, local, lse, after):
+    owners, message, width = local.shape
     tokens = owners * message // ROWS
-    width = local.shape[1]
     vmem = pl.BlockSpec(memory_space=pltpu.VMEM)
     return pl.pallas_call(
-        functools.partial(mix_kernel, chunk),
-        in_specs=[pl.BlockSpec(memory_space=pltpu.SMEM), vmem, vmem, vmem],
+        mix_kernel,
+        in_specs=[pl.BlockSpec(memory_space=pltpu.SMEM), vmem, vmem, vmem, ANYWHERE],
         out_specs=[vmem, vmem],
         out_shape=[jax.ShapeDtypeStruct((2, tokens, width), BF16)] * 2,
         scratch_shapes=[pltpu.VMEM((ROWS, tokens, width), BF16)],
-        compiler_params=params(16),
-        cost_estimate=cost(8 * tokens * ROWS * width, 4 * MIB),
+        compiler_params=params(),
+        cost_estimate=cost(),
         name="mix",
-    )(pos, column, local, lse)
-
-
-def out_kernel(which_ref, a_ref, b_ref, wa_ref, wb_ref, out_ref):
-    total = dot(a_ref[0], wa_ref[...]) + dot(b_ref[0], wb_ref[...])
-    out_ref[...] = total.astype(out_ref.dtype)
-
-
-def out_project(which, own, other, w_own, w_other, dtype):
+    )(pos, column, local, lse, after)
+
+
+def out_kernel(pos_ref, a_ref, b_ref, wa_ref, wb_ref, send_ref, keep_ref):
+    tokens = send_ref.shape[0]
+    a = a_ref[...].reshape(2 * tokens, -1)
+    b = b_ref[...].reshape(2 * tokens, -1)
+    total = dot(a, wa_ref[...]) + dot(b, wb_ref[...])
+    low_side = pos_ref[2] == 0
+    send_ref[...] = jnp.where(low_side, total[tokens:], total[:tokens]).astype(BF16)
+    keep_ref[...] = jnp.where(low_side, total[:tokens], total[tokens:])
+
+
+def out_project(pos, own, other, w_own, w_other):
     _, tokens, width = own.shape
     columns = w_own.shape[1]
     tile = 512
-    rows = pl.BlockSpec((1, tokens, width), lambda n, s: (s[0], 0, 0))
+    rows = pl.BlockSpec((2, tokens, width), lambda n, s: (0, 0, 0))
     cols = pl.BlockSpec((width, tile), lambda n, s: (0, n))
     return pl.pallas_call(
         out_kernel,
@@ -304,13 +316,16 @@
             num_scalar_prefetch=1,
             grid=(columns // tile,),
             in_specs=[rows, rows, cols, cols],
-            out_specs=pl.BlockSpec((tokens, tile), lambda n, s: (0, n)),
+            out_specs=[pl.BlockSpec((tokens, tile), lambda n, s: (0, n))] * 2,
         ),
-        out_shape=jax.ShapeDtypeStruct((tokens, columns), dtype),
-        compiler_params=params(16),
-        cost_estimate=cost(4 * tokens * width * columns, 5 * MIB),
+        out_shape=[
+            jax.ShapeDtypeStruct((tokens, columns), BF16),
+            jax.ShapeDtypeStruct((tokens, columns), F32),
+        ],
+        compiler_params=params(),
+        cost_estimate=cost(),
         name="out_project",
-    )(which, own, other, w_own, w_other)
+    )(pos, own, other, w_own, w_other)
 
 
 def join_kernel(*refs):
@@ -338,8 +353,8 @@
         in_specs=[spec] * (2 * len(pairs)),
         out_specs=pl.BlockSpec((STRIDE, tile), lambda n: (0, n)),
         out_shape=jax.ShapeDtypeStruct((STRIDE, columns), BF16),
-        compiler_params=params(16),
-        cost_estimate=cost(STRIDE * columns, 4 * MIB),
+        compiler_params=params(),
+        cost_estimate=cost(),
         name="join",
     )(*[x for pair in pairs for x in pair])
 
@@ -363,26 +378,25 @@
     block = lax.axis_index("seq")
     weights = (w_query, w_key, w_value)
     order = jnp.bitwise_xor(jnp.arange(4, dtype=jnp.int32), head.astype(jnp.int32))
-    pos = jnp.stack([block, head % 2]).astype(jnp.int32)
-    side = (head // 2).astype(jnp.int32).reshape(1)
-
-    messages = pack(tokens, owners)
+    pos = jnp.stack([block, head % 2, head // 2]).astype(jnp.int32)
+
     block_pieces = gather(tokens)
+    classes = [exchange(m) for m in pack(tokens, owners)]
     w_other = swap(w_out, 1)
-    classes = [exchange(m) for m in messages]
-    q, k, v, halo = project(order, block_pieces, weights)
-    peers = owners
-    halo = lax.ppermute(halo, "seq", [(i, i + 1) for i in range(peers - 1)])
-    local, lse = local_part(pos, q, k, v, halo)
-    columns = [exchange(column_part(order, gather(c), weights)) for c in classes]
-    pairs = []
-    for i, column in enumerate(columns):
-        own, send = mix(pos, i, column, local, lse)
-        other = swap(send, 1)
-        out = out_project(1 - side, own, other, w_out, w_other, BF16)
-        got = swap(out, 2)
-        keep = out_project(side, own, other, w_out, w_other, F32)
-        pairs.append((keep, got))
+    q, k, v, halo = project(order, block_pieces, weights, classes[0])
+    halo = lax.ppermute(halo, "seq", [(i, i + 1) for i in range(owners - 1)])
+    columns, after = [], q
+    for i, c in enumerate(classes):
+        columns.append(column_part(order, gather(c), weights, after))
+        if i == 0:
+            locals_ = local_part(pos, q, k, v, halo, owners, columns[0])
+            after = locals_[-1][-1]
+    pairs, after = [], columns[-1]
+    for column, (local, lse) in zip(columns, locals_):
+        own, send = mix(pos, exchange(column), local, lse, after)
+        out, keep = out_project(pos, own, swap(send, 1), w_out, w_other)
+        after = keep
+        pairs.append((keep, swap(out, 2)))
     return join(pairs)
 
 

time: 174 us -> 185 us (1.063)
  Pallas kernels: 57.5 us -> 79.4 us
  local copies, waits for them, and re-layouts: 22.8 us -> 3.06 us
  starting transfers between devices: 35.6 us -> 40.9 us
  waiting for transfers between devices: 56.3 us -> 59.3 us
    unnamed x40 -> x20, local copies, waits for them, and re-layouts: 22.8 us -> 3.06 us
    pallas_call x2, Pallas kernels: 8.18 us -> 18.5 us  [mix(): pl.pallas_call(mix_kernel, in_specs=[pl.BlockSpec(memory_space=pltpu.SMEM...]
    ppermute x14, waiting for transfers between devices: 33 us -> 39.9 us  [swap(): return lax.ppermute(value, 'head', [(i, i ^ distance) for i in range(4)])]
    all_to_all x4, waiting for transfers between devices: 13 us -> 7.51 us  [exchange(): return lax.all_to_all(value, 'seq', split_axis=0, concat_axis=0, tiled=True)]
    pallas_call x2, Pallas kernels: 15.4 us -> 20.8 us  [column_part(): pl.pallas_call(column_kernel, grid_spec=pltpu.PrefetchScalarGridSpec(num_...]
    all_to_all x4, starting transfers between devices: 22.6 us -> 26.7 us  [exchange(): return lax.all_to_all(value, 'seq', split_axis=0, concat_axis=0, tiled=True)]
    pallas_call x1, Pallas kernels: 7.12 us -> 10.4 us  [local_part(): pl.pallas_call(local_kernel, grid_spec=pltpu.PrefetchScalarGridSpec(num_s...]
    pallas_call x1, Pallas kernels: 9.75 us -> 12.1 us  [project(): pl.pallas_call(project_kernel, grid_spec=pltpu.PrefetchScalarGridSpec(num...]
  transfers between devices with their start and end apart: 19 -> 19, of which waited for: 8 -> 8; matrix products, arithmetic and copies ran while one was open for 0% -> 1% of each run, Pallas kernels for 31% -> 36%
where the time goes in v2:
time: 185 us; the launch traced here: 184 us
  Pallas kernels  79.4 us (43%)
  waiting for transfers between devices  59.3 us (32%)
  starting transfers between devices  40.9 us (22%)
  local copies, waits for them, and re-layouts  3.06 us (2%)
    ppermute x14, waiting for transfers between devices, swap(): return lax.ppermute(value, 'head', [(i, i ^ distance) for i in range(4)])  39.9 us
    all_to_all x4, starting transfers between devices, exchange(): return lax.all_to_all(value, 'seq', split_axis=0, concat_axis=0, tiled=True)  26.7 us
    pallas_call x2, Pallas kernels, column_part(): pl.pallas_call(column_kernel, grid_spec=pltpu.PrefetchScalarGridSpec(num_...  20.8 us
    pallas_call x2, Pallas kernels, mix(): pl.pallas_call(mix_kernel, in_specs=[pl.BlockSpec(memory_space=pltpu.SMEM...  18.5 us
    pallas_call x1, Pallas kernels, project(): pl.pallas_call(project_kernel, grid_spec=pltpu.PrefetchScalarGridSpec(num...  12.1 us
    ppermute x1, waiting for transfers between devices, chunked(): halo = lax.ppermute(halo, 'seq', [(i, i + 1) for i in range(owners - 1)])  11.9 us
    pallas_call x2, Pallas kernels, out_project(): pl.pallas_call(out_kernel, grid_spec=pltpu.PrefetchScalarGridSpec(num_sca...  11.5 us
    pallas_call x1, Pallas kernels, local_part(): pl.pallas_call(local_kernel, grid_spec=pltpu.PrefetchScalarGridSpec(num_s...  10.4 us
  transfers between devices with their start and end apart: 19, of which 8 were waited for; matrix products, arithmetic and copies ran while one was open for 1% of the time, Pallas kernels for 36%

profile of v2, /device:TPU:0, one launch (start us, length us, event | category | flops | bytes accessed | tf_op | source)
XLA Modules:
  0.0 183.9 jit_solution(6813560160102025092)
XLA Ops:
  0.0 2.9 %collective-permute-start.4 = (bf16[1024,512]{1,0:T(8,128)(2,1)}, bf16[1024,512]{1,0:T(8,128)(2,1)}, u32[]{:S(2)}, u32[]{:S(2)}) collective-permute-start(bf16[1024,512]{1,0:T(8,128)(2,1)} %x0.1), channel_id=1, source_target_pairs={{0,2},{1,3},{2,0},{3,1},{4,6},{5,7},{6,4},{7,5},{8,10},{9,11},{10,... | collective-permute-start | bytes 3145736 | tf_op jit(solution)/shard_map/ppermute | solution.py:363
  2.9 2.3 %pack_tokens.1 = (bf16[8,64,512]{2,1,0:T(8,128)(2,1)}, bf16[8,64,512]{2,1,0:T(8,128)(2,1)}) custom-call(bf16[1024,512]{1,0:T(8,128)(2,1)} %x0.1), custom_call_target="tpu_custom_call" | custom-call | bytes 1048576 | tf_op jit(solution)/shard_map/pack_tokens/pallas_call | solution.py:65
  5.3 5.8 %all-to-all-start = ((bf16[8,64,512]{2,1,0:T(8,128)(2,1)}), bf16[8,64,512]{2,1,0:T(8,128)(2,1)S(1)}, u32[]{:S(2)}, u32[]{:S(2)}) async-start(bf16[8,64,512]{2,1,0:T(8,128)(2,1)} %get-tuple-element.23), calls=%async_computation | async-start | bytes 1048576 | tf_op jit(solution)/shard_map/all_to_all | solution.py:367
  11.1 15.3 %collective-permute-done.4.x2 = bf16[1024,512]{1,0:T(8,128)(2,1)} collective-permute-done((bf16[1024,512]{1,0:T(8,128)(2,1)}, bf16[1024,512]{1,0:T(8,128)(2,1)}, u32[]{:S(2)}, u32[]{:S(2)}) %collective-permute-start.4) | collective-permute-done | bytes 1048608 | tf_op jit(solution)/shard_map/ppermute | solution.py:363
  26.4 1.8 collective-permute-start.1
  28.2 5.8 %all-to-all-start.2 = ((bf16[8,64,512]{2,1,0:T(8,128)(2,1)}), bf16[8,64,512]{2,1,0:T(8,128)(2,1)S(1)}, u32[]{:S(2)}, u32[]{:S(2)}) async-start(bf16[8,64,512]{2,1,0:T(8,128)(2,1)} %get-tuple-element.30), calls=%async_computation.2 | async-start | bytes 1048576 | tf_op jit(solution)/shard_map/all_to_all | solution.py:367
  34.1 6.8 %collective-permute-done.1.x2 = bf16[8,64,512]{2,1,0:T(8,128)(2,1)} collective-permute-done((bf16[8,64,512]{2,1,0:T(8,128)(2,1)S(1)}, bf16[8,64,512]{2,1,0:T(8,128)(2,1)}, u32[]{:S(2)}, u32[]{:S(2)}) %collective-permute-start.1) | collective-permute-done | bytes 524320 | tf_op jit(solution)/shard_map/ppermute | solution.py:363
  41.4 7.5 %all-to-all-done.2.x0 = bf16[8,64,512]{2,1,0:T(8,128)(2,1)S(1)} async-done(((bf16[8,64,512]{2,1,0:T(8,128)(2,1)}), bf16[8,64,512]{2,1,0:T(8,128)(2,1)S(1)}, u32[]{:S(2)}, u32[]{:S(2)}) %all-to-all-start.2) | async-done | bytes 524320 | tf_op jit(solution)/shard_map/all_to_all | solution.py:367
  50.0 12.1 %project_block.1 = (bf16[1024,512]{1,0:T(8,128)(2,1)}, bf16[1024,512]{1,0:T(8,128)(2,1)}, bf16[1024,512]{1,0:T(8,128)(2,1)}, bf16[512,512]{1,0:T(8,128)(2,1)}) custom-call(s32[4]{0:T(128)} %iota_xor_fusion.order_ref, bf16[1024,512]{1,0:T(8,128)(2,1)} %x0.1, bf16[1024,512]{1,0:T(8,128)(2,1)} %collective-permute-done.3.x1, ...), custom_call_target="tpu_custom_call" | custom-call | bytes 1048576 | tf_op jit(solution)/shard_map/project_block/pallas_call | solution.py:92
  62.1 10.4 %column_part.2.after = bf16[8,272,128]{2,1,0:T(8,128)(2,1)} custom-call(s32[4]{0:T(128)} %iota_xor_fusion.order_ref, bf16[8,64,512]{2,1,0:T(8,128)(2,1)} %copy-done.1, bf16[8,64,512]{2,1,0:T(8,128)(2,1)} %collective-permute-done.x1, bf16[8,64,512]{2,1,0:T(8,128)(2,1)} %collective-permute-done.1.x2, bf16[8,64,512]{2,1,0:T(8,128)(2,1)} %collective-permute-done.2.x3, ...), custom_call_target="tpu_custom_call" | custom-call | bytes 1048576 | tf_op jit(solution)/shard_map/column_part/pallas_call | solution.py:231
  72.5 3.6 %all-to-all-start.1 = ((bf16[8,272,128]{2,1,0:T(8,128)(2,1)}), bf16[8,272,128]{2,1,0:T(8,128)(2,1)S(1)}, u32[]{:S(2)}, u32[]{:S(2)}) async-start(bf16[8,272,128]{2,1,0:T(8,128)(2,1)} %column_part.2.after), calls=%async_computation.1 | async-start | bytes 1114112 | tf_op jit(solution)/shard_map/all_to_all | solution.py:367
  76.1 4.7 %collective-permute-start.6 = (bf16[512,512]{1,0:T(8,128)(2,1)}, bf16[512,512]{1,0:T(8,128)(2,1)}, u32[]{:S(2)}, u32[]{:S(2)}) collective-permute-start(bf16[512,512]{1,0:T(8,128)(2,1)} %get-tuple-element.27), channel_id=1, source_target_pairs={{0,4},{4,8},{8,12},{12,16},{16,20},{20,24},{24,28},{1,5},{5,9},{9,... | collective-permute-start | bytes 1572872 | tf_op jit(solution)/shard_map/ppermute | solution.py:387
  82.0 11.9 %collective-permute-done.6.halo_ref = bf16[512,512]{1,0:T(8,128)(2,1)} collective-permute-done((bf16[512,512]{1,0:T(8,128)(2,1)}, bf16[512,512]{1,0:T(8,128)(2,1)}, u32[]{:S(2)}, u32[]{:S(2)}) %collective-permute-start.6) | collective-permute-done | bytes 524320 | tf_op jit(solution)/shard_map/ppermute | solution.py:387
  93.9 10.4 %local_part.1 = (f32[8,2,4,8,512]{4,3,2,1,0:T(8,128)}, f32[8,2,4,8,512]{4,3,2,1,0:T(8,128)}, f32[8,2,4,8,128]{4,3,2,1,0:T(8,128)}, f32[8,2,4,8,128]{4,3,2,1,0:T(8,128)}) custom-call(s32[3]{0:T(128)} %pad_add_fusion.pos_ref, bf16[1024,512]{1,0:T(8,128)(2,1)} %get-tuple-element.24.after.q_ref, bf16[1024,512]{1,0:T(8,128)(2,1)} %get-tuple-element.25.k_ref.kp_ref, ...), custom_call_target="tpu_custom_call" | custom-call | bytes 1048576 | tf_op jit(solution)/shard_map/local_part/pallas_call | solution.py:164
  104.3 10.4 %column_part.3.after = bf16[8,272,128]{2,1,0:T(8,128)(2,1)} custom-call(s32[4]{0:T(128)} %iota_xor_fusion.order_ref, bf16[8,64,512]{2,1,0:T(8,128)(2,1)} %copy-done.4, bf16[8,64,512]{2,1,0:T(8,128)(2,1)} %collective-permute-done.7.x1, bf16[8,64,512]{2,1,0:T(8,128)(2,1)} %collective-permute-done.8.x2, bf16[8,64,512]{2,1,0:T(8,128)(2,1)} %collective-permute-done.9.x3, ...), custom_call_target="tpu_custom_call" | custom-call | bytes 1048576 | tf_op jit(solution)/shard_map/column_part/pallas_call | solution.py:231
  114.7 11.4 %all-to-all-start.3 = ((bf16[8,272,128]{2,1,0:T(8,128)(2,1)}), bf16[8,272,128]{2,1,0:T(8,128)(2,1)S(1)}, u32[]{:S(2)}, u32[]{:S(2)}) async-start(bf16[8,272,128]{2,1,0:T(8,128)(2,1)} %column_part.3.after), calls=%async_computation.3 | async-start | bytes 1114112 | tf_op jit(solution)/shard_map/all_to_all | solution.py:367
  126.1 9.2 %mix.2 = (bf16[2,128,512]{2,1,0:T(8,128)(2,1)}, bf16[2,128,512]{2,1,0:T(8,128)(2,1)}) custom-call(s32[3]{0:T(128)} %pad_add_fusion.pos_ref, bf16[8,272,128]{2,1,0:T(8,128)(2,1)} %copy-done.2, f32[8,64,512]{2,1,0:T(8,128)} %bitcast.10, f32[8,64,128]{2,1,0:T(8,128)} %bitcast.11, bf16[8,272,128]{2,1,0:T(8,128)(2,1)} %column_part.3.after), custom_call_target="tpu_custom_call" | custom-call | bytes 1048576 | tf_op jit(solution)/shard_map/mix/pallas_call | solution.py:285
  135.4 1.7 collective-permute-done.10.b_ref
  137.8 5.8 %out_project.2 = (bf16[128,2048]{1,0:T(8,128)(2,1)}, f32[128,2048]{1,0:T(8,128)}) custom-call(s32[3]{0:T(128)} %pad_add_fusion.pos_ref, bf16[2,128,512]{2,1,0:T(8,128)(2,1)} %get-tuple-element.32.a_ref, bf16[2,128,512]{2,1,0:T(8,128)(2,1)} %copy-done.8, bf16[512,2048]{1,0:T(8,128)(2,1)} %wa_ref.3, bf16[512,2048]{1,0:T(8,128)(2,1)} %collective-permute-done.11.wb_ref), custom_call_target="tpu_custom_call" | custom-call | bytes 1048576 | tf_op jit(solution)/shard_map/out_project/pallas_call | solution.py:313
  144.5 9.3 %mix.3 = (bf16[2,128,512]{2,1,0:T(8,128)(2,1)}, bf16[2,128,512]{2,1,0:T(8,128)(2,1)}) custom-call(s32[3]{0:T(128)} %pad_add_fusion.pos_ref, bf16[8,272,128]{2,1,0:T(8,128)(2,1)} %copy-done.3, f32[8,64,512]{2,1,0:T(8,128)} %bitcast.7, f32[8,64,128]{2,1,0:T(8,128)} %bitcast.9, f32[128,2048]{1,0:T(8,128)} %get-tuple-element.34.after.refs_0_), custom_call_target="tpu_custom_call" | custom-call | bytes 1048576 | tf_op jit(solution)/shard_map/mix/pallas_call | solution.py:285
  156.2 5.7 %out_project.3 = (bf16[128,2048]{1,0:T(8,128)(2,1)}, f32[128,2048]{1,0:T(8,128)}) custom-call(s32[3]{0:T(128)} %pad_add_fusion.pos_ref, bf16[2,128,512]{2,1,0:T(8,128)(2,1)} %get-tuple-element.37.a_ref, bf16[2,128,512]{2,1,0:T(8,128)(2,1)} %copy-done.7, bf16[512,2048]{1,0:T(8,128)(2,1)} %wa_ref.3, bf16[512,2048]{1,0:T(8,128)(2,1)} %collective-permute-done.11.wb_ref), custom_call_target="tpu_custom_call" | custom-call | bytes 1048576 | tf_op jit(solution)/shard_map/out_project/pallas_call | solution.py:313
  163.4 5.3 %collective-permute-done.12.refs_1_ = bf16[128,2048]{1,0:T(8,128)(2,1)S(1)} collective-permute-done((bf16[128,2048]{1,0:T(8,128)(2,1)S(1)}, bf16[128,2048]{1,0:T(8,128)(2,1)S(1)}, u32[]{:S(2)}, u32[]{:S(2)}) %collective-permute-start.12) | collective-permute-done | bytes 524320 | tf_op jit(solution)/shard_map/ppermute | solution.py:363
  168.6 10.7 %collective-permute-done.14.refs_3_ = bf16[128,2048]{1,0:T(8,128)(2,1)S(1)} collective-permute-done((bf16[128,2048]{1,0:T(8,128)(2,1)}, bf16[128,2048]{1,0:T(8,128)(2,1)S(1)}, u32[]{:S(2)}, u32[]{:S(2)}) %collective-permute-start.14) | collective-permute-done | bytes 524320 | tf_op jit(solution)/shard_map/ppermute | solution.py:363
  180.1 3.8 %join.1 = bf16[256,2048]{1,0:T(8,128)(2,1)} custom-call(f32[128,2048]{1,0:T(8,128)} %get-tuple-element.34.after.refs_0_, bf16[128,2048]{1,0:T(8,128)(2,1)} %copy-done.5, f32[128,2048]{1,0:T(8,128)} %get-tuple-element.39.refs_2_, bf16[128,2048]{1,0:T(8,128)(2,1)} %copy-done.6), custom_call_target="tpu_custom_call" | custom-call | bytes 1048576 | tf_op jit(solution)/shard_map/join/pallas_call | solution.py:350
  (46 shorter events, 9.1 us)
Async XLA Ops:
  0.0 40.9 %copy-start = (bf16[512,2048]{1,0:T(8,128)(2,1)S(1)}, bf16[512,2048]{1,0:T(8,128)(2,1)}, u32[]{:S(2)}) copy-start(bf16[512,2048]{1,0:T(8,128)(2,1)} %wa_ref.3) | copy-start | bytes 6291460
  0.0 26.4 %collective-permute-start.4 = (bf16[1024,512]{1,0:T(8,128)(2,1)}, bf16[1024,512]{1,0:T(8,128)(2,1)}, u32[]{:S(2)}, u32[]{:S(2)}) collective-permute-start(bf16[1024,512]{1,0:T(8,128)(2,1)} %x0.1), channel_id=1, source_target_pairs={{0,2},{1,3},{2,0},{3,1},{4,6},{5,7},{6,4},{7,5},{8,10},{9,11},{10,... | collective-permute-start | bytes 3145736 | tf_op jit(solution)/shard_map/ppermute | solution.py:363
  5.3 21.1 %all-to-all-start = ((bf16[8,64,512]{2,1,0:T(8,128)(2,1)}), bf16[8,64,512]{2,1,0:T(8,128)(2,1)S(1)}, u32[]{:S(2)}, u32[]{:S(2)}) async-start(bf16[8,64,512]{2,1,0:T(8,128)(2,1)} %get-tuple-element.23), calls=%async_computation | async-start | bytes 1048576 | tf_op jit(solution)/shard_map/all_to_all | solution.py:367
  11.1 37.8 %collective-permute-start.3 = (bf16[1024,512]{1,0:T(8,128)(2,1)}, bf16[1024,512]{1,0:T(8,128)(2,1)}, u32[]{:S(2)}, u32[]{:S(2)}) collective-permute-start(bf16[1024,512]{1,0:T(8,128)(2,1)} %x0.1), channel_id=1, source_target_pairs={{0,1},{1,0},{2,3},{3,2},{4,5},{5,4},{6,7},{7,6},{8,9},{9,8},{10,11... | collective-permute-start | bytes 3145736 | tf_op jit(solution)/shard_map/ppermute | solution.py:363
  26.4 23.6 %collective-permute-start.5 = (bf16[1024,512]{1,0:T(8,128)(2,1)}, bf16[1024,512]{1,0:T(8,128)(2,1)}, u32[]{:S(2)}, u32[]{:S(2)}) collective-permute-start(bf16[1024,512]{1,0:T(8,128)(2,1)} %collective-permute-done.4.x2), channel_id=1, source_target_pairs={{0,1},{1,0},{2,3},{3,2},{4,5},{5,4},{6,7},{7,6},{8,9},{9,8},{10,11... | collective-permute-start | bytes 3145736 | tf_op jit(solution)/shard_map/ppermute | solution.py:363
  26.4 23.6 %copy-start.1 = (bf16[8,64,512]{2,1,0:T(8,128)(2,1)}, bf16[8,64,512]{2,1,0:T(8,128)(2,1)S(1)}, u32[]{:S(2)}) copy-start(bf16[8,64,512]{2,1,0:T(8,128)(2,1)S(1)} %all-to-all-done.after.x0) | copy-start | bytes 1572868
  26.4 14.4 %collective-permute-start.1 = (bf16[8,64,512]{2,1,0:T(8,128)(2,1)S(1)}, bf16[8,64,512]{2,1,0:T(8,128)(2,1)}, u32[]{:S(2)}, u32[]{:S(2)}) collective-permute-start(bf16[8,64,512]{2,1,0:T(8,128)(2,1)S(1)} %all-to-all-done.after.x0), channel_id=1, source_target_pairs={{0,2},{1,3},{2,0},{3,1},{4,6},{5,7},{6,4},{7,5},{8,10},{9,11},{10,... | collective-permute-start | bytes 1572872 | tf_op jit(solution)/shard_map/ppermute | solution.py:363
  28.2 20.6 %all-to-all-start.2 = ((bf16[8,64,512]{2,1,0:T(8,128)(2,1)}), bf16[8,64,512]{2,1,0:T(8,128)(2,1)S(1)}, u32[]{:S(2)}, u32[]{:S(2)}) async-start(bf16[8,64,512]{2,1,0:T(8,128)(2,1)} %get-tuple-element.30), calls=%async_computation.2 | async-start | bytes 1048576 | tf_op jit(solution)/shard_map/all_to_all | solution.py:367
  34.1 28.0 %collective-permute-start = (bf16[8,64,512]{2,1,0:T(8,128)(2,1)S(1)}, bf16[8,64,512]{2,1,0:T(8,128)(2,1)}, u32[]{:S(2)}, u32[]{:S(2)}) collective-permute-start(bf16[8,64,512]{2,1,0:T(8,128)(2,1)S(1)} %all-to-all-done.after.x0), channel_id=1, source_target_pairs={{0,1},{1,0},{2,3},{3,2},{4,5},{5,4},{6,7},{7,6},{8,9},{9,8},{10,11... | collective-permute-start | bytes 1572872 | tf_op jit(solution)/shard_map/ppermute | solution.py:363
  40.9 21.2 %collective-permute-start.2 = (bf16[8,64,512]{2,1,0:T(8,128)(2,1)}, bf16[8,64,512]{2,1,0:T(8,128)(2,1)}, u32[]{:S(2)}, u32[]{:S(2)}) collective-permute-start(bf16[8,64,512]{2,1,0:T(8,128)(2,1)} %collective-permute-done.1.x2), channel_id=1, source_target_pairs={{0,1},{1,0},{2,3},{3,2},{4,5},{5,4},{6,7},{7,6},{8,9},{9,8},{10,11... | collective-permute-start | bytes 1572872 | tf_op jit(solution)/shard_map/ppermute | solution.py:363
  40.9 94.5 %collective-permute-start.11 = (bf16[512,2048]{1,0:T(8,128)(2,1)S(1)}, bf16[512,2048]{1,0:T(8,128)(2,1)}, u32[]{:S(2)}, u32[]{:S(2)}) collective-permute-start(bf16[512,2048]{1,0:T(8,128)(2,1)S(1)} %copy-done), channel_id=1, source_target_pairs={{0,1},{1,0},{2,3},{3,2},{4,5},{5,4},{6,7},{7,6},{8,9},{9,8},{10,11... | collective-permute-start | bytes 6291464 | tf_op jit(solution)/shard_map/ppermute | solution.py:363
  48.9 32.0 %copy-start.4 = (bf16[8,64,512]{2,1,0:T(8,128)(2,1)}, bf16[8,64,512]{2,1,0:T(8,128)(2,1)S(1)}, u32[]{:S(2)}) copy-start(bf16[8,64,512]{2,1,0:T(8,128)(2,1)S(1)} %all-to-all-done.2.x0) | copy-start | bytes 1572868
  48.9 32.0 %collective-permute-start.8 = (bf16[8,64,512]{2,1,0:T(8,128)(2,1)S(1)}, bf16[8,64,512]{2,1,0:T(8,128)(2,1)}, u32[]{:S(2)}, u32[]{:S(2)}) collective-permute-start(bf16[8,64,512]{2,1,0:T(8,128)(2,1)S(1)} %all-to-all-done.2.x0), channel_id=1, source_target_pairs={{0,2},{1,3},{2,0},{3,1},{4,6},{5,7},{6,4},{7,5},{8,10},{9,11},{10,... | collective-permute-start | bytes 1572872 | tf_op jit(solution)/shard_map/ppermute | solution.py:363
  72.5 42.2 %all-to-all-start.1 = ((bf16[8,272,128]{2,1,0:T(8,128)(2,1)}), bf16[8,272,128]{2,1,0:T(8,128)(2,1)S(1)}, u32[]{:S(2)}, u32[]{:S(2)}) async-start(bf16[8,272,128]{2,1,0:T(8,128)(2,1)} %column_part.2.after), calls=%async_computation.1 | async-start | bytes 1114112 | tf_op jit(solution)/shard_map/all_to_all | solution.py:367
  76.1 17.8 %collective-permute-start.6 = (bf16[512,512]{1,0:T(8,128)(2,1)}, bf16[512,512]{1,0:T(8,128)(2,1)}, u32[]{:S(2)}, u32[]{:S(2)}) collective-permute-start(bf16[512,512]{1,0:T(8,128)(2,1)} %get-tuple-element.27), channel_id=1, source_target_pairs={{0,4},{4,8},{8,12},{12,16},{16,20},{20,24},{24,28},{1,5},{5,9},{9,... | collective-permute-start | bytes 1572872 | tf_op jit(solution)/shard_map/ppermute | solution.py:387
  80.9 23.4 %collective-permute-start.7 = (bf16[8,64,512]{2,1,0:T(8,128)(2,1)S(1)}, bf16[8,64,512]{2,1,0:T(8,128)(2,1)}, u32[]{:S(2)}, u32[]{:S(2)}) collective-permute-start(bf16[8,64,512]{2,1,0:T(8,128)(2,1)S(1)} %all-to-all-done.2.x0), channel_id=1, source_target_pairs={{0,1},{1,0},{2,3},{3,2},{4,5},{5,4},{6,7},{7,6},{8,9},{9,8},{10,11... | collective-permute-start | bytes 1572872 | tf_op jit(solution)/shard_map/ppermute | solution.py:363
  80.9 23.4 %collective-permute-start.9 = (bf16[8,64,512]{2,1,0:T(8,128)(2,1)}, bf16[8,64,512]{2,1,0:T(8,128)(2,1)}, u32[]{:S(2)}, u32[]{:S(2)}) collective-permute-start(bf16[8,64,512]{2,1,0:T(8,128)(2,1)} %collective-permute-done.8.x2), channel_id=1, source_target_pairs={{0,1},{1,0},{2,3},{3,2},{4,5},{5,4},{6,7},{7,6},{8,9},{9,8},{10,11... | collective-permute-start | bytes 1572872 | tf_op jit(solution)/shard_map/ppermute | solution.py:363
  114.7 11.4 %copy-start.2 = (bf16[8,272,128]{2,1,0:T(8,128)(2,1)}, bf16[8,272,128]{2,1,0:T(8,128)(2,1)S(1)}, u32[]{:S(2)}) copy-start(bf16[8,272,128]{2,1,0:T(8,128)(2,1)S(1)} %all-to-all-done.1.col_ref) | copy-start | bytes 1671172
  114.7 28.9 %all-to-all-start.3 = ((bf16[8,272,128]{2,1,0:T(8,128)(2,1)}), bf16[8,272,128]{2,1,0:T(8,128)(2,1)S(1)}, u32[]{:S(2)}, u32[]{:S(2)}) async-start(bf16[8,272,128]{2,1,0:T(8,128)(2,1)} %column_part.3.after), calls=%async_computation.3 | async-start | bytes 1114112 | tf_op jit(solution)/shard_map/all_to_all | solution.py:367
  135.4 1.7 collective-permute-start.10
  153.7 1.7 collective-permute-start.13
  153.8 14.8 %collective-permute-start.12 = (bf16[128,2048]{1,0:T(8,128)(2,1)S(1)}, bf16[128,2048]{1,0:T(8,128)(2,1)S(1)}, u32[]{:S(2)}, u32[]{:S(2)}) collective-permute-start(bf16[128,2048]{1,0:T(8,128)(2,1)S(1)} %copy-done.9), channel_id=1, source_target_pairs={{0,2},{1,3},{2,0},{3,1},{4,6},{5,7},{6,4},{7,5},{8,10},{9,11},{10,... | collective-permute-start | bytes 1572872 | tf_op jit(solution)/shard_map/ppermute | solution.py:363
  161.9 17.4 %collective-permute-start.14 = (bf16[128,2048]{1,0:T(8,128)(2,1)}, bf16[128,2048]{1,0:T(8,128)(2,1)S(1)}, u32[]{:S(2)}, u32[]{:S(2)}) collective-permute-start(bf16[128,2048]{1,0:T(8,128)(2,1)} %get-tuple-element.40), channel_id=1, source_target_pairs={{0,2},{1,3},{2,0},{3,1},{4,6},{5,7},{6,4},{7,5},{8,10},{9,11},{10,... | collective-permute-start | bytes 1572872 | tf_op jit(solution)/shard_map/ppermute | solution.py:363
  168.6 10.7 %copy-start.5 = (bf16[128,2048]{1,0:T(8,128)(2,1)}, bf16[128,2048]{1,0:T(8,128)(2,1)S(1)}, u32[]{:S(2)}) copy-start(bf16[128,2048]{1,0:T(8,128)(2,1)S(1)} %collective-permute-done.12.refs_1_) | copy-start | bytes 1572868
  (5 other events, 13.3 us)

commit v3 on v0

--- a/solution.py
+++ b/solution.py
@@ -1,10 +1,396 @@
 import jax
 import jax.numpy as jnp
 from jax import lax
+from jax.experimental import pallas as pl
+from jax.experimental.pallas import tpu as pltpu
 from jax.sharding import PartitionSpec as P
 
 DH = 128
 STRIDE = 256
+HEADS = 4
+ROWS = 4
+SUB = 8
+CHUNKS = 2
+SCALE2 = DH ** (-0.5) * 1.4426950408889634
+FLOOR = -1e29
+MIB = 1024 * 1024
+F32 = jnp.float32
+BF16 = jnp.bfloat16
+
+
+ANYWHERE = pl.BlockSpec(memory_space=pl.ANY)
+IN_VMEM = pl.BlockSpec(memory_space=pltpu.VMEM)
+IN_SMEM = pl.BlockSpec(memory_space=pltpu.SMEM)
+
+
+def call(body, name, micros, out_shape, args, after=(), scratch=(), mib=24):
+    specs = [IN_SMEM if x.dtype == jnp.int32 else IN_VMEM for x in args]
+    extra = len(after)
+
+    def run(*refs):
+        n = len(args)
+        body(*refs[:n], *refs[n + extra :])
+
+    return pl.pallas_call(
+        run,
+        in_specs=specs + [ANYWHERE] * extra,
+        out_specs=jax.tree.map(lambda _: IN_VMEM, out_shape),
+        out_shape=out_shape,
+        scratch_shapes=list(scratch),
+        compiler_params=pltpu.CompilerParams(vmem_limit_bytes=mib * MIB),
+        cost_estimate=pl.CostEstimate(
+            flops=int(micros * 1.1e9), bytes_accessed=MIB, transcendentals=0
+        ),
+        name=name,
+    )(*args, *after)
+
+
+def shape(dims, dtype=BF16):
+    return jax.ShapeDtypeStruct(tuple(dims), dtype)
+
+
+def dot(a, b):
+    return jnp.dot(a, b, preferred_element_type=F32)
+
+
+def dot_t(a, b):
+    return lax.dot_general(a, b, (((1,), (1,)), ((), ())), preferred_element_type=F32)
+
+
+def dot_l(a, b):
+    return lax.dot_general(a, b, (((0,), (0,)), ((), ())), preferred_element_type=F32)
+
+
+def pack_kernel(pos_ref, tok_ref, *out_refs):
+    owners = len(out_refs) // CHUNKS
+    per_owner = STRIDE // owners
+    groups = per_owner // SUB
+    per_chunk = groups // CHUNKS
+    for k in range(owners):
+        d = pos_ref[0] ^ k
+        rows = [
+            tok_ref[pl.ds(pl.multiple_of(r * STRIDE + d * per_owner, per_owner), per_owner), :]
+            for r in range(ROWS)
+        ]
+        rows = [x.astype(F32) for x in rows]
+        for g in range(groups):
+            piece = jnp.concatenate([x[g * SUB : (g + 1) * SUB] for x in rows], 0)
+            at = (g % per_chunk) * ROWS * SUB
+            out = out_refs[(g // per_chunk) * owners + k]
+            out[at : at + ROWS * SUB, :] = piece.astype(BF16)
+
+
+def pack(pos, tokens, owners):
+    message = tokens.shape[0] // owners // CHUNKS
+    shapes = [shape((message, tokens.shape[1]))] * (CHUNKS * owners)
+    outs = call(pack_kernel, "pack_tokens", 2, shapes, (pos, tokens))
+    return [outs[i * owners : (i + 1) * owners] for i in range(CHUNKS)]
+
+
+def stage_kernel(order_ref, wq, wk, wv, oq, ok, ov, sems):
+    copies = []
+    for n, (w, o) in enumerate(((wq, oq), (wk, ok), (wv, ov))):
+        for p in range(4):
+            rows = pl.ds(pl.multiple_of(order_ref[p] * 512, 512), 512)
+            copies.append(
+                pltpu.make_async_copy(w.at[rows], o.at[p * 512 : (p + 1) * 512], sems.at[4 * n + p])
+            )
+    for c in copies:
+        c.start()
+    for c in copies:
+        c.wait()
+
+
+def stage(order, weights, after):
+    def body(order_ref, wq, wk, wv, _, *rest):
+        stage_kernel(order_ref, wq, wk, wv, *rest)
+
+    return pl.pallas_call(
+        body,
+        in_specs=[IN_SMEM] + [ANYWHERE] * 4,
+        out_specs=[IN_VMEM] * 3,
+        out_shape=[shape(w.shape) for w in weights],
+        scratch_shapes=[pltpu.SemaphoreType.DMA((12,))],
+        compiler_params=pltpu.CompilerParams(vmem_limit_bytes=16 * MIB),
+        cost_estimate=pl.CostEstimate(flops=0, bytes_accessed=6 * MIB, transcendentals=0),
+        name="stage_weights",
+    )(order, *weights, after)
+
+
+def gathered(x_refs, at, w_ref):
+    width = x_refs[0].shape[1]
+    total = None
+    for p, x_ref in enumerate(x_refs):
+        term = dot(x_ref[at, :], w_ref[p * width : (p + 1) * width, :])
+        total = term if total is None else total + term
+    return total.astype(BF16)
+
+
+def halo_kernel(x0, x1, x2, x3, wk, wv, out_ref):
+    rows = x0.shape[0]
+    at = slice(rows - STRIDE, rows)
+    out_ref[:STRIDE, :] = gathered((x0, x1, x2, x3), at, wk)
+    out_ref[STRIDE:, :] = gathered((x0, x1, x2, x3), at, wv)
+
+
+def project_kernel(x0, x1, x2, x3, wq, wk, wv, halo, q_ref, k_ref, v_ref):
+    rows = x0.shape[0]
+    xs = (x0, x1, x2, x3)
+    last = slice(rows - STRIDE, rows)
+    k_ref[last, :] = halo[:STRIDE, :]
+    v_ref[last, :] = halo[STRIDE:, :]
+    for w, out, upto in ((wq, q_ref, rows), (wk, k_ref, rows - STRIDE), (wv, v_ref, rows - STRIDE)):
+        out[:upto, :] = gathered(xs, slice(0, upto), w)
+
+
+def softmax_columns(s):
+    m = jnp.maximum(jnp.max(s, 0, keepdims=True), FLOOR)
+    p = jnp.exp2((s - m) * SCALE2)
+    total = jnp.maximum(jnp.sum(p, 0, keepdims=True), 1.0)
+    return p, total, m * SCALE2 + jnp.log2(total)
+
+
+def local_kernel(pos_ref, q_ref, k_ref, v_ref, halo_ref, *outs):
+    out_refs, lse_refs = outs[:CHUNKS], outs[CHUNKS:]
+    owners, message, _ = out_refs[0].shape
+    groups = message // ROWS // SUB
+    block = pos_ref[0]
+    u = lax.broadcasted_iota(jnp.int32, (STRIDE, STRIDE), 0)
+    t = lax.broadcasted_iota(jnp.int32, (STRIDE, STRIDE), 1)
+    current = u <= t
+    low = jnp.where(block == 0, -1e30, 0.0).astype(F32)
+    for r in range(ROWS):
+        lses = []
+        here = slice(r * STRIDE, (r + 1) * STRIDE)
+        back = slice((r - 1) * STRIDE, r * STRIDE)
+        for h in range(HEADS):
+            cols = slice(h * DH, (h + 1) * DH)
+            q = q_ref[here, cols]
+            k_prev = k_ref[back, cols] if r else halo_ref[:STRIDE, cols]
+            v_prev = v_ref[back, cols] if r else halo_ref[STRIDE:, cols]
+            s_prev = dot_t(k_prev, q)
+            if r == 0:
+                s_prev = s_prev + low
+            p, total, lse = softmax_columns(jnp.where(current, dot_t(k_ref[here, cols], q), s_prev))
+            p_now = jnp.where(current, p, 0.0).astype(BF16)
+            p_prev = jnp.where(current, 0.0, p).astype(BF16)
+            o = dot_l(v_ref[here, cols], p_now) + dot_l(v_prev, p_prev)
+            o = (o * (1.0 / total)).T
+            lses.append(lse)
+            for d in range(owners):
+                for i in range(CHUNKS):
+                    for g in range(groups):
+                        at = ((d * CHUNKS + i) * groups + g) * SUB
+                        to = (g * ROWS + r) * SUB
+                        out_refs[i][d, to : to + SUB, cols] = o[at : at + SUB]
+        lses.append(jnp.zeros((128 - HEADS, STRIDE), F32))
+        turned = jnp.concatenate(lses, 0).T
+        for i in range(CHUNKS):
+            for g in range(groups):
+                total = None
+                for d in range(owners):
+                    at = ((d * CHUNKS + i) * groups + g) * SUB
+                    moved = pltpu.roll(turned[at : at + SUB], 8 * (block ^ d), 1)
+                    total = moved if total is None else total + moved
+                to = (g * ROWS + r) * SUB
+                lse_refs[i][to : to + SUB, :] = total
+
+
+def local_part(pos, q, k, v, halo, owners, after):
+    rows, width = q.shape
+    message = rows // owners // CHUNKS
+    shapes = [shape((owners, message, width), F32)] * CHUNKS + [shape((message, 128), F32)] * CHUNKS
+    outs = call(local_kernel, "local_part", 5, shapes, (pos, q, k, v, halo), after)
+    return list(zip(outs[:CHUNKS], outs[CHUNKS:]))
+
+
+def column_kernel(pos_ref, x0, x1, x2, x3, wq, wk, wv, *rest):
+    out_refs, scratch = rest[:-3], rest[-3:]
+    owners, message, _ = scratch[0].shape
+    groups = message // (ROWS * SUB)
+    everything = slice(0, owners * message)
+    for w, a in zip((wq, wk, wv), scratch):
+        a[...] = gathered((x0, x1, x2, x3), everything, w).reshape(a.shape)
+    part = ROWS * SUB
+    size = owners * part
+
+    def row_and_class(dim):
+        i = lax.broadcasted_iota(jnp.int32, (size, size), dim)
+        return ((i // part) ^ pos_ref[0]) * ROWS + (i % part) // SUB, i % SUB
+
+    (row_j, class_j), (row_i, class_i) = row_and_class(0), row_and_class(1)
+    earlier = jnp.logical_and(class_i == class_j, row_i > row_j)
+    stats = []
+    for g in range(groups):
+        at = slice(g * part, (g + 1) * part)
+        lses = []
+        for h in range(HEADS):
+            cols = slice(h * DH, (h + 1) * DH)
+            q, k, v = (a[:, at, cols].reshape(size, DH) for a in scratch)
+            p, total, lse = softmax_columns(jnp.where(earlier, dot_t(k, q), -1e30))
+            o = (dot_l(v, p.astype(BF16)) * (1.0 / total)).T.astype(BF16)
+            rows = slice(h * message + g * part, h * message + (g + 1) * part)
+            for n in range(owners):
+                out_refs[n][rows, :] = o[n * part : (n + 1) * part]
+            lses.append(lse)
+        stats.append(jnp.concatenate(lses + lses, 0))
+    upper = lax.broadcasted_iota(jnp.int32, (8, 128), 0) < HEADS
+    blank = [jnp.zeros((8, 128 - message), F32)] if message < 128 else []
+    for n in range(owners):
+        x = jnp.concatenate([s[:, n * part : (n + 1) * part] for s in stats] + blank, 1)
+        hi = x.astype(BF16).astype(F32)
+        mid = (x - hi).astype(BF16).astype(F32)
+        lo = x - hi - mid
+        tail = jnp.concatenate([jnp.where(upper, hi, lo), jnp.where(upper, mid, 0.0)], 0)
+        out_refs[n][HEADS * message : HEADS * message + 16, :] = tail.astype(BF16)
+
+
+def column_part(pos, pieces, weights, owners, after):
+    tokens, width = pieces[0].shape
+    message = tokens // owners
+    shapes = [shape((HEADS * message + 16, DH))] * owners
+    scratch = [pltpu.VMEM((owners, message, width), BF16)] * 3
+    return call(column_kernel, "column_part", 6, shapes, (pos, *pieces, *weights), after, scratch)
+
+
+def mix_kernel(pos_ref, loc_ref, lse_ref, *rest):
+    col_refs, (own_ref, send_ref, mixed) = rest[:-3], rest[-3:]
+    owners, message, _ = loc_ref.shape
+    groups = message // (ROWS * SUB)
+    base = HEADS * message
+    tiles = []
+    for col_ref in col_refs:
+        tail = col_ref[base : base + 16, :].astype(F32)
+        tiles.append(tail[:8] + tail[8:])
+    tiles.append(jnp.zeros((128 - 8 * owners, 128), F32))
+    turned = jnp.concatenate(tiles, 0).T[:message]
+    col_lse = turned + pltpu.roll(turned, 124, 1)
+    loc_lse = lse_ref[...]
+    top = jnp.maximum(col_lse, loc_lse)
+    w_col = jnp.exp2(col_lse - top)
+    w_loc = jnp.exp2(loc_lse - top)
+    share = 1.0 / (w_col + w_loc)
+    w_col = w_col * share
+    w_loc = w_loc * share
+    span = groups * SUB
+    for k, col_ref in enumerate(col_refs):
+        d = pos_ref[0] ^ k
+        spot = pl.ds(pl.multiple_of(d * span, span), span)
+        for h in range(HEADS):
+            cols = slice(h * DH, (h + 1) * DH)
+            at = slice(8 * k + h, 8 * k + h + 1)
+            col = col_ref[h * message : (h + 1) * message, :].astype(F32)
+            both = loc_ref[d, :, cols] * w_loc[:, at] + col * w_col[:, at]
+            for r in range(ROWS):
+                starts = [(g * ROWS + r) * SUB for g in range(groups)]
+                piece = jnp.concatenate([both[s : s + SUB] for s in starts], 0)
+                mixed[r, spot, cols] = piece.astype(BF16)
+    core = pos_ref[1]
+    for x in range(2):
+        own_ref[x] = mixed[2 * x + core]
+        send_ref[x] = mixed[2 * x + 1 - core]
+
+
+def mix(pos, columns, local, lse, after):
+    owners, message, width = local.shape
+    tokens = owners * message // ROWS
+    shapes = [shape((2, tokens, width))] * 2
+    scratch = [pltpu.VMEM((ROWS, tokens, width), BF16)]
+    return call(mix_kernel, "mix", 3, shapes, (pos, local, lse, *columns), after, scratch)
+
+
+def out_kernel(pos_ref, a_ref, b_ref, wa_ref, wb_ref, send_ref, keep_ref):
+    tokens, columns = send_ref.shape
+    a = a_ref[...].reshape(2 * tokens, -1)
+    b = b_ref[...].reshape(2 * tokens, -1)
+    low_side = pos_ref[2] == 0
+    tile = 512
+    for n in range(0, columns, tile):
+        at = slice(n, n + tile)
+        total = dot(a, wa_ref[:, at]) + dot(b, wb_ref[:, at])
+        send_ref[:, at] = jnp.where(low_side, total[tokens:], total[:tokens]).astype(BF16)
+        keep_ref[:, at] = jnp.where(low_side, total[:tokens], total[tokens:])
+
+
+def out_project(pos, own, other, w_own, w_other):
+    dims = (own.shape[1], w_own.shape[1])
+    shapes = [shape(dims), shape(dims, F32)]
+    return call(out_kernel, "out_project", 3, shapes, (pos, own, other, w_own, w_other))
+
+
+def join_kernel(*refs):
+    out_ref = refs[-1]
+    chunks = (len(refs) - 1) // 2
+    tokens = refs[0].shape[0]
+    span = 32 // chunks
+    for i in range(chunks):
+        keep, got = refs[2 * i], refs[2 * i + 1]
+        for d in range(tokens // span):
+            rows = slice(d * span, (d + 1) * span)
+            at = (d * chunks + i) * span
+            total = keep[rows, :] + got[rows, :].astype(F32)
+            out_ref[at : at + span, :] = total.astype(BF16)
+
+
+def join(pairs):
+    columns = pairs[0][0].shape[1]
+    args = [x for pair in pairs for x in pair]
+    return call(join_kernel, "join", 2, shape((STRIDE, columns)), args)
+
+
+def swap(value, distance):
+    return lax.ppermute(value, "head", [(i, i ^ distance) for i in range(4)])
+
+
+def exchange(messages):
+    n = len(messages)
+    return [messages[0]] + [
+        lax.ppermute(messages[k], "seq", [(i, i ^ k) for i in range(n)]) for k in range(1, n)
+    ]
+
+
+def gather(own):
+    far = swap(own, 2)
+    return own, swap(own, 1), far, swap(far, 1)
+
+
+def chunked(tokens, w_query, w_key, w_value, w_out):
+    owners = lax.axis_size("seq")
+    head = lax.axis_index("head")
+    block = lax.axis_index("seq")
+    order = jnp.bitwise_xor(jnp.arange(4, dtype=jnp.int32), head.astype(jnp.int32))
+    pos = jnp.stack([block, head % 2, head // 2]).astype(jnp.int32)
+    rows, width = tokens.shape
+
+    pieces = gather(tokens)
+    classes = [exchange(m) for m in pack(pos, tokens, owners)]
+    weights = stage(order, (w_query, w_key, w_value), classes[0][1])
+    w_other = swap(w_out, 1)
+    own_halo = call(
+        halo_kernel, "project_halo", 1.5, shape((2 * STRIDE, width)), (*pieces, *weights[1:])
+    )
+    halo = lax.ppermute(own_halo, "seq", [(i, i + 1) for i in range(owners - 1)])
+    q, k, v = call(
+        project_kernel,
+        "project_block",
+        7,
+        [shape((rows, width))] * 3,
+        (*pieces, *weights, own_halo),
+    )
+    columns, after = [], (q, halo)
+    for i, messages in enumerate(classes):
+        class_pieces = gather(jnp.concatenate(messages, 0))
+        columns.append(column_part(pos, class_pieces, weights, owners, after))
+        if i == 0:
+            locals_ = local_part(pos, q, k, v, halo, owners, (columns[0][0],))
+            after = (locals_[-1][-1],)
+    pairs, after = [], (columns[-1][0],)
+    for column, (local, lse) in zip(columns, locals_):
+        own, send = mix(pos, exchange(column), local, lse, after)
+        out, keep = out_project(pos, own, swap(send, 1), w_out, w_other)
+        after = (keep,)
+        pairs.append((keep, swap(out, 2)))
+    return join(pairs)
 
 
 def from_behind(value, axis, by):
@@ -13,7 +399,7 @@
     return lax.ppermute(value, axis, pairs)
 
 
-def shards(tokens, w_query, w_key, w_value, w_out):
+def general(tokens, w_query, w_key, w_value, w_out):
     tok_rows = tokens.shape[0]
     head_width = w_query.shape[1]
     head_count = head_width // DH
@@ -147,6 +533,18 @@
     )
 
 
+def shards(tokens, w_query, w_key, w_value, w_out):
+    rows, width = w_query.shape
+    fits = (
+        lax.axis_size("seq") == STRIDE // 32
+        and lax.axis_size("head") == 4
+        and tokens.shape == (ROWS * STRIDE, HEADS * DH)
+        and (rows, width) == (4 * HEADS * DH, HEADS * DH)
+    )
+    plan = chunked if fits else general
+    return plan(tokens, w_query, w_key, w_value, w_out)
+
+
 def solution(mesh):
     in_specs = (
         P("seq", "head"),

time: 263 us -> 146 us (0.56)
  waiting for transfers between devices: 110 us -> 41.6 us
  local copies, waits for them, and re-layouts: 49.5 us -> 1.34 us
  matrix products: 38.6 us -> 0 us
  Pallas kernels: 0 us -> 35 us
  starting transfers between devices: 38 us -> 67.4 us
  between operations: 13.7 us -> 0.31 us
  other arithmetic: 12.2 us -> 0.08 us
    ppermute x2 -> x43, starting transfers between devices: 7.83 us -> 67.4 us  [the longest x28 57 us: exchange(): lax.ppermute(messages[k], 'seq', [(i, i ^ k) for i in range(n)])]
    reduce_scatter x1 -> x0, waiting for transfers between devices: 42.6 us -> none  [shards(): lax.psum_scatter(jnp.dot(mixed, w_out, preferred_element_type=jnp.float32...]
    ppermute x2 -> x43, waiting for transfers between devices: 0.01 us -> 41.6 us  [the longest x14 29.6 us: swap(): return lax.ppermute(value, 'head', [(i, i ^ distance) for i in range(4)])]
    all_gather x1 -> x0, waiting for transfers between devices: 38.9 us -> none  [shards(): shard_piece = lax.all_gather(tokens, 'head', axis=1, tiled=True)]
    dot_general x8 -> x0, matrix products: 38.6 us -> none  [the longest x3 17.6 us: shards(): jnp.dot(shard_piece, weight, preferred_element_type=jnp.float32)]
    pallas_call x0 -> x12, Pallas kernels: none -> 35 us  [the longest x11 33.9 us: call(): pl.pallas_call(run, in_specs=specs + [ANYWHERE] * extra, out_specs=jax.tr...]
    all_to_all x6 -> x0, starting transfers between devices: 29.9 us -> none  [the longest x1 8.67 us: shards(): lax.all_to_all(column_top.astype(jnp.bfloat16), 'seq', split_axis=0, conc...]
    all_to_all x6 -> x0, waiting for transfers between devices: 28.3 us -> none  [the longest x1 15.4 us: shards(): lax.all_to_all(key_heads.reshape(row_count, STRIDE, head_count, DH), 'seq...]
  transfers between devices with their start and end apart: 10 -> 43, of which waited for: 7 -> 11; matrix products, arithmetic and copies ran while one was open for 30% -> 0% of each run, Pallas kernels for 0% -> 22%
where the time goes in v3:
time: 146 us
  starting transfers between devices  67.4 us (46%)
  waiting for transfers between devices  41.6 us (28%)
  Pallas kernels  35 us (24%)
    ppermute x28, starting transfers between devices, exchange(): lax.ppermute(messages[k], 'seq', [(i, i ^ k) for i in range(n)])  57 us
    pallas_call x11, Pallas kernels, call(): pl.pallas_call(run, in_specs=specs + [ANYWHERE] * extra, out_specs=jax.tr...  33.9 us
    ppermute x14, waiting for transfers between devices, swap(): return lax.ppermute(value, 'head', [(i, i ^ distance) for i in range(4)])  29.6 us
    ppermute x28, waiting for transfers between devices, exchange(): lax.ppermute(messages[k], 'seq', [(i, i ^ k) for i in range(n)])  9.35 us
    ppermute x14, starting transfers between devices, swap(): return lax.ppermute(value, 'head', [(i, i ^ distance) for i in range(4)])  7.72 us
  transfers between devices with their start and end apart: 43, of which 11 were waited for; matrix products, arithmetic and copies ran while one was open for 0% of the time, Pallas kernels for 22%

profile of v3, /device:TPU:0, one launch (start us, length us, event | category | flops | bytes accessed | tf_op | source)
XLA Modules:
  0.0 145.7 jit_solution(1675237865949412020)
XLA Ops:
  0.5 2.5 %collective-permute-start.1 = (bf16[1024,512]{1,0:T(8,128)(2,1)}, bf16[1024,512]{1,0:T(8,128)(2,1)S(1)}, u32[]{:S(2)}, u32[]{:S(2)}) collective-permute-start(bf16[1024,512]{1,0:T(8,128)(2,1)} %refs_0_.3), channel_id=1, source_target_pairs={{0,2},{1,3},{2,0},{3,1},{4,6},{5,7},{6,4},{7,5},{8,10},{9,11},{10,... | collective-permute-start | bytes 3145736 | tf_op jit(solution)/shard_map/ppermute | solution.py:342
  9.2 2.6 %collective-permute-start.7 = (bf16[64,512]{1,0:T(8,128)(2,1)S(1)}, bf16[64,512]{1,0:T(8,128)(2,1)S(1)}, u32[]{:S(2)}, u32[]{:S(2)}) collective-permute-start(bf16[64,512]{1,0:T(8,128)(2,1)S(1)} %get-tuple-element.65), channel_id=1, source_target_pairs={{0,16},{4,20},{8,24},{12,28},{16,0},{20,4},{24,8},{28,12},{1,17},{... | collective-permute-start | bytes 196616 | tf_op jit(solution)/shard_map/ppermute | solution.py:348
  13.9 2.9 %collective-permute-start.9 = (bf16[64,512]{1,0:T(8,128)(2,1)S(1)}, bf16[64,512]{1,0:T(8,128)(2,1)S(1)}, u32[]{:S(2)}, u32[]{:S(2)}) collective-permute-start(bf16[64,512]{1,0:T(8,128)(2,1)S(1)} %get-tuple-element.67), channel_id=1, source_target_pairs={{0,24},{4,28},{8,16},{12,20},{16,8},{20,12},{24,0},{28,4},{1,25},{... | collective-permute-start | bytes 196616 | tf_op jit(solution)/shard_map/ppermute | solution.py:348
  16.9 5.1 %collective-permute-start.10 = (bf16[64,512]{1,0:T(8,128)(2,1)S(1)}, bf16[64,512]{1,0:T(8,128)(2,1)S(1)}, u32[]{:S(2)}, u32[]{:S(2)}) collective-permute-start(bf16[64,512]{1,0:T(8,128)(2,1)S(1)} %get-tuple-element.68), channel_id=1, source_target_pairs={{0,28},{4,24},{8,20},{12,16},{16,12},{20,8},{24,4},{28,0},{1,29},{... | collective-permute-start | bytes 196616 | tf_op jit(solution)/shard_map/ppermute | solution.py:348
  23.0 4.0 %collective-permute-done.1.refs_2_ = bf16[1024,512]{1,0:T(8,128)(2,1)S(1)} collective-permute-done((bf16[1024,512]{1,0:T(8,128)(2,1)}, bf16[1024,512]{1,0:T(8,128)(2,1)S(1)}, u32[]{:S(2)}, u32[]{:S(2)}) %collective-permute-start.1) | collective-permute-done | bytes 1048608 | tf_op jit(solution)/shard_map/ppermute | solution.py:342
  31.6 2.7 %collective-permute-start.24 = (bf16[64,512]{1,0:T(8,128)(2,1)S(1)}, bf16[64,512]{1,0:T(8,128)(2,1)S(1)}, u32[]{:S(2)}, u32[]{:S(2)}) collective-permute-start(bf16[64,512]{1,0:T(8,128)(2,1)S(1)} %get-tuple-element.83), channel_id=1, source_target_pairs={{0,16},{4,20},{8,24},{12,28},{16,0},{20,4},{24,8},{28,12},{1,17},{... | collective-permute-start | bytes 196616 | tf_op jit(solution)/shard_map/ppermute | solution.py:348
  34.2 2.4 %collective-permute-start.25 = (bf16[64,512]{1,0:T(8,128)(2,1)S(1)}, bf16[64,512]{1,0:T(8,128)(2,1)S(1)}, u32[]{:S(2)}, u32[]{:S(2)}) collective-permute-start(bf16[64,512]{1,0:T(8,128)(2,1)S(1)} %get-tuple-element.84), channel_id=1, source_target_pairs={{0,20},{4,16},{8,28},{12,24},{16,4},{20,0},{24,12},{28,8},{1,21},{... | collective-permute-start | bytes 196616 | tf_op jit(solution)/shard_map/ppermute | solution.py:348
  38.3 4.8 %collective-permute-start.26 = (bf16[64,512]{1,0:T(8,128)(2,1)S(1)}, bf16[64,512]{1,0:T(8,128)(2,1)S(1)}, u32[]{:S(2)}, u32[]{:S(2)}) collective-permute-start(bf16[64,512]{1,0:T(8,128)(2,1)S(1)} %get-tuple-element.85), channel_id=1, source_target_pairs={{0,24},{4,28},{8,16},{12,20},{16,8},{20,12},{24,0},{28,4},{1,25},{... | collective-permute-start | bytes 196616 | tf_op jit(solution)/shard_map/ppermute | solution.py:348
  43.1 2.3 %collective-permute-start.27 = (bf16[64,512]{1,0:T(8,128)(2,1)S(1)}, bf16[64,512]{1,0:T(8,128)(2,1)S(1)}, u32[]{:S(2)}, u32[]{:S(2)}) collective-permute-start(bf16[64,512]{1,0:T(8,128)(2,1)S(1)} %get-tuple-element.86), channel_id=1, source_target_pairs={{0,28},{4,24},{8,20},{12,16},{16,12},{20,8},{24,4},{28,0},{1,29},{... | collective-permute-start | bytes 196616 | tf_op jit(solution)/shard_map/ppermute | solution.py:348
  45.5 4.6 %collective-permute-done.27 = bf16[64,512]{1,0:T(8,128)(2,1)S(1)} collective-permute-done((bf16[64,512]{1,0:T(8,128)(2,1)S(1)}, bf16[64,512]{1,0:T(8,128)(2,1)S(1)}, u32[]{:S(2)}, u32[]{:S(2)}) %collective-permute-start.27) | collective-permute-done | bytes 65568 | tf_op jit(solution)/shard_map/ppermute | solution.py:348
  53.2 2.6 %collective-permute-start.4 = (bf16[512,512]{1,0:T(8,128)(2,1)S(1)}, bf16[512,512]{1,0:T(8,128)(2,1)S(1)}, u32[]{:S(2)}, u32[]{:S(2)}) collective-permute-start(bf16[512,512]{1,0:T(8,128)(2,1)S(1)} %project_halo.1.refs_7_), channel_id=1, source_target_pairs={{0,4},{4,8},{8,12},{12,16},{16,20},{20,24},{24,28},{1,5},{5,9},{9,... | collective-permute-start | bytes 1572872 | tf_op jit(solution)/shard_map/ppermute | solution.py:372
  55.8 5.6 %project_block.1 = (bf16[1024,512]{1,0:T(8,128)(2,1)S(1)}, bf16[1024,512]{1,0:T(8,128)(2,1)S(1)}, bf16[1024,512]{1,0:T(8,128)(2,1)S(1)}) custom-call(bf16[1024,512]{1,0:T(8,128)(2,1)S(1)} %copy-done.4, bf16[1024,512]{1,0:T(8,128)(2,1)S(1)} %collective-permute-done.refs_1_, bf16[1024,512]{1,0:T(8,128)(2,1)S(1)} %collective-permute-done.1.refs_2_, ...), custom_call_target="tpu_custom_call" | custom-call | flops 7699999744 | bytes 1048576 | tf_op jit(solution)/shard_map/project_block/pallas_call | solution.py:34
  61.5 3.1 %collective-permute-done.29.refs_3_ = bf16[512,512]{1,0:T(8,128)(2,1)S(1)} collective-permute-done((bf16[512,512]{1,0:T(8,128)(2,1)S(1)}, bf16[512,512]{1,0:T(8,128)(2,1)S(1)}, u32[]{:S(2)}, u32[]{:S(2)}) %collective-permute-start.29) | collective-permute-done | bytes 524320 | tf_op jit(solution)/shard_map/ppermute | solution.py:342
  64.6 2.7 %collective-permute-done.4.refs_9_.refs_4_ = bf16[512,512]{1,0:T(8,128)(2,1)S(1)} collective-permute-done((bf16[512,512]{1,0:T(8,128)(2,1)S(1)}, bf16[512,512]{1,0:T(8,128)(2,1)S(1)}, u32[]{:S(2)}, u32[]{:S(2)}) %collective-permute-start.4) | collective-permute-done | bytes 524320 | tf_op jit(solution)/shard_map/ppermute | solution.py:372
  67.2 6.4 %column_part.2 = (bf16[272,128]{1,0:T(8,128)(2,1)S(1)}, bf16[272,128]{1,0:T(8,128)(2,1)S(1)}, bf16[272,128]{1,0:T(8,128)(2,1)S(1)}, bf16[272,128]{1,0:T(8,128)(2...) custom-call(s32[3]{0:T(128)S(1)} %pad_add_fusion.refs_0_, ...), custom_call_target="tpu_custom_call" | custom-call | flops 6600000000 | bytes 1048576 | tf_op jit(solution)/shard_map/column_part/pallas_call | solution.py:34
  73.6 2.5 %collective-permute-start.14 = (bf16[272,128]{1,0:T(8,128)(2,1)S(1)}, bf16[272,128]{1,0:T(8,128)(2,1)S(1)}, u32[]{:S(2)}, u32[]{:S(2)}) collective-permute-start(bf16[272,128]{1,0:T(8,128)(2,1)S(1)} %get-tuple-element.72), channel_id=1, source_target_pairs={{0,4},{4,0},{8,12},{12,8},{16,20},{20,16},{24,28},{28,24},{1,5},{5... | collective-permute-start | bytes 208904 | tf_op jit(solution)/shard_map/ppermute | solution.py:348
  79.3 5.8 %local_part.1 = (f32[8,64,512]{2,1,0:T(8,128)S(1)}, f32[8,64,512]{2,1,0:T(8,128)S(1)}, f32[64,128]{1,0:T(8,128)S(1)}, f32[64,128]{1,0:T(8,128)S(1)}) custom-call(s32[3]{0:T(128)S(1)} %pad_add_fusion.refs_0_, bf16[1024,512]{1,0:T(8,128)(2,1)S(1)} %get-tuple-element.59.refs_8_.refs_1_, bf16[1024,512]{1,0:T(8,128)(2,1)S(1)} %get-tuple-element.60.refs_2_, ...), custom_call_target="tpu_custom_call" | custom-call | flops 5500000256 | bytes 1048576 | tf_op jit(solution)/shard_map/local_part/pallas_call | solution.py:34
  88.1 2.6 %collective-permute-start.19 = (bf16[272,128]{1,0:T(8,128)(2,1)S(1)}, bf16[272,128]{1,0:T(8,128)(2,1)S(1)}, u32[]{:S(2)}, u32[]{:S(2)}) collective-permute-start(bf16[272,128]{1,0:T(8,128)(2,1)S(1)} %get-tuple-element.77), channel_id=1, source_target_pairs={{0,24},{4,28},{8,16},{12,20},{16,8},{20,12},{24,0},{28,4},{1,25},{... | collective-permute-start | bytes 208904 | tf_op jit(solution)/shard_map/ppermute | solution.py:348
  92.8 6.6 %column_part.3 = (bf16[272,128]{1,0:T(8,128)(2,1)S(1)}, bf16[272,128]{1,0:T(8,128)(2,1)S(1)}, bf16[272,128]{1,0:T(8,128)(2,1)S(1)}, bf16[272,128]{1,0:T(8,128)(2...) custom-call(s32[3]{0:T(128)S(1)} %pad_add_fusion.refs_0_, ...), custom_call_target="tpu_custom_call" | custom-call | flops 6600000000 | bytes 1048576 | tf_op jit(solution)/shard_map/column_part/pallas_call | solution.py:34
  104.5 2.2 %collective-permute-start.37 = (bf16[272,128]{1,0:T(8,128)(2,1)S(1)}, bf16[272,128]{1,0:T(8,128)(2,1)S(1)}, u32[]{:S(2)}, u32[]{:S(2)}) collective-permute-start(bf16[272,128]{1,0:T(8,128)(2,1)S(1)} %get-tuple-element.97), channel_id=1, source_target_pairs={{0,16},{4,20},{8,24},{12,28},{16,0},{20,4},{24,8},{28,12},{1,17},{... | collective-permute-start | bytes 208904 | tf_op jit(solution)/shard_map/ppermute | solution.py:348
  110.1 2.4 %collective-permute-start.40 = (bf16[272,128]{1,0:T(8,128)(2,1)S(1)}, bf16[272,128]{1,0:T(8,128)(2,1)S(1)}, u32[]{:S(2)}, u32[]{:S(2)}) collective-permute-start(bf16[272,128]{1,0:T(8,128)(2,1)S(1)} %get-tuple-element.100), channel_id=1, source_target_pairs={{0,28},{4,24},{8,20},{12,16},{16,12},{20,8},{24,4},{28,0},{1,29},{... | collective-permute-start | bytes 208904 | tf_op jit(solution)/shard_map/ppermute | solution.py:348
  114.3 3.1 %collective-permute-done.38.refs_8_ = bf16[272,128]{1,0:T(8,128)(2,1)S(1)} collective-permute-done((bf16[272,128]{1,0:T(8,128)(2,1)S(1)}, bf16[272,128]{1,0:T(8,128)(2,1)S(1)}, u32[]{:S(2)}, u32[]{:S(2)}) %collective-permute-start.38) | collective-permute-done | bytes 69664 | tf_op jit(solution)/shard_map/ppermute | solution.py:348
  123.0 10.8 %collective-permute-done.33.refs_1_ = bf16[128,2048]{1,0:T(8,128)(2,1)S(1)} collective-permute-done((bf16[128,2048]{1,0:T(8,128)(2,1)S(1)}, bf16[128,2048]{1,0:T(8,128)(2,1)S(1)}, u32[]{:S(2)}, u32[]{:S(2)}) %collective-permute-start.33) | collective-permute-done | bytes 524320 | tf_op jit(solution)/shard_map/ppermute | solution.py:342
  133.8 10.8 %collective-permute-done.42.refs_3_ = bf16[128,2048]{1,0:T(8,128)(2,1)S(1)} collective-permute-done((bf16[128,2048]{1,0:T(8,128)(2,1)S(1)}, bf16[128,2048]{1,0:T(8,128)(2,1)S(1)}, u32[]{:S(2)}, u32[]{:S(2)}) %collective-permute-start.42) | collective-permute-done | bytes 524320 | tf_op jit(solution)/shard_map/ppermute | solution.py:342
  (104 shorter events, 44.3 us)
Async XLA Ops:
  0.0 51.7 %collective-permute-start = (bf16[1024,512]{1,0:T(8,128)(2,1)}, bf16[1024,512]{1,0:T(8,128)(2,1)S(1)}, u32[]{:S(2)}, u32[]{:S(2)}) collective-permute-start(bf16[1024,512]{1,0:T(8,128)(2,1)} %refs_0_.3), channel_id=1, source_target_pairs={{0,1},{1,0},{2,3},{3,2},{4,5},{5,4},{6,7},{7,6},{8,9},{9,8},{10,11... | collective-permute-start | bytes 3145736 | tf_op jit(solution)/shard_map/ppermute | solution.py:342
  0.5 26.5 %collective-permute-start.1 = (bf16[1024,512]{1,0:T(8,128)(2,1)}, bf16[1024,512]{1,0:T(8,128)(2,1)S(1)}, u32[]{:S(2)}, u32[]{:S(2)}) collective-permute-start(bf16[1024,512]{1,0:T(8,128)(2,1)} %refs_0_.3), channel_id=1, source_target_pairs={{0,2},{1,3},{2,0},{3,1},{4,6},{5,7},{6,4},{7,5},{8,10},{9,11},{10,... | collective-permute-start | bytes 3145736 | tf_op jit(solution)/shard_map/ppermute | solution.py:342
  11.8 10.2 %collective-permute-start.8 = (bf16[64,512]{1,0:T(8,128)(2,1)S(1)}, bf16[64,512]{1,0:T(8,128)(2,1)S(1)}, u32[]{:S(2)}, u32[]{:S(2)}) collective-permute-start(bf16[64,512]{1,0:T(8,128)(2,1)S(1)} %get-tuple-element.66), channel_id=1, source_target_pairs={{0,20},{4,16},{8,28},{12,24},{16,4},{20,0},{24,12},{28,8},{1,21},{... | collective-permute-start | bytes 196616 | tf_op jit(solution)/shard_map/ppermute | solution.py:348
  13.9 14.3 %collective-permute-start.9 = (bf16[64,512]{1,0:T(8,128)(2,1)S(1)}, bf16[64,512]{1,0:T(8,128)(2,1)S(1)}, u32[]{:S(2)}, u32[]{:S(2)}) collective-permute-start(bf16[64,512]{1,0:T(8,128)(2,1)S(1)} %get-tuple-element.67), channel_id=1, source_target_pairs={{0,24},{4,28},{8,16},{12,20},{16,8},{20,12},{24,0},{28,4},{1,25},{... | collective-permute-start | bytes 196616 | tf_op jit(solution)/shard_map/ppermute | solution.py:348
  16.9 13.2 %collective-permute-start.10 = (bf16[64,512]{1,0:T(8,128)(2,1)S(1)}, bf16[64,512]{1,0:T(8,128)(2,1)S(1)}, u32[]{:S(2)}, u32[]{:S(2)}) collective-permute-start(bf16[64,512]{1,0:T(8,128)(2,1)S(1)} %get-tuple-element.68), channel_id=1, source_target_pairs={{0,28},{4,24},{8,20},{12,16},{16,12},{20,8},{24,4},{28,0},{1,29},{... | collective-permute-start | bytes 196616 | tf_op jit(solution)/shard_map/ppermute | solution.py:348
  27.0 25.0 %collective-permute-start.2 = (bf16[1024,512]{1,0:T(8,128)(2,1)S(1)}, bf16[1024,512]{1,0:T(8,128)(2,1)S(1)}, u32[]{:S(2)}, u32[]{:S(2)}) collective-permute-start(bf16[1024,512]{1,0:T(8,128)(2,1)S(1)} %collective-permute-done.1.refs_2_), channel_id=1, source_target_pairs={{0,1},{1,0},{2,3},{3,2},{4,5},{5,4},{6,7},{7,6},{8,9},{9,8},{10,11... | collective-permute-start | bytes 3145736 | tf_op jit(solution)/shard_map/ppermute | solution.py:342
  36.8 13.4 %collective-permute-start.12 = (bf16[512,512]{1,0:T(8,128)(2,1)S(1)}, bf16[512,512]{1,0:T(8,128)(2,1)S(1)}, u32[]{:S(2)}, u32[]{:S(2)}) collective-permute-start(bf16[512,512]{1,0:T(8,128)(2,1)S(1)} %constant_dynamic-update-slice_fusion.refs_1_), channel_id=1, source_target_pairs={{0,2},{1,3},{2,0},{3,1},{4,6},{5,7},{6,4},{7,5},{8,10},{9,11},{10,... | collective-permute-start | bytes 1572872 | tf_op jit(solution)/shard_map/ppermute | solution.py:342
  45.4 59.1 %collective-permute-start.32 = (bf16[512,2048]{1,0:T(8,128)(2,1)S(1)}, bf16[512,2048]{1,0:T(8,128)(2,1)S(1)}, u32[]{:S(2)}, u32[]{:S(2)}) collective-permute-start(bf16[512,2048]{1,0:T(8,128)(2,1)S(1)} %copy-done.5), channel_id=1, source_target_pairs={{0,1},{1,0},{2,3},{3,2},{4,5},{5,4},{6,7},{7,6},{8,9},{9,8},{10,11... | collective-permute-start | bytes 6291464 | tf_op jit(solution)/shard_map/ppermute | solution.py:342
  50.1 11.3 %collective-permute-start.11 = (bf16[512,512]{1,0:T(8,128)(2,1)S(1)}, bf16[512,512]{1,0:T(8,128)(2,1)S(1)}, u32[]{:S(2)}, u32[]{:S(2)}) collective-permute-start(bf16[512,512]{1,0:T(8,128)(2,1)S(1)} %constant_dynamic-update-slice_fusion.refs_1_), channel_id=1, source_target_pairs={{0,1},{1,0},{2,3},{3,2},{4,5},{5,4},{6,7},{7,6},{8,9},{9,8},{10,11... | collective-permute-start | bytes 1572872 | tf_op jit(solution)/shard_map/ppermute | solution.py:342
  50.2 14.4 %collective-permute-start.29 = (bf16[512,512]{1,0:T(8,128)(2,1)S(1)}, bf16[512,512]{1,0:T(8,128)(2,1)S(1)}, u32[]{:S(2)}, u32[]{:S(2)}) collective-permute-start(bf16[512,512]{1,0:T(8,128)(2,1)S(1)} %constant_dynamic-update-slice_fusion.8.refs_1_), channel_id=1, source_target_pairs={{0,2},{1,3},{2,0},{3,1},{4,6},{5,7},{6,4},{7,5},{8,10},{9,11},{10,... | collective-permute-start | bytes 1572872 | tf_op jit(solution)/shard_map/ppermute | solution.py:342
  51.7 12.8 %collective-permute-start.13 = (bf16[512,512]{1,0:T(8,128)(2,1)S(1)}, bf16[512,512]{1,0:T(8,128)(2,1)S(1)}, u32[]{:S(2)}, u32[]{:S(2)}) collective-permute-start(bf16[512,512]{1,0:T(8,128)(2,1)S(1)} %collective-permute-done.12.refs_3_), channel_id=1, source_target_pairs={{0,1},{1,0},{2,3},{3,2},{4,5},{5,4},{6,7},{7,6},{8,9},{9,8},{10,11... | collective-permute-start | bytes 1572872 | tf_op jit(solution)/shard_map/ppermute | solution.py:342
  53.2 14.0 %collective-permute-start.4 = (bf16[512,512]{1,0:T(8,128)(2,1)S(1)}, bf16[512,512]{1,0:T(8,128)(2,1)S(1)}, u32[]{:S(2)}, u32[]{:S(2)}) collective-permute-start(bf16[512,512]{1,0:T(8,128)(2,1)S(1)} %project_halo.1.refs_7_), channel_id=1, source_target_pairs={{0,4},{4,8},{8,12},{12,16},{16,20},{20,24},{24,28},{1,5},{5,9},{9,... | collective-permute-start | bytes 1572872 | tf_op jit(solution)/shard_map/ppermute | solution.py:372
  61.4 16.5 %collective-permute-start.28 = (bf16[512,512]{1,0:T(8,128)(2,1)S(1)}, bf16[512,512]{1,0:T(8,128)(2,1)S(1)}, u32[]{:S(2)}, u32[]{:S(2)}) collective-permute-start(bf16[512,512]{1,0:T(8,128)(2,1)S(1)} %constant_dynamic-update-slice_fusion.8.refs_1_), channel_id=1, source_target_pairs={{0,1},{1,0},{2,3},{3,2},{4,5},{5,4},{6,7},{7,6},{8,9},{9,8},{10,11... | collective-permute-start | bytes 1572872 | tf_op jit(solution)/shard_map/ppermute | solution.py:342
  64.5 20.5 %collective-permute-start.30 = (bf16[512,512]{1,0:T(8,128)(2,1)S(1)}, bf16[512,512]{1,0:T(8,128)(2,1)S(1)}, u32[]{:S(2)}, u32[]{:S(2)}) collective-permute-start(bf16[512,512]{1,0:T(8,128)(2,1)S(1)} %collective-permute-done.29.refs_3_), channel_id=1, source_target_pairs={{0,1},{1,0},{2,3},{3,2},{4,5},{5,4},{6,7},{7,6},{8,9},{9,8},{10,11... | collective-permute-start | bytes 1572872 | tf_op jit(solution)/shard_map/ppermute | solution.py:342
  73.6 13.3 %collective-permute-start.14 = (bf16[272,128]{1,0:T(8,128)(2,1)S(1)}, bf16[272,128]{1,0:T(8,128)(2,1)S(1)}, u32[]{:S(2)}, u32[]{:S(2)}) collective-permute-start(bf16[272,128]{1,0:T(8,128)(2,1)S(1)} %get-tuple-element.72), channel_id=1, source_target_pairs={{0,4},{4,0},{8,12},{12,8},{16,20},{20,16},{24,28},{28,24},{1,5},{5... | collective-permute-start | bytes 208904 | tf_op jit(solution)/shard_map/ppermute | solution.py:348
  76.2 11.9 %collective-permute-start.15 = (bf16[272,128]{1,0:T(8,128)(2,1)S(1)}, bf16[272,128]{1,0:T(8,128)(2,1)S(1)}, u32[]{:S(2)}, u32[]{:S(2)}) collective-permute-start(bf16[272,128]{1,0:T(8,128)(2,1)S(1)} %get-tuple-element.73), channel_id=1, source_target_pairs={{0,8},{4,12},{8,0},{12,4},{16,24},{20,28},{24,16},{28,20},{1,9},{5... | collective-permute-start | bytes 208904 | tf_op jit(solution)/shard_map/ppermute | solution.py:348
  77.9 12.8 %collective-permute-start.16 = (bf16[272,128]{1,0:T(8,128)(2,1)S(1)}, bf16[272,128]{1,0:T(8,128)(2,1)S(1)}, u32[]{:S(2)}, u32[]{:S(2)}) collective-permute-start(bf16[272,128]{1,0:T(8,128)(2,1)S(1)} %get-tuple-element.74), channel_id=1, source_target_pairs={{0,12},{4,8},{8,4},{12,0},{16,28},{20,24},{24,20},{28,16},{1,13},{... | collective-permute-start | bytes 208904 | tf_op jit(solution)/shard_map/ppermute | solution.py:348
  85.1 14.3 %collective-permute-start.17 = (bf16[272,128]{1,0:T(8,128)(2,1)S(1)}, bf16[272,128]{1,0:T(8,128)(2,1)S(1)}, u32[]{:S(2)}, u32[]{:S(2)}) collective-permute-start(bf16[272,128]{1,0:T(8,128)(2,1)S(1)} %get-tuple-element.75), channel_id=1, source_target_pairs={{0,16},{4,20},{8,24},{12,28},{16,0},{20,4},{24,8},{28,12},{1,17},{... | collective-permute-start | bytes 208904 | tf_op jit(solution)/shard_map/ppermute | solution.py:348
  87.0 12.5 %collective-permute-start.18 = (bf16[272,128]{1,0:T(8,128)(2,1)S(1)}, bf16[272,128]{1,0:T(8,128)(2,1)S(1)}, u32[]{:S(2)}, u32[]{:S(2)}) collective-permute-start(bf16[272,128]{1,0:T(8,128)(2,1)S(1)} %get-tuple-element.76), channel_id=1, source_target_pairs={{0,20},{4,16},{8,28},{12,24},{16,4},{20,0},{24,12},{28,8},{1,21},{... | collective-permute-start | bytes 208904 | tf_op jit(solution)/shard_map/ppermute | solution.py:348
  88.1 11.4 %collective-permute-start.19 = (bf16[272,128]{1,0:T(8,128)(2,1)S(1)}, bf16[272,128]{1,0:T(8,128)(2,1)S(1)}, u32[]{:S(2)}, u32[]{:S(2)}) collective-permute-start(bf16[272,128]{1,0:T(8,128)(2,1)S(1)} %get-tuple-element.77), channel_id=1, source_target_pairs={{0,24},{4,28},{8,16},{12,20},{16,8},{20,12},{24,0},{28,4},{1,25},{... | collective-permute-start | bytes 208904 | tf_op jit(solution)/shard_map/ppermute | solution.py:348
  103.7 10.6 %collective-permute-start.36 = (bf16[272,128]{1,0:T(8,128)(2,1)S(1)}, bf16[272,128]{1,0:T(8,128)(2,1)S(1)}, u32[]{:S(2)}, u32[]{:S(2)}) collective-permute-start(bf16[272,128]{1,0:T(8,128)(2,1)S(1)} %get-tuple-element.96), channel_id=1, source_target_pairs={{0,12},{4,8},{8,4},{12,0},{16,28},{20,24},{24,20},{28,16},{1,13},{... | collective-permute-start | bytes 208904 | tf_op jit(solution)/shard_map/ppermute | solution.py:348
  106.7 10.8 %collective-permute-start.38 = (bf16[272,128]{1,0:T(8,128)(2,1)S(1)}, bf16[272,128]{1,0:T(8,128)(2,1)S(1)}, u32[]{:S(2)}, u32[]{:S(2)}) collective-permute-start(bf16[272,128]{1,0:T(8,128)(2,1)S(1)} %get-tuple-element.98), channel_id=1, source_target_pairs={{0,20},{4,16},{8,28},{12,24},{16,4},{20,0},{24,12},{28,8},{1,21},{... | collective-permute-start | bytes 208904 | tf_op jit(solution)/shard_map/ppermute | solution.py:348
  119.0 14.8 %collective-permute-start.33 = (bf16[128,2048]{1,0:T(8,128)(2,1)S(1)}, bf16[128,2048]{1,0:T(8,128)(2,1)S(1)}, u32[]{:S(2)}, u32[]{:S(2)}) collective-permute-start(bf16[128,2048]{1,0:T(8,128)(2,1)S(1)} %get-tuple-element.92), channel_id=1, source_target_pairs={{0,2},{1,3},{2,0},{3,1},{4,6},{5,7},{6,4},{7,5},{8,10},{9,11},{10,... | collective-permute-start | bytes 1572872 | tf_op jit(solution)/shard_map/ppermute | solution.py:342
  122.4 22.2 %collective-permute-start.42 = (bf16[128,2048]{1,0:T(8,128)(2,1)S(1)}, bf16[128,2048]{1,0:T(8,128)(2,1)S(1)}, u32[]{:S(2)}, u32[]{:S(2)}) collective-permute-start(bf16[128,2048]{1,0:T(8,128)(2,1)S(1)} %get-tuple-element.104), channel_id=1, source_target_pairs={{0,2},{1,3},{2,0},{3,1},{4,6},{5,7},{6,4},{7,5},{8,10},{9,11},{10,... | collective-permute-start | bytes 1572872 | tf_op jit(solution)/shard_map/ppermute | solution.py:342
  (25 other events, 246.5 us)

commit v4 on v3

--- a/solution.py
+++ b/solution.py
@@ -61,30 +61,44 @@
     return lax.dot_general(a, b, (((0,), (0,)), ((), ())), preferred_element_type=F32)
 
 
-def pack_kernel(pos_ref, tok_ref, *out_refs):
-    owners = len(out_refs) // CHUNKS
+def pack_kernel(tok_hbm, *rest):
+    out_refs, (tok_ref, sems) = rest[:-2], rest[-2:]
+    owners = out_refs[0].shape[0]
     per_owner = STRIDE // owners
     groups = per_owner // SUB
     per_chunk = groups // CHUNKS
-    for k in range(owners):
-        d = pos_ref[0] ^ k
+    spans = [slice(r * STRIDE, (r + 1) * STRIDE) for r in range(ROWS)]
+    copies = [
+        pltpu.make_async_copy(tok_hbm.at[at], tok_ref.at[at], sems.at[r])
+        for r, at in enumerate(spans)
+    ]
+    for c in copies:
+        c.start()
+    for c in copies:
+        c.wait()
+    for d in range(owners):
         rows = [
-            tok_ref[pl.ds(pl.multiple_of(r * STRIDE + d * per_owner, per_owner), per_owner), :]
+            tok_ref[r * STRIDE + d * per_owner : r * STRIDE + (d + 1) * per_owner, :].astype(F32)
             for r in range(ROWS)
         ]
-        rows = [x.astype(F32) for x in rows]
         for g in range(groups):
             piece = jnp.concatenate([x[g * SUB : (g + 1) * SUB] for x in rows], 0)
             at = (g % per_chunk) * ROWS * SUB
-            out = out_refs[(g // per_chunk) * owners + k]
-            out[at : at + ROWS * SUB, :] = piece.astype(BF16)
-
-
-def pack(pos, tokens, owners):
+            out_refs[g // per_chunk][d, at : at + ROWS * SUB, :] = piece.astype(BF16)
+
+
+def pack(tokens, owners):
     message = tokens.shape[0] // owners // CHUNKS
-    shapes = [shape((message, tokens.shape[1]))] * (CHUNKS * owners)
-    outs = call(pack_kernel, "pack_tokens", 2, shapes, (pos, tokens))
-    return [outs[i * owners : (i + 1) * owners] for i in range(CHUNKS)]
+    return pl.pallas_call(
+        pack_kernel,
+        in_specs=[ANYWHERE],
+        out_specs=[IN_VMEM] * CHUNKS,
+        out_shape=[shape((owners, message, tokens.shape[1]))] * CHUNKS,
+        scratch_shapes=[pltpu.VMEM(tokens.shape, BF16), pltpu.SemaphoreType.DMA((ROWS,))],
+        compiler_params=pltpu.CompilerParams(vmem_limit_bytes=8 * MIB),
+        cost_estimate=pl.CostEstimate(flops=0, bytes_accessed=2 * MIB, transcendentals=0),
+        name="pack_tokens",
+    )(tokens)
 
 
 def stage_kernel(order_ref, wq, wk, wv, oq, ok, ov, sems):
@@ -102,19 +116,19 @@
 
 
 def stage(order, weights, after):
-    def body(order_ref, wq, wk, wv, _, *rest):
-        stage_kernel(order_ref, wq, wk, wv, *rest)
+    def body(order_ref, wq, wk, wv, *rest):
+        stage_kernel(order_ref, wq, wk, wv, *rest[len(after) :])
 
     return pl.pallas_call(
         body,
-        in_specs=[IN_SMEM] + [ANYWHERE] * 4,
+        in_specs=[IN_SMEM] + [ANYWHERE] * (3 + len(after)),
         out_specs=[IN_VMEM] * 3,
         out_shape=[shape(w.shape) for w in weights],
         scratch_shapes=[pltpu.SemaphoreType.DMA((12,))],
         compiler_params=pltpu.CompilerParams(vmem_limit_bytes=16 * MIB),
         cost_estimate=pl.CostEstimate(flops=0, bytes_accessed=6 * MIB, transcendentals=0),
         name="stage_weights",
-    )(order, *weights, after)
+    )(order, *weights, *after)
 
 
 def gathered(x_refs, at, w_ref):
@@ -190,7 +204,7 @@
                 total = None
                 for d in range(owners):
                     at = ((d * CHUNKS + i) * groups + g) * SUB
-                    moved = pltpu.roll(turned[at : at + SUB], 8 * (block ^ d), 1)
+                    moved = pltpu.roll(turned[at : at + SUB], 8 * d, 1)
                     total = moved if total is None else total + moved
                 to = (g * ROWS + r) * SUB
                 lse_refs[i][to : to + SUB, :] = total
@@ -204,8 +218,7 @@
     return list(zip(outs[:CHUNKS], outs[CHUNKS:]))
 
 
-def column_kernel(pos_ref, x0, x1, x2, x3, wq, wk, wv, *rest):
-    out_refs, scratch = rest[:-3], rest[-3:]
+def column_kernel(x0, x1, x2, x3, wq, wk, wv, out_ref, *scratch):
     owners, message, _ = scratch[0].shape
     groups = message // (ROWS * SUB)
     everything = slice(0, owners * message)
@@ -214,12 +227,9 @@
     part = ROWS * SUB
     size = owners * part
 
-    def row_and_class(dim):
-        i = lax.broadcasted_iota(jnp.int32, (size, size), dim)
-        return ((i // part) ^ pos_ref[0]) * ROWS + (i % part) // SUB, i % SUB
-
-    (row_j, class_j), (row_i, class_i) = row_and_class(0), row_and_class(1)
-    earlier = jnp.logical_and(class_i == class_j, row_i > row_j)
+    j = lax.broadcasted_iota(jnp.int32, (size, size), 0)
+    i = lax.broadcasted_iota(jnp.int32, (size, size), 1)
+    earlier = jnp.logical_and(i % SUB == j % SUB, i > j)
     stats = []
     for g in range(groups):
         at = slice(g * part, (g + 1) * part)
@@ -230,8 +240,7 @@
             p, total, lse = softmax_columns(jnp.where(earlier, dot_t(k, q), -1e30))
             o = (dot_l(v, p.astype(BF16)) * (1.0 / total)).T.astype(BF16)
             rows = slice(h * message + g * part, h * message + (g + 1) * part)
-            for n in range(owners):
-                out_refs[n][rows, :] = o[n * part : (n + 1) * part]
+            out_ref[:, rows, :] = o.reshape(owners, part, DH)
             lses.append(lse)
         stats.append(jnp.concatenate(lses + lses, 0))
     upper = lax.broadcasted_iota(jnp.int32, (8, 128), 0) < HEADS
@@ -242,25 +251,24 @@
         mid = (x - hi).astype(BF16).astype(F32)
         lo = x - hi - mid
         tail = jnp.concatenate([jnp.where(upper, hi, lo), jnp.where(upper, mid, 0.0)], 0)
-        out_refs[n][HEADS * message : HEADS * message + 16, :] = tail.astype(BF16)
-
-
-def column_part(pos, pieces, weights, owners, after):
-    tokens, width = pieces[0].shape
-    message = tokens // owners
-    shapes = [shape((HEADS * message + 16, DH))] * owners
+        out_ref[n, HEADS * message : HEADS * message + 16, :] = tail.astype(BF16)
+
+
+def column_part(pieces, weights, after):
+    owners, message, width = pieces[0].shape
+    dims = shape((owners, HEADS * message + 16, DH))
     scratch = [pltpu.VMEM((owners, message, width), BF16)] * 3
-    return call(column_kernel, "column_part", 6, shapes, (pos, *pieces, *weights), after, scratch)
-
-
-def mix_kernel(pos_ref, loc_ref, lse_ref, *rest):
-    col_refs, (own_ref, send_ref, mixed) = rest[:-3], rest[-3:]
+    pieces = [x.reshape(owners * message, width) for x in pieces]
+    return call(column_kernel, "column_part", 6, dims, (*pieces, *weights), after, scratch)
+
+
+def mix_kernel(pos_ref, loc_ref, lse_ref, col_ref, own_ref, send_ref, mixed):
     owners, message, _ = loc_ref.shape
     groups = message // (ROWS * SUB)
     base = HEADS * message
     tiles = []
-    for col_ref in col_refs:
-        tail = col_ref[base : base + 16, :].astype(F32)
+    for d in range(owners):
+        tail = col_ref[d, base : base + 16, :].astype(F32)
         tiles.append(tail[:8] + tail[8:])
     tiles.append(jnp.zeros((128 - 8 * owners, 128), F32))
     turned = jnp.concatenate(tiles, 0).T[:message]
@@ -273,13 +281,12 @@
     w_col = w_col * share
     w_loc = w_loc * share
     span = groups * SUB
-    for k, col_ref in enumerate(col_refs):
-        d = pos_ref[0] ^ k
-        spot = pl.ds(pl.multiple_of(d * span, span), span)
+    for d in range(owners):
+        spot = slice(d * span, (d + 1) * span)
         for h in range(HEADS):
             cols = slice(h * DH, (h + 1) * DH)
-            at = slice(8 * k + h, 8 * k + h + 1)
-            col = col_ref[h * message : (h + 1) * message, :].astype(F32)
+            at = slice(8 * d + h, 8 * d + h + 1)
+            col = col_ref[d, h * message : (h + 1) * message, :].astype(F32)
             both = loc_ref[d, :, cols] * w_loc[:, at] + col * w_col[:, at]
             for r in range(ROWS):
                 starts = [(g * ROWS + r) * SUB for g in range(groups)]
@@ -291,12 +298,12 @@
         send_ref[x] = mixed[2 * x + 1 - core]
 
 
-def mix(pos, columns, local, lse, after):
+def mix(pos, column, local, lse, after):
     owners, message, width = local.shape
     tokens = owners * message // ROWS
     shapes = [shape((2, tokens, width))] * 2
     scratch = [pltpu.VMEM((ROWS, tokens, width), BF16)]
-    return call(mix_kernel, "mix", 3, shapes, (pos, local, lse, *columns), after, scratch)
+    return call(mix_kernel, "mix", 2, shapes, (pos, local, lse, column), after, scratch)
 
 
 def out_kernel(pos_ref, a_ref, b_ref, wa_ref, wb_ref, send_ref, keep_ref):
@@ -343,10 +350,7 @@
 
 
 def exchange(messages):
-    n = len(messages)
-    return [messages[0]] + [
-        lax.ppermute(messages[k], "seq", [(i, i ^ k) for i in range(n)]) for k in range(1, n)
-    ]
+    return lax.all_to_all(messages, "seq", split_axis=0, concat_axis=0, tiled=True)
 
 
 def gather(own):
@@ -363,8 +367,9 @@
     rows, width = tokens.shape
 
     pieces = gather(tokens)
-    classes = [exchange(m) for m in pack(pos, tokens, owners)]
-    weights = stage(order, (w_query, w_key, w_value), classes[0][1])
+    messages = pack(tokens, owners)
+    classes = [exchange(m) for m in messages]
+    weights = stage(order, (w_query, w_key, w_value), (messages[0], pieces[1]))
     w_other = swap(w_out, 1)
     own_halo = call(
         halo_kernel, "project_halo", 1.5, shape((2 * STRIDE, width)), (*pieces, *weights[1:])
@@ -377,19 +382,18 @@
         [shape((rows, width))] * 3,
         (*pieces, *weights, own_halo),
     )
-    columns, after = [], (q, halo)
-    for i, messages in enumerate(classes):
-        class_pieces = gather(jnp.concatenate(messages, 0))
-        columns.append(column_part(pos, class_pieces, weights, owners, after))
+    columns, after = [], (q,)
+    for i, c in enumerate(classes):
+        columns.append(column_part(gather(c), weights, after))
         if i == 0:
-            locals_ = local_part(pos, q, k, v, halo, owners, (columns[0][0],))
+            locals_ = local_part(pos, q, k, v, halo, owners, (columns[0],))
             after = (locals_[-1][-1],)
-    pairs, after = [], (columns[-1][0],)
+    pairs, after = [], (columns[-1],)
     for column, (local, lse) in zip(columns, locals_):
         own, send = mix(pos, exchange(column), local, lse, after)
         out, keep = out_project(pos, own, swap(send, 1), w_out, w_other)
-        after = (keep,)
         pairs.append((keep, swap(out, 2)))
+        after = (pairs[-1][1],)
     return join(pairs)
 
 

time: 146 us -> 158 us (1.082)
  starting transfers between devices: 67.4 us -> 34.5 us
  waiting for transfers between devices: 41.6 us -> 61.2 us
  local copies, waits for them, and re-layouts: 1.34 us -> 16.3 us
  Pallas kernels: 35 us -> 44.8 us
    ppermute x28 -> x0, starting transfers between devices: 57 us -> none  [exchange(): lax.ppermute(messages[k], 'seq', [(i, i ^ k) for i in range(n)])]
    all_to_all x0 -> x4, waiting for transfers between devices: none -> 30.1 us  [exchange(): lax.all_to_all(messages, 'seq', split_axis=0, concat_axis=0, tiled=True)]
    all_to_all x0 -> x4, starting transfers between devices: none -> 22 us  [exchange(): lax.all_to_all(messages, 'seq', split_axis=0, concat_axis=0, tiled=True)]
    unnamed x26 -> x52, local copies, waits for them, and re-layouts: 1.32 us -> 16.3 us
    ppermute x28 -> x0, waiting for transfers between devices: 9.35 us -> none  [exchange(): lax.ppermute(messages[k], 'seq', [(i, i ^ k) for i in range(n)])]
    pallas_call x11 -> x10, Pallas kernels: 33.9 us -> 42.5 us  [call(): pl.pallas_call(run, in_specs=specs + [ANYWHERE] * extra, out_specs=jax.tr...]
    ppermute x1, waiting for transfers between devices: 2.68 us -> 0.01 us  [chunked(): lax.ppermute(own_halo, 'seq', [(i, i + 1) for i in range(owners - 1)])]
  transfers between devices with their start and end apart: 43 -> 19, of which waited for: 11 -> 8; matrix products, arithmetic and copies ran while one was open for 0% -> 0% of each run, Pallas kernels for 22% -> 24%
where the time goes in v4:
time: 158 us; the launch traced here: 157 us
  waiting for transfers between devices  61.2 us (39%)
  Pallas kernels  44.8 us (28%)
  starting transfers between devices  34.5 us (22%)
  local copies, waits for them, and re-layouts  16.3 us (10%)
    pallas_call x10, Pallas kernels, call(): pl.pallas_call(run, in_specs=specs + [ANYWHERE] * extra, out_specs=jax.tr...  42.5 us
    ppermute x14, waiting for transfers between devices, swap(): return lax.ppermute(value, 'head', [(i, i ^ distance) for i in range(4)])  31 us
    all_to_all x4, waiting for transfers between devices, exchange(): lax.all_to_all(messages, 'seq', split_axis=0, concat_axis=0, tiled=True)  30.1 us
    all_to_all x4, starting transfers between devices, exchange(): lax.all_to_all(messages, 'seq', split_axis=0, concat_axis=0, tiled=True)  22 us
    unnamed x52, local copies, waits for them, and re-layouts  16.3 us
    ppermute x14, starting transfers between devices, swap(): return lax.ppermute(value, 'head', [(i, i ^ distance) for i in range(4)])  8.91 us
    ppermute x1, starting transfers between devices, chunked(): lax.ppermute(own_halo, 'seq', [(i, i + 1) for i in range(owners - 1)])  3.6 us
  transfers between devices with their start and end apart: 19, of which 8 were waited for; matrix products, arithmetic and copies ran while one was open for 0% of the time, Pallas kernels for 24%

profile of v4, /device:TPU:0, one launch (start us, length us, event | category | flops | bytes accessed | tf_op | source)
XLA Modules:
  0.0 157.1 jit_solution(16396221879294076676)
XLA Ops:
  2.4 7.3 %all-to-all-start = ((bf16[8,64,512]{2,1,0:T(8,128)(2,1)}), bf16[8,64,512]{2,1,0:T(8,128)(2,1)S(1)}, u32[]{:S(2)}, u32[]{:S(2)}) async-start(bf16[8,64,512]{2,1,0:T(8,128)(2,1)} %get-tuple-element.25.rest_0_), calls=%async_computation | async-start | bytes 1048576 | tf_op jit(solution)/shard_map/all_to_all | solution.py:353
  9.7 1.6 collective-permute-start.1
  11.2 12.9 %all-to-all-done = bf16[8,64,512]{2,1,0:T(8,128)(2,1)S(1)} async-done(((bf16[8,64,512]{2,1,0:T(8,128)(2,1)}), bf16[8,64,512]{2,1,0:T(8,128)(2,1)S(1)}, u32[]{:S(2)}, u32[]{:S(2)}) %all-to-all-start) | async-done | bytes 524320 | tf_op jit(solution)/shard_map/all_to_all | solution.py:353
  25.0 4.1 %all-to-all-start.2 = ((bf16[8,64,512]{2,1,0:T(8,128)(2,1)}), bf16[8,64,512]{2,1,0:T(8,128)(2,1)}, u32[]{:S(2)}, u32[]{:S(2)}) async-start(bf16[8,64,512]{2,1,0:T(8,128)(2,1)} %get-tuple-element.34), calls=%async_computation.2 | async-start | bytes 1048576 | tf_op jit(solution)/shard_map/all_to_all | solution.py:353
  29.2 5.2 %collective-permute-done.1.refs_2_ = bf16[1024,512]{1,0:T(8,128)(2,1)S(1)} collective-permute-done((bf16[1024,512]{1,0:T(8,128)(2,1)S(1)}, bf16[1024,512]{1,0:T(8,128)(2,1)S(1)}, u32[]{:S(2)}, u32[]{:S(2)}) %collective-permute-start.1) | collective-permute-done | bytes 1048608 | tf_op jit(solution)/shard_map/ppermute | solution.py:349
  35.9 7.5 %all-to-all-done.2 = bf16[8,64,512]{2,1,0:T(8,128)(2,1)} async-done(((bf16[8,64,512]{2,1,0:T(8,128)(2,1)}), bf16[8,64,512]{2,1,0:T(8,128)(2,1)}, u32[]{:S(2)}, u32[]{:S(2)}) %all-to-all-start.2) | async-done | bytes 524320 | tf_op jit(solution)/shard_map/all_to_all | solution.py:353
  45.5 1.6 %copy-done.6 = bf16[2048,512]{1,0:T(8,128)(2,1)S(1)} copy-done((bf16[2048,512]{1,0:T(8,128)(2,1)S(1)}, bf16[2048,512]{1,0:T(8,128)(2,1)}, u32[]{:S(2)}) %copy-start.6) | copy-done | bytes 2097176
  47.1 1.6 %copy-done.7 = bf16[2048,512]{1,0:T(8,128)(2,1)S(1)} copy-done((bf16[2048,512]{1,0:T(8,128)(2,1)S(1)}, bf16[2048,512]{1,0:T(8,128)(2,1)}, u32[]{:S(2)}) %copy-start.7) | copy-done | bytes 2097176
  48.7 1.6 %copy-done.8 = bf16[2048,512]{1,0:T(8,128)(2,1)S(1)} copy-done((bf16[2048,512]{1,0:T(8,128)(2,1)S(1)}, bf16[2048,512]{1,0:T(8,128)(2,1)}, u32[]{:S(2)}) %copy-start.8) | copy-done | bytes 2097176
  51.5 8.7 %collective-permute-done.8 = bf16[8,64,512]{2,1,0:T(8,128)(2,1)} collective-permute-done((bf16[8,64,512]{2,1,0:T(8,128)(2,1)}, bf16[8,64,512]{2,1,0:T(8,128)(2,1)}, u32[]{:S(2)}, u32[]{:S(2)}) %collective-permute-start.8) | collective-permute-done | bytes 524320 | tf_op jit(solution)/shard_map/ppermute | solution.py:349
  60.8 3.3 %project_halo.1.refs_7_ = bf16[512,512]{1,0:T(8,128)(2,1)} custom-call(bf16[1024,512]{1,0:T(8,128)(2,1)S(1)} %copy-done.1, bf16[1024,512]{1,0:T(8,128)(2,1)S(1)} %collective-permute-done.rest_1_.refs_1_, bf16[1024,512]{1,0:T(8,128)(2,1)S(1)} %collective-permute-done.1.refs_2_, bf16[1024,512]{1,0:T(8,128)(2,1)} %collective-permute-done.2.refs_3_, ...), custom_call_target="tpu_custom_call" | custom-call | flops 1650000000 | bytes 1048576 | tf_op jit(solution)/shard_map/project_halo/pallas_call | solution.py:34
  64.1 7.0 %project_block.1 = (bf16[1024,512]{1,0:T(8,128)(2,1)S(1)}, bf16[1024,512]{1,0:T(8,128)(2,1)S(1)}, bf16[1024,512]{1,0:T(8,128)(2,1)S(1)}) custom-call(bf16[1024,512]{1,0:T(8,128)(2,1)S(1)} %copy-done.1, bf16[1024,512]{1,0:T(8,128)(2,1)S(1)} %collective-permute-done.rest_1_.refs_1_, bf16[1024,512]{1,0:T(8,128)(2,1)S(1)} %collective-permute-done.1.refs_2_, ...), custom_call_target="tpu_custom_call" | custom-call | flops 7699999744 | bytes 1048576 | tf_op jit(solution)/shard_map/project_block/pallas_call | solution.py:34
  73.0 3.6 %collective-permute-start.3 = (bf16[512,512]{1,0:T(8,128)(2,1)}, bf16[512,512]{1,0:T(8,128)(2,1)S(1)}, u32[]{:S(2)}, u32[]{:S(2)}) collective-permute-start(bf16[512,512]{1,0:T(8,128)(2,1)} %project_halo.1.refs_7_), channel_id=1, source_target_pairs={{0,4},{4,8},{8,12},{12,16},{16,20},{20,24},{24,28},{1,5},{5,9},{9,... | collective-permute-start | bytes 1572872 | tf_op jit(solution)/shard_map/ppermute | solution.py:377
  76.7 7.7 %column_part.2.refs_5_ = bf16[8,272,128]{2,1,0:T(8,128)(2,1)} custom-call(bf16[512,512]{1,0:T(8,128)(2,1)S(1)} %bitcast.11, bf16[512,512]{1,0:T(8,128)(2,1)S(1)} %bitcast.12, bf16[512,512]{1,0:T(8,128)(2,1)} %bitcast.5.refs_2_, bf16[512,512]{1,0:T(8,128)(2,1)S(1)} %bitcast.13, bf16[2048,512]{1,0:T(8,128)(2,1)S(1)} %get-tuple-element.26.refs_4_, ...), custom_call_target="tpu_custom_call" | custom-call | flops 6600000000 | bytes 1048576 | tf_op jit(solution)/shard_map/column_part/pallas_call | solution.py:34
  85.4 4.5 %all-to-all-start.1 = ((bf16[8,272,128]{2,1,0:T(8,128)(2,1)}), bf16[8,272,128]{2,1,0:T(8,128)(2,1)S(1)}, u32[]{:S(2)}, u32[]{:S(2)}) async-start(bf16[8,272,128]{2,1,0:T(8,128)(2,1)} %column_part.2.refs_5_), calls=%async_computation.1 | async-start | bytes 1114112 | tf_op jit(solution)/shard_map/all_to_all | solution.py:353
  91.2 5.8 %local_part.1 = (f32[8,64,512]{2,1,0:T(8,128)S(1)}, f32[8,64,512]{2,1,0:T(8,128)S(1)}, f32[64,128]{1,0:T(8,128)S(1)}, f32[64,128]{1,0:T(8,128)S(1)}) custom-call(s32[3]{0:T(128)S(1)} %pad_add_fusion.refs_0_, bf16[1024,512]{1,0:T(8,128)(2,1)S(1)} %copy-done.21, bf16[1024,512]{1,0:T(8,128)(2,1)S(1)} %copy-done.23, bf16[1024,512]{1,0:T(8,128)(2,1)S(1)} %copy-done.25, ...), custom_call_target="tpu_custom_call" | custom-call | flops 5500000256 | bytes 1048576 | tf_op jit(solution)/shard_map/local_part/pallas_call | solution.py:34
  98.9 8.1 %column_part.3.refs_4_ = bf16[8,272,128]{2,1,0:T(8,128)(2,1)} custom-call(bf16[512,512]{1,0:T(8,128)(2,1)} %bitcast.7.refs_0_, bf16[512,512]{1,0:T(8,128)(2,1)} %bitcast.8.refs_1_, bf16[512,512]{1,0:T(8,128)(2,1)} %bitcast.9.refs_2_, bf16[512,512]{1,0:T(8,128)(2,1)} %bitcast.10.refs_3_, bf16[2048,512]{1,0:T(8,128)(2,1)S(1)} %copy-done.13, ...), custom_call_target="tpu_custom_call" | custom-call | flops 6600000000 | bytes 1048576 | tf_op jit(solution)/shard_map/column_part/pallas_call | solution.py:34
  109.7 6.0 %all-to-all-start.3 = ((bf16[8,272,128]{2,1,0:T(8,128)(2,1)}), bf16[8,272,128]{2,1,0:T(8,128)(2,1)S(1)}, u32[]{:S(2)}, u32[]{:S(2)}) async-start(bf16[8,272,128]{2,1,0:T(8,128)(2,1)} %column_part.3.refs_4_), calls=%async_computation.3 | async-start | bytes 1114112 | tf_op jit(solution)/shard_map/all_to_all | solution.py:353
  115.7 3.7 %out_project.2 = (bf16[128,2048]{1,0:T(8,128)(2,1)}, f32[128,2048]{1,0:T(8,128)S(1)}) custom-call(s32[3]{0:T(128)S(1)} %pad_add_fusion.refs_0_, bf16[2,128,512]{2,1,0:T(8,128)(2,1)S(1)} %get-tuple-element.36.refs_1_, bf16[2,128,512]{2,1,0:T(8,128)(2,1)S(1)} %collective-permute-done.10.refs_2_, bf16[512,2048]{1,0:T(8,128)(2,1)S(1)} %copy-done.11, ...), custom_call_target="tpu_custom_call" | custom-call | flops 3300000000 | bytes 1048576 | tf_op jit(solution)/shard_map/out_project/pallas_call | solution.py:34
  121.9 9.7 %all-to-all-done.3.refs_3_ = bf16[8,272,128]{2,1,0:T(8,128)(2,1)S(1)} async-done(((bf16[8,272,128]{2,1,0:T(8,128)(2,1)}), bf16[8,272,128]{2,1,0:T(8,128)(2,1)S(1)}, u32[]{:S(2)}, u32[]{:S(2)}) %all-to-all-start.3) | async-done | bytes 557088 | tf_op jit(solution)/shard_map/all_to_all | solution.py:353
  131.5 3.1 %collective-permute-done.12.refs_4_.refs_1_ = bf16[128,2048]{1,0:T(8,128)(2,1)S(1)} collective-permute-done((bf16[128,2048]{1,0:T(8,128)(2,1)}, bf16[128,2048]{1,0:T(8,128)(2,1)S(1)}, u32[]{:S(2)}, u32[]{:S(2)}) %collective-permute-start.12) | collective-permute-done | bytes 524320 | tf_op jit(solution)/shard_map/ppermute | solution.py:349
  138.9 3.0 %out_project.3 = (bf16[128,2048]{1,0:T(8,128)(2,1)S(1)}, f32[128,2048]{1,0:T(8,128)S(1)}) custom-call(s32[3]{0:T(128)S(1)} %pad_add_fusion.refs_0_, bf16[2,128,512]{2,1,0:T(8,128)(2,1)S(1)} %get-tuple-element.41.refs_1_, bf16[2,128,512]{2,1,0:T(8,128)(2,1)S(1)} %collective-permute-done.13.refs_2_, bf16[512,2048]{1,0:T(8,128)(2,1)S(1)} %copy-done.11, ...), custom_call_target="tpu_custom_call" | custom-call | flops 3300000000 | bytes 1048576 | tf_op jit(solution)/shard_map/out_project/pallas_call | solution.py:34
  141.9 1.6 collective-permute-start.14
  143.4 12.5 %collective-permute-done.14.refs_3_ = bf16[128,2048]{1,0:T(8,128)(2,1)S(1)} collective-permute-done((bf16[128,2048]{1,0:T(8,128)(2,1)S(1)}, bf16[128,2048]{1,0:T(8,128)(2,1)S(1)}, u32[]{:S(2)}, u32[]{:S(2)}) %collective-permute-start.14) | collective-permute-done | bytes 524320 | tf_op jit(solution)/shard_map/ppermute | solution.py:349
  (80 shorter events, 25.2 us)
Async XLA Ops:
  2.4 21.8 %all-to-all-start = ((bf16[8,64,512]{2,1,0:T(8,128)(2,1)}), bf16[8,64,512]{2,1,0:T(8,128)(2,1)S(1)}, u32[]{:S(2)}, u32[]{:S(2)}) async-start(bf16[8,64,512]{2,1,0:T(8,128)(2,1)} %get-tuple-element.25.rest_0_), calls=%async_computation | async-start | bytes 1048576 | tf_op jit(solution)/shard_map/all_to_all | solution.py:353
  9.7 24.7 %collective-permute-start.1 = (bf16[1024,512]{1,0:T(8,128)(2,1)S(1)}, bf16[1024,512]{1,0:T(8,128)(2,1)S(1)}, u32[]{:S(2)}, u32[]{:S(2)}) collective-permute-start(bf16[1024,512]{1,0:T(8,128)(2,1)S(1)} %copy-done.1), channel_id=1, source_target_pairs={{0,2},{1,3},{2,0},{3,1},{4,6},{5,7},{6,4},{7,5},{8,10},{9,11},{10,... | collective-permute-start | bytes 3145736 | tf_op jit(solution)/shard_map/ppermute | solution.py:349
  25.0 18.4 %all-to-all-start.2 = ((bf16[8,64,512]{2,1,0:T(8,128)(2,1)}), bf16[8,64,512]{2,1,0:T(8,128)(2,1)}, u32[]{:S(2)}, u32[]{:S(2)}) async-start(bf16[8,64,512]{2,1,0:T(8,128)(2,1)} %get-tuple-element.34), calls=%async_computation.2 | async-start | bytes 1048576 | tf_op jit(solution)/shard_map/all_to_all | solution.py:353
  29.1 15.9 %collective-permute-start = (bf16[1024,512]{1,0:T(8,128)(2,1)S(1)}, bf16[1024,512]{1,0:T(8,128)(2,1)S(1)}, u32[]{:S(2)}, u32[]{:S(2)}) collective-permute-start(bf16[1024,512]{1,0:T(8,128)(2,1)S(1)} %copy-done.1), channel_id=1, source_target_pairs={{0,1},{1,0},{2,3},{3,2},{4,5},{5,4},{6,7},{7,6},{8,9},{9,8},{10,11... | collective-permute-start | bytes 3145736 | tf_op jit(solution)/shard_map/ppermute | solution.py:349
  34.4 25.9 %collective-permute-start.2 = (bf16[1024,512]{1,0:T(8,128)(2,1)S(1)}, bf16[1024,512]{1,0:T(8,128)(2,1)}, u32[]{:S(2)}, u32[]{:S(2)}) collective-permute-start(bf16[1024,512]{1,0:T(8,128)(2,1)S(1)} %collective-permute-done.1.refs_2_), channel_id=1, source_target_pairs={{0,1},{1,0},{2,3},{3,2},{4,5},{5,4},{6,7},{7,6},{8,9},{9,8},{10,11... | collective-permute-start | bytes 3145736 | tf_op jit(solution)/shard_map/ppermute | solution.py:349
  34.4 17.0 %collective-permute-start.5 = (bf16[8,64,512]{2,1,0:T(8,128)(2,1)}, bf16[8,64,512]{2,1,0:T(8,128)(2,1)}, u32[]{:S(2)}, u32[]{:S(2)}) collective-permute-start(bf16[8,64,512]{2,1,0:T(8,128)(2,1)} %copy-done.9), channel_id=1, source_target_pairs={{0,2},{1,3},{2,0},{3,1},{4,6},{5,7},{6,4},{7,5},{8,10},{9,11},{10,... | collective-permute-start | bytes 1572872 | tf_op jit(solution)/shard_map/ppermute | solution.py:349
  43.4 16.9 %collective-permute-start.8 = (bf16[8,64,512]{2,1,0:T(8,128)(2,1)}, bf16[8,64,512]{2,1,0:T(8,128)(2,1)}, u32[]{:S(2)}, u32[]{:S(2)}) collective-permute-start(bf16[8,64,512]{2,1,0:T(8,128)(2,1)} %all-to-all-done.2), channel_id=1, source_target_pairs={{0,2},{1,3},{2,0},{3,1},{4,6},{5,7},{6,4},{7,5},{8,10},{9,11},{10,... | collective-permute-start | bytes 1572872 | tf_op jit(solution)/shard_map/ppermute | solution.py:349
  44.9 70.8 %collective-permute-start.11 = (bf16[512,2048]{1,0:T(8,128)(2,1)}, bf16[512,2048]{1,0:T(8,128)(2,1)}, u32[]{:S(2)}, u32[]{:S(2)}) collective-permute-start(bf16[512,2048]{1,0:T(8,128)(2,1)} %refs_3_.3), channel_id=1, source_target_pairs={{0,1},{1,0},{2,3},{3,2},{4,5},{5,4},{6,7},{7,6},{8,9},{9,8},{10,11... | collective-permute-start | bytes 6291464 | tf_op jit(solution)/shard_map/ppermute | solution.py:349
  45.0 28.0 %collective-permute-start.4 = (bf16[8,64,512]{2,1,0:T(8,128)(2,1)}, bf16[8,64,512]{2,1,0:T(8,128)(2,1)S(1)}, u32[]{:S(2)}, u32[]{:S(2)}) collective-permute-start(bf16[8,64,512]{2,1,0:T(8,128)(2,1)} %copy-done.9), channel_id=1, source_target_pairs={{0,1},{1,0},{2,3},{3,2},{4,5},{5,4},{6,7},{7,6},{8,9},{9,8},{10,11... | collective-permute-start | bytes 1572872 | tf_op jit(solution)/shard_map/ppermute | solution.py:349
  51.4 25.2 %copy-start.2 = (bf16[2048,512]{1,0:T(8,128)(2,1)}, bf16[2048,512]{1,0:T(8,128)(2,1)S(1)}, u32[]{:S(2)}) copy-start(bf16[2048,512]{1,0:T(8,128)(2,1)S(1)} %get-tuple-element.27.refs_4_.refs_5_) | copy-start | bytes 6291460
  51.4 25.2 %copy-start.4 = (bf16[2048,512]{1,0:T(8,128)(2,1)}, bf16[2048,512]{1,0:T(8,128)(2,1)S(1)}, u32[]{:S(2)}) copy-start(bf16[2048,512]{1,0:T(8,128)(2,1)S(1)} %get-tuple-element.28.refs_5_.refs_6_) | copy-start | bytes 6291460
  51.4 25.2 %copy-start.12 = (bf16[2048,512]{1,0:T(8,128)(2,1)}, bf16[2048,512]{1,0:T(8,128)(2,1)S(1)}, u32[]{:S(2)}) copy-start(bf16[2048,512]{1,0:T(8,128)(2,1)S(1)} %get-tuple-element.26.refs_4_) | copy-start | bytes 6291460
  51.4 47.4 %collective-permute-start.7 = (bf16[8,64,512]{2,1,0:T(8,128)(2,1)}, bf16[8,64,512]{2,1,0:T(8,128)(2,1)}, u32[]{:S(2)}, u32[]{:S(2)}) collective-permute-start(bf16[8,64,512]{2,1,0:T(8,128)(2,1)} %all-to-all-done.2), channel_id=1, source_target_pairs={{0,1},{1,0},{2,3},{3,2},{4,5},{5,4},{6,7},{7,6},{8,9},{9,8},{10,11... | collective-permute-start | bytes 1572872 | tf_op jit(solution)/shard_map/ppermute | solution.py:349
  60.3 16.4 %collective-permute-start.6 = (bf16[8,64,512]{2,1,0:T(8,128)(2,1)}, bf16[8,64,512]{2,1,0:T(8,128)(2,1)S(1)}, u32[]{:S(2)}, u32[]{:S(2)}) collective-permute-start(bf16[8,64,512]{2,1,0:T(8,128)(2,1)} %collective-permute-done.5), channel_id=1, source_target_pairs={{0,1},{1,0},{2,3},{3,2},{4,5},{5,4},{6,7},{7,6},{8,9},{9,8},{10,11... | collective-permute-start | bytes 1572872 | tf_op jit(solution)/shard_map/ppermute | solution.py:349
  60.3 38.6 %collective-permute-start.9 = (bf16[8,64,512]{2,1,0:T(8,128)(2,1)}, bf16[8,64,512]{2,1,0:T(8,128)(2,1)}, u32[]{:S(2)}, u32[]{:S(2)}) collective-permute-start(bf16[8,64,512]{2,1,0:T(8,128)(2,1)} %collective-permute-done.8), channel_id=1, source_target_pairs={{0,1},{1,0},{2,3},{3,2},{4,5},{5,4},{6,7},{7,6},{8,9},{9,8},{10,11... | collective-permute-start | bytes 1572872 | tf_op jit(solution)/shard_map/ppermute | solution.py:349
  73.0 16.9 %collective-permute-start.3 = (bf16[512,512]{1,0:T(8,128)(2,1)}, bf16[512,512]{1,0:T(8,128)(2,1)S(1)}, u32[]{:S(2)}, u32[]{:S(2)}) collective-permute-start(bf16[512,512]{1,0:T(8,128)(2,1)} %project_halo.1.refs_7_), channel_id=1, source_target_pairs={{0,4},{4,8},{8,12},{12,16},{16,20},{20,24},{24,28},{1,5},{5,9},{9,... | collective-permute-start | bytes 1572872 | tf_op jit(solution)/shard_map/ppermute | solution.py:377
  76.7 13.2 %copy-start.23 = (bf16[1024,512]{1,0:T(8,128)(2,1)S(1)}, bf16[1024,512]{1,0:T(8,128)(2,1)}, u32[]{:S(2)}) copy-start(bf16[1024,512]{1,0:T(8,128)(2,1)} %copy-done.22) | copy-start | bytes 3145732
  85.4 21.6 %all-to-all-start.1 = ((bf16[8,272,128]{2,1,0:T(8,128)(2,1)}), bf16[8,272,128]{2,1,0:T(8,128)(2,1)S(1)}, u32[]{:S(2)}, u32[]{:S(2)}) async-start(bf16[8,272,128]{2,1,0:T(8,128)(2,1)} %column_part.2.refs_5_), calls=%async_computation.1 | async-start | bytes 1114112 | tf_op jit(solution)/shard_map/all_to_all | solution.py:353
  109.6 6.1 %collective-permute-start.10 = (bf16[2,128,512]{2,1,0:T(8,128)(2,1)S(1)}, bf16[2,128,512]{2,1,0:T(8,128)(2,1)S(1)}, u32[]{:S(2)}, u32[]{:S(2)}) collective-permute-start(bf16[2,128,512]{2,1,0:T(8,128)(2,1)S(1)} %get-tuple-element.37), channel_id=1, source_target_pairs={{0,1},{1,0},{2,3},{3,2},{4,5},{5,4},{6,7},{7,6},{8,9},{9,8},{10,11... | collective-permute-start | bytes 786440 | tf_op jit(solution)/shard_map/ppermute | solution.py:349
  109.7 21.8 %all-to-all-start.3 = ((bf16[8,272,128]{2,1,0:T(8,128)(2,1)}), bf16[8,272,128]{2,1,0:T(8,128)(2,1)S(1)}, u32[]{:S(2)}, u32[]{:S(2)}) async-start(bf16[8,272,128]{2,1,0:T(8,128)(2,1)} %column_part.3.refs_4_), calls=%async_computation.3 | async-start | bytes 1114112 | tf_op jit(solution)/shard_map/all_to_all | solution.py:353
  120.4 14.2 %collective-permute-start.12 = (bf16[128,2048]{1,0:T(8,128)(2,1)}, bf16[128,2048]{1,0:T(8,128)(2,1)S(1)}, u32[]{:S(2)}, u32[]{:S(2)}) collective-permute-start(bf16[128,2048]{1,0:T(8,128)(2,1)} %get-tuple-element.39), channel_id=1, source_target_pairs={{0,2},{1,3},{2,0},{3,1},{4,6},{5,7},{6,4},{7,5},{8,10},{9,11},{10,... | collective-permute-start | bytes 1572872 | tf_op jit(solution)/shard_map/ppermute | solution.py:349
  137.3 1.6 %collective-permute-start.13 = (bf16[2,128,512]{2,1,0:T(8,128)(2,1)S(1)}, bf16[2,128,512]{2,1,0:T(8,128)(2,1)S(1)}, u32[]{:S(2)}, u32[]{:S(2)}) collective-permute-start(bf16[2,128,512]{2,1,0:T(8,128)(2,1)S(1)} %get-tuple-element.42), channel_id=1, source_target_pairs={{0,1},{1,0},{2,3},{3,2},{4,5},{5,4},{6,7},{7,6},{8,9},{9,8},{10,11... | collective-permute-start | bytes 786440 | tf_op jit(solution)/shard_map/ppermute | solution.py:349
  138.9 17.0 %copy-start.15 = (f32[128,2048]{1,0:T(8,128)S(1)}, f32[128,2048]{1,0:T(8,128)}, u32[]{:S(2)}) copy-start(f32[128,2048]{1,0:T(8,128)} %copy-done.14) | copy-start | bytes 3145732
  141.9 14.0 %collective-permute-start.14 = (bf16[128,2048]{1,0:T(8,128)(2,1)S(1)}, bf16[128,2048]{1,0:T(8,128)(2,1)S(1)}, u32[]{:S(2)}, u32[]{:S(2)}) collective-permute-start(bf16[128,2048]{1,0:T(8,128)(2,1)S(1)} %get-tuple-element.44), channel_id=1, source_target_pairs={{0,2},{1,3},{2,0},{3,1},{4,6},{5,7},{6,4},{7,5},{8,10},{9,11},{10,... | collective-permute-start | bytes 1572872 | tf_op jit(solution)/shard_map/ppermute | solution.py:349
  (21 other events, 81.2 us)

commit v5 on v4

--- a/solution.py
+++ b/solution.py
@@ -23,7 +23,7 @@
 IN_SMEM = pl.BlockSpec(memory_space=pltpu.SMEM)
 
 
-def call(body, name, micros, out_shape, args, after=(), scratch=(), mib=24):
+def call(body, name, micros, out_shape, args, after=(), scratch=(), mib=16):
     specs = [IN_SMEM if x.dtype == jnp.int32 else IN_VMEM for x in args]
     extra = len(after)
 
@@ -43,6 +43,22 @@
         ),
         name=name,
     )(*args, *after)
+
+
+def fence(value, *after):
+    return pl.pallas_call(
+        lambda *refs: None,
+        in_specs=[ANYWHERE] * (1 + len(after)),
+        out_specs=ANYWHERE,
+        out_shape=jax.ShapeDtypeStruct(value.shape, value.dtype),
+        input_output_aliases={0: 0},
+        cost_estimate=pl.CostEstimate(flops=0, bytes_accessed=0, transcendentals=0),
+        name="fence",
+    )(value, *after)
+
+
+def in_hbm(value):
+    return pltpu.with_memory_space_constraint(value, pltpu.HBM)
 
 
 def shape(dims, dtype=BF16):
@@ -98,17 +114,19 @@
         compiler_params=pltpu.CompilerParams(vmem_limit_bytes=8 * MIB),
         cost_estimate=pl.CostEstimate(flops=0, bytes_accessed=2 * MIB, transcendentals=0),
         name="pack_tokens",
-    )(tokens)
-
-
-def stage_kernel(order_ref, wq, wk, wv, oq, ok, ov, sems):
+    )(in_hbm(tokens))
+
+
+def stage_kernel(order_ref, wq, wk, wv, wo, *rest):
+    oq, ok, ov, oo, sems = rest[-5:]
     copies = []
-    for n, (w, o) in enumerate(((wq, oq), (wk, ok), (wv, ov))):
+    for w, o, ordered in ((wq, oq, True), (wk, ok, True), (wv, ov, True), (wo, oo, False)):
+        part = w.shape[0] // 4
         for p in range(4):
-            rows = pl.ds(pl.multiple_of(order_ref[p] * 512, 512), 512)
-            copies.append(
-                pltpu.make_async_copy(w.at[rows], o.at[p * 512 : (p + 1) * 512], sems.at[4 * n + p])
-            )
+            source = pl.multiple_of(order_ref[p] * part, part) if ordered else p * part
+            to = slice(p * part, (p + 1) * part)
+            sem = sems.at[len(copies)]
+            copies.append(pltpu.make_async_copy(w.at[pl.ds(source, part)], o.at[to], sem))
     for c in copies:
         c.start()
     for c in copies:
@@ -116,19 +134,16 @@
 
 
 def stage(order, weights, after):
-    def body(order_ref, wq, wk, wv, *rest):
-        stage_kernel(order_ref, wq, wk, wv, *rest[len(after) :])
-
     return pl.pallas_call(
-        body,
-        in_specs=[IN_SMEM] + [ANYWHERE] * (3 + len(after)),
-        out_specs=[IN_VMEM] * 3,
-        out_shape=[shape(w.shape) for w in weights],
-        scratch_shapes=[pltpu.SemaphoreType.DMA((12,))],
+        stage_kernel,
+        in_specs=[IN_SMEM] + [ANYWHERE] * (4 + len(after)),
+        out_specs=[IN_VMEM] * 4,
+        out_shape=[pltpu.VMEM(w.shape, BF16) for w in weights],
+        scratch_shapes=[pltpu.SemaphoreType.DMA((16,))],
         compiler_params=pltpu.CompilerParams(vmem_limit_bytes=16 * MIB),
-        cost_estimate=pl.CostEstimate(flops=0, bytes_accessed=6 * MIB, transcendentals=0),
+        cost_estimate=pl.CostEstimate(flops=0, bytes_accessed=8 * MIB, transcendentals=0),
         name="stage_weights",
-    )(order, *weights, *after)
+    )(order, *[in_hbm(w) for w in weights], *after)
 
 
 def gathered(x_refs, at, w_ref):
@@ -319,10 +334,10 @@
         keep_ref[:, at] = jnp.where(low_side, total[:tokens], total[tokens:])
 
 
-def out_project(pos, own, other, w_own, w_other):
+def out_project(pos, own, other, w_own, w_other, after):
     dims = (own.shape[1], w_own.shape[1])
     shapes = [shape(dims), shape(dims, F32)]
-    return call(out_kernel, "out_project", 3, shapes, (pos, own, other, w_own, w_other))
+    return call(out_kernel, "out_project", 2, shapes, (pos, own, other, w_own, w_other), after)
 
 
 def join_kernel(*refs):
@@ -369,8 +384,9 @@
     pieces = gather(tokens)
     messages = pack(tokens, owners)
     classes = [exchange(m) for m in messages]
-    weights = stage(order, (w_query, w_key, w_value), (messages[0], pieces[1]))
+    *weights, w_own = stage(order, (w_query, w_key, w_value, w_out), (messages[0], pieces[1]))
     w_other = swap(w_out, 1)
+    classes[0] = fence(classes[0], pieces[2], weights[0], w_other)
     own_halo = call(
         halo_kernel, "project_halo", 1.5, shape((2 * STRIDE, width)), (*pieces, *weights[1:])
     )
@@ -381,6 +397,8 @@
         7,
         [shape((rows, width))] * 3,
         (*pieces, *weights, own_halo),
+        (classes[0],),
+        mib=20,
     )
     columns, after = [], (q,)
     for i, c in enumerate(classes):
@@ -388,10 +406,10 @@
         if i == 0:
             locals_ = local_part(pos, q, k, v, halo, owners, (columns[0],))
             after = (locals_[-1][-1],)
-    pairs, after = [], (columns[-1],)
+    pairs, after = [], ()
     for column, (local, lse) in zip(columns, locals_):
-        own, send = mix(pos, exchange(column), local, lse, after)
-        out, keep = out_project(pos, own, swap(send, 1), w_out, w_other)
+        own, send = mix(pos, exchange(column), local, lse, (columns[-1],))
+        out, keep = out_project(pos, own, swap(send, 1), w_own, w_other, after)
         pairs.append((keep, swap(out, 2)))
         after = (pairs[-1][1],)
     return join(pairs)

time: 158 us -> 151 us (0.956)
  waiting for transfers between devices: 61.2 us -> 46.4 us
  local copies, waits for them, and re-layouts: 16.3 us -> 23.8 us
  Pallas kernels: 44.8 us -> 46.9 us
  starting transfers between devices: 34.5 us -> 32.8 us
    all_to_all x4, waiting for transfers between devices: 30.1 us -> 20 us  [exchange(): lax.all_to_all(messages, 'seq', split_axis=0, concat_axis=0, tiled=True)]
    unnamed x52 -> x64, local copies, waits for them, and re-layouts: 16.3 us -> 23.8 us
    ppermute x14, waiting for transfers between devices: 31 us -> 26.4 us  [swap(): return lax.ppermute(value, 'head', [(i, i ^ distance) for i in range(4)])]
    pallas_call x1 -> x2, Pallas kernels: 1.11 us -> 4.11 us  [the longest x1 4.1 us: stage(): pl.pallas_call(stage_kernel, in_specs=[IN_SMEM] + [ANYWHERE] * (4 + len(a...]
    ppermute x14, starting transfers between devices: 8.91 us -> 6.45 us  [swap(): return lax.ppermute(value, 'head', [(i, i ^ distance) for i in range(4)])]
    pallas_call x10, Pallas kernels: 42.5 us -> 40.7 us  [call(): pl.pallas_call(run, in_specs=specs + [ANYWHERE] * extra, out_specs=jax.tr...]
  transfers between devices with their start and end apart: 19 -> 19, of which waited for: 8 -> 9; matrix products, arithmetic and copies ran while one was open for 0% -> 0% of each run, Pallas kernels for 24% -> 28%
where the time goes in v5:
time: 151 us; the launch traced here: 150 us
  Pallas kernels  46.9 us (31%)
  waiting for transfers between devices  46.4 us (31%)
  starting transfers between devices  32.8 us (22%)
  local copies, waits for them, and re-layouts  23.8 us (16%)
    pallas_call x10, Pallas kernels, call(): pl.pallas_call(run, in_specs=specs + [ANYWHERE] * extra, out_specs=jax.tr...  40.7 us
    ppermute x14, waiting for transfers between devices, swap(): return lax.ppermute(value, 'head', [(i, i ^ distance) for i in range(4)])  26.4 us
    unnamed x64, local copies, waits for them, and re-layouts  23.8 us
    all_to_all x4, starting transfers between devices, exchange(): lax.all_to_all(messages, 'seq', split_axis=0, concat_axis=0, tiled=True)  22.7 us
    all_to_all x4, waiting for transfers between devices, exchange(): lax.all_to_all(messages, 'seq', split_axis=0, concat_axis=0, tiled=True)  20 us
    ppermute x14, starting transfers between devices, swap(): return lax.ppermute(value, 'head', [(i, i ^ distance) for i in range(4)])  6.45 us
    pallas_call x1, Pallas kernels, stage(): pl.pallas_call(stage_kernel, in_specs=[IN_SMEM] + [ANYWHERE] * (4 + len(a...  4.1 us
    ppermute x1, starting transfers between devices, chunked(): lax.ppermute(own_halo, 'seq', [(i, i + 1) for i in range(owners - 1)])  3.61 us
  transfers between devices with their start and end apart: 19, of which 9 were waited for; matrix products, arithmetic and copies ran while one was open for 0% of the time, Pallas kernels for 28%

profile of v5, /device:TPU:0, one launch (start us, length us, event | category | flops | bytes accessed | tf_op | source)
XLA Modules:
  0.0 150.2 jit_solution(7531679581159858277)
XLA Ops:
  0.5 2.0 %pack_tokens.1 = (bf16[8,64,512]{2,1,0:T(8,128)(2,1)S(1)}, bf16[8,64,512]{2,1,0:T(8,128)(2,1)}) custom-call(bf16[1024,512]{1,0:T(8,128)(2,1)} %refs_0_.3), custom_call_target="tpu_custom_call" | custom-call | bytes 2097152 | tf_op jit(solution)/shard_map/pack_tokens/pallas_call | solution.py:108
  3.3 6.9 %all-to-all-start.2 = ((bf16[8,64,512]{2,1,0:T(8,128)(2,1)}), bf16[8,64,512]{2,1,0:T(8,128)(2,1)}, u32[]{:S(2)}, u32[]{:S(2)}) async-start(bf16[8,64,512]{2,1,0:T(8,128)(2,1)} %get-tuple-element.35), calls=%async_computation.2 | async-start | bytes 1048576 | tf_op jit(solution)/shard_map/all_to_all | solution.py:368
  10.3 1.6 %collective-permute-start.1 = (bf16[1024,512]{1,0:T(8,128)(2,1)S(1)}, bf16[1024,512]{1,0:T(8,128)(2,1)S(1)}, u32[]{:S(2)}, u32[]{:S(2)}) collective-permute-start(bf16[1024,512]{1,0:T(8,128)(2,1)S(1)} %copy-done), channel_id=1, source_target_pairs={{0,2},{1,3},{2,0},{3,1},{4,6},{5,7},{6,4},{7,5},{8,10},{9,11},{10,... | collective-permute-start | bytes 3145736 | tf_op jit(solution)/shard_map/ppermute | solution.py:364
  11.8 13.6 %all-to-all-done.2 = bf16[8,64,512]{2,1,0:T(8,128)(2,1)} async-done(((bf16[8,64,512]{2,1,0:T(8,128)(2,1)}), bf16[8,64,512]{2,1,0:T(8,128)(2,1)}, u32[]{:S(2)}, u32[]{:S(2)}) %all-to-all-start.2) | async-done | bytes 524320 | tf_op jit(solution)/shard_map/all_to_all | solution.py:368
  25.5 4.1 %all-to-all-start = ((bf16[8,64,512]{2,1,0:T(8,128)(2,1)}), bf16[8,64,512]{2,1,0:T(8,128)(2,1)}, u32[]{:S(2)}, u32[]{:S(2)}) async-start(bf16[8,64,512]{2,1,0:T(8,128)(2,1)} %copy-done.15), calls=%async_computation | async-start | bytes 1048576 | tf_op jit(solution)/shard_map/all_to_all | solution.py:368
  29.6 5.9 %collective-permute-done.1.refs_2_.refs_1_ = bf16[1024,512]{1,0:T(8,128)(2,1)S(1)} collective-permute-done((bf16[1024,512]{1,0:T(8,128)(2,1)S(1)}, bf16[1024,512]{1,0:T(8,128)(2,1)S(1)}, u32[]{:S(2)}, u32[]{:S(2)}) %collective-permute-start.1) | collective-permute-done | bytes 1048608 | tf_op jit(solution)/shard_map/ppermute | solution.py:364
  38.1 4.1 %stage_weights.1 = (bf16[2048,512]{1,0:T(8,128)(2,1)S(1)}, bf16[2048,512]{1,0:T(8,128)(2,1)S(1)}, bf16[2048,512]{1,0:T(8,128)(2,1)S(1)}, bf16[512,2048]{1,0:T(8,128)(2,1)S(1)}) custom-call(s32[4]{0:T(128)S(1)} %iota_xor_fusion.order_ref, bf16[2048,512]{1,0:T(8,128)(2,1)} %wq.1, bf16[2048,512]{1,0:T(8,128)(2,1)} %wk.1, bf16[2048,512]{1,0:T(8,128)(2,1)} %wv.1, ...), custom_call_target="tpu_custom_call" | custom-call | bytes 8388608 | tf_op jit(solution)/shard_map/stage_weights/pallas_call | solution.py:137
  48.4 1.8 %collective-permute-done.9 = bf16[8,64,512]{2,1,0:T(8,128)(2,1)} collective-permute-done((bf16[8,64,512]{2,1,0:T(8,128)(2,1)}, bf16[8,64,512]{2,1,0:T(8,128)(2,1)}, u32[]{:S(2)}, u32[]{:S(2)}) %collective-permute-start.9) | collective-permute-done | bytes 524320 | tf_op jit(solution)/shard_map/ppermute | solution.py:364
  51.9 1.6 %copy-done.8 = bf16[2048,512]{1,0:T(8,128)(2,1)S(1)} copy-done((bf16[2048,512]{1,0:T(8,128)(2,1)S(1)}, bf16[2048,512]{1,0:T(8,128)(2,1)}, u32[]{:S(2)}) %copy-start.8) | copy-done | bytes 2097176
  53.5 1.6 %copy-done.12 = bf16[2048,512]{1,0:T(8,128)(2,1)S(1)} copy-done((bf16[2048,512]{1,0:T(8,128)(2,1)S(1)}, bf16[2048,512]{1,0:T(8,128)(2,1)}, u32[]{:S(2)}) %copy-start.12) | copy-done | bytes 2097176
  55.1 2.6 %project_halo.1.refs_7_ = bf16[512,512]{1,0:T(8,128)(2,1)S(1)} custom-call(bf16[1024,512]{1,0:T(8,128)(2,1)S(1)} %copy-done, bf16[1024,512]{1,0:T(8,128)(2,1)S(1)} %collective-permute-done.rest_1_.refs_1_, bf16[1024,512]{1,0:T(8,128)(2,1)S(1)} %copy-done.2, bf16[1024,512]{1,0:T(8,128)(2,1)} %collective-permute-done.2.refs_3_, ...), custom_call_target="tpu_custom_call" | custom-call | flops 1650000000 | bytes 1048576 | tf_op jit(solution)/shard_map/project_halo/pallas_call | solution.py:34
  57.8 3.6 %collective-permute-start.4 = (bf16[512,512]{1,0:T(8,128)(2,1)S(1)}, bf16[512,512]{1,0:T(8,128)(2,1)S(1)}, u32[]{:S(2)}, u32[]{:S(2)}) collective-permute-start(bf16[512,512]{1,0:T(8,128)(2,1)S(1)} %project_halo.1.refs_7_), channel_id=1, source_target_pairs={{0,4},{4,8},{8,12},{12,16},{16,20},{20,24},{24,28},{1,5},{5,9},{9,... | collective-permute-start | bytes 1572872 | tf_op jit(solution)/shard_map/ppermute | solution.py:393
  62.1 6.8 %project_block.1 = (bf16[1024,512]{1,0:T(8,128)(2,1)S(1)}, bf16[1024,512]{1,0:T(8,128)(2,1)S(1)}, bf16[1024,512]{1,0:T(8,128)(2,1)S(1)}) custom-call(bf16[1024,512]{1,0:T(8,128)(2,1)S(1)} %copy-done, bf16[1024,512]{1,0:T(8,128)(2,1)S(1)} %collective-permute-done.rest_1_.refs_1_, bf16[1024,512]{1,0:T(8,128)(2,1)S(1)} %copy-done.3, ...), custom_call_target="tpu_custom_call" | custom-call | flops 7699999744 | bytes 1048576 | tf_op jit(solution)/shard_map/project_block/pallas_call | solution.py:34
  71.0 7.7 %column_part.2.refs_5_ = bf16[8,272,128]{2,1,0:T(8,128)(2,1)} custom-call(bf16[512,512]{1,0:T(8,128)(2,1)} %bitcast.3.refs_0_, bf16[512,512]{1,0:T(8,128)(2,1)S(1)} %bitcast.11, bf16[512,512]{1,0:T(8,128)(2,1)} %bitcast.5.refs_2_, bf16[512,512]{1,0:T(8,128)(2,1)S(1)} %bitcast.12, bf16[2048,512]{1,0:T(8,128)(2,1)S(1)} %copy-done.5, ...), custom_call_target="tpu_custom_call" | custom-call | flops 6600000000 | bytes 1048576 | tf_op jit(solution)/shard_map/column_part/pallas_call | solution.py:34
  79.7 5.7 %all-to-all-start.1 = ((bf16[8,272,128]{2,1,0:T(8,128)(2,1)}), bf16[8,272,128]{2,1,0:T(8,128)(2,1)S(1)}, u32[]{:S(2)}, u32[]{:S(2)}) async-start(bf16[8,272,128]{2,1,0:T(8,128)(2,1)} %column_part.2.refs_5_), calls=%async_computation.1 | async-start | bytes 1114112 | tf_op jit(solution)/shard_map/all_to_all | solution.py:368
  89.0 5.7 %local_part.1 = (f32[8,64,512]{2,1,0:T(8,128)S(1)}, f32[8,64,512]{2,1,0:T(8,128)S(1)}, f32[64,128]{1,0:T(8,128)S(1)}, f32[64,128]{1,0:T(8,128)S(1)}) custom-call(s32[3]{0:T(128)S(1)} %pad_add_fusion.refs_0_, bf16[1024,512]{1,0:T(8,128)(2,1)S(1)} %copy-done.27, bf16[1024,512]{1,0:T(8,128)(2,1)S(1)} %copy-done.29, bf16[1024,512]{1,0:T(8,128)(2,1)S(1)} %copy-done.31, ...), custom_call_target="tpu_custom_call" | custom-call | flops 5500000256 | bytes 1048576 | tf_op jit(solution)/shard_map/local_part/pallas_call | solution.py:34
  96.8 8.1 %column_part.3.refs_4_ = bf16[8,272,128]{2,1,0:T(8,128)(2,1)} custom-call(bf16[512,512]{1,0:T(8,128)(2,1)} %bitcast.7.refs_0_, bf16[512,512]{1,0:T(8,128)(2,1)} %bitcast.8.refs_1_, bf16[512,512]{1,0:T(8,128)(2,1)} %bitcast.9.refs_2_, bf16[512,512]{1,0:T(8,128)(2,1)} %bitcast.10.refs_3_, bf16[2048,512]{1,0:T(8,128)(2,1)S(1)} %copy-done.6, ...), custom_call_target="tpu_custom_call" | custom-call | flops 6600000000 | bytes 1048576 | tf_op jit(solution)/shard_map/column_part/pallas_call | solution.py:34
  104.8 6.0 %all-to-all-start.3 = ((bf16[8,272,128]{2,1,0:T(8,128)(2,1)}), bf16[8,272,128]{2,1,0:T(8,128)(2,1)S(1)}, u32[]{:S(2)}, u32[]{:S(2)}) async-start(bf16[8,272,128]{2,1,0:T(8,128)(2,1)} %column_part.3.refs_4_), calls=%async_computation.3 | async-start | bytes 1114112 | tf_op jit(solution)/shard_map/all_to_all | solution.py:368
  113.6 1.5 %collective-permute-done.11.refs_2_ = bf16[2,128,512]{2,1,0:T(8,128)(2,1)S(1)} collective-permute-done((bf16[2,128,512]{2,1,0:T(8,128)(2,1)S(1)}, bf16[2,128,512]{2,1,0:T(8,128)(2,1)S(1)}, u32[]{:S(2)}, u32[]{:S(2)}) %collective-permute-start.11) | collective-permute-done | bytes 262176 | tf_op jit(solution)/shard_map/ppermute | solution.py:364
  115.1 2.9 %out_project.2 = (bf16[128,2048]{1,0:T(8,128)(2,1)S(1)}, f32[128,2048]{1,0:T(8,128)S(1)}) custom-call(s32[3]{0:T(128)S(1)} %pad_add_fusion.refs_0_, bf16[2,128,512]{2,1,0:T(8,128)(2,1)S(1)} %get-tuple-element.37.refs_1_, bf16[2,128,512]{2,1,0:T(8,128)(2,1)S(1)} %collective-permute-done.11.refs_2_, bf16[512,2048]{1,0:T(8,128)(2,1)S(1)} %copy-done.18, ...), custom_call_target="tpu_custom_call" | custom-call | flops 2200000000 | bytes 1048576 | tf_op jit(solution)/shard_map/out_project/pallas_call | solution.py:34
  119.7 6.4 %all-to-all-done.3.refs_3_ = bf16[8,272,128]{2,1,0:T(8,128)(2,1)S(1)} async-done(((bf16[8,272,128]{2,1,0:T(8,128)(2,1)}), bf16[8,272,128]{2,1,0:T(8,128)(2,1)S(1)}, u32[]{:S(2)}, u32[]{:S(2)}) %all-to-all-start.3) | async-done | bytes 557088 | tf_op jit(solution)/shard_map/all_to_all | solution.py:368
  130.4 2.5 %collective-permute-done.12.refs_5_.refs_1_ = bf16[128,2048]{1,0:T(8,128)(2,1)S(1)} collective-permute-done((bf16[128,2048]{1,0:T(8,128)(2,1)S(1)}, bf16[128,2048]{1,0:T(8,128)(2,1)S(1)}, u32[]{:S(2)}, u32[]{:S(2)}) %collective-permute-start.12) | collective-permute-done | bytes 524320 | tf_op jit(solution)/shard_map/ppermute | solution.py:364
  132.9 2.9 %out_project.3 = (bf16[128,2048]{1,0:T(8,128)(2,1)S(1)}, f32[128,2048]{1,0:T(8,128)S(1)}) custom-call(s32[3]{0:T(128)S(1)} %pad_add_fusion.refs_0_, bf16[2,128,512]{2,1,0:T(8,128)(2,1)S(1)} %get-tuple-element.43.refs_1_, bf16[2,128,512]{2,1,0:T(8,128)(2,1)S(1)} %collective-permute-done.13.refs_2_, bf16[512,2048]{1,0:T(8,128)(2,1)S(1)} %copy-done.19, ...), custom_call_target="tpu_custom_call" | custom-call | flops 2200000000 | bytes 1048576 | tf_op jit(solution)/shard_map/out_project/pallas_call | solution.py:34
  136.7 12.3 %collective-permute-done.14.refs_3_ = bf16[128,2048]{1,0:T(8,128)(2,1)S(1)} collective-permute-done((bf16[128,2048]{1,0:T(8,128)(2,1)S(1)}, bf16[128,2048]{1,0:T(8,128)(2,1)S(1)}, u32[]{:S(2)}, u32[]{:S(2)}) %collective-permute-start.14) | collective-permute-done | bytes 524320 | tf_op jit(solution)/shard_map/ppermute | solution.py:364
  (93 shorter events, 31.8 us)
Async XLA Ops:
  0.0 10.3 %copy-start = (bf16[1024,512]{1,0:T(8,128)(2,1)S(1)}, bf16[1024,512]{1,0:T(8,128)(2,1)}, u32[]{:S(2)}) copy-start(bf16[1024,512]{1,0:T(8,128)(2,1)} %refs_0_.3) | copy-start | bytes 3145732
  0.0 47.7 %collective-permute-start.3 = (bf16[512,2048]{1,0:T(8,128)(2,1)}, bf16[512,2048]{1,0:T(8,128)(2,1)}, u32[]{:S(2)}, u32[]{:S(2)}) collective-permute-start(bf16[512,2048]{1,0:T(8,128)(2,1)} %wo.1), channel_id=1, source_target_pairs={{0,1},{1,0},{2,3},{3,2},{4,5},{5,4},{6,7},{7,6},{8,9},{9,8},{10,11... | collective-permute-start | bytes 6291464 | tf_op jit(solution)/shard_map/ppermute | solution.py:364
  3.3 22.1 %all-to-all-start.2 = ((bf16[8,64,512]{2,1,0:T(8,128)(2,1)}), bf16[8,64,512]{2,1,0:T(8,128)(2,1)}, u32[]{:S(2)}, u32[]{:S(2)}) async-start(bf16[8,64,512]{2,1,0:T(8,128)(2,1)} %get-tuple-element.35), calls=%async_computation.2 | async-start | bytes 1048576 | tf_op jit(solution)/shard_map/all_to_all | solution.py:368
  10.3 25.3 %collective-permute-start.1 = (bf16[1024,512]{1,0:T(8,128)(2,1)S(1)}, bf16[1024,512]{1,0:T(8,128)(2,1)S(1)}, u32[]{:S(2)}, u32[]{:S(2)}) collective-permute-start(bf16[1024,512]{1,0:T(8,128)(2,1)S(1)} %copy-done), channel_id=1, source_target_pairs={{0,2},{1,3},{2,0},{3,1},{4,6},{5,7},{6,4},{7,5},{8,10},{9,11},{10,... | collective-permute-start | bytes 3145736 | tf_op jit(solution)/shard_map/ppermute | solution.py:364
  11.8 25.2 %collective-permute-start = (bf16[1024,512]{1,0:T(8,128)(2,1)S(1)}, bf16[1024,512]{1,0:T(8,128)(2,1)S(1)}, u32[]{:S(2)}, u32[]{:S(2)}) collective-permute-start(bf16[1024,512]{1,0:T(8,128)(2,1)S(1)} %copy-done), channel_id=1, source_target_pairs={{0,1},{1,0},{2,3},{3,2},{4,5},{5,4},{6,7},{7,6},{8,9},{9,8},{10,11... | collective-permute-start | bytes 3145736 | tf_op jit(solution)/shard_map/ppermute | solution.py:364
  25.5 22.2 %all-to-all-start = ((bf16[8,64,512]{2,1,0:T(8,128)(2,1)}), bf16[8,64,512]{2,1,0:T(8,128)(2,1)}, u32[]{:S(2)}, u32[]{:S(2)}) async-start(bf16[8,64,512]{2,1,0:T(8,128)(2,1)} %copy-done.15), calls=%async_computation | async-start | bytes 1048576 | tf_op jit(solution)/shard_map/all_to_all | solution.py:368
  35.5 12.1 %copy-start.1 = (bf16[1024,512]{1,0:T(8,128)(2,1)}, bf16[1024,512]{1,0:T(8,128)(2,1)S(1)}, u32[]{:S(2)}) copy-start(bf16[1024,512]{1,0:T(8,128)(2,1)S(1)} %collective-permute-done.1.refs_2_.refs_1_) | copy-start | bytes 3145732
  35.6 15.2 %collective-permute-start.2 = (bf16[1024,512]{1,0:T(8,128)(2,1)S(1)}, bf16[1024,512]{1,0:T(8,128)(2,1)}, u32[]{:S(2)}, u32[]{:S(2)}) collective-permute-start(bf16[1024,512]{1,0:T(8,128)(2,1)S(1)} %collective-permute-done.1.refs_2_.refs_1_), channel_id=1, source_target_pairs={{0,1},{1,0},{2,3},{3,2},{4,5},{5,4},{6,7},{7,6},{8,9},{9,8},{10,11... | collective-permute-start | bytes 3145736 | tf_op jit(solution)/shard_map/ppermute | solution.py:364
  35.6 14.7 %collective-permute-start.9 = (bf16[8,64,512]{2,1,0:T(8,128)(2,1)}, bf16[8,64,512]{2,1,0:T(8,128)(2,1)}, u32[]{:S(2)}, u32[]{:S(2)}) collective-permute-start(bf16[8,64,512]{2,1,0:T(8,128)(2,1)} %all-to-all-done.2), channel_id=1, source_target_pairs={{0,2},{1,3},{2,0},{3,1},{4,6},{5,7},{6,4},{7,5},{8,10},{9,11},{10,... | collective-permute-start | bytes 1572872 | tf_op jit(solution)/shard_map/ppermute | solution.py:364
  47.7 14.4 %collective-permute-start.6 = (bf16[8,64,512]{2,1,0:T(8,128)(2,1)}, bf16[8,64,512]{2,1,0:T(8,128)(2,1)}, u32[]{:S(2)}, u32[]{:S(2)}) collective-permute-start(bf16[8,64,512]{2,1,0:T(8,128)(2,1)} %fence.1.refs_8_), channel_id=1, source_target_pairs={{0,2},{1,3},{2,0},{3,1},{4,6},{5,7},{6,4},{7,5},{8,10},{9,11},{10,... | collective-permute-start | bytes 1572872 | tf_op jit(solution)/shard_map/ppermute | solution.py:364
  48.4 48.4 %collective-permute-start.8 = (bf16[8,64,512]{2,1,0:T(8,128)(2,1)}, bf16[8,64,512]{2,1,0:T(8,128)(2,1)}, u32[]{:S(2)}, u32[]{:S(2)}) collective-permute-start(bf16[8,64,512]{2,1,0:T(8,128)(2,1)} %all-to-all-done.2), channel_id=1, source_target_pairs={{0,1},{1,0},{2,3},{3,2},{4,5},{5,4},{6,7},{7,6},{8,9},{9,8},{10,11... | collective-permute-start | bytes 1572872 | tf_op jit(solution)/shard_map/ppermute | solution.py:364
  50.2 46.5 %collective-permute-start.10 = (bf16[8,64,512]{2,1,0:T(8,128)(2,1)}, bf16[8,64,512]{2,1,0:T(8,128)(2,1)}, u32[]{:S(2)}, u32[]{:S(2)}) collective-permute-start(bf16[8,64,512]{2,1,0:T(8,128)(2,1)} %collective-permute-done.9), channel_id=1, source_target_pairs={{0,1},{1,0},{2,3},{3,2},{4,5},{5,4},{6,7},{7,6},{8,9},{9,8},{10,11... | collective-permute-start | bytes 1572872 | tf_op jit(solution)/shard_map/ppermute | solution.py:364
  50.2 20.8 %collective-permute-start.5 = (bf16[8,64,512]{2,1,0:T(8,128)(2,1)}, bf16[8,64,512]{2,1,0:T(8,128)(2,1)S(1)}, u32[]{:S(2)}, u32[]{:S(2)}) collective-permute-start(bf16[8,64,512]{2,1,0:T(8,128)(2,1)} %fence.1.refs_8_), channel_id=1, source_target_pairs={{0,1},{1,0},{2,3},{3,2},{4,5},{5,4},{6,7},{7,6},{8,9},{9,8},{10,11... | collective-permute-start | bytes 1572872 | tf_op jit(solution)/shard_map/ppermute | solution.py:364
  57.8 27.6 %collective-permute-start.4 = (bf16[512,512]{1,0:T(8,128)(2,1)S(1)}, bf16[512,512]{1,0:T(8,128)(2,1)S(1)}, u32[]{:S(2)}, u32[]{:S(2)}) collective-permute-start(bf16[512,512]{1,0:T(8,128)(2,1)S(1)} %project_halo.1.refs_7_), channel_id=1, source_target_pairs={{0,4},{4,8},{8,12},{12,16},{16,20},{20,24},{24,28},{1,5},{5,9},{9,... | collective-permute-start | bytes 1572872 | tf_op jit(solution)/shard_map/ppermute | solution.py:393
  62.1 8.9 %collective-permute-start.7 = (bf16[8,64,512]{2,1,0:T(8,128)(2,1)}, bf16[8,64,512]{2,1,0:T(8,128)(2,1)S(1)}, u32[]{:S(2)}, u32[]{:S(2)}) collective-permute-start(bf16[8,64,512]{2,1,0:T(8,128)(2,1)} %collective-permute-done.6), channel_id=1, source_target_pairs={{0,1},{1,0},{2,3},{3,2},{4,5},{5,4},{6,7},{7,6},{8,9},{9,8},{10,11... | collective-permute-start | bytes 1572872 | tf_op jit(solution)/shard_map/ppermute | solution.py:364
  79.7 25.2 %all-to-all-start.1 = ((bf16[8,272,128]{2,1,0:T(8,128)(2,1)}), bf16[8,272,128]{2,1,0:T(8,128)(2,1)S(1)}, u32[]{:S(2)}, u32[]{:S(2)}) async-start(bf16[8,272,128]{2,1,0:T(8,128)(2,1)} %column_part.2.refs_5_), calls=%async_computation.1 | async-start | bytes 1114112 | tf_op jit(solution)/shard_map/all_to_all | solution.py:368
  89.0 7.7 %copy-start.10 = (bf16[2048,512]{1,0:T(8,128)(2,1)S(1)}, bf16[2048,512]{1,0:T(8,128)(2,1)}, u32[]{:S(2)}) copy-start(bf16[2048,512]{1,0:T(8,128)(2,1)} %copy-done.7) | copy-start | bytes 6291460
  89.0 7.7 %copy-start.14 = (bf16[2048,512]{1,0:T(8,128)(2,1)S(1)}, bf16[2048,512]{1,0:T(8,128)(2,1)}, u32[]{:S(2)}) copy-start(bf16[2048,512]{1,0:T(8,128)(2,1)} %copy-done.11) | copy-start | bytes 6291460
  104.8 21.3 %all-to-all-start.3 = ((bf16[8,272,128]{2,1,0:T(8,128)(2,1)}), bf16[8,272,128]{2,1,0:T(8,128)(2,1)S(1)}, u32[]{:S(2)}, u32[]{:S(2)}) async-start(bf16[8,272,128]{2,1,0:T(8,128)(2,1)} %column_part.3.refs_4_), calls=%async_computation.3 | async-start | bytes 1114112 | tf_op jit(solution)/shard_map/all_to_all | solution.py:368
  113.5 1.6 %collective-permute-start.11 = (bf16[2,128,512]{2,1,0:T(8,128)(2,1)S(1)}, bf16[2,128,512]{2,1,0:T(8,128)(2,1)S(1)}, u32[]{:S(2)}, u32[]{:S(2)}) collective-permute-start(bf16[2,128,512]{2,1,0:T(8,128)(2,1)S(1)} %get-tuple-element.38), channel_id=1, source_target_pairs={{0,1},{1,0},{2,3},{3,2},{4,5},{5,4},{6,7},{7,6},{8,9},{9,8},{10,11... | collective-permute-start | bytes 786440 | tf_op jit(solution)/shard_map/ppermute | solution.py:364
  118.9 14.0 %collective-permute-start.12 = (bf16[128,2048]{1,0:T(8,128)(2,1)S(1)}, bf16[128,2048]{1,0:T(8,128)(2,1)S(1)}, u32[]{:S(2)}, u32[]{:S(2)}) collective-permute-start(bf16[128,2048]{1,0:T(8,128)(2,1)S(1)} %get-tuple-element.41), channel_id=1, source_target_pairs={{0,2},{1,3},{2,0},{3,1},{4,6},{5,7},{6,4},{7,5},{8,10},{9,11},{10,... | collective-permute-start | bytes 1572872 | tf_op jit(solution)/shard_map/ppermute | solution.py:364
  128.8 1.6 %collective-permute-start.13 = (bf16[2,128,512]{2,1,0:T(8,128)(2,1)S(1)}, bf16[2,128,512]{2,1,0:T(8,128)(2,1)S(1)}, u32[]{:S(2)}, u32[]{:S(2)}) collective-permute-start(bf16[2,128,512]{2,1,0:T(8,128)(2,1)S(1)} %get-tuple-element.44), channel_id=1, source_target_pairs={{0,1},{1,0},{2,3},{3,2},{4,5},{5,4},{6,7},{7,6},{8,9},{9,8},{10,11... | collective-permute-start | bytes 786440 | tf_op jit(solution)/shard_map/ppermute | solution.py:364
  132.9 16.2 %copy-start.21 = (f32[128,2048]{1,0:T(8,128)S(1)}, f32[128,2048]{1,0:T(8,128)}, u32[]{:S(2)}) copy-start(f32[128,2048]{1,0:T(8,128)} %copy-done.20) | copy-start | bytes 3145732
  135.9 13.2 %collective-permute-start.14 = (bf16[128,2048]{1,0:T(8,128)(2,1)S(1)}, bf16[128,2048]{1,0:T(8,128)(2,1)S(1)}, u32[]{:S(2)}, u32[]{:S(2)}) collective-permute-start(bf16[128,2048]{1,0:T(8,128)(2,1)S(1)} %get-tuple-element.46), channel_id=1, source_target_pairs={{0,2},{1,3},{2,0},{3,1},{4,6},{5,7},{6,4},{7,5},{8,10},{9,11},{10,... | collective-permute-start | bytes 1572872 | tf_op jit(solution)/shard_map/ppermute | solution.py:364
  (27 other events, 68.1 us)

commit v6 on v5

--- a/solution.py
+++ b/solution.py
@@ -1,3 +1,5 @@
+import functools
+
 import jax
 import jax.numpy as jnp
 from jax import lax
@@ -10,7 +12,7 @@
 HEADS = 4
 ROWS = 4
 SUB = 8
-CHUNKS = 2
+NEAR = 4
 SCALE2 = DH ** (-0.5) * 1.4426950408889634
 FLOOR = -1e29
 MIB = 1024 * 1024
@@ -23,7 +25,7 @@
 IN_SMEM = pl.BlockSpec(memory_space=pltpu.SMEM)
 
 
-def call(body, name, micros, out_shape, args, after=(), scratch=(), mib=16):
+def call(body, name, micros, out_shape, args, after=(), scratch=(), mib=24):
     specs = [IN_SMEM if x.dtype == jnp.int32 else IN_VMEM for x in args]
     extra = len(after)
 
@@ -45,18 +47,6 @@
     )(*args, *after)
 
 
-def fence(value, *after):
-    return pl.pallas_call(
-        lambda *refs: None,
-        in_specs=[ANYWHERE] * (1 + len(after)),
-        out_specs=ANYWHERE,
-        out_shape=jax.ShapeDtypeStruct(value.shape, value.dtype),
-        input_output_aliases={0: 0},
-        cost_estimate=pl.CostEstimate(flops=0, bytes_accessed=0, transcendentals=0),
-        name="fence",
-    )(value, *after)
-
-
 def in_hbm(value):
     return pltpu.with_memory_space_constraint(value, pltpu.HBM)
 
@@ -77,12 +67,10 @@
     return lax.dot_general(a, b, (((0,), (0,)), ((), ())), preferred_element_type=F32)
 
 
-def pack_kernel(tok_hbm, *rest):
+def pack_kernel(pos_ref, tok_hbm, *rest):
     out_refs, (tok_ref, sems) = rest[:-2], rest[-2:]
-    owners = out_refs[0].shape[0]
-    per_owner = STRIDE // owners
-    groups = per_owner // SUB
-    per_chunk = groups // CHUNKS
+    per_owner = STRIDE // len(out_refs)
+    part = ROWS * SUB
     spans = [slice(r * STRIDE, (r + 1) * STRIDE) for r in range(ROWS)]
     copies = [
         pltpu.make_async_copy(tok_hbm.at[at], tok_ref.at[at], sems.at[r])
@@ -92,29 +80,30 @@
         c.start()
     for c in copies:
         c.wait()
-    for d in range(owners):
+    for k, out_ref in enumerate(out_refs):
+        d = pos_ref[0] ^ k
         rows = [
-            tok_ref[r * STRIDE + d * per_owner : r * STRIDE + (d + 1) * per_owner, :].astype(F32)
+            tok_ref[pl.ds(pl.multiple_of(r * STRIDE + d * per_owner, per_owner), per_owner), :]
             for r in range(ROWS)
         ]
-        for g in range(groups):
+        rows = [x.astype(F32) for x in rows]
+        for g in range(per_owner // SUB):
             piece = jnp.concatenate([x[g * SUB : (g + 1) * SUB] for x in rows], 0)
-            at = (g % per_chunk) * ROWS * SUB
-            out_refs[g // per_chunk][d, at : at + ROWS * SUB, :] = piece.astype(BF16)
-
-
-def pack(tokens, owners):
-    message = tokens.shape[0] // owners // CHUNKS
+            out_ref[g * part : (g + 1) * part, :] = piece.astype(BF16)
+
+
+def pack(pos, tokens, owners):
+    message = tokens.shape[0] // owners
     return pl.pallas_call(
         pack_kernel,
-        in_specs=[ANYWHERE],
-        out_specs=[IN_VMEM] * CHUNKS,
-        out_shape=[shape((owners, message, tokens.shape[1]))] * CHUNKS,
+        in_specs=[IN_SMEM, ANYWHERE],
+        out_specs=[IN_VMEM] * owners,
+        out_shape=[shape((message, tokens.shape[1]))] * owners,
         scratch_shapes=[pltpu.VMEM(tokens.shape, BF16), pltpu.SemaphoreType.DMA((ROWS,))],
         compiler_params=pltpu.CompilerParams(vmem_limit_bytes=8 * MIB),
         cost_estimate=pl.CostEstimate(flops=0, bytes_accessed=2 * MIB, transcendentals=0),
         name="pack_tokens",
-    )(in_hbm(tokens))
+    )(pos, in_hbm(tokens))
 
 
 def stage_kernel(order_ref, wq, wk, wv, wo, *rest):
@@ -172,6 +161,12 @@
         out[:upto, :] = gathered(xs, slice(0, upto), w)
 
 
+def near_kernel(x0, x1, x2, x3, wq, wk, wv, q_ref, k_ref, v_ref):
+    everything = slice(0, x0.shape[0])
+    for w, out in ((wq, q_ref), (wk, k_ref), (wv, v_ref)):
+        out[...] = gathered((x0, x1, x2, x3), everything, w)
+
+
 def softmax_columns(s):
     m = jnp.maximum(jnp.max(s, 0, keepdims=True), FLOOR)
     p = jnp.exp2((s - m) * SCALE2)
@@ -179,9 +174,8 @@
     return p, total, m * SCALE2 + jnp.log2(total)
 
 
-def local_kernel(pos_ref, q_ref, k_ref, v_ref, halo_ref, *outs):
-    out_refs, lse_refs = outs[:CHUNKS], outs[CHUNKS:]
-    owners, message, _ = out_refs[0].shape
+def local_kernel(pos_ref, q_ref, k_ref, v_ref, halo_ref, out_ref, lse_ref):
+    owners, message, _ = out_ref.shape
     groups = message // ROWS // SUB
     block = pos_ref[0]
     u = lax.broadcasted_iota(jnp.int32, (STRIDE, STRIDE), 0)
@@ -207,44 +201,47 @@
             o = (o * (1.0 / total)).T
             lses.append(lse)
             for d in range(owners):
-                for i in range(CHUNKS):
-                    for g in range(groups):
-                        at = ((d * CHUNKS + i) * groups + g) * SUB
-                        to = (g * ROWS + r) * SUB
-                        out_refs[i][d, to : to + SUB, cols] = o[at : at + SUB]
+                for g in range(groups):
+                    at = (d * groups + g) * SUB
+                    to = (g * ROWS + r) * SUB
+                    out_ref[d, to : to + SUB, cols] = o[at : at + SUB]
         lses.append(jnp.zeros((128 - HEADS, STRIDE), F32))
         turned = jnp.concatenate(lses, 0).T
-        for i in range(CHUNKS):
-            for g in range(groups):
-                total = None
-                for d in range(owners):
-                    at = ((d * CHUNKS + i) * groups + g) * SUB
-                    moved = pltpu.roll(turned[at : at + SUB], 8 * d, 1)
-                    total = moved if total is None else total + moved
-                to = (g * ROWS + r) * SUB
-                lse_refs[i][to : to + SUB, :] = total
+        for g in range(groups):
+            total = None
+            for d in range(owners):
+                at = (d * groups + g) * SUB
+                moved = pltpu.roll(turned[at : at + SUB], 8 * (block ^ d), 1)
+                total = moved if total is None else total + moved
+            to = (g * ROWS + r) * SUB
+            lse_ref[to : to + SUB, :] = total
 
 
 def local_part(pos, q, k, v, halo, owners, after):
     rows, width = q.shape
-    message = rows // owners // CHUNKS
-    shapes = [shape((owners, message, width), F32)] * CHUNKS + [shape((message, 128), F32)] * CHUNKS
-    outs = call(local_kernel, "local_part", 5, shapes, (pos, q, k, v, halo), after)
-    return list(zip(outs[:CHUNKS], outs[CHUNKS:]))
-
-
-def column_kernel(x0, x1, x2, x3, wq, wk, wv, out_ref, *scratch):
-    owners, message, _ = scratch[0].shape
+    message = rows // owners
+    shapes = [shape((owners, message, width), F32), shape((message, 128), F32)]
+    return call(local_kernel, "local_part", 5, shapes, (pos, q, k, v, halo), after)
+
+
+def column_kernel(pos_ref, x0, x1, x2, x3, wq, wk, wv, nq, nk, nv, *rest):
+    out_refs, scratch = rest[:-3], rest[-3:]
+    owners, message, width = scratch[0].shape
     groups = message // (ROWS * SUB)
-    everything = slice(0, owners * message)
-    for w, a in zip((wq, wk, wv), scratch):
-        a[...] = gathered((x0, x1, x2, x3), everything, w).reshape(a.shape)
+    everything = slice(0, x0.shape[0])
+    for w, near, a in zip((wq, wk, wv), (nq, nk, nv), scratch):
+        a[:NEAR] = near[...].reshape(NEAR, message, width)
+        far = gathered((x0, x1, x2, x3), everything, w)
+        a[NEAR:] = far.reshape(owners - NEAR, message, width)
     part = ROWS * SUB
     size = owners * part
 
-    j = lax.broadcasted_iota(jnp.int32, (size, size), 0)
-    i = lax.broadcasted_iota(jnp.int32, (size, size), 1)
-    earlier = jnp.logical_and(i % SUB == j % SUB, i > j)
+    def row_and_class(dim):
+        i = lax.broadcasted_iota(jnp.int32, (size, size), dim)
+        return ((i // part) ^ pos_ref[0]) * ROWS + (i % part) // SUB, i % SUB
+
+    (row_j, class_j), (row_i, class_i) = row_and_class(0), row_and_class(1)
+    earlier = jnp.logical_and(class_i == class_j, row_i > row_j)
     stats = []
     for g in range(groups):
         at = slice(g * part, (g + 1) * part)
@@ -255,7 +252,8 @@
             p, total, lse = softmax_columns(jnp.where(earlier, dot_t(k, q), -1e30))
             o = (dot_l(v, p.astype(BF16)) * (1.0 / total)).T.astype(BF16)
             rows = slice(h * message + g * part, h * message + (g + 1) * part)
-            out_ref[:, rows, :] = o.reshape(owners, part, DH)
+            for n in range(owners):
+                out_refs[n][rows, :] = o[n * part : (n + 1) * part]
             lses.append(lse)
         stats.append(jnp.concatenate(lses + lses, 0))
     upper = lax.broadcasted_iota(jnp.int32, (8, 128), 0) < HEADS
@@ -266,26 +264,27 @@
         mid = (x - hi).astype(BF16).astype(F32)
         lo = x - hi - mid
         tail = jnp.concatenate([jnp.where(upper, hi, lo), jnp.where(upper, mid, 0.0)], 0)
-        out_ref[n, HEADS * message : HEADS * message + 16, :] = tail.astype(BF16)
-
-
-def column_part(pieces, weights, after):
-    owners, message, width = pieces[0].shape
-    dims = shape((owners, HEADS * message + 16, DH))
+        out_refs[n][HEADS * message : HEADS * message + 16, :] = tail.astype(BF16)
+
+
+def column_part(pos, pieces, weights, near, owners, after):
+    tokens, width = pieces[0].shape
+    message = tokens // (owners - NEAR)
+    shapes = [shape((HEADS * message + 16, DH))] * owners
     scratch = [pltpu.VMEM((owners, message, width), BF16)] * 3
-    pieces = [x.reshape(owners * message, width) for x in pieces]
-    return call(column_kernel, "column_part", 6, dims, (*pieces, *weights), after, scratch)
-
-
-def mix_kernel(pos_ref, loc_ref, lse_ref, col_ref, own_ref, send_ref, mixed):
+    args = (pos, *pieces, *weights, *near)
+    return call(column_kernel, "column_part", 9, shapes, args, after, scratch)
+
+
+def mix_kernel(first, pos_ref, loc_ref, lse_ref, *rest):
+    col_refs, (own_ref, send_ref, mixed) = rest[:-3], rest[-3:]
     owners, message, _ = loc_ref.shape
     groups = message // (ROWS * SUB)
     base = HEADS * message
-    tiles = []
-    for d in range(owners):
-        tail = col_ref[d, base : base + 16, :].astype(F32)
-        tiles.append(tail[:8] + tail[8:])
-    tiles.append(jnp.zeros((128 - 8 * owners, 128), F32))
+    tiles = [jnp.zeros((8, 128), F32)] * 16
+    for n, col_ref in enumerate(col_refs):
+        tail = col_ref[base : base + 16, :].astype(F32)
+        tiles[first + n] = tail[:8] + tail[8:]
     turned = jnp.concatenate(tiles, 0).T[:message]
     col_lse = turned + pltpu.roll(turned, 124, 1)
     loc_lse = lse_ref[...]
@@ -296,12 +295,14 @@
     w_col = w_col * share
     w_loc = w_loc * share
     span = groups * SUB
-    for d in range(owners):
-        spot = slice(d * span, (d + 1) * span)
+    for n, col_ref in enumerate(col_refs):
+        k = first + n
+        d = pos_ref[0] ^ k
+        spot = slice(n * span, (n + 1) * span)
         for h in range(HEADS):
             cols = slice(h * DH, (h + 1) * DH)
-            at = slice(8 * d + h, 8 * d + h + 1)
-            col = col_ref[d, h * message : (h + 1) * message, :].astype(F32)
+            at = slice(8 * k + h, 8 * k + h + 1)
+            col = col_ref[h * message : (h + 1) * message, :].astype(F32)
             both = loc_ref[d, :, cols] * w_loc[:, at] + col * w_col[:, at]
             for r in range(ROWS):
                 starts = [(g * ROWS + r) * SUB for g in range(groups)]
@@ -313,12 +314,13 @@
         send_ref[x] = mixed[2 * x + 1 - core]
 
 
-def mix(pos, column, local, lse, after):
-    owners, message, width = local.shape
-    tokens = owners * message // ROWS
+def mix(pos, first, columns, local, lse, after):
+    _, message, width = local.shape
+    tokens = len(columns) * message // ROWS
     shapes = [shape((2, tokens, width))] * 2
     scratch = [pltpu.VMEM((ROWS, tokens, width), BF16)]
-    return call(mix_kernel, "mix", 2, shapes, (pos, local, lse, column), after, scratch)
+    body = functools.partial(mix_kernel, first)
+    return call(body, "mix", 2, shapes, (pos, local, lse, *columns), after, scratch)
 
 
 def out_kernel(pos_ref, a_ref, b_ref, wa_ref, wb_ref, send_ref, keep_ref):
@@ -340,24 +342,22 @@
     return call(out_kernel, "out_project", 2, shapes, (pos, own, other, w_own, w_other), after)
 
 
-def join_kernel(*refs):
+def join_kernel(pos_ref, *refs):
     out_ref = refs[-1]
-    chunks = (len(refs) - 1) // 2
-    tokens = refs[0].shape[0]
-    span = 32 // chunks
-    for i in range(chunks):
-        keep, got = refs[2 * i], refs[2 * i + 1]
-        for d in range(tokens // span):
-            rows = slice(d * span, (d + 1) * span)
-            at = (d * chunks + i) * span
-            total = keep[rows, :] + got[rows, :].astype(F32)
-            out_ref[at : at + span, :] = total.astype(BF16)
-
-
-def join(pairs):
+    span = STRIDE // 8
+    k = 0
+    for keep, got in zip(refs[0:-1:2], refs[1:-1:2]):
+        for n in range(keep.shape[0] // span):
+            rows = slice(n * span, (n + 1) * span)
+            to = pl.ds(pl.multiple_of((pos_ref[0] ^ k) * span, span), span)
+            out_ref[to, :] = (keep[rows, :] + got[rows, :].astype(F32)).astype(BF16)
+            k += 1
+
+
+def join(pos, pairs):
     columns = pairs[0][0].shape[1]
     args = [x for pair in pairs for x in pair]
-    return call(join_kernel, "join", 2, shape((STRIDE, columns)), args)
+    return call(join_kernel, "join", 2, shape((STRIDE, columns)), (pos, *args))
 
 
 def swap(value, distance):
@@ -365,7 +365,10 @@
 
 
 def exchange(messages):
-    return lax.all_to_all(messages, "seq", split_axis=0, concat_axis=0, tiled=True)
+    n = len(messages)
+    return [messages[0]] + [
+        lax.ppermute(messages[k], "seq", [(i, i ^ k) for i in range(n)]) for k in range(1, n)
+    ]
 
 
 def gather(own):
@@ -382,37 +385,36 @@
     rows, width = tokens.shape
 
     pieces = gather(tokens)
-    messages = pack(tokens, owners)
-    classes = [exchange(m) for m in messages]
-    *weights, w_own = stage(order, (w_query, w_key, w_value, w_out), (messages[0], pieces[1]))
+    sent = pack(pos, tokens, owners)
+    messages = exchange(sent)
+    *weights, w_own = stage(order, (w_query, w_key, w_value, w_out), (sent[0], pieces[1]))
     w_other = swap(w_out, 1)
-    classes[0] = fence(classes[0], pieces[2], weights[0], w_other)
+    near_own = jnp.concatenate(messages[:NEAR], 0)
+    far_own = jnp.concatenate(messages[NEAR:], 0)
+    near_pieces, far_pieces = gather(near_own), gather(far_own)
+    half = [shape((2 * STRIDE, width))]
     own_halo = call(
-        halo_kernel, "project_halo", 1.5, shape((2 * STRIDE, width)), (*pieces, *weights[1:])
+        halo_kernel, "project_halo", 1.5, half[0], (*pieces, *weights[1:]), (near_own,)
     )
     halo = lax.ppermute(own_halo, "seq", [(i, i + 1) for i in range(owners - 1)])
     q, k, v = call(
         project_kernel,
         "project_block",
-        7,
+        6,
         [shape((rows, width))] * 3,
         (*pieces, *weights, own_halo),
-        (classes[0],),
-        mib=20,
-    )
-    columns, after = [], (q,)
-    for i, c in enumerate(classes):
-        columns.append(column_part(gather(c), weights, after))
-        if i == 0:
-            locals_ = local_part(pos, q, k, v, halo, owners, (columns[0],))
-            after = (locals_[-1][-1],)
+        (far_own,),
+    )
+    near = call(near_kernel, "project_near", 3, half * 3, (*near_pieces, *weights), (q,))
+    local, lse = local_part(pos, q, k, v, halo, owners, (near[0],))
+    columns = exchange(column_part(pos, far_pieces, weights, near, owners, (lse,)))
     pairs, after = [], ()
-    for column, (local, lse) in zip(columns, locals_):
-        own, send = mix(pos, exchange(column), local, lse, (columns[-1],))
+    for first, some in ((0, columns[:NEAR]), (NEAR, columns[NEAR:])):
+        own, send = mix(pos, first, some, local, lse, tuple(x for x, _ in pairs))
         out, keep = out_project(pos, own, swap(send, 1), w_own, w_other, after)
         pairs.append((keep, swap(out, 2)))
-        after = (pairs[-1][1],)
-    return join(pairs)
+        after = (pairs[0][1],)
+    return join(pos, pairs)
 
 
 def from_behind(value, axis, by):
@@ -558,7 +560,7 @@
 def shards(tokens, w_query, w_key, w_value, w_out):
     rows, width = w_query.shape
     fits = (
-        lax.axis_size("seq") == STRIDE // 32
+        lax.axis_size("seq") == 2 * NEAR
         and lax.axis_size("head") == 4
         and tokens.shape == (ROWS * STRIDE, HEADS * DH)
         and (rows, width) == (4 * HEADS * DH, HEADS * DH)

time: 151 us -> 152 us (level)
  the two profiles are of different devices: /device:TPU:0 before, /device:TPU:8 now
where the time goes in v6:
time: 152 us; the launch traced here: 151 us
  waiting for transfers between devices  75.5 us (50%)
  Pallas kernels  39.1 us (26%)
  starting transfers between devices  36.5 us (24%)
    ppermute x14, waiting for transfers between devices, exchange(): lax.ppermute(messages[k], 'seq', [(i, i ^ k) for i in range(n)])  37.2 us
    ppermute x14, waiting for transfers between devices, swap(): return lax.ppermute(value, 'head', [(i, i ^ distance) for i in range(4)])  35 us
    pallas_call x10, Pallas kernels, call(): pl.pallas_call(run, in_specs=specs + [ANYWHERE] * extra, out_specs=jax.tr...  33.1 us
    ppermute x14, starting transfers between devices, exchange(): lax.ppermute(messages[k], 'seq', [(i, i ^ k) for i in range(n)])  25.6 us
    ppermute x14, starting transfers between devices, swap(): return lax.ppermute(value, 'head', [(i, i ^ distance) for i in range(4)])  6.8 us
    pallas_call x1, Pallas kernels, stage(): pl.pallas_call(stage_kernel, in_specs=[IN_SMEM] + [ANYWHERE] * (4 + len(a...  4.1 us
    ppermute x1, starting transfers between devices, chunked(): lax.ppermute(own_halo, 'seq', [(i, i + 1) for i in range(owners - 1)])  4.06 us
    ppermute x1, waiting for transfers between devices, chunked(): lax.ppermute(own_halo, 'seq', [(i, i + 1) for i in range(owners - 1)])  3.26 us
  transfers between devices with their start and end apart: 29, of which 16 were waited for; matrix products, arithmetic and copies ran while one was open for 0% of the time, Pallas kernels for 23%

profile of v6, /device:TPU:8, one launch (start us, length us, event | category | flops | bytes accessed | tf_op | source)
XLA Modules:
  0.0 151.5 jit_solution(18426067120732574170)
XLA Ops:
  5.0 20.1 %collective-permute-done.1.refs_2_ = bf16[1024,512]{1,0:T(8,128)(2,1)S(1)} collective-permute-done((bf16[1024,512]{1,0:T(8,128)(2,1)}, bf16[1024,512]{1,0:T(8,128)(2,1)S(1)}, u32[]{:S(2)}, u32[]{:S(2)}) %collective-permute-start.1) | collective-permute-done | bytes 1048608 | tf_op jit(solution)/shard_map/ppermute | solution.py:364
  25.3 2.8 %collective-permute-start.5 = (bf16[128,512]{1,0:T(8,128)(2,1)S(1)}, bf16[128,512]{1,0:T(8,128)(2,1)S(1)}, u32[]{:S(2)}, u32[]{:S(2)}) collective-permute-start(bf16[128,512]{1,0:T(8,128)(2,1)S(1)} %get-tuple-element.47), channel_id=1, source_target_pairs={{0,12},{4,8},{8,4},{12,0},{16,28},{20,24},{24,20},{28,16},{1,13},{... | collective-permute-start | bytes 393224 | tf_op jit(solution)/shard_map/ppermute | solution.py:370
  28.1 2.7 %collective-permute-start.6 = (bf16[128,512]{1,0:T(8,128)(2,1)S(1)}, bf16[128,512]{1,0:T(8,128)(2,1)S(1)}, u32[]{:S(2)}, u32[]{:S(2)}) collective-permute-start(bf16[128,512]{1,0:T(8,128)(2,1)S(1)} %get-tuple-element.48), channel_id=1, source_target_pairs={{0,16},{4,20},{8,24},{12,28},{16,0},{20,4},{24,8},{28,12},{1,17},{... | collective-permute-start | bytes 393224 | tf_op jit(solution)/shard_map/ppermute | solution.py:370
  31.4 6.4 %collective-permute-start.7 = (bf16[128,512]{1,0:T(8,128)(2,1)S(1)}, bf16[128,512]{1,0:T(8,128)(2,1)S(1)}, u32[]{:S(2)}, u32[]{:S(2)}) collective-permute-start(bf16[128,512]{1,0:T(8,128)(2,1)S(1)} %get-tuple-element.49), channel_id=1, source_target_pairs={{0,20},{4,16},{8,28},{12,24},{16,4},{20,0},{24,12},{28,8},{1,21},{... | collective-permute-start | bytes 393224 | tf_op jit(solution)/shard_map/ppermute | solution.py:370
  40.0 4.1 %collective-permute-done.7 = bf16[128,512]{1,0:T(8,128)(2,1)S(1)} collective-permute-done((bf16[128,512]{1,0:T(8,128)(2,1)S(1)}, bf16[128,512]{1,0:T(8,128)(2,1)S(1)}, u32[]{:S(2)}, u32[]{:S(2)}) %collective-permute-start.7) | collective-permute-done | bytes 131104 | tf_op jit(solution)/shard_map/ppermute | solution.py:370
  44.1 2.3 %collective-permute-start.9 = (bf16[128,512]{1,0:T(8,128)(2,1)S(1)}, bf16[128,512]{1,0:T(8,128)(2,1)S(1)}, u32[]{:S(2)}, u32[]{:S(2)}) collective-permute-start(bf16[128,512]{1,0:T(8,128)(2,1)S(1)} %get-tuple-element.51), channel_id=1, source_target_pairs={{0,28},{4,24},{8,20},{12,16},{16,12},{20,8},{24,4},{28,0},{1,29},{... | collective-permute-start | bytes 393224 | tf_op jit(solution)/shard_map/ppermute | solution.py:370
  46.4 3.4 %collective-permute-done.8 = bf16[128,512]{1,0:T(8,128)(2,1)S(1)} collective-permute-done((bf16[128,512]{1,0:T(8,128)(2,1)S(1)}, bf16[128,512]{1,0:T(8,128)(2,1)S(1)}, u32[]{:S(2)}, u32[]{:S(2)}) %collective-permute-start.8) | collective-permute-done | bytes 131104 | tf_op jit(solution)/shard_map/ppermute | solution.py:370
  49.9 3.5 %collective-permute-done.9 = bf16[128,512]{1,0:T(8,128)(2,1)S(1)} collective-permute-done((bf16[128,512]{1,0:T(8,128)(2,1)S(1)}, bf16[128,512]{1,0:T(8,128)(2,1)S(1)}, u32[]{:S(2)}, u32[]{:S(2)}) %collective-permute-start.9) | collective-permute-done | bytes 131104 | tf_op jit(solution)/shard_map/ppermute | solution.py:370
  55.2 4.1 %stage_weights.1 = (bf16[2048,512]{1,0:T(8,128)(2,1)S(1)}, bf16[2048,512]{1,0:T(8,128)(2,1)S(1)}, bf16[2048,512]{1,0:T(8,128)(2,1)S(1)}, bf16[512,2048]{1,0:T(8,128)(2,1)S(1)}) custom-call(s32[4]{0:T(128)S(1)} %iota_xor_fusion.order_ref, bf16[2048,512]{1,0:T(8,128)(2,1)} %wq.1, bf16[2048,512]{1,0:T(8,128)(2,1)} %wk.1, bf16[2048,512]{1,0:T(8,128)(2,1)} %wv.1, ...), custom_call_target="tpu_custom_call" | custom-call | bytes 8388608 | tf_op jit(solution)/shard_map/stage_weights/pallas_call | solution.py:126
  60.6 4.1 %collective-permute-start.10 = (bf16[512,512]{1,0:T(8,128)(2,1)S(1)}, bf16[512,512]{1,0:T(8,128)(2,1)S(1)}, u32[]{:S(2)}, u32[]{:S(2)}) collective-permute-start(bf16[512,512]{1,0:T(8,128)(2,1)S(1)} %project_halo.1.refs_7_), channel_id=1, source_target_pairs={{0,4},{4,8},{8,12},{12,16},{16,20},{20,24},{24,28},{1,5},{5,9},{9,... | collective-permute-start | bytes 1572872 | tf_op jit(solution)/shard_map/ppermute | solution.py:399
  64.6 5.6 %project_block.1 = (bf16[1024,512]{1,0:T(8,128)(2,1)S(1)}, bf16[1024,512]{1,0:T(8,128)(2,1)S(1)}, bf16[1024,512]{1,0:T(8,128)(2,1)S(1)}) custom-call(bf16[1024,512]{1,0:T(8,128)(2,1)S(1)} %copy-done, bf16[1024,512]{1,0:T(8,128)(2,1)S(1)} %collective-permute-done.rest_1_.refs_1_, bf16[1024,512]{1,0:T(8,128)(2,1)S(1)} %collective-permute-done.1.refs_2_, ...), custom_call_target="tpu_custom_call" | custom-call | flops 6600000000 | bytes 1048576 | tf_op jit(solution)/shard_map/project_block/pallas_call | solution.py:36
  70.8 3.4 %project_near.1 = (bf16[512,512]{1,0:T(8,128)(2,1)S(1)}, bf16[512,512]{1,0:T(8,128)(2,1)S(1)}, bf16[512,512]{1,0:T(8,128)(2,1)S(1)}) custom-call(bf16[512,512]{1,0:T(8,128)(2,1)S(1)} %constant_dynamic-update-slice_fusion.refs_6_.refs_0_, bf16[512,512]{1,0:T(8,128)(2,1)S(1)} %collective-permute-done.11.refs_1_, ...), custom_call_target="tpu_custom_call" | custom-call | flops 3300000000 | bytes 1048576 | tf_op jit(solution)/shard_map/project_near/pallas_call | solution.py:36
  74.2 3.3 %collective-permute-done.10.refs_4_ = bf16[512,512]{1,0:T(8,128)(2,1)S(1)} collective-permute-done((bf16[512,512]{1,0:T(8,128)(2,1)S(1)}, bf16[512,512]{1,0:T(8,128)(2,1)S(1)}, u32[]{:S(2)}, u32[]{:S(2)}) %collective-permute-start.10) | collective-permute-done | bytes 524320 | tf_op jit(solution)/shard_map/ppermute | solution.py:399
  77.5 5.8 %local_part.1 = (f32[8,128,512]{2,1,0:T(8,128)S(1)}, f32[128,128]{1,0:T(8,128)S(1)}) custom-call(s32[3]{0:T(128)S(1)} %pad_add_fusion.pos_ref.refs_0_, bf16[1024,512]{1,0:T(8,128)(2,1)S(1)} %get-tuple-element.52.refs_7_.refs_1_, bf16[1024,512]{1,0:T(8,128)(2,1)S(1)} %get-tuple-element.53.refs_2_, bf16[1024,512]{1,0:T(8,128)(2,1)S(1)} %get-tuple-element.54.refs_3_, ...), custom_call_target="tpu_custom_call" | custom-call | flops 5500000256 | bytes 1048576 | tf_op jit(solution)/shard_map/local_part/pallas_call | solution.py:36
  83.2 9.0 %column_part.1 = (bf16[528,128]{1,0:T(8,128)(2,1)S(1)}, bf16[528,128]{1,0:T(8,128)(2,1)S(1)}, bf16[528,128]{1,0:T(8,128)(2,1)S(1)}, bf16[528,128]{1,0:T(8,128)(2...) custom-call(s32[3]{0:T(128)S(1)} %pad_add_fusion.pos_ref.refs_0_, ...), custom_call_target="tpu_custom_call" | custom-call | flops 9900000256 | bytes 1048576 | tf_op jit(solution)/shard_map/column_part/pallas_call | solution.py:36
  97.3 2.6 %collective-permute-done.18.refs_5_ = bf16[528,128]{1,0:T(8,128)(2,1)S(1)} collective-permute-done((bf16[528,128]{1,0:T(8,128)(2,1)S(1)}, bf16[528,128]{1,0:T(8,128)(2,1)S(1)}, u32[]{:S(2)}, u32[]{:S(2)}) %collective-permute-start.18) | collective-permute-done | bytes 135200 | tf_op jit(solution)/shard_map/ppermute | solution.py:370
  103.2 3.0 %collective-permute-start.23 = (bf16[528,128]{1,0:T(8,128)(2,1)S(1)}, bf16[528,128]{1,0:T(8,128)(2,1)S(1)}, u32[]{:S(2)}, u32[]{:S(2)}) collective-permute-start(bf16[528,128]{1,0:T(8,128)(2,1)S(1)} %get-tuple-element.69), channel_id=1, source_target_pairs={{0,16},{4,20},{8,24},{12,28},{16,0},{20,4},{24,8},{28,12},{1,17},{... | collective-permute-start | bytes 405512 | tf_op jit(solution)/shard_map/ppermute | solution.py:370
  106.7 1.9 %collective-permute-start.25 = (bf16[528,128]{1,0:T(8,128)(2,1)S(1)}, bf16[528,128]{1,0:T(8,128)(2,1)S(1)}, u32[]{:S(2)}, u32[]{:S(2)}) collective-permute-start(bf16[528,128]{1,0:T(8,128)(2,1)S(1)} %get-tuple-element.71), channel_id=1, source_target_pairs={{0,24},{4,28},{8,16},{12,20},{16,8},{20,12},{24,0},{28,4},{1,25},{... | collective-permute-start | bytes 405512 | tf_op jit(solution)/shard_map/ppermute | solution.py:370
  111.8 9.7 %collective-permute-done.23.refs_3_ = bf16[528,128]{1,0:T(8,128)(2,1)S(1)} collective-permute-done((bf16[528,128]{1,0:T(8,128)(2,1)S(1)}, bf16[528,128]{1,0:T(8,128)(2,1)S(1)}, u32[]{:S(2)}, u32[]{:S(2)}) %collective-permute-start.23) | collective-permute-done | bytes 135200 | tf_op jit(solution)/shard_map/ppermute | solution.py:370
  121.5 2.9 %collective-permute-done.24.refs_4_ = bf16[528,128]{1,0:T(8,128)(2,1)S(1)} collective-permute-done((bf16[528,128]{1,0:T(8,128)(2,1)S(1)}, bf16[528,128]{1,0:T(8,128)(2,1)S(1)}, u32[]{:S(2)}, u32[]{:S(2)}) %collective-permute-start.24) | collective-permute-done | bytes 135200 | tf_op jit(solution)/shard_map/ppermute | solution.py:370
  124.4 3.3 %collective-permute-done.25.refs_5_ = bf16[528,128]{1,0:T(8,128)(2,1)S(1)} collective-permute-done((bf16[528,128]{1,0:T(8,128)(2,1)S(1)}, bf16[528,128]{1,0:T(8,128)(2,1)S(1)}, u32[]{:S(2)}, u32[]{:S(2)}) %collective-permute-start.25) | collective-permute-done | bytes 135200 | tf_op jit(solution)/shard_map/ppermute | solution.py:370
  127.6 3.3 %collective-permute-done.26.refs_6_ = bf16[528,128]{1,0:T(8,128)(2,1)S(1)} collective-permute-done((bf16[528,128]{1,0:T(8,128)(2,1)S(1)}, bf16[528,128]{1,0:T(8,128)(2,1)S(1)}, u32[]{:S(2)}, u32[]{:S(2)}) %collective-permute-start.26) | collective-permute-done | bytes 135200 | tf_op jit(solution)/shard_map/ppermute | solution.py:370
  133.9 1.9 %out_project.3 = (bf16[128,2048]{1,0:T(8,128)(2,1)S(1)}, f32[128,2048]{1,0:T(8,128)S(1)}) custom-call(s32[3]{0:T(128)S(1)} %pad_add_fusion.pos_ref.refs_0_, bf16[2,128,512]{2,1,0:T(8,128)(2,1)S(1)} %get-tuple-element.73.refs_1_, bf16[2,128,512]{2,1,0:T(8,128)(2,1)S(1)} %collective-permute-done.27.refs_2_, bf16[512,2048]{1,0:T(8,128)(2,1)S(1)} %get-tuple-element.66.refs_3_, ...), custom_call_target="tpu_custom_call" | custom-call | flops 2200000000 | bytes 1048576 | tf_op jit(solution)/shard_map/out_project/pallas_call | solution.py:36
  136.4 13.4 %collective-permute-done.28.refs_4_ = bf16[128,2048]{1,0:T(8,128)(2,1)S(1)} collective-permute-done((bf16[128,2048]{1,0:T(8,128)(2,1)S(1)}, bf16[128,2048]{1,0:T(8,128)(2,1)S(1)}, u32[]{:S(2)}, u32[]{:S(2)}) %collective-permute-start.28) | collective-permute-done | bytes 524320 | tf_op jit(solution)/shard_map/ppermute | solution.py:364
  (60 shorter events, 29.0 us)
Async XLA Ops:
  0.0 25.1 %collective-permute-start.1 = (bf16[1024,512]{1,0:T(8,128)(2,1)}, bf16[1024,512]{1,0:T(8,128)(2,1)S(1)}, u32[]{:S(2)}, u32[]{:S(2)}) collective-permute-start(bf16[1024,512]{1,0:T(8,128)(2,1)} %refs_0_.3), channel_id=1, source_target_pairs={{0,2},{1,3},{2,0},{3,1},{4,6},{5,7},{6,4},{7,5},{8,10},{9,11},{10,... | collective-permute-start | bytes 3145736 | tf_op jit(solution)/shard_map/ppermute | solution.py:364
  3.4 24.7 %collective-permute-start.3 = (bf16[128,512]{1,0:T(8,128)(2,1)S(1)}, bf16[128,512]{1,0:T(8,128)(2,1)S(1)}, u32[]{:S(2)}, u32[]{:S(2)}) collective-permute-start(bf16[128,512]{1,0:T(8,128)(2,1)S(1)} %get-tuple-element.45), channel_id=1, source_target_pairs={{0,4},{4,0},{8,12},{12,8},{16,20},{20,16},{24,28},{28,24},{1,5},{5... | collective-permute-start | bytes 393224 | tf_op jit(solution)/shard_map/ppermute | solution.py:370
  5.0 50.0 %collective-permute-start = (bf16[1024,512]{1,0:T(8,128)(2,1)}, bf16[1024,512]{1,0:T(8,128)(2,1)S(1)}, u32[]{:S(2)}, u32[]{:S(2)}) collective-permute-start(bf16[1024,512]{1,0:T(8,128)(2,1)} %refs_0_.3), channel_id=1, source_target_pairs={{0,1},{1,0},{2,3},{3,2},{4,5},{5,4},{6,7},{7,6},{8,9},{9,8},{10,11... | collective-permute-start | bytes 3145736 | tf_op jit(solution)/shard_map/ppermute | solution.py:364
  25.1 34.2 %collective-permute-start.2 = (bf16[1024,512]{1,0:T(8,128)(2,1)S(1)}, bf16[1024,512]{1,0:T(8,128)(2,1)S(1)}, u32[]{:S(2)}, u32[]{:S(2)}) collective-permute-start(bf16[1024,512]{1,0:T(8,128)(2,1)S(1)} %collective-permute-done.1.refs_2_), channel_id=1, source_target_pairs={{0,1},{1,0},{2,3},{3,2},{4,5},{5,4},{6,7},{7,6},{8,9},{9,8},{10,11... | collective-permute-start | bytes 3145736 | tf_op jit(solution)/shard_map/ppermute | solution.py:364
  25.3 12.5 %collective-permute-start.5 = (bf16[128,512]{1,0:T(8,128)(2,1)S(1)}, bf16[128,512]{1,0:T(8,128)(2,1)S(1)}, u32[]{:S(2)}, u32[]{:S(2)}) collective-permute-start(bf16[128,512]{1,0:T(8,128)(2,1)S(1)} %get-tuple-element.47), channel_id=1, source_target_pairs={{0,12},{4,8},{8,4},{12,0},{16,28},{20,24},{24,20},{28,16},{1,13},{... | collective-permute-start | bytes 393224 | tf_op jit(solution)/shard_map/ppermute | solution.py:370
  28.1 11.9 %collective-permute-start.6 = (bf16[128,512]{1,0:T(8,128)(2,1)S(1)}, bf16[128,512]{1,0:T(8,128)(2,1)S(1)}, u32[]{:S(2)}, u32[]{:S(2)}) collective-permute-start(bf16[128,512]{1,0:T(8,128)(2,1)S(1)} %get-tuple-element.48), channel_id=1, source_target_pairs={{0,16},{4,20},{8,24},{12,28},{16,0},{20,4},{24,8},{28,12},{1,17},{... | collective-permute-start | bytes 393224 | tf_op jit(solution)/shard_map/ppermute | solution.py:370
  31.4 12.7 %collective-permute-start.7 = (bf16[128,512]{1,0:T(8,128)(2,1)S(1)}, bf16[128,512]{1,0:T(8,128)(2,1)S(1)}, u32[]{:S(2)}, u32[]{:S(2)}) collective-permute-start(bf16[128,512]{1,0:T(8,128)(2,1)S(1)} %get-tuple-element.49), channel_id=1, source_target_pairs={{0,20},{4,16},{8,28},{12,24},{16,4},{20,0},{24,12},{28,8},{1,21},{... | collective-permute-start | bytes 393224 | tf_op jit(solution)/shard_map/ppermute | solution.py:370
  37.8 15.6 %collective-permute-start.12 = (bf16[512,512]{1,0:T(8,128)(2,1)S(1)}, bf16[512,512]{1,0:T(8,128)(2,1)S(1)}, u32[]{:S(2)}, u32[]{:S(2)}) collective-permute-start(bf16[512,512]{1,0:T(8,128)(2,1)S(1)} %constant_dynamic-update-slice_fusion.refs_6_.refs_0_), channel_id=1, source_target_pairs={{0,2},{1,3},{2,0},{3,1},{4,6},{5,7},{6,4},{7,5},{8,10},{9,11},{10,... | collective-permute-start | bytes 1572872 | tf_op jit(solution)/shard_map/ppermute | solution.py:364
  40.0 9.8 %collective-permute-start.8 = (bf16[128,512]{1,0:T(8,128)(2,1)S(1)}, bf16[128,512]{1,0:T(8,128)(2,1)S(1)}, u32[]{:S(2)}, u32[]{:S(2)}) collective-permute-start(bf16[128,512]{1,0:T(8,128)(2,1)S(1)} %get-tuple-element.50), channel_id=1, source_target_pairs={{0,24},{4,28},{8,16},{12,20},{16,8},{20,12},{24,0},{28,4},{1,25},{... | collective-permute-start | bytes 393224 | tf_op jit(solution)/shard_map/ppermute | solution.py:370
  44.1 9.3 %collective-permute-start.9 = (bf16[128,512]{1,0:T(8,128)(2,1)S(1)}, bf16[128,512]{1,0:T(8,128)(2,1)S(1)}, u32[]{:S(2)}, u32[]{:S(2)}) collective-permute-start(bf16[128,512]{1,0:T(8,128)(2,1)S(1)} %get-tuple-element.51), channel_id=1, source_target_pairs={{0,28},{4,24},{8,20},{12,16},{16,12},{20,8},{24,4},{28,0},{1,29},{... | collective-permute-start | bytes 393224 | tf_op jit(solution)/shard_map/ppermute | solution.py:370
  49.8 58.8 %collective-permute-start.21 = (bf16[512,2048]{1,0:T(8,128)(2,1)S(1)}, bf16[512,2048]{1,0:T(8,128)(2,1)S(1)}, u32[]{:S(2)}, u32[]{:S(2)}) collective-permute-start(bf16[512,2048]{1,0:T(8,128)(2,1)S(1)} %copy-done.1), channel_id=1, source_target_pairs={{0,1},{1,0},{2,3},{3,2},{4,5},{5,4},{6,7},{7,6},{8,9},{9,8},{10,11... | collective-permute-start | bytes 6291464 | tf_op jit(solution)/shard_map/ppermute | solution.py:364
  53.4 16.8 %collective-permute-start.11 = (bf16[512,512]{1,0:T(8,128)(2,1)S(1)}, bf16[512,512]{1,0:T(8,128)(2,1)S(1)}, u32[]{:S(2)}, u32[]{:S(2)}) collective-permute-start(bf16[512,512]{1,0:T(8,128)(2,1)S(1)} %constant_dynamic-update-slice_fusion.refs_6_.refs_0_), channel_id=1, source_target_pairs={{0,1},{1,0},{2,3},{3,2},{4,5},{5,4},{6,7},{7,6},{8,9},{9,8},{10,11... | collective-permute-start | bytes 1572872 | tf_op jit(solution)/shard_map/ppermute | solution.py:364
  53.4 16.9 %collective-permute-start.15 = (bf16[512,512]{1,0:T(8,128)(2,1)S(1)}, bf16[512,512]{1,0:T(8,128)(2,1)S(1)}, u32[]{:S(2)}, u32[]{:S(2)}) collective-permute-start(bf16[512,512]{1,0:T(8,128)(2,1)S(1)} %constant_dynamic-update-slice_fusion.4.refs_8_.refs_1_), channel_id=1, source_target_pairs={{0,2},{1,3},{2,0},{3,1},{4,6},{5,7},{6,4},{7,5},{8,10},{9,11},{10,... | collective-permute-start | bytes 1572872 | tf_op jit(solution)/shard_map/ppermute | solution.py:364
  55.0 15.8 %collective-permute-start.13 = (bf16[512,512]{1,0:T(8,128)(2,1)S(1)}, bf16[512,512]{1,0:T(8,128)(2,1)S(1)}, u32[]{:S(2)}, u32[]{:S(2)}) collective-permute-start(bf16[512,512]{1,0:T(8,128)(2,1)S(1)} %collective-permute-done.12.refs_2_), channel_id=1, source_target_pairs={{0,1},{1,0},{2,3},{3,2},{4,5},{5,4},{6,7},{7,6},{8,9},{9,8},{10,11... | collective-permute-start | bytes 1572872 | tf_op jit(solution)/shard_map/ppermute | solution.py:364
  60.6 16.9 %collective-permute-start.10 = (bf16[512,512]{1,0:T(8,128)(2,1)S(1)}, bf16[512,512]{1,0:T(8,128)(2,1)S(1)}, u32[]{:S(2)}, u32[]{:S(2)}) collective-permute-start(bf16[512,512]{1,0:T(8,128)(2,1)S(1)} %project_halo.1.refs_7_), channel_id=1, source_target_pairs={{0,4},{4,8},{8,12},{12,16},{16,20},{20,24},{24,28},{1,5},{5,9},{9,... | collective-permute-start | bytes 1572872 | tf_op jit(solution)/shard_map/ppermute | solution.py:399
  70.2 13.0 %collective-permute-start.14 = (bf16[512,512]{1,0:T(8,128)(2,1)S(1)}, bf16[512,512]{1,0:T(8,128)(2,1)S(1)}, u32[]{:S(2)}, u32[]{:S(2)}) collective-permute-start(bf16[512,512]{1,0:T(8,128)(2,1)S(1)} %constant_dynamic-update-slice_fusion.4.refs_8_.refs_1_), channel_id=1, source_target_pairs={{0,1},{1,0},{2,3},{3,2},{4,5},{5,4},{6,7},{7,6},{8,9},{9,8},{10,11... | collective-permute-start | bytes 1572872 | tf_op jit(solution)/shard_map/ppermute | solution.py:364
  70.3 12.9 %collective-permute-start.16 = (bf16[512,512]{1,0:T(8,128)(2,1)S(1)}, bf16[512,512]{1,0:T(8,128)(2,1)S(1)}, u32[]{:S(2)}, u32[]{:S(2)}) collective-permute-start(bf16[512,512]{1,0:T(8,128)(2,1)S(1)} %collective-permute-done.15.refs_3_), channel_id=1, source_target_pairs={{0,1},{1,0},{2,3},{3,2},{4,5},{5,4},{6,7},{7,6},{8,9},{9,8},{10,11... | collective-permute-start | bytes 1572872 | tf_op jit(solution)/shard_map/ppermute | solution.py:364
  93.4 6.5 %collective-permute-start.18 = (bf16[528,128]{1,0:T(8,128)(2,1)S(1)}, bf16[528,128]{1,0:T(8,128)(2,1)S(1)}, u32[]{:S(2)}, u32[]{:S(2)}) collective-permute-start(bf16[528,128]{1,0:T(8,128)(2,1)S(1)} %get-tuple-element.62), channel_id=1, source_target_pairs={{0,8},{4,12},{8,0},{12,4},{16,24},{20,28},{24,16},{28,20},{1,9},{5... | collective-permute-start | bytes 405512 | tf_op jit(solution)/shard_map/ppermute | solution.py:370
  103.2 18.3 %collective-permute-start.23 = (bf16[528,128]{1,0:T(8,128)(2,1)S(1)}, bf16[528,128]{1,0:T(8,128)(2,1)S(1)}, u32[]{:S(2)}, u32[]{:S(2)}) collective-permute-start(bf16[528,128]{1,0:T(8,128)(2,1)S(1)} %get-tuple-element.69), channel_id=1, source_target_pairs={{0,16},{4,20},{8,24},{12,28},{16,0},{20,4},{24,8},{28,12},{1,17},{... | collective-permute-start | bytes 405512 | tf_op jit(solution)/shard_map/ppermute | solution.py:370
  106.1 18.2 %collective-permute-start.24 = (bf16[528,128]{1,0:T(8,128)(2,1)S(1)}, bf16[528,128]{1,0:T(8,128)(2,1)S(1)}, u32[]{:S(2)}, u32[]{:S(2)}) collective-permute-start(bf16[528,128]{1,0:T(8,128)(2,1)S(1)} %get-tuple-element.70), channel_id=1, source_target_pairs={{0,20},{4,16},{8,28},{12,24},{16,4},{20,0},{24,12},{28,8},{1,21},{... | collective-permute-start | bytes 405512 | tf_op jit(solution)/shard_map/ppermute | solution.py:370
  106.7 20.9 %collective-permute-start.25 = (bf16[528,128]{1,0:T(8,128)(2,1)S(1)}, bf16[528,128]{1,0:T(8,128)(2,1)S(1)}, u32[]{:S(2)}, u32[]{:S(2)}) collective-permute-start(bf16[528,128]{1,0:T(8,128)(2,1)S(1)} %get-tuple-element.71), channel_id=1, source_target_pairs={{0,24},{4,28},{8,16},{12,20},{16,8},{20,12},{24,0},{28,4},{1,25},{... | collective-permute-start | bytes 405512 | tf_op jit(solution)/shard_map/ppermute | solution.py:370
  108.6 22.3 %collective-permute-start.26 = (bf16[528,128]{1,0:T(8,128)(2,1)S(1)}, bf16[528,128]{1,0:T(8,128)(2,1)S(1)}, u32[]{:S(2)}, u32[]{:S(2)}) collective-permute-start(bf16[528,128]{1,0:T(8,128)(2,1)S(1)} %get-tuple-element.72), channel_id=1, source_target_pairs={{0,28},{4,24},{8,20},{12,16},{16,12},{20,8},{24,4},{28,0},{1,29},{... | collective-permute-start | bytes 405512 | tf_op jit(solution)/shard_map/ppermute | solution.py:370
  111.2 22.7 %collective-permute-start.22 = (bf16[128,2048]{1,0:T(8,128)(2,1)S(1)}, bf16[128,2048]{1,0:T(8,128)(2,1)S(1)}, u32[]{:S(2)}, u32[]{:S(2)}) collective-permute-start(bf16[128,2048]{1,0:T(8,128)(2,1)S(1)} %get-tuple-element.68), channel_id=1, source_target_pairs={{0,2},{1,3},{2,0},{3,1},{4,6},{5,7},{6,4},{7,5},{8,10},{9,11},{10,... | collective-permute-start | bytes 1572872 | tf_op jit(solution)/shard_map/ppermute | solution.py:364
  135.8 14.0 %collective-permute-start.28 = (bf16[128,2048]{1,0:T(8,128)(2,1)S(1)}, bf16[128,2048]{1,0:T(8,128)(2,1)S(1)}, u32[]{:S(2)}, u32[]{:S(2)}) collective-permute-start(bf16[128,2048]{1,0:T(8,128)(2,1)S(1)} %get-tuple-element.76), channel_id=1, source_target_pairs={{0,2},{1,3},{2,0},{3,1},{4,6},{5,7},{6,4},{7,5},{8,10},{9,11},{10,... | collective-permute-start | bytes 1572872 | tf_op jit(solution)/shard_map/ppermute | solution.py:364
  (7 other events, 81.5 us)

commit v7 on v3

--- a/solution.py
+++ b/solution.py
@@ -45,6 +45,23 @@
     )(*args, *after)
 
 
+def fence(value, *after):
+    return pl.pallas_call(
+        lambda *refs: None,
+        in_specs=[ANYWHERE] * (1 + len(after)),
+        out_specs=ANYWHERE,
+        out_shape=jax.ShapeDtypeStruct(value.shape, value.dtype),
+        input_output_aliases={0: 0},
+        compiler_params=pltpu.CompilerParams(vmem_limit_bytes=MIB),
+        cost_estimate=pl.CostEstimate(flops=0, bytes_accessed=0, transcendentals=0),
+        name="fence",
+    )(value, *after)
+
+
+def in_hbm(value):
+    return pltpu.with_memory_space_constraint(value, pltpu.HBM)
+
+
 def shape(dims, dtype=BF16):
     return jax.ShapeDtypeStruct(tuple(dims), dtype)
 
@@ -61,30 +78,44 @@
     return lax.dot_general(a, b, (((0,), (0,)), ((), ())), preferred_element_type=F32)
 
 
-def pack_kernel(pos_ref, tok_ref, *out_refs):
-    owners = len(out_refs) // CHUNKS
-    per_owner = STRIDE // owners
-    groups = per_owner // SUB
-    per_chunk = groups // CHUNKS
-    for k in range(owners):
+def pack_kernel(pos_ref, tok_hbm, tok_ref, *rest):
+    out_refs, sems = rest[:-1], rest[-1]
+    spans = [slice(r * STRIDE, (r + 1) * STRIDE) for r in range(ROWS)]
+    copies = [
+        pltpu.make_async_copy(tok_hbm.at[at], tok_ref.at[at], sems.at[r])
+        for r, at in enumerate(spans)
+    ]
+    for c in copies:
+        c.start()
+    for c in copies:
+        c.wait()
+    per_owner = STRIDE // len(out_refs)
+    part = ROWS * SUB
+    for k, out_ref in enumerate(out_refs):
         d = pos_ref[0] ^ k
         rows = [
             tok_ref[pl.ds(pl.multiple_of(r * STRIDE + d * per_owner, per_owner), per_owner), :]
             for r in range(ROWS)
         ]
         rows = [x.astype(F32) for x in rows]
-        for g in range(groups):
+        for g in range(per_owner // SUB):
             piece = jnp.concatenate([x[g * SUB : (g + 1) * SUB] for x in rows], 0)
-            at = (g % per_chunk) * ROWS * SUB
-            out = out_refs[(g // per_chunk) * owners + k]
-            out[at : at + ROWS * SUB, :] = piece.astype(BF16)
+            out_ref[g * part : (g + 1) * part, :] = piece.astype(BF16)
 
 
 def pack(pos, tokens, owners):
-    message = tokens.shape[0] // owners // CHUNKS
-    shapes = [shape((message, tokens.shape[1]))] * (CHUNKS * owners)
-    outs = call(pack_kernel, "pack_tokens", 2, shapes, (pos, tokens))
-    return [outs[i * owners : (i + 1) * owners] for i in range(CHUNKS)]
+    message = shape((tokens.shape[0] // owners, tokens.shape[1]))
+    outs = pl.pallas_call(
+        pack_kernel,
+        in_specs=[IN_SMEM, ANYWHERE],
+        out_specs=[IN_VMEM] * (1 + owners),
+        out_shape=[shape(tokens.shape)] + [message] * owners,
+        scratch_shapes=[pltpu.SemaphoreType.DMA((ROWS,))],
+        compiler_params=pltpu.CompilerParams(vmem_limit_bytes=8 * MIB),
+        cost_estimate=pl.CostEstimate(flops=0, bytes_accessed=2 * MIB, transcendentals=0),
+        name="pack_tokens",
+    )(pos, in_hbm(tokens))
+    return outs[0], outs[1:]
 
 
 def stage_kernel(order_ref, wq, wk, wv, oq, ok, ov, sems):
@@ -312,10 +343,10 @@
         keep_ref[:, at] = jnp.where(low_side, total[:tokens], total[tokens:])
 
 
-def out_project(pos, own, other, w_own, w_other):
+def out_project(pos, own, other, w_own, w_other, after):
     dims = (own.shape[1], w_own.shape[1])
     shapes = [shape(dims), shape(dims, F32)]
-    return call(out_kernel, "out_project", 3, shapes, (pos, own, other, w_own, w_other))
+    return call(out_kernel, "out_project", 2, shapes, (pos, own, other, w_own, w_other), after)
 
 
 def join_kernel(*refs):
@@ -350,8 +381,8 @@
 
 
 def gather(own):
-    far = swap(own, 2)
-    return own, swap(own, 1), far, swap(far, 1)
+    across = swap(own, 2)
+    return own, swap(own, 1), across, swap(across, 1)
 
 
 def chunked(tokens, w_query, w_key, w_value, w_out):
@@ -362,9 +393,20 @@
     pos = jnp.stack([block, head % 2, head // 2]).astype(jnp.int32)
     rows, width = tokens.shape
 
-    pieces = gather(tokens)
-    classes = [exchange(m) for m in pack(pos, tokens, owners)]
-    weights = stage(order, (w_query, w_key, w_value), classes[0][1])
+    across = swap(tokens, 2)
+    block_tokens, sent = pack(pos, tokens, owners)
+    messages = exchange(sent)
+    part = rows // owners // CHUNKS
+    classes = [
+        jnp.concatenate([m[i * part : (i + 1) * part] for m in messages], 0) for i in range(CHUNKS)
+    ]
+    across = fence(across, classes[0])
+    pieces = (block_tokens, swap(fence(block_tokens, classes[0]), 1), across, swap(across, 1))
+    class_pieces = []
+    for c in classes:
+        c = fence(c, class_pieces[-1][2]) if class_pieces else c
+        class_pieces.append(gather(c))
+    weights = stage(order, (w_query, w_key, w_value), messages[1])
     w_other = swap(w_out, 1)
     own_halo = call(
         halo_kernel, "project_halo", 1.5, shape((2 * STRIDE, width)), (*pieces, *weights[1:])
@@ -373,23 +415,21 @@
     q, k, v = call(
         project_kernel,
         "project_block",
-        7,
+        6,
         [shape((rows, width))] * 3,
         (*pieces, *weights, own_halo),
     )
-    columns, after = [], (q, halo)
-    for i, messages in enumerate(classes):
-        class_pieces = gather(jnp.concatenate(messages, 0))
-        columns.append(column_part(pos, class_pieces, weights, owners, after))
-        if i == 0:
-            locals_ = local_part(pos, q, k, v, halo, owners, (columns[0][0],))
-            after = (locals_[-1][-1],)
-    pairs, after = [], (columns[-1][0],)
+    locals_ = local_part(pos, q, k, v, halo, owners, ())
+    columns, after = [], (locals_[0][0],)
+    for c in class_pieces:
+        columns.append(column_part(pos, c, weights, owners, after))
+        after = (columns[-1][0],)
+    pairs, after, gate = [], (columns[-1][0],), ()
     for column, (local, lse) in zip(columns, locals_):
         own, send = mix(pos, exchange(column), local, lse, after)
-        out, keep = out_project(pos, own, swap(send, 1), w_out, w_other)
-        after = (keep,)
+        out, keep = out_project(pos, own, swap(send, 1), w_out, w_other, gate)
         pairs.append((keep, swap(out, 2)))
+        after, gate = (keep,), (pairs[-1][1],)
     return join(pairs)
 
 

time: 146 us -> 140 us (0.959)
  starting transfers between devices: 67.4 us -> 54.6 us
  waiting for transfers between devices: 41.6 us -> 48.3 us
    ppermute x28 -> x21, starting transfers between devices: 57 us -> 43.7 us  [exchange(): lax.ppermute(messages[k], 'seq', [(i, i ^ k) for i in range(n)])]
    ppermute x28 -> x21, waiting for transfers between devices: 9.35 us -> 12.9 us  [exchange(): lax.ppermute(messages[k], 'seq', [(i, i ^ k) for i in range(n)])]
    ppermute x14, waiting for transfers between devices: 29.6 us -> 32.6 us  [swap(): return lax.ppermute(value, 'head', [(i, i ^ distance) for i in range(4)])]
    pallas_call x0 -> x4, Pallas kernels: none -> 1.84 us  [the longest x1 1.83 us: pack(): pl.pallas_call(pack_kernel, in_specs=[IN_SMEM, ANYWHERE], out_specs=[IN_V...]
    pallas_call x11 -> x10, Pallas kernels: 33.9 us -> 33.3 us  [call(): pl.pallas_call(run, in_specs=specs + [ANYWHERE] * extra, out_specs=jax.tr...]
  transfers between devices with their start and end apart: 43 -> 36, of which waited for: 11 -> 9; matrix products, arithmetic and copies ran while one was open for 0% -> 0% of each run, Pallas kernels for 22% -> 24%
where the time goes in v7:
time: 140 us
  starting transfers between devices  54.6 us (39%)
  waiting for transfers between devices  48.3 us (34%)
  Pallas kernels  36.2 us (26%)
    ppermute x21, starting transfers between devices, exchange(): lax.ppermute(messages[k], 'seq', [(i, i ^ k) for i in range(n)])  43.7 us
    pallas_call x10, Pallas kernels, call(): pl.pallas_call(run, in_specs=specs + [ANYWHERE] * extra, out_specs=jax.tr...  33.3 us
    ppermute x14, waiting for transfers between devices, swap(): return lax.ppermute(value, 'head', [(i, i ^ distance) for i in range(4)])  32.6 us
    ppermute x21, waiting for transfers between devices, exchange(): lax.ppermute(messages[k], 'seq', [(i, i ^ k) for i in range(n)])  12.9 us
    ppermute x14, starting transfers between devices, swap(): return lax.ppermute(value, 'head', [(i, i ^ distance) for i in range(4)])  8.34 us
    ppermute x1, waiting for transfers between devices, chunked(): lax.ppermute(own_halo, 'seq', [(i, i + 1) for i in range(owners - 1)])  2.85 us
  transfers between devices with their start and end apart: 36, of which 9 were waited for; matrix products, arithmetic and copies ran while one was open for 0% of the time, Pallas kernels for 24%

profile of v7, /device:TPU:0, one launch (start us, length us, event | category | flops | bytes accessed | tf_op | source)
XLA Modules:
  0.0 140.3 jit_solution(7810965537863596422)
XLA Ops:
  0.0 2.9 %collective-permute-start.8 = (bf16[1024,512]{1,0:T(8,128)(2,1)}, bf16[1024,512]{1,0:T(8,128)(2,1)S(1)}, u32[]{:S(2)}, u32[]{:S(2)}) collective-permute-start(bf16[1024,512]{1,0:T(8,128)(2,1)} %tok_hbm.1), channel_id=1, source_target_pairs={{0,2},{1,3},{2,0},{3,1},{4,6},{5,7},{6,4},{7,5},{8,10},{9,11},{10,... | collective-permute-start | bytes 3145736 | tf_op jit(solution)/shard_map/ppermute | solution.py:373
  8.4 2.6 %collective-permute-start.3 = (bf16[128,512]{1,0:T(8,128)(2,1)S(1)}, bf16[128,512]{1,0:T(8,128)(2,1)S(1)}, u32[]{:S(2)}, u32[]{:S(2)}) collective-permute-start(bf16[128,512]{1,0:T(8,128)(2,1)S(1)} %get-tuple-element.53), channel_id=1, source_target_pairs={{0,16},{4,20},{8,24},{12,28},{16,0},{20,4},{24,8},{28,12},{1,17},{... | collective-permute-start | bytes 393224 | tf_op jit(solution)/shard_map/ppermute | solution.py:379
  11.1 2.9 %collective-permute-start.4 = (bf16[128,512]{1,0:T(8,128)(2,1)S(1)}, bf16[128,512]{1,0:T(8,128)(2,1)S(1)}, u32[]{:S(2)}, u32[]{:S(2)}) collective-permute-start(bf16[128,512]{1,0:T(8,128)(2,1)S(1)} %get-tuple-element.54), channel_id=1, source_target_pairs={{0,20},{4,16},{8,28},{12,24},{16,4},{20,0},{24,12},{28,8},{1,21},{... | collective-permute-start | bytes 393224 | tf_op jit(solution)/shard_map/ppermute | solution.py:379
  14.0 2.2 %collective-permute-done.1 = bf16[128,512]{1,0:T(8,128)(2,1)S(1)} collective-permute-done((bf16[128,512]{1,0:T(8,128)(2,1)S(1)}, bf16[128,512]{1,0:T(8,128)(2,1)S(1)}, u32[]{:S(2)}, u32[]{:S(2)}) %collective-permute-start.1) | collective-permute-done | bytes 131104 | tf_op jit(solution)/shard_map/ppermute | solution.py:379
  16.2 2.4 %collective-permute-start.5 = (bf16[128,512]{1,0:T(8,128)(2,1)S(1)}, bf16[128,512]{1,0:T(8,128)(2,1)S(1)}, u32[]{:S(2)}, u32[]{:S(2)}) collective-permute-start(bf16[128,512]{1,0:T(8,128)(2,1)S(1)} %get-tuple-element.55), channel_id=1, source_target_pairs={{0,24},{4,28},{8,16},{12,20},{16,8},{20,12},{24,0},{28,4},{1,25},{... | collective-permute-start | bytes 393224 | tf_op jit(solution)/shard_map/ppermute | solution.py:379
  18.6 2.6 %collective-permute-start.6 = (bf16[128,512]{1,0:T(8,128)(2,1)S(1)}, bf16[128,512]{1,0:T(8,128)(2,1)S(1)}, u32[]{:S(2)}, u32[]{:S(2)}) collective-permute-start(bf16[128,512]{1,0:T(8,128)(2,1)S(1)} %get-tuple-element.56), channel_id=1, source_target_pairs={{0,28},{4,24},{8,20},{12,16},{16,12},{20,8},{24,4},{28,0},{1,29},{... | collective-permute-start | bytes 393224 | tf_op jit(solution)/shard_map/ppermute | solution.py:379
  21.3 9.3 %collective-permute-done.4 = bf16[128,512]{1,0:T(8,128)(2,1)S(1)} collective-permute-done((bf16[128,512]{1,0:T(8,128)(2,1)S(1)}, bf16[128,512]{1,0:T(8,128)(2,1)S(1)}, u32[]{:S(2)}, u32[]{:S(2)}) %collective-permute-start.4) | collective-permute-done | bytes 131104 | tf_op jit(solution)/shard_map/ppermute | solution.py:379
  34.0 11.2 %collective-permute-done.12.refs_3_.refs_1_ = bf16[512,512]{1,0:T(8,128)(2,1)S(1)} collective-permute-done((bf16[512,512]{1,0:T(8,128)(2,1)S(1)}, bf16[512,512]{1,0:T(8,128)(2,1)S(1)}, u32[]{:S(2)}, u32[]{:S(2)}) %collective-permute-start.12) | collective-permute-done | bytes 524320 | tf_op jit(solution)/shard_map/ppermute | solution.py:373
  47.0 2.5 %collective-permute-start.10 = (bf16[512,512]{1,0:T(8,128)(2,1)S(1)}, bf16[512,512]{1,0:T(8,128)(2,1)S(1)}, u32[]{:S(2)}, u32[]{:S(2)}) collective-permute-start(bf16[512,512]{1,0:T(8,128)(2,1)S(1)} %project_halo.1.refs_7_), channel_id=1, source_target_pairs={{0,4},{4,8},{8,12},{12,16},{16,20},{20,24},{24,28},{1,5},{5,9},{9,... | collective-permute-start | bytes 1572872 | tf_op jit(solution)/shard_map/ppermute | solution.py:414
  49.5 5.6 %project_block.1 = (bf16[1024,512]{1,0:T(8,128)(2,1)S(1)}, bf16[1024,512]{1,0:T(8,128)(2,1)S(1)}, bf16[1024,512]{1,0:T(8,128)(2,1)S(1)}) custom-call(bf16[1024,512]{1,0:T(8,128)(2,1)S(1)} %get-tuple-element.48.refs_0_, bf16[1024,512]{1,0:T(8,128)(2,1)S(1)} %collective-permute-done.7.refs_1_, bf16[1024,512]{1,0:T(8,128)(2,1)S(1)} %fence.4.refs_2_, ...), custom_call_target="tpu_custom_call" | custom-call | flops 6600000000 | bytes 1048576 | tf_op jit(solution)/shard_map/project_block/pallas_call | solution.py:34
  55.1 3.2 %collective-permute-done.22.refs_3_ = bf16[512,512]{1,0:T(8,128)(2,1)S(1)} collective-permute-done((bf16[512,512]{1,0:T(8,128)(2,1)S(1)}, bf16[512,512]{1,0:T(8,128)(2,1)S(1)}, u32[]{:S(2)}, u32[]{:S(2)}) %collective-permute-start.22) | collective-permute-done | bytes 524320 | tf_op jit(solution)/shard_map/ppermute | solution.py:373
  58.3 2.9 %collective-permute-done.10.refs_4_ = bf16[512,512]{1,0:T(8,128)(2,1)S(1)} collective-permute-done((bf16[512,512]{1,0:T(8,128)(2,1)S(1)}, bf16[512,512]{1,0:T(8,128)(2,1)S(1)}, u32[]{:S(2)}, u32[]{:S(2)}) %collective-permute-start.10) | collective-permute-done | bytes 524320 | tf_op jit(solution)/shard_map/ppermute | solution.py:414
  61.1 5.8 %local_part.1 = (f32[8,64,512]{2,1,0:T(8,128)S(1)}, f32[8,64,512]{2,1,0:T(8,128)S(1)}, f32[64,128]{1,0:T(8,128)S(1)}, f32[64,128]{1,0:T(8,128)S(1)}) custom-call(s32[3]{0:T(128)S(1)} %pad_add_fusion.pos_ref.refs_0_, bf16[1024,512]{1,0:T(8,128)(2,1)S(1)} %get-tuple-element.60.refs_1_, bf16[1024,512]{1,0:T(8,128)(2,1)S(1)} %get-tuple-element.61.refs_2_, ...), custom_call_target="tpu_custom_call" | custom-call | flops 5500000256 | bytes 1048576 | tf_op jit(solution)/shard_map/local_part/pallas_call | solution.py:34
  66.9 6.4 %column_part.2 = (bf16[272,128]{1,0:T(8,128)(2,1)S(1)}, bf16[272,128]{1,0:T(8,128)(2,1)S(1)}, bf16[272,128]{1,0:T(8,128)(2,1)S(1)}, bf16[272,128]{1,0:T(8,128)(2...) custom-call(s32[3]{0:T(128)S(1)} %pad_add_fusion.pos_ref.refs_0_, ...), custom_call_target="tpu_custom_call" | custom-call | flops 6600000000 | bytes 1048576 | tf_op jit(solution)/shard_map/column_part/pallas_call | solution.py:34
  73.3 6.0 %collective-permute-start.14 = (bf16[272,128]{1,0:T(8,128)(2,1)S(1)}, bf16[272,128]{1,0:T(8,128)(2,1)S(1)}, u32[]{:S(2)}, u32[]{:S(2)}) collective-permute-start(bf16[272,128]{1,0:T(8,128)(2,1)S(1)} %get-tuple-element.66), channel_id=1, source_target_pairs={{0,4},{4,0},{8,12},{12,8},{16,20},{20,16},{24,28},{28,24},{1,5},{5... | collective-permute-start | bytes 208904 | tf_op jit(solution)/shard_map/ppermute | solution.py:379
  79.3 2.0 %collective-permute-start.15 = (bf16[272,128]{1,0:T(8,128)(2,1)S(1)}, bf16[272,128]{1,0:T(8,128)(2,1)S(1)}, u32[]{:S(2)}, u32[]{:S(2)}) collective-permute-start(bf16[272,128]{1,0:T(8,128)(2,1)S(1)} %get-tuple-element.67), channel_id=1, source_target_pairs={{0,8},{4,12},{8,0},{12,4},{16,24},{20,28},{24,16},{28,20},{1,9},{5... | collective-permute-start | bytes 208904 | tf_op jit(solution)/shard_map/ppermute | solution.py:379
  82.7 3.3 %collective-permute-start.17 = (bf16[272,128]{1,0:T(8,128)(2,1)S(1)}, bf16[272,128]{1,0:T(8,128)(2,1)S(1)}, u32[]{:S(2)}, u32[]{:S(2)}) collective-permute-start(bf16[272,128]{1,0:T(8,128)(2,1)S(1)} %get-tuple-element.69), channel_id=1, source_target_pairs={{0,16},{4,20},{8,24},{12,28},{16,0},{20,4},{24,8},{28,12},{1,17},{... | collective-permute-start | bytes 208904 | tf_op jit(solution)/shard_map/ppermute | solution.py:379
  88.4 3.4 %collective-permute-start.20 = (bf16[272,128]{1,0:T(8,128)(2,1)S(1)}, bf16[272,128]{1,0:T(8,128)(2,1)S(1)}, u32[]{:S(2)}, u32[]{:S(2)}) collective-permute-start(bf16[272,128]{1,0:T(8,128)(2,1)S(1)} %get-tuple-element.72), channel_id=1, source_target_pairs={{0,28},{4,24},{8,20},{12,16},{16,12},{20,8},{24,4},{28,0},{1,29},{... | collective-permute-start | bytes 208904 | tf_op jit(solution)/shard_map/ppermute | solution.py:379
  91.8 6.6 %column_part.3 = (bf16[272,128]{1,0:T(8,128)(2,1)S(1)}, bf16[272,128]{1,0:T(8,128)(2,1)S(1)}, bf16[272,128]{1,0:T(8,128)(2,1)S(1)}, bf16[272,128]{1,0:T(8,128)(2...) custom-call(s32[3]{0:T(128)S(1)} %pad_add_fusion.pos_ref.refs_0_, ...), custom_call_target="tpu_custom_call" | custom-call | flops 6600000000 | bytes 1048576 | tf_op jit(solution)/shard_map/column_part/pallas_call | solution.py:34
  100.3 2.0 %collective-permute-start.28 = (bf16[272,128]{1,0:T(8,128)(2,1)S(1)}, bf16[272,128]{1,0:T(8,128)(2,1)S(1)}, u32[]{:S(2)}, u32[]{:S(2)}) collective-permute-start(bf16[272,128]{1,0:T(8,128)(2,1)S(1)} %get-tuple-element.81), channel_id=1, source_target_pairs={{0,8},{4,12},{8,0},{12,4},{16,24},{20,28},{24,16},{28,20},{1,9},{5... | collective-permute-start | bytes 208904 | tf_op jit(solution)/shard_map/ppermute | solution.py:379
  108.7 2.5 %collective-permute-start.33 = (bf16[272,128]{1,0:T(8,128)(2,1)S(1)}, bf16[272,128]{1,0:T(8,128)(2,1)S(1)}, u32[]{:S(2)}, u32[]{:S(2)}) collective-permute-start(bf16[272,128]{1,0:T(8,128)(2,1)S(1)} %get-tuple-element.86), channel_id=1, source_target_pairs={{0,28},{4,24},{8,20},{12,16},{16,12},{20,8},{24,4},{28,0},{1,29},{... | collective-permute-start | bytes 208904 | tf_op jit(solution)/shard_map/ppermute | solution.py:379
  111.2 1.8 %out_project.2 = (bf16[128,2048]{1,0:T(8,128)(2,1)S(1)}, f32[128,2048]{1,0:T(8,128)S(1)}) custom-call(s32[3]{0:T(128)S(1)} %pad_add_fusion.pos_ref.refs_0_, bf16[2,128,512]{2,1,0:T(8,128)(2,1)S(1)} %get-tuple-element.74.refs_1_, bf16[2,128,512]{2,1,0:T(8,128)(2,1)S(1)} %collective-permute-done.24.refs_2_, bf16[512,2048]{1,0:T(8,128)(2,1)S(1)} %copy-done.3, ...), custom_call_target="tpu_custom_call" | custom-call | flops 2200000000 | bytes 1048576 | tf_op jit(solution)/shard_map/out_project/pallas_call | solution.py:34
  119.1 6.6 %collective-permute-done.26.refs_5_.refs_1_ = bf16[128,2048]{1,0:T(8,128)(2,1)S(1)} collective-permute-done((bf16[128,2048]{1,0:T(8,128)(2,1)S(1)}, bf16[128,2048]{1,0:T(8,128)(2,1)S(1)}, u32[]{:S(2)}, u32[]{:S(2)}) %collective-permute-start.26) | collective-permute-done | bytes 524320 | tf_op jit(solution)/shard_map/ppermute | solution.py:373
  129.0 10.1 %collective-permute-done.35.refs_3_ = bf16[128,2048]{1,0:T(8,128)(2,1)S(1)} collective-permute-done((bf16[128,2048]{1,0:T(8,128)(2,1)S(1)}, bf16[128,2048]{1,0:T(8,128)(2,1)S(1)}, u32[]{:S(2)}, u32[]{:S(2)}) %collective-permute-start.35) | collective-permute-done | bytes 524320 | tf_op jit(solution)/shard_map/ppermute | solution.py:373
  (82 shorter events, 33.2 us)
Async XLA Ops:
  0.0 30.7 %collective-permute-start.8 = (bf16[1024,512]{1,0:T(8,128)(2,1)}, bf16[1024,512]{1,0:T(8,128)(2,1)S(1)}, u32[]{:S(2)}, u32[]{:S(2)}) collective-permute-start(bf16[1024,512]{1,0:T(8,128)(2,1)} %tok_hbm.1), channel_id=1, source_target_pairs={{0,2},{1,3},{2,0},{3,1},{4,6},{5,7},{6,4},{7,5},{8,10},{9,11},{10,... | collective-permute-start | bytes 3145736 | tf_op jit(solution)/shard_map/ppermute | solution.py:373
  8.4 12.8 %collective-permute-start.3 = (bf16[128,512]{1,0:T(8,128)(2,1)S(1)}, bf16[128,512]{1,0:T(8,128)(2,1)S(1)}, u32[]{:S(2)}, u32[]{:S(2)}) collective-permute-start(bf16[128,512]{1,0:T(8,128)(2,1)S(1)} %get-tuple-element.53), channel_id=1, source_target_pairs={{0,16},{4,20},{8,24},{12,28},{16,0},{20,4},{24,8},{28,12},{1,17},{... | collective-permute-start | bytes 393224 | tf_op jit(solution)/shard_map/ppermute | solution.py:379
  11.1 19.5 %collective-permute-start.4 = (bf16[128,512]{1,0:T(8,128)(2,1)S(1)}, bf16[128,512]{1,0:T(8,128)(2,1)S(1)}, u32[]{:S(2)}, u32[]{:S(2)}) collective-permute-start(bf16[128,512]{1,0:T(8,128)(2,1)S(1)} %get-tuple-element.54), channel_id=1, source_target_pairs={{0,20},{4,16},{8,28},{12,24},{16,4},{20,0},{24,12},{28,8},{1,21},{... | collective-permute-start | bytes 393224 | tf_op jit(solution)/shard_map/ppermute | solution.py:379
  16.2 14.4 %collective-permute-start.5 = (bf16[128,512]{1,0:T(8,128)(2,1)S(1)}, bf16[128,512]{1,0:T(8,128)(2,1)S(1)}, u32[]{:S(2)}, u32[]{:S(2)}) collective-permute-start(bf16[128,512]{1,0:T(8,128)(2,1)S(1)} %get-tuple-element.55), channel_id=1, source_target_pairs={{0,24},{4,28},{8,16},{12,20},{16,8},{20,12},{24,0},{28,4},{1,25},{... | collective-permute-start | bytes 393224 | tf_op jit(solution)/shard_map/ppermute | solution.py:379
  18.6 12.0 %collective-permute-start.6 = (bf16[128,512]{1,0:T(8,128)(2,1)S(1)}, bf16[128,512]{1,0:T(8,128)(2,1)S(1)}, u32[]{:S(2)}, u32[]{:S(2)}) collective-permute-start(bf16[128,512]{1,0:T(8,128)(2,1)S(1)} %get-tuple-element.56), channel_id=1, source_target_pairs={{0,28},{4,24},{8,20},{12,16},{16,12},{20,8},{24,4},{28,0},{1,29},{... | collective-permute-start | bytes 393224 | tf_op jit(solution)/shard_map/ppermute | solution.py:379
  30.7 15.0 %collective-permute-start.7 = (bf16[1024,512]{1,0:T(8,128)(2,1)S(1)}, bf16[1024,512]{1,0:T(8,128)(2,1)S(1)}, u32[]{:S(2)}, u32[]{:S(2)}) collective-permute-start(bf16[1024,512]{1,0:T(8,128)(2,1)S(1)} %fence.3), channel_id=1, source_target_pairs={{0,1},{1,0},{2,3},{3,2},{4,5},{5,4},{6,7},{7,6},{8,9},{9,8},{10,11... | collective-permute-start | bytes 3145736 | tf_op jit(solution)/shard_map/ppermute | solution.py:373
  30.8 15.0 %collective-permute-start.9 = (bf16[1024,512]{1,0:T(8,128)(2,1)S(1)}, bf16[1024,512]{1,0:T(8,128)(2,1)S(1)}, u32[]{:S(2)}, u32[]{:S(2)}) collective-permute-start(bf16[1024,512]{1,0:T(8,128)(2,1)S(1)} %fence.4.refs_2_), channel_id=1, source_target_pairs={{0,1},{1,0},{2,3},{3,2},{4,5},{5,4},{6,7},{7,6},{8,9},{9,8},{10,11... | collective-permute-start | bytes 3145736 | tf_op jit(solution)/shard_map/ppermute | solution.py:373
  31.2 13.9 %collective-permute-start.12 = (bf16[512,512]{1,0:T(8,128)(2,1)S(1)}, bf16[512,512]{1,0:T(8,128)(2,1)S(1)}, u32[]{:S(2)}, u32[]{:S(2)}) collective-permute-start(bf16[512,512]{1,0:T(8,128)(2,1)S(1)} %get-tuple-element.92.refs_1_), channel_id=1, source_target_pairs={{0,2},{1,3},{2,0},{3,1},{4,6},{5,7},{6,4},{7,5},{8,10},{9,11},{10,... | collective-permute-start | bytes 1572872 | tf_op jit(solution)/shard_map/ppermute | solution.py:373
  31.8 71.8 %collective-permute-start.25 = (bf16[512,2048]{1,0:T(8,128)(2,1)S(1)}, bf16[512,2048]{1,0:T(8,128)(2,1)S(1)}, u32[]{:S(2)}, u32[]{:S(2)}) collective-permute-start(bf16[512,2048]{1,0:T(8,128)(2,1)S(1)} %copy-done.3), channel_id=1, source_target_pairs={{0,1},{1,0},{2,3},{3,2},{4,5},{5,4},{6,7},{7,6},{8,9},{9,8},{10,11... | collective-permute-start | bytes 6291464 | tf_op jit(solution)/shard_map/ppermute | solution.py:373
  31.8 35.1 %collective-permute-start.11 = (bf16[512,512]{1,0:T(8,128)(2,1)S(1)}, bf16[512,512]{1,0:T(8,128)(2,1)S(1)}, u32[]{:S(2)}, u32[]{:S(2)}) collective-permute-start(bf16[512,512]{1,0:T(8,128)(2,1)S(1)} %get-tuple-element.92.refs_1_), channel_id=1, source_target_pairs={{0,1},{1,0},{2,3},{3,2},{4,5},{5,4},{6,7},{7,6},{8,9},{9,8},{10,11... | collective-permute-start | bytes 1572872 | tf_op jit(solution)/shard_map/ppermute | solution.py:373
  45.2 13.1 %collective-permute-start.22 = (bf16[512,512]{1,0:T(8,128)(2,1)S(1)}, bf16[512,512]{1,0:T(8,128)(2,1)S(1)}, u32[]{:S(2)}, u32[]{:S(2)}) collective-permute-start(bf16[512,512]{1,0:T(8,128)(2,1)S(1)} %fence.5.refs_1_), channel_id=1, source_target_pairs={{0,2},{1,3},{2,0},{3,1},{4,6},{5,7},{6,4},{7,5},{8,10},{9,11},{10,... | collective-permute-start | bytes 1572872 | tf_op jit(solution)/shard_map/ppermute | solution.py:373
  45.7 21.2 %collective-permute-start.13 = (bf16[512,512]{1,0:T(8,128)(2,1)S(1)}, bf16[512,512]{1,0:T(8,128)(2,1)S(1)}, u32[]{:S(2)}, u32[]{:S(2)}) collective-permute-start(bf16[512,512]{1,0:T(8,128)(2,1)S(1)} %collective-permute-done.12.refs_3_.refs_1_), channel_id=1, source_target_pairs={{0,1},{1,0},{2,3},{3,2},{4,5},{5,4},{6,7},{7,6},{8,9},{9,8},{10,11... | collective-permute-start | bytes 1572872 | tf_op jit(solution)/shard_map/ppermute | solution.py:373
  47.0 14.1 %collective-permute-start.10 = (bf16[512,512]{1,0:T(8,128)(2,1)S(1)}, bf16[512,512]{1,0:T(8,128)(2,1)S(1)}, u32[]{:S(2)}, u32[]{:S(2)}) collective-permute-start(bf16[512,512]{1,0:T(8,128)(2,1)S(1)} %project_halo.1.refs_7_), channel_id=1, source_target_pairs={{0,4},{4,8},{8,12},{12,16},{16,20},{20,24},{24,28},{1,5},{5,9},{9,... | collective-permute-start | bytes 1572872 | tf_op jit(solution)/shard_map/ppermute | solution.py:414
  58.3 23.1 %collective-permute-start.21 = (bf16[512,512]{1,0:T(8,128)(2,1)S(1)}, bf16[512,512]{1,0:T(8,128)(2,1)S(1)}, u32[]{:S(2)}, u32[]{:S(2)}) collective-permute-start(bf16[512,512]{1,0:T(8,128)(2,1)S(1)} %fence.5.refs_1_), channel_id=1, source_target_pairs={{0,1},{1,0},{2,3},{3,2},{4,5},{5,4},{6,7},{7,6},{8,9},{9,8},{10,11... | collective-permute-start | bytes 1572872 | tf_op jit(solution)/shard_map/ppermute | solution.py:373
  61.1 21.6 %collective-permute-start.23 = (bf16[512,512]{1,0:T(8,128)(2,1)S(1)}, bf16[512,512]{1,0:T(8,128)(2,1)S(1)}, u32[]{:S(2)}, u32[]{:S(2)}) collective-permute-start(bf16[512,512]{1,0:T(8,128)(2,1)S(1)} %collective-permute-done.22.refs_3_), channel_id=1, source_target_pairs={{0,1},{1,0},{2,3},{3,2},{4,5},{5,4},{6,7},{7,6},{8,9},{9,8},{10,11... | collective-permute-start | bytes 1572872 | tf_op jit(solution)/shard_map/ppermute | solution.py:373
  73.3 12.7 %collective-permute-start.14 = (bf16[272,128]{1,0:T(8,128)(2,1)S(1)}, bf16[272,128]{1,0:T(8,128)(2,1)S(1)}, u32[]{:S(2)}, u32[]{:S(2)}) collective-permute-start(bf16[272,128]{1,0:T(8,128)(2,1)S(1)} %get-tuple-element.66), channel_id=1, source_target_pairs={{0,4},{4,0},{8,12},{12,8},{16,20},{20,16},{24,28},{28,24},{1,5},{5... | collective-permute-start | bytes 208904 | tf_op jit(solution)/shard_map/ppermute | solution.py:379
  82.7 15.7 %collective-permute-start.17 = (bf16[272,128]{1,0:T(8,128)(2,1)S(1)}, bf16[272,128]{1,0:T(8,128)(2,1)S(1)}, u32[]{:S(2)}, u32[]{:S(2)}) collective-permute-start(bf16[272,128]{1,0:T(8,128)(2,1)S(1)} %get-tuple-element.69), channel_id=1, source_target_pairs={{0,16},{4,20},{8,24},{12,28},{16,0},{20,4},{24,8},{28,12},{1,17},{... | collective-permute-start | bytes 208904 | tf_op jit(solution)/shard_map/ppermute | solution.py:379
  86.0 12.4 %collective-permute-start.18 = (bf16[272,128]{1,0:T(8,128)(2,1)S(1)}, bf16[272,128]{1,0:T(8,128)(2,1)S(1)}, u32[]{:S(2)}, u32[]{:S(2)}) collective-permute-start(bf16[272,128]{1,0:T(8,128)(2,1)S(1)} %get-tuple-element.70), channel_id=1, source_target_pairs={{0,20},{4,16},{8,28},{12,24},{16,4},{20,0},{24,12},{28,8},{1,21},{... | collective-permute-start | bytes 208904 | tf_op jit(solution)/shard_map/ppermute | solution.py:379
  86.8 11.6 %collective-permute-start.19 = (bf16[272,128]{1,0:T(8,128)(2,1)S(1)}, bf16[272,128]{1,0:T(8,128)(2,1)S(1)}, u32[]{:S(2)}, u32[]{:S(2)}) collective-permute-start(bf16[272,128]{1,0:T(8,128)(2,1)S(1)} %get-tuple-element.71), channel_id=1, source_target_pairs={{0,24},{4,28},{8,16},{12,20},{16,8},{20,12},{24,0},{28,4},{1,25},{... | collective-permute-start | bytes 208904 | tf_op jit(solution)/shard_map/ppermute | solution.py:379
  102.3 10.7 %collective-permute-start.29 = (bf16[272,128]{1,0:T(8,128)(2,1)S(1)}, bf16[272,128]{1,0:T(8,128)(2,1)S(1)}, u32[]{:S(2)}, u32[]{:S(2)}) collective-permute-start(bf16[272,128]{1,0:T(8,128)(2,1)S(1)} %get-tuple-element.82), channel_id=1, source_target_pairs={{0,12},{4,8},{8,4},{12,0},{16,28},{20,24},{24,20},{28,16},{1,13},{... | collective-permute-start | bytes 208904 | tf_op jit(solution)/shard_map/ppermute | solution.py:379
  103.5 11.1 %collective-permute-start.30 = (bf16[272,128]{1,0:T(8,128)(2,1)S(1)}, bf16[272,128]{1,0:T(8,128)(2,1)S(1)}, u32[]{:S(2)}, u32[]{:S(2)}) collective-permute-start(bf16[272,128]{1,0:T(8,128)(2,1)S(1)} %get-tuple-element.83), channel_id=1, source_target_pairs={{0,16},{4,20},{8,24},{12,28},{16,0},{20,4},{24,8},{28,12},{1,17},{... | collective-permute-start | bytes 208904 | tf_op jit(solution)/shard_map/ppermute | solution.py:379
  105.3 10.7 %collective-permute-start.31 = (bf16[272,128]{1,0:T(8,128)(2,1)S(1)}, bf16[272,128]{1,0:T(8,128)(2,1)S(1)}, u32[]{:S(2)}, u32[]{:S(2)}) collective-permute-start(bf16[272,128]{1,0:T(8,128)(2,1)S(1)} %get-tuple-element.84), channel_id=1, source_target_pairs={{0,20},{4,16},{8,28},{12,24},{16,4},{20,0},{24,12},{28,8},{1,21},{... | collective-permute-start | bytes 208904 | tf_op jit(solution)/shard_map/ppermute | solution.py:379
  113.1 12.6 %collective-permute-start.26 = (bf16[128,2048]{1,0:T(8,128)(2,1)S(1)}, bf16[128,2048]{1,0:T(8,128)(2,1)S(1)}, u32[]{:S(2)}, u32[]{:S(2)}) collective-permute-start(bf16[128,2048]{1,0:T(8,128)(2,1)S(1)} %get-tuple-element.77), channel_id=1, source_target_pairs={{0,2},{1,3},{2,0},{3,1},{4,6},{5,7},{6,4},{7,5},{8,10},{9,11},{10,... | collective-permute-start | bytes 1572872 | tf_op jit(solution)/shard_map/ppermute | solution.py:373
  127.5 11.7 %collective-permute-start.35 = (bf16[128,2048]{1,0:T(8,128)(2,1)S(1)}, bf16[128,2048]{1,0:T(8,128)(2,1)S(1)}, u32[]{:S(2)}, u32[]{:S(2)}) collective-permute-start(bf16[128,2048]{1,0:T(8,128)(2,1)S(1)} %get-tuple-element.90), channel_id=1, source_target_pairs={{0,2},{1,3},{2,0},{3,1},{4,6},{5,7},{6,4},{7,5},{8,10},{9,11},{10,... | collective-permute-start | bytes 1572872 | tf_op jit(solution)/shard_map/ppermute | solution.py:373
  (16 other events, 125.6 us)

commit v8 on v7

--- a/solution.py
+++ b/solution.py
@@ -1,3 +1,5 @@
+import functools
+
 import jax
 import jax.numpy as jnp
 from jax import lax
@@ -11,6 +13,8 @@
 ROWS = 4
 SUB = 8
 CHUNKS = 2
+ORDER = (0, 4, 5, 6, 7, 1, 2, 3)
+HALVES = ((0, 4, 5, 1), (6, 7, 2, 3))
 SCALE2 = DH ** (-0.5) * 1.4426950408889634
 FLOOR = -1e29
 MIB = 1024 * 1024
@@ -91,7 +95,7 @@
         c.wait()
     per_owner = STRIDE // len(out_refs)
     part = ROWS * SUB
-    for k, out_ref in enumerate(out_refs):
+    for k, out_ref in zip(ORDER, out_refs):
         d = pos_ref[0] ^ k
         rows = [
             tok_ref[pl.ds(pl.multiple_of(r * STRIDE + d * per_owner, per_owner), per_owner), :]
@@ -236,8 +240,13 @@
 
 
 def column_kernel(pos_ref, x0, x1, x2, x3, wq, wk, wv, *rest):
-    out_refs, scratch = rest[:-3], rest[-3:]
+    refs, scratch = rest[:-3], rest[-3:]
     owners, message, _ = scratch[0].shape
+    out_refs = refs[-owners:]
+    size = HEADS * message + 16
+    base = out_refs[0].shape[0] - size
+    for old, new in zip(refs[:-owners], out_refs):
+        new[:base, :] = old[...]
     groups = message // (ROWS * SUB)
     everything = slice(0, owners * message)
     for w, a in zip((wq, wk, wv), scratch):
@@ -247,7 +256,9 @@
 
     def row_and_class(dim):
         i = lax.broadcasted_iota(jnp.int32, (size, size), dim)
-        return ((i // part) ^ pos_ref[0]) * ROWS + (i % part) // SUB, i % SUB
+        slot = i // part
+        far = jnp.where(slot < 5, slot + 3, slot - 4)
+        return (jnp.where(slot == 0, 0, far) ^ pos_ref[0]) * ROWS + (i % part) // SUB, i % SUB
 
     (row_j, class_j), (row_i, class_i) = row_and_class(0), row_and_class(1)
     earlier = jnp.logical_and(class_i == class_j, row_i > row_j)
@@ -260,7 +271,8 @@
             q, k, v = (a[:, at, cols].reshape(size, DH) for a in scratch)
             p, total, lse = softmax_columns(jnp.where(earlier, dot_t(k, q), -1e30))
             o = (dot_l(v, p.astype(BF16)) * (1.0 / total)).T.astype(BF16)
-            rows = slice(h * message + g * part, h * message + (g + 1) * part)
+            to = base + h * message + g * part
+            rows = slice(to, to + part)
             for n in range(owners):
                 out_refs[n][rows, :] = o[n * part : (n + 1) * part]
             lses.append(lse)
@@ -273,61 +285,67 @@
         mid = (x - hi).astype(BF16).astype(F32)
         lo = x - hi - mid
         tail = jnp.concatenate([jnp.where(upper, hi, lo), jnp.where(upper, mid, 0.0)], 0)
-        out_refs[n][HEADS * message : HEADS * message + 16, :] = tail.astype(BF16)
-
-
-def column_part(pos, pieces, weights, owners, after):
+        to = base + HEADS * message
+        out_refs[n][to : to + 16, :] = tail.astype(BF16)
+
+
+def column_part(pos, pieces, weights, earlier, owners, after):
     tokens, width = pieces[0].shape
     message = tokens // owners
-    shapes = [shape((HEADS * message + 16, DH))] * owners
+    rows = HEADS * message + 16 + (earlier[0].shape[0] if earlier else 0)
     scratch = [pltpu.VMEM((owners, message, width), BF16)] * 3
-    return call(column_kernel, "column_part", 6, shapes, (pos, *pieces, *weights), after, scratch)
-
-
-def mix_kernel(pos_ref, loc_ref, lse_ref, *rest):
-    col_refs, (own_ref, send_ref, mixed) = rest[:-3], rest[-3:]
-    owners, message, _ = loc_ref.shape
+    args = (pos, *pieces, *weights, *earlier)
+    return call(column_kernel, "column_part", 6, [shape((rows, DH))] * owners, args, after, scratch)
+
+
+def mix_kernel(half, pos_ref, *refs):
+    local_refs, refs = refs[: 2 * CHUNKS], refs[2 * CHUNKS :]
+    col_refs, (own_ref, send_ref, mixed) = refs[:-3], refs[-3:]
+    message = local_refs[0].shape[1]
     groups = message // (ROWS * SUB)
-    base = HEADS * message
-    tiles = []
-    for col_ref in col_refs:
-        tail = col_ref[base : base + 16, :].astype(F32)
-        tiles.append(tail[:8] + tail[8:])
-    tiles.append(jnp.zeros((128 - 8 * owners, 128), F32))
-    turned = jnp.concatenate(tiles, 0).T[:message]
-    col_lse = turned + pltpu.roll(turned, 124, 1)
-    loc_lse = lse_ref[...]
-    top = jnp.maximum(col_lse, loc_lse)
-    w_col = jnp.exp2(col_lse - top)
-    w_loc = jnp.exp2(loc_lse - top)
-    share = 1.0 / (w_col + w_loc)
-    w_col = w_col * share
-    w_loc = w_loc * share
+    size = HEADS * message + 16
     span = groups * SUB
-    for k, col_ref in enumerate(col_refs):
-        d = pos_ref[0] ^ k
-        spot = pl.ds(pl.multiple_of(d * span, span), span)
-        for h in range(HEADS):
-            cols = slice(h * DH, (h + 1) * DH)
-            at = slice(8 * k + h, 8 * k + h + 1)
-            col = col_ref[h * message : (h + 1) * message, :].astype(F32)
-            both = loc_ref[d, :, cols] * w_loc[:, at] + col * w_col[:, at]
-            for r in range(ROWS):
-                starts = [(g * ROWS + r) * SUB for g in range(groups)]
-                piece = jnp.concatenate([both[s : s + SUB] for s in starts], 0)
-                mixed[r, spot, cols] = piece.astype(BF16)
+    for i in range(CHUNKS):
+        loc_ref, lse_ref = local_refs[2 * i : 2 * i + 2]
+        tiles = [jnp.zeros((8, 128), F32)] * 16
+        base = i * size
+        for k, col_ref in zip(half, col_refs):
+            tail = col_ref[base + HEADS * message : base + size, :].astype(F32)
+            tiles[k] = tail[:8] + tail[8:]
+        turned = jnp.concatenate(tiles, 0).T[:message]
+        col_lse = turned + pltpu.roll(turned, 124, 1)
+        loc_lse = lse_ref[...]
+        top = jnp.maximum(col_lse, loc_lse)
+        w_col = jnp.exp2(col_lse - top)
+        w_loc = jnp.exp2(loc_lse - top)
+        share = 1.0 / (w_col + w_loc)
+        w_col = w_col * share
+        w_loc = w_loc * share
+        for n, (k, col_ref) in enumerate(zip(half, col_refs)):
+            d = pos_ref[0] ^ k
+            to = (n * CHUNKS + i) * span
+            for h in range(HEADS):
+                cols = slice(h * DH, (h + 1) * DH)
+                at = slice(8 * k + h, 8 * k + h + 1)
+                col = col_ref[base + h * message : base + (h + 1) * message, :].astype(F32)
+                both = loc_ref[d, :, cols] * w_loc[:, at] + col * w_col[:, at]
+                for r in range(ROWS):
+                    starts = [(g * ROWS + r) * SUB for g in range(groups)]
+                    piece = jnp.concatenate([both[s : s + SUB] for s in starts], 0)
+                    mixed[r, to : to + span, cols] = piece.astype(BF16)
     core = pos_ref[1]
     for x in range(2):
         own_ref[x] = mixed[2 * x + core]
         send_ref[x] = mixed[2 * x + 1 - core]
 
 
-def mix(pos, columns, local, lse, after):
-    owners, message, width = local.shape
-    tokens = owners * message // ROWS
+def mix(pos, half, columns, locals_, after):
+    owners, message, width = locals_[0][0].shape
+    tokens = len(half) * CHUNKS * message // ROWS
     shapes = [shape((2, tokens, width))] * 2
     scratch = [pltpu.VMEM((ROWS, tokens, width), BF16)]
-    return call(mix_kernel, "mix", 3, shapes, (pos, local, lse, *columns), after, scratch)
+    args = (pos, *[x for pair in locals_ for x in pair], *columns)
+    return call(functools.partial(mix_kernel, half), "mix", 2, shapes, args, after, scratch)
 
 
 def out_kernel(pos_ref, a_ref, b_ref, wa_ref, wb_ref, send_ref, keep_ref):
@@ -349,24 +367,20 @@
     return call(out_kernel, "out_project", 2, shapes, (pos, own, other, w_own, w_other), after)
 
 
-def join_kernel(*refs):
+def join_kernel(pos_ref, *refs):
     out_ref = refs[-1]
-    chunks = (len(refs) - 1) // 2
-    tokens = refs[0].shape[0]
-    span = 32 // chunks
-    for i in range(chunks):
-        keep, got = refs[2 * i], refs[2 * i + 1]
-        for d in range(tokens // span):
-            rows = slice(d * span, (d + 1) * span)
-            at = (d * chunks + i) * span
-            total = keep[rows, :] + got[rows, :].astype(F32)
-            out_ref[at : at + span, :] = total.astype(BF16)
-
-
-def join(pairs):
+    for half, keep, got in zip(HALVES, refs[0:-1:2], refs[1:-1:2]):
+        span = keep.shape[0] // len(half)
+        for n, k in enumerate(half):
+            rows = slice(n * span, (n + 1) * span)
+            to = pl.ds(pl.multiple_of((pos_ref[0] ^ k) * span, span), span)
+            out_ref[to, :] = (keep[rows, :] + got[rows, :].astype(F32)).astype(BF16)
+
+
+def join(pos, pairs):
     columns = pairs[0][0].shape[1]
     args = [x for pair in pairs for x in pair]
-    return call(join_kernel, "join", 2, shape((STRIDE, columns)), args)
+    return call(join_kernel, "join", 2, shape((STRIDE, columns)), (pos, *args))
 
 
 def swap(value, distance):
@@ -374,10 +388,12 @@
 
 
 def exchange(messages):
-    n = len(messages)
-    return [messages[0]] + [
-        lax.ppermute(messages[k], "seq", [(i, i ^ k) for i in range(n)]) for k in range(1, n)
-    ]
+    peers = lax.axis_size("seq")
+
+    def move(value, k):
+        return lax.ppermute(value, "seq", [(i, i ^ k) for i in range(peers)]) if k else value
+
+    return [move(m, k) for m, k in zip(messages, ORDER)]
 
 
 def gather(own):
@@ -402,10 +418,7 @@
     ]
     across = fence(across, classes[0])
     pieces = (block_tokens, swap(fence(block_tokens, classes[0]), 1), across, swap(across, 1))
-    class_pieces = []
-    for c in classes:
-        c = fence(c, class_pieces[-1][2]) if class_pieces else c
-        class_pieces.append(gather(c))
+    first_pieces = gather(classes[0])
     weights = stage(order, (w_query, w_key, w_value), messages[1])
     w_other = swap(w_out, 1)
     own_halo = call(
@@ -419,18 +432,20 @@
         [shape((rows, width))] * 3,
         (*pieces, *weights, own_halo),
     )
+    class_pieces = (first_pieces, gather(fence(classes[1], first_pieces[2], q)))
     locals_ = local_part(pos, q, k, v, halo, owners, ())
     columns, after = [], (locals_[0][0],)
     for c in class_pieces:
-        columns.append(column_part(pos, c, weights, owners, after))
-        after = (columns[-1][0],)
-    pairs, after, gate = [], (columns[-1][0],), ()
-    for column, (local, lse) in zip(columns, locals_):
-        own, send = mix(pos, exchange(column), local, lse, after)
+        columns = column_part(pos, c, weights, columns, owners, after)
+        after = ()
+    columns = dict(zip(ORDER, exchange(columns)))
+    pairs, after, gate = [], (), ()
+    for half in HALVES:
+        own, send = mix(pos, half, [columns[n] for n in half], locals_, after)
         out, keep = out_project(pos, own, swap(send, 1), w_out, w_other, gate)
         pairs.append((keep, swap(out, 2)))
         after, gate = (keep,), (pairs[-1][1],)
-    return join(pairs)
+    return join(pos, pairs)
 
 
 def from_behind(value, axis, by):
@@ -576,7 +591,7 @@
 def shards(tokens, w_query, w_key, w_value, w_out):
     rows, width = w_query.shape
     fits = (
-        lax.axis_size("seq") == STRIDE // 32
+        lax.axis_size("seq") == len(ORDER)
         and lax.axis_size("head") == 4
         and tokens.shape == (ROWS * STRIDE, HEADS * DH)
         and (rows, width) == (4 * HEADS * DH, HEADS * DH)

time: 140 us -> 138 us (0.986)
  starting transfers between devices: 54.6 us -> 33.1 us
  waiting for transfers between devices: 48.3 us -> 65.8 us
    ppermute x21 -> x14, waiting for transfers between devices: 12.9 us -> 37 us  [move(): lax.ppermute(value, 'seq', [(i, i ^ k) for i in range(peers)])]
    ppermute x21 -> x14, starting transfers between devices: 43.7 us -> 24.1 us  [move(): lax.ppermute(value, 'seq', [(i, i ^ k) for i in range(peers)])]
    ppermute x14, waiting for transfers between devices: 32.6 us -> 25.1 us  [swap(): return lax.ppermute(value, 'head', [(i, i ^ distance) for i in range(4)])]
    ppermute x14, starting transfers between devices: 8.34 us -> 6.43 us  [swap(): return lax.ppermute(value, 'head', [(i, i ^ distance) for i in range(4)])]
  transfers between devices with their start and end apart: 36 -> 29, of which waited for: 9 -> 16; matrix products, arithmetic and copies ran while one was open for 0% -> 0% of each run, Pallas kernels for 24% -> 24%
where the time goes in v8:
time: 138 us
  waiting for transfers between devices  65.8 us (48%)
  Pallas kernels  37.2 us (27%)
  starting transfers between devices  33.1 us (24%)
    ppermute x14, waiting for transfers between devices, move(): lax.ppermute(value, 'seq', [(i, i ^ k) for i in range(peers)])  37 us
    pallas_call x10, Pallas kernels, call(): pl.pallas_call(run, in_specs=specs + [ANYWHERE] * extra, out_specs=jax.tr...  34.2 us
    ppermute x14, waiting for transfers between devices, swap(): return lax.ppermute(value, 'head', [(i, i ^ distance) for i in range(4)])  25.1 us
    ppermute x14, starting transfers between devices, move(): lax.ppermute(value, 'seq', [(i, i ^ k) for i in range(peers)])  24.1 us
    ppermute x14, starting transfers between devices, swap(): return lax.ppermute(value, 'head', [(i, i ^ distance) for i in range(4)])  6.43 us
    ppermute x1, waiting for transfers between devices, chunked(): lax.ppermute(own_halo, 'seq', [(i, i + 1) for i in range(owners - 1)])  3.8 us
  transfers between devices with their start and end apart: 29, of which 16 were waited for; matrix products, arithmetic and copies ran while one was open for 0% of the time, Pallas kernels for 24%

profile of v8, /device:TPU:0, one launch (start us, length us, event | category | flops | bytes accessed | tf_op | source)
XLA Modules:
  0.0 137.7 jit_solution(13000457249710427860)
XLA Ops:
  0.0 2.9 %collective-permute-start.8 = (bf16[1024,512]{1,0:T(8,128)(2,1)}, bf16[1024,512]{1,0:T(8,128)(2,1)S(1)}, u32[]{:S(2)}, u32[]{:S(2)}) collective-permute-start(bf16[1024,512]{1,0:T(8,128)(2,1)} %tok_hbm.1), channel_id=1, source_target_pairs={{0,2},{1,3},{2,0},{3,1},{4,6},{5,7},{6,4},{7,5},{8,10},{9,11},{10,... | collective-permute-start | bytes 3145736 | tf_op jit(solution)/shard_map/ppermute | solution.py:387
  4.9 2.7 %collective-permute-start = (bf16[128,512]{1,0:T(8,128)(2,1)S(1)}, bf16[128,512]{1,0:T(8,128)(2,1)S(1)}, u32[]{:S(2)}, u32[]{:S(2)}) collective-permute-start(bf16[128,512]{1,0:T(8,128)(2,1)S(1)} %get-tuple-element.50), channel_id=1, source_target_pairs={{0,16},{4,20},{8,24},{12,28},{16,0},{20,4},{24,8},{28,12},{1,17},{... | collective-permute-start | bytes 393224 | tf_op jit(solution)/shard_map/ppermute | solution.py:394
  8.8 3.6 %collective-permute-start.2 = (bf16[128,512]{1,0:T(8,128)(2,1)S(1)}, bf16[128,512]{1,0:T(8,128)(2,1)S(1)}, u32[]{:S(2)}, u32[]{:S(2)}) collective-permute-start(bf16[128,512]{1,0:T(8,128)(2,1)S(1)} %get-tuple-element.52), channel_id=1, source_target_pairs={{0,24},{4,28},{8,16},{12,20},{16,8},{20,12},{24,0},{28,4},{1,25},{... | collective-permute-start | bytes 393224 | tf_op jit(solution)/shard_map/ppermute | solution.py:394
  12.7 10.5 %collective-permute-done._ = bf16[128,512]{1,0:T(8,128)(2,1)S(1)} collective-permute-done((bf16[128,512]{1,0:T(8,128)(2,1)S(1)}, bf16[128,512]{1,0:T(8,128)(2,1)S(1)}, u32[]{:S(2)}, u32[]{:S(2)}) %collective-permute-start) | collective-permute-done | bytes 131104 | tf_op jit(solution)/shard_map/ppermute | solution.py:394
  24.7 2.2 %collective-permute-done.1 = bf16[128,512]{1,0:T(8,128)(2,1)S(1)} collective-permute-done((bf16[128,512]{1,0:T(8,128)(2,1)S(1)}, bf16[128,512]{1,0:T(8,128)(2,1)S(1)}, u32[]{:S(2)}, u32[]{:S(2)}) %collective-permute-start.1) | collective-permute-done | bytes 131104 | tf_op jit(solution)/shard_map/ppermute | solution.py:394
  27.0 3.3 %collective-permute-start.6 = (bf16[128,512]{1,0:T(8,128)(2,1)S(1)}, bf16[128,512]{1,0:T(8,128)(2,1)S(1)}, u32[]{:S(2)}, u32[]{:S(2)}) collective-permute-start(bf16[128,512]{1,0:T(8,128)(2,1)S(1)} %get-tuple-element.56), channel_id=1, source_target_pairs={{0,12},{4,8},{8,4},{12,0},{16,28},{20,24},{24,20},{28,16},{1,13},{... | collective-permute-start | bytes 393224 | tf_op jit(solution)/shard_map/ppermute | solution.py:394
  32.0 2.3 %collective-permute-done.6 = bf16[128,512]{1,0:T(8,128)(2,1)S(1)} collective-permute-done((bf16[128,512]{1,0:T(8,128)(2,1)S(1)}, bf16[128,512]{1,0:T(8,128)(2,1)S(1)}, u32[]{:S(2)}, u32[]{:S(2)}) %collective-permute-start.6) | collective-permute-done | bytes 131104 | tf_op jit(solution)/shard_map/ppermute | solution.py:394
  39.9 2.6 %collective-permute-start.10 = (bf16[512,512]{1,0:T(8,128)(2,1)S(1)}, bf16[512,512]{1,0:T(8,128)(2,1)S(1)}, u32[]{:S(2)}, u32[]{:S(2)}) collective-permute-start(bf16[512,512]{1,0:T(8,128)(2,1)S(1)} %project_halo.1.refs_7_), channel_id=1, source_target_pairs={{0,4},{4,8},{8,12},{12,16},{16,20},{20,24},{24,28},{1,5},{5,9},{9,... | collective-permute-start | bytes 1572872 | tf_op jit(solution)/shard_map/ppermute | solution.py:427
  42.5 5.6 %project_block.1 = (bf16[1024,512]{1,0:T(8,128)(2,1)S(1)}, bf16[1024,512]{1,0:T(8,128)(2,1)S(1)}, bf16[1024,512]{1,0:T(8,128)(2,1)S(1)}) custom-call(bf16[1024,512]{1,0:T(8,128)(2,1)S(1)} %get-tuple-element.48.refs_0_, bf16[1024,512]{1,0:T(8,128)(2,1)S(1)} %collective-permute-done.7.refs_1_, bf16[1024,512]{1,0:T(8,128)(2,1)S(1)} %fence.4.refs_2_, ...), custom_call_target="tpu_custom_call" | custom-call | flops 6600000000 | bytes 1048576 | tf_op jit(solution)/shard_map/project_block/pallas_call | solution.py:38
  49.9 3.8 %collective-permute-done.10.refs_4_ = bf16[512,512]{1,0:T(8,128)(2,1)S(1)} collective-permute-done((bf16[512,512]{1,0:T(8,128)(2,1)S(1)}, bf16[512,512]{1,0:T(8,128)(2,1)S(1)}, u32[]{:S(2)}, u32[]{:S(2)}) %collective-permute-start.10) | collective-permute-done | bytes 524320 | tf_op jit(solution)/shard_map/ppermute | solution.py:427
  53.8 8.2 %collective-permute-done.13.refs_3_ = bf16[512,512]{1,0:T(8,128)(2,1)S(1)} collective-permute-done((bf16[512,512]{1,0:T(8,128)(2,1)S(1)}, bf16[512,512]{1,0:T(8,128)(2,1)S(1)}, u32[]{:S(2)}, u32[]{:S(2)}) %collective-permute-start.13) | collective-permute-done | bytes 524320 | tf_op jit(solution)/shard_map/ppermute | solution.py:387
  62.0 5.8 %local_part.1 = (f32[8,64,512]{2,1,0:T(8,128)S(1)}, f32[8,64,512]{2,1,0:T(8,128)S(1)}, f32[64,128]{1,0:T(8,128)S(1)}, f32[64,128]{1,0:T(8,128)S(1)}) custom-call(s32[3]{0:T(128)S(1)} %pad_add_fusion.pos_ref.refs_0_, bf16[1024,512]{1,0:T(8,128)(2,1)S(1)} %get-tuple-element.60.refs_1_.refs_2_, bf16[1024,512]{1,0:T(8,128)(2,1)S(1)} %get-tuple-element.61.refs_2_, ...), custom_call_target="tpu_custom_call" | custom-call | flops 5500000256 | bytes 1048576 | tf_op jit(solution)/shard_map/local_part/pallas_call | solution.py:38
  67.8 6.4 %column_part.2 = (bf16[272,128]{1,0:T(8,128)(2,1)S(1)}, bf16[272,128]{1,0:T(8,128)(2,1)S(1)}, bf16[272,128]{1,0:T(8,128)(2,1)S(1)}, bf16[272,128]{1,0:T(8,128)(2...) custom-call(s32[3]{0:T(128)S(1)} %pad_add_fusion.pos_ref.refs_0_, ...), custom_call_target="tpu_custom_call" | custom-call | flops 6600000000 | bytes 1048576 | tf_op jit(solution)/shard_map/column_part/pallas_call | solution.py:38
  74.2 6.7 %column_part.3 = (bf16[544,128]{1,0:T(8,128)(2,1)S(1)}, bf16[544,128]{1,0:T(8,128)(2,1)S(1)}, bf16[544,128]{1,0:T(8,128)(2,1)S(1)}, bf16[544,128]{1,0:T(8,128)(2...) custom-call(s32[3]{0:T(128)S(1)} %pad_add_fusion.pos_ref.refs_0_, ...), custom_call_target="tpu_custom_call" | custom-call | flops 6600000000 | bytes 1048576 | tf_op jit(solution)/shard_map/column_part/pallas_call | solution.py:38
  80.9 3.1 %collective-permute-start.17 = (bf16[544,128]{1,0:T(8,128)(2,1)S(1)}, bf16[544,128]{1,0:T(8,128)(2,1)S(1)}, u32[]{:S(2)}, u32[]{:S(2)}) collective-permute-start(bf16[544,128]{1,0:T(8,128)(2,1)S(1)} %get-tuple-element.76), channel_id=1, source_target_pairs={{0,16},{4,20},{8,24},{12,28},{16,0},{20,4},{24,8},{28,12},{1,17},{... | collective-permute-start | bytes 417800 | tf_op jit(solution)/shard_map/ppermute | solution.py:394
  85.6 9.0 %collective-permute-done.17.refs_6_ = bf16[544,128]{1,0:T(8,128)(2,1)S(1)} collective-permute-done((bf16[544,128]{1,0:T(8,128)(2,1)S(1)}, bf16[544,128]{1,0:T(8,128)(2,1)S(1)}, u32[]{:S(2)}, u32[]{:S(2)}) %collective-permute-start.17) | collective-permute-done | bytes 139296 | tf_op jit(solution)/shard_map/ppermute | solution.py:394
  94.5 3.6 %collective-permute-done.18.refs_7_ = bf16[544,128]{1,0:T(8,128)(2,1)S(1)} collective-permute-done((bf16[544,128]{1,0:T(8,128)(2,1)S(1)}, bf16[544,128]{1,0:T(8,128)(2,1)S(1)}, u32[]{:S(2)}, u32[]{:S(2)}) %collective-permute-start.18) | collective-permute-done | bytes 139296 | tf_op jit(solution)/shard_map/ppermute | solution.py:394
  99.9 2.9 %collective-permute-start.23 = (bf16[544,128]{1,0:T(8,128)(2,1)S(1)}, bf16[544,128]{1,0:T(8,128)(2,1)S(1)}, u32[]{:S(2)}, u32[]{:S(2)}) collective-permute-start(bf16[544,128]{1,0:T(8,128)(2,1)S(1)} %get-tuple-element.83), channel_id=1, source_target_pairs={{0,24},{4,28},{8,16},{12,20},{16,8},{20,12},{24,0},{28,4},{1,25},{... | collective-permute-start | bytes 417800 | tf_op jit(solution)/shard_map/ppermute | solution.py:394
  103.9 2.9 %collective-permute-start.26 = (bf16[544,128]{1,0:T(8,128)(2,1)S(1)}, bf16[544,128]{1,0:T(8,128)(2,1)S(1)}, u32[]{:S(2)}, u32[]{:S(2)}) collective-permute-start(bf16[544,128]{1,0:T(8,128)(2,1)S(1)} %get-tuple-element.86), channel_id=1, source_target_pairs={{0,12},{4,8},{8,4},{12,0},{16,28},{20,24},{24,20},{28,16},{1,13},{... | collective-permute-start | bytes 417800 | tf_op jit(solution)/shard_map/ppermute | solution.py:394
  109.2 2.8 %collective-permute-done.24.refs_6_ = bf16[544,128]{1,0:T(8,128)(2,1)S(1)} collective-permute-done((bf16[544,128]{1,0:T(8,128)(2,1)S(1)}, bf16[544,128]{1,0:T(8,128)(2,1)S(1)}, u32[]{:S(2)}, u32[]{:S(2)}) %collective-permute-start.24) | collective-permute-done | bytes 139296 | tf_op jit(solution)/shard_map/ppermute | solution.py:394
  112.0 2.0 %collective-permute-done.25.refs_7_ = bf16[544,128]{1,0:T(8,128)(2,1)S(1)} collective-permute-done((bf16[544,128]{1,0:T(8,128)(2,1)S(1)}, bf16[544,128]{1,0:T(8,128)(2,1)S(1)}, u32[]{:S(2)}, u32[]{:S(2)}) %collective-permute-start.25) | collective-permute-done | bytes 139296 | tf_op jit(solution)/shard_map/ppermute | solution.py:394
  114.0 3.0 %collective-permute-done.26.refs_8_ = bf16[544,128]{1,0:T(8,128)(2,1)S(1)} collective-permute-done((bf16[544,128]{1,0:T(8,128)(2,1)S(1)}, bf16[544,128]{1,0:T(8,128)(2,1)S(1)}, u32[]{:S(2)}, u32[]{:S(2)}) %collective-permute-start.26) | collective-permute-done | bytes 139296 | tf_op jit(solution)/shard_map/ppermute | solution.py:394
  120.0 1.9 %collective-permute-done.22.refs_5_.refs_2_ = bf16[128,2048]{1,0:T(8,128)(2,1)S(1)} collective-permute-done((bf16[128,2048]{1,0:T(8,128)(2,1)S(1)}, bf16[128,2048]{1,0:T(8,128)(2,1)S(1)}, u32[]{:S(2)}, u32[]{:S(2)}) %collective-permute-start.22) | collective-permute-done | bytes 524320 | tf_op jit(solution)/shard_map/ppermute | solution.py:387
  124.3 11.7 %collective-permute-done.28.refs_4_ = bf16[128,2048]{1,0:T(8,128)(2,1)S(1)} collective-permute-done((bf16[128,2048]{1,0:T(8,128)(2,1)S(1)}, bf16[128,2048]{1,0:T(8,128)(2,1)S(1)}, u32[]{:S(2)}, u32[]{:S(2)}) %collective-permute-start.28) | collective-permute-done | bytes 524320 | tf_op jit(solution)/shard_map/ppermute | solution.py:387
  (68 shorter events, 28.0 us)
Async XLA Ops:
  0.0 34.5 %collective-permute-start.8 = (bf16[1024,512]{1,0:T(8,128)(2,1)}, bf16[1024,512]{1,0:T(8,128)(2,1)S(1)}, u32[]{:S(2)}, u32[]{:S(2)}) collective-permute-start(bf16[1024,512]{1,0:T(8,128)(2,1)} %tok_hbm.1), channel_id=1, source_target_pairs={{0,2},{1,3},{2,0},{3,1},{4,6},{5,7},{6,4},{7,5},{8,10},{9,11},{10,... | collective-permute-start | bytes 3145736 | tf_op jit(solution)/shard_map/ppermute | solution.py:387
  4.9 18.3 %collective-permute-start = (bf16[128,512]{1,0:T(8,128)(2,1)S(1)}, bf16[128,512]{1,0:T(8,128)(2,1)S(1)}, u32[]{:S(2)}, u32[]{:S(2)}) collective-permute-start(bf16[128,512]{1,0:T(8,128)(2,1)S(1)} %get-tuple-element.50), channel_id=1, source_target_pairs={{0,16},{4,20},{8,24},{12,28},{16,0},{20,4},{24,8},{28,12},{1,17},{... | collective-permute-start | bytes 393224 | tf_op jit(solution)/shard_map/ppermute | solution.py:394
  7.5 19.4 %collective-permute-start.1 = (bf16[128,512]{1,0:T(8,128)(2,1)S(1)}, bf16[128,512]{1,0:T(8,128)(2,1)S(1)}, u32[]{:S(2)}, u32[]{:S(2)}) collective-permute-start(bf16[128,512]{1,0:T(8,128)(2,1)S(1)} %get-tuple-element.51), channel_id=1, source_target_pairs={{0,20},{4,16},{8,28},{12,24},{16,4},{20,0},{24,12},{28,8},{1,21},{... | collective-permute-start | bytes 393224 | tf_op jit(solution)/shard_map/ppermute | solution.py:394
  8.8 18.2 %collective-permute-start.2 = (bf16[128,512]{1,0:T(8,128)(2,1)S(1)}, bf16[128,512]{1,0:T(8,128)(2,1)S(1)}, u32[]{:S(2)}, u32[]{:S(2)}) collective-permute-start(bf16[128,512]{1,0:T(8,128)(2,1)S(1)} %get-tuple-element.52), channel_id=1, source_target_pairs={{0,24},{4,28},{8,16},{12,20},{16,8},{20,12},{24,0},{28,4},{1,25},{... | collective-permute-start | bytes 393224 | tf_op jit(solution)/shard_map/ppermute | solution.py:394
  12.4 17.9 %collective-permute-start.3 = (bf16[128,512]{1,0:T(8,128)(2,1)S(1)}, bf16[128,512]{1,0:T(8,128)(2,1)S(1)}, u32[]{:S(2)}, u32[]{:S(2)}) collective-permute-start(bf16[128,512]{1,0:T(8,128)(2,1)S(1)} %get-tuple-element.53), channel_id=1, source_target_pairs={{0,28},{4,24},{8,20},{12,16},{16,12},{20,8},{24,4},{28,0},{1,29},{... | collective-permute-start | bytes 393224 | tf_op jit(solution)/shard_map/ppermute | solution.py:394
  23.2 7.2 %collective-permute-start.4 = (bf16[128,512]{1,0:T(8,128)(2,1)S(1)}, bf16[128,512]{1,0:T(8,128)(2,1)S(1)}, u32[]{:S(2)}, u32[]{:S(2)}) collective-permute-start(bf16[128,512]{1,0:T(8,128)(2,1)S(1)} %get-tuple-element.54), channel_id=1, source_target_pairs={{0,4},{4,0},{8,12},{12,8},{16,20},{20,16},{24,28},{28,24},{1,5},{5... | collective-permute-start | bytes 393224 | tf_op jit(solution)/shard_map/ppermute | solution.py:394
  27.0 7.4 %collective-permute-start.6 = (bf16[128,512]{1,0:T(8,128)(2,1)S(1)}, bf16[128,512]{1,0:T(8,128)(2,1)S(1)}, u32[]{:S(2)}, u32[]{:S(2)}) collective-permute-start(bf16[128,512]{1,0:T(8,128)(2,1)S(1)} %get-tuple-element.56), channel_id=1, source_target_pairs={{0,12},{4,8},{8,4},{12,0},{16,28},{20,24},{24,20},{28,16},{1,13},{... | collective-permute-start | bytes 393224 | tf_op jit(solution)/shard_map/ppermute | solution.py:394
  35.0 13.9 %collective-permute-start.11 = (bf16[512,512]{1,0:T(8,128)(2,1)S(1)}, bf16[512,512]{1,0:T(8,128)(2,1)S(1)}, u32[]{:S(2)}, u32[]{:S(2)}) collective-permute-start(bf16[512,512]{1,0:T(8,128)(2,1)S(1)} %get-tuple-element.92.refs_1_), channel_id=1, source_target_pairs={{0,2},{1,3},{2,0},{3,1},{4,6},{5,7},{6,4},{7,5},{8,10},{9,11},{10,... | collective-permute-start | bytes 1572872 | tf_op jit(solution)/shard_map/ppermute | solution.py:387
  39.9 13.9 %collective-permute-start.10 = (bf16[512,512]{1,0:T(8,128)(2,1)S(1)}, bf16[512,512]{1,0:T(8,128)(2,1)S(1)}, u32[]{:S(2)}, u32[]{:S(2)}) collective-permute-start(bf16[512,512]{1,0:T(8,128)(2,1)S(1)} %project_halo.1.refs_7_), channel_id=1, source_target_pairs={{0,4},{4,8},{8,12},{12,16},{16,20},{20,24},{24,28},{1,5},{5,9},{9,... | collective-permute-start | bytes 1572872 | tf_op jit(solution)/shard_map/ppermute | solution.py:427
  48.9 13.1 %collective-permute-start.13 = (bf16[512,512]{1,0:T(8,128)(2,1)S(1)}, bf16[512,512]{1,0:T(8,128)(2,1)S(1)}, u32[]{:S(2)}, u32[]{:S(2)}) collective-permute-start(bf16[512,512]{1,0:T(8,128)(2,1)S(1)} %fence.5.refs_1_), channel_id=1, source_target_pairs={{0,2},{1,3},{2,0},{3,1},{4,6},{5,7},{6,4},{7,5},{8,10},{9,11},{10,... | collective-permute-start | bytes 1572872 | tf_op jit(solution)/shard_map/ppermute | solution.py:387
  49.4 18.3 %collective-permute-start.15 = (bf16[512,512]{1,0:T(8,128)(2,1)S(1)}, bf16[512,512]{1,0:T(8,128)(2,1)S(1)}, u32[]{:S(2)}, u32[]{:S(2)}) collective-permute-start(bf16[512,512]{1,0:T(8,128)(2,1)S(1)} %get-tuple-element.92.refs_1_), channel_id=1, source_target_pairs={{0,1},{1,0},{2,3},{3,2},{4,5},{5,4},{6,7},{7,6},{8,9},{9,8},{10,11... | collective-permute-start | bytes 1572872 | tf_op jit(solution)/shard_map/ppermute | solution.py:387
  49.4 18.3 %collective-permute-start.16 = (bf16[512,512]{1,0:T(8,128)(2,1)S(1)}, bf16[512,512]{1,0:T(8,128)(2,1)S(1)}, u32[]{:S(2)}, u32[]{:S(2)}) collective-permute-start(bf16[512,512]{1,0:T(8,128)(2,1)S(1)} %collective-permute-done.11.refs_1_.refs_3_), channel_id=1, source_target_pairs={{0,1},{1,0},{2,3},{3,2},{4,5},{5,4},{6,7},{7,6},{8,9},{9,8},{10,11... | collective-permute-start | bytes 1572872 | tf_op jit(solution)/shard_map/ppermute | solution.py:387
  49.9 53.9 %collective-permute-start.21 = (bf16[512,2048]{1,0:T(8,128)(2,1)S(1)}, bf16[512,2048]{1,0:T(8,128)(2,1)S(1)}, u32[]{:S(2)}, u32[]{:S(2)}) collective-permute-start(bf16[512,2048]{1,0:T(8,128)(2,1)S(1)} %copy-done.3), channel_id=1, source_target_pairs={{0,1},{1,0},{2,3},{3,2},{4,5},{5,4},{6,7},{7,6},{8,9},{9,8},{10,11... | collective-permute-start | bytes 6291464 | tf_op jit(solution)/shard_map/ppermute | solution.py:387
  53.7 20.4 %collective-permute-start.12 = (bf16[512,512]{1,0:T(8,128)(2,1)S(1)}, bf16[512,512]{1,0:T(8,128)(2,1)S(1)}, u32[]{:S(2)}, u32[]{:S(2)}) collective-permute-start(bf16[512,512]{1,0:T(8,128)(2,1)S(1)} %fence.5.refs_1_), channel_id=1, source_target_pairs={{0,1},{1,0},{2,3},{3,2},{4,5},{5,4},{6,7},{7,6},{8,9},{9,8},{10,11... | collective-permute-start | bytes 1572872 | tf_op jit(solution)/shard_map/ppermute | solution.py:387
  62.0 12.2 %collective-permute-start.14 = (bf16[512,512]{1,0:T(8,128)(2,1)S(1)}, bf16[512,512]{1,0:T(8,128)(2,1)S(1)}, u32[]{:S(2)}, u32[]{:S(2)}) collective-permute-start(bf16[512,512]{1,0:T(8,128)(2,1)S(1)} %collective-permute-done.13.refs_3_), channel_id=1, source_target_pairs={{0,1},{1,0},{2,3},{3,2},{4,5},{5,4},{6,7},{7,6},{8,9},{9,8},{10,11... | collective-permute-start | bytes 1572872 | tf_op jit(solution)/shard_map/ppermute | solution.py:387
  80.9 13.6 %collective-permute-start.17 = (bf16[544,128]{1,0:T(8,128)(2,1)S(1)}, bf16[544,128]{1,0:T(8,128)(2,1)S(1)}, u32[]{:S(2)}, u32[]{:S(2)}) collective-permute-start(bf16[544,128]{1,0:T(8,128)(2,1)S(1)} %get-tuple-element.76), channel_id=1, source_target_pairs={{0,16},{4,20},{8,24},{12,28},{16,0},{20,4},{24,8},{28,12},{1,17},{... | collective-permute-start | bytes 417800 | tf_op jit(solution)/shard_map/ppermute | solution.py:394
  84.0 14.1 %collective-permute-start.18 = (bf16[544,128]{1,0:T(8,128)(2,1)S(1)}, bf16[544,128]{1,0:T(8,128)(2,1)S(1)}, u32[]{:S(2)}, u32[]{:S(2)}) collective-permute-start(bf16[544,128]{1,0:T(8,128)(2,1)S(1)} %get-tuple-element.77), channel_id=1, source_target_pairs={{0,20},{4,16},{8,28},{12,24},{16,4},{20,0},{24,12},{28,8},{1,21},{... | collective-permute-start | bytes 417800 | tf_op jit(solution)/shard_map/ppermute | solution.py:394
  85.0 13.1 %collective-permute-start.19 = (bf16[544,128]{1,0:T(8,128)(2,1)S(1)}, bf16[544,128]{1,0:T(8,128)(2,1)S(1)}, u32[]{:S(2)}, u32[]{:S(2)}) collective-permute-start(bf16[544,128]{1,0:T(8,128)(2,1)S(1)} %get-tuple-element.78), channel_id=1, source_target_pairs={{0,4},{4,0},{8,12},{12,8},{16,20},{20,16},{24,28},{28,24},{1,5},{5... | collective-permute-start | bytes 417800 | tf_op jit(solution)/shard_map/ppermute | solution.py:394
  99.9 9.3 %collective-permute-start.23 = (bf16[544,128]{1,0:T(8,128)(2,1)S(1)}, bf16[544,128]{1,0:T(8,128)(2,1)S(1)}, u32[]{:S(2)}, u32[]{:S(2)}) collective-permute-start(bf16[544,128]{1,0:T(8,128)(2,1)S(1)} %get-tuple-element.83), channel_id=1, source_target_pairs={{0,24},{4,28},{8,16},{12,20},{16,8},{20,12},{24,0},{28,4},{1,25},{... | collective-permute-start | bytes 417800 | tf_op jit(solution)/shard_map/ppermute | solution.py:394
  102.8 9.2 %collective-permute-start.24 = (bf16[544,128]{1,0:T(8,128)(2,1)S(1)}, bf16[544,128]{1,0:T(8,128)(2,1)S(1)}, u32[]{:S(2)}, u32[]{:S(2)}) collective-permute-start(bf16[544,128]{1,0:T(8,128)(2,1)S(1)} %get-tuple-element.84), channel_id=1, source_target_pairs={{0,28},{4,24},{8,20},{12,16},{16,12},{20,8},{24,4},{28,0},{1,29},{... | collective-permute-start | bytes 417800 | tf_op jit(solution)/shard_map/ppermute | solution.py:394
  103.9 10.1 %collective-permute-start.25 = (bf16[544,128]{1,0:T(8,128)(2,1)S(1)}, bf16[544,128]{1,0:T(8,128)(2,1)S(1)}, u32[]{:S(2)}, u32[]{:S(2)}) collective-permute-start(bf16[544,128]{1,0:T(8,128)(2,1)S(1)} %get-tuple-element.85), channel_id=1, source_target_pairs={{0,8},{4,12},{8,0},{12,4},{16,24},{20,28},{24,16},{28,20},{1,9},{5... | collective-permute-start | bytes 417800 | tf_op jit(solution)/shard_map/ppermute | solution.py:394
  103.9 13.0 %collective-permute-start.26 = (bf16[544,128]{1,0:T(8,128)(2,1)S(1)}, bf16[544,128]{1,0:T(8,128)(2,1)S(1)}, u32[]{:S(2)}, u32[]{:S(2)}) collective-permute-start(bf16[544,128]{1,0:T(8,128)(2,1)S(1)} %get-tuple-element.86), channel_id=1, source_target_pairs={{0,12},{4,8},{8,4},{12,0},{16,28},{20,24},{24,20},{28,16},{1,13},{... | collective-permute-start | bytes 417800 | tf_op jit(solution)/shard_map/ppermute | solution.py:394
  108.6 13.2 %collective-permute-start.22 = (bf16[128,2048]{1,0:T(8,128)(2,1)S(1)}, bf16[128,2048]{1,0:T(8,128)(2,1)S(1)}, u32[]{:S(2)}, u32[]{:S(2)}) collective-permute-start(bf16[128,2048]{1,0:T(8,128)(2,1)S(1)} %get-tuple-element.82), channel_id=1, source_target_pairs={{0,2},{1,3},{2,0},{3,1},{4,6},{5,7},{6,4},{7,5},{8,10},{9,11},{10,... | collective-permute-start | bytes 1572872 | tf_op jit(solution)/shard_map/ppermute | solution.py:387
  123.7 12.3 %collective-permute-start.28 = (bf16[128,2048]{1,0:T(8,128)(2,1)S(1)}, bf16[128,2048]{1,0:T(8,128)(2,1)S(1)}, u32[]{:S(2)}, u32[]{:S(2)}) collective-permute-start(bf16[128,2048]{1,0:T(8,128)(2,1)S(1)} %get-tuple-element.90), channel_id=1, source_target_pairs={{0,2},{1,3},{2,0},{3,1},{4,6},{5,7},{6,4},{7,5},{8,10},{9,11},{10,... | collective-permute-start | bytes 1572872 | tf_op jit(solution)/shard_map/ppermute | solution.py:387
  (9 other events, 31.8 us)

commit v9 on v8

--- a/solution.py
+++ b/solution.py
@@ -13,8 +13,8 @@
 ROWS = 4
 SUB = 8
 CHUNKS = 2
-ORDER = (0, 4, 5, 6, 7, 1, 2, 3)
-HALVES = ((0, 4, 5, 1), (6, 7, 2, 3))
+PEERS = 8
+SHARES = ((4, 5, 1, 2, 3, 0), (6, 7))
 SCALE2 = DH ** (-0.5) * 1.4426950408889634
 FLOOR = -1e29
 MIB = 1024 * 1024
@@ -95,7 +95,7 @@
         c.wait()
     per_owner = STRIDE // len(out_refs)
     part = ROWS * SUB
-    for k, out_ref in zip(ORDER, out_refs):
+    for k, out_ref in enumerate(out_refs):
         d = pos_ref[0] ^ k
         rows = [
             tok_ref[pl.ds(pl.multiple_of(r * STRIDE + d * per_owner, per_owner), per_owner), :]
@@ -256,9 +256,7 @@
 
     def row_and_class(dim):
         i = lax.broadcasted_iota(jnp.int32, (size, size), dim)
-        slot = i // part
-        far = jnp.where(slot < 5, slot + 3, slot - 4)
-        return (jnp.where(slot == 0, 0, far) ^ pos_ref[0]) * ROWS + (i % part) // SUB, i % SUB
+        return ((i // part) ^ pos_ref[0]) * ROWS + (i % part) // SUB, i % SUB
 
     (row_j, class_j), (row_i, class_i) = row_and_class(0), row_and_class(1)
     earlier = jnp.logical_and(class_i == class_j, row_i > row_j)
@@ -298,7 +296,7 @@
     return call(column_kernel, "column_part", 6, [shape((rows, DH))] * owners, args, after, scratch)
 
 
-def mix_kernel(half, pos_ref, *refs):
+def mix_kernel(share, pos_ref, *refs):
     local_refs, refs = refs[: 2 * CHUNKS], refs[2 * CHUNKS :]
     col_refs, (own_ref, send_ref, mixed) = refs[:-3], refs[-3:]
     message = local_refs[0].shape[1]
@@ -309,7 +307,7 @@
         loc_ref, lse_ref = local_refs[2 * i : 2 * i + 2]
         tiles = [jnp.zeros((8, 128), F32)] * 16
         base = i * size
-        for k, col_ref in zip(half, col_refs):
+        for k, col_ref in zip(share, col_refs):
             tail = col_ref[base + HEADS * message : base + size, :].astype(F32)
             tiles[k] = tail[:8] + tail[8:]
         turned = jnp.concatenate(tiles, 0).T[:message]
@@ -318,10 +316,10 @@
         top = jnp.maximum(col_lse, loc_lse)
         w_col = jnp.exp2(col_lse - top)
         w_loc = jnp.exp2(loc_lse - top)
-        share = 1.0 / (w_col + w_loc)
-        w_col = w_col * share
-        w_loc = w_loc * share
-        for n, (k, col_ref) in enumerate(zip(half, col_refs)):
+        scale = 1.0 / (w_col + w_loc)
+        w_col = w_col * scale
+        w_loc = w_loc * scale
+        for n, (k, col_ref) in enumerate(zip(share, col_refs)):
             d = pos_ref[0] ^ k
             to = (n * CHUNKS + i) * span
             for h in range(HEADS):
@@ -339,13 +337,13 @@
         send_ref[x] = mixed[2 * x + 1 - core]
 
 
-def mix(pos, half, columns, locals_, after):
+def mix(pos, share, columns, locals_, after):
     owners, message, width = locals_[0][0].shape
-    tokens = len(half) * CHUNKS * message // ROWS
+    tokens = len(share) * CHUNKS * message // ROWS
     shapes = [shape((2, tokens, width))] * 2
     scratch = [pltpu.VMEM((ROWS, tokens, width), BF16)]
     args = (pos, *[x for pair in locals_ for x in pair], *columns)
-    return call(functools.partial(mix_kernel, half), "mix", 2, shapes, args, after, scratch)
+    return call(functools.partial(mix_kernel, share), "mix", 2, shapes, args, after, scratch)
 
 
 def out_kernel(pos_ref, a_ref, b_ref, wa_ref, wb_ref, send_ref, keep_ref):
@@ -361,17 +359,17 @@
         keep_ref[:, at] = jnp.where(low_side, total[:tokens], total[tokens:])
 
 
-def out_project(pos, own, other, w_own, w_other, after):
+def out_project(pos, own, other, w_own, w_other):
     dims = (own.shape[1], w_own.shape[1])
     shapes = [shape(dims), shape(dims, F32)]
-    return call(out_kernel, "out_project", 2, shapes, (pos, own, other, w_own, w_other), after)
+    return call(out_kernel, "out_project", 2, shapes, (pos, own, other, w_own, w_other))
 
 
 def join_kernel(pos_ref, *refs):
     out_ref = refs[-1]
-    for half, keep, got in zip(HALVES, refs[0:-1:2], refs[1:-1:2]):
-        span = keep.shape[0] // len(half)
-        for n, k in enumerate(half):
+    for share, keep, got in zip(SHARES, refs[0:-1:2], refs[1:-1:2]):
+        span = keep.shape[0] // len(share)
+        for n, k in enumerate(share):
             rows = slice(n * span, (n + 1) * span)
             to = pl.ds(pl.multiple_of((pos_ref[0] ^ k) * span, span), span)
             out_ref[to, :] = (keep[rows, :] + got[rows, :].astype(F32)).astype(BF16)
@@ -393,12 +391,7 @@
     def move(value, k):
         return lax.ppermute(value, "seq", [(i, i ^ k) for i in range(peers)]) if k else value
 
-    return [move(m, k) for m, k in zip(messages, ORDER)]
-
-
-def gather(own):
-    across = swap(own, 2)
-    return own, swap(own, 1), across, swap(across, 1)
+    return [move(m, k) for k, m in enumerate(messages)]
 
 
 def chunked(tokens, w_query, w_key, w_value, w_out):
@@ -418,7 +411,7 @@
     ]
     across = fence(across, classes[0])
     pieces = (block_tokens, swap(fence(block_tokens, classes[0]), 1), across, swap(across, 1))
-    first_pieces = gather(classes[0])
+    first, first_core, first_across = classes[0], swap(classes[0], 1), swap(classes[0], 2)
     weights = stage(order, (w_query, w_key, w_value), messages[1])
     w_other = swap(w_out, 1)
     own_halo = call(
@@ -431,20 +424,24 @@
         6,
         [shape((rows, width))] * 3,
         (*pieces, *weights, own_halo),
-    )
-    class_pieces = (first_pieces, gather(fence(classes[1], first_pieces[2], q)))
+        (w_other,),
+    )
+    first_across = fence(first_across, q)
+    first_pieces = (first, first_core, first_across, swap(first_across, 1))
+    second = fence(classes[1], first_across)
+    second_core, second_across = swap(second, 1), swap(second, 2)
     locals_ = local_part(pos, q, k, v, halo, owners, ())
-    columns, after = [], (locals_[0][0],)
-    for c in class_pieces:
-        columns = column_part(pos, c, weights, columns, owners, after)
-        after = ()
-    columns = dict(zip(ORDER, exchange(columns)))
-    pairs, after, gate = [], (), ()
-    for half in HALVES:
-        own, send = mix(pos, half, [columns[n] for n in half], locals_, after)
-        out, keep = out_project(pos, own, swap(send, 1), w_out, w_other, gate)
+    columns = column_part(pos, first_pieces, weights, (), owners, (locals_[0][0],))
+    second_across = fence(second_across, columns[0])
+    second_pieces = (second, second_core, second_across, swap(second_across, 1))
+    columns = column_part(pos, second_pieces, weights, columns, owners, ())
+    columns = exchange(columns)
+    pairs, after = [], ()
+    for share in SHARES:
+        own, send = mix(pos, share, [columns[n] for n in share], locals_, after)
+        out, keep = out_project(pos, own, swap(send, 1), w_out, w_other)
         pairs.append((keep, swap(out, 2)))
-        after, gate = (keep,), (pairs[-1][1],)
+        after = (keep,)
     return join(pos, pairs)
 
 
@@ -591,7 +588,7 @@
 def shards(tokens, w_query, w_key, w_value, w_out):
     rows, width = w_query.shape
     fits = (
-        lax.axis_size("seq") == len(ORDER)
+        lax.axis_size("seq") == PEERS
         and lax.axis_size("head") == 4
         and tokens.shape == (ROWS * STRIDE, HEADS * DH)
         and (rows, width) == (4 * HEADS * DH, HEADS * DH)

time: 138 us -> 131 us (0.949)
  waiting for transfers between devices: 65.8 us -> 51.6 us
  starting transfers between devices: 33.1 us -> 40.3 us
    ppermute x14, waiting for transfers between devices: 37 us -> 26.7 us  [move(): lax.ppermute(value, 'seq', [(i, i ^ k) for i in range(peers)])]
    ppermute x14, starting transfers between devices: 24.1 us -> 31.3 us  [move(): lax.ppermute(value, 'seq', [(i, i ^ k) for i in range(peers)])]
    ppermute x14, waiting for transfers between devices: 25.1 us -> 20.7 us  [swap(): return lax.ppermute(value, 'head', [(i, i ^ distance) for i in range(4)])]
  transfers between devices with their start and end apart: 29 -> 29, of which waited for: 16 -> 14; matrix products, arithmetic and copies ran while one was open for 0% -> 0% of each run, Pallas kernels for 24% -> 21%
where the time goes in v9:
time: 131 us
  waiting for transfers between devices  51.6 us (39%)
  starting transfers between devices  40.3 us (31%)
  Pallas kernels  37.3 us (28%)
    pallas_call x10, Pallas kernels, call(): pl.pallas_call(run, in_specs=specs + [ANYWHERE] * extra, out_specs=jax.tr...  34.3 us
    ppermute x14, starting transfers between devices, move(): lax.ppermute(value, 'seq', [(i, i ^ k) for i in range(peers)])  31.3 us
    ppermute x14, waiting for transfers between devices, move(): lax.ppermute(value, 'seq', [(i, i ^ k) for i in range(peers)])  26.7 us
    ppermute x14, waiting for transfers between devices, swap(): return lax.ppermute(value, 'head', [(i, i ^ distance) for i in range(4)])  20.7 us
    ppermute x14, starting transfers between devices, swap(): return lax.ppermute(value, 'head', [(i, i ^ distance) for i in range(4)])  6.28 us
    ppermute x1, waiting for transfers between devices, chunked(): lax.ppermute(own_halo, 'seq', [(i, i + 1) for i in range(owners - 1)])  4.16 us
    ppermute x1, starting transfers between devices, chunked(): lax.ppermute(own_halo, 'seq', [(i, i + 1) for i in range(owners - 1)])  2.7 us
  transfers between devices with their start and end apart: 29, of which 14 were waited for; matrix products, arithmetic and copies ran while one was open for 0% of the time, Pallas kernels for 21%

profile of v9, /device:TPU:0, one launch (start us, length us, event | category | flops | bytes accessed | tf_op | source)
XLA Modules:
  0.0 130.8 jit_solution(12596788169906109196)
XLA Ops:
  0.0 2.9 %collective-permute-start.8 = (bf16[1024,512]{1,0:T(8,128)(2,1)}, bf16[1024,512]{1,0:T(8,128)(2,1)S(1)}, u32[]{:S(2)}, u32[]{:S(2)}) collective-permute-start(bf16[1024,512]{1,0:T(8,128)(2,1)} %tok_hbm.1), channel_id=1, source_target_pairs={{0,2},{1,3},{2,0},{3,1},{4,6},{5,7},{6,4},{7,5},{8,10},{9,11},{10,... | collective-permute-start | bytes 3145736 | tf_op jit(solution)/shard_map/ppermute | solution.py:385
  3.0 1.9 %pack_tokens.1 = (bf16[1024,512]{1,0:T(8,128)(2,1)S(1)}, bf16[128,512]{1,0:T(8,128)(2,1)S(1)}, bf16[128,512]{1,0:T(8,128)(2,1)S(1)}, bf16[128,512]{1,0:T(8,128)(...) custom-call(s32[3]{0:T(128)S(1)} %pad_add_fusion.pos_ref.refs_0_, ...), custom_call_target="tpu_custom_call" | custom-call | bytes 2097152 | tf_op jit(solution)/shard_map/pack_tokens/pallas_call | solution.py:112
  8.5 2.6 %collective-permute-start.3 = (bf16[128,512]{1,0:T(8,128)(2,1)S(1)}, bf16[128,512]{1,0:T(8,128)(2,1)S(1)}, u32[]{:S(2)}, u32[]{:S(2)}) collective-permute-start(bf16[128,512]{1,0:T(8,128)(2,1)S(1)} %get-tuple-element.53), channel_id=1, source_target_pairs={{0,16},{4,20},{8,24},{12,28},{16,0},{20,4},{24,8},{28,12},{1,17},{... | collective-permute-start | bytes 393224 | tf_op jit(solution)/shard_map/ppermute | solution.py:392
  11.2 2.9 %collective-permute-start.4 = (bf16[128,512]{1,0:T(8,128)(2,1)S(1)}, bf16[128,512]{1,0:T(8,128)(2,1)S(1)}, u32[]{:S(2)}, u32[]{:S(2)}) collective-permute-start(bf16[128,512]{1,0:T(8,128)(2,1)S(1)} %get-tuple-element.54), channel_id=1, source_target_pairs={{0,20},{4,16},{8,28},{12,24},{16,4},{20,0},{24,12},{28,8},{1,21},{... | collective-permute-start | bytes 393224 | tf_op jit(solution)/shard_map/ppermute | solution.py:392
  14.1 2.2 %collective-permute-done.1 = bf16[128,512]{1,0:T(8,128)(2,1)S(1)} collective-permute-done((bf16[128,512]{1,0:T(8,128)(2,1)S(1)}, bf16[128,512]{1,0:T(8,128)(2,1)S(1)}, u32[]{:S(2)}, u32[]{:S(2)}) %collective-permute-start.1) | collective-permute-done | bytes 131104 | tf_op jit(solution)/shard_map/ppermute | solution.py:392
  16.3 2.4 %collective-permute-start.5 = (bf16[128,512]{1,0:T(8,128)(2,1)S(1)}, bf16[128,512]{1,0:T(8,128)(2,1)S(1)}, u32[]{:S(2)}, u32[]{:S(2)}) collective-permute-start(bf16[128,512]{1,0:T(8,128)(2,1)S(1)} %get-tuple-element.55), channel_id=1, source_target_pairs={{0,24},{4,28},{8,16},{12,20},{16,8},{20,12},{24,0},{28,4},{1,25},{... | collective-permute-start | bytes 393224 | tf_op jit(solution)/shard_map/ppermute | solution.py:392
  18.7 2.6 %collective-permute-start.6 = (bf16[128,512]{1,0:T(8,128)(2,1)S(1)}, bf16[128,512]{1,0:T(8,128)(2,1)S(1)}, u32[]{:S(2)}, u32[]{:S(2)}) collective-permute-start(bf16[128,512]{1,0:T(8,128)(2,1)S(1)} %get-tuple-element.56), channel_id=1, source_target_pairs={{0,28},{4,24},{8,20},{12,16},{16,12},{20,8},{24,4},{28,0},{1,29},{... | collective-permute-start | bytes 393224 | tf_op jit(solution)/shard_map/ppermute | solution.py:392
  21.5 9.2 %collective-permute-done.4 = bf16[128,512]{1,0:T(8,128)(2,1)S(1)} collective-permute-done((bf16[128,512]{1,0:T(8,128)(2,1)S(1)}, bf16[128,512]{1,0:T(8,128)(2,1)S(1)}, u32[]{:S(2)}, u32[]{:S(2)}) %collective-permute-start.4) | collective-permute-done | bytes 131104 | tf_op jit(solution)/shard_map/ppermute | solution.py:392
  36.2 2.7 %collective-permute-start.11 = (bf16[512,512]{1,0:T(8,128)(2,1)S(1)}, bf16[512,512]{1,0:T(8,128)(2,1)S(1)}, u32[]{:S(2)}, u32[]{:S(2)}) collective-permute-start(bf16[512,512]{1,0:T(8,128)(2,1)S(1)} %project_halo.1.refs_7_), channel_id=1, source_target_pairs={{0,4},{4,8},{8,12},{12,16},{16,20},{20,24},{24,28},{1,5},{5,9},{9,... | collective-permute-start | bytes 1572872 | tf_op jit(solution)/shard_map/ppermute | solution.py:420
  39.0 5.6 %project_block.1 = (bf16[1024,512]{1,0:T(8,128)(2,1)S(1)}, bf16[1024,512]{1,0:T(8,128)(2,1)S(1)}, bf16[1024,512]{1,0:T(8,128)(2,1)S(1)}) custom-call(bf16[1024,512]{1,0:T(8,128)(2,1)S(1)} %get-tuple-element.48.refs_0_, bf16[1024,512]{1,0:T(8,128)(2,1)S(1)} %collective-permute-done.7.refs_1_, bf16[1024,512]{1,0:T(8,128)(2,1)S(1)} %fence.6.refs_2_, ...), custom_call_target="tpu_custom_call" | custom-call | flops 6600000000 | bytes 1048576 | tf_op jit(solution)/shard_map/project_block/pallas_call | solution.py:38
  46.0 4.2 %collective-permute-done.11.refs_4_ = bf16[512,512]{1,0:T(8,128)(2,1)S(1)} collective-permute-done((bf16[512,512]{1,0:T(8,128)(2,1)S(1)}, bf16[512,512]{1,0:T(8,128)(2,1)S(1)}, u32[]{:S(2)}, u32[]{:S(2)}) %collective-permute-start.11) | collective-permute-done | bytes 524320 | tf_op jit(solution)/shard_map/ppermute | solution.py:420
  50.2 5.8 %local_part.1 = (f32[8,64,512]{2,1,0:T(8,128)S(1)}, f32[8,64,512]{2,1,0:T(8,128)S(1)}, f32[64,128]{1,0:T(8,128)S(1)}, f32[64,128]{1,0:T(8,128)S(1)}) custom-call(s32[3]{0:T(128)S(1)} %pad_add_fusion.pos_ref.refs_0_, bf16[1024,512]{1,0:T(8,128)(2,1)S(1)} %get-tuple-element.60.refs_1_, bf16[1024,512]{1,0:T(8,128)(2,1)S(1)} %get-tuple-element.61.refs_2_, ...), custom_call_target="tpu_custom_call" | custom-call | flops 5500000256 | bytes 1048576 | tf_op jit(solution)/shard_map/local_part/pallas_call | solution.py:38
  56.0 6.4 %column_part.2 = (bf16[272,128]{1,0:T(8,128)(2,1)S(1)}, bf16[272,128]{1,0:T(8,128)(2,1)S(1)}, bf16[272,128]{1,0:T(8,128)(2,1)S(1)}, bf16[272,128]{1,0:T(8,128)(2...) custom-call(s32[3]{0:T(128)S(1)} %pad_add_fusion.pos_ref.refs_0_, ...), custom_call_target="tpu_custom_call" | custom-call | flops 6600000000 | bytes 1048576 | tf_op jit(solution)/shard_map/column_part/pallas_call | solution.py:38
  62.5 1.9 %collective-permute-done.17.refs_4_ = bf16[512,512]{1,0:T(8,128)(2,1)S(1)} collective-permute-done((bf16[512,512]{1,0:T(8,128)(2,1)S(1)}, bf16[512,512]{1,0:T(8,128)(2,1)S(1)}, u32[]{:S(2)}, u32[]{:S(2)}) %collective-permute-start.17) | collective-permute-done | bytes 524320 | tf_op jit(solution)/shard_map/ppermute | solution.py:385
  64.4 6.7 %column_part.3 = (bf16[544,128]{1,0:T(8,128)(2,1)S(1)}, bf16[544,128]{1,0:T(8,128)(2,1)S(1)}, bf16[544,128]{1,0:T(8,128)(2,1)S(1)}, bf16[544,128]{1,0:T(8,128)(2...) custom-call(s32[3]{0:T(128)S(1)} %pad_add_fusion.pos_ref.refs_0_, ...), custom_call_target="tpu_custom_call" | custom-call | flops 6600000000 | bytes 1048576 | tf_op jit(solution)/shard_map/column_part/pallas_call | solution.py:38
  71.0 9.0 %collective-permute-start.18 = (bf16[544,128]{1,0:T(8,128)(2,1)S(1)}, bf16[544,128]{1,0:T(8,128)(2,1)S(1)}, u32[]{:S(2)}, u32[]{:S(2)}) collective-permute-start(bf16[544,128]{1,0:T(8,128)(2,1)S(1)} %get-tuple-element.75), channel_id=1, source_target_pairs={{0,16},{4,20},{8,24},{12,28},{16,0},{20,4},{24,8},{28,12},{1,17},{... | collective-permute-start | bytes 417800 | tf_op jit(solution)/shard_map/ppermute | solution.py:392
  83.5 6.9 %collective-permute-done.18.refs_5_ = bf16[544,128]{1,0:T(8,128)(2,1)S(1)} collective-permute-done((bf16[544,128]{1,0:T(8,128)(2,1)S(1)}, bf16[544,128]{1,0:T(8,128)(2,1)S(1)}, u32[]{:S(2)}, u32[]{:S(2)}) %collective-permute-start.18) | collective-permute-done | bytes 139296 | tf_op jit(solution)/shard_map/ppermute | solution.py:392
  90.4 2.0 %collective-permute-done.19.refs_6_ = bf16[544,128]{1,0:T(8,128)(2,1)S(1)} collective-permute-done((bf16[544,128]{1,0:T(8,128)(2,1)S(1)}, bf16[544,128]{1,0:T(8,128)(2,1)S(1)}, u32[]{:S(2)}, u32[]{:S(2)}) %collective-permute-start.19) | collective-permute-done | bytes 139296 | tf_op jit(solution)/shard_map/ppermute | solution.py:392
  94.8 2.1 %mix.2 = (bf16[2,192,512]{2,1,0:T(8,128)(2,1)S(1)}, bf16[2,192,512]{2,1,0:T(8,128)(2,1)S(1)}) custom-call(s32[3]{0:T(128)S(1)} %pad_add_fusion.pos_ref.refs_0_, f32[8,64,512]{2,1,0:T(8,128)S(1)} %get-tuple-element.63.refs_8_.refs_1_, f32[64,128]{1,0:T(8,128)S(1)} %get-tuple-element.64.refs_2_, f32[8,64,512]{2,1,0:T(8,128)S(1)} %get-tuple-element.65.refs_3_, ...), custom_call_target="tpu_custom_call" | custom-call | flops 2200000000 | bytes 1048576 | tf_op jit(solution)/shard_map/mix/pallas_call | solution.py:38
  97.3 4.4 %collective-permute-start.26 = (bf16[544,128]{1,0:T(8,128)(2,1)S(1)}, bf16[544,128]{1,0:T(8,128)(2,1)S(1)}, u32[]{:S(2)}, u32[]{:S(2)}) collective-permute-start(bf16[544,128]{1,0:T(8,128)(2,1)S(1)} %get-tuple-element.86), channel_id=1, source_target_pairs={{0,28},{4,24},{8,20},{12,16},{16,12},{20,8},{24,4},{28,0},{1,29},{... | collective-permute-start | bytes 417800 | tf_op jit(solution)/shard_map/ppermute | solution.py:392
  101.7 2.4 %out_project.2 = (bf16[192,2048]{1,0:T(8,128)(2,1)S(1)}, f32[192,2048]{1,0:T(8,128)S(1)}) custom-call(s32[3]{0:T(128)S(1)} %pad_add_fusion.pos_ref.refs_0_, bf16[2,192,512]{2,1,0:T(8,128)(2,1)S(1)} %get-tuple-element.81.refs_1_, bf16[2,192,512]{2,1,0:T(8,128)(2,1)S(1)} %collective-permute-done.23.refs_2_, bf16[512,2048]{1,0:T(8,128)(2,1)S(1)} %copy-done.3, ...), custom_call_target="tpu_custom_call" | custom-call | flops 2200000000 | bytes 1048576 | tf_op jit(solution)/shard_map/out_project/pallas_call | solution.py:38
  105.4 3.4 %collective-permute-done.26.refs_6_ = bf16[544,128]{1,0:T(8,128)(2,1)S(1)} collective-permute-done((bf16[544,128]{1,0:T(8,128)(2,1)S(1)}, bf16[544,128]{1,0:T(8,128)(2,1)S(1)}, u32[]{:S(2)}, u32[]{:S(2)}) %collective-permute-start.26) | collective-permute-done | bytes 139296 | tf_op jit(solution)/shard_map/ppermute | solution.py:392
  113.3 15.8 %collective-permute-done.28.refs_4_ = bf16[64,2048]{1,0:T(8,128)(2,1)S(1)} collective-permute-done((bf16[64,2048]{1,0:T(8,128)(2,1)S(1)}, bf16[64,2048]{1,0:T(8,128)(2,1)S(1)}, u32[]{:S(2)}, u32[]{:S(2)}) %collective-permute-start.28) | collective-permute-done | bytes 262176 | tf_op jit(solution)/shard_map/ppermute | solution.py:385
  129.1 1.7 %join.1 = bf16[256,2048]{1,0:T(8,128)(2,1)} custom-call(s32[3]{0:T(128)S(1)} %pad_add_fusion.pos_ref.refs_0_, f32[192,2048]{1,0:T(8,128)S(1)} %get-tuple-element.83.refs_7_.refs_1_, bf16[192,2048]{1,0:T(8,128)(2,1)S(1)} %collective-permute-done.24.refs_2_, f32[64,2048]{1,0:T(8,128)S(1)} %get-tuple-element.89.refs_3_, ...), custom_call_target="tpu_custom_call" | custom-call | flops 2200000000 | bytes 1048576 | tf_op jit(solution)/shard_map/join/pallas_call | solution.py:38
  (70 shorter events, 22.9 us)
Async XLA Ops:
  0.0 30.8 %collective-permute-start.8 = (bf16[1024,512]{1,0:T(8,128)(2,1)}, bf16[1024,512]{1,0:T(8,128)(2,1)S(1)}, u32[]{:S(2)}, u32[]{:S(2)}) collective-permute-start(bf16[1024,512]{1,0:T(8,128)(2,1)} %tok_hbm.1), channel_id=1, source_target_pairs={{0,2},{1,3},{2,0},{3,1},{4,6},{5,7},{6,4},{7,5},{8,10},{9,11},{10,... | collective-permute-start | bytes 3145736 | tf_op jit(solution)/shard_map/ppermute | solution.py:385
  4.9 6.2 %collective-permute-start = (bf16[128,512]{1,0:T(8,128)(2,1)S(1)}, bf16[128,512]{1,0:T(8,128)(2,1)S(1)}, u32[]{:S(2)}, u32[]{:S(2)}) collective-permute-start(bf16[128,512]{1,0:T(8,128)(2,1)S(1)} %get-tuple-element.50), channel_id=1, source_target_pairs={{0,4},{4,0},{8,12},{12,8},{16,20},{20,16},{24,28},{28,24},{1,5},{5... | collective-permute-start | bytes 393224 | tf_op jit(solution)/shard_map/ppermute | solution.py:392
  6.5 9.8 %collective-permute-start.1 = (bf16[128,512]{1,0:T(8,128)(2,1)S(1)}, bf16[128,512]{1,0:T(8,128)(2,1)S(1)}, u32[]{:S(2)}, u32[]{:S(2)}) collective-permute-start(bf16[128,512]{1,0:T(8,128)(2,1)S(1)} %get-tuple-element.51), channel_id=1, source_target_pairs={{0,8},{4,12},{8,0},{12,4},{16,24},{20,28},{24,16},{28,20},{1,9},{5... | collective-permute-start | bytes 393224 | tf_op jit(solution)/shard_map/ppermute | solution.py:392
  8.1 10.6 %collective-permute-start.2 = (bf16[128,512]{1,0:T(8,128)(2,1)S(1)}, bf16[128,512]{1,0:T(8,128)(2,1)S(1)}, u32[]{:S(2)}, u32[]{:S(2)}) collective-permute-start(bf16[128,512]{1,0:T(8,128)(2,1)S(1)} %get-tuple-element.52), channel_id=1, source_target_pairs={{0,12},{4,8},{8,4},{12,0},{16,28},{20,24},{24,20},{28,16},{1,13},{... | collective-permute-start | bytes 393224 | tf_op jit(solution)/shard_map/ppermute | solution.py:392
  8.5 12.8 %collective-permute-start.3 = (bf16[128,512]{1,0:T(8,128)(2,1)S(1)}, bf16[128,512]{1,0:T(8,128)(2,1)S(1)}, u32[]{:S(2)}, u32[]{:S(2)}) collective-permute-start(bf16[128,512]{1,0:T(8,128)(2,1)S(1)} %get-tuple-element.53), channel_id=1, source_target_pairs={{0,16},{4,20},{8,24},{12,28},{16,0},{20,4},{24,8},{28,12},{1,17},{... | collective-permute-start | bytes 393224 | tf_op jit(solution)/shard_map/ppermute | solution.py:392
  11.2 19.5 %collective-permute-start.4 = (bf16[128,512]{1,0:T(8,128)(2,1)S(1)}, bf16[128,512]{1,0:T(8,128)(2,1)S(1)}, u32[]{:S(2)}, u32[]{:S(2)}) collective-permute-start(bf16[128,512]{1,0:T(8,128)(2,1)S(1)} %get-tuple-element.54), channel_id=1, source_target_pairs={{0,20},{4,16},{8,28},{12,24},{16,4},{20,0},{24,12},{28,8},{1,21},{... | collective-permute-start | bytes 393224 | tf_op jit(solution)/shard_map/ppermute | solution.py:392
  16.3 14.4 %collective-permute-start.5 = (bf16[128,512]{1,0:T(8,128)(2,1)S(1)}, bf16[128,512]{1,0:T(8,128)(2,1)S(1)}, u32[]{:S(2)}, u32[]{:S(2)}) collective-permute-start(bf16[128,512]{1,0:T(8,128)(2,1)S(1)} %get-tuple-element.55), channel_id=1, source_target_pairs={{0,24},{4,28},{8,16},{12,20},{16,8},{20,12},{24,0},{28,4},{1,25},{... | collective-permute-start | bytes 393224 | tf_op jit(solution)/shard_map/ppermute | solution.py:392
  18.7 12.0 %collective-permute-start.6 = (bf16[128,512]{1,0:T(8,128)(2,1)S(1)}, bf16[128,512]{1,0:T(8,128)(2,1)S(1)}, u32[]{:S(2)}, u32[]{:S(2)}) collective-permute-start(bf16[128,512]{1,0:T(8,128)(2,1)S(1)} %get-tuple-element.56), channel_id=1, source_target_pairs={{0,28},{4,24},{8,20},{12,16},{16,12},{20,8},{24,4},{28,0},{1,29},{... | collective-permute-start | bytes 393224 | tf_op jit(solution)/shard_map/ppermute | solution.py:392
  21.3 17.6 %collective-permute-start.10 = (bf16[512,2048]{1,0:T(8,128)(2,1)S(1)}, bf16[512,2048]{1,0:T(8,128)(2,1)S(1)}, u32[]{:S(2)}, u32[]{:S(2)}) collective-permute-start(bf16[512,2048]{1,0:T(8,128)(2,1)S(1)} %copy-done.3), channel_id=1, source_target_pairs={{0,1},{1,0},{2,3},{3,2},{4,5},{5,4},{6,7},{7,6},{8,9},{9,8},{10,11... | collective-permute-start | bytes 6291464 | tf_op jit(solution)/shard_map/ppermute | solution.py:385
  31.3 13.9 %collective-permute-start.12 = (bf16[512,512]{1,0:T(8,128)(2,1)S(1)}, bf16[512,512]{1,0:T(8,128)(2,1)S(1)}, u32[]{:S(2)}, u32[]{:S(2)}) collective-permute-start(bf16[512,512]{1,0:T(8,128)(2,1)S(1)} %get-tuple-element.92.refs_1_), channel_id=1, source_target_pairs={{0,2},{1,3},{2,0},{3,1},{4,6},{5,7},{6,4},{7,5},{8,10},{9,11},{10,... | collective-permute-start | bytes 1572872 | tf_op jit(solution)/shard_map/ppermute | solution.py:385
  31.9 24.1 %collective-permute-start.15 = (bf16[512,512]{1,0:T(8,128)(2,1)S(1)}, bf16[512,512]{1,0:T(8,128)(2,1)S(1)}, u32[]{:S(2)}, u32[]{:S(2)}) collective-permute-start(bf16[512,512]{1,0:T(8,128)(2,1)S(1)} %get-tuple-element.92.refs_1_), channel_id=1, source_target_pairs={{0,1},{1,0},{2,3},{3,2},{4,5},{5,4},{6,7},{7,6},{8,9},{9,8},{10,11... | collective-permute-start | bytes 1572872 | tf_op jit(solution)/shard_map/ppermute | solution.py:385
  36.2 14.0 %collective-permute-start.11 = (bf16[512,512]{1,0:T(8,128)(2,1)S(1)}, bf16[512,512]{1,0:T(8,128)(2,1)S(1)}, u32[]{:S(2)}, u32[]{:S(2)}) collective-permute-start(bf16[512,512]{1,0:T(8,128)(2,1)S(1)} %project_halo.1.refs_7_), channel_id=1, source_target_pairs={{0,4},{4,8},{8,12},{12,16},{16,20},{20,24},{24,28},{1,5},{5,9},{9,... | collective-permute-start | bytes 1572872 | tf_op jit(solution)/shard_map/ppermute | solution.py:420
  45.3 10.7 %collective-permute-start.16 = (bf16[512,512]{1,0:T(8,128)(2,1)S(1)}, bf16[512,512]{1,0:T(8,128)(2,1)S(1)}, u32[]{:S(2)}, u32[]{:S(2)}) collective-permute-start(bf16[512,512]{1,0:T(8,128)(2,1)S(1)} %fence.7.refs_1_.refs_3_), channel_id=1, source_target_pairs={{0,1},{1,0},{2,3},{3,2},{4,5},{5,4},{6,7},{7,6},{8,9},{9,8},{10,11... | collective-permute-start | bytes 1572872 | tf_op jit(solution)/shard_map/ppermute | solution.py:385
  45.3 17.1 %collective-permute-start.14 = (bf16[512,512]{1,0:T(8,128)(2,1)S(1)}, bf16[512,512]{1,0:T(8,128)(2,1)S(1)}, u32[]{:S(2)}, u32[]{:S(2)}) collective-permute-start(bf16[512,512]{1,0:T(8,128)(2,1)S(1)} %fence.8.refs_1_), channel_id=1, source_target_pairs={{0,2},{1,3},{2,0},{3,1},{4,6},{5,7},{6,4},{7,5},{8,10},{9,11},{10,... | collective-permute-start | bytes 1572872 | tf_op jit(solution)/shard_map/ppermute | solution.py:385
  45.8 16.7 %collective-permute-start.13 = (bf16[512,512]{1,0:T(8,128)(2,1)S(1)}, bf16[512,512]{1,0:T(8,128)(2,1)S(1)}, u32[]{:S(2)}, u32[]{:S(2)}) collective-permute-start(bf16[512,512]{1,0:T(8,128)(2,1)S(1)} %fence.8.refs_1_), channel_id=1, source_target_pairs={{0,1},{1,0},{2,3},{3,2},{4,5},{5,4},{6,7},{7,6},{8,9},{9,8},{10,11... | collective-permute-start | bytes 1572872 | tf_op jit(solution)/shard_map/ppermute | solution.py:385
  71.0 19.4 %collective-permute-start.18 = (bf16[544,128]{1,0:T(8,128)(2,1)S(1)}, bf16[544,128]{1,0:T(8,128)(2,1)S(1)}, u32[]{:S(2)}, u32[]{:S(2)}) collective-permute-start(bf16[544,128]{1,0:T(8,128)(2,1)S(1)} %get-tuple-element.75), channel_id=1, source_target_pairs={{0,16},{4,20},{8,24},{12,28},{16,0},{20,4},{24,8},{28,12},{1,17},{... | collective-permute-start | bytes 417800 | tf_op jit(solution)/shard_map/ppermute | solution.py:392
  80.0 12.5 %collective-permute-start.19 = (bf16[544,128]{1,0:T(8,128)(2,1)S(1)}, bf16[544,128]{1,0:T(8,128)(2,1)S(1)}, u32[]{:S(2)}, u32[]{:S(2)}) collective-permute-start(bf16[544,128]{1,0:T(8,128)(2,1)S(1)} %get-tuple-element.76), channel_id=1, source_target_pairs={{0,20},{4,16},{8,28},{12,24},{16,4},{20,0},{24,12},{28,8},{1,21},{... | collective-permute-start | bytes 417800 | tf_op jit(solution)/shard_map/ppermute | solution.py:392
  80.0 12.5 %collective-permute-start.20 = (bf16[544,128]{1,0:T(8,128)(2,1)S(1)}, bf16[544,128]{1,0:T(8,128)(2,1)S(1)}, u32[]{:S(2)}, u32[]{:S(2)}) collective-permute-start(bf16[544,128]{1,0:T(8,128)(2,1)S(1)} %get-tuple-element.77), channel_id=1, source_target_pairs={{0,4},{4,0},{8,12},{12,8},{16,20},{20,16},{24,28},{28,24},{1,5},{5... | collective-permute-start | bytes 417800 | tf_op jit(solution)/shard_map/ppermute | solution.py:392
  81.5 11.6 %collective-permute-start.21 = (bf16[544,128]{1,0:T(8,128)(2,1)S(1)}, bf16[544,128]{1,0:T(8,128)(2,1)S(1)}, u32[]{:S(2)}, u32[]{:S(2)}) collective-permute-start(bf16[544,128]{1,0:T(8,128)(2,1)S(1)} %get-tuple-element.78), channel_id=1, source_target_pairs={{0,8},{4,12},{8,0},{12,4},{16,24},{20,28},{24,16},{28,20},{1,9},{5... | collective-permute-start | bytes 417800 | tf_op jit(solution)/shard_map/ppermute | solution.py:392
  83.2 11.6 %collective-permute-start.22 = (bf16[544,128]{1,0:T(8,128)(2,1)S(1)}, bf16[544,128]{1,0:T(8,128)(2,1)S(1)}, u32[]{:S(2)}, u32[]{:S(2)}) collective-permute-start(bf16[544,128]{1,0:T(8,128)(2,1)S(1)} %get-tuple-element.79), channel_id=1, source_target_pairs={{0,12},{4,8},{8,4},{12,0},{16,28},{20,24},{24,20},{28,16},{1,13},{... | collective-permute-start | bytes 417800 | tf_op jit(solution)/shard_map/ppermute | solution.py:392
  97.0 8.4 %collective-permute-start.25 = (bf16[544,128]{1,0:T(8,128)(2,1)S(1)}, bf16[544,128]{1,0:T(8,128)(2,1)S(1)}, u32[]{:S(2)}, u32[]{:S(2)}) collective-permute-start(bf16[544,128]{1,0:T(8,128)(2,1)S(1)} %get-tuple-element.85), channel_id=1, source_target_pairs={{0,24},{4,28},{8,16},{12,20},{16,8},{20,12},{24,0},{28,4},{1,25},{... | collective-permute-start | bytes 417800 | tf_op jit(solution)/shard_map/ppermute | solution.py:392
  97.3 11.5 %collective-permute-start.26 = (bf16[544,128]{1,0:T(8,128)(2,1)S(1)}, bf16[544,128]{1,0:T(8,128)(2,1)S(1)}, u32[]{:S(2)}, u32[]{:S(2)}) collective-permute-start(bf16[544,128]{1,0:T(8,128)(2,1)S(1)} %get-tuple-element.86), channel_id=1, source_target_pairs={{0,28},{4,24},{8,20},{12,16},{16,12},{20,8},{24,4},{28,0},{1,29},{... | collective-permute-start | bytes 417800 | tf_op jit(solution)/shard_map/ppermute | solution.py:392
  104.1 25.0 %collective-permute-start.24 = (bf16[192,2048]{1,0:T(8,128)(2,1)S(1)}, bf16[192,2048]{1,0:T(8,128)(2,1)S(1)}, u32[]{:S(2)}, u32[]{:S(2)}) collective-permute-start(bf16[192,2048]{1,0:T(8,128)(2,1)S(1)} %get-tuple-element.84), channel_id=1, source_target_pairs={{0,2},{1,3},{2,0},{3,1},{4,6},{5,7},{6,4},{7,5},{8,10},{9,11},{10,... | collective-permute-start | bytes 2359304 | tf_op jit(solution)/shard_map/ppermute | solution.py:385
  112.7 16.4 %collective-permute-start.28 = (bf16[64,2048]{1,0:T(8,128)(2,1)S(1)}, bf16[64,2048]{1,0:T(8,128)(2,1)S(1)}, u32[]{:S(2)}, u32[]{:S(2)}) collective-permute-start(bf16[64,2048]{1,0:T(8,128)(2,1)S(1)} %get-tuple-element.90), channel_id=1, source_target_pairs={{0,2},{1,3},{2,0},{3,1},{4,6},{5,7},{6,4},{7,5},{8,10},{9,11},{10,... | collective-permute-start | bytes 786440 | tf_op jit(solution)/shard_map/ppermute | solution.py:385
  (9 other events, 48.3 us)

commit v10 on v9

--- a/solution.py
+++ b/solution.py
@@ -430,9 +430,9 @@
     first_pieces = (first, first_core, first_across, swap(first_across, 1))
     second = fence(classes[1], first_across)
     second_core, second_across = swap(second, 1), swap(second, 2)
-    locals_ = local_part(pos, q, k, v, halo, owners, ())
-    columns = column_part(pos, first_pieces, weights, (), owners, (locals_[0][0],))
-    second_across = fence(second_across, columns[0])
+    columns = column_part(pos, first_pieces, weights, (), owners, ())
+    locals_ = local_part(pos, q, k, v, halo, owners, (columns[0],))
+    second_across = fence(second_across, locals_[0][0])
     second_pieces = (second, second_core, second_across, swap(second_across, 1))
     columns = column_part(pos, second_pieces, weights, columns, owners, ())
     columns = exchange(columns)

time: 131 us -> 134 us (1.023)
  waiting for transfers between devices: 51.6 us -> 54.8 us
    ppermute x14, waiting for transfers between devices: 20.7 us -> 23.5 us  [swap(): return lax.ppermute(value, 'head', [(i, i ^ distance) for i in range(4)])]
  transfers between devices with their start and end apart: 29 -> 29, of which waited for: 14 -> 14; matrix products, arithmetic and copies ran while one was open for 0% -> 0% of each run, Pallas kernels for 21% -> 20%
where the time goes in v10:
time: 134 us
  waiting for transfers between devices  54.8 us (41%)
  starting transfers between devices  40.1 us (30%)
  Pallas kernels  37.3 us (28%)
    pallas_call x10, Pallas kernels, call(): pl.pallas_call(run, in_specs=specs + [ANYWHERE] * extra, out_specs=jax.tr...  34.2 us
    ppermute x14, starting transfers between devices, move(): lax.ppermute(value, 'seq', [(i, i ^ k) for i in range(peers)])  31.5 us
    ppermute x14, waiting for transfers between devices, move(): lax.ppermute(value, 'seq', [(i, i ^ k) for i in range(peers)])  26.8 us
    ppermute x14, waiting for transfers between devices, swap(): return lax.ppermute(value, 'head', [(i, i ^ distance) for i in range(4)])  23.5 us
    ppermute x14, starting transfers between devices, swap(): return lax.ppermute(value, 'head', [(i, i ^ distance) for i in range(4)])  6.07 us
    ppermute x1, waiting for transfers between devices, chunked(): lax.ppermute(own_halo, 'seq', [(i, i + 1) for i in range(owners - 1)])  4.6 us
  transfers between devices with their start and end apart: 29, of which 14 were waited for; matrix products, arithmetic and copies ran while one was open for 0% of the time, Pallas kernels for 20%

profile of v10, /device:TPU:0, one launch (start us, length us, event | category | flops | bytes accessed | tf_op | source)
XLA Modules:
  0.0 133.8 jit_solution(8722405582700667984)
XLA Ops:
  0.0 2.9 %collective-permute-start.8 = (bf16[1024,512]{1,0:T(8,128)(2,1)}, bf16[1024,512]{1,0:T(8,128)(2,1)S(1)}, u32[]{:S(2)}, u32[]{:S(2)}) collective-permute-start(bf16[1024,512]{1,0:T(8,128)(2,1)} %tok_hbm.1), channel_id=1, source_target_pairs={{0,2},{1,3},{2,0},{3,1},{4,6},{5,7},{6,4},{7,5},{8,10},{9,11},{10,... | collective-permute-start | bytes 3145736 | tf_op jit(solution)/shard_map/ppermute | solution.py:385
  3.0 1.9 %pack_tokens.1 = (bf16[1024,512]{1,0:T(8,128)(2,1)S(1)}, bf16[128,512]{1,0:T(8,128)(2,1)S(1)}, bf16[128,512]{1,0:T(8,128)(2,1)S(1)}, bf16[128,512]{1,0:T(8,128)(...) custom-call(s32[3]{0:T(128)S(1)} %pad_add_fusion.pos_ref.refs_0_, ...), custom_call_target="tpu_custom_call" | custom-call | bytes 2097152 | tf_op jit(solution)/shard_map/pack_tokens/pallas_call | solution.py:112
  8.5 2.6 %collective-permute-start.3 = (bf16[128,512]{1,0:T(8,128)(2,1)S(1)}, bf16[128,512]{1,0:T(8,128)(2,1)S(1)}, u32[]{:S(2)}, u32[]{:S(2)}) collective-permute-start(bf16[128,512]{1,0:T(8,128)(2,1)S(1)} %get-tuple-element.53), channel_id=1, source_target_pairs={{0,16},{4,20},{8,24},{12,28},{16,0},{20,4},{24,8},{28,12},{1,17},{... | collective-permute-start | bytes 393224 | tf_op jit(solution)/shard_map/ppermute | solution.py:392
  11.2 2.9 %collective-permute-start.4 = (bf16[128,512]{1,0:T(8,128)(2,1)S(1)}, bf16[128,512]{1,0:T(8,128)(2,1)S(1)}, u32[]{:S(2)}, u32[]{:S(2)}) collective-permute-start(bf16[128,512]{1,0:T(8,128)(2,1)S(1)} %get-tuple-element.54), channel_id=1, source_target_pairs={{0,20},{4,16},{8,28},{12,24},{16,4},{20,0},{24,12},{28,8},{1,21},{... | collective-permute-start | bytes 393224 | tf_op jit(solution)/shard_map/ppermute | solution.py:392
  14.1 2.2 %collective-permute-done.1 = bf16[128,512]{1,0:T(8,128)(2,1)S(1)} collective-permute-done((bf16[128,512]{1,0:T(8,128)(2,1)S(1)}, bf16[128,512]{1,0:T(8,128)(2,1)S(1)}, u32[]{:S(2)}, u32[]{:S(2)}) %collective-permute-start.1) | collective-permute-done | bytes 131104 | tf_op jit(solution)/shard_map/ppermute | solution.py:392
  16.3 2.4 %collective-permute-start.5 = (bf16[128,512]{1,0:T(8,128)(2,1)S(1)}, bf16[128,512]{1,0:T(8,128)(2,1)S(1)}, u32[]{:S(2)}, u32[]{:S(2)}) collective-permute-start(bf16[128,512]{1,0:T(8,128)(2,1)S(1)} %get-tuple-element.55), channel_id=1, source_target_pairs={{0,24},{4,28},{8,16},{12,20},{16,8},{20,12},{24,0},{28,4},{1,25},{... | collective-permute-start | bytes 393224 | tf_op jit(solution)/shard_map/ppermute | solution.py:392
  18.7 2.6 %collective-permute-start.6 = (bf16[128,512]{1,0:T(8,128)(2,1)S(1)}, bf16[128,512]{1,0:T(8,128)(2,1)S(1)}, u32[]{:S(2)}, u32[]{:S(2)}) collective-permute-start(bf16[128,512]{1,0:T(8,128)(2,1)S(1)} %get-tuple-element.56), channel_id=1, source_target_pairs={{0,28},{4,24},{8,20},{12,16},{16,12},{20,8},{24,4},{28,0},{1,29},{... | collective-permute-start | bytes 393224 | tf_op jit(solution)/shard_map/ppermute | solution.py:392
  21.5 9.2 %collective-permute-done.4 = bf16[128,512]{1,0:T(8,128)(2,1)S(1)} collective-permute-done((bf16[128,512]{1,0:T(8,128)(2,1)S(1)}, bf16[128,512]{1,0:T(8,128)(2,1)S(1)}, u32[]{:S(2)}, u32[]{:S(2)}) %collective-permute-start.4) | collective-permute-done | bytes 131104 | tf_op jit(solution)/shard_map/ppermute | solution.py:392
  36.2 5.6 %project_block.1 = (bf16[1024,512]{1,0:T(8,128)(2,1)S(1)}, bf16[1024,512]{1,0:T(8,128)(2,1)S(1)}, bf16[1024,512]{1,0:T(8,128)(2,1)S(1)}) custom-call(bf16[1024,512]{1,0:T(8,128)(2,1)S(1)} %get-tuple-element.48.refs_0_, bf16[1024,512]{1,0:T(8,128)(2,1)S(1)} %collective-permute-done.7.refs_1_, bf16[1024,512]{1,0:T(8,128)(2,1)S(1)} %fence.6.refs_2_, ...), custom_call_target="tpu_custom_call" | custom-call | flops 6600000000 | bytes 1048576 | tf_op jit(solution)/shard_map/project_block/pallas_call | solution.py:38
  41.8 3.4 %collective-permute-done.13.refs_0_ = bf16[512,512]{1,0:T(8,128)(2,1)S(1)} collective-permute-done((bf16[512,512]{1,0:T(8,128)(2,1)S(1)}, bf16[512,512]{1,0:T(8,128)(2,1)S(1)}, u32[]{:S(2)}, u32[]{:S(2)}) %collective-permute-start.13) | collective-permute-done | bytes 524320 | tf_op jit(solution)/shard_map/ppermute | solution.py:385
  45.3 2.5 %collective-permute-start.11 = (bf16[512,512]{1,0:T(8,128)(2,1)S(1)}, bf16[512,512]{1,0:T(8,128)(2,1)S(1)}, u32[]{:S(2)}, u32[]{:S(2)}) collective-permute-start(bf16[512,512]{1,0:T(8,128)(2,1)S(1)} %project_halo.1.refs_7_), channel_id=1, source_target_pairs={{0,4},{4,8},{8,12},{12,16},{16,20},{20,24},{24,28},{1,5},{5,9},{9,... | collective-permute-start | bytes 1572872 | tf_op jit(solution)/shard_map/ppermute | solution.py:420
  48.4 6.4 %column_part.2 = (bf16[272,128]{1,0:T(8,128)(2,1)S(1)}, bf16[272,128]{1,0:T(8,128)(2,1)S(1)}, bf16[272,128]{1,0:T(8,128)(2,1)S(1)}, bf16[272,128]{1,0:T(8,128)(2...) custom-call(s32[3]{0:T(128)S(1)} %pad_add_fusion.pos_ref.refs_0_, ...), custom_call_target="tpu_custom_call" | custom-call | flops 6600000000 | bytes 1048576 | tf_op jit(solution)/shard_map/column_part/pallas_call | solution.py:38
  54.8 4.6 %collective-permute-done.11.refs_4_ = bf16[512,512]{1,0:T(8,128)(2,1)S(1)} collective-permute-done((bf16[512,512]{1,0:T(8,128)(2,1)S(1)}, bf16[512,512]{1,0:T(8,128)(2,1)S(1)}, u32[]{:S(2)}, u32[]{:S(2)}) %collective-permute-start.11) | collective-permute-done | bytes 524320 | tf_op jit(solution)/shard_map/ppermute | solution.py:420
  59.4 5.7 %local_part.1 = (f32[8,64,512]{2,1,0:T(8,128)S(1)}, f32[8,64,512]{2,1,0:T(8,128)S(1)}, f32[64,128]{1,0:T(8,128)S(1)}, f32[64,128]{1,0:T(8,128)S(1)}) custom-call(s32[3]{0:T(128)S(1)} %pad_add_fusion.pos_ref.refs_0_, bf16[1024,512]{1,0:T(8,128)(2,1)S(1)} %get-tuple-element.60.refs_1_, bf16[1024,512]{1,0:T(8,128)(2,1)S(1)} %get-tuple-element.61.refs_2_, ...), custom_call_target="tpu_custom_call" | custom-call | flops 5500000256 | bytes 1048576 | tf_op jit(solution)/shard_map/local_part/pallas_call | solution.py:38
  65.3 1.9 %collective-permute-done.17.refs_4_ = bf16[512,512]{1,0:T(8,128)(2,1)S(1)} collective-permute-done((bf16[512,512]{1,0:T(8,128)(2,1)S(1)}, bf16[512,512]{1,0:T(8,128)(2,1)S(1)}, u32[]{:S(2)}, u32[]{:S(2)}) %collective-permute-start.17) | collective-permute-done | bytes 524320 | tf_op jit(solution)/shard_map/ppermute | solution.py:385
  67.1 6.4 %column_part.3 = (bf16[544,128]{1,0:T(8,128)(2,1)S(1)}, bf16[544,128]{1,0:T(8,128)(2,1)S(1)}, bf16[544,128]{1,0:T(8,128)(2,1)S(1)}, bf16[544,128]{1,0:T(8,128)(2...) custom-call(s32[3]{0:T(128)S(1)} %pad_add_fusion.pos_ref.refs_0_, ...), custom_call_target="tpu_custom_call" | custom-call | flops 6600000000 | bytes 1048576 | tf_op jit(solution)/shard_map/column_part/pallas_call | solution.py:38
  73.6 9.2 %collective-permute-start.18 = (bf16[544,128]{1,0:T(8,128)(2,1)S(1)}, bf16[544,128]{1,0:T(8,128)(2,1)S(1)}, u32[]{:S(2)}, u32[]{:S(2)}) collective-permute-start(bf16[544,128]{1,0:T(8,128)(2,1)S(1)} %get-tuple-element.75), channel_id=1, source_target_pairs={{0,16},{4,20},{8,24},{12,28},{16,0},{20,4},{24,8},{28,12},{1,17},{... | collective-permute-start | bytes 417800 | tf_op jit(solution)/shard_map/ppermute | solution.py:392
  86.3 6.9 %collective-permute-done.18.refs_5_ = bf16[544,128]{1,0:T(8,128)(2,1)S(1)} collective-permute-done((bf16[544,128]{1,0:T(8,128)(2,1)S(1)}, bf16[544,128]{1,0:T(8,128)(2,1)S(1)}, u32[]{:S(2)}, u32[]{:S(2)}) %collective-permute-start.18) | collective-permute-done | bytes 139296 | tf_op jit(solution)/shard_map/ppermute | solution.py:392
  93.2 2.0 %collective-permute-done.19.refs_6_ = bf16[544,128]{1,0:T(8,128)(2,1)S(1)} collective-permute-done((bf16[544,128]{1,0:T(8,128)(2,1)S(1)}, bf16[544,128]{1,0:T(8,128)(2,1)S(1)}, u32[]{:S(2)}, u32[]{:S(2)}) %collective-permute-start.19) | collective-permute-done | bytes 139296 | tf_op jit(solution)/shard_map/ppermute | solution.py:392
  97.5 2.3 %mix.2 = (bf16[2,192,512]{2,1,0:T(8,128)(2,1)S(1)}, bf16[2,192,512]{2,1,0:T(8,128)(2,1)S(1)}) custom-call(s32[3]{0:T(128)S(1)} %pad_add_fusion.pos_ref.refs_0_, f32[8,64,512]{2,1,0:T(8,128)S(1)} %get-tuple-element.64.refs_1_, f32[64,128]{1,0:T(8,128)S(1)} %get-tuple-element.65.refs_2_, f32[8,64,512]{2,1,0:T(8,128)S(1)} %get-tuple-element.66.refs_3_, ...), custom_call_target="tpu_custom_call" | custom-call | flops 2200000000 | bytes 1048576 | tf_op jit(solution)/shard_map/mix/pallas_call | solution.py:38
  100.3 4.4 %collective-permute-start.26 = (bf16[544,128]{1,0:T(8,128)(2,1)S(1)}, bf16[544,128]{1,0:T(8,128)(2,1)S(1)}, u32[]{:S(2)}, u32[]{:S(2)}) collective-permute-start(bf16[544,128]{1,0:T(8,128)(2,1)S(1)} %get-tuple-element.86), channel_id=1, source_target_pairs={{0,28},{4,24},{8,20},{12,16},{16,12},{20,8},{24,4},{28,0},{1,29},{... | collective-permute-start | bytes 417800 | tf_op jit(solution)/shard_map/ppermute | solution.py:392
  104.7 2.4 %out_project.2 = (bf16[192,2048]{1,0:T(8,128)(2,1)S(1)}, f32[192,2048]{1,0:T(8,128)S(1)}) custom-call(s32[3]{0:T(128)S(1)} %pad_add_fusion.pos_ref.refs_0_, bf16[2,192,512]{2,1,0:T(8,128)(2,1)S(1)} %get-tuple-element.81.refs_1_, bf16[2,192,512]{2,1,0:T(8,128)(2,1)S(1)} %collective-permute-done.23.refs_2_, bf16[512,2048]{1,0:T(8,128)(2,1)S(1)} %copy-done.3, ...), custom_call_target="tpu_custom_call" | custom-call | flops 2200000000 | bytes 1048576 | tf_op jit(solution)/shard_map/out_project/pallas_call | solution.py:38
  108.4 3.4 %collective-permute-done.26.refs_6_ = bf16[544,128]{1,0:T(8,128)(2,1)S(1)} collective-permute-done((bf16[544,128]{1,0:T(8,128)(2,1)S(1)}, bf16[544,128]{1,0:T(8,128)(2,1)S(1)}, u32[]{:S(2)}, u32[]{:S(2)}) %collective-permute-start.26) | collective-permute-done | bytes 139296 | tf_op jit(solution)/shard_map/ppermute | solution.py:392
  116.2 15.9 %collective-permute-done.28.refs_4_ = bf16[64,2048]{1,0:T(8,128)(2,1)S(1)} collective-permute-done((bf16[64,2048]{1,0:T(8,128)(2,1)S(1)}, bf16[64,2048]{1,0:T(8,128)(2,1)S(1)}, u32[]{:S(2)}, u32[]{:S(2)}) %collective-permute-start.28) | collective-permute-done | bytes 262176 | tf_op jit(solution)/shard_map/ppermute | solution.py:385
  (70 shorter events, 23.6 us)
Async XLA Ops:
  0.0 30.8 %collective-permute-start.8 = (bf16[1024,512]{1,0:T(8,128)(2,1)}, bf16[1024,512]{1,0:T(8,128)(2,1)S(1)}, u32[]{:S(2)}, u32[]{:S(2)}) collective-permute-start(bf16[1024,512]{1,0:T(8,128)(2,1)} %tok_hbm.1), channel_id=1, source_target_pairs={{0,2},{1,3},{2,0},{3,1},{4,6},{5,7},{6,4},{7,5},{8,10},{9,11},{10,... | collective-permute-start | bytes 3145736 | tf_op jit(solution)/shard_map/ppermute | solution.py:385
  4.9 6.2 %collective-permute-start = (bf16[128,512]{1,0:T(8,128)(2,1)S(1)}, bf16[128,512]{1,0:T(8,128)(2,1)S(1)}, u32[]{:S(2)}, u32[]{:S(2)}) collective-permute-start(bf16[128,512]{1,0:T(8,128)(2,1)S(1)} %get-tuple-element.50), channel_id=1, source_target_pairs={{0,4},{4,0},{8,12},{12,8},{16,20},{20,16},{24,28},{28,24},{1,5},{5... | collective-permute-start | bytes 393224 | tf_op jit(solution)/shard_map/ppermute | solution.py:392
  6.5 9.8 %collective-permute-start.1 = (bf16[128,512]{1,0:T(8,128)(2,1)S(1)}, bf16[128,512]{1,0:T(8,128)(2,1)S(1)}, u32[]{:S(2)}, u32[]{:S(2)}) collective-permute-start(bf16[128,512]{1,0:T(8,128)(2,1)S(1)} %get-tuple-element.51), channel_id=1, source_target_pairs={{0,8},{4,12},{8,0},{12,4},{16,24},{20,28},{24,16},{28,20},{1,9},{5... | collective-permute-start | bytes 393224 | tf_op jit(solution)/shard_map/ppermute | solution.py:392
  8.1 10.6 %collective-permute-start.2 = (bf16[128,512]{1,0:T(8,128)(2,1)S(1)}, bf16[128,512]{1,0:T(8,128)(2,1)S(1)}, u32[]{:S(2)}, u32[]{:S(2)}) collective-permute-start(bf16[128,512]{1,0:T(8,128)(2,1)S(1)} %get-tuple-element.52), channel_id=1, source_target_pairs={{0,12},{4,8},{8,4},{12,0},{16,28},{20,24},{24,20},{28,16},{1,13},{... | collective-permute-start | bytes 393224 | tf_op jit(solution)/shard_map/ppermute | solution.py:392
  8.5 12.8 %collective-permute-start.3 = (bf16[128,512]{1,0:T(8,128)(2,1)S(1)}, bf16[128,512]{1,0:T(8,128)(2,1)S(1)}, u32[]{:S(2)}, u32[]{:S(2)}) collective-permute-start(bf16[128,512]{1,0:T(8,128)(2,1)S(1)} %get-tuple-element.53), channel_id=1, source_target_pairs={{0,16},{4,20},{8,24},{12,28},{16,0},{20,4},{24,8},{28,12},{1,17},{... | collective-permute-start | bytes 393224 | tf_op jit(solution)/shard_map/ppermute | solution.py:392
  11.2 19.5 %collective-permute-start.4 = (bf16[128,512]{1,0:T(8,128)(2,1)S(1)}, bf16[128,512]{1,0:T(8,128)(2,1)S(1)}, u32[]{:S(2)}, u32[]{:S(2)}) collective-permute-start(bf16[128,512]{1,0:T(8,128)(2,1)S(1)} %get-tuple-element.54), channel_id=1, source_target_pairs={{0,20},{4,16},{8,28},{12,24},{16,4},{20,0},{24,12},{28,8},{1,21},{... | collective-permute-start | bytes 393224 | tf_op jit(solution)/shard_map/ppermute | solution.py:392
  16.3 14.4 %collective-permute-start.5 = (bf16[128,512]{1,0:T(8,128)(2,1)S(1)}, bf16[128,512]{1,0:T(8,128)(2,1)S(1)}, u32[]{:S(2)}, u32[]{:S(2)}) collective-permute-start(bf16[128,512]{1,0:T(8,128)(2,1)S(1)} %get-tuple-element.55), channel_id=1, source_target_pairs={{0,24},{4,28},{8,16},{12,20},{16,8},{20,12},{24,0},{28,4},{1,25},{... | collective-permute-start | bytes 393224 | tf_op jit(solution)/shard_map/ppermute | solution.py:392
  18.7 12.0 %collective-permute-start.6 = (bf16[128,512]{1,0:T(8,128)(2,1)S(1)}, bf16[128,512]{1,0:T(8,128)(2,1)S(1)}, u32[]{:S(2)}, u32[]{:S(2)}) collective-permute-start(bf16[128,512]{1,0:T(8,128)(2,1)S(1)} %get-tuple-element.56), channel_id=1, source_target_pairs={{0,28},{4,24},{8,20},{12,16},{16,12},{20,8},{24,4},{28,0},{1,29},{... | collective-permute-start | bytes 393224 | tf_op jit(solution)/shard_map/ppermute | solution.py:392
  21.3 14.9 %collective-permute-start.10 = (bf16[512,2048]{1,0:T(8,128)(2,1)S(1)}, bf16[512,2048]{1,0:T(8,128)(2,1)S(1)}, u32[]{:S(2)}, u32[]{:S(2)}) collective-permute-start(bf16[512,2048]{1,0:T(8,128)(2,1)S(1)} %copy-done.3), channel_id=1, source_target_pairs={{0,1},{1,0},{2,3},{3,2},{4,5},{5,4},{6,7},{7,6},{8,9},{9,8},{10,11... | collective-permute-start | bytes 6291464 | tf_op jit(solution)/shard_map/ppermute | solution.py:385
  31.3 13.9 %collective-permute-start.13 = (bf16[512,512]{1,0:T(8,128)(2,1)S(1)}, bf16[512,512]{1,0:T(8,128)(2,1)S(1)}, u32[]{:S(2)}, u32[]{:S(2)}) collective-permute-start(bf16[512,512]{1,0:T(8,128)(2,1)S(1)} %get-tuple-element.92.refs_1_), channel_id=1, source_target_pairs={{0,2},{1,3},{2,0},{3,1},{4,6},{5,7},{6,4},{7,5},{8,10},{9,11},{10,... | collective-permute-start | bytes 1572872 | tf_op jit(solution)/shard_map/ppermute | solution.py:385
  31.9 16.5 %collective-permute-start.12 = (bf16[512,512]{1,0:T(8,128)(2,1)S(1)}, bf16[512,512]{1,0:T(8,128)(2,1)S(1)}, u32[]{:S(2)}, u32[]{:S(2)}) collective-permute-start(bf16[512,512]{1,0:T(8,128)(2,1)S(1)} %get-tuple-element.92.refs_1_), channel_id=1, source_target_pairs={{0,1},{1,0},{2,3},{3,2},{4,5},{5,4},{6,7},{7,6},{8,9},{9,8},{10,11... | collective-permute-start | bytes 1572872 | tf_op jit(solution)/shard_map/ppermute | solution.py:385
  45.3 14.1 %collective-permute-start.11 = (bf16[512,512]{1,0:T(8,128)(2,1)S(1)}, bf16[512,512]{1,0:T(8,128)(2,1)S(1)}, u32[]{:S(2)}, u32[]{:S(2)}) collective-permute-start(bf16[512,512]{1,0:T(8,128)(2,1)S(1)} %project_halo.1.refs_7_), channel_id=1, source_target_pairs={{0,4},{4,8},{8,12},{12,16},{16,20},{20,24},{24,28},{1,5},{5,9},{9,... | collective-permute-start | bytes 1572872 | tf_op jit(solution)/shard_map/ppermute | solution.py:420
  47.8 17.4 %collective-permute-start.16 = (bf16[512,512]{1,0:T(8,128)(2,1)S(1)}, bf16[512,512]{1,0:T(8,128)(2,1)S(1)}, u32[]{:S(2)}, u32[]{:S(2)}) collective-permute-start(bf16[512,512]{1,0:T(8,128)(2,1)S(1)} %fence.8.refs_1_), channel_id=1, source_target_pairs={{0,2},{1,3},{2,0},{3,1},{4,6},{5,7},{6,4},{7,5},{8,10},{9,11},{10,... | collective-permute-start | bytes 1572872 | tf_op jit(solution)/shard_map/ppermute | solution.py:385
  48.4 16.9 %collective-permute-start.15 = (bf16[512,512]{1,0:T(8,128)(2,1)S(1)}, bf16[512,512]{1,0:T(8,128)(2,1)S(1)}, u32[]{:S(2)}, u32[]{:S(2)}) collective-permute-start(bf16[512,512]{1,0:T(8,128)(2,1)S(1)} %fence.8.refs_1_), channel_id=1, source_target_pairs={{0,1},{1,0},{2,3},{3,2},{4,5},{5,4},{6,7},{7,6},{8,9},{9,8},{10,11... | collective-permute-start | bytes 1572872 | tf_op jit(solution)/shard_map/ppermute | solution.py:385
  73.6 19.6 %collective-permute-start.18 = (bf16[544,128]{1,0:T(8,128)(2,1)S(1)}, bf16[544,128]{1,0:T(8,128)(2,1)S(1)}, u32[]{:S(2)}, u32[]{:S(2)}) collective-permute-start(bf16[544,128]{1,0:T(8,128)(2,1)S(1)} %get-tuple-element.75), channel_id=1, source_target_pairs={{0,16},{4,20},{8,24},{12,28},{16,0},{20,4},{24,8},{28,12},{1,17},{... | collective-permute-start | bytes 417800 | tf_op jit(solution)/shard_map/ppermute | solution.py:392
  82.8 12.4 %collective-permute-start.19 = (bf16[544,128]{1,0:T(8,128)(2,1)S(1)}, bf16[544,128]{1,0:T(8,128)(2,1)S(1)}, u32[]{:S(2)}, u32[]{:S(2)}) collective-permute-start(bf16[544,128]{1,0:T(8,128)(2,1)S(1)} %get-tuple-element.76), channel_id=1, source_target_pairs={{0,20},{4,16},{8,28},{12,24},{16,4},{20,0},{24,12},{28,8},{1,21},{... | collective-permute-start | bytes 417800 | tf_op jit(solution)/shard_map/ppermute | solution.py:392
  82.8 12.4 %collective-permute-start.20 = (bf16[544,128]{1,0:T(8,128)(2,1)S(1)}, bf16[544,128]{1,0:T(8,128)(2,1)S(1)}, u32[]{:S(2)}, u32[]{:S(2)}) collective-permute-start(bf16[544,128]{1,0:T(8,128)(2,1)S(1)} %get-tuple-element.77), channel_id=1, source_target_pairs={{0,4},{4,0},{8,12},{12,8},{16,20},{20,16},{24,28},{28,24},{1,5},{5... | collective-permute-start | bytes 417800 | tf_op jit(solution)/shard_map/ppermute | solution.py:392
  84.3 11.6 %collective-permute-start.21 = (bf16[544,128]{1,0:T(8,128)(2,1)S(1)}, bf16[544,128]{1,0:T(8,128)(2,1)S(1)}, u32[]{:S(2)}, u32[]{:S(2)}) collective-permute-start(bf16[544,128]{1,0:T(8,128)(2,1)S(1)} %get-tuple-element.78), channel_id=1, source_target_pairs={{0,8},{4,12},{8,0},{12,4},{16,24},{20,28},{24,16},{28,20},{1,9},{5... | collective-permute-start | bytes 417800 | tf_op jit(solution)/shard_map/ppermute | solution.py:392
  85.9 11.6 %collective-permute-start.22 = (bf16[544,128]{1,0:T(8,128)(2,1)S(1)}, bf16[544,128]{1,0:T(8,128)(2,1)S(1)}, u32[]{:S(2)}, u32[]{:S(2)}) collective-permute-start(bf16[544,128]{1,0:T(8,128)(2,1)S(1)} %get-tuple-element.79), channel_id=1, source_target_pairs={{0,12},{4,8},{8,4},{12,0},{16,28},{20,24},{24,20},{28,16},{1,13},{... | collective-permute-start | bytes 417800 | tf_op jit(solution)/shard_map/ppermute | solution.py:392
  99.9 4.8 %collective-permute-start.23 = (bf16[2,192,512]{2,1,0:T(8,128)(2,1)S(1)}, bf16[2,192,512]{2,1,0:T(8,128)(2,1)S(1)}, u32[]{:S(2)}, u32[]{:S(2)}) collective-permute-start(bf16[2,192,512]{2,1,0:T(8,128)(2,1)S(1)} %get-tuple-element.82), channel_id=1, source_target_pairs={{0,1},{1,0},{2,3},{3,2},{4,5},{5,4},{6,7},{7,6},{8,9},{9,8},{10,11... | collective-permute-start | bytes 1179656 | tf_op jit(solution)/shard_map/ppermute | solution.py:385
  99.9 8.4 %collective-permute-start.25 = (bf16[544,128]{1,0:T(8,128)(2,1)S(1)}, bf16[544,128]{1,0:T(8,128)(2,1)S(1)}, u32[]{:S(2)}, u32[]{:S(2)}) collective-permute-start(bf16[544,128]{1,0:T(8,128)(2,1)S(1)} %get-tuple-element.85), channel_id=1, source_target_pairs={{0,24},{4,28},{8,16},{12,20},{16,8},{20,12},{24,0},{28,4},{1,25},{... | collective-permute-start | bytes 417800 | tf_op jit(solution)/shard_map/ppermute | solution.py:392
  100.3 11.5 %collective-permute-start.26 = (bf16[544,128]{1,0:T(8,128)(2,1)S(1)}, bf16[544,128]{1,0:T(8,128)(2,1)S(1)}, u32[]{:S(2)}, u32[]{:S(2)}) collective-permute-start(bf16[544,128]{1,0:T(8,128)(2,1)S(1)} %get-tuple-element.86), channel_id=1, source_target_pairs={{0,28},{4,24},{8,20},{12,16},{16,12},{20,8},{24,4},{28,0},{1,29},{... | collective-permute-start | bytes 417800 | tf_op jit(solution)/shard_map/ppermute | solution.py:392
  107.1 25.0 %collective-permute-start.24 = (bf16[192,2048]{1,0:T(8,128)(2,1)S(1)}, bf16[192,2048]{1,0:T(8,128)(2,1)S(1)}, u32[]{:S(2)}, u32[]{:S(2)}) collective-permute-start(bf16[192,2048]{1,0:T(8,128)(2,1)S(1)} %get-tuple-element.84), channel_id=1, source_target_pairs={{0,2},{1,3},{2,0},{3,1},{4,6},{5,7},{6,4},{7,5},{8,10},{9,11},{10,... | collective-permute-start | bytes 2359304 | tf_op jit(solution)/shard_map/ppermute | solution.py:385
  115.7 16.4 %collective-permute-start.28 = (bf16[64,2048]{1,0:T(8,128)(2,1)S(1)}, bf16[64,2048]{1,0:T(8,128)(2,1)S(1)}, u32[]{:S(2)}, u32[]{:S(2)}) collective-permute-start(bf16[64,2048]{1,0:T(8,128)(2,1)S(1)} %get-tuple-element.90), channel_id=1, source_target_pairs={{0,2},{1,3},{2,0},{3,1},{4,6},{5,7},{6,4},{7,5},{8,10},{9,11},{10,... | collective-permute-start | bytes 786440 | tf_op jit(solution)/shard_map/ppermute | solution.py:385
  (9 other events, 46.5 us)

commit v11 on v10

--- a/solution.py
+++ b/solution.py
@@ -12,7 +12,7 @@
 HEADS = 4
 ROWS = 4
 SUB = 8
-CHUNKS = 2
+CHUNKS = ((0, 1, 2), (3,))
 PEERS = 8
 SHARES = ((4, 5, 1, 2, 3, 0), (6, 7))
 SCALE2 = DH ** (-0.5) * 1.4426950408889634
@@ -186,9 +186,9 @@
 
 
 def local_kernel(pos_ref, q_ref, k_ref, v_ref, halo_ref, *outs):
-    out_refs, lse_refs = outs[:CHUNKS], outs[CHUNKS:]
-    owners, message, _ = out_refs[0].shape
-    groups = message // ROWS // SUB
+    out_refs, lse_refs = outs[: len(CHUNKS)], outs[len(CHUNKS) :]
+    owners = out_refs[0].shape[0]
+    groups = STRIDE // owners // SUB
     block = pos_ref[0]
     u = lax.broadcasted_iota(jnp.int32, (STRIDE, STRIDE), 0)
     t = lax.broadcasted_iota(jnp.int32, (STRIDE, STRIDE), 1)
@@ -213,30 +213,30 @@
             o = (o * (1.0 / total)).T
             lses.append(lse)
             for d in range(owners):
-                for i in range(CHUNKS):
-                    for g in range(groups):
-                        at = ((d * CHUNKS + i) * groups + g) * SUB
-                        to = (g * ROWS + r) * SUB
-                        out_refs[i][d, to : to + SUB, cols] = o[at : at + SUB]
+                for chunk, out_ref in zip(CHUNKS, out_refs):
+                    for n, g in enumerate(chunk):
+                        at = (d * groups + g) * SUB
+                        to = (n * ROWS + r) * SUB
+                        out_ref[d, to : to + SUB, cols] = o[at : at + SUB]
         lses.append(jnp.zeros((128 - HEADS, STRIDE), F32))
         turned = jnp.concatenate(lses, 0).T
-        for i in range(CHUNKS):
-            for g in range(groups):
+        for chunk, lse_ref in zip(CHUNKS, lse_refs):
+            for n, g in enumerate(chunk):
                 total = None
                 for d in range(owners):
-                    at = ((d * CHUNKS + i) * groups + g) * SUB
+                    at = (d * groups + g) * SUB
                     moved = pltpu.roll(turned[at : at + SUB], 8 * (block ^ d), 1)
                     total = moved if total is None else total + moved
-                to = (g * ROWS + r) * SUB
-                lse_refs[i][to : to + SUB, :] = total
+                to = (n * ROWS + r) * SUB
+                lse_ref[to : to + SUB, :] = total
 
 
 def local_part(pos, q, k, v, halo, owners, after):
     rows, width = q.shape
-    message = rows // owners // CHUNKS
-    shapes = [shape((owners, message, width), F32)] * CHUNKS + [shape((message, 128), F32)] * CHUNKS
+    sizes = [len(chunk) * ROWS * SUB for chunk in CHUNKS]
+    shapes = [shape((owners, m, width), F32) for m in sizes] + [shape((m, 128), F32) for m in sizes]
     outs = call(local_kernel, "local_part", 5, shapes, (pos, q, k, v, halo), after)
-    return list(zip(outs[:CHUNKS], outs[CHUNKS:]))
+    return list(zip(outs[: len(sizes)], outs[len(sizes) :]))
 
 
 def column_kernel(pos_ref, x0, x1, x2, x3, wq, wk, wv, *rest):
@@ -293,20 +293,18 @@
     rows = HEADS * message + 16 + (earlier[0].shape[0] if earlier else 0)
     scratch = [pltpu.VMEM((owners, message, width), BF16)] * 3
     args = (pos, *pieces, *weights, *earlier)
-    return call(column_kernel, "column_part", 6, [shape((rows, DH))] * owners, args, after, scratch)
+    return call(column_kernel, "column_part", 0, [shape((rows, DH))] * owners, args, after, scratch)
 
 
 def mix_kernel(share, pos_ref, *refs):
-    local_refs, refs = refs[: 2 * CHUNKS], refs[2 * CHUNKS :]
-    col_refs, (own_ref, send_ref, mixed) = refs[:-3], refs[-3:]
-    message = local_refs[0].shape[1]
-    groups = message // (ROWS * SUB)
-    size = HEADS * message + 16
-    span = groups * SUB
-    for i in range(CHUNKS):
-        loc_ref, lse_ref = local_refs[2 * i : 2 * i + 2]
+    count = 2 * len(CHUNKS)
+    local_refs, col_refs, (own_ref, send_ref, mixed) = refs[:count], refs[count:-3], refs[-3:]
+    per_owner = mixed.shape[1] // len(share)
+    base = 0
+    for chunk, loc_ref, lse_ref in zip(CHUNKS, local_refs[::2], local_refs[1::2]):
+        message = loc_ref.shape[1]
+        size = HEADS * message + 16
         tiles = [jnp.zeros((8, 128), F32)] * 16
-        base = i * size
         for k, col_ref in zip(share, col_refs):
             tail = col_ref[base + HEADS * message : base + size, :].astype(F32)
             tiles[k] = tail[:8] + tail[8:]
@@ -321,27 +319,28 @@
         w_loc = w_loc * scale
         for n, (k, col_ref) in enumerate(zip(share, col_refs)):
             d = pos_ref[0] ^ k
-            to = (n * CHUNKS + i) * span
             for h in range(HEADS):
                 cols = slice(h * DH, (h + 1) * DH)
                 at = slice(8 * k + h, 8 * k + h + 1)
                 col = col_ref[base + h * message : base + (h + 1) * message, :].astype(F32)
                 both = loc_ref[d, :, cols] * w_loc[:, at] + col * w_col[:, at]
                 for r in range(ROWS):
-                    starts = [(g * ROWS + r) * SUB for g in range(groups)]
-                    piece = jnp.concatenate([both[s : s + SUB] for s in starts], 0)
-                    mixed[r, to : to + span, cols] = piece.astype(BF16)
+                    for m, g in enumerate(chunk):
+                        start = (m * ROWS + r) * SUB
+                        to = n * per_owner + g * SUB
+                        mixed[r, to : to + SUB, cols] = both[start : start + SUB]
+        base += size
     core = pos_ref[1]
     for x in range(2):
-        own_ref[x] = mixed[2 * x + core]
-        send_ref[x] = mixed[2 * x + 1 - core]
+        own_ref[x] = mixed[2 * x + core].astype(BF16)
+        send_ref[x] = mixed[2 * x + 1 - core].astype(BF16)
 
 
 def mix(pos, share, columns, locals_, after):
-    owners, message, width = locals_[0][0].shape
-    tokens = len(share) * CHUNKS * message // ROWS
+    owners, _, width = locals_[0][0].shape
+    tokens = len(share) * STRIDE // owners
     shapes = [shape((2, tokens, width))] * 2
-    scratch = [pltpu.VMEM((ROWS, tokens, width), BF16)]
+    scratch = [pltpu.VMEM((ROWS, tokens, width), F32)]
     args = (pos, *[x for pair in locals_ for x in pair], *columns)
     return call(functools.partial(mix_kernel, share), "mix", 2, shapes, args, after, scratch)
 
@@ -405,18 +404,20 @@
     across = swap(tokens, 2)
     block_tokens, sent = pack(pos, tokens, owners)
     messages = exchange(sent)
-    part = rows // owners // CHUNKS
+    part = ROWS * SUB
     classes = [
-        jnp.concatenate([m[i * part : (i + 1) * part] for m in messages], 0) for i in range(CHUNKS)
+        jnp.concatenate([m[chunk[0] * part : (chunk[-1] + 1) * part] for m in messages], 0)
+        for chunk in CHUNKS
     ]
     across = fence(across, classes[0])
     pieces = (block_tokens, swap(fence(block_tokens, classes[0]), 1), across, swap(across, 1))
-    first, first_core, first_across = classes[0], swap(classes[0], 1), swap(classes[0], 2)
     weights = stage(order, (w_query, w_key, w_value), messages[1])
     w_other = swap(w_out, 1)
     own_halo = call(
         halo_kernel, "project_halo", 1.5, shape((2 * STRIDE, width)), (*pieces, *weights[1:])
     )
+    first = classes[0]
+    first_core, first_across = swap(first, 1), swap(first, 2)
     halo = lax.ppermute(own_halo, "seq", [(i, i + 1) for i in range(owners - 1)])
     q, k, v = call(
         project_kernel,
@@ -431,10 +432,10 @@
     second = fence(classes[1], first_across)
     second_core, second_across = swap(second, 1), swap(second, 2)
     columns = column_part(pos, first_pieces, weights, (), owners, ())
+    second_across = fence(second_across, columns[0])
+    second_pieces = (second, second_core, second_across, swap(second_across, 1))
+    columns = column_part(pos, second_pieces, weights, columns, owners, (halo,))
     locals_ = local_part(pos, q, k, v, halo, owners, (columns[0],))
-    second_across = fence(second_across, locals_[0][0])
-    second_pieces = (second, second_core, second_across, swap(second_across, 1))
-    columns = column_part(pos, second_pieces, weights, columns, owners, ())
     columns = exchange(columns)
     pairs, after = [], ()
     for share in SHARES:

time: 134 us -> 129 us (0.963)
  waiting for transfers between devices: 54.8 us -> 46.2 us
  starting transfers between devices: 40.1 us -> 42.5 us
    ppermute x14, waiting for transfers between devices: 26.8 us -> 19.3 us  [move(): lax.ppermute(value, 'seq', [(i, i ^ k) for i in range(peers)])]
    ppermute x1, waiting for transfers between devices: 4.6 us -> 1.45 us  [chunked(): lax.ppermute(own_halo, 'seq', [(i, i + 1) for i in range(owners - 1)])]
    ppermute x14, starting transfers between devices: 6.07 us -> 8.59 us  [swap(): return lax.ppermute(value, 'head', [(i, i ^ distance) for i in range(4)])]
    ppermute x14, waiting for transfers between devices: 23.5 us -> 25.5 us  [swap(): return lax.ppermute(value, 'head', [(i, i ^ distance) for i in range(4)])]
  transfers between devices with their start and end apart: 29 -> 29, of which waited for: 14 -> 12; matrix products, arithmetic and copies ran while one was open for 0% -> 0% of each run, Pallas kernels for 20% -> 23%
where the time goes in v11:
time: 129 us
  waiting for transfers between devices  46.2 us (36%)
  starting transfers between devices  42.5 us (33%)
  Pallas kernels  37.6 us (29%)
  local copies, waits for them, and re-layouts  1.83 us (1%)
    pallas_call x10, Pallas kernels, call(): pl.pallas_call(run, in_specs=specs + [ANYWHERE] * extra, out_specs=jax.tr...  34.7 us
    ppermute x14, starting transfers between devices, move(): lax.ppermute(value, 'seq', [(i, i ^ k) for i in range(peers)])  31.5 us
    ppermute x14, waiting for transfers between devices, swap(): return lax.ppermute(value, 'head', [(i, i ^ distance) for i in range(4)])  25.5 us
    ppermute x14, waiting for transfers between devices, move(): lax.ppermute(value, 'seq', [(i, i ^ k) for i in range(peers)])  19.3 us
    ppermute x14, starting transfers between devices, swap(): return lax.ppermute(value, 'head', [(i, i ^ distance) for i in range(4)])  8.59 us
  transfers between devices with their start and end apart: 29, of which 12 were waited for; matrix products, arithmetic and copies ran while one was open for 0% of the time, Pallas kernels for 23%

profile of v11, /device:TPU:0, one launch (start us, length us, event | category | flops | bytes accessed | tf_op | source)
XLA Modules:
  0.0 128.7 jit_solution(15781542685114297974)
XLA Ops:
  0.0 2.9 %collective-permute-start.8 = (bf16[1024,512]{1,0:T(8,128)(2,1)}, bf16[1024,512]{1,0:T(8,128)(2,1)S(1)}, u32[]{:S(2)}, u32[]{:S(2)}) collective-permute-start(bf16[1024,512]{1,0:T(8,128)(2,1)} %tok_hbm.1), channel_id=1, source_target_pairs={{0,2},{1,3},{2,0},{3,1},{4,6},{5,7},{6,4},{7,5},{8,10},{9,11},{10,... | collective-permute-start | bytes 3145736 | tf_op jit(solution)/shard_map/ppermute | solution.py:384
  3.0 1.8 %pack_tokens.1 = (bf16[1024,512]{1,0:T(8,128)(2,1)S(1)}, bf16[128,512]{1,0:T(8,128)(2,1)S(1)}, bf16[128,512]{1,0:T(8,128)(2,1)S(1)}, bf16[128,512]{1,0:T(8,128)(...) custom-call(s32[3]{0:T(128)S(1)} %pad_add_fusion.pos_ref.refs_0_, ...), custom_call_target="tpu_custom_call" | custom-call | bytes 2097152 | tf_op jit(solution)/shard_map/pack_tokens/pallas_call | solution.py:112
  4.9 1.6 %collective-permute-start = (bf16[128,512]{1,0:T(8,128)(2,1)S(1)}, bf16[128,512]{1,0:T(8,128)(2,1)S(1)}, u32[]{:S(2)}, u32[]{:S(2)}) collective-permute-start(bf16[128,512]{1,0:T(8,128)(2,1)S(1)} %get-tuple-element.50), channel_id=1, source_target_pairs={{0,4},{4,0},{8,12},{12,8},{16,20},{20,16},{24,28},{28,24},{1,5},{5... | collective-permute-start | bytes 393224 | tf_op jit(solution)/shard_map/ppermute | solution.py:391
  6.4 1.6 %collective-permute-start.1 = (bf16[128,512]{1,0:T(8,128)(2,1)S(1)}, bf16[128,512]{1,0:T(8,128)(2,1)S(1)}, u32[]{:S(2)}, u32[]{:S(2)}) collective-permute-start(bf16[128,512]{1,0:T(8,128)(2,1)S(1)} %get-tuple-element.51), channel_id=1, source_target_pairs={{0,8},{4,12},{8,0},{12,4},{16,24},{20,28},{24,16},{28,20},{1,9},{5... | collective-permute-start | bytes 393224 | tf_op jit(solution)/shard_map/ppermute | solution.py:391
  8.4 2.6 %collective-permute-start.3 = (bf16[128,512]{1,0:T(8,128)(2,1)S(1)}, bf16[128,512]{1,0:T(8,128)(2,1)S(1)}, u32[]{:S(2)}, u32[]{:S(2)}) collective-permute-start(bf16[128,512]{1,0:T(8,128)(2,1)S(1)} %get-tuple-element.53), channel_id=1, source_target_pairs={{0,16},{4,20},{8,24},{12,28},{16,0},{20,4},{24,8},{28,12},{1,17},{... | collective-permute-start | bytes 393224 | tf_op jit(solution)/shard_map/ppermute | solution.py:391
  11.1 2.9 %collective-permute-start.4 = (bf16[128,512]{1,0:T(8,128)(2,1)S(1)}, bf16[128,512]{1,0:T(8,128)(2,1)S(1)}, u32[]{:S(2)}, u32[]{:S(2)}) collective-permute-start(bf16[128,512]{1,0:T(8,128)(2,1)S(1)} %get-tuple-element.54), channel_id=1, source_target_pairs={{0,20},{4,16},{8,28},{12,24},{16,4},{20,0},{24,12},{28,8},{1,21},{... | collective-permute-start | bytes 393224 | tf_op jit(solution)/shard_map/ppermute | solution.py:391
  14.0 2.2 %collective-permute-done.1 = bf16[128,512]{1,0:T(8,128)(2,1)S(1)} collective-permute-done((bf16[128,512]{1,0:T(8,128)(2,1)S(1)}, bf16[128,512]{1,0:T(8,128)(2,1)S(1)}, u32[]{:S(2)}, u32[]{:S(2)}) %collective-permute-start.1) | collective-permute-done | bytes 131104 | tf_op jit(solution)/shard_map/ppermute | solution.py:391
  16.2 2.4 %collective-permute-start.5 = (bf16[128,512]{1,0:T(8,128)(2,1)S(1)}, bf16[128,512]{1,0:T(8,128)(2,1)S(1)}, u32[]{:S(2)}, u32[]{:S(2)}) collective-permute-start(bf16[128,512]{1,0:T(8,128)(2,1)S(1)} %get-tuple-element.55), channel_id=1, source_target_pairs={{0,24},{4,28},{8,16},{12,20},{16,8},{20,12},{24,0},{28,4},{1,25},{... | collective-permute-start | bytes 393224 | tf_op jit(solution)/shard_map/ppermute | solution.py:391
  18.6 2.6 %collective-permute-start.6 = (bf16[128,512]{1,0:T(8,128)(2,1)S(1)}, bf16[128,512]{1,0:T(8,128)(2,1)S(1)}, u32[]{:S(2)}, u32[]{:S(2)}) collective-permute-start(bf16[128,512]{1,0:T(8,128)(2,1)S(1)} %get-tuple-element.56), channel_id=1, source_target_pairs={{0,28},{4,24},{8,20},{12,16},{16,12},{20,8},{24,4},{28,0},{1,29},{... | collective-permute-start | bytes 393224 | tf_op jit(solution)/shard_map/ppermute | solution.py:391
  21.3 9.2 %collective-permute-done.4 = bf16[128,512]{1,0:T(8,128)(2,1)S(1)} collective-permute-done((bf16[128,512]{1,0:T(8,128)(2,1)S(1)}, bf16[128,512]{1,0:T(8,128)(2,1)S(1)}, u32[]{:S(2)}, u32[]{:S(2)}) %collective-permute-start.4) | collective-permute-done | bytes 131104 | tf_op jit(solution)/shard_map/ppermute | solution.py:391
  36.2 5.6 %project_block.1 = (bf16[1024,512]{1,0:T(8,128)(2,1)S(1)}, bf16[1024,512]{1,0:T(8,128)(2,1)S(1)}, bf16[1024,512]{1,0:T(8,128)(2,1)S(1)}) custom-call(bf16[1024,512]{1,0:T(8,128)(2,1)S(1)} %get-tuple-element.48.refs_0_, bf16[1024,512]{1,0:T(8,128)(2,1)S(1)} %collective-permute-done.7.refs_1_, bf16[1024,512]{1,0:T(8,128)(2,1)S(1)} %fence.6.refs_2_, ...), custom_call_target="tpu_custom_call" | custom-call | flops 6600000000 | bytes 1048576 | tf_op jit(solution)/shard_map/project_block/pallas_call | solution.py:38
  41.7 9.1 %collective-permute-done.12.refs_0_ = bf16[768,512]{1,0:T(8,128)(2,1)S(1)} collective-permute-done((bf16[768,512]{1,0:T(8,128)(2,1)S(1)}, bf16[768,512]{1,0:T(8,128)(2,1)S(1)}, u32[]{:S(2)}, u32[]{:S(2)}) %collective-permute-start.12) | collective-permute-done | bytes 786464 | tf_op jit(solution)/shard_map/ppermute | solution.py:384
  51.5 2.5 %collective-permute-start.11 = (bf16[512,512]{1,0:T(8,128)(2,1)S(1)}, bf16[512,512]{1,0:T(8,128)(2,1)S(1)}, u32[]{:S(2)}, u32[]{:S(2)}) collective-permute-start(bf16[512,512]{1,0:T(8,128)(2,1)S(1)} %project_halo.1.refs_7_), channel_id=1, source_target_pairs={{0,4},{4,8},{8,12},{12,16},{16,20},{20,24},{24,28},{1,5},{5,9},{9,... | collective-permute-start | bytes 1572872 | tf_op jit(solution)/shard_map/ppermute | solution.py:421
  54.1 9.2 %column_part.2 = (bf16[400,128]{1,0:T(8,128)(2,1)S(1)}, bf16[400,128]{1,0:T(8,128)(2,1)S(1)}, bf16[400,128]{1,0:T(8,128)(2,1)S(1)}, bf16[400,128]{1,0:T(8,128)(2...) custom-call(s32[3]{0:T(128)S(1)} %pad_add_fusion.pos_ref.refs_0_, ...), custom_call_target="tpu_custom_call" | custom-call | bytes 1048576 | tf_op jit(solution)/shard_map/column_part/pallas_call | solution.py:38
  65.3 3.7 %column_part.3 = (bf16[544,128]{1,0:T(8,128)(2,1)S(1)}, bf16[544,128]{1,0:T(8,128)(2,1)S(1)}, bf16[544,128]{1,0:T(8,128)(2,1)S(1)}, bf16[544,128]{1,0:T(8,128)(2...) custom-call(s32[3]{0:T(128)S(1)} %pad_add_fusion.pos_ref.refs_0_, ...), custom_call_target="tpu_custom_call" | custom-call | bytes 1048576 | tf_op jit(solution)/shard_map/column_part/pallas_call | solution.py:38
  69.0 9.2 %collective-permute-start.18 = (bf16[544,128]{1,0:T(8,128)(2,1)S(1)}, bf16[544,128]{1,0:T(8,128)(2,1)S(1)}, u32[]{:S(2)}, u32[]{:S(2)}) collective-permute-start(bf16[544,128]{1,0:T(8,128)(2,1)S(1)} %get-tuple-element.76), channel_id=1, source_target_pairs={{0,16},{4,20},{8,24},{12,28},{16,0},{20,4},{24,8},{28,12},{1,17},{... | collective-permute-start | bytes 417800 | tf_op jit(solution)/shard_map/ppermute | solution.py:391
  79.7 1.6 %collective-permute-start.21 = (bf16[544,128]{1,0:T(8,128)(2,1)S(1)}, bf16[544,128]{1,0:T(8,128)(2,1)S(1)}, u32[]{:S(2)}, u32[]{:S(2)}) collective-permute-start(bf16[544,128]{1,0:T(8,128)(2,1)S(1)} %get-tuple-element.79), channel_id=1, source_target_pairs={{0,8},{4,12},{8,0},{12,4},{16,24},{20,28},{24,16},{28,20},{1,9},{5... | collective-permute-start | bytes 417800 | tf_op jit(solution)/shard_map/ppermute | solution.py:391
  81.6 5.8 %local_part.1 = (f32[8,96,512]{2,1,0:T(8,128)S(1)}, f32[8,32,512]{2,1,0:T(8,128)S(1)}, f32[96,128]{1,0:T(8,128)S(1)}, f32[32,128]{1,0:T(8,128)S(1)}) custom-call(s32[3]{0:T(128)S(1)} %pad_add_fusion.pos_ref.refs_0_, bf16[1024,512]{1,0:T(8,128)(2,1)S(1)} %get-tuple-element.60.refs_1_, bf16[1024,512]{1,0:T(8,128)(2,1)S(1)} %get-tuple-element.61.refs_2_, ...), custom_call_target="tpu_custom_call" | custom-call | flops 5500000256 | bytes 1048576 | tf_op jit(solution)/shard_map/local_part/pallas_call | solution.py:38
  92.2 2.5 %mix.2 = (bf16[2,192,512]{2,1,0:T(8,128)(2,1)S(1)}, bf16[2,192,512]{2,1,0:T(8,128)(2,1)S(1)}) custom-call(s32[3]{0:T(128)S(1)} %pad_add_fusion.pos_ref.refs_0_, f32[8,96,512]{2,1,0:T(8,128)S(1)} %get-tuple-element.72.refs_1_, f32[96,128]{1,0:T(8,128)S(1)} %get-tuple-element.73.refs_2_, f32[8,32,512]{2,1,0:T(8,128)S(1)} %get-tuple-element.74.refs_3_, ...), custom_call_target="tpu_custom_call" | custom-call | flops 2200000000 | bytes 1048576 | tf_op jit(solution)/shard_map/mix/pallas_call | solution.py:38
  96.1 3.4 %collective-permute-start.26 = (bf16[544,128]{1,0:T(8,128)(2,1)S(1)}, bf16[544,128]{1,0:T(8,128)(2,1)S(1)}, u32[]{:S(2)}, u32[]{:S(2)}) collective-permute-start(bf16[544,128]{1,0:T(8,128)(2,1)S(1)} %get-tuple-element.86), channel_id=1, source_target_pairs={{0,28},{4,24},{8,20},{12,16},{16,12},{20,8},{24,4},{28,0},{1,29},{... | collective-permute-start | bytes 417800 | tf_op jit(solution)/shard_map/ppermute | solution.py:391
  99.5 2.4 %out_project.2 = (bf16[192,2048]{1,0:T(8,128)(2,1)S(1)}, f32[192,2048]{1,0:T(8,128)S(1)}) custom-call(s32[3]{0:T(128)S(1)} %pad_add_fusion.pos_ref.refs_0_, bf16[2,192,512]{2,1,0:T(8,128)(2,1)S(1)} %get-tuple-element.81.refs_1_, bf16[2,192,512]{2,1,0:T(8,128)(2,1)S(1)} %collective-permute-done.23.refs_2_, bf16[512,2048]{1,0:T(8,128)(2,1)S(1)} %copy-done.3, ...), custom_call_target="tpu_custom_call" | custom-call | flops 2200000000 | bytes 1048576 | tf_op jit(solution)/shard_map/out_project/pallas_call | solution.py:38
  103.5 3.1 %collective-permute-done.26.refs_6_ = bf16[544,128]{1,0:T(8,128)(2,1)S(1)} collective-permute-done((bf16[544,128]{1,0:T(8,128)(2,1)S(1)}, bf16[544,128]{1,0:T(8,128)(2,1)S(1)}, u32[]{:S(2)}, u32[]{:S(2)}) %collective-permute-start.26) | collective-permute-done | bytes 139296 | tf_op jit(solution)/shard_map/ppermute | solution.py:391
  112.2 14.7 %collective-permute-done.28.refs_4_ = bf16[64,2048]{1,0:T(8,128)(2,1)S(1)} collective-permute-done((bf16[64,2048]{1,0:T(8,128)(2,1)S(1)}, bf16[64,2048]{1,0:T(8,128)(2,1)S(1)}, u32[]{:S(2)}, u32[]{:S(2)}) %collective-permute-start.28) | collective-permute-done | bytes 262176 | tf_op jit(solution)/shard_map/ppermute | solution.py:384
  126.9 1.7 %join.1 = bf16[256,2048]{1,0:T(8,128)(2,1)} custom-call(s32[3]{0:T(128)S(1)} %pad_add_fusion.pos_ref.refs_0_, f32[192,2048]{1,0:T(8,128)S(1)} %get-tuple-element.83.refs_7_.refs_1_, bf16[192,2048]{1,0:T(8,128)(2,1)S(1)} %collective-permute-done.24.refs_2_, f32[64,2048]{1,0:T(8,128)S(1)} %get-tuple-element.89.refs_3_, ...), custom_call_target="tpu_custom_call" | custom-call | flops 2200000000 | bytes 1048576 | tf_op jit(solution)/shard_map/join/pallas_call | solution.py:38
  (78 shorter events, 24.0 us)
Async XLA Ops:
  0.0 30.8 %collective-permute-start.8 = (bf16[1024,512]{1,0:T(8,128)(2,1)}, bf16[1024,512]{1,0:T(8,128)(2,1)S(1)}, u32[]{:S(2)}, u32[]{:S(2)}) collective-permute-start(bf16[1024,512]{1,0:T(8,128)(2,1)} %tok_hbm.1), channel_id=1, source_target_pairs={{0,2},{1,3},{2,0},{3,1},{4,6},{5,7},{6,4},{7,5},{8,10},{9,11},{10,... | collective-permute-start | bytes 3145736 | tf_op jit(solution)/shard_map/ppermute | solution.py:384
  4.9 6.2 %collective-permute-start = (bf16[128,512]{1,0:T(8,128)(2,1)S(1)}, bf16[128,512]{1,0:T(8,128)(2,1)S(1)}, u32[]{:S(2)}, u32[]{:S(2)}) collective-permute-start(bf16[128,512]{1,0:T(8,128)(2,1)S(1)} %get-tuple-element.50), channel_id=1, source_target_pairs={{0,4},{4,0},{8,12},{12,8},{16,20},{20,16},{24,28},{28,24},{1,5},{5... | collective-permute-start | bytes 393224 | tf_op jit(solution)/shard_map/ppermute | solution.py:391
  6.4 9.8 %collective-permute-start.1 = (bf16[128,512]{1,0:T(8,128)(2,1)S(1)}, bf16[128,512]{1,0:T(8,128)(2,1)S(1)}, u32[]{:S(2)}, u32[]{:S(2)}) collective-permute-start(bf16[128,512]{1,0:T(8,128)(2,1)S(1)} %get-tuple-element.51), channel_id=1, source_target_pairs={{0,8},{4,12},{8,0},{12,4},{16,24},{20,28},{24,16},{28,20},{1,9},{5... | collective-permute-start | bytes 393224 | tf_op jit(solution)/shard_map/ppermute | solution.py:391
  8.0 10.6 %collective-permute-start.2 = (bf16[128,512]{1,0:T(8,128)(2,1)S(1)}, bf16[128,512]{1,0:T(8,128)(2,1)S(1)}, u32[]{:S(2)}, u32[]{:S(2)}) collective-permute-start(bf16[128,512]{1,0:T(8,128)(2,1)S(1)} %get-tuple-element.52), channel_id=1, source_target_pairs={{0,12},{4,8},{8,4},{12,0},{16,28},{20,24},{24,20},{28,16},{1,13},{... | collective-permute-start | bytes 393224 | tf_op jit(solution)/shard_map/ppermute | solution.py:391
  8.4 12.8 %collective-permute-start.3 = (bf16[128,512]{1,0:T(8,128)(2,1)S(1)}, bf16[128,512]{1,0:T(8,128)(2,1)S(1)}, u32[]{:S(2)}, u32[]{:S(2)}) collective-permute-start(bf16[128,512]{1,0:T(8,128)(2,1)S(1)} %get-tuple-element.53), channel_id=1, source_target_pairs={{0,16},{4,20},{8,24},{12,28},{16,0},{20,4},{24,8},{28,12},{1,17},{... | collective-permute-start | bytes 393224 | tf_op jit(solution)/shard_map/ppermute | solution.py:391
  11.1 19.5 %collective-permute-start.4 = (bf16[128,512]{1,0:T(8,128)(2,1)S(1)}, bf16[128,512]{1,0:T(8,128)(2,1)S(1)}, u32[]{:S(2)}, u32[]{:S(2)}) collective-permute-start(bf16[128,512]{1,0:T(8,128)(2,1)S(1)} %get-tuple-element.54), channel_id=1, source_target_pairs={{0,20},{4,16},{8,28},{12,24},{16,4},{20,0},{24,12},{28,8},{1,21},{... | collective-permute-start | bytes 393224 | tf_op jit(solution)/shard_map/ppermute | solution.py:391
  16.2 14.4 %collective-permute-start.5 = (bf16[128,512]{1,0:T(8,128)(2,1)S(1)}, bf16[128,512]{1,0:T(8,128)(2,1)S(1)}, u32[]{:S(2)}, u32[]{:S(2)}) collective-permute-start(bf16[128,512]{1,0:T(8,128)(2,1)S(1)} %get-tuple-element.55), channel_id=1, source_target_pairs={{0,24},{4,28},{8,16},{12,20},{16,8},{20,12},{24,0},{28,4},{1,25},{... | collective-permute-start | bytes 393224 | tf_op jit(solution)/shard_map/ppermute | solution.py:391
  18.6 12.0 %collective-permute-start.6 = (bf16[128,512]{1,0:T(8,128)(2,1)S(1)}, bf16[128,512]{1,0:T(8,128)(2,1)S(1)}, u32[]{:S(2)}, u32[]{:S(2)}) collective-permute-start(bf16[128,512]{1,0:T(8,128)(2,1)S(1)} %get-tuple-element.56), channel_id=1, source_target_pairs={{0,28},{4,24},{8,20},{12,16},{16,12},{20,8},{24,4},{28,0},{1,29},{... | collective-permute-start | bytes 393224 | tf_op jit(solution)/shard_map/ppermute | solution.py:391
  21.2 14.9 %collective-permute-start.10 = (bf16[512,2048]{1,0:T(8,128)(2,1)S(1)}, bf16[512,2048]{1,0:T(8,128)(2,1)S(1)}, u32[]{:S(2)}, u32[]{:S(2)}) collective-permute-start(bf16[512,2048]{1,0:T(8,128)(2,1)S(1)} %copy-done.3), channel_id=1, source_target_pairs={{0,1},{1,0},{2,3},{3,2},{4,5},{5,4},{6,7},{7,6},{8,9},{9,8},{10,11... | collective-permute-start | bytes 6291464 | tf_op jit(solution)/shard_map/ppermute | solution.py:384
  31.3 19.6 %collective-permute-start.12 = (bf16[768,512]{1,0:T(8,128)(2,1)S(1)}, bf16[768,512]{1,0:T(8,128)(2,1)S(1)}, u32[]{:S(2)}, u32[]{:S(2)}) collective-permute-start(bf16[768,512]{1,0:T(8,128)(2,1)S(1)} %slice_dynamic-update-slice_fusion.refs_1_), channel_id=1, source_target_pairs={{0,2},{1,3},{2,0},{3,1},{4,6},{5,7},{6,4},{7,5},{8,10},{9,11},{10,... | collective-permute-start | bytes 2359304 | tf_op jit(solution)/shard_map/ppermute | solution.py:384
  31.8 22.3 %collective-permute-start.15 = (bf16[768,512]{1,0:T(8,128)(2,1)S(1)}, bf16[768,512]{1,0:T(8,128)(2,1)S(1)}, u32[]{:S(2)}, u32[]{:S(2)}) collective-permute-start(bf16[768,512]{1,0:T(8,128)(2,1)S(1)} %slice_dynamic-update-slice_fusion.refs_1_), channel_id=1, source_target_pairs={{0,1},{1,0},{2,3},{3,2},{4,5},{5,4},{6,7},{7,6},{8,9},{9,8},{10,11... | collective-permute-start | bytes 2359304 | tf_op jit(solution)/shard_map/ppermute | solution.py:384
  50.9 12.4 %collective-permute-start.14 = (bf16[256,512]{1,0:T(8,128)(2,1)S(1)}, bf16[256,512]{1,0:T(8,128)(2,1)S(1)}, u32[]{:S(2)}, u32[]{:S(2)}) collective-permute-start(bf16[256,512]{1,0:T(8,128)(2,1)S(1)} %fence.8.refs_1_), channel_id=1, source_target_pairs={{0,2},{1,3},{2,0},{3,1},{4,6},{5,7},{6,4},{7,5},{8,10},{9,11},{10,... | collective-permute-start | bytes 786440 | tf_op jit(solution)/shard_map/ppermute | solution.py:384
  51.5 13.8 %collective-permute-start.11 = (bf16[512,512]{1,0:T(8,128)(2,1)S(1)}, bf16[512,512]{1,0:T(8,128)(2,1)S(1)}, u32[]{:S(2)}, u32[]{:S(2)}) collective-permute-start(bf16[512,512]{1,0:T(8,128)(2,1)S(1)} %project_halo.1.refs_7_), channel_id=1, source_target_pairs={{0,4},{4,8},{8,12},{12,16},{16,20},{20,24},{24,28},{1,5},{5,9},{9,... | collective-permute-start | bytes 1572872 | tf_op jit(solution)/shard_map/ppermute | solution.py:421
  54.0 9.9 %collective-permute-start.13 = (bf16[256,512]{1,0:T(8,128)(2,1)S(1)}, bf16[256,512]{1,0:T(8,128)(2,1)S(1)}, u32[]{:S(2)}, u32[]{:S(2)}) collective-permute-start(bf16[256,512]{1,0:T(8,128)(2,1)S(1)} %fence.8.refs_1_), channel_id=1, source_target_pairs={{0,1},{1,0},{2,3},{3,2},{4,5},{5,4},{6,7},{7,6},{8,9},{9,8},{10,11... | collective-permute-start | bytes 786440 | tf_op jit(solution)/shard_map/ppermute | solution.py:384
  69.0 19.4 %collective-permute-start.18 = (bf16[544,128]{1,0:T(8,128)(2,1)S(1)}, bf16[544,128]{1,0:T(8,128)(2,1)S(1)}, u32[]{:S(2)}, u32[]{:S(2)}) collective-permute-start(bf16[544,128]{1,0:T(8,128)(2,1)S(1)} %get-tuple-element.76), channel_id=1, source_target_pairs={{0,16},{4,20},{8,24},{12,28},{16,0},{20,4},{24,8},{28,12},{1,17},{... | collective-permute-start | bytes 417800 | tf_op jit(solution)/shard_map/ppermute | solution.py:391
  78.2 11.8 %collective-permute-start.19 = (bf16[544,128]{1,0:T(8,128)(2,1)S(1)}, bf16[544,128]{1,0:T(8,128)(2,1)S(1)}, u32[]{:S(2)}, u32[]{:S(2)}) collective-permute-start(bf16[544,128]{1,0:T(8,128)(2,1)S(1)} %get-tuple-element.77), channel_id=1, source_target_pairs={{0,20},{4,16},{8,28},{12,24},{16,4},{20,0},{24,12},{28,8},{1,21},{... | collective-permute-start | bytes 417800 | tf_op jit(solution)/shard_map/ppermute | solution.py:391
  78.2 11.8 %collective-permute-start.20 = (bf16[544,128]{1,0:T(8,128)(2,1)S(1)}, bf16[544,128]{1,0:T(8,128)(2,1)S(1)}, u32[]{:S(2)}, u32[]{:S(2)}) collective-permute-start(bf16[544,128]{1,0:T(8,128)(2,1)S(1)} %get-tuple-element.78), channel_id=1, source_target_pairs={{0,4},{4,0},{8,12},{12,8},{16,20},{20,16},{24,28},{28,24},{1,5},{5... | collective-permute-start | bytes 417800 | tf_op jit(solution)/shard_map/ppermute | solution.py:391
  79.7 10.9 %collective-permute-start.21 = (bf16[544,128]{1,0:T(8,128)(2,1)S(1)}, bf16[544,128]{1,0:T(8,128)(2,1)S(1)}, u32[]{:S(2)}, u32[]{:S(2)}) collective-permute-start(bf16[544,128]{1,0:T(8,128)(2,1)S(1)} %get-tuple-element.79), channel_id=1, source_target_pairs={{0,8},{4,12},{8,0},{12,4},{16,24},{20,28},{24,16},{28,20},{1,9},{5... | collective-permute-start | bytes 417800 | tf_op jit(solution)/shard_map/ppermute | solution.py:391
  81.3 10.9 %collective-permute-start.22 = (bf16[544,128]{1,0:T(8,128)(2,1)S(1)}, bf16[544,128]{1,0:T(8,128)(2,1)S(1)}, u32[]{:S(2)}, u32[]{:S(2)}) collective-permute-start(bf16[544,128]{1,0:T(8,128)(2,1)S(1)} %get-tuple-element.80), channel_id=1, source_target_pairs={{0,12},{4,8},{8,4},{12,0},{16,28},{20,24},{24,20},{28,16},{1,13},{... | collective-permute-start | bytes 417800 | tf_op jit(solution)/shard_map/ppermute | solution.py:391
  94.7 4.8 %collective-permute-start.23 = (bf16[2,192,512]{2,1,0:T(8,128)(2,1)S(1)}, bf16[2,192,512]{2,1,0:T(8,128)(2,1)S(1)}, u32[]{:S(2)}, u32[]{:S(2)}) collective-permute-start(bf16[2,192,512]{2,1,0:T(8,128)(2,1)S(1)} %get-tuple-element.82), channel_id=1, source_target_pairs={{0,1},{1,0},{2,3},{3,2},{4,5},{5,4},{6,7},{7,6},{8,9},{9,8},{10,11... | collective-permute-start | bytes 1179656 | tf_op jit(solution)/shard_map/ppermute | solution.py:384
  94.8 8.7 %collective-permute-start.25 = (bf16[544,128]{1,0:T(8,128)(2,1)S(1)}, bf16[544,128]{1,0:T(8,128)(2,1)S(1)}, u32[]{:S(2)}, u32[]{:S(2)}) collective-permute-start(bf16[544,128]{1,0:T(8,128)(2,1)S(1)} %get-tuple-element.85), channel_id=1, source_target_pairs={{0,24},{4,28},{8,16},{12,20},{16,8},{20,12},{24,0},{28,4},{1,25},{... | collective-permute-start | bytes 417800 | tf_op jit(solution)/shard_map/ppermute | solution.py:391
  96.1 10.5 %collective-permute-start.26 = (bf16[544,128]{1,0:T(8,128)(2,1)S(1)}, bf16[544,128]{1,0:T(8,128)(2,1)S(1)}, u32[]{:S(2)}, u32[]{:S(2)}) collective-permute-start(bf16[544,128]{1,0:T(8,128)(2,1)S(1)} %get-tuple-element.86), channel_id=1, source_target_pairs={{0,28},{4,24},{8,20},{12,16},{16,12},{20,8},{24,4},{28,0},{1,29},{... | collective-permute-start | bytes 417800 | tf_op jit(solution)/shard_map/ppermute | solution.py:391
  101.9 25.0 %collective-permute-start.24 = (bf16[192,2048]{1,0:T(8,128)(2,1)S(1)}, bf16[192,2048]{1,0:T(8,128)(2,1)S(1)}, u32[]{:S(2)}, u32[]{:S(2)}) collective-permute-start(bf16[192,2048]{1,0:T(8,128)(2,1)S(1)} %get-tuple-element.84), channel_id=1, source_target_pairs={{0,2},{1,3},{2,0},{3,1},{4,6},{5,7},{6,4},{7,5},{8,10},{9,11},{10,... | collective-permute-start | bytes 2359304 | tf_op jit(solution)/shard_map/ppermute | solution.py:384
  110.7 16.3 %collective-permute-start.28 = (bf16[64,2048]{1,0:T(8,128)(2,1)S(1)}, bf16[64,2048]{1,0:T(8,128)(2,1)S(1)}, u32[]{:S(2)}, u32[]{:S(2)}) collective-permute-start(bf16[64,2048]{1,0:T(8,128)(2,1)S(1)} %get-tuple-element.90), channel_id=1, source_target_pairs={{0,2},{1,3},{2,0},{3,1},{4,6},{5,7},{6,4},{7,5},{8,10},{9,11},{10,... | collective-permute-start | bytes 786440 | tf_op jit(solution)/shard_map/ppermute | solution.py:384
  (9 other events, 42.6 us)

commit v12 on v11

--- a/solution.py
+++ b/solution.py
@@ -159,6 +159,17 @@
         term = dot(x_ref[at, :], w_ref[p * width : (p + 1) * width, :])
         total = term if total is None else total + term
     return total.astype(BF16)
+
+
+def half_kernel(x0, x1, wq, wk, wv, *outs):
+    width = x0.shape[1]
+    for w, out in zip((wq, wk, wv), outs):
+        out[...] = dot(x0[...], w[:width, :]) + dot(x1[...], w[width : 2 * width, :])
+
+
+def half_sums(own, core, weights, after):
+    shapes = [shape(own.shape, F32)] * 3
+    return call(half_kernel, "half_sums", 3, shapes, (own, core, *weights), after)
 
 
 def halo_kernel(x0, x1, x2, x3, wk, wv, out_ref):
@@ -239,7 +250,7 @@
     return list(zip(outs[: len(sizes)], outs[len(sizes) :]))
 
 
-def column_kernel(pos_ref, x0, x1, x2, x3, wq, wk, wv, *rest):
+def column_kernel(pos_ref, x2, x3, hq, hk, hv, wq, wk, wv, *rest):
     refs, scratch = rest[:-3], rest[-3:]
     owners, message, _ = scratch[0].shape
     out_refs = refs[-owners:]
@@ -248,9 +259,11 @@
     for old, new in zip(refs[:-owners], out_refs):
         new[:base, :] = old[...]
     groups = message // (ROWS * SUB)
-    everything = slice(0, owners * message)
-    for w, a in zip((wq, wk, wv), scratch):
-        a[...] = gathered((x0, x1, x2, x3), everything, w).reshape(a.shape)
+    width = x2.shape[1]
+    for h, w, a in zip((hq, hk, hv), (wq, wk, wv), scratch):
+        total = h[...] + dot(x2[...], w[2 * width : 3 * width, :])
+        total = total + dot(x3[...], w[3 * width :, :])
+        a[...] = total.astype(BF16).reshape(a.shape)
     part = ROWS * SUB
     size = owners * part
 
@@ -287,13 +300,13 @@
         out_refs[n][to : to + 16, :] = tail.astype(BF16)
 
 
-def column_part(pos, pieces, weights, earlier, owners, after):
-    tokens, width = pieces[0].shape
+def column_part(pos, across, halves, weights, earlier, owners):
+    tokens, width = across.shape
     message = tokens // owners
     rows = HEADS * message + 16 + (earlier[0].shape[0] if earlier else 0)
     scratch = [pltpu.VMEM((owners, message, width), BF16)] * 3
-    args = (pos, *pieces, *weights, *earlier)
-    return call(column_kernel, "column_part", 0, [shape((rows, DH))] * owners, args, after, scratch)
+    args = (pos, across, swap(across, 1), *halves, *weights, *earlier)
+    return call(column_kernel, "column_part", 0, [shape((rows, DH))] * owners, args, (), scratch)
 
 
 def mix_kernel(share, pos_ref, *refs):
@@ -364,20 +377,33 @@
     return call(out_kernel, "out_project", 2, shapes, (pos, own, other, w_own, w_other))
 
 
-def join_kernel(pos_ref, *refs):
-    out_ref = refs[-1]
-    for share, keep, got in zip(SHARES, refs[0:-1:2], refs[1:-1:2]):
-        span = keep.shape[0] // len(share)
-        for n, k in enumerate(share):
-            rows = slice(n * span, (n + 1) * span)
-            to = pl.ds(pl.multiple_of((pos_ref[0] ^ k) * span, span), span)
-            out_ref[to, :] = (keep[rows, :] + got[rows, :].astype(F32)).astype(BF16)
-
-
-def join(pos, pairs):
-    columns = pairs[0][0].shape[1]
-    args = [x for pair in pairs for x in pair]
-    return call(join_kernel, "join", 2, shape((STRIDE, columns)), (pos, *args))
+def join_kernel(share, pos_ref, keep, got, *rest):
+    out_hbm, joined, sems = rest[-3:]
+    span = keep.shape[0] // len(share)
+    joined[...] = (keep[...] + got[...].astype(F32)).astype(BF16)
+    copies = []
+    for n, k in enumerate(share):
+        to = pl.ds(pl.multiple_of((pos_ref[0] ^ k) * span, span), span)
+        rows = slice(n * span, (n + 1) * span)
+        copies.append(pltpu.make_async_copy(joined.at[rows], out_hbm.at[to], sems.at[n]))
+    for c in copies:
+        c.start()
+    for c in copies:
+        c.wait()
+
+
+def join(pos, share, keep, got, earlier):
+    return pl.pallas_call(
+        functools.partial(join_kernel, share),
+        in_specs=[IN_SMEM, IN_VMEM, IN_VMEM] + [ANYWHERE] * len(earlier),
+        out_specs=ANYWHERE,
+        out_shape=shape((STRIDE, keep.shape[1])),
+        input_output_aliases={3: 0} if earlier else {},
+        scratch_shapes=[pltpu.VMEM(keep.shape, BF16), pltpu.SemaphoreType.DMA((len(share),))],
+        compiler_params=pltpu.CompilerParams(vmem_limit_bytes=16 * MIB),
+        cost_estimate=pl.CostEstimate(flops=int(1.1e9), bytes_accessed=MIB, transcendentals=0),
+        name="join",
+    )(pos, keep, got, *earlier)
 
 
 def swap(value, distance):
@@ -427,23 +453,26 @@
         (*pieces, *weights, own_halo),
         (w_other,),
     )
-    first_across = fence(first_across, q)
-    first_pieces = (first, first_core, first_across, swap(first_across, 1))
-    second = fence(classes[1], first_across)
-    second_core, second_across = swap(second, 1), swap(second, 2)
-    columns = column_part(pos, first_pieces, weights, (), owners, ())
+    second_core = swap(classes[1], 1)
+    first_half = half_sums(first, first_core, weights, (q,))
+    second_half = half_sums(classes[1], second_core, weights, (first_half[0],))
+    first_across = fence(first_across, halo, second_half[0])
+    second_across = swap(fence(classes[1], first_across), 2)
+    columns = column_part(pos, first_across, first_half, weights, (), owners)
     second_across = fence(second_across, columns[0])
-    second_pieces = (second, second_core, second_across, swap(second_across, 1))
-    columns = column_part(pos, second_pieces, weights, columns, owners, (halo,))
+    columns = column_part(pos, second_across, second_half, weights, columns, owners)
     locals_ = local_part(pos, q, k, v, halo, owners, (columns[0],))
     columns = exchange(columns)
-    pairs, after = [], ()
+    sums, after = [], ()
     for share in SHARES:
         own, send = mix(pos, share, [columns[n] for n in share], locals_, after)
         out, keep = out_project(pos, own, swap(send, 1), w_out, w_other)
-        pairs.append((keep, swap(out, 2)))
+        sums.append((keep, swap(out, 2)))
         after = (keep,)
-    return join(pos, pairs)
+    result = ()
+    for share, (keep, got) in zip(SHARES, sums):
+        result = (join(pos, share, keep, got, result),)
+    return result[0]
 
 
 def from_behind(value, axis, by):

time: 129 us -> 125 us (0.969)
  waiting for transfers between devices: 46.2 us -> 41.2 us
  Pallas kernels: 37.6 us -> 39.1 us
    ppermute x14, waiting for transfers between devices: 25.5 us -> 20.4 us  [swap(): return lax.ppermute(value, 'head', [(i, i ^ distance) for i in range(4)])]
    pallas_call x0 -> x2, Pallas kernels: none -> 2.89 us  [join(): pl.pallas_call(functools.partial(join_kernel, share), in_specs=[IN_SMEM,...]
    pallas_call x10 -> x11, Pallas kernels: 34.7 us -> 33.3 us  [call(): pl.pallas_call(run, in_specs=specs + [ANYWHERE] * extra, out_specs=jax.tr...]
  transfers between devices with their start and end apart: 29 -> 29, of which waited for: 12 -> 16; matrix products, arithmetic and copies ran while one was open for 0% -> 0% of each run, Pallas kernels for 23% -> 26%
where the time goes in v12:
time: 125 us
  starting transfers between devices  41.7 us (33%)
  waiting for transfers between devices  41.2 us (33%)
  Pallas kernels  39.1 us (31%)
  local copies, waits for them, and re-layouts  1.91 us (2%)
    pallas_call x11, Pallas kernels, call(): pl.pallas_call(run, in_specs=specs + [ANYWHERE] * extra, out_specs=jax.tr...  33.3 us
    ppermute x14, starting transfers between devices, move(): lax.ppermute(value, 'seq', [(i, i ^ k) for i in range(peers)])  31.3 us
    ppermute x14, waiting for transfers between devices, swap(): return lax.ppermute(value, 'head', [(i, i ^ distance) for i in range(4)])  20.4 us
    ppermute x14, waiting for transfers between devices, move(): lax.ppermute(value, 'seq', [(i, i ^ k) for i in range(peers)])  20.3 us
    ppermute x14, starting transfers between devices, swap(): return lax.ppermute(value, 'head', [(i, i ^ distance) for i in range(4)])  7.65 us
    pallas_call x2, Pallas kernels, join(): pl.pallas_call(functools.partial(join_kernel, share), in_specs=[IN_SMEM,...  2.89 us
    ppermute x1, starting transfers between devices, chunked(): lax.ppermute(own_halo, 'seq', [(i, i + 1) for i in range(owners - 1)])  2.73 us
  transfers between devices with their start and end apart: 29, of which 16 were waited for; matrix products, arithmetic and copies ran while one was open for 0% of the time, Pallas kernels for 26%

profile of v12, /device:TPU:0, one launch (start us, length us, event | category | flops | bytes accessed | tf_op | source)
XLA Modules:
  0.0 124.5 jit_solution(10889132632994453604)
XLA Ops:
  0.0 2.9 %collective-permute-start.8 = (bf16[1024,512]{1,0:T(8,128)(2,1)}, bf16[1024,512]{1,0:T(8,128)(2,1)S(1)}, u32[]{:S(2)}, u32[]{:S(2)}) collective-permute-start(bf16[1024,512]{1,0:T(8,128)(2,1)} %tok_hbm.1), channel_id=1, source_target_pairs={{0,2},{1,3},{2,0},{3,1},{4,6},{5,7},{6,4},{7,5},{8,10},{9,11},{10,... | collective-permute-start | bytes 3145736 | tf_op jit(solution)/shard_map/ppermute | solution.py:410
  3.0 1.8 %pack_tokens.1 = (bf16[1024,512]{1,0:T(8,128)(2,1)S(1)}, bf16[128,512]{1,0:T(8,128)(2,1)S(1)}, bf16[128,512]{1,0:T(8,128)(2,1)S(1)}, bf16[128,512]{1,0:T(8,128)(...) custom-call(s32[3]{0:T(128)S(1)} %pad_add_fusion.pos_ref.refs_0_, ...), custom_call_target="tpu_custom_call" | custom-call | bytes 2097152 | tf_op jit(solution)/shard_map/pack_tokens/pallas_call | solution.py:112
  8.4 2.6 %collective-permute-start.3 = (bf16[128,512]{1,0:T(8,128)(2,1)S(1)}, bf16[128,512]{1,0:T(8,128)(2,1)S(1)}, u32[]{:S(2)}, u32[]{:S(2)}) collective-permute-start(bf16[128,512]{1,0:T(8,128)(2,1)S(1)} %get-tuple-element.59), channel_id=1, source_target_pairs={{0,16},{4,20},{8,24},{12,28},{16,0},{20,4},{24,8},{28,12},{1,17},{... | collective-permute-start | bytes 393224 | tf_op jit(solution)/shard_map/ppermute | solution.py:417
  11.1 2.9 %collective-permute-start.4 = (bf16[128,512]{1,0:T(8,128)(2,1)S(1)}, bf16[128,512]{1,0:T(8,128)(2,1)S(1)}, u32[]{:S(2)}, u32[]{:S(2)}) collective-permute-start(bf16[128,512]{1,0:T(8,128)(2,1)S(1)} %get-tuple-element.60), channel_id=1, source_target_pairs={{0,20},{4,16},{8,28},{12,24},{16,4},{20,0},{24,12},{28,8},{1,21},{... | collective-permute-start | bytes 393224 | tf_op jit(solution)/shard_map/ppermute | solution.py:417
  14.0 2.2 %collective-permute-done.1 = bf16[128,512]{1,0:T(8,128)(2,1)S(1)} collective-permute-done((bf16[128,512]{1,0:T(8,128)(2,1)S(1)}, bf16[128,512]{1,0:T(8,128)(2,1)S(1)}, u32[]{:S(2)}, u32[]{:S(2)}) %collective-permute-start.1) | collective-permute-done | bytes 131104 | tf_op jit(solution)/shard_map/ppermute | solution.py:417
  16.2 2.4 %collective-permute-start.5 = (bf16[128,512]{1,0:T(8,128)(2,1)S(1)}, bf16[128,512]{1,0:T(8,128)(2,1)S(1)}, u32[]{:S(2)}, u32[]{:S(2)}) collective-permute-start(bf16[128,512]{1,0:T(8,128)(2,1)S(1)} %get-tuple-element.61), channel_id=1, source_target_pairs={{0,24},{4,28},{8,16},{12,20},{16,8},{20,12},{24,0},{28,4},{1,25},{... | collective-permute-start | bytes 393224 | tf_op jit(solution)/shard_map/ppermute | solution.py:417
  18.6 2.6 %collective-permute-start.6 = (bf16[128,512]{1,0:T(8,128)(2,1)S(1)}, bf16[128,512]{1,0:T(8,128)(2,1)S(1)}, u32[]{:S(2)}, u32[]{:S(2)}) collective-permute-start(bf16[128,512]{1,0:T(8,128)(2,1)S(1)} %get-tuple-element.62), channel_id=1, source_target_pairs={{0,28},{4,24},{8,20},{12,16},{16,12},{20,8},{24,4},{28,0},{1,29},{... | collective-permute-start | bytes 393224 | tf_op jit(solution)/shard_map/ppermute | solution.py:417
  21.3 9.2 %collective-permute-done.4 = bf16[128,512]{1,0:T(8,128)(2,1)S(1)} collective-permute-done((bf16[128,512]{1,0:T(8,128)(2,1)S(1)}, bf16[128,512]{1,0:T(8,128)(2,1)S(1)}, u32[]{:S(2)}, u32[]{:S(2)}) %collective-permute-start.4) | collective-permute-done | bytes 131104 | tf_op jit(solution)/shard_map/ppermute | solution.py:417
  37.2 2.7 %collective-permute-start.11 = (bf16[512,512]{1,0:T(8,128)(2,1)S(1)}, bf16[512,512]{1,0:T(8,128)(2,1)S(1)}, u32[]{:S(2)}, u32[]{:S(2)}) collective-permute-start(bf16[512,512]{1,0:T(8,128)(2,1)S(1)} %project_halo.1.refs_7_), channel_id=1, source_target_pairs={{0,4},{4,8},{8,12},{12,16},{16,20},{20,24},{24,28},{1,5},{5,9},{9,... | collective-permute-start | bytes 1572872 | tf_op jit(solution)/shard_map/ppermute | solution.py:447
  40.0 5.6 %project_block.1 = (bf16[1024,512]{1,0:T(8,128)(2,1)S(1)}, bf16[1024,512]{1,0:T(8,128)(2,1)S(1)}, bf16[1024,512]{1,0:T(8,128)(2,1)S(1)}) custom-call(bf16[1024,512]{1,0:T(8,128)(2,1)S(1)} %get-tuple-element.54.refs_0_, bf16[1024,512]{1,0:T(8,128)(2,1)S(1)} %collective-permute-done.7.refs_1_, bf16[1024,512]{1,0:T(8,128)(2,1)S(1)} %fence.6.refs_2_, ...), custom_call_target="tpu_custom_call" | custom-call | flops 6600000000 | bytes 1048576 | tf_op jit(solution)/shard_map/project_block/pallas_call | solution.py:38
  45.6 2.6 %half_sums.2 = (f32[768,512]{1,0:T(8,128)S(1)}, f32[768,512]{1,0:T(8,128)S(1)}, f32[768,512]{1,0:T(8,128)S(1)}) custom-call(bf16[768,512]{1,0:T(8,128)(2,1)S(1)} %slice_dynamic-update-slice_fusion.refs_1_.refs_0_, bf16[768,512]{1,0:T(8,128)(2,1)S(1)} %collective-permute-done.14.refs_1_, bf16[2048,512]{1,0:T(8,128)(2,1)S(1)} %get-tuple-element.63.refs_4_.refs_2_.refs_6_, ...), custom_call_target="tpu_custom_call" | custom-call | flops 3300000000 | bytes 1048576 | tf_op jit(solution)/shard_map/half_sums/pallas_call | solution.py:38
  53.5 6.8 %column_part.2 = (bf16[400,128]{1,0:T(8,128)(2,1)S(1)}, bf16[400,128]{1,0:T(8,128)(2,1)S(1)}, bf16[400,128]{1,0:T(8,128)(2,1)S(1)}, bf16[400,128]{1,0:T(8,128)(2...) custom-call(s32[3]{0:T(128)S(1)} %pad_add_fusion.pos_ref.refs_0_, ...), custom_call_target="tpu_custom_call" | custom-call | bytes 1048576 | tf_op jit(solution)/shard_map/column_part/pallas_call | solution.py:38
  61.9 2.9 %column_part.3 = (bf16[544,128]{1,0:T(8,128)(2,1)S(1)}, bf16[544,128]{1,0:T(8,128)(2,1)S(1)}, bf16[544,128]{1,0:T(8,128)(2,1)S(1)}, bf16[544,128]{1,0:T(8,128)(2...) custom-call(s32[3]{0:T(128)S(1)} %pad_add_fusion.pos_ref.refs_0_, ...), custom_call_target="tpu_custom_call" | custom-call | bytes 1048576 | tf_op jit(solution)/shard_map/column_part/pallas_call | solution.py:38
  64.8 9.0 %collective-permute-start.20 = (bf16[544,128]{1,0:T(8,128)(2,1)S(1)}, bf16[544,128]{1,0:T(8,128)(2,1)S(1)}, u32[]{:S(2)}, u32[]{:S(2)}) collective-permute-start(bf16[544,128]{1,0:T(8,128)(2,1)S(1)} %get-tuple-element.90), channel_id=1, source_target_pairs={{0,16},{4,20},{8,24},{12,28},{16,0},{20,4},{24,8},{28,12},{1,17},{... | collective-permute-start | bytes 417800 | tf_op jit(solution)/shard_map/ppermute | solution.py:417
  75.3 1.6 %collective-permute-start.23 = (bf16[544,128]{1,0:T(8,128)(2,1)S(1)}, bf16[544,128]{1,0:T(8,128)(2,1)S(1)}, u32[]{:S(2)}, u32[]{:S(2)}) collective-permute-start(bf16[544,128]{1,0:T(8,128)(2,1)S(1)} %get-tuple-element.93), channel_id=1, source_target_pairs={{0,8},{4,12},{8,0},{12,4},{16,24},{20,28},{24,16},{28,20},{1,9},{5... | collective-permute-start | bytes 417800 | tf_op jit(solution)/shard_map/ppermute | solution.py:417
  77.2 6.0 %local_part.1 = (f32[8,96,512]{2,1,0:T(8,128)S(1)}, f32[8,32,512]{2,1,0:T(8,128)S(1)}, f32[96,128]{1,0:T(8,128)S(1)}, f32[32,128]{1,0:T(8,128)S(1)}) custom-call(s32[3]{0:T(128)S(1)} %pad_add_fusion.pos_ref.refs_0_, bf16[1024,512]{1,0:T(8,128)(2,1)S(1)} %get-tuple-element.66.refs_5_.refs_1_, bf16[1024,512]{1,0:T(8,128)(2,1)S(1)} %get-tuple-element.67.refs_2_, ...), custom_call_target="tpu_custom_call" | custom-call | flops 5500000256 | bytes 1048576 | tf_op jit(solution)/shard_map/local_part/pallas_call | solution.py:38
  84.2 2.0 %collective-permute-done.21.refs_6_ = bf16[544,128]{1,0:T(8,128)(2,1)S(1)} collective-permute-done((bf16[544,128]{1,0:T(8,128)(2,1)S(1)}, bf16[544,128]{1,0:T(8,128)(2,1)S(1)}, u32[]{:S(2)}, u32[]{:S(2)}) %collective-permute-start.21) | collective-permute-done | bytes 139296 | tf_op jit(solution)/shard_map/ppermute | solution.py:417
  88.5 2.3 %mix.2 = (bf16[2,192,512]{2,1,0:T(8,128)(2,1)S(1)}, bf16[2,192,512]{2,1,0:T(8,128)(2,1)S(1)}) custom-call(s32[3]{0:T(128)S(1)} %pad_add_fusion.pos_ref.refs_0_, f32[8,96,512]{2,1,0:T(8,128)S(1)} %get-tuple-element.84.refs_1_, f32[96,128]{1,0:T(8,128)S(1)} %get-tuple-element.85.refs_2_, f32[8,32,512]{2,1,0:T(8,128)S(1)} %get-tuple-element.86.refs_3_, ...), custom_call_target="tpu_custom_call" | custom-call | flops 2200000000 | bytes 1048576 | tf_op jit(solution)/shard_map/mix/pallas_call | solution.py:38
  91.2 4.4 %collective-permute-start.19 = (bf16[544,128]{1,0:T(8,128)(2,1)S(1)}, bf16[544,128]{1,0:T(8,128)(2,1)S(1)}, u32[]{:S(2)}, u32[]{:S(2)}) collective-permute-start(bf16[544,128]{1,0:T(8,128)(2,1)S(1)} %get-tuple-element.89), channel_id=1, source_target_pairs={{0,28},{4,24},{8,20},{12,16},{16,12},{20,8},{24,4},{28,0},{1,29},{... | collective-permute-start | bytes 417800 | tf_op jit(solution)/shard_map/ppermute | solution.py:417
  95.6 2.4 %out_project.2 = (bf16[192,2048]{1,0:T(8,128)(2,1)S(1)}, f32[192,2048]{1,0:T(8,128)S(1)}) custom-call(s32[3]{0:T(128)S(1)} %pad_add_fusion.pos_ref.refs_0_, bf16[2,192,512]{2,1,0:T(8,128)(2,1)S(1)} %get-tuple-element.95.refs_1_, bf16[2,192,512]{2,1,0:T(8,128)(2,1)S(1)} %collective-permute-done.25.refs_2_, bf16[512,2048]{1,0:T(8,128)(2,1)S(1)} %copy-done.3, ...), custom_call_target="tpu_custom_call" | custom-call | flops 2200000000 | bytes 1048576 | tf_op jit(solution)/shard_map/out_project/pallas_call | solution.py:38
  99.3 3.4 %collective-permute-done.19.refs_6_ = bf16[544,128]{1,0:T(8,128)(2,1)S(1)} collective-permute-done((bf16[544,128]{1,0:T(8,128)(2,1)S(1)}, bf16[544,128]{1,0:T(8,128)(2,1)S(1)}, u32[]{:S(2)}, u32[]{:S(2)}) %collective-permute-start.19) | collective-permute-done | bytes 139296 | tf_op jit(solution)/shard_map/ppermute | solution.py:417
  107.9 10.6 %collective-permute-done.28.got = bf16[192,2048]{1,0:T(8,128)(2,1)S(1)} collective-permute-done((bf16[192,2048]{1,0:T(8,128)(2,1)S(1)}, bf16[192,2048]{1,0:T(8,128)(2,1)S(1)}, u32[]{:S(2)}, u32[]{:S(2)}) %collective-permute-start.28) | collective-permute-done | bytes 786464 | tf_op jit(solution)/shard_map/ppermute | solution.py:410
  118.5 1.6 %join.2.rest_0_ = bf16[256,2048]{1,0:T(8,128)(2,1)} custom-call(s32[3]{0:T(128)S(1)} %pad_add_fusion.pos_ref.refs_0_, f32[192,2048]{1,0:T(8,128)S(1)} %get-tuple-element.97.refs_7_.keep, bf16[192,2048]{1,0:T(8,128)(2,1)S(1)} %collective-permute-done.28.got), custom_call_target="tpu_custom_call" | custom-call | flops 1100000000 | bytes 1048576 | tf_op jit(solution)/shard_map/join/pallas_call | solution.py:396
  120.1 2.9 %collective-permute-done.27.got = bf16[64,2048]{1,0:T(8,128)(2,1)S(1)} collective-permute-done((bf16[64,2048]{1,0:T(8,128)(2,1)S(1)}, bf16[64,2048]{1,0:T(8,128)(2,1)S(1)}, u32[]{:S(2)}, u32[]{:S(2)}) %collective-permute-start.27) | collective-permute-done | bytes 262176 | tf_op jit(solution)/shard_map/ppermute | solution.py:410
  (81 shorter events, 30.6 us)
Async XLA Ops:
  0.0 31.5 %collective-permute-start.8 = (bf16[1024,512]{1,0:T(8,128)(2,1)}, bf16[1024,512]{1,0:T(8,128)(2,1)S(1)}, u32[]{:S(2)}, u32[]{:S(2)}) collective-permute-start(bf16[1024,512]{1,0:T(8,128)(2,1)} %tok_hbm.1), channel_id=1, source_target_pairs={{0,2},{1,3},{2,0},{3,1},{4,6},{5,7},{6,4},{7,5},{8,10},{9,11},{10,... | collective-permute-start | bytes 3145736 | tf_op jit(solution)/shard_map/ppermute | solution.py:410
  4.9 6.3 %collective-permute-start = (bf16[128,512]{1,0:T(8,128)(2,1)S(1)}, bf16[128,512]{1,0:T(8,128)(2,1)S(1)}, u32[]{:S(2)}, u32[]{:S(2)}) collective-permute-start(bf16[128,512]{1,0:T(8,128)(2,1)S(1)} %get-tuple-element.56), channel_id=1, source_target_pairs={{0,4},{4,0},{8,12},{12,8},{16,20},{20,16},{24,28},{28,24},{1,5},{5... | collective-permute-start | bytes 393224 | tf_op jit(solution)/shard_map/ppermute | solution.py:417
  6.4 9.8 %collective-permute-start.1 = (bf16[128,512]{1,0:T(8,128)(2,1)S(1)}, bf16[128,512]{1,0:T(8,128)(2,1)S(1)}, u32[]{:S(2)}, u32[]{:S(2)}) collective-permute-start(bf16[128,512]{1,0:T(8,128)(2,1)S(1)} %get-tuple-element.57), channel_id=1, source_target_pairs={{0,8},{4,12},{8,0},{12,4},{16,24},{20,28},{24,16},{28,20},{1,9},{5... | collective-permute-start | bytes 393224 | tf_op jit(solution)/shard_map/ppermute | solution.py:417
  8.0 10.6 %collective-permute-start.2 = (bf16[128,512]{1,0:T(8,128)(2,1)S(1)}, bf16[128,512]{1,0:T(8,128)(2,1)S(1)}, u32[]{:S(2)}, u32[]{:S(2)}) collective-permute-start(bf16[128,512]{1,0:T(8,128)(2,1)S(1)} %get-tuple-element.58), channel_id=1, source_target_pairs={{0,12},{4,8},{8,4},{12,0},{16,28},{20,24},{24,20},{28,16},{1,13},{... | collective-permute-start | bytes 393224 | tf_op jit(solution)/shard_map/ppermute | solution.py:417
  8.4 12.8 %collective-permute-start.3 = (bf16[128,512]{1,0:T(8,128)(2,1)S(1)}, bf16[128,512]{1,0:T(8,128)(2,1)S(1)}, u32[]{:S(2)}, u32[]{:S(2)}) collective-permute-start(bf16[128,512]{1,0:T(8,128)(2,1)S(1)} %get-tuple-element.59), channel_id=1, source_target_pairs={{0,16},{4,20},{8,24},{12,28},{16,0},{20,4},{24,8},{28,12},{1,17},{... | collective-permute-start | bytes 393224 | tf_op jit(solution)/shard_map/ppermute | solution.py:417
  11.1 19.4 %collective-permute-start.4 = (bf16[128,512]{1,0:T(8,128)(2,1)S(1)}, bf16[128,512]{1,0:T(8,128)(2,1)S(1)}, u32[]{:S(2)}, u32[]{:S(2)}) collective-permute-start(bf16[128,512]{1,0:T(8,128)(2,1)S(1)} %get-tuple-element.60), channel_id=1, source_target_pairs={{0,20},{4,16},{8,28},{12,24},{16,4},{20,0},{24,12},{28,8},{1,21},{... | collective-permute-start | bytes 393224 | tf_op jit(solution)/shard_map/ppermute | solution.py:417
  16.2 14.4 %collective-permute-start.5 = (bf16[128,512]{1,0:T(8,128)(2,1)S(1)}, bf16[128,512]{1,0:T(8,128)(2,1)S(1)}, u32[]{:S(2)}, u32[]{:S(2)}) collective-permute-start(bf16[128,512]{1,0:T(8,128)(2,1)S(1)} %get-tuple-element.61), channel_id=1, source_target_pairs={{0,24},{4,28},{8,16},{12,20},{16,8},{20,12},{24,0},{28,4},{1,25},{... | collective-permute-start | bytes 393224 | tf_op jit(solution)/shard_map/ppermute | solution.py:417
  18.6 12.0 %collective-permute-start.6 = (bf16[128,512]{1,0:T(8,128)(2,1)S(1)}, bf16[128,512]{1,0:T(8,128)(2,1)S(1)}, u32[]{:S(2)}, u32[]{:S(2)}) collective-permute-start(bf16[128,512]{1,0:T(8,128)(2,1)S(1)} %get-tuple-element.62), channel_id=1, source_target_pairs={{0,28},{4,24},{8,20},{12,16},{16,12},{20,8},{24,4},{28,0},{1,29},{... | collective-permute-start | bytes 393224 | tf_op jit(solution)/shard_map/ppermute | solution.py:417
  21.2 18.7 %collective-permute-start.10 = (bf16[512,2048]{1,0:T(8,128)(2,1)S(1)}, bf16[512,2048]{1,0:T(8,128)(2,1)S(1)}, u32[]{:S(2)}, u32[]{:S(2)}) collective-permute-start(bf16[512,2048]{1,0:T(8,128)(2,1)S(1)} %copy-done.3), channel_id=1, source_target_pairs={{0,1},{1,0},{2,3},{3,2},{4,5},{5,4},{6,7},{7,6},{8,9},{9,8},{10,11... | collective-permute-start | bytes 6291464 | tf_op jit(solution)/shard_map/ppermute | solution.py:410
  30.6 14.9 %collective-permute-start.14 = (bf16[768,512]{1,0:T(8,128)(2,1)S(1)}, bf16[768,512]{1,0:T(8,128)(2,1)S(1)}, u32[]{:S(2)}, u32[]{:S(2)}) collective-permute-start(bf16[768,512]{1,0:T(8,128)(2,1)S(1)} %slice_dynamic-update-slice_fusion.refs_1_.refs_0_), channel_id=1, source_target_pairs={{0,1},{1,0},{2,3},{3,2},{4,5},{5,4},{6,7},{7,6},{8,9},{9,8},{10,11... | collective-permute-start | bytes 2359304 | tf_op jit(solution)/shard_map/ppermute | solution.py:410
  30.7 20.0 %collective-permute-start.12 = (bf16[768,512]{1,0:T(8,128)(2,1)S(1)}, bf16[768,512]{1,0:T(8,128)(2,1)S(1)}, u32[]{:S(2)}, u32[]{:S(2)}) collective-permute-start(bf16[768,512]{1,0:T(8,128)(2,1)S(1)} %slice_dynamic-update-slice_fusion.refs_1_.refs_0_), channel_id=1, source_target_pairs={{0,2},{1,3},{2,0},{3,1},{4,6},{5,7},{6,4},{7,5},{8,10},{9,11},{10,... | collective-permute-start | bytes 2359304 | tf_op jit(solution)/shard_map/ppermute | solution.py:410
  34.8 13.3 %collective-permute-start.13 = (bf16[256,512]{1,0:T(8,128)(2,1)S(1)}, bf16[256,512]{1,0:T(8,128)(2,1)S(1)}, u32[]{:S(2)}, u32[]{:S(2)}) collective-permute-start(bf16[256,512]{1,0:T(8,128)(2,1)S(1)} %constant_dynamic-update-slice_fusion.refs_0_), channel_id=1, source_target_pairs={{0,1},{1,0},{2,3},{3,2},{4,5},{5,4},{6,7},{7,6},{8,9},{9,8},{10,11... | collective-permute-start | bytes 786440 | tf_op jit(solution)/shard_map/ppermute | solution.py:410
  37.2 14.0 %collective-permute-start.11 = (bf16[512,512]{1,0:T(8,128)(2,1)S(1)}, bf16[512,512]{1,0:T(8,128)(2,1)S(1)}, u32[]{:S(2)}, u32[]{:S(2)}) collective-permute-start(bf16[512,512]{1,0:T(8,128)(2,1)S(1)} %project_halo.1.refs_7_), channel_id=1, source_target_pairs={{0,4},{4,8},{8,12},{12,16},{16,20},{20,24},{24,28},{1,5},{5,9},{9,... | collective-permute-start | bytes 1572872 | tf_op jit(solution)/shard_map/ppermute | solution.py:447
  51.2 9.0 %collective-permute-start.15 = (bf16[256,512]{1,0:T(8,128)(2,1)S(1)}, bf16[256,512]{1,0:T(8,128)(2,1)S(1)}, u32[]{:S(2)}, u32[]{:S(2)}) collective-permute-start(bf16[256,512]{1,0:T(8,128)(2,1)S(1)} %fence.8), channel_id=1, source_target_pairs={{0,2},{1,3},{2,0},{3,1},{4,6},{5,7},{6,4},{7,5},{8,10},{9,11},{10,... | collective-permute-start | bytes 786440 | tf_op jit(solution)/shard_map/ppermute | solution.py:410
  64.8 19.4 %collective-permute-start.20 = (bf16[544,128]{1,0:T(8,128)(2,1)S(1)}, bf16[544,128]{1,0:T(8,128)(2,1)S(1)}, u32[]{:S(2)}, u32[]{:S(2)}) collective-permute-start(bf16[544,128]{1,0:T(8,128)(2,1)S(1)} %get-tuple-element.90), channel_id=1, source_target_pairs={{0,16},{4,20},{8,24},{12,28},{16,0},{20,4},{24,8},{28,12},{1,17},{... | collective-permute-start | bytes 417800 | tf_op jit(solution)/shard_map/ppermute | solution.py:417
  73.7 12.5 %collective-permute-start.21 = (bf16[544,128]{1,0:T(8,128)(2,1)S(1)}, bf16[544,128]{1,0:T(8,128)(2,1)S(1)}, u32[]{:S(2)}, u32[]{:S(2)}) collective-permute-start(bf16[544,128]{1,0:T(8,128)(2,1)S(1)} %get-tuple-element.91), channel_id=1, source_target_pairs={{0,20},{4,16},{8,28},{12,24},{16,4},{20,0},{24,12},{28,8},{1,21},{... | collective-permute-start | bytes 417800 | tf_op jit(solution)/shard_map/ppermute | solution.py:417
  73.7 12.5 %collective-permute-start.22 = (bf16[544,128]{1,0:T(8,128)(2,1)S(1)}, bf16[544,128]{1,0:T(8,128)(2,1)S(1)}, u32[]{:S(2)}, u32[]{:S(2)}) collective-permute-start(bf16[544,128]{1,0:T(8,128)(2,1)S(1)} %get-tuple-element.92), channel_id=1, source_target_pairs={{0,4},{4,0},{8,12},{12,8},{16,20},{20,16},{24,28},{28,24},{1,5},{5... | collective-permute-start | bytes 417800 | tf_op jit(solution)/shard_map/ppermute | solution.py:417
  75.3 11.6 %collective-permute-start.23 = (bf16[544,128]{1,0:T(8,128)(2,1)S(1)}, bf16[544,128]{1,0:T(8,128)(2,1)S(1)}, u32[]{:S(2)}, u32[]{:S(2)}) collective-permute-start(bf16[544,128]{1,0:T(8,128)(2,1)S(1)} %get-tuple-element.93), channel_id=1, source_target_pairs={{0,8},{4,12},{8,0},{12,4},{16,24},{20,28},{24,16},{28,20},{1,9},{5... | collective-permute-start | bytes 417800 | tf_op jit(solution)/shard_map/ppermute | solution.py:417
  76.9 11.6 %collective-permute-start.24 = (bf16[544,128]{1,0:T(8,128)(2,1)S(1)}, bf16[544,128]{1,0:T(8,128)(2,1)S(1)}, u32[]{:S(2)}, u32[]{:S(2)}) collective-permute-start(bf16[544,128]{1,0:T(8,128)(2,1)S(1)} %get-tuple-element.94), channel_id=1, source_target_pairs={{0,12},{4,8},{8,4},{12,0},{16,28},{20,24},{24,20},{28,16},{1,13},{... | collective-permute-start | bytes 417800 | tf_op jit(solution)/shard_map/ppermute | solution.py:417
  90.8 4.8 %collective-permute-start.25 = (bf16[2,192,512]{2,1,0:T(8,128)(2,1)S(1)}, bf16[2,192,512]{2,1,0:T(8,128)(2,1)S(1)}, u32[]{:S(2)}, u32[]{:S(2)}) collective-permute-start(bf16[2,192,512]{2,1,0:T(8,128)(2,1)S(1)} %get-tuple-element.96), channel_id=1, source_target_pairs={{0,1},{1,0},{2,3},{3,2},{4,5},{5,4},{6,7},{7,6},{8,9},{9,8},{10,11... | collective-permute-start | bytes 1179656 | tf_op jit(solution)/shard_map/ppermute | solution.py:410
  90.9 8.4 %collective-permute-start.18 = (bf16[544,128]{1,0:T(8,128)(2,1)S(1)}, bf16[544,128]{1,0:T(8,128)(2,1)S(1)}, u32[]{:S(2)}, u32[]{:S(2)}) collective-permute-start(bf16[544,128]{1,0:T(8,128)(2,1)S(1)} %get-tuple-element.88), channel_id=1, source_target_pairs={{0,24},{4,28},{8,16},{12,20},{16,8},{20,12},{24,0},{28,4},{1,25},{... | collective-permute-start | bytes 417800 | tf_op jit(solution)/shard_map/ppermute | solution.py:417
  91.2 11.5 %collective-permute-start.19 = (bf16[544,128]{1,0:T(8,128)(2,1)S(1)}, bf16[544,128]{1,0:T(8,128)(2,1)S(1)}, u32[]{:S(2)}, u32[]{:S(2)}) collective-permute-start(bf16[544,128]{1,0:T(8,128)(2,1)S(1)} %get-tuple-element.89), channel_id=1, source_target_pairs={{0,28},{4,24},{8,20},{12,16},{16,12},{20,8},{24,4},{28,0},{1,29},{... | collective-permute-start | bytes 417800 | tf_op jit(solution)/shard_map/ppermute | solution.py:417
  98.0 20.5 %collective-permute-start.28 = (bf16[192,2048]{1,0:T(8,128)(2,1)S(1)}, bf16[192,2048]{1,0:T(8,128)(2,1)S(1)}, u32[]{:S(2)}, u32[]{:S(2)}) collective-permute-start(bf16[192,2048]{1,0:T(8,128)(2,1)S(1)} %get-tuple-element.102), channel_id=1, source_target_pairs={{0,2},{1,3},{2,0},{3,1},{4,6},{5,7},{6,4},{7,5},{8,10},{9,11},{10,... | collective-permute-start | bytes 2359304 | tf_op jit(solution)/shard_map/ppermute | solution.py:410
  106.8 16.2 %collective-permute-start.27 = (bf16[64,2048]{1,0:T(8,128)(2,1)S(1)}, bf16[64,2048]{1,0:T(8,128)(2,1)S(1)}, u32[]{:S(2)}, u32[]{:S(2)}) collective-permute-start(bf16[64,2048]{1,0:T(8,128)(2,1)S(1)} %get-tuple-element.101), channel_id=1, source_target_pairs={{0,2},{1,3},{2,0},{3,1},{4,6},{5,7},{6,4},{7,5},{8,10},{9,11},{10,... | collective-permute-start | bytes 786440 | tf_op jit(solution)/shard_map/ppermute | solution.py:410
  (9 other events, 40.2 us)

commit v13 on v12

--- a/solution.py
+++ b/solution.py
@@ -12,7 +12,8 @@
 HEADS = 4
 ROWS = 4
 SUB = 8
-CHUNKS = ((0, 1, 2), (3,))
+CHUNKS = ((0, 1, 2, 3),)
+NEAR = 4
 PEERS = 8
 SHARES = ((4, 5, 1, 2, 3, 0), (6, 7))
 SCALE2 = DH ** (-0.5) * 1.4426950408889634
@@ -43,7 +44,7 @@
         scratch_shapes=list(scratch),
         compiler_params=pltpu.CompilerParams(vmem_limit_bytes=mib * MIB),
         cost_estimate=pl.CostEstimate(
-            flops=int(micros * 1.1e9), bytes_accessed=MIB, transcendentals=0
+            flops=int(micros * 1.1e9), bytes_accessed=0, transcendentals=0
         ),
         name=name,
     )(*args, *after)
@@ -147,7 +148,7 @@
         out_shape=[shape(w.shape) for w in weights],
         scratch_shapes=[pltpu.SemaphoreType.DMA((12,))],
         compiler_params=pltpu.CompilerParams(vmem_limit_bytes=16 * MIB),
-        cost_estimate=pl.CostEstimate(flops=0, bytes_accessed=6 * MIB, transcendentals=0),
+        cost_estimate=pl.CostEstimate(flops=0, bytes_accessed=0, transcendentals=0),
         name="stage_weights",
     )(order, *weights, after)
 
@@ -169,7 +170,13 @@
 
 def half_sums(own, core, weights, after):
     shapes = [shape(own.shape, F32)] * 3
-    return call(half_kernel, "half_sums", 3, shapes, (own, core, *weights), after)
+    return call(half_kernel, "half_sums", 0, shapes, (own, core, *weights), after)
+
+
+def near_kernel(x0, x1, x2, x3, wq, wk, wv, *outs):
+    everything = slice(0, x0.shape[0])
+    for w, out in zip((wq, wk, wv), outs):
+        out[...] = gathered((x0, x1, x2, x3), everything, w)
 
 
 def halo_kernel(x0, x1, x2, x3, wk, wv, out_ref):
@@ -250,20 +257,15 @@
     return list(zip(outs[: len(sizes)], outs[len(sizes) :]))
 
 
-def column_kernel(pos_ref, x2, x3, hq, hk, hv, wq, wk, wv, *rest):
-    refs, scratch = rest[:-3], rest[-3:]
-    owners, message, _ = scratch[0].shape
-    out_refs = refs[-owners:]
-    size = HEADS * message + 16
-    base = out_refs[0].shape[0] - size
-    for old, new in zip(refs[:-owners], out_refs):
-        new[:base, :] = old[...]
+def column_kernel(pos_ref, x2, x3, hq, hk, hv, wq, wk, wv, nq, nk, nv, *rest):
+    out_refs, scratch = rest[:-3], rest[-3:]
+    owners, message, width = scratch[0].shape
     groups = message // (ROWS * SUB)
-    width = x2.shape[1]
-    for h, w, a in zip((hq, hk, hv), (wq, wk, wv), scratch):
+    for h, w, near, a in zip((hq, hk, hv), (wq, wk, wv), (nq, nk, nv), scratch):
         total = h[...] + dot(x2[...], w[2 * width : 3 * width, :])
         total = total + dot(x3[...], w[3 * width :, :])
-        a[...] = total.astype(BF16).reshape(a.shape)
+        a[:NEAR] = near[...].reshape(NEAR, message, width)
+        a[NEAR:] = total.astype(BF16).reshape(owners - NEAR, message, width)
     part = ROWS * SUB
     size = owners * part
 
@@ -282,7 +284,7 @@
             q, k, v = (a[:, at, cols].reshape(size, DH) for a in scratch)
             p, total, lse = softmax_columns(jnp.where(earlier, dot_t(k, q), -1e30))
             o = (dot_l(v, p.astype(BF16)) * (1.0 / total)).T.astype(BF16)
-            to = base + h * message + g * part
+            to = h * message + g * part
             rows = slice(to, to + part)
             for n in range(owners):
                 out_refs[n][rows, :] = o[n * part : (n + 1) * part]
@@ -296,17 +298,17 @@
         mid = (x - hi).astype(BF16).astype(F32)
         lo = x - hi - mid
         tail = jnp.concatenate([jnp.where(upper, hi, lo), jnp.where(upper, mid, 0.0)], 0)
-        to = base + HEADS * message
+        to = HEADS * message
         out_refs[n][to : to + 16, :] = tail.astype(BF16)
 
 
-def column_part(pos, across, halves, weights, earlier, owners):
+def column_part(pos, across, halves, weights, near, owners, after):
     tokens, width = across.shape
-    message = tokens // owners
-    rows = HEADS * message + 16 + (earlier[0].shape[0] if earlier else 0)
+    message = tokens // (owners - NEAR)
+    shapes = [shape((HEADS * message + 16, DH))] * owners
     scratch = [pltpu.VMEM((owners, message, width), BF16)] * 3
-    args = (pos, across, swap(across, 1), *halves, *weights, *earlier)
-    return call(column_kernel, "column_part", 0, [shape((rows, DH))] * owners, args, (), scratch)
+    args = (pos, across, swap(across, 1), *halves, *weights, *near)
+    return call(column_kernel, "column_part", 0, shapes, args, after, scratch)
 
 
 def mix_kernel(share, pos_ref, *refs):
@@ -401,7 +403,7 @@
         input_output_aliases={3: 0} if earlier else {},
         scratch_shapes=[pltpu.VMEM(keep.shape, BF16), pltpu.SemaphoreType.DMA((len(share),))],
         compiler_params=pltpu.CompilerParams(vmem_limit_bytes=16 * MIB),
-        cost_estimate=pl.CostEstimate(flops=int(1.1e9), bytes_accessed=MIB, transcendentals=0),
+        cost_estimate=pl.CostEstimate(flops=int(1.1e9), bytes_accessed=0, transcendentals=0),
         name="join",
     )(pos, keep, got, *earlier)
 
@@ -430,37 +432,38 @@
     across = swap(tokens, 2)
     block_tokens, sent = pack(pos, tokens, owners)
     messages = exchange(sent)
-    part = ROWS * SUB
-    classes = [
-        jnp.concatenate([m[chunk[0] * part : (chunk[-1] + 1) * part] for m in messages], 0)
-        for chunk in CHUNKS
-    ]
-    across = fence(across, classes[0])
-    pieces = (block_tokens, swap(fence(block_tokens, classes[0]), 1), across, swap(across, 1))
+    near_own = jnp.concatenate(messages[:NEAR], 0)
+    near_core, near_across = swap(near_own, 1), swap(near_own, 2)
+    w_other = swap(w_out, 1)
+    far_own = jnp.concatenate(messages[NEAR:], 0)
+    far_core, far_across = swap(far_own, 1), swap(far_own, 2)
     weights = stage(order, (w_query, w_key, w_value), messages[1])
-    w_other = swap(w_out, 1)
+    block_core = swap(fence(block_tokens, near_own, far_own), 1)
+    across = fence(across, near_across, far_own)
+    pieces = (block_tokens, block_core, across, swap(across, 1))
     own_halo = call(
         halo_kernel, "project_halo", 1.5, shape((2 * STRIDE, width)), (*pieces, *weights[1:])
     )
-    first = classes[0]
-    first_core, first_across = swap(first, 1), swap(first, 2)
     halo = lax.ppermute(own_halo, "seq", [(i, i + 1) for i in range(owners - 1)])
     q, k, v = call(
         project_kernel,
         "project_block",
-        6,
+        0,
         [shape((rows, width))] * 3,
         (*pieces, *weights, own_halo),
-        (w_other,),
-    )
-    second_core = swap(classes[1], 1)
-    first_half = half_sums(first, first_core, weights, (q,))
-    second_half = half_sums(classes[1], second_core, weights, (first_half[0],))
-    first_across = fence(first_across, halo, second_half[0])
-    second_across = swap(fence(classes[1], first_across), 2)
-    columns = column_part(pos, first_across, first_half, weights, (), owners)
-    second_across = fence(second_across, columns[0])
-    columns = column_part(pos, second_across, second_half, weights, columns, owners)
+        (far_own,),
+    )
+    near = call(
+        near_kernel,
+        "project_near",
+        0,
+        [shape(near_own.shape)] * 3,
+        (near_own, near_core, near_across, swap(near_across, 1), *weights),
+        (q,),
+    )
+    far_half = half_sums(far_own, far_core, weights, (near[0],))
+    far_across = fence(far_across, near[0], halo)
+    columns = column_part(pos, far_across, far_half, weights, near, owners, (w_other,))
     locals_ = local_part(pos, q, k, v, halo, owners, (columns[0],))
     columns = exchange(columns)
     sums, after = [], ()

time: 125 us -> 122 us (0.976)
  waiting for transfers between devices: 41.2 us -> 45.9 us
  starting transfers between devices: 41.7 us -> 38 us
  local copies, waits for them, and re-layouts: 1.91 us -> 0.17 us
  Pallas kernels: 39.1 us -> 37.6 us
    ppermute x14, starting transfers between devices: 31.3 us -> 26.9 us  [move(): lax.ppermute(value, 'seq', [(i, i ^ k) for i in range(peers)])]
    ppermute x14, waiting for transfers between devices: 20.3 us -> 22.4 us  [move(): lax.ppermute(value, 'seq', [(i, i ^ k) for i in range(peers)])]
    unnamed x23 -> x15, local copies, waits for them, and re-layouts: 1.89 us -> 0.15 us
    pallas_call x11 -> x10, Pallas kernels: 33.3 us -> 31.7 us  [call(): pl.pallas_call(run, in_specs=specs + [ANYWHERE] * extra, out_specs=jax.tr...]
    ppermute x1, waiting for transfers between devices: 0.55 us -> 2.03 us  [chunked(): lax.ppermute(own_halo, 'seq', [(i, i + 1) for i in range(owners - 1)])]
  transfers between devices with their start and end apart: 29 -> 29, of which waited for: 16 -> 14; matrix products, arithmetic and copies ran while one was open for 0% -> 0% of each run, Pallas kernels for 26% -> 22%
where the time goes in v13:
time: 122 us
  waiting for transfers between devices  45.9 us (38%)
  starting transfers between devices  38 us (31%)
  Pallas kernels  37.6 us (31%)
    pallas_call x10, Pallas kernels, call(): pl.pallas_call(run, in_specs=specs + [ANYWHERE] * extra, out_specs=jax.tr...  31.7 us
    ppermute x14, starting transfers between devices, move(): lax.ppermute(value, 'seq', [(i, i ^ k) for i in range(peers)])  26.9 us
    ppermute x14, waiting for transfers between devices, move(): lax.ppermute(value, 'seq', [(i, i ^ k) for i in range(peers)])  22.4 us
    ppermute x14, waiting for transfers between devices, swap(): return lax.ppermute(value, 'head', [(i, i ^ distance) for i in range(4)])  21.5 us
    ppermute x14, starting transfers between devices, swap(): return lax.ppermute(value, 'head', [(i, i ^ distance) for i in range(4)])  7.43 us
    ppermute x1, starting transfers between devices, chunked(): lax.ppermute(own_halo, 'seq', [(i, i + 1) for i in range(owners - 1)])  3.64 us
    pallas_call x2, Pallas kernels, join(): pl.pallas_call(functools.partial(join_kernel, share), in_specs=[IN_SMEM,...  2.91 us
  transfers between devices with their start and end apart: 29, of which 14 were waited for; matrix products, arithmetic and copies ran while one was open for 0% of the time, Pallas kernels for 22%

profile of v13, /device:TPU:0, one launch (start us, length us, event | category | flops | bytes accessed | tf_op | source)
XLA Modules:
  0.0 122.2 jit_solution(13172999810420803378)
XLA Ops:
  0.0 2.9 %collective-permute-start.8 = (bf16[1024,512]{1,0:T(8,128)(2,1)}, bf16[1024,512]{1,0:T(8,128)(2,1)S(1)}, u32[]{:S(2)}, u32[]{:S(2)}) collective-permute-start(bf16[1024,512]{1,0:T(8,128)(2,1)} %tok_hbm.1), channel_id=1, source_target_pairs={{0,2},{1,3},{2,0},{3,1},{4,6},{5,7},{6,4},{7,5},{8,10},{9,11},{10,... | collective-permute-start | bytes 3145736 | tf_op jit(solution)/shard_map/ppermute | solution.py:412
  3.0 1.8 %pack_tokens.1 = (bf16[1024,512]{1,0:T(8,128)(2,1)S(1)}, bf16[128,512]{1,0:T(8,128)(2,1)S(1)}, bf16[128,512]{1,0:T(8,128)(2,1)S(1)}, bf16[128,512]{1,0:T(8,128)(...) custom-call(s32[3]{0:T(128)S(1)} %pad_add_fusion.pos_ref.refs_0_, ...), custom_call_target="tpu_custom_call" | custom-call | bytes 2097152 | tf_op jit(solution)/shard_map/pack_tokens/pallas_call | solution.py:113
  8.4 2.6 %collective-permute-start.3 = (bf16[128,512]{1,0:T(8,128)(2,1)S(1)}, bf16[128,512]{1,0:T(8,128)(2,1)S(1)}, u32[]{:S(2)}, u32[]{:S(2)}) collective-permute-start(bf16[128,512]{1,0:T(8,128)(2,1)S(1)} %get-tuple-element.49), channel_id=1, source_target_pairs={{0,16},{4,20},{8,24},{12,28},{16,0},{20,4},{24,8},{28,12},{1,17},{... | collective-permute-start | bytes 393224 | tf_op jit(solution)/shard_map/ppermute | solution.py:419
  11.0 4.3 %collective-permute-done.1 = bf16[128,512]{1,0:T(8,128)(2,1)S(1)} collective-permute-done((bf16[128,512]{1,0:T(8,128)(2,1)S(1)}, bf16[128,512]{1,0:T(8,128)(2,1)S(1)}, u32[]{:S(2)}, u32[]{:S(2)}) %collective-permute-start.1) | collective-permute-done | bytes 131104 | tf_op jit(solution)/shard_map/ppermute | solution.py:419
  17.2 2.3 %collective-permute-start.4 = (bf16[128,512]{1,0:T(8,128)(2,1)S(1)}, bf16[128,512]{1,0:T(8,128)(2,1)S(1)}, u32[]{:S(2)}, u32[]{:S(2)}) collective-permute-start(bf16[128,512]{1,0:T(8,128)(2,1)S(1)} %get-tuple-element.50), channel_id=1, source_target_pairs={{0,20},{4,16},{8,28},{12,24},{16,4},{20,0},{24,12},{28,8},{1,21},{... | collective-permute-start | bytes 393224 | tf_op jit(solution)/shard_map/ppermute | solution.py:419
  20.9 3.1 %collective-permute-start.6 = (bf16[128,512]{1,0:T(8,128)(2,1)S(1)}, bf16[128,512]{1,0:T(8,128)(2,1)S(1)}, u32[]{:S(2)}, u32[]{:S(2)}) collective-permute-start(bf16[128,512]{1,0:T(8,128)(2,1)S(1)} %get-tuple-element.52), channel_id=1, source_target_pairs={{0,28},{4,24},{8,20},{12,16},{16,12},{20,8},{24,4},{28,0},{1,29},{... | collective-permute-start | bytes 393224 | tf_op jit(solution)/shard_map/ppermute | solution.py:419
  24.0 7.4 %collective-permute-done.4 = bf16[128,512]{1,0:T(8,128)(2,1)S(1)} collective-permute-done((bf16[128,512]{1,0:T(8,128)(2,1)S(1)}, bf16[128,512]{1,0:T(8,128)(2,1)S(1)}, u32[]{:S(2)}, u32[]{:S(2)}) %collective-permute-start.4) | collective-permute-done | bytes 131104 | tf_op jit(solution)/shard_map/ppermute | solution.py:419
  31.6 6.0 %collective-permute-done.9.refs_1_.refs_2_ = bf16[512,512]{1,0:T(8,128)(2,1)S(1)} collective-permute-done((bf16[512,512]{1,0:T(8,128)(2,1)S(1)}, bf16[512,512]{1,0:T(8,128)(2,1)S(1)}, u32[]{:S(2)}, u32[]{:S(2)}) %collective-permute-start.9) | collective-permute-done | bytes 524320 | tf_op jit(solution)/shard_map/ppermute | solution.py:412
  38.1 1.7 %collective-permute-start.12 = (bf16[512,512]{1,0:T(8,128)(2,1)S(1)}, bf16[512,512]{1,0:T(8,128)(2,1)S(1)}, u32[]{:S(2)}, u32[]{:S(2)}) collective-permute-start(bf16[512,512]{1,0:T(8,128)(2,1)S(1)} %constant_dynamic-update-slice_fusion.4.refs_2_.refs_8_.refs_0_), channel_id=1, source_target_pairs={{0,2},{1,3},{2,0},{3,1},{4,6},{5,7},{6,4},{7,5},{8,10},{9,11},{10,... | collective-permute-start | bytes 1572872 | tf_op jit(solution)/shard_map/ppermute | solution.py:412
  42.8 3.6 %collective-permute-start.11 = (bf16[512,512]{1,0:T(8,128)(2,1)S(1)}, bf16[512,512]{1,0:T(8,128)(2,1)S(1)}, u32[]{:S(2)}, u32[]{:S(2)}) collective-permute-start(bf16[512,512]{1,0:T(8,128)(2,1)S(1)} %project_halo.1.refs_7_), channel_id=1, source_target_pairs={{0,4},{4,8},{8,12},{12,16},{16,20},{20,24},{24,28},{1,5},{5,9},{9,... | collective-permute-start | bytes 1572872 | tf_op jit(solution)/shard_map/ppermute | solution.py:447
  46.4 5.6 %project_block.1 = (bf16[1024,512]{1,0:T(8,128)(2,1)S(1)}, bf16[1024,512]{1,0:T(8,128)(2,1)S(1)}, bf16[1024,512]{1,0:T(8,128)(2,1)S(1)}) custom-call(bf16[1024,512]{1,0:T(8,128)(2,1)S(1)} %get-tuple-element.44.refs_0_, bf16[1024,512]{1,0:T(8,128)(2,1)S(1)} %collective-permute-done.7.refs_1_, bf16[1024,512]{1,0:T(8,128)(2,1)S(1)} %fence.4.refs_2_, ...), custom_call_target="tpu_custom_call" | custom-call | tf_op jit(solution)/shard_map/project_block/pallas_call | solution.py:39
  52.1 3.4 %project_near.1 = (bf16[512,512]{1,0:T(8,128)(2,1)S(1)}, bf16[512,512]{1,0:T(8,128)(2,1)S(1)}, bf16[512,512]{1,0:T(8,128)(2,1)S(1)}) custom-call(bf16[512,512]{1,0:T(8,128)(2,1)S(1)} %constant_dynamic-update-slice_fusion.refs_1_.refs_0_, bf16[512,512]{1,0:T(8,128)(2,1)S(1)} %collective-permute-done.13.refs_1_, ...), custom_call_target="tpu_custom_call" | custom-call | tf_op jit(solution)/shard_map/project_near/pallas_call | solution.py:39
  55.5 2.0 %collective-permute-done.11.refs_2_.refs_4_ = bf16[512,512]{1,0:T(8,128)(2,1)S(1)} collective-permute-done((bf16[512,512]{1,0:T(8,128)(2,1)S(1)}, bf16[512,512]{1,0:T(8,128)(2,1)S(1)}, u32[]{:S(2)}, u32[]{:S(2)}) %collective-permute-start.11) | collective-permute-done | bytes 524320 | tf_op jit(solution)/shard_map/ppermute | solution.py:447
  57.6 1.8 %half_sums.1 = (f32[512,512]{1,0:T(8,128)S(1)}, f32[512,512]{1,0:T(8,128)S(1)}, f32[512,512]{1,0:T(8,128)S(1)}) custom-call(bf16[512,512]{1,0:T(8,128)(2,1)S(1)} %constant_dynamic-update-slice_fusion.4.refs_2_.refs_8_.refs_0_, bf16[512,512]{1,0:T(8,128)(2,1)S(1)} %collective-permute-done.16.refs_1_, ...), custom_call_target="tpu_custom_call" | custom-call | tf_op jit(solution)/shard_map/half_sums/pallas_call | solution.py:39
  59.5 7.2 %column_part.1 = (bf16[528,128]{1,0:T(8,128)(2,1)S(1)}, bf16[528,128]{1,0:T(8,128)(2,1)S(1)}, bf16[528,128]{1,0:T(8,128)(2,1)S(1)}, bf16[528,128]{1,0:T(8,128)(2...) custom-call(s32[3]{0:T(128)S(1)} %pad_add_fusion.pos_ref.refs_0_, ...), custom_call_target="tpu_custom_call" | custom-call | tf_op jit(solution)/shard_map/column_part/pallas_call | solution.py:39
  66.7 4.5 %collective-permute-start.20 = (bf16[528,128]{1,0:T(8,128)(2,1)S(1)}, bf16[528,128]{1,0:T(8,128)(2,1)S(1)}, u32[]{:S(2)}, u32[]{:S(2)}) collective-permute-start(bf16[528,128]{1,0:T(8,128)(2,1)S(1)} %get-tuple-element.70), channel_id=1, source_target_pairs={{0,16},{4,20},{8,24},{12,28},{16,0},{20,4},{24,8},{28,12},{1,17},{... | collective-permute-start | bytes 405512 | tf_op jit(solution)/shard_map/ppermute | solution.py:419
  72.7 1.8 %collective-permute-start.23 = (bf16[528,128]{1,0:T(8,128)(2,1)S(1)}, bf16[528,128]{1,0:T(8,128)(2,1)S(1)}, u32[]{:S(2)}, u32[]{:S(2)}) collective-permute-start(bf16[528,128]{1,0:T(8,128)(2,1)S(1)} %get-tuple-element.73), channel_id=1, source_target_pairs={{0,8},{4,12},{8,0},{12,4},{16,24},{20,28},{24,16},{28,20},{1,9},{5... | collective-permute-start | bytes 405512 | tf_op jit(solution)/shard_map/ppermute | solution.py:419
  75.1 6.0 %local_part.1 = (f32[8,128,512]{2,1,0:T(8,128)S(1)}, f32[128,128]{1,0:T(8,128)S(1)}) custom-call(s32[3]{0:T(128)S(1)} %pad_add_fusion.pos_ref.refs_0_, bf16[1024,512]{1,0:T(8,128)(2,1)S(1)} %get-tuple-element.56.refs_7_.refs_1_, bf16[1024,512]{1,0:T(8,128)(2,1)S(1)} %get-tuple-element.57.refs_2_, bf16[1024,512]{1,0:T(8,128)(2,1)S(1)} %get-tuple-element.58.refs_3_, ...), custom_call_target="tpu_custom_call" | custom-call | flops 5500000256 | tf_op jit(solution)/shard_map/local_part/pallas_call | solution.py:39
  81.5 2.8 %collective-permute-done.21.refs_4_ = bf16[528,128]{1,0:T(8,128)(2,1)S(1)} collective-permute-done((bf16[528,128]{1,0:T(8,128)(2,1)S(1)}, bf16[528,128]{1,0:T(8,128)(2,1)S(1)}, u32[]{:S(2)}, u32[]{:S(2)}) %collective-permute-start.21) | collective-permute-done | bytes 135200 | tf_op jit(solution)/shard_map/ppermute | solution.py:419
  87.5 4.7 %collective-permute-start.18 = (bf16[528,128]{1,0:T(8,128)(2,1)S(1)}, bf16[528,128]{1,0:T(8,128)(2,1)S(1)}, u32[]{:S(2)}, u32[]{:S(2)}) collective-permute-start(bf16[528,128]{1,0:T(8,128)(2,1)S(1)} %get-tuple-element.68), channel_id=1, source_target_pairs={{0,24},{4,28},{8,16},{12,20},{16,8},{20,12},{24,0},{28,4},{1,25},{... | collective-permute-start | bytes 405512 | tf_op jit(solution)/shard_map/ppermute | solution.py:419
  93.1 2.4 %out_project.2 = (bf16[192,2048]{1,0:T(8,128)(2,1)S(1)}, f32[192,2048]{1,0:T(8,128)S(1)}) custom-call(s32[3]{0:T(128)S(1)} %pad_add_fusion.pos_ref.refs_0_, bf16[2,192,512]{2,1,0:T(8,128)(2,1)S(1)} %get-tuple-element.75.refs_1_, bf16[2,192,512]{2,1,0:T(8,128)(2,1)S(1)} %collective-permute-done.25.refs_2_, bf16[512,2048]{1,0:T(8,128)(2,1)S(1)} %copy-done.3, ...), custom_call_target="tpu_custom_call" | custom-call | flops 2200000000 | tf_op jit(solution)/shard_map/out_project/pallas_call | solution.py:39
  96.5 4.1 %collective-permute-done.19.refs_4_ = bf16[528,128]{1,0:T(8,128)(2,1)S(1)} collective-permute-done((bf16[528,128]{1,0:T(8,128)(2,1)S(1)}, bf16[528,128]{1,0:T(8,128)(2,1)S(1)}, u32[]{:S(2)}, u32[]{:S(2)}) %collective-permute-start.19) | collective-permute-done | bytes 135200 | tf_op jit(solution)/shard_map/ppermute | solution.py:419
  105.0 11.0 %collective-permute-done.28.got = bf16[192,2048]{1,0:T(8,128)(2,1)S(1)} collective-permute-done((bf16[192,2048]{1,0:T(8,128)(2,1)S(1)}, bf16[192,2048]{1,0:T(8,128)(2,1)S(1)}, u32[]{:S(2)}, u32[]{:S(2)}) %collective-permute-start.28) | collective-permute-done | bytes 786464 | tf_op jit(solution)/shard_map/ppermute | solution.py:412
  117.6 3.1 %collective-permute-done.27.got = bf16[64,2048]{1,0:T(8,128)(2,1)S(1)} collective-permute-done((bf16[64,2048]{1,0:T(8,128)(2,1)S(1)}, bf16[64,2048]{1,0:T(8,128)(2,1)S(1)}, u32[]{:S(2)}, u32[]{:S(2)}) %collective-permute-start.27) | collective-permute-done | bytes 262176 | tf_op jit(solution)/shard_map/ppermute | solution.py:412
  (70 shorter events, 25.6 us)
Async XLA Ops:
  0.0 37.5 %collective-permute-start.8 = (bf16[1024,512]{1,0:T(8,128)(2,1)}, bf16[1024,512]{1,0:T(8,128)(2,1)S(1)}, u32[]{:S(2)}, u32[]{:S(2)}) collective-permute-start(bf16[1024,512]{1,0:T(8,128)(2,1)} %tok_hbm.1), channel_id=1, source_target_pairs={{0,2},{1,3},{2,0},{3,1},{4,6},{5,7},{6,4},{7,5},{8,10},{9,11},{10,... | collective-permute-start | bytes 3145736 | tf_op jit(solution)/shard_map/ppermute | solution.py:412
  4.9 6.2 %collective-permute-start = (bf16[128,512]{1,0:T(8,128)(2,1)S(1)}, bf16[128,512]{1,0:T(8,128)(2,1)S(1)}, u32[]{:S(2)}, u32[]{:S(2)}) collective-permute-start(bf16[128,512]{1,0:T(8,128)(2,1)S(1)} %get-tuple-element.46), channel_id=1, source_target_pairs={{0,4},{4,0},{8,12},{12,8},{16,20},{20,16},{24,28},{28,24},{1,5},{5... | collective-permute-start | bytes 393224 | tf_op jit(solution)/shard_map/ppermute | solution.py:419
  6.4 8.9 %collective-permute-start.1 = (bf16[128,512]{1,0:T(8,128)(2,1)S(1)}, bf16[128,512]{1,0:T(8,128)(2,1)S(1)}, u32[]{:S(2)}, u32[]{:S(2)}) collective-permute-start(bf16[128,512]{1,0:T(8,128)(2,1)S(1)} %get-tuple-element.47), channel_id=1, source_target_pairs={{0,8},{4,12},{8,0},{12,4},{16,24},{20,28},{24,16},{28,20},{1,9},{5... | collective-permute-start | bytes 393224 | tf_op jit(solution)/shard_map/ppermute | solution.py:419
  8.0 9.0 %collective-permute-start.2 = (bf16[128,512]{1,0:T(8,128)(2,1)S(1)}, bf16[128,512]{1,0:T(8,128)(2,1)S(1)}, u32[]{:S(2)}, u32[]{:S(2)}) collective-permute-start(bf16[128,512]{1,0:T(8,128)(2,1)S(1)} %get-tuple-element.48), channel_id=1, source_target_pairs={{0,12},{4,8},{8,4},{12,0},{16,28},{20,24},{24,20},{28,16},{1,13},{... | collective-permute-start | bytes 393224 | tf_op jit(solution)/shard_map/ppermute | solution.py:419
  8.4 12.4 %collective-permute-start.3 = (bf16[128,512]{1,0:T(8,128)(2,1)S(1)}, bf16[128,512]{1,0:T(8,128)(2,1)S(1)}, u32[]{:S(2)}, u32[]{:S(2)}) collective-permute-start(bf16[128,512]{1,0:T(8,128)(2,1)S(1)} %get-tuple-element.49), channel_id=1, source_target_pairs={{0,16},{4,20},{8,24},{12,28},{16,0},{20,4},{24,8},{28,12},{1,17},{... | collective-permute-start | bytes 393224 | tf_op jit(solution)/shard_map/ppermute | solution.py:419
  17.0 20.6 %collective-permute-start.9 = (bf16[512,512]{1,0:T(8,128)(2,1)S(1)}, bf16[512,512]{1,0:T(8,128)(2,1)S(1)}, u32[]{:S(2)}, u32[]{:S(2)}) collective-permute-start(bf16[512,512]{1,0:T(8,128)(2,1)S(1)} %constant_dynamic-update-slice_fusion.refs_1_.refs_0_), channel_id=1, source_target_pairs={{0,2},{1,3},{2,0},{3,1},{4,6},{5,7},{6,4},{7,5},{8,10},{9,11},{10,... | collective-permute-start | bytes 1572872 | tf_op jit(solution)/shard_map/ppermute | solution.py:412
  17.2 14.2 %collective-permute-start.4 = (bf16[128,512]{1,0:T(8,128)(2,1)S(1)}, bf16[128,512]{1,0:T(8,128)(2,1)S(1)}, u32[]{:S(2)}, u32[]{:S(2)}) collective-permute-start(bf16[128,512]{1,0:T(8,128)(2,1)S(1)} %get-tuple-element.50), channel_id=1, source_target_pairs={{0,20},{4,16},{8,28},{12,24},{16,4},{20,0},{24,12},{28,8},{1,21},{... | collective-permute-start | bytes 393224 | tf_op jit(solution)/shard_map/ppermute | solution.py:419
  19.4 12.0 %collective-permute-start.5 = (bf16[128,512]{1,0:T(8,128)(2,1)S(1)}, bf16[128,512]{1,0:T(8,128)(2,1)S(1)}, u32[]{:S(2)}, u32[]{:S(2)}) collective-permute-start(bf16[128,512]{1,0:T(8,128)(2,1)S(1)} %get-tuple-element.51), channel_id=1, source_target_pairs={{0,24},{4,28},{8,16},{12,20},{16,8},{20,12},{24,0},{28,4},{1,25},{... | collective-permute-start | bytes 393224 | tf_op jit(solution)/shard_map/ppermute | solution.py:419
  20.9 10.6 %collective-permute-start.6 = (bf16[128,512]{1,0:T(8,128)(2,1)S(1)}, bf16[128,512]{1,0:T(8,128)(2,1)S(1)}, u32[]{:S(2)}, u32[]{:S(2)}) collective-permute-start(bf16[128,512]{1,0:T(8,128)(2,1)S(1)} %get-tuple-element.52), channel_id=1, source_target_pairs={{0,28},{4,24},{8,20},{12,16},{16,12},{20,8},{24,4},{28,0},{1,29},{... | collective-permute-start | bytes 393224 | tf_op jit(solution)/shard_map/ppermute | solution.py:419
  31.5 9.5 %collective-permute-start.7 = (bf16[1024,512]{1,0:T(8,128)(2,1)S(1)}, bf16[1024,512]{1,0:T(8,128)(2,1)S(1)}, u32[]{:S(2)}, u32[]{:S(2)}) collective-permute-start(bf16[1024,512]{1,0:T(8,128)(2,1)S(1)} %fence.3), channel_id=1, source_target_pairs={{0,1},{1,0},{2,3},{3,2},{4,5},{5,4},{6,7},{7,6},{8,9},{9,8},{10,11... | collective-permute-start | bytes 3145736 | tf_op jit(solution)/shard_map/ppermute | solution.py:412
  37.6 21.8 %collective-permute-start.17 = (bf16[512,2048]{1,0:T(8,128)(2,1)S(1)}, bf16[512,2048]{1,0:T(8,128)(2,1)S(1)}, u32[]{:S(2)}, u32[]{:S(2)}) collective-permute-start(bf16[512,2048]{1,0:T(8,128)(2,1)S(1)} %copy-done.3), channel_id=1, source_target_pairs={{0,1},{1,0},{2,3},{3,2},{4,5},{5,4},{6,7},{7,6},{8,9},{9,8},{10,11... | collective-permute-start | bytes 6291464 | tf_op jit(solution)/shard_map/ppermute | solution.py:412
  38.1 17.5 %collective-permute-start.12 = (bf16[512,512]{1,0:T(8,128)(2,1)S(1)}, bf16[512,512]{1,0:T(8,128)(2,1)S(1)}, u32[]{:S(2)}, u32[]{:S(2)}) collective-permute-start(bf16[512,512]{1,0:T(8,128)(2,1)S(1)} %constant_dynamic-update-slice_fusion.4.refs_2_.refs_8_.refs_0_), channel_id=1, source_target_pairs={{0,2},{1,3},{2,0},{3,1},{4,6},{5,7},{6,4},{7,5},{8,10},{9,11},{10,... | collective-permute-start | bytes 1572872 | tf_op jit(solution)/shard_map/ppermute | solution.py:412
  39.8 12.2 %collective-permute-start.13 = (bf16[512,512]{1,0:T(8,128)(2,1)S(1)}, bf16[512,512]{1,0:T(8,128)(2,1)S(1)}, u32[]{:S(2)}, u32[]{:S(2)}) collective-permute-start(bf16[512,512]{1,0:T(8,128)(2,1)S(1)} %constant_dynamic-update-slice_fusion.refs_1_.refs_0_), channel_id=1, source_target_pairs={{0,1},{1,0},{2,3},{3,2},{4,5},{5,4},{6,7},{7,6},{8,9},{9,8},{10,11... | collective-permute-start | bytes 1572872 | tf_op jit(solution)/shard_map/ppermute | solution.py:412
  41.0 11.1 %collective-permute-start.14 = (bf16[512,512]{1,0:T(8,128)(2,1)S(1)}, bf16[512,512]{1,0:T(8,128)(2,1)S(1)}, u32[]{:S(2)}, u32[]{:S(2)}) collective-permute-start(bf16[512,512]{1,0:T(8,128)(2,1)S(1)} %collective-permute-done.9.refs_1_.refs_2_), channel_id=1, source_target_pairs={{0,1},{1,0},{2,3},{3,2},{4,5},{5,4},{6,7},{7,6},{8,9},{9,8},{10,11... | collective-permute-start | bytes 1572872 | tf_op jit(solution)/shard_map/ppermute | solution.py:412
  42.8 14.8 %collective-permute-start.11 = (bf16[512,512]{1,0:T(8,128)(2,1)S(1)}, bf16[512,512]{1,0:T(8,128)(2,1)S(1)}, u32[]{:S(2)}, u32[]{:S(2)}) collective-permute-start(bf16[512,512]{1,0:T(8,128)(2,1)S(1)} %project_halo.1.refs_7_), channel_id=1, source_target_pairs={{0,4},{4,8},{8,12},{12,16},{16,20},{20,24},{24,28},{1,5},{5,9},{9,... | collective-permute-start | bytes 1572872 | tf_op jit(solution)/shard_map/ppermute | solution.py:447
  66.7 14.8 %collective-permute-start.20 = (bf16[528,128]{1,0:T(8,128)(2,1)S(1)}, bf16[528,128]{1,0:T(8,128)(2,1)S(1)}, u32[]{:S(2)}, u32[]{:S(2)}) collective-permute-start(bf16[528,128]{1,0:T(8,128)(2,1)S(1)} %get-tuple-element.70), channel_id=1, source_target_pairs={{0,16},{4,20},{8,24},{12,28},{16,0},{20,4},{24,8},{28,12},{1,17},{... | collective-permute-start | bytes 405512 | tf_op jit(solution)/shard_map/ppermute | solution.py:419
  71.2 13.1 %collective-permute-start.21 = (bf16[528,128]{1,0:T(8,128)(2,1)S(1)}, bf16[528,128]{1,0:T(8,128)(2,1)S(1)}, u32[]{:S(2)}, u32[]{:S(2)}) collective-permute-start(bf16[528,128]{1,0:T(8,128)(2,1)S(1)} %get-tuple-element.71), channel_id=1, source_target_pairs={{0,20},{4,16},{8,28},{12,24},{16,4},{20,0},{24,12},{28,8},{1,21},{... | collective-permute-start | bytes 405512 | tf_op jit(solution)/shard_map/ppermute | solution.py:419
  71.6 12.7 %collective-permute-start.22 = (bf16[528,128]{1,0:T(8,128)(2,1)S(1)}, bf16[528,128]{1,0:T(8,128)(2,1)S(1)}, u32[]{:S(2)}, u32[]{:S(2)}) collective-permute-start(bf16[528,128]{1,0:T(8,128)(2,1)S(1)} %get-tuple-element.72), channel_id=1, source_target_pairs={{0,4},{4,0},{8,12},{12,8},{16,20},{20,16},{24,28},{28,24},{1,5},{5... | collective-permute-start | bytes 405512 | tf_op jit(solution)/shard_map/ppermute | solution.py:419
  72.7 11.6 %collective-permute-start.23 = (bf16[528,128]{1,0:T(8,128)(2,1)S(1)}, bf16[528,128]{1,0:T(8,128)(2,1)S(1)}, u32[]{:S(2)}, u32[]{:S(2)}) collective-permute-start(bf16[528,128]{1,0:T(8,128)(2,1)S(1)} %get-tuple-element.73), channel_id=1, source_target_pairs={{0,8},{4,12},{8,0},{12,4},{16,24},{20,28},{24,16},{28,20},{1,9},{5... | collective-permute-start | bytes 405512 | tf_op jit(solution)/shard_map/ppermute | solution.py:419
  74.5 11.2 %collective-permute-start.24 = (bf16[528,128]{1,0:T(8,128)(2,1)S(1)}, bf16[528,128]{1,0:T(8,128)(2,1)S(1)}, u32[]{:S(2)}, u32[]{:S(2)}) collective-permute-start(bf16[528,128]{1,0:T(8,128)(2,1)S(1)} %get-tuple-element.74), channel_id=1, source_target_pairs={{0,12},{4,8},{8,4},{12,0},{16,28},{20,24},{24,20},{28,16},{1,13},{... | collective-permute-start | bytes 405512 | tf_op jit(solution)/shard_map/ppermute | solution.py:419
  87.5 9.0 %collective-permute-start.18 = (bf16[528,128]{1,0:T(8,128)(2,1)S(1)}, bf16[528,128]{1,0:T(8,128)(2,1)S(1)}, u32[]{:S(2)}, u32[]{:S(2)}) collective-permute-start(bf16[528,128]{1,0:T(8,128)(2,1)S(1)} %get-tuple-element.68), channel_id=1, source_target_pairs={{0,24},{4,28},{8,16},{12,20},{16,8},{20,12},{24,0},{28,4},{1,25},{... | collective-permute-start | bytes 405512 | tf_op jit(solution)/shard_map/ppermute | solution.py:419
  92.2 8.4 %collective-permute-start.19 = (bf16[528,128]{1,0:T(8,128)(2,1)S(1)}, bf16[528,128]{1,0:T(8,128)(2,1)S(1)}, u32[]{:S(2)}, u32[]{:S(2)}) collective-permute-start(bf16[528,128]{1,0:T(8,128)(2,1)S(1)} %get-tuple-element.69), channel_id=1, source_target_pairs={{0,28},{4,24},{8,20},{12,16},{16,12},{20,8},{24,4},{28,0},{1,29},{... | collective-permute-start | bytes 405512 | tf_op jit(solution)/shard_map/ppermute | solution.py:419
  95.5 20.5 %collective-permute-start.28 = (bf16[192,2048]{1,0:T(8,128)(2,1)S(1)}, bf16[192,2048]{1,0:T(8,128)(2,1)S(1)}, u32[]{:S(2)}, u32[]{:S(2)}) collective-permute-start(bf16[192,2048]{1,0:T(8,128)(2,1)S(1)} %get-tuple-element.82), channel_id=1, source_target_pairs={{0,2},{1,3},{2,0},{3,1},{4,6},{5,7},{6,4},{7,5},{8,10},{9,11},{10,... | collective-permute-start | bytes 2359304 | tf_op jit(solution)/shard_map/ppermute | solution.py:412
  104.4 16.3 %collective-permute-start.27 = (bf16[64,2048]{1,0:T(8,128)(2,1)S(1)}, bf16[64,2048]{1,0:T(8,128)(2,1)S(1)}, u32[]{:S(2)}, u32[]{:S(2)}) collective-permute-start(bf16[64,2048]{1,0:T(8,128)(2,1)S(1)} %get-tuple-element.81), channel_id=1, source_target_pairs={{0,2},{1,3},{2,0},{3,1},{4,6},{5,7},{6,4},{7,5},{8,10},{9,11},{10,... | collective-permute-start | bytes 786440 | tf_op jit(solution)/shard_map/ppermute | solution.py:412
  (9 other events, 60.4 us)

commit v14 on v13

--- a/solution.py
+++ b/solution.py
@@ -216,20 +216,26 @@
         lses = []
         here = slice(r * STRIDE, (r + 1) * STRIDE)
         back = slice((r - 1) * STRIDE, r * STRIDE)
-        for h in range(HEADS):
-            cols = slice(h * DH, (h + 1) * DH)
+        heads = [slice(h * DH, (h + 1) * DH) for h in range(HEADS)]
+        scores = []
+        for cols in heads:
             q = q_ref[here, cols]
-            k_prev = k_ref[back, cols] if r else halo_ref[:STRIDE, cols]
-            v_prev = v_ref[back, cols] if r else halo_ref[STRIDE:, cols]
-            s_prev = dot_t(k_prev, q)
+            s_prev = dot_t(k_ref[back, cols] if r else halo_ref[:STRIDE, cols], q)
             if r == 0:
                 s_prev = s_prev + low
-            p, total, lse = softmax_columns(jnp.where(current, dot_t(k_ref[here, cols], q), s_prev))
-            p_now = jnp.where(current, p, 0.0).astype(BF16)
-            p_prev = jnp.where(current, 0.0, p).astype(BF16)
-            o = dot_l(v_ref[here, cols], p_now) + dot_l(v_prev, p_prev)
-            o = (o * (1.0 / total)).T
+            scores.append(jnp.where(current, dot_t(k_ref[here, cols], q), s_prev))
+        parts = []
+        for p, total, lse in [softmax_columns(s) for s in scores]:
+            now = jnp.where(current, p, 0.0).astype(BF16)
+            before = jnp.where(current, 0.0, p).astype(BF16)
+            parts.append((now, before, 1.0 / total))
             lses.append(lse)
+        results = []
+        for cols, (now, before, share) in zip(heads, parts):
+            v_prev = v_ref[back, cols] if r else halo_ref[STRIDE:, cols]
+            results.append((dot_l(v_ref[here, cols], now) + dot_l(v_prev, before)) * share)
+        for cols, o in zip(heads, results):
+            o = o.T
             for d in range(owners):
                 for chunk, out_ref in zip(CHUNKS, out_refs):
                     for n, g in enumerate(chunk):
@@ -278,17 +284,20 @@
     stats = []
     for g in range(groups):
         at = slice(g * part, (g + 1) * part)
-        lses = []
-        for h in range(HEADS):
-            cols = slice(h * DH, (h + 1) * DH)
-            q, k, v = (a[:, at, cols].reshape(size, DH) for a in scratch)
-            p, total, lse = softmax_columns(jnp.where(earlier, dot_t(k, q), -1e30))
-            o = (dot_l(v, p.astype(BF16)) * (1.0 / total)).T.astype(BF16)
+        heads = [slice(h * DH, (h + 1) * DH) for h in range(HEADS)]
+        operands = [[a[:, at, cols].reshape(size, DH) for a in scratch] for cols in heads]
+        scores = [jnp.where(earlier, dot_t(k, q), -1e30) for q, k, _ in operands]
+        parts = [softmax_columns(s) for s in scores]
+        results = [
+            dot_l(v, p.astype(BF16)) * (1.0 / total)
+            for (_, _, v), (p, total, _) in zip(operands, parts)
+        ]
+        lses = [lse for _, _, lse in parts]
+        for h, o in enumerate(results):
+            o = o.T.astype(BF16)
             to = h * message + g * part
-            rows = slice(to, to + part)
             for n in range(owners):
-                out_refs[n][rows, :] = o[n * part : (n + 1) * part]
-            lses.append(lse)
+                out_refs[n][to : to + part, :] = o[n * part : (n + 1) * part]
         stats.append(jnp.concatenate(lses + lses, 0))
     upper = lax.broadcasted_iota(jnp.int32, (8, 128), 0) < HEADS
     blank = [jnp.zeros((8, 128 - message), F32)] if message < 128 else []
@@ -360,23 +369,20 @@
     return call(functools.partial(mix_kernel, share), "mix", 2, shapes, args, after, scratch)
 
 
-def out_kernel(pos_ref, a_ref, b_ref, wa_ref, wb_ref, send_ref, keep_ref):
-    tokens, columns = send_ref.shape
-    a = a_ref[...].reshape(2 * tokens, -1)
-    b = b_ref[...].reshape(2 * tokens, -1)
-    low_side = pos_ref[2] == 0
+def out_kernel(here, pos_ref, a_ref, b_ref, wa_ref, wb_ref, out_ref):
+    side = pos_ref[2] if here else 1 - pos_ref[2]
+    a, b = a_ref[side], b_ref[side]
     tile = 512
-    for n in range(0, columns, tile):
+    for n in range(0, out_ref.shape[1], tile):
         at = slice(n, n + tile)
         total = dot(a, wa_ref[:, at]) + dot(b, wb_ref[:, at])
-        send_ref[:, at] = jnp.where(low_side, total[tokens:], total[:tokens]).astype(BF16)
-        keep_ref[:, at] = jnp.where(low_side, total[:tokens], total[tokens:])
-
-
-def out_project(pos, own, other, w_own, w_other):
-    dims = (own.shape[1], w_own.shape[1])
-    shapes = [shape(dims), shape(dims, F32)]
-    return call(out_kernel, "out_project", 2, shapes, (pos, own, other, w_own, w_other))
+        out_ref[:, at] = total.astype(out_ref.dtype)
+
+
+def out_project(pos, here, own, other, w_own, w_other):
+    dims = shape((own.shape[1], w_own.shape[1]), F32 if here else BF16)
+    body = functools.partial(out_kernel, here)
+    return call(body, "out_project", 2, dims, (pos, own, other, w_own, w_other))
 
 
 def join_kernel(share, pos_ref, keep, got, *rest):
@@ -469,9 +475,11 @@
     sums, after = [], ()
     for share in SHARES:
         own, send = mix(pos, share, [columns[n] for n in share], locals_, after)
-        out, keep = out_project(pos, own, swap(send, 1), w_out, w_other)
+        other = swap(send, 1)
+        out = out_project(pos, False, own, other, w_out, w_other)
+        keep = out_project(pos, True, own, other, w_out, w_other)
         sums.append((keep, swap(out, 2)))
-        after = (keep,)
+        after = (out,)
     result = ()
     for share, (keep, got) in zip(SHARES, sums):
         result = (join(pos, share, keep, got, result),)

time: 122 us -> 119 us (0.975)
  Pallas kernels: 37.6 us -> 34.8 us
    ppermute x14, waiting for transfers between devices: 21.5 us -> 17.6 us  [swap(): return lax.ppermute(value, 'head', [(i, i ^ distance) for i in range(4)])]
    ppermute x14, waiting for transfers between devices: 22.4 us -> 26 us  [move(): lax.ppermute(value, 'seq', [(i, i ^ k) for i in range(peers)])]
    pallas_call x10 -> x12, Pallas kernels: 31.7 us -> 28.9 us  [call(): pl.pallas_call(run, in_specs=specs + [ANYWHERE] * extra, out_specs=jax.tr...]
  transfers between devices with their start and end apart: 29 -> 29, of which waited for: 14 -> 13; matrix products, arithmetic and copies ran while one was open for 0% -> 0% of each run, Pallas kernels for 22% -> 23%
where the time goes in v14:
time: 119 us
  waiting for transfers between devices  45.6 us (38%)
  starting transfers between devices  37.9 us (32%)
  Pallas kernels  34.8 us (29%)
    pallas_call x12, Pallas kernels, call(): pl.pallas_call(run, in_specs=specs + [ANYWHERE] * extra, out_specs=jax.tr...  28.9 us
    ppermute x14, starting transfers between devices, move(): lax.ppermute(value, 'seq', [(i, i ^ k) for i in range(peers)])  26.9 us
    ppermute x14, waiting for transfers between devices, move(): lax.ppermute(value, 'seq', [(i, i ^ k) for i in range(peers)])  26 us
    ppermute x14, waiting for transfers between devices, swap(): return lax.ppermute(value, 'head', [(i, i ^ distance) for i in range(4)])  17.6 us
    ppermute x14, starting transfers between devices, swap(): return lax.ppermute(value, 'head', [(i, i ^ distance) for i in range(4)])  7.42 us
    ppermute x1, starting transfers between devices, chunked(): lax.ppermute(own_halo, 'seq', [(i, i + 1) for i in range(owners - 1)])  3.64 us
    pallas_call x2, Pallas kernels, join(): pl.pallas_call(functools.partial(join_kernel, share), in_specs=[IN_SMEM,...  2.98 us
  transfers between devices with their start and end apart: 29, of which 13 were waited for; matrix products, arithmetic and copies ran while one was open for 0% of the time, Pallas kernels for 23%

profile of v14, /device:TPU:0, one launch (start us, length us, event | category | flops | bytes accessed | tf_op | source)
XLA Modules:
  0.0 119.1 jit_solution(4501372843386638835)
XLA Ops:
  0.0 2.9 %collective-permute-start.8 = (bf16[1024,512]{1,0:T(8,128)(2,1)}, bf16[1024,512]{1,0:T(8,128)(2,1)S(1)}, u32[]{:S(2)}, u32[]{:S(2)}) collective-permute-start(bf16[1024,512]{1,0:T(8,128)(2,1)} %tok_hbm.1), channel_id=1, source_target_pairs={{0,2},{1,3},{2,0},{3,1},{4,6},{5,7},{6,4},{7,5},{8,10},{9,11},{10,... | collective-permute-start | bytes 3145736 | tf_op jit(solution)/shard_map/ppermute | solution.py:418
  3.0 1.8 %pack_tokens.1 = (bf16[1024,512]{1,0:T(8,128)(2,1)S(1)}, bf16[128,512]{1,0:T(8,128)(2,1)S(1)}, bf16[128,512]{1,0:T(8,128)(2,1)S(1)}, bf16[128,512]{1,0:T(8,128)(...) custom-call(s32[3]{0:T(128)S(1)} %pad_add_fusion.pos_ref.refs_0_, ...), custom_call_target="tpu_custom_call" | custom-call | bytes 2097152 | tf_op jit(solution)/shard_map/pack_tokens/pallas_call | solution.py:113
  8.4 2.6 %collective-permute-start.3 = (bf16[128,512]{1,0:T(8,128)(2,1)S(1)}, bf16[128,512]{1,0:T(8,128)(2,1)S(1)}, u32[]{:S(2)}, u32[]{:S(2)}) collective-permute-start(bf16[128,512]{1,0:T(8,128)(2,1)S(1)} %get-tuple-element.45), channel_id=1, source_target_pairs={{0,16},{4,20},{8,24},{12,28},{16,0},{20,4},{24,8},{28,12},{1,17},{... | collective-permute-start | bytes 393224 | tf_op jit(solution)/shard_map/ppermute | solution.py:425
  11.0 4.3 %collective-permute-done.1 = bf16[128,512]{1,0:T(8,128)(2,1)S(1)} collective-permute-done((bf16[128,512]{1,0:T(8,128)(2,1)S(1)}, bf16[128,512]{1,0:T(8,128)(2,1)S(1)}, u32[]{:S(2)}, u32[]{:S(2)}) %collective-permute-start.1) | collective-permute-done | bytes 131104 | tf_op jit(solution)/shard_map/ppermute | solution.py:425
  17.2 2.3 %collective-permute-start.4 = (bf16[128,512]{1,0:T(8,128)(2,1)S(1)}, bf16[128,512]{1,0:T(8,128)(2,1)S(1)}, u32[]{:S(2)}, u32[]{:S(2)}) collective-permute-start(bf16[128,512]{1,0:T(8,128)(2,1)S(1)} %get-tuple-element.46), channel_id=1, source_target_pairs={{0,20},{4,16},{8,28},{12,24},{16,4},{20,0},{24,12},{28,8},{1,21},{... | collective-permute-start | bytes 393224 | tf_op jit(solution)/shard_map/ppermute | solution.py:425
  20.9 3.1 %collective-permute-start.6 = (bf16[128,512]{1,0:T(8,128)(2,1)S(1)}, bf16[128,512]{1,0:T(8,128)(2,1)S(1)}, u32[]{:S(2)}, u32[]{:S(2)}) collective-permute-start(bf16[128,512]{1,0:T(8,128)(2,1)S(1)} %get-tuple-element.48), channel_id=1, source_target_pairs={{0,28},{4,24},{8,20},{12,16},{16,12},{20,8},{24,4},{28,0},{1,29},{... | collective-permute-start | bytes 393224 | tf_op jit(solution)/shard_map/ppermute | solution.py:425
  24.0 7.4 %collective-permute-done.4 = bf16[128,512]{1,0:T(8,128)(2,1)S(1)} collective-permute-done((bf16[128,512]{1,0:T(8,128)(2,1)S(1)}, bf16[128,512]{1,0:T(8,128)(2,1)S(1)}, u32[]{:S(2)}, u32[]{:S(2)}) %collective-permute-start.4) | collective-permute-done | bytes 131104 | tf_op jit(solution)/shard_map/ppermute | solution.py:425
  31.6 6.0 %collective-permute-done.9.refs_1_.refs_2_ = bf16[512,512]{1,0:T(8,128)(2,1)S(1)} collective-permute-done((bf16[512,512]{1,0:T(8,128)(2,1)S(1)}, bf16[512,512]{1,0:T(8,128)(2,1)S(1)}, u32[]{:S(2)}, u32[]{:S(2)}) %collective-permute-start.9) | collective-permute-done | bytes 524320 | tf_op jit(solution)/shard_map/ppermute | solution.py:418
  42.8 3.6 %collective-permute-start.11 = (bf16[512,512]{1,0:T(8,128)(2,1)S(1)}, bf16[512,512]{1,0:T(8,128)(2,1)S(1)}, u32[]{:S(2)}, u32[]{:S(2)}) collective-permute-start(bf16[512,512]{1,0:T(8,128)(2,1)S(1)} %project_halo.1.refs_7_), channel_id=1, source_target_pairs={{0,4},{4,8},{8,12},{12,16},{16,20},{20,24},{24,28},{1,5},{5,9},{9,... | collective-permute-start | bytes 1572872 | tf_op jit(solution)/shard_map/ppermute | solution.py:453
  46.4 5.6 %project_block.1 = (bf16[1024,512]{1,0:T(8,128)(2,1)S(1)}, bf16[1024,512]{1,0:T(8,128)(2,1)S(1)}, bf16[1024,512]{1,0:T(8,128)(2,1)S(1)}) custom-call(bf16[1024,512]{1,0:T(8,128)(2,1)S(1)} %get-tuple-element.40.refs_0_, bf16[1024,512]{1,0:T(8,128)(2,1)S(1)} %collective-permute-done.7.refs_1_, bf16[1024,512]{1,0:T(8,128)(2,1)S(1)} %fence.4.refs_2_, ...), custom_call_target="tpu_custom_call" | custom-call | tf_op jit(solution)/shard_map/project_block/pallas_call | solution.py:39
  52.1 3.4 %project_near.1 = (bf16[512,512]{1,0:T(8,128)(2,1)S(1)}, bf16[512,512]{1,0:T(8,128)(2,1)S(1)}, bf16[512,512]{1,0:T(8,128)(2,1)S(1)}) custom-call(bf16[512,512]{1,0:T(8,128)(2,1)S(1)} %constant_dynamic-update-slice_fusion.refs_1_.refs_0_, bf16[512,512]{1,0:T(8,128)(2,1)S(1)} %collective-permute-done.13.refs_1_, ...), custom_call_target="tpu_custom_call" | custom-call | tf_op jit(solution)/shard_map/project_near/pallas_call | solution.py:39
  55.5 2.0 %collective-permute-done.11.refs_2_.refs_4_ = bf16[512,512]{1,0:T(8,128)(2,1)S(1)} collective-permute-done((bf16[512,512]{1,0:T(8,128)(2,1)S(1)}, bf16[512,512]{1,0:T(8,128)(2,1)S(1)}, u32[]{:S(2)}, u32[]{:S(2)}) %collective-permute-start.11) | collective-permute-done | bytes 524320 | tf_op jit(solution)/shard_map/ppermute | solution.py:453
  57.6 1.8 %half_sums.1 = (f32[512,512]{1,0:T(8,128)S(1)}, f32[512,512]{1,0:T(8,128)S(1)}, f32[512,512]{1,0:T(8,128)S(1)}) custom-call(bf16[512,512]{1,0:T(8,128)(2,1)S(1)} %constant_dynamic-update-slice_fusion.4.refs_2_.refs_8_.refs_0_, bf16[512,512]{1,0:T(8,128)(2,1)S(1)} %collective-permute-done.16.refs_1_, ...), custom_call_target="tpu_custom_call" | custom-call | tf_op jit(solution)/shard_map/half_sums/pallas_call | solution.py:39
  59.5 4.7 %column_part.1 = (bf16[528,128]{1,0:T(8,128)(2,1)S(1)}, bf16[528,128]{1,0:T(8,128)(2,1)S(1)}, bf16[528,128]{1,0:T(8,128)(2,1)S(1)}, bf16[528,128]{1,0:T(8,128)(2...) custom-call(s32[3]{0:T(128)S(1)} %pad_add_fusion.pos_ref.refs_0_, ...), custom_call_target="tpu_custom_call" | custom-call | tf_op jit(solution)/shard_map/column_part/pallas_call | solution.py:39
  64.2 4.5 %collective-permute-start.20 = (bf16[528,128]{1,0:T(8,128)(2,1)S(1)}, bf16[528,128]{1,0:T(8,128)(2,1)S(1)}, u32[]{:S(2)}, u32[]{:S(2)}) collective-permute-start(bf16[528,128]{1,0:T(8,128)(2,1)S(1)} %get-tuple-element.66), channel_id=1, source_target_pairs={{0,16},{4,20},{8,24},{12,28},{16,0},{20,4},{24,8},{28,12},{1,17},{... | collective-permute-start | bytes 405512 | tf_op jit(solution)/shard_map/ppermute | solution.py:425
  70.2 1.8 %collective-permute-start.23 = (bf16[528,128]{1,0:T(8,128)(2,1)S(1)}, bf16[528,128]{1,0:T(8,128)(2,1)S(1)}, u32[]{:S(2)}, u32[]{:S(2)}) collective-permute-start(bf16[528,128]{1,0:T(8,128)(2,1)S(1)} %get-tuple-element.69), channel_id=1, source_target_pairs={{0,8},{4,12},{8,0},{12,4},{16,24},{20,28},{24,16},{28,20},{1,9},{5... | collective-permute-start | bytes 405512 | tf_op jit(solution)/shard_map/ppermute | solution.py:425
  72.6 3.2 %local_part.1 = (f32[8,128,512]{2,1,0:T(8,128)S(1)}, f32[128,128]{1,0:T(8,128)S(1)}) custom-call(s32[3]{0:T(128)S(1)} %pad_add_fusion.pos_ref.refs_0_, bf16[1024,512]{1,0:T(8,128)(2,1)S(1)} %get-tuple-element.52.refs_7_.refs_1_, bf16[1024,512]{1,0:T(8,128)(2,1)S(1)} %get-tuple-element.53.refs_2_, bf16[1024,512]{1,0:T(8,128)(2,1)S(1)} %get-tuple-element.54.refs_3_, ...), custom_call_target="tpu_custom_call" | custom-call | flops 5500000256 | tf_op jit(solution)/shard_map/local_part/pallas_call | solution.py:39
  75.8 3.2 %collective-permute-done.20.refs_3_ = bf16[528,128]{1,0:T(8,128)(2,1)S(1)} collective-permute-done((bf16[528,128]{1,0:T(8,128)(2,1)S(1)}, bf16[528,128]{1,0:T(8,128)(2,1)S(1)}, u32[]{:S(2)}, u32[]{:S(2)}) %collective-permute-start.20) | collective-permute-done | bytes 135200 | tf_op jit(solution)/shard_map/ppermute | solution.py:425
  79.0 2.8 %collective-permute-done.21.refs_4_ = bf16[528,128]{1,0:T(8,128)(2,1)S(1)} collective-permute-done((bf16[528,128]{1,0:T(8,128)(2,1)S(1)}, bf16[528,128]{1,0:T(8,128)(2,1)S(1)}, u32[]{:S(2)}, u32[]{:S(2)}) %collective-permute-start.21) | collective-permute-done | bytes 135200 | tf_op jit(solution)/shard_map/ppermute | solution.py:425
  83.2 1.9 %mix.2 = (bf16[2,192,512]{2,1,0:T(8,128)(2,1)S(1)}, bf16[2,192,512]{2,1,0:T(8,128)(2,1)S(1)}) custom-call(s32[3]{0:T(128)S(1)} %pad_add_fusion.pos_ref.refs_0_, f32[8,128,512]{2,1,0:T(8,128)S(1)} %get-tuple-element.62.refs_1_, f32[128,128]{1,0:T(8,128)S(1)} %get-tuple-element.63.refs_2_, bf16[528,128]{1,0:T(8,128)(2,1)S(1)} %collective-permute-done.20.refs_3_, ...), custom_call_target="tpu_custom_call" | custom-call | flops 2200000000 | tf_op jit(solution)/shard_map/mix/pallas_call | solution.py:39
  85.3 4.7 %collective-permute-start.18 = (bf16[528,128]{1,0:T(8,128)(2,1)S(1)}, bf16[528,128]{1,0:T(8,128)(2,1)S(1)}, u32[]{:S(2)}, u32[]{:S(2)}) collective-permute-start(bf16[528,128]{1,0:T(8,128)(2,1)S(1)} %get-tuple-element.64), channel_id=1, source_target_pairs={{0,24},{4,28},{8,16},{12,20},{16,8},{20,12},{24,0},{28,4},{1,25},{... | collective-permute-start | bytes 405512 | tf_op jit(solution)/shard_map/ppermute | solution.py:425
  94.2 4.1 %collective-permute-done.19.refs_4_ = bf16[528,128]{1,0:T(8,128)(2,1)S(1)} collective-permute-done((bf16[528,128]{1,0:T(8,128)(2,1)S(1)}, bf16[528,128]{1,0:T(8,128)(2,1)S(1)}, u32[]{:S(2)}, u32[]{:S(2)}) %collective-permute-start.19) | collective-permute-done | bytes 135200 | tf_op jit(solution)/shard_map/ppermute | solution.py:425
  104.4 8.5 %collective-permute-done.28.got = bf16[192,2048]{1,0:T(8,128)(2,1)S(1)} collective-permute-done((bf16[192,2048]{1,0:T(8,128)(2,1)S(1)}, bf16[192,2048]{1,0:T(8,128)(2,1)S(1)}, u32[]{:S(2)}, u32[]{:S(2)}) %collective-permute-start.28) | collective-permute-done | bytes 786464 | tf_op jit(solution)/shard_map/ppermute | solution.py:418
  114.6 3.0 %collective-permute-done.27.got = bf16[64,2048]{1,0:T(8,128)(2,1)S(1)} collective-permute-done((bf16[64,2048]{1,0:T(8,128)(2,1)S(1)}, bf16[64,2048]{1,0:T(8,128)(2,1)S(1)}, u32[]{:S(2)}, u32[]{:S(2)}) %collective-permute-start.27) | collective-permute-done | bytes 262176 | tf_op jit(solution)/shard_map/ppermute | solution.py:418
  (72 shorter events, 29.3 us)
Async XLA Ops:
  0.0 37.5 %collective-permute-start.8 = (bf16[1024,512]{1,0:T(8,128)(2,1)}, bf16[1024,512]{1,0:T(8,128)(2,1)S(1)}, u32[]{:S(2)}, u32[]{:S(2)}) collective-permute-start(bf16[1024,512]{1,0:T(8,128)(2,1)} %tok_hbm.1), channel_id=1, source_target_pairs={{0,2},{1,3},{2,0},{3,1},{4,6},{5,7},{6,4},{7,5},{8,10},{9,11},{10,... | collective-permute-start | bytes 3145736 | tf_op jit(solution)/shard_map/ppermute | solution.py:418
  4.9 6.2 %collective-permute-start = (bf16[128,512]{1,0:T(8,128)(2,1)S(1)}, bf16[128,512]{1,0:T(8,128)(2,1)S(1)}, u32[]{:S(2)}, u32[]{:S(2)}) collective-permute-start(bf16[128,512]{1,0:T(8,128)(2,1)S(1)} %get-tuple-element.42), channel_id=1, source_target_pairs={{0,4},{4,0},{8,12},{12,8},{16,20},{20,16},{24,28},{28,24},{1,5},{5... | collective-permute-start | bytes 393224 | tf_op jit(solution)/shard_map/ppermute | solution.py:425
  6.4 8.9 %collective-permute-start.1 = (bf16[128,512]{1,0:T(8,128)(2,1)S(1)}, bf16[128,512]{1,0:T(8,128)(2,1)S(1)}, u32[]{:S(2)}, u32[]{:S(2)}) collective-permute-start(bf16[128,512]{1,0:T(8,128)(2,1)S(1)} %get-tuple-element.43), channel_id=1, source_target_pairs={{0,8},{4,12},{8,0},{12,4},{16,24},{20,28},{24,16},{28,20},{1,9},{5... | collective-permute-start | bytes 393224 | tf_op jit(solution)/shard_map/ppermute | solution.py:425
  8.0 9.0 %collective-permute-start.2 = (bf16[128,512]{1,0:T(8,128)(2,1)S(1)}, bf16[128,512]{1,0:T(8,128)(2,1)S(1)}, u32[]{:S(2)}, u32[]{:S(2)}) collective-permute-start(bf16[128,512]{1,0:T(8,128)(2,1)S(1)} %get-tuple-element.44), channel_id=1, source_target_pairs={{0,12},{4,8},{8,4},{12,0},{16,28},{20,24},{24,20},{28,16},{1,13},{... | collective-permute-start | bytes 393224 | tf_op jit(solution)/shard_map/ppermute | solution.py:425
  8.4 12.4 %collective-permute-start.3 = (bf16[128,512]{1,0:T(8,128)(2,1)S(1)}, bf16[128,512]{1,0:T(8,128)(2,1)S(1)}, u32[]{:S(2)}, u32[]{:S(2)}) collective-permute-start(bf16[128,512]{1,0:T(8,128)(2,1)S(1)} %get-tuple-element.45), channel_id=1, source_target_pairs={{0,16},{4,20},{8,24},{12,28},{16,0},{20,4},{24,8},{28,12},{1,17},{... | collective-permute-start | bytes 393224 | tf_op jit(solution)/shard_map/ppermute | solution.py:425
  17.0 20.6 %collective-permute-start.9 = (bf16[512,512]{1,0:T(8,128)(2,1)S(1)}, bf16[512,512]{1,0:T(8,128)(2,1)S(1)}, u32[]{:S(2)}, u32[]{:S(2)}) collective-permute-start(bf16[512,512]{1,0:T(8,128)(2,1)S(1)} %constant_dynamic-update-slice_fusion.refs_1_.refs_0_), channel_id=1, source_target_pairs={{0,2},{1,3},{2,0},{3,1},{4,6},{5,7},{6,4},{7,5},{8,10},{9,11},{10,... | collective-permute-start | bytes 1572872 | tf_op jit(solution)/shard_map/ppermute | solution.py:418
  17.2 14.2 %collective-permute-start.4 = (bf16[128,512]{1,0:T(8,128)(2,1)S(1)}, bf16[128,512]{1,0:T(8,128)(2,1)S(1)}, u32[]{:S(2)}, u32[]{:S(2)}) collective-permute-start(bf16[128,512]{1,0:T(8,128)(2,1)S(1)} %get-tuple-element.46), channel_id=1, source_target_pairs={{0,20},{4,16},{8,28},{12,24},{16,4},{20,0},{24,12},{28,8},{1,21},{... | collective-permute-start | bytes 393224 | tf_op jit(solution)/shard_map/ppermute | solution.py:425
  19.4 12.0 %collective-permute-start.5 = (bf16[128,512]{1,0:T(8,128)(2,1)S(1)}, bf16[128,512]{1,0:T(8,128)(2,1)S(1)}, u32[]{:S(2)}, u32[]{:S(2)}) collective-permute-start(bf16[128,512]{1,0:T(8,128)(2,1)S(1)} %get-tuple-element.47), channel_id=1, source_target_pairs={{0,24},{4,28},{8,16},{12,20},{16,8},{20,12},{24,0},{28,4},{1,25},{... | collective-permute-start | bytes 393224 | tf_op jit(solution)/shard_map/ppermute | solution.py:425
  20.9 10.6 %collective-permute-start.6 = (bf16[128,512]{1,0:T(8,128)(2,1)S(1)}, bf16[128,512]{1,0:T(8,128)(2,1)S(1)}, u32[]{:S(2)}, u32[]{:S(2)}) collective-permute-start(bf16[128,512]{1,0:T(8,128)(2,1)S(1)} %get-tuple-element.48), channel_id=1, source_target_pairs={{0,28},{4,24},{8,20},{12,16},{16,12},{20,8},{24,4},{28,0},{1,29},{... | collective-permute-start | bytes 393224 | tf_op jit(solution)/shard_map/ppermute | solution.py:425
  31.5 9.5 %collective-permute-start.7 = (bf16[1024,512]{1,0:T(8,128)(2,1)S(1)}, bf16[1024,512]{1,0:T(8,128)(2,1)S(1)}, u32[]{:S(2)}, u32[]{:S(2)}) collective-permute-start(bf16[1024,512]{1,0:T(8,128)(2,1)S(1)} %fence.3), channel_id=1, source_target_pairs={{0,1},{1,0},{2,3},{3,2},{4,5},{5,4},{6,7},{7,6},{8,9},{9,8},{10,11... | collective-permute-start | bytes 3145736 | tf_op jit(solution)/shard_map/ppermute | solution.py:418
  37.6 21.8 %collective-permute-start.17 = (bf16[512,2048]{1,0:T(8,128)(2,1)S(1)}, bf16[512,2048]{1,0:T(8,128)(2,1)S(1)}, u32[]{:S(2)}, u32[]{:S(2)}) collective-permute-start(bf16[512,2048]{1,0:T(8,128)(2,1)S(1)} %copy-done.3), channel_id=1, source_target_pairs={{0,1},{1,0},{2,3},{3,2},{4,5},{5,4},{6,7},{7,6},{8,9},{9,8},{10,11... | collective-permute-start | bytes 6291464 | tf_op jit(solution)/shard_map/ppermute | solution.py:418
  38.1 17.5 %collective-permute-start.12 = (bf16[512,512]{1,0:T(8,128)(2,1)S(1)}, bf16[512,512]{1,0:T(8,128)(2,1)S(1)}, u32[]{:S(2)}, u32[]{:S(2)}) collective-permute-start(bf16[512,512]{1,0:T(8,128)(2,1)S(1)} %constant_dynamic-update-slice_fusion.4.refs_2_.refs_8_.refs_0_), channel_id=1, source_target_pairs={{0,2},{1,3},{2,0},{3,1},{4,6},{5,7},{6,4},{7,5},{8,10},{9,11},{10,... | collective-permute-start | bytes 1572872 | tf_op jit(solution)/shard_map/ppermute | solution.py:418
  39.8 12.2 %collective-permute-start.13 = (bf16[512,512]{1,0:T(8,128)(2,1)S(1)}, bf16[512,512]{1,0:T(8,128)(2,1)S(1)}, u32[]{:S(2)}, u32[]{:S(2)}) collective-permute-start(bf16[512,512]{1,0:T(8,128)(2,1)S(1)} %constant_dynamic-update-slice_fusion.refs_1_.refs_0_), channel_id=1, source_target_pairs={{0,1},{1,0},{2,3},{3,2},{4,5},{5,4},{6,7},{7,6},{8,9},{9,8},{10,11... | collective-permute-start | bytes 1572872 | tf_op jit(solution)/shard_map/ppermute | solution.py:418
  41.0 11.1 %collective-permute-start.14 = (bf16[512,512]{1,0:T(8,128)(2,1)S(1)}, bf16[512,512]{1,0:T(8,128)(2,1)S(1)}, u32[]{:S(2)}, u32[]{:S(2)}) collective-permute-start(bf16[512,512]{1,0:T(8,128)(2,1)S(1)} %collective-permute-done.9.refs_1_.refs_2_), channel_id=1, source_target_pairs={{0,1},{1,0},{2,3},{3,2},{4,5},{5,4},{6,7},{7,6},{8,9},{9,8},{10,11... | collective-permute-start | bytes 1572872 | tf_op jit(solution)/shard_map/ppermute | solution.py:418
  42.8 14.8 %collective-permute-start.11 = (bf16[512,512]{1,0:T(8,128)(2,1)S(1)}, bf16[512,512]{1,0:T(8,128)(2,1)S(1)}, u32[]{:S(2)}, u32[]{:S(2)}) collective-permute-start(bf16[512,512]{1,0:T(8,128)(2,1)S(1)} %project_halo.1.refs_7_), channel_id=1, source_target_pairs={{0,4},{4,8},{8,12},{12,16},{16,20},{20,24},{24,28},{1,5},{5,9},{9,... | collective-permute-start | bytes 1572872 | tf_op jit(solution)/shard_map/ppermute | solution.py:453
  64.2 14.8 %collective-permute-start.20 = (bf16[528,128]{1,0:T(8,128)(2,1)S(1)}, bf16[528,128]{1,0:T(8,128)(2,1)S(1)}, u32[]{:S(2)}, u32[]{:S(2)}) collective-permute-start(bf16[528,128]{1,0:T(8,128)(2,1)S(1)} %get-tuple-element.66), channel_id=1, source_target_pairs={{0,16},{4,20},{8,24},{12,28},{16,0},{20,4},{24,8},{28,12},{1,17},{... | collective-permute-start | bytes 405512 | tf_op jit(solution)/shard_map/ppermute | solution.py:425
  68.7 13.1 %collective-permute-start.21 = (bf16[528,128]{1,0:T(8,128)(2,1)S(1)}, bf16[528,128]{1,0:T(8,128)(2,1)S(1)}, u32[]{:S(2)}, u32[]{:S(2)}) collective-permute-start(bf16[528,128]{1,0:T(8,128)(2,1)S(1)} %get-tuple-element.67), channel_id=1, source_target_pairs={{0,20},{4,16},{8,28},{12,24},{16,4},{20,0},{24,12},{28,8},{1,21},{... | collective-permute-start | bytes 405512 | tf_op jit(solution)/shard_map/ppermute | solution.py:425
  69.1 12.7 %collective-permute-start.22 = (bf16[528,128]{1,0:T(8,128)(2,1)S(1)}, bf16[528,128]{1,0:T(8,128)(2,1)S(1)}, u32[]{:S(2)}, u32[]{:S(2)}) collective-permute-start(bf16[528,128]{1,0:T(8,128)(2,1)S(1)} %get-tuple-element.68), channel_id=1, source_target_pairs={{0,4},{4,0},{8,12},{12,8},{16,20},{20,16},{24,28},{28,24},{1,5},{5... | collective-permute-start | bytes 405512 | tf_op jit(solution)/shard_map/ppermute | solution.py:425
  70.2 11.6 %collective-permute-start.23 = (bf16[528,128]{1,0:T(8,128)(2,1)S(1)}, bf16[528,128]{1,0:T(8,128)(2,1)S(1)}, u32[]{:S(2)}, u32[]{:S(2)}) collective-permute-start(bf16[528,128]{1,0:T(8,128)(2,1)S(1)} %get-tuple-element.69), channel_id=1, source_target_pairs={{0,8},{4,12},{8,0},{12,4},{16,24},{20,28},{24,16},{28,20},{1,9},{5... | collective-permute-start | bytes 405512 | tf_op jit(solution)/shard_map/ppermute | solution.py:425
  72.1 11.2 %collective-permute-start.24 = (bf16[528,128]{1,0:T(8,128)(2,1)S(1)}, bf16[528,128]{1,0:T(8,128)(2,1)S(1)}, u32[]{:S(2)}, u32[]{:S(2)}) collective-permute-start(bf16[528,128]{1,0:T(8,128)(2,1)S(1)} %get-tuple-element.70), channel_id=1, source_target_pairs={{0,12},{4,8},{8,4},{12,0},{16,28},{20,24},{24,20},{28,16},{1,13},{... | collective-permute-start | bytes 405512 | tf_op jit(solution)/shard_map/ppermute | solution.py:425
  85.3 8.9 %collective-permute-start.18 = (bf16[528,128]{1,0:T(8,128)(2,1)S(1)}, bf16[528,128]{1,0:T(8,128)(2,1)S(1)}, u32[]{:S(2)}, u32[]{:S(2)}) collective-permute-start(bf16[528,128]{1,0:T(8,128)(2,1)S(1)} %get-tuple-element.64), channel_id=1, source_target_pairs={{0,24},{4,28},{8,16},{12,20},{16,8},{20,12},{24,0},{28,4},{1,25},{... | collective-permute-start | bytes 405512 | tf_op jit(solution)/shard_map/ppermute | solution.py:425
  89.9 8.4 %collective-permute-start.19 = (bf16[528,128]{1,0:T(8,128)(2,1)S(1)}, bf16[528,128]{1,0:T(8,128)(2,1)S(1)}, u32[]{:S(2)}, u32[]{:S(2)}) collective-permute-start(bf16[528,128]{1,0:T(8,128)(2,1)S(1)} %get-tuple-element.65), channel_id=1, source_target_pairs={{0,28},{4,24},{8,20},{12,16},{16,12},{20,8},{24,4},{28,0},{1,29},{... | collective-permute-start | bytes 405512 | tf_op jit(solution)/shard_map/ppermute | solution.py:425
  92.4 20.5 %collective-permute-start.28 = (bf16[192,2048]{1,0:T(8,128)(2,1)S(1)}, bf16[192,2048]{1,0:T(8,128)(2,1)S(1)}, u32[]{:S(2)}, u32[]{:S(2)}) collective-permute-start(bf16[192,2048]{1,0:T(8,128)(2,1)S(1)} %out_project.4.refs_5_), channel_id=1, source_target_pairs={{0,2},{1,3},{2,0},{3,1},{4,6},{5,7},{6,4},{7,5},{8,10},{9,11},{10,... | collective-permute-start | bytes 2359304 | tf_op jit(solution)/shard_map/ppermute | solution.py:418
  102.4 15.2 %collective-permute-start.27 = (bf16[64,2048]{1,0:T(8,128)(2,1)S(1)}, bf16[64,2048]{1,0:T(8,128)(2,1)S(1)}, u32[]{:S(2)}, u32[]{:S(2)}) collective-permute-start(bf16[64,2048]{1,0:T(8,128)(2,1)S(1)} %out_project.6), channel_id=1, source_target_pairs={{0,2},{1,3},{2,0},{3,1},{4,6},{5,7},{6,4},{7,5},{8,10},{9,11},{10,... | collective-permute-start | bytes 786440 | tf_op jit(solution)/shard_map/ppermute | solution.py:418
  (9 other events, 60.6 us)

commit v15 on v14

--- a/solution.py
+++ b/solution.py
@@ -123,14 +123,16 @@
     return outs[0], outs[1:]
 
 
-def stage_kernel(order_ref, wq, wk, wv, oq, ok, ov, sems):
+def stage_kernel(order_ref, wq, wk, wv, wo, after, oq, ok, ov, oo, sems):
     copies = []
-    for n, (w, o) in enumerate(((wq, oq), (wk, ok), (wv, ov))):
+    for w, o in ((wq, oq), (wk, ok), (wv, ov), (wo, oo)):
+        part = w.shape[0] // 4
         for p in range(4):
-            rows = pl.ds(pl.multiple_of(order_ref[p] * 512, 512), 512)
-            copies.append(
-                pltpu.make_async_copy(w.at[rows], o.at[p * 512 : (p + 1) * 512], sems.at[4 * n + p])
-            )
+            place = p if w is wo else order_ref[p]
+            rows = pl.ds(pl.multiple_of(place * part, part), part)
+            to = slice(p * part, (p + 1) * part)
+            sem = sems.at[len(copies)]
+            copies.append(pltpu.make_async_copy(w.at[rows], o.at[to], sem))
     for c in copies:
         c.start()
     for c in copies:
@@ -138,15 +140,12 @@
 
 
 def stage(order, weights, after):
-    def body(order_ref, wq, wk, wv, _, *rest):
-        stage_kernel(order_ref, wq, wk, wv, *rest)
-
     return pl.pallas_call(
-        body,
-        in_specs=[IN_SMEM] + [ANYWHERE] * 4,
-        out_specs=[IN_VMEM] * 3,
+        stage_kernel,
+        in_specs=[IN_SMEM] + [ANYWHERE] * 5,
+        out_specs=[IN_VMEM] * 4,
         out_shape=[shape(w.shape) for w in weights],
-        scratch_shapes=[pltpu.SemaphoreType.DMA((12,))],
+        scratch_shapes=[pltpu.SemaphoreType.DMA((16,))],
         compiler_params=pltpu.CompilerParams(vmem_limit_bytes=16 * MIB),
         cost_estimate=pl.CostEstimate(flops=0, bytes_accessed=0, transcendentals=0),
         name="stage_weights",
@@ -186,14 +185,16 @@
     out_ref[STRIDE:, :] = gathered((x0, x1, x2, x3), at, wv)
 
 
-def project_kernel(x0, x1, x2, x3, wq, wk, wv, halo, q_ref, k_ref, v_ref):
-    rows = x0.shape[0]
-    xs = (x0, x1, x2, x3)
-    last = slice(rows - STRIDE, rows)
-    k_ref[last, :] = halo[:STRIDE, :]
-    v_ref[last, :] = halo[STRIDE:, :]
-    for w, out, upto in ((wq, q_ref, rows), (wk, k_ref, rows - STRIDE), (wv, v_ref, rows - STRIDE)):
-        out[:upto, :] = gathered(xs, slice(0, upto), w)
+def query_kernel(x0, x1, x2, x3, wq, q_ref):
+    q_ref[...] = gathered((x0, x1, x2, x3), slice(0, x0.shape[0]), wq)
+
+
+def key_kernel(x0, x1, x2, x3, wk, wv, halo, k_ref, v_ref):
+    upto = x0.shape[0] - STRIDE
+    k_ref[upto:, :] = halo[:STRIDE, :]
+    v_ref[upto:, :] = halo[STRIDE:, :]
+    for w, out in ((wk, k_ref), (wv, v_ref)):
+        out[:upto, :] = gathered((x0, x1, x2, x3), slice(0, upto), w)
 
 
 def softmax_columns(s):
@@ -263,13 +264,14 @@
     return list(zip(outs[: len(sizes)], outs[len(sizes) :]))
 
 
-def column_kernel(pos_ref, x2, x3, hq, hk, hv, wq, wk, wv, nq, nk, nv, *rest):
+def column_kernel(pos_ref, x2, x3a, x3b, hq, hk, hv, wq, wk, wv, nq, nk, nv, *rest):
     out_refs, scratch = rest[:-3], rest[-3:]
     owners, message, width = scratch[0].shape
     groups = message // (ROWS * SUB)
     for h, w, near, a in zip((hq, hk, hv), (wq, wk, wv), (nq, nk, nv), scratch):
         total = h[...] + dot(x2[...], w[2 * width : 3 * width, :])
-        total = total + dot(x3[...], w[3 * width :, :])
+        diagonal = [dot(x[...], w[3 * width :, :]) for x in (x3a, x3b)]
+        total = total + jnp.concatenate(diagonal, 0)
         a[:NEAR] = near[...].reshape(NEAR, message, width)
         a[NEAR:] = total.astype(BF16).reshape(owners - NEAR, message, width)
     part = ROWS * SUB
@@ -316,7 +318,9 @@
     message = tokens // (owners - NEAR)
     shapes = [shape((HEADS * message + 16, DH))] * owners
     scratch = [pltpu.VMEM((owners, message, width), BF16)] * 3
-    args = (pos, across, swap(across, 1), *halves, *weights, *near)
+    middle = tokens // 2
+    diagonal = [swap(x, 1) for x in (across[:middle], across[middle:])]
+    args = (pos, across, *diagonal, *halves, *weights, *near)
     return call(column_kernel, "column_part", 0, shapes, args, after, scratch)
 
 
@@ -440,10 +444,10 @@
     messages = exchange(sent)
     near_own = jnp.concatenate(messages[:NEAR], 0)
     near_core, near_across = swap(near_own, 1), swap(near_own, 2)
-    w_other = swap(w_out, 1)
     far_own = jnp.concatenate(messages[NEAR:], 0)
     far_core, far_across = swap(far_own, 1), swap(far_own, 2)
-    weights = stage(order, (w_query, w_key, w_value), messages[1])
+    *weights, w_own = stage(order, (w_query, w_key, w_value, w_out), messages[1])
+    w_other = swap(w_own, 1)
     block_core = swap(fence(block_tokens, near_own, far_own), 1)
     across = fence(across, near_across, far_own)
     pieces = (block_tokens, block_core, across, swap(across, 1))
@@ -451,12 +455,12 @@
         halo_kernel, "project_halo", 1.5, shape((2 * STRIDE, width)), (*pieces, *weights[1:])
     )
     halo = lax.ppermute(own_halo, "seq", [(i, i + 1) for i in range(owners - 1)])
-    q, k, v = call(
-        project_kernel,
-        "project_block",
+    q = call(
+        query_kernel,
+        "project_query",
         0,
-        [shape((rows, width))] * 3,
-        (*pieces, *weights, own_halo),
+        shape((rows, width)),
+        (*pieces, weights[0]),
         (far_own,),
     )
     near = call(
@@ -468,16 +472,26 @@
         (q,),
     )
     far_half = half_sums(far_own, far_core, weights, (near[0],))
-    far_across = fence(far_across, near[0], halo)
+    far_across = fence(far_across, near[0])
     columns = column_part(pos, far_across, far_half, weights, near, owners, (w_other,))
+    k, v = call(
+        key_kernel,
+        "project_key",
+        0,
+        [shape((rows, width))] * 2,
+        (*pieces, *weights[1:], own_halo),
+        (columns[0],),
+    )
     locals_ = local_part(pos, q, k, v, halo, owners, (columns[0],))
+    columns = list(columns)
+    columns[1] = fence(columns[1], halo)
     columns = exchange(columns)
     sums, after = [], ()
     for share in SHARES:
         own, send = mix(pos, share, [columns[n] for n in share], locals_, after)
         other = swap(send, 1)
-        out = out_project(pos, False, own, other, w_out, w_other)
-        keep = out_project(pos, True, own, other, w_out, w_other)
+        out = out_project(pos, False, own, other, w_own, w_other)
+        keep = out_project(pos, True, own, other, w_own, w_other)
         sums.append((keep, swap(out, 2)))
         after = (out,)
     result = ()

time: 119 us -> 118 us (level)
  waiting for transfers between devices: 45.6 us -> 36 us
  starting transfers between devices: 37.9 us -> 42.5 us
  local copies, waits for them, and re-layouts: 0.17 us -> 3.37 us
    ppermute x14, waiting for transfers between devices: 26 us -> 13 us  [move(): lax.ppermute(value, 'seq', [(i, i ^ k) for i in range(peers)])]
    ppermute x14 -> x15, waiting for transfers between devices: 17.6 us -> 23 us  [swap(): return lax.ppermute(value, 'head', [(i, i ^ distance) for i in range(4)])]
    ppermute x14, starting transfers between devices: 26.9 us -> 31.9 us  [move(): lax.ppermute(value, 'seq', [(i, i ^ k) for i in range(peers)])]
    unnamed x15, local copies, waits for them, and re-layouts: 0.15 us -> 3.31 us
    ppermute x1, waiting for transfers between devices: 2.03 us -> 0.01 us  [chunked(): lax.ppermute(own_halo, 'seq', [(i, i + 1) for i in range(owners - 1)])]
    ppermute x14 -> x15, starting transfers between devices: 7.42 us -> 7.26 us  [swap(): return lax.ppermute(value, 'head', [(i, i ^ distance) for i in range(4)])]
    pallas_call x12 -> x13, Pallas kernels: 28.9 us -> 28.9 us  [call(): pl.pallas_call(run, in_specs=specs + [ANYWHERE] * extra, out_specs=jax.tr...]
  transfers between devices with their start and end apart: 29 -> 30, of which waited for: 13 -> 11; matrix products, arithmetic and copies ran while one was open for 0% -> 0% of each run, Pallas kernels for 23% -> 27%
where the time goes in v15:
time: 118 us
  starting transfers between devices  42.5 us (36%)
  waiting for transfers between devices  36 us (31%)
  Pallas kernels  35.2 us (30%)
  local copies, waits for them, and re-layouts  3.37 us (3%)
    ppermute x14, starting transfers between devices, move(): lax.ppermute(value, 'seq', [(i, i ^ k) for i in range(peers)])  31.9 us
    pallas_call x13, Pallas kernels, call(): pl.pallas_call(run, in_specs=specs + [ANYWHERE] * extra, out_specs=jax.tr...  28.9 us
    ppermute x15, waiting for transfers between devices, swap(): return lax.ppermute(value, 'head', [(i, i ^ distance) for i in range(4)])  23 us
    ppermute x14, waiting for transfers between devices, move(): lax.ppermute(value, 'seq', [(i, i ^ k) for i in range(peers)])  13 us
    ppermute x15, starting transfers between devices, swap(): return lax.ppermute(value, 'head', [(i, i ^ distance) for i in range(4)])  7.26 us
    unnamed x15, local copies, waits for them, and re-layouts  3.31 us
    ppermute x1, starting transfers between devices, chunked(): lax.ppermute(own_halo, 'seq', [(i, i + 1) for i in range(owners - 1)])  3.28 us
    pallas_call x2, Pallas kernels, join(): pl.pallas_call(functools.partial(join_kernel, share), in_specs=[IN_SMEM,...  2.89 us
  transfers between devices with their start and end apart: 30, of which 11 were waited for; matrix products, arithmetic and copies ran while one was open for 0% of the time, Pallas kernels for 27%

profile of v15, /device:TPU:0, one launch (start us, length us, event | category | flops | bytes accessed | tf_op | source)
XLA Modules:
  0.0 117.7 jit_solution(8395608345154733390)
XLA Ops:
  0.0 2.9 %collective-permute-start.8 = (bf16[1024,512]{1,0:T(8,128)(2,1)}, bf16[1024,512]{1,0:T(8,128)(2,1)S(1)}, u32[]{:S(2)}, u32[]{:S(2)}) collective-permute-start(bf16[1024,512]{1,0:T(8,128)(2,1)} %tok_hbm.1), channel_id=1, source_target_pairs={{0,2},{1,3},{2,0},{3,1},{4,6},{5,7},{6,4},{7,5},{8,10},{9,11},{10,... | collective-permute-start | bytes 3145736 | tf_op jit(solution)/shard_map/ppermute | solution.py:422
  3.0 2.1 %pack_tokens.1 = (bf16[1024,512]{1,0:T(8,128)(2,1)S(1)}, bf16[128,512]{1,0:T(8,128)(2,1)S(1)}, bf16[128,512]{1,0:T(8,128)(2,1)S(1)}, bf16[128,512]{1,0:T(8,128)(...) custom-call(s32[3]{0:T(128)S(1)} %pad_add_fusion.pos_ref.refs_0_, ...), custom_call_target="tpu_custom_call" | custom-call | bytes 2097152 | tf_op jit(solution)/shard_map/pack_tokens/pallas_call | solution.py:113
  5.1 2.7 %collective-permute-start.3 = (bf16[128,512]{1,0:T(8,128)(2,1)S(1)}, bf16[128,512]{1,0:T(8,128)(2,1)S(1)}, u32[]{:S(2)}, u32[]{:S(2)}) collective-permute-start(bf16[128,512]{1,0:T(8,128)(2,1)S(1)} %get-tuple-element.45), channel_id=1, source_target_pairs={{0,16},{4,20},{8,24},{12,28},{16,0},{20,4},{24,8},{28,12},{1,17},{... | collective-permute-start | bytes 393224 | tf_op jit(solution)/shard_map/ppermute | solution.py:429
  11.3 2.8 %collective-permute-done.after = bf16[128,512]{1,0:T(8,128)(2,1)S(1)} collective-permute-done((bf16[128,512]{1,0:T(8,128)(2,1)S(1)}, bf16[128,512]{1,0:T(8,128)(2,1)S(1)}, u32[]{:S(2)}, u32[]{:S(2)}) %collective-permute-start) | collective-permute-done | bytes 131104 | tf_op jit(solution)/shard_map/ppermute | solution.py:429
  14.0 3.8 %collective-permute-start.2 = (bf16[128,512]{1,0:T(8,128)(2,1)S(1)}, bf16[128,512]{1,0:T(8,128)(2,1)S(1)}, u32[]{:S(2)}, u32[]{:S(2)}) collective-permute-start(bf16[128,512]{1,0:T(8,128)(2,1)S(1)} %get-tuple-element.44), channel_id=1, source_target_pairs={{0,12},{4,8},{8,4},{12,0},{16,28},{20,24},{24,20},{28,16},{1,13},{... | collective-permute-start | bytes 393224 | tf_op jit(solution)/shard_map/ppermute | solution.py:429
  17.9 7.0 %collective-permute-start.5 = (bf16[128,512]{1,0:T(8,128)(2,1)S(1)}, bf16[128,512]{1,0:T(8,128)(2,1)S(1)}, u32[]{:S(2)}, u32[]{:S(2)}) collective-permute-start(bf16[128,512]{1,0:T(8,128)(2,1)S(1)} %get-tuple-element.47), channel_id=1, source_target_pairs={{0,24},{4,28},{8,16},{12,20},{16,8},{20,12},{24,0},{28,4},{1,25},{... | collective-permute-start | bytes 393224 | tf_op jit(solution)/shard_map/ppermute | solution.py:429
  24.9 3.5 %collective-permute-start.6 = (bf16[128,512]{1,0:T(8,128)(2,1)S(1)}, bf16[128,512]{1,0:T(8,128)(2,1)S(1)}, u32[]{:S(2)}, u32[]{:S(2)}) collective-permute-start(bf16[128,512]{1,0:T(8,128)(2,1)S(1)} %get-tuple-element.48), channel_id=1, source_target_pairs={{0,28},{4,24},{8,20},{12,16},{16,12},{20,8},{24,4},{28,0},{1,29},{... | collective-permute-start | bytes 393224 | tf_op jit(solution)/shard_map/ppermute | solution.py:429
  34.3 7.7 %collective-permute-done.9.refs_1_.refs_2_ = bf16[512,512]{1,0:T(8,128)(2,1)S(1)} collective-permute-done((bf16[512,512]{1,0:T(8,128)(2,1)S(1)}, bf16[512,512]{1,0:T(8,128)(2,1)S(1)}, u32[]{:S(2)}, u32[]{:S(2)}) %collective-permute-start.9) | collective-permute-done | bytes 524320 | tf_op jit(solution)/shard_map/ppermute | solution.py:422
  46.1 3.3 %collective-permute-start.18 = (bf16[512,512]{1,0:T(8,128)(2,1)S(1)}, bf16[512,512]{1,0:T(8,128)(2,1)S(1)}, u32[]{:S(2)}, u32[]{:S(2)}) collective-permute-start(bf16[512,512]{1,0:T(8,128)(2,1)S(1)} %project_halo.1.refs_6_), channel_id=1, source_target_pairs={{0,4},{4,8},{8,12},{12,16},{16,20},{20,24},{24,28},{1,5},{5,9},{9,... | collective-permute-start | bytes 1572872 | tf_op jit(solution)/shard_map/ppermute | solution.py:457
  49.3 2.3 %project_query.1.refs_7_.refs_1_ = bf16[1024,512]{1,0:T(8,128)(2,1)S(1)} custom-call(bf16[1024,512]{1,0:T(8,128)(2,1)S(1)} %get-tuple-element.40.refs_0_, bf16[1024,512]{1,0:T(8,128)(2,1)S(1)} %collective-permute-done.7.refs_1_, bf16[1024,512]{1,0:T(8,128)(2,1)S(1)} %fence.5.refs_2_, bf16[1024,512]{1,0:T(8,128)(2,1)S(1)} %collective-permute-done.10.refs_3_, ...), custom_call_target="tpu_custom_call" | custom-call | tf_op jit(solution)/shard_map/project_query/pallas_call | solution.py:39
  51.7 3.4 %project_near.1 = (bf16[512,512]{1,0:T(8,128)(2,1)S(1)}, bf16[512,512]{1,0:T(8,128)(2,1)S(1)}, bf16[512,512]{1,0:T(8,128)(2,1)S(1)}) custom-call(bf16[512,512]{1,0:T(8,128)(2,1)S(1)} %constant_dynamic-update-slice_fusion.refs_1_.refs_0_, bf16[512,512]{1,0:T(8,128)(2,1)S(1)} %collective-permute-done.12.refs_1_, ...), custom_call_target="tpu_custom_call" | custom-call | tf_op jit(solution)/shard_map/project_near/pallas_call | solution.py:39
  59.3 4.7 %column_part.1 = (bf16[528,128]{1,0:T(8,128)(2,1)S(1)}, bf16[528,128]{1,0:T(8,128)(2,1)S(1)}, bf16[528,128]{1,0:T(8,128)(2,1)S(1)}, bf16[528,128]{1,0:T(8,128)(2...) custom-call(s32[3]{0:T(128)S(1)} %pad_add_fusion.pos_ref.refs_0_, ...), custom_call_target="tpu_custom_call" | custom-call | tf_op jit(solution)/shard_map/column_part/pallas_call | solution.py:39
  64.1 3.5 %collective-permute-start.22 = (bf16[528,128]{1,0:T(8,128)(2,1)S(1)}, bf16[528,128]{1,0:T(8,128)(2,1)S(1)}, u32[]{:S(2)}, u32[]{:S(2)}) collective-permute-start(bf16[528,128]{1,0:T(8,128)(2,1)S(1)} %get-tuple-element.67), channel_id=1, source_target_pairs={{0,20},{4,16},{8,28},{12,24},{16,4},{20,0},{24,12},{28,8},{1,21},{... | collective-permute-start | bytes 405512 | tf_op jit(solution)/shard_map/ppermute | solution.py:429
  67.6 2.3 %collective-permute-start.25 = (bf16[528,128]{1,0:T(8,128)(2,1)S(1)}, bf16[528,128]{1,0:T(8,128)(2,1)S(1)}, u32[]{:S(2)}, u32[]{:S(2)}) collective-permute-start(bf16[528,128]{1,0:T(8,128)(2,1)S(1)} %get-tuple-element.70), channel_id=1, source_target_pairs={{0,12},{4,8},{8,4},{12,0},{16,28},{20,24},{24,20},{28,16},{1,13},{... | collective-permute-start | bytes 405512 | tf_op jit(solution)/shard_map/ppermute | solution.py:429
  69.9 3.4 %project_key.1 = (bf16[1024,512]{1,0:T(8,128)(2,1)S(1)}, bf16[1024,512]{1,0:T(8,128)(2,1)S(1)}) custom-call(bf16[1024,512]{1,0:T(8,128)(2,1)S(1)} %get-tuple-element.40.refs_0_, bf16[1024,512]{1,0:T(8,128)(2,1)S(1)} %collective-permute-done.7.refs_1_, bf16[1024,512]{1,0:T(8,128)(2,1)S(1)} %fence.5.refs_2_, ...), custom_call_target="tpu_custom_call" | custom-call | tf_op jit(solution)/shard_map/project_key/pallas_call | solution.py:39
  74.6 3.2 %local_part.1 = (f32[8,128,512]{2,1,0:T(8,128)S(1)}, f32[128,128]{1,0:T(8,128)S(1)}) custom-call(s32[3]{0:T(128)S(1)} %pad_add_fusion.pos_ref.refs_0_, bf16[1024,512]{1,0:T(8,128)(2,1)S(1)} %project_query.1.refs_7_.refs_1_, bf16[1024,512]{1,0:T(8,128)(2,1)S(1)} %get-tuple-element.60.refs_2_, bf16[1024,512]{1,0:T(8,128)(2,1)S(1)} %get-tuple-element.61.refs_3_, ...), custom_call_target="tpu_custom_call" | custom-call | flops 5500000256 | tf_op jit(solution)/shard_map/local_part/pallas_call | solution.py:39
  77.7 1.9 %collective-permute-done.24.refs_6_ = bf16[528,128]{1,0:T(8,128)(2,1)S(1)} collective-permute-done((bf16[528,128]{1,0:T(8,128)(2,1)S(1)}, bf16[528,128]{1,0:T(8,128)(2,1)S(1)}, u32[]{:S(2)}, u32[]{:S(2)}) %collective-permute-start.24) | collective-permute-done | bytes 135200 | tf_op jit(solution)/shard_map/ppermute | solution.py:429
  79.6 1.9 %collective-permute-done.25.refs_7_ = bf16[528,128]{1,0:T(8,128)(2,1)S(1)} collective-permute-done((bf16[528,128]{1,0:T(8,128)(2,1)S(1)}, bf16[528,128]{1,0:T(8,128)(2,1)S(1)}, u32[]{:S(2)}, u32[]{:S(2)}) %collective-permute-start.25) | collective-permute-done | bytes 135200 | tf_op jit(solution)/shard_map/ppermute | solution.py:429
  83.2 1.9 %mix.2 = (bf16[2,192,512]{2,1,0:T(8,128)(2,1)S(1)}, bf16[2,192,512]{2,1,0:T(8,128)(2,1)S(1)}) custom-call(s32[3]{0:T(128)S(1)} %pad_add_fusion.pos_ref.refs_0_, f32[8,128,512]{2,1,0:T(8,128)S(1)} %get-tuple-element.62.refs_1_, f32[128,128]{1,0:T(8,128)S(1)} %get-tuple-element.63.refs_2_, bf16[528,128]{1,0:T(8,128)(2,1)S(1)} %collective-permute-done.21.refs_3_, ...), custom_call_target="tpu_custom_call" | custom-call | flops 2200000000 | tf_op jit(solution)/shard_map/mix/pallas_call | solution.py:39
  85.3 4.3 %collective-permute-start.20 = (bf16[528,128]{1,0:T(8,128)(2,1)S(1)}, bf16[528,128]{1,0:T(8,128)(2,1)S(1)}, u32[]{:S(2)}, u32[]{:S(2)}) collective-permute-start(bf16[528,128]{1,0:T(8,128)(2,1)S(1)} %get-tuple-element.65), channel_id=1, source_target_pairs={{0,28},{4,24},{8,20},{12,16},{16,12},{20,8},{24,4},{28,0},{1,29},{... | collective-permute-start | bytes 405512 | tf_op jit(solution)/shard_map/ppermute | solution.py:429
  91.7 1.8 %collective-permute-done.19.refs_3_ = bf16[528,128]{1,0:T(8,128)(2,1)S(1)} collective-permute-done((bf16[528,128]{1,0:T(8,128)(2,1)S(1)}, bf16[528,128]{1,0:T(8,128)(2,1)S(1)}, u32[]{:S(2)}, u32[]{:S(2)}) %collective-permute-start.19) | collective-permute-done | bytes 135200 | tf_op jit(solution)/shard_map/ppermute | solution.py:429
  93.6 3.0 %collective-permute-done.20.refs_4_ = bf16[528,128]{1,0:T(8,128)(2,1)S(1)} collective-permute-done((bf16[528,128]{1,0:T(8,128)(2,1)S(1)}, bf16[528,128]{1,0:T(8,128)(2,1)S(1)}, u32[]{:S(2)}, u32[]{:S(2)}) %collective-permute-start.20) | collective-permute-done | bytes 135200 | tf_op jit(solution)/shard_map/ppermute | solution.py:429
  102.6 9.1 %collective-permute-done.29.got = bf16[192,2048]{1,0:T(8,128)(2,1)S(1)} collective-permute-done((bf16[192,2048]{1,0:T(8,128)(2,1)S(1)}, bf16[192,2048]{1,0:T(8,128)(2,1)S(1)}, u32[]{:S(2)}, u32[]{:S(2)}) %collective-permute-start.29) | collective-permute-done | bytes 786464 | tf_op jit(solution)/shard_map/ppermute | solution.py:422
  113.3 2.9 %collective-permute-done.28.got = bf16[64,2048]{1,0:T(8,128)(2,1)S(1)} collective-permute-done((bf16[64,2048]{1,0:T(8,128)(2,1)S(1)}, bf16[64,2048]{1,0:T(8,128)(2,1)S(1)}, u32[]{:S(2)}, u32[]{:S(2)}) %collective-permute-start.28) | collective-permute-done | bytes 262176 | tf_op jit(solution)/shard_map/ppermute | solution.py:422
  (77 shorter events, 31.6 us)
Async XLA Ops:
  0.0 42.0 %collective-permute-start.8 = (bf16[1024,512]{1,0:T(8,128)(2,1)}, bf16[1024,512]{1,0:T(8,128)(2,1)S(1)}, u32[]{:S(2)}, u32[]{:S(2)}) collective-permute-start(bf16[1024,512]{1,0:T(8,128)(2,1)} %tok_hbm.1), channel_id=1, source_target_pairs={{0,2},{1,3},{2,0},{3,1},{4,6},{5,7},{6,4},{7,5},{8,10},{9,11},{10,... | collective-permute-start | bytes 3145736 | tf_op jit(solution)/shard_map/ppermute | solution.py:422
  5.1 23.3 %collective-permute-start.3 = (bf16[128,512]{1,0:T(8,128)(2,1)S(1)}, bf16[128,512]{1,0:T(8,128)(2,1)S(1)}, u32[]{:S(2)}, u32[]{:S(2)}) collective-permute-start(bf16[128,512]{1,0:T(8,128)(2,1)S(1)} %get-tuple-element.45), channel_id=1, source_target_pairs={{0,16},{4,20},{8,24},{12,28},{16,0},{20,4},{24,8},{28,12},{1,17},{... | collective-permute-start | bytes 393224 | tf_op jit(solution)/shard_map/ppermute | solution.py:429
  7.8 25.8 %collective-permute-start.4 = (bf16[128,512]{1,0:T(8,128)(2,1)S(1)}, bf16[128,512]{1,0:T(8,128)(2,1)S(1)}, u32[]{:S(2)}, u32[]{:S(2)}) collective-permute-start(bf16[128,512]{1,0:T(8,128)(2,1)S(1)} %get-tuple-element.46), channel_id=1, source_target_pairs={{0,20},{4,16},{8,28},{12,24},{16,4},{20,0},{24,12},{28,8},{1,21},{... | collective-permute-start | bytes 393224 | tf_op jit(solution)/shard_map/ppermute | solution.py:429
  9.1 5.0 %collective-permute-start = (bf16[128,512]{1,0:T(8,128)(2,1)S(1)}, bf16[128,512]{1,0:T(8,128)(2,1)S(1)}, u32[]{:S(2)}, u32[]{:S(2)}) collective-permute-start(bf16[128,512]{1,0:T(8,128)(2,1)S(1)} %get-tuple-element.42), channel_id=1, source_target_pairs={{0,4},{4,0},{8,12},{12,8},{16,20},{20,16},{24,28},{28,24},{1,5},{5... | collective-permute-start | bytes 393224 | tf_op jit(solution)/shard_map/ppermute | solution.py:429
  9.6 8.3 %collective-permute-start.1 = (bf16[128,512]{1,0:T(8,128)(2,1)S(1)}, bf16[128,512]{1,0:T(8,128)(2,1)S(1)}, u32[]{:S(2)}, u32[]{:S(2)}) collective-permute-start(bf16[128,512]{1,0:T(8,128)(2,1)S(1)} %get-tuple-element.43), channel_id=1, source_target_pairs={{0,8},{4,12},{8,0},{12,4},{16,24},{20,28},{24,16},{28,20},{1,9},{5... | collective-permute-start | bytes 393224 | tf_op jit(solution)/shard_map/ppermute | solution.py:429
  14.0 10.9 %collective-permute-start.2 = (bf16[128,512]{1,0:T(8,128)(2,1)S(1)}, bf16[128,512]{1,0:T(8,128)(2,1)S(1)}, u32[]{:S(2)}, u32[]{:S(2)}) collective-permute-start(bf16[128,512]{1,0:T(8,128)(2,1)S(1)} %get-tuple-element.44), channel_id=1, source_target_pairs={{0,12},{4,8},{8,4},{12,0},{16,28},{20,24},{24,20},{28,16},{1,13},{... | collective-permute-start | bytes 393224 | tf_op jit(solution)/shard_map/ppermute | solution.py:429
  17.9 15.8 %collective-permute-start.5 = (bf16[128,512]{1,0:T(8,128)(2,1)S(1)}, bf16[128,512]{1,0:T(8,128)(2,1)S(1)}, u32[]{:S(2)}, u32[]{:S(2)}) collective-permute-start(bf16[128,512]{1,0:T(8,128)(2,1)S(1)} %get-tuple-element.47), channel_id=1, source_target_pairs={{0,24},{4,28},{8,16},{12,20},{16,8},{20,12},{24,0},{28,4},{1,25},{... | collective-permute-start | bytes 393224 | tf_op jit(solution)/shard_map/ppermute | solution.py:429
  24.9 8.8 %collective-permute-start.6 = (bf16[128,512]{1,0:T(8,128)(2,1)S(1)}, bf16[128,512]{1,0:T(8,128)(2,1)S(1)}, u32[]{:S(2)}, u32[]{:S(2)}) collective-permute-start(bf16[128,512]{1,0:T(8,128)(2,1)S(1)} %get-tuple-element.48), channel_id=1, source_target_pairs={{0,28},{4,24},{8,20},{12,16},{16,12},{20,8},{24,4},{28,0},{1,29},{... | collective-permute-start | bytes 393224 | tf_op jit(solution)/shard_map/ppermute | solution.py:429
  28.4 13.5 %collective-permute-start.9 = (bf16[512,512]{1,0:T(8,128)(2,1)S(1)}, bf16[512,512]{1,0:T(8,128)(2,1)S(1)}, u32[]{:S(2)}, u32[]{:S(2)}) collective-permute-start(bf16[512,512]{1,0:T(8,128)(2,1)S(1)} %constant_dynamic-update-slice_fusion.refs_1_.refs_0_), channel_id=1, source_target_pairs={{0,2},{1,3},{2,0},{3,1},{4,6},{5,7},{6,4},{7,5},{8,10},{9,11},{10,... | collective-permute-start | bytes 1572872 | tf_op jit(solution)/shard_map/ppermute | solution.py:422
  33.6 25.7 %collective-permute-start.17 = (bf16[512,2048]{1,0:T(8,128)(2,1)S(1)}, bf16[512,2048]{1,0:T(8,128)(2,1)S(1)}, u32[]{:S(2)}, u32[]{:S(2)}) collective-permute-start(bf16[512,2048]{1,0:T(8,128)(2,1)S(1)} %get-tuple-element.58.refs_3_), channel_id=1, source_target_pairs={{0,1},{1,0},{2,3},{3,2},{4,5},{5,4},{6,7},{7,6},{8,9},{9,8},{10,11... | collective-permute-start | bytes 6291464 | tf_op jit(solution)/shard_map/ppermute | solution.py:422
  33.7 8.8 %collective-permute-start.7 = (bf16[1024,512]{1,0:T(8,128)(2,1)S(1)}, bf16[1024,512]{1,0:T(8,128)(2,1)S(1)}, u32[]{:S(2)}, u32[]{:S(2)}) collective-permute-start(bf16[1024,512]{1,0:T(8,128)(2,1)S(1)} %fence.4), channel_id=1, source_target_pairs={{0,1},{1,0},{2,3},{3,2},{4,5},{5,4},{6,7},{7,6},{8,9},{9,8},{10,11... | collective-permute-start | bytes 3145736 | tf_op jit(solution)/shard_map/ppermute | solution.py:422
  42.5 9.2 %collective-permute-start.13 = (bf16[512,512]{1,0:T(8,128)(2,1)S(1)}, bf16[512,512]{1,0:T(8,128)(2,1)S(1)}, u32[]{:S(2)}, u32[]{:S(2)}) collective-permute-start(bf16[512,512]{1,0:T(8,128)(2,1)S(1)} %collective-permute-done.9.refs_1_.refs_2_), channel_id=1, source_target_pairs={{0,1},{1,0},{2,3},{3,2},{4,5},{5,4},{6,7},{7,6},{8,9},{9,8},{10,11... | collective-permute-start | bytes 1572872 | tf_op jit(solution)/shard_map/ppermute | solution.py:422
  42.6 14.3 %collective-permute-start.11 = (bf16[512,512]{1,0:T(8,128)(2,1)S(1)}, bf16[512,512]{1,0:T(8,128)(2,1)S(1)}, u32[]{:S(2)}, u32[]{:S(2)}) collective-permute-start(bf16[512,512]{1,0:T(8,128)(2,1)S(1)} %constant_dynamic-update-slice_fusion.4.refs_2_.refs_5_.refs_0_), channel_id=1, source_target_pairs={{0,2},{1,3},{2,0},{3,1},{4,6},{5,7},{6,4},{7,5},{8,10},{9,11},{10,... | collective-permute-start | bytes 1572872 | tf_op jit(solution)/shard_map/ppermute | solution.py:422
  44.7 12.8 %collective-permute-start.16 = (bf16[512,512]{1,0:T(8,128)(2,1)S(1)}, bf16[512,512]{1,0:T(8,128)(2,1)S(1)}, u32[]{:S(2)}, u32[]{:S(2)}) collective-permute-start(bf16[512,512]{1,0:T(8,128)(2,1)S(1)} %constant_dynamic-update-slice_fusion.4.refs_2_.refs_5_.refs_0_), channel_id=1, source_target_pairs={{0,1},{1,0},{2,3},{3,2},{4,5},{5,4},{6,7},{7,6},{8,9},{9,8},{10,11... | collective-permute-start | bytes 1572872 | tf_op jit(solution)/shard_map/ppermute | solution.py:422
  46.1 27.3 %collective-permute-start.18 = (bf16[512,512]{1,0:T(8,128)(2,1)S(1)}, bf16[512,512]{1,0:T(8,128)(2,1)S(1)}, u32[]{:S(2)}, u32[]{:S(2)}) collective-permute-start(bf16[512,512]{1,0:T(8,128)(2,1)S(1)} %project_halo.1.refs_6_), channel_id=1, source_target_pairs={{0,4},{4,8},{8,12},{12,16},{16,20},{20,24},{24,28},{1,5},{5,9},{9,... | collective-permute-start | bytes 1572872 | tf_op jit(solution)/shard_map/ppermute | solution.py:457
  64.0 13.7 %collective-permute-start.21 = (bf16[528,128]{1,0:T(8,128)(2,1)S(1)}, bf16[528,128]{1,0:T(8,128)(2,1)S(1)}, u32[]{:S(2)}, u32[]{:S(2)}) collective-permute-start(bf16[528,128]{1,0:T(8,128)(2,1)S(1)} %get-tuple-element.66), channel_id=1, source_target_pairs={{0,16},{4,20},{8,24},{12,28},{16,0},{20,4},{24,8},{28,12},{1,17},{... | collective-permute-start | bytes 405512 | tf_op jit(solution)/shard_map/ppermute | solution.py:429
  64.1 13.7 %collective-permute-start.22 = (bf16[528,128]{1,0:T(8,128)(2,1)S(1)}, bf16[528,128]{1,0:T(8,128)(2,1)S(1)}, u32[]{:S(2)}, u32[]{:S(2)}) collective-permute-start(bf16[528,128]{1,0:T(8,128)(2,1)S(1)} %get-tuple-element.67), channel_id=1, source_target_pairs={{0,20},{4,16},{8,28},{12,24},{16,4},{20,0},{24,12},{28,8},{1,21},{... | collective-permute-start | bytes 405512 | tf_op jit(solution)/shard_map/ppermute | solution.py:429
  67.6 12.1 %collective-permute-start.24 = (bf16[528,128]{1,0:T(8,128)(2,1)S(1)}, bf16[528,128]{1,0:T(8,128)(2,1)S(1)}, u32[]{:S(2)}, u32[]{:S(2)}) collective-permute-start(bf16[528,128]{1,0:T(8,128)(2,1)S(1)} %get-tuple-element.69), channel_id=1, source_target_pairs={{0,8},{4,12},{8,0},{12,4},{16,24},{20,28},{24,16},{28,20},{1,9},{5... | collective-permute-start | bytes 405512 | tf_op jit(solution)/shard_map/ppermute | solution.py:429
  67.6 14.0 %collective-permute-start.25 = (bf16[528,128]{1,0:T(8,128)(2,1)S(1)}, bf16[528,128]{1,0:T(8,128)(2,1)S(1)}, u32[]{:S(2)}, u32[]{:S(2)}) collective-permute-start(bf16[528,128]{1,0:T(8,128)(2,1)S(1)} %get-tuple-element.70), channel_id=1, source_target_pairs={{0,12},{4,8},{8,4},{12,0},{16,28},{20,24},{24,20},{28,16},{1,13},{... | collective-permute-start | bytes 405512 | tf_op jit(solution)/shard_map/ppermute | solution.py:429
  73.3 9.8 %collective-permute-start.23 = (bf16[528,128]{1,0:T(8,128)(2,1)S(1)}, bf16[528,128]{1,0:T(8,128)(2,1)S(1)}, u32[]{:S(2)}, u32[]{:S(2)}) collective-permute-start(bf16[528,128]{1,0:T(8,128)(2,1)S(1)} %fence.7), channel_id=1, source_target_pairs={{0,4},{4,0},{8,12},{12,8},{16,20},{20,16},{24,28},{28,24},{1,5},{5... | collective-permute-start | bytes 405512 | tf_op jit(solution)/shard_map/ppermute | solution.py:429
  85.2 8.3 %collective-permute-start.19 = (bf16[528,128]{1,0:T(8,128)(2,1)S(1)}, bf16[528,128]{1,0:T(8,128)(2,1)S(1)}, u32[]{:S(2)}, u32[]{:S(2)}) collective-permute-start(bf16[528,128]{1,0:T(8,128)(2,1)S(1)} %get-tuple-element.64), channel_id=1, source_target_pairs={{0,24},{4,28},{8,16},{12,20},{16,8},{20,12},{24,0},{28,4},{1,25},{... | collective-permute-start | bytes 405512 | tf_op jit(solution)/shard_map/ppermute | solution.py:429
  85.3 11.3 %collective-permute-start.20 = (bf16[528,128]{1,0:T(8,128)(2,1)S(1)}, bf16[528,128]{1,0:T(8,128)(2,1)S(1)}, u32[]{:S(2)}, u32[]{:S(2)}) collective-permute-start(bf16[528,128]{1,0:T(8,128)(2,1)S(1)} %get-tuple-element.65), channel_id=1, source_target_pairs={{0,28},{4,24},{8,20},{12,16},{16,12},{20,8},{24,4},{28,0},{1,29},{... | collective-permute-start | bytes 405512 | tf_op jit(solution)/shard_map/ppermute | solution.py:429
  91.2 20.5 %collective-permute-start.29 = (bf16[192,2048]{1,0:T(8,128)(2,1)S(1)}, bf16[192,2048]{1,0:T(8,128)(2,1)S(1)}, u32[]{:S(2)}, u32[]{:S(2)}) collective-permute-start(bf16[192,2048]{1,0:T(8,128)(2,1)S(1)} %out_project.4.refs_5_), channel_id=1, source_target_pairs={{0,2},{1,3},{2,0},{3,1},{4,6},{5,7},{6,4},{7,5},{8,10},{9,11},{10,... | collective-permute-start | bytes 2359304 | tf_op jit(solution)/shard_map/ppermute | solution.py:422
  100.7 15.5 %collective-permute-start.28 = (bf16[64,2048]{1,0:T(8,128)(2,1)S(1)}, bf16[64,2048]{1,0:T(8,128)(2,1)S(1)}, u32[]{:S(2)}, u32[]{:S(2)}) collective-permute-start(bf16[64,2048]{1,0:T(8,128)(2,1)S(1)} %out_project.6), channel_id=1, source_target_pairs={{0,2},{1,3},{2,0},{3,1},{4,6},{5,7},{6,4},{7,5},{8,10},{9,11},{10,... | collective-permute-start | bytes 786440 | tf_op jit(solution)/shard_map/ppermute | solution.py:422
  (10 other events, 72.8 us)

commit v16 on v15

--- a/solution.py
+++ b/solution.py
@@ -480,11 +480,10 @@
         0,
         [shape((rows, width))] * 2,
         (*pieces, *weights[1:], own_halo),
-        (columns[0],),
+        (columns[0], halo),
     )
     locals_ = local_part(pos, q, k, v, halo, owners, (columns[0],))
     columns = list(columns)
-    columns[1] = fence(columns[1], halo)
     columns = exchange(columns)
     sums, after = [], ()
     for share in SHARES:

time: 118 us -> 117 us (level)
  transfers between devices with their start and end apart: 30 -> 30, of which waited for: 11 -> 10; matrix products, arithmetic and copies ran while one was open for 0% -> 0% of each run, Pallas kernels for 27% -> 28%
where the time goes in v16:
time: 117 us
  starting transfers between devices  41.7 us (36%)
  waiting for transfers between devices  35.5 us (30%)
  Pallas kernels  35.4 us (30%)
  local copies, waits for them, and re-layouts  3.37 us (3%)
    ppermute x14, starting transfers between devices, move(): lax.ppermute(value, 'seq', [(i, i ^ k) for i in range(peers)])  31.6 us
    pallas_call x13, Pallas kernels, call(): pl.pallas_call(run, in_specs=specs + [ANYWHERE] * extra, out_specs=jax.tr...  29 us
    ppermute x15, waiting for transfers between devices, swap(): return lax.ppermute(value, 'head', [(i, i ^ distance) for i in range(4)])  23.1 us
    ppermute x14, waiting for transfers between devices, move(): lax.ppermute(value, 'seq', [(i, i ^ k) for i in range(peers)])  12.4 us
    ppermute x15, starting transfers between devices, swap(): return lax.ppermute(value, 'head', [(i, i ^ distance) for i in range(4)])  6.8 us
    unnamed x15, local copies, waits for them, and re-layouts  3.31 us
    ppermute x1, starting transfers between devices, chunked(): lax.ppermute(own_halo, 'seq', [(i, i + 1) for i in range(owners - 1)])  3.28 us
    pallas_call x2, Pallas kernels, join(): pl.pallas_call(functools.partial(join_kernel, share), in_specs=[IN_SMEM,...  2.98 us
  transfers between devices with their start and end apart: 30, of which 10 were waited for; matrix products, arithmetic and copies ran while one was open for 0% of the time, Pallas kernels for 28%

profile of v16, /device:TPU:0, one launch (start us, length us, event | category | flops | bytes accessed | tf_op | source)
XLA Modules:
  0.0 116.6 jit_solution(7085486189297360350)
XLA Ops:
  0.0 2.9 %collective-permute-start.8 = (bf16[1024,512]{1,0:T(8,128)(2,1)}, bf16[1024,512]{1,0:T(8,128)(2,1)S(1)}, u32[]{:S(2)}, u32[]{:S(2)}) collective-permute-start(bf16[1024,512]{1,0:T(8,128)(2,1)} %tok_hbm.1), channel_id=1, source_target_pairs={{0,2},{1,3},{2,0},{3,1},{4,6},{5,7},{6,4},{7,5},{8,10},{9,11},{10,... | collective-permute-start | bytes 3145736 | tf_op jit(solution)/shard_map/ppermute | solution.py:422
  3.0 2.1 %pack_tokens.1 = (bf16[1024,512]{1,0:T(8,128)(2,1)S(1)}, bf16[128,512]{1,0:T(8,128)(2,1)S(1)}, bf16[128,512]{1,0:T(8,128)(2,1)S(1)}, bf16[128,512]{1,0:T(8,128)(...) custom-call(s32[3]{0:T(128)S(1)} %pad_add_fusion.pos_ref.refs_0_, ...), custom_call_target="tpu_custom_call" | custom-call | bytes 2097152 | tf_op jit(solution)/shard_map/pack_tokens/pallas_call | solution.py:113
  5.1 2.7 %collective-permute-start.3 = (bf16[128,512]{1,0:T(8,128)(2,1)S(1)}, bf16[128,512]{1,0:T(8,128)(2,1)S(1)}, u32[]{:S(2)}, u32[]{:S(2)}) collective-permute-start(bf16[128,512]{1,0:T(8,128)(2,1)S(1)} %get-tuple-element.45), channel_id=1, source_target_pairs={{0,16},{4,20},{8,24},{12,28},{16,0},{20,4},{24,8},{28,12},{1,17},{... | collective-permute-start | bytes 393224 | tf_op jit(solution)/shard_map/ppermute | solution.py:429
  11.3 2.8 %collective-permute-done.after = bf16[128,512]{1,0:T(8,128)(2,1)S(1)} collective-permute-done((bf16[128,512]{1,0:T(8,128)(2,1)S(1)}, bf16[128,512]{1,0:T(8,128)(2,1)S(1)}, u32[]{:S(2)}, u32[]{:S(2)}) %collective-permute-start) | collective-permute-done | bytes 131104 | tf_op jit(solution)/shard_map/ppermute | solution.py:429
  14.0 3.8 %collective-permute-start.2 = (bf16[128,512]{1,0:T(8,128)(2,1)S(1)}, bf16[128,512]{1,0:T(8,128)(2,1)S(1)}, u32[]{:S(2)}, u32[]{:S(2)}) collective-permute-start(bf16[128,512]{1,0:T(8,128)(2,1)S(1)} %get-tuple-element.44), channel_id=1, source_target_pairs={{0,12},{4,8},{8,4},{12,0},{16,28},{20,24},{24,20},{28,16},{1,13},{... | collective-permute-start | bytes 393224 | tf_op jit(solution)/shard_map/ppermute | solution.py:429
  17.9 7.0 %collective-permute-start.5 = (bf16[128,512]{1,0:T(8,128)(2,1)S(1)}, bf16[128,512]{1,0:T(8,128)(2,1)S(1)}, u32[]{:S(2)}, u32[]{:S(2)}) collective-permute-start(bf16[128,512]{1,0:T(8,128)(2,1)S(1)} %get-tuple-element.47), channel_id=1, source_target_pairs={{0,24},{4,28},{8,16},{12,20},{16,8},{20,12},{24,0},{28,4},{1,25},{... | collective-permute-start | bytes 393224 | tf_op jit(solution)/shard_map/ppermute | solution.py:429
  24.9 3.5 %collective-permute-start.6 = (bf16[128,512]{1,0:T(8,128)(2,1)S(1)}, bf16[128,512]{1,0:T(8,128)(2,1)S(1)}, u32[]{:S(2)}, u32[]{:S(2)}) collective-permute-start(bf16[128,512]{1,0:T(8,128)(2,1)S(1)} %get-tuple-element.48), channel_id=1, source_target_pairs={{0,28},{4,24},{8,20},{12,16},{16,12},{20,8},{24,4},{28,0},{1,29},{... | collective-permute-start | bytes 393224 | tf_op jit(solution)/shard_map/ppermute | solution.py:429
  34.3 7.7 %collective-permute-done.9.refs_1_.refs_2_ = bf16[512,512]{1,0:T(8,128)(2,1)S(1)} collective-permute-done((bf16[512,512]{1,0:T(8,128)(2,1)S(1)}, bf16[512,512]{1,0:T(8,128)(2,1)S(1)}, u32[]{:S(2)}, u32[]{:S(2)}) %collective-permute-start.9) | collective-permute-done | bytes 524320 | tf_op jit(solution)/shard_map/ppermute | solution.py:422
  46.1 3.3 %collective-permute-start.18 = (bf16[512,512]{1,0:T(8,128)(2,1)S(1)}, bf16[512,512]{1,0:T(8,128)(2,1)S(1)}, u32[]{:S(2)}, u32[]{:S(2)}) collective-permute-start(bf16[512,512]{1,0:T(8,128)(2,1)S(1)} %project_halo.1.refs_6_), channel_id=1, source_target_pairs={{0,4},{4,8},{8,12},{12,16},{16,20},{20,24},{24,28},{1,5},{5,9},{9,... | collective-permute-start | bytes 1572872 | tf_op jit(solution)/shard_map/ppermute | solution.py:457
  49.3 2.3 %project_query.1.refs_7_.refs_1_ = bf16[1024,512]{1,0:T(8,128)(2,1)S(1)} custom-call(bf16[1024,512]{1,0:T(8,128)(2,1)S(1)} %get-tuple-element.40.refs_0_, bf16[1024,512]{1,0:T(8,128)(2,1)S(1)} %collective-permute-done.7.refs_1_, bf16[1024,512]{1,0:T(8,128)(2,1)S(1)} %fence.4.refs_2_, bf16[1024,512]{1,0:T(8,128)(2,1)S(1)} %collective-permute-done.10.refs_3_, ...), custom_call_target="tpu_custom_call" | custom-call | tf_op jit(solution)/shard_map/project_query/pallas_call | solution.py:39
  51.7 3.4 %project_near.1 = (bf16[512,512]{1,0:T(8,128)(2,1)S(1)}, bf16[512,512]{1,0:T(8,128)(2,1)S(1)}, bf16[512,512]{1,0:T(8,128)(2,1)S(1)}) custom-call(bf16[512,512]{1,0:T(8,128)(2,1)S(1)} %constant_dynamic-update-slice_fusion.refs_1_.refs_0_, bf16[512,512]{1,0:T(8,128)(2,1)S(1)} %collective-permute-done.12.refs_1_, ...), custom_call_target="tpu_custom_call" | custom-call | tf_op jit(solution)/shard_map/project_near/pallas_call | solution.py:39
  59.3 4.7 %column_part.1 = (bf16[528,128]{1,0:T(8,128)(2,1)S(1)}, bf16[528,128]{1,0:T(8,128)(2,1)S(1)}, bf16[528,128]{1,0:T(8,128)(2,1)S(1)}, bf16[528,128]{1,0:T(8,128)(2...) custom-call(s32[3]{0:T(128)S(1)} %pad_add_fusion.pos_ref.refs_0_, ...), custom_call_target="tpu_custom_call" | custom-call | tf_op jit(solution)/shard_map/column_part/pallas_call | solution.py:39
  64.1 3.5 %collective-permute-start.22 = (bf16[528,128]{1,0:T(8,128)(2,1)S(1)}, bf16[528,128]{1,0:T(8,128)(2,1)S(1)}, u32[]{:S(2)}, u32[]{:S(2)}) collective-permute-start(bf16[528,128]{1,0:T(8,128)(2,1)S(1)} %get-tuple-element.67), channel_id=1, source_target_pairs={{0,20},{4,16},{8,28},{12,24},{16,4},{20,0},{24,12},{28,8},{1,21},{... | collective-permute-start | bytes 405512 | tf_op jit(solution)/shard_map/ppermute | solution.py:429
  68.5 2.6 %collective-permute-start.25 = (bf16[528,128]{1,0:T(8,128)(2,1)S(1)}, bf16[528,128]{1,0:T(8,128)(2,1)S(1)}, u32[]{:S(2)}, u32[]{:S(2)}) collective-permute-start(bf16[528,128]{1,0:T(8,128)(2,1)S(1)} %get-tuple-element.70), channel_id=1, source_target_pairs={{0,12},{4,8},{8,4},{12,0},{16,28},{20,24},{24,20},{28,16},{1,13},{... | collective-permute-start | bytes 405512 | tf_op jit(solution)/shard_map/ppermute | solution.py:429
  71.1 3.4 %project_key.1 = (bf16[1024,512]{1,0:T(8,128)(2,1)S(1)}, bf16[1024,512]{1,0:T(8,128)(2,1)S(1)}) custom-call(bf16[1024,512]{1,0:T(8,128)(2,1)S(1)} %get-tuple-element.40.refs_0_, bf16[1024,512]{1,0:T(8,128)(2,1)S(1)} %collective-permute-done.7.refs_1_, bf16[1024,512]{1,0:T(8,128)(2,1)S(1)} %fence.4.refs_2_, ...), custom_call_target="tpu_custom_call" | custom-call | tf_op jit(solution)/shard_map/project_key/pallas_call | solution.py:39
  74.5 3.2 %local_part.1 = (f32[8,128,512]{2,1,0:T(8,128)S(1)}, f32[128,128]{1,0:T(8,128)S(1)}) custom-call(s32[3]{0:T(128)S(1)} %pad_add_fusion.pos_ref.refs_0_, bf16[1024,512]{1,0:T(8,128)(2,1)S(1)} %project_query.1.refs_7_.refs_1_, bf16[1024,512]{1,0:T(8,128)(2,1)S(1)} %get-tuple-element.60.refs_2_, bf16[1024,512]{1,0:T(8,128)(2,1)S(1)} %get-tuple-element.61.refs_3_, ...), custom_call_target="tpu_custom_call" | custom-call | flops 5500000256 | tf_op jit(solution)/shard_map/local_part/pallas_call | solution.py:39
  77.7 2.3 %collective-permute-done.24.refs_6_ = bf16[528,128]{1,0:T(8,128)(2,1)S(1)} collective-permute-done((bf16[528,128]{1,0:T(8,128)(2,1)S(1)}, bf16[528,128]{1,0:T(8,128)(2,1)S(1)}, u32[]{:S(2)}, u32[]{:S(2)}) %collective-permute-start.24) | collective-permute-done | bytes 135200 | tf_op jit(solution)/shard_map/ppermute | solution.py:429
  80.0 2.3 %collective-permute-done.25.refs_7_ = bf16[528,128]{1,0:T(8,128)(2,1)S(1)} collective-permute-done((bf16[528,128]{1,0:T(8,128)(2,1)S(1)}, bf16[528,128]{1,0:T(8,128)(2,1)S(1)}, u32[]{:S(2)}, u32[]{:S(2)}) %collective-permute-start.25) | collective-permute-done | bytes 135200 | tf_op jit(solution)/shard_map/ppermute | solution.py:429
  82.3 1.9 %mix.2 = (bf16[2,192,512]{2,1,0:T(8,128)(2,1)S(1)}, bf16[2,192,512]{2,1,0:T(8,128)(2,1)S(1)}) custom-call(s32[3]{0:T(128)S(1)} %pad_add_fusion.pos_ref.refs_0_, f32[8,128,512]{2,1,0:T(8,128)S(1)} %get-tuple-element.62.refs_1_, f32[128,128]{1,0:T(8,128)S(1)} %get-tuple-element.63.refs_2_, bf16[528,128]{1,0:T(8,128)(2,1)S(1)} %collective-permute-done.21.refs_3_, ...), custom_call_target="tpu_custom_call" | custom-call | flops 2200000000 | tf_op jit(solution)/shard_map/mix/pallas_call | solution.py:39
  84.4 4.1 %collective-permute-start.20 = (bf16[528,128]{1,0:T(8,128)(2,1)S(1)}, bf16[528,128]{1,0:T(8,128)(2,1)S(1)}, u32[]{:S(2)}, u32[]{:S(2)}) collective-permute-start(bf16[528,128]{1,0:T(8,128)(2,1)S(1)} %get-tuple-element.65), channel_id=1, source_target_pairs={{0,28},{4,24},{8,20},{12,16},{16,12},{20,8},{24,4},{28,0},{1,29},{... | collective-permute-start | bytes 405512 | tf_op jit(solution)/shard_map/ppermute | solution.py:429
  90.4 2.3 %collective-permute-done.19.refs_3_ = bf16[528,128]{1,0:T(8,128)(2,1)S(1)} collective-permute-done((bf16[528,128]{1,0:T(8,128)(2,1)S(1)}, bf16[528,128]{1,0:T(8,128)(2,1)S(1)}, u32[]{:S(2)}, u32[]{:S(2)}) %collective-permute-start.19) | collective-permute-done | bytes 135200 | tf_op jit(solution)/shard_map/ppermute | solution.py:429
  92.7 2.7 %collective-permute-done.20.refs_4_ = bf16[528,128]{1,0:T(8,128)(2,1)S(1)} collective-permute-done((bf16[528,128]{1,0:T(8,128)(2,1)S(1)}, bf16[528,128]{1,0:T(8,128)(2,1)S(1)}, u32[]{:S(2)}, u32[]{:S(2)}) %collective-permute-start.20) | collective-permute-done | bytes 135200 | tf_op jit(solution)/shard_map/ppermute | solution.py:429
  101.3 9.3 %collective-permute-done.29.got = bf16[192,2048]{1,0:T(8,128)(2,1)S(1)} collective-permute-done((bf16[192,2048]{1,0:T(8,128)(2,1)S(1)}, bf16[192,2048]{1,0:T(8,128)(2,1)S(1)}, u32[]{:S(2)}, u32[]{:S(2)}) %collective-permute-start.29) | collective-permute-done | bytes 786464 | tf_op jit(solution)/shard_map/ppermute | solution.py:422
  112.3 2.8 %collective-permute-done.28.got = bf16[64,2048]{1,0:T(8,128)(2,1)S(1)} collective-permute-done((bf16[64,2048]{1,0:T(8,128)(2,1)S(1)}, bf16[64,2048]{1,0:T(8,128)(2,1)S(1)}, u32[]{:S(2)}, u32[]{:S(2)}) %collective-permute-start.28) | collective-permute-done | bytes 262176 | tf_op jit(solution)/shard_map/ppermute | solution.py:422
  (76 shorter events, 29.3 us)
Async XLA Ops:
  0.0 42.0 %collective-permute-start.8 = (bf16[1024,512]{1,0:T(8,128)(2,1)}, bf16[1024,512]{1,0:T(8,128)(2,1)S(1)}, u32[]{:S(2)}, u32[]{:S(2)}) collective-permute-start(bf16[1024,512]{1,0:T(8,128)(2,1)} %tok_hbm.1), channel_id=1, source_target_pairs={{0,2},{1,3},{2,0},{3,1},{4,6},{5,7},{6,4},{7,5},{8,10},{9,11},{10,... | collective-permute-start | bytes 3145736 | tf_op jit(solution)/shard_map/ppermute | solution.py:422
  5.1 23.3 %collective-permute-start.3 = (bf16[128,512]{1,0:T(8,128)(2,1)S(1)}, bf16[128,512]{1,0:T(8,128)(2,1)S(1)}, u32[]{:S(2)}, u32[]{:S(2)}) collective-permute-start(bf16[128,512]{1,0:T(8,128)(2,1)S(1)} %get-tuple-element.45), channel_id=1, source_target_pairs={{0,16},{4,20},{8,24},{12,28},{16,0},{20,4},{24,8},{28,12},{1,17},{... | collective-permute-start | bytes 393224 | tf_op jit(solution)/shard_map/ppermute | solution.py:429
  7.8 25.8 %collective-permute-start.4 = (bf16[128,512]{1,0:T(8,128)(2,1)S(1)}, bf16[128,512]{1,0:T(8,128)(2,1)S(1)}, u32[]{:S(2)}, u32[]{:S(2)}) collective-permute-start(bf16[128,512]{1,0:T(8,128)(2,1)S(1)} %get-tuple-element.46), channel_id=1, source_target_pairs={{0,20},{4,16},{8,28},{12,24},{16,4},{20,0},{24,12},{28,8},{1,21},{... | collective-permute-start | bytes 393224 | tf_op jit(solution)/shard_map/ppermute | solution.py:429
  9.1 5.0 %collective-permute-start = (bf16[128,512]{1,0:T(8,128)(2,1)S(1)}, bf16[128,512]{1,0:T(8,128)(2,1)S(1)}, u32[]{:S(2)}, u32[]{:S(2)}) collective-permute-start(bf16[128,512]{1,0:T(8,128)(2,1)S(1)} %get-tuple-element.42), channel_id=1, source_target_pairs={{0,4},{4,0},{8,12},{12,8},{16,20},{20,16},{24,28},{28,24},{1,5},{5... | collective-permute-start | bytes 393224 | tf_op jit(solution)/shard_map/ppermute | solution.py:429
  9.6 8.3 %collective-permute-start.1 = (bf16[128,512]{1,0:T(8,128)(2,1)S(1)}, bf16[128,512]{1,0:T(8,128)(2,1)S(1)}, u32[]{:S(2)}, u32[]{:S(2)}) collective-permute-start(bf16[128,512]{1,0:T(8,128)(2,1)S(1)} %get-tuple-element.43), channel_id=1, source_target_pairs={{0,8},{4,12},{8,0},{12,4},{16,24},{20,28},{24,16},{28,20},{1,9},{5... | collective-permute-start | bytes 393224 | tf_op jit(solution)/shard_map/ppermute | solution.py:429
  14.0 10.9 %collective-permute-start.2 = (bf16[128,512]{1,0:T(8,128)(2,1)S(1)}, bf16[128,512]{1,0:T(8,128)(2,1)S(1)}, u32[]{:S(2)}, u32[]{:S(2)}) collective-permute-start(bf16[128,512]{1,0:T(8,128)(2,1)S(1)} %get-tuple-element.44), channel_id=1, source_target_pairs={{0,12},{4,8},{8,4},{12,0},{16,28},{20,24},{24,20},{28,16},{1,13},{... | collective-permute-start | bytes 393224 | tf_op jit(solution)/shard_map/ppermute | solution.py:429
  17.9 15.8 %collective-permute-start.5 = (bf16[128,512]{1,0:T(8,128)(2,1)S(1)}, bf16[128,512]{1,0:T(8,128)(2,1)S(1)}, u32[]{:S(2)}, u32[]{:S(2)}) collective-permute-start(bf16[128,512]{1,0:T(8,128)(2,1)S(1)} %get-tuple-element.47), channel_id=1, source_target_pairs={{0,24},{4,28},{8,16},{12,20},{16,8},{20,12},{24,0},{28,4},{1,25},{... | collective-permute-start | bytes 393224 | tf_op jit(solution)/shard_map/ppermute | solution.py:429
  24.9 8.8 %collective-permute-start.6 = (bf16[128,512]{1,0:T(8,128)(2,1)S(1)}, bf16[128,512]{1,0:T(8,128)(2,1)S(1)}, u32[]{:S(2)}, u32[]{:S(2)}) collective-permute-start(bf16[128,512]{1,0:T(8,128)(2,1)S(1)} %get-tuple-element.48), channel_id=1, source_target_pairs={{0,28},{4,24},{8,20},{12,16},{16,12},{20,8},{24,4},{28,0},{1,29},{... | collective-permute-start | bytes 393224 | tf_op jit(solution)/shard_map/ppermute | solution.py:429
  28.4 13.5 %collective-permute-start.9 = (bf16[512,512]{1,0:T(8,128)(2,1)S(1)}, bf16[512,512]{1,0:T(8,128)(2,1)S(1)}, u32[]{:S(2)}, u32[]{:S(2)}) collective-permute-start(bf16[512,512]{1,0:T(8,128)(2,1)S(1)} %constant_dynamic-update-slice_fusion.refs_1_.refs_0_), channel_id=1, source_target_pairs={{0,2},{1,3},{2,0},{3,1},{4,6},{5,7},{6,4},{7,5},{8,10},{9,11},{10,... | collective-permute-start | bytes 1572872 | tf_op jit(solution)/shard_map/ppermute | solution.py:422
  33.6 25.7 %collective-permute-start.17 = (bf16[512,2048]{1,0:T(8,128)(2,1)S(1)}, bf16[512,2048]{1,0:T(8,128)(2,1)S(1)}, u32[]{:S(2)}, u32[]{:S(2)}) collective-permute-start(bf16[512,2048]{1,0:T(8,128)(2,1)S(1)} %get-tuple-element.58.refs_3_), channel_id=1, source_target_pairs={{0,1},{1,0},{2,3},{3,2},{4,5},{5,4},{6,7},{7,6},{8,9},{9,8},{10,11... | collective-permute-start | bytes 6291464 | tf_op jit(solution)/shard_map/ppermute | solution.py:422
  33.7 8.8 %collective-permute-start.7 = (bf16[1024,512]{1,0:T(8,128)(2,1)S(1)}, bf16[1024,512]{1,0:T(8,128)(2,1)S(1)}, u32[]{:S(2)}, u32[]{:S(2)}) collective-permute-start(bf16[1024,512]{1,0:T(8,128)(2,1)S(1)} %fence.3), channel_id=1, source_target_pairs={{0,1},{1,0},{2,3},{3,2},{4,5},{5,4},{6,7},{7,6},{8,9},{9,8},{10,11... | collective-permute-start | bytes 3145736 | tf_op jit(solution)/shard_map/ppermute | solution.py:422
  42.5 9.2 %collective-permute-start.13 = (bf16[512,512]{1,0:T(8,128)(2,1)S(1)}, bf16[512,512]{1,0:T(8,128)(2,1)S(1)}, u32[]{:S(2)}, u32[]{:S(2)}) collective-permute-start(bf16[512,512]{1,0:T(8,128)(2,1)S(1)} %collective-permute-done.9.refs_1_.refs_2_), channel_id=1, source_target_pairs={{0,1},{1,0},{2,3},{3,2},{4,5},{5,4},{6,7},{7,6},{8,9},{9,8},{10,11... | collective-permute-start | bytes 1572872 | tf_op jit(solution)/shard_map/ppermute | solution.py:422
  42.6 14.3 %collective-permute-start.11 = (bf16[512,512]{1,0:T(8,128)(2,1)S(1)}, bf16[512,512]{1,0:T(8,128)(2,1)S(1)}, u32[]{:S(2)}, u32[]{:S(2)}) collective-permute-start(bf16[512,512]{1,0:T(8,128)(2,1)S(1)} %constant_dynamic-update-slice_fusion.4.refs_2_.refs_5_.refs_0_), channel_id=1, source_target_pairs={{0,2},{1,3},{2,0},{3,1},{4,6},{5,7},{6,4},{7,5},{8,10},{9,11},{10,... | collective-permute-start | bytes 1572872 | tf_op jit(solution)/shard_map/ppermute | solution.py:422
  44.7 12.8 %collective-permute-start.16 = (bf16[512,512]{1,0:T(8,128)(2,1)S(1)}, bf16[512,512]{1,0:T(8,128)(2,1)S(1)}, u32[]{:S(2)}, u32[]{:S(2)}) collective-permute-start(bf16[512,512]{1,0:T(8,128)(2,1)S(1)} %constant_dynamic-update-slice_fusion.4.refs_2_.refs_5_.refs_0_), channel_id=1, source_target_pairs={{0,1},{1,0},{2,3},{3,2},{4,5},{5,4},{6,7},{7,6},{8,9},{9,8},{10,11... | collective-permute-start | bytes 1572872 | tf_op jit(solution)/shard_map/ppermute | solution.py:422
  46.1 22.4 %collective-permute-start.18 = (bf16[512,512]{1,0:T(8,128)(2,1)S(1)}, bf16[512,512]{1,0:T(8,128)(2,1)S(1)}, u32[]{:S(2)}, u32[]{:S(2)}) collective-permute-start(bf16[512,512]{1,0:T(8,128)(2,1)S(1)} %project_halo.1.refs_6_), channel_id=1, source_target_pairs={{0,4},{4,8},{8,12},{12,16},{16,20},{20,24},{24,28},{1,5},{5,9},{9,... | collective-permute-start | bytes 1572872 | tf_op jit(solution)/shard_map/ppermute | solution.py:457
  64.0 13.7 %collective-permute-start.21 = (bf16[528,128]{1,0:T(8,128)(2,1)S(1)}, bf16[528,128]{1,0:T(8,128)(2,1)S(1)}, u32[]{:S(2)}, u32[]{:S(2)}) collective-permute-start(bf16[528,128]{1,0:T(8,128)(2,1)S(1)} %get-tuple-element.66), channel_id=1, source_target_pairs={{0,16},{4,20},{8,24},{12,28},{16,0},{20,4},{24,8},{28,12},{1,17},{... | collective-permute-start | bytes 405512 | tf_op jit(solution)/shard_map/ppermute | solution.py:429
  64.1 13.6 %collective-permute-start.22 = (bf16[528,128]{1,0:T(8,128)(2,1)S(1)}, bf16[528,128]{1,0:T(8,128)(2,1)S(1)}, u32[]{:S(2)}, u32[]{:S(2)}) collective-permute-start(bf16[528,128]{1,0:T(8,128)(2,1)S(1)} %get-tuple-element.67), channel_id=1, source_target_pairs={{0,20},{4,16},{8,28},{12,24},{16,4},{20,0},{24,12},{28,8},{1,21},{... | collective-permute-start | bytes 405512 | tf_op jit(solution)/shard_map/ppermute | solution.py:429
  67.6 10.2 %collective-permute-start.23 = (bf16[528,128]{1,0:T(8,128)(2,1)S(1)}, bf16[528,128]{1,0:T(8,128)(2,1)S(1)}, u32[]{:S(2)}, u32[]{:S(2)}) collective-permute-start(bf16[528,128]{1,0:T(8,128)(2,1)S(1)} %get-tuple-element.68), channel_id=1, source_target_pairs={{0,4},{4,0},{8,12},{12,8},{16,20},{20,16},{24,28},{28,24},{1,5},{5... | collective-permute-start | bytes 405512 | tf_op jit(solution)/shard_map/ppermute | solution.py:429
  68.5 11.6 %collective-permute-start.24 = (bf16[528,128]{1,0:T(8,128)(2,1)S(1)}, bf16[528,128]{1,0:T(8,128)(2,1)S(1)}, u32[]{:S(2)}, u32[]{:S(2)}) collective-permute-start(bf16[528,128]{1,0:T(8,128)(2,1)S(1)} %get-tuple-element.69), channel_id=1, source_target_pairs={{0,8},{4,12},{8,0},{12,4},{16,24},{20,28},{24,16},{28,20},{1,9},{5... | collective-permute-start | bytes 405512 | tf_op jit(solution)/shard_map/ppermute | solution.py:429
  68.5 13.9 %collective-permute-start.25 = (bf16[528,128]{1,0:T(8,128)(2,1)S(1)}, bf16[528,128]{1,0:T(8,128)(2,1)S(1)}, u32[]{:S(2)}, u32[]{:S(2)}) collective-permute-start(bf16[528,128]{1,0:T(8,128)(2,1)S(1)} %get-tuple-element.70), channel_id=1, source_target_pairs={{0,12},{4,8},{8,4},{12,0},{16,28},{20,24},{24,20},{28,16},{1,13},{... | collective-permute-start | bytes 405512 | tf_op jit(solution)/shard_map/ppermute | solution.py:429
  84.4 8.4 %collective-permute-start.19 = (bf16[528,128]{1,0:T(8,128)(2,1)S(1)}, bf16[528,128]{1,0:T(8,128)(2,1)S(1)}, u32[]{:S(2)}, u32[]{:S(2)}) collective-permute-start(bf16[528,128]{1,0:T(8,128)(2,1)S(1)} %get-tuple-element.64), channel_id=1, source_target_pairs={{0,24},{4,28},{8,16},{12,20},{16,8},{20,12},{24,0},{28,4},{1,25},{... | collective-permute-start | bytes 405512 | tf_op jit(solution)/shard_map/ppermute | solution.py:429
  84.4 11.0 %collective-permute-start.20 = (bf16[528,128]{1,0:T(8,128)(2,1)S(1)}, bf16[528,128]{1,0:T(8,128)(2,1)S(1)}, u32[]{:S(2)}, u32[]{:S(2)}) collective-permute-start(bf16[528,128]{1,0:T(8,128)(2,1)S(1)} %get-tuple-element.65), channel_id=1, source_target_pairs={{0,28},{4,24},{8,20},{12,16},{16,12},{20,8},{24,4},{28,0},{1,29},{... | collective-permute-start | bytes 405512 | tf_op jit(solution)/shard_map/ppermute | solution.py:429
  90.1 20.5 %collective-permute-start.29 = (bf16[192,2048]{1,0:T(8,128)(2,1)S(1)}, bf16[192,2048]{1,0:T(8,128)(2,1)S(1)}, u32[]{:S(2)}, u32[]{:S(2)}) collective-permute-start(bf16[192,2048]{1,0:T(8,128)(2,1)S(1)} %out_project.4.refs_5_), channel_id=1, source_target_pairs={{0,2},{1,3},{2,0},{3,1},{4,6},{5,7},{6,4},{7,5},{8,10},{9,11},{10,... | collective-permute-start | bytes 2359304 | tf_op jit(solution)/shard_map/ppermute | solution.py:422
  99.6 15.5 %collective-permute-start.28 = (bf16[64,2048]{1,0:T(8,128)(2,1)S(1)}, bf16[64,2048]{1,0:T(8,128)(2,1)S(1)}, u32[]{:S(2)}, u32[]{:S(2)}) collective-permute-start(bf16[64,2048]{1,0:T(8,128)(2,1)S(1)} %out_project.6), channel_id=1, source_target_pairs={{0,2},{1,3},{2,0},{3,1},{4,6},{5,7},{6,4},{7,5},{8,10},{9,11},{10,... | collective-permute-start | bytes 786440 | tf_op jit(solution)/shard_map/ppermute | solution.py:422
  (10 other events, 72.6 us)

commit v17 on v16

--- a/solution.py
+++ b/solution.py
@@ -284,10 +284,13 @@
     (row_j, class_j), (row_i, class_i) = row_and_class(0), row_and_class(1)
     earlier = jnp.logical_and(class_i == class_j, row_i > row_j)
     stats = []
-    for g in range(groups):
-        at = slice(g * part, (g + 1) * part)
-        heads = [slice(h * DH, (h + 1) * DH) for h in range(HEADS)]
-        operands = [[a[:, at, cols].reshape(size, DH) for a in scratch] for cols in heads]
+    heads = [slice(h * DH, (h + 1) * DH) for h in range(HEADS)]
+    for pair in range(0, groups, 2):
+        tiles = [(g, h) for g in range(pair, pair + 2) for h in range(HEADS)]
+        operands = [
+            [a[:, g * part : (g + 1) * part, heads[h]].reshape(size, DH) for a in scratch]
+            for g, h in tiles
+        ]
         scores = [jnp.where(earlier, dot_t(k, q), -1e30) for q, k, _ in operands]
         parts = [softmax_columns(s) for s in scores]
         results = [
@@ -295,12 +298,13 @@
             for (_, _, v), (p, total, _) in zip(operands, parts)
         ]
         lses = [lse for _, _, lse in parts]
-        for h, o in enumerate(results):
+        for (g, h), o in zip(tiles, results):
             o = o.T.astype(BF16)
             to = h * message + g * part
             for n in range(owners):
                 out_refs[n][to : to + part, :] = o[n * part : (n + 1) * part]
-        stats.append(jnp.concatenate(lses + lses, 0))
+        for some in (lses[:HEADS], lses[HEADS:]):
+            stats.append(jnp.concatenate(some + some, 0))
     upper = lax.broadcasted_iota(jnp.int32, (8, 128), 0) < HEADS
     blank = [jnp.zeros((8, 128 - message), F32)] if message < 128 else []
     for n in range(owners):
@@ -326,8 +330,9 @@
 
 def mix_kernel(share, pos_ref, *refs):
     count = 2 * len(CHUNKS)
-    local_refs, col_refs, (own_ref, send_ref, mixed) = refs[:count], refs[count:-3], refs[-3:]
-    per_owner = mixed.shape[1] // len(share)
+    local_refs, col_refs, (own_ref, send_ref) = refs[:count], refs[count:-2], refs[-2:]
+    per_owner = own_ref.shape[1] // len(share)
+    first_core = pos_ref[1] == 0
     base = 0
     for chunk, loc_ref, lse_ref in zip(CHUNKS, local_refs[::2], local_refs[1::2]):
         message = loc_ref.shape[1]
@@ -352,25 +357,25 @@
                 at = slice(8 * k + h, 8 * k + h + 1)
                 col = col_ref[base + h * message : base + (h + 1) * message, :].astype(F32)
                 both = loc_ref[d, :, cols] * w_loc[:, at] + col * w_col[:, at]
+                rows = []
                 for r in range(ROWS):
-                    for m, g in enumerate(chunk):
-                        start = (m * ROWS + r) * SUB
-                        to = n * per_owner + g * SUB
-                        mixed[r, to : to + SUB, cols] = both[start : start + SUB]
+                    starts = [(m * ROWS + r) * SUB for m in range(len(chunk))]
+                    rows.append(jnp.concatenate([both[t : t + SUB] for t in starts], 0))
+                to = n * per_owner + chunk[0] * SUB
+                spot = slice(to, to + len(chunk) * SUB)
+                for x in range(2):
+                    even, odd = rows[2 * x], rows[2 * x + 1]
+                    own_ref[x, spot, cols] = jnp.where(first_core, even, odd).astype(BF16)
+                    send_ref[x, spot, cols] = jnp.where(first_core, odd, even).astype(BF16)
         base += size
-    core = pos_ref[1]
-    for x in range(2):
-        own_ref[x] = mixed[2 * x + core].astype(BF16)
-        send_ref[x] = mixed[2 * x + 1 - core].astype(BF16)
 
 
 def mix(pos, share, columns, locals_, after):
     owners, _, width = locals_[0][0].shape
     tokens = len(share) * STRIDE // owners
     shapes = [shape((2, tokens, width))] * 2
-    scratch = [pltpu.VMEM((ROWS, tokens, width), F32)]
     args = (pos, *[x for pair in locals_ for x in pair], *columns)
-    return call(functools.partial(mix_kernel, share), "mix", 2, shapes, args, after, scratch)
+    return call(functools.partial(mix_kernel, share), "mix", 2, shapes, args, after)
 
 
 def out_kernel(here, pos_ref, a_ref, b_ref, wa_ref, wb_ref, out_ref):

time: 117 us -> 116 us (level)
  transfers between devices with their start and end apart: 30 -> 30, of which waited for: 10 -> 10; matrix products, arithmetic and copies ran while one was open for 0% -> 0% of each run, Pallas kernels for 28% -> 27%
where the time goes in v17:
time: 116 us
  starting transfers between devices  41.7 us (36%)
  waiting for transfers between devices  35.6 us (31%)
  Pallas kernels  35.1 us (30%)
  local copies, waits for them, and re-layouts  3.37 us (3%)
    ppermute x14, starting transfers between devices, move(): lax.ppermute(value, 'seq', [(i, i ^ k) for i in range(peers)])  31.6 us
    pallas_call x13, Pallas kernels, call(): pl.pallas_call(run, in_specs=specs + [ANYWHERE] * extra, out_specs=jax.tr...  28.7 us
    ppermute x15, waiting for transfers between devices, swap(): return lax.ppermute(value, 'head', [(i, i ^ distance) for i in range(4)])  23.2 us
    ppermute x14, waiting for transfers between devices, move(): lax.ppermute(value, 'seq', [(i, i ^ k) for i in range(peers)])  12.4 us
    ppermute x15, starting transfers between devices, swap(): return lax.ppermute(value, 'head', [(i, i ^ distance) for i in range(4)])  6.78 us
    unnamed x15, local copies, waits for them, and re-layouts  3.31 us
    ppermute x1, starting transfers between devices, chunked(): lax.ppermute(own_halo, 'seq', [(i, i + 1) for i in range(owners - 1)])  3.28 us
    pallas_call x2, Pallas kernels, join(): pl.pallas_call(functools.partial(join_kernel, share), in_specs=[IN_SMEM,...  2.98 us
  transfers between devices with their start and end apart: 30, of which 10 were waited for; matrix products, arithmetic and copies ran while one was open for 0% of the time, Pallas kernels for 27%

profile of v17, /device:TPU:0, one launch (start us, length us, event | category | flops | bytes accessed | tf_op | source)
XLA Modules:
  0.0 116.3 jit_solution(13565859566890914722)
XLA Ops:
  0.0 2.9 %collective-permute-start.8 = (bf16[1024,512]{1,0:T(8,128)(2,1)}, bf16[1024,512]{1,0:T(8,128)(2,1)S(1)}, u32[]{:S(2)}, u32[]{:S(2)}) collective-permute-start(bf16[1024,512]{1,0:T(8,128)(2,1)} %tok_hbm.1), channel_id=1, source_target_pairs={{0,2},{1,3},{2,0},{3,1},{4,6},{5,7},{6,4},{7,5},{8,10},{9,11},{10,... | collective-permute-start | bytes 3145736 | tf_op jit(solution)/shard_map/ppermute | solution.py:427
  3.0 2.1 %pack_tokens.1 = (bf16[1024,512]{1,0:T(8,128)(2,1)S(1)}, bf16[128,512]{1,0:T(8,128)(2,1)S(1)}, bf16[128,512]{1,0:T(8,128)(2,1)S(1)}, bf16[128,512]{1,0:T(8,128)(...) custom-call(s32[3]{0:T(128)S(1)} %pad_add_fusion.pos_ref.refs_0_, ...), custom_call_target="tpu_custom_call" | custom-call | bytes 2097152 | tf_op jit(solution)/shard_map/pack_tokens/pallas_call | solution.py:113
  5.1 2.7 %collective-permute-start.3 = (bf16[128,512]{1,0:T(8,128)(2,1)S(1)}, bf16[128,512]{1,0:T(8,128)(2,1)S(1)}, u32[]{:S(2)}, u32[]{:S(2)}) collective-permute-start(bf16[128,512]{1,0:T(8,128)(2,1)S(1)} %get-tuple-element.45), channel_id=1, source_target_pairs={{0,16},{4,20},{8,24},{12,28},{16,0},{20,4},{24,8},{28,12},{1,17},{... | collective-permute-start | bytes 393224 | tf_op jit(solution)/shard_map/ppermute | solution.py:434
  11.3 2.8 %collective-permute-done.after = bf16[128,512]{1,0:T(8,128)(2,1)S(1)} collective-permute-done((bf16[128,512]{1,0:T(8,128)(2,1)S(1)}, bf16[128,512]{1,0:T(8,128)(2,1)S(1)}, u32[]{:S(2)}, u32[]{:S(2)}) %collective-permute-start) | collective-permute-done | bytes 131104 | tf_op jit(solution)/shard_map/ppermute | solution.py:434
  14.0 3.8 %collective-permute-start.2 = (bf16[128,512]{1,0:T(8,128)(2,1)S(1)}, bf16[128,512]{1,0:T(8,128)(2,1)S(1)}, u32[]{:S(2)}, u32[]{:S(2)}) collective-permute-start(bf16[128,512]{1,0:T(8,128)(2,1)S(1)} %get-tuple-element.44), channel_id=1, source_target_pairs={{0,12},{4,8},{8,4},{12,0},{16,28},{20,24},{24,20},{28,16},{1,13},{... | collective-permute-start | bytes 393224 | tf_op jit(solution)/shard_map/ppermute | solution.py:434
  17.9 7.0 %collective-permute-start.5 = (bf16[128,512]{1,0:T(8,128)(2,1)S(1)}, bf16[128,512]{1,0:T(8,128)(2,1)S(1)}, u32[]{:S(2)}, u32[]{:S(2)}) collective-permute-start(bf16[128,512]{1,0:T(8,128)(2,1)S(1)} %get-tuple-element.47), channel_id=1, source_target_pairs={{0,24},{4,28},{8,16},{12,20},{16,8},{20,12},{24,0},{28,4},{1,25},{... | collective-permute-start | bytes 393224 | tf_op jit(solution)/shard_map/ppermute | solution.py:434
  24.9 3.5 %collective-permute-start.6 = (bf16[128,512]{1,0:T(8,128)(2,1)S(1)}, bf16[128,512]{1,0:T(8,128)(2,1)S(1)}, u32[]{:S(2)}, u32[]{:S(2)}) collective-permute-start(bf16[128,512]{1,0:T(8,128)(2,1)S(1)} %get-tuple-element.48), channel_id=1, source_target_pairs={{0,28},{4,24},{8,20},{12,16},{16,12},{20,8},{24,4},{28,0},{1,29},{... | collective-permute-start | bytes 393224 | tf_op jit(solution)/shard_map/ppermute | solution.py:434
  34.3 7.7 %collective-permute-done.9.refs_1_.refs_2_ = bf16[512,512]{1,0:T(8,128)(2,1)S(1)} collective-permute-done((bf16[512,512]{1,0:T(8,128)(2,1)S(1)}, bf16[512,512]{1,0:T(8,128)(2,1)S(1)}, u32[]{:S(2)}, u32[]{:S(2)}) %collective-permute-start.9) | collective-permute-done | bytes 524320 | tf_op jit(solution)/shard_map/ppermute | solution.py:427
  46.1 3.3 %collective-permute-start.18 = (bf16[512,512]{1,0:T(8,128)(2,1)S(1)}, bf16[512,512]{1,0:T(8,128)(2,1)S(1)}, u32[]{:S(2)}, u32[]{:S(2)}) collective-permute-start(bf16[512,512]{1,0:T(8,128)(2,1)S(1)} %project_halo.1.refs_6_), channel_id=1, source_target_pairs={{0,4},{4,8},{8,12},{12,16},{16,20},{20,24},{24,28},{1,5},{5,9},{9,... | collective-permute-start | bytes 1572872 | tf_op jit(solution)/shard_map/ppermute | solution.py:462
  49.3 2.3 %project_query.1.refs_7_.refs_1_ = bf16[1024,512]{1,0:T(8,128)(2,1)S(1)} custom-call(bf16[1024,512]{1,0:T(8,128)(2,1)S(1)} %get-tuple-element.40.refs_0_, bf16[1024,512]{1,0:T(8,128)(2,1)S(1)} %collective-permute-done.7.refs_1_, bf16[1024,512]{1,0:T(8,128)(2,1)S(1)} %fence.4.refs_2_, bf16[1024,512]{1,0:T(8,128)(2,1)S(1)} %collective-permute-done.10.refs_3_, ...), custom_call_target="tpu_custom_call" | custom-call | tf_op jit(solution)/shard_map/project_query/pallas_call | solution.py:39
  51.7 3.4 %project_near.1 = (bf16[512,512]{1,0:T(8,128)(2,1)S(1)}, bf16[512,512]{1,0:T(8,128)(2,1)S(1)}, bf16[512,512]{1,0:T(8,128)(2,1)S(1)}) custom-call(bf16[512,512]{1,0:T(8,128)(2,1)S(1)} %constant_dynamic-update-slice_fusion.refs_1_.refs_0_, bf16[512,512]{1,0:T(8,128)(2,1)S(1)} %collective-permute-done.12.refs_1_, ...), custom_call_target="tpu_custom_call" | custom-call | tf_op jit(solution)/shard_map/project_near/pallas_call | solution.py:39
  59.3 4.5 %column_part.1 = (bf16[528,128]{1,0:T(8,128)(2,1)S(1)}, bf16[528,128]{1,0:T(8,128)(2,1)S(1)}, bf16[528,128]{1,0:T(8,128)(2,1)S(1)}, bf16[528,128]{1,0:T(8,128)(2...) custom-call(s32[3]{0:T(128)S(1)} %pad_add_fusion.pos_ref.refs_0_, ...), custom_call_target="tpu_custom_call" | custom-call | tf_op jit(solution)/shard_map/column_part/pallas_call | solution.py:39
  63.8 3.5 %collective-permute-start.22 = (bf16[528,128]{1,0:T(8,128)(2,1)S(1)}, bf16[528,128]{1,0:T(8,128)(2,1)S(1)}, u32[]{:S(2)}, u32[]{:S(2)}) collective-permute-start(bf16[528,128]{1,0:T(8,128)(2,1)S(1)} %get-tuple-element.67), channel_id=1, source_target_pairs={{0,20},{4,16},{8,28},{12,24},{16,4},{20,0},{24,12},{28,8},{1,21},{... | collective-permute-start | bytes 405512 | tf_op jit(solution)/shard_map/ppermute | solution.py:434
  68.2 2.6 %collective-permute-start.25 = (bf16[528,128]{1,0:T(8,128)(2,1)S(1)}, bf16[528,128]{1,0:T(8,128)(2,1)S(1)}, u32[]{:S(2)}, u32[]{:S(2)}) collective-permute-start(bf16[528,128]{1,0:T(8,128)(2,1)S(1)} %get-tuple-element.70), channel_id=1, source_target_pairs={{0,12},{4,8},{8,4},{12,0},{16,28},{20,24},{24,20},{28,16},{1,13},{... | collective-permute-start | bytes 405512 | tf_op jit(solution)/shard_map/ppermute | solution.py:434
  70.8 3.4 %project_key.1 = (bf16[1024,512]{1,0:T(8,128)(2,1)S(1)}, bf16[1024,512]{1,0:T(8,128)(2,1)S(1)}) custom-call(bf16[1024,512]{1,0:T(8,128)(2,1)S(1)} %get-tuple-element.40.refs_0_, bf16[1024,512]{1,0:T(8,128)(2,1)S(1)} %collective-permute-done.7.refs_1_, bf16[1024,512]{1,0:T(8,128)(2,1)S(1)} %fence.4.refs_2_, ...), custom_call_target="tpu_custom_call" | custom-call | tf_op jit(solution)/shard_map/project_key/pallas_call | solution.py:39
  74.2 3.2 %local_part.1 = (f32[8,128,512]{2,1,0:T(8,128)S(1)}, f32[128,128]{1,0:T(8,128)S(1)}) custom-call(s32[3]{0:T(128)S(1)} %pad_add_fusion.pos_ref.refs_0_, bf16[1024,512]{1,0:T(8,128)(2,1)S(1)} %project_query.1.refs_7_.refs_1_, bf16[1024,512]{1,0:T(8,128)(2,1)S(1)} %get-tuple-element.60.refs_2_, bf16[1024,512]{1,0:T(8,128)(2,1)S(1)} %get-tuple-element.61.refs_3_, ...), custom_call_target="tpu_custom_call" | custom-call | flops 5500000256 | tf_op jit(solution)/shard_map/local_part/pallas_call | solution.py:39
  77.5 2.3 %collective-permute-done.24.refs_6_ = bf16[528,128]{1,0:T(8,128)(2,1)S(1)} collective-permute-done((bf16[528,128]{1,0:T(8,128)(2,1)S(1)}, bf16[528,128]{1,0:T(8,128)(2,1)S(1)}, u32[]{:S(2)}, u32[]{:S(2)}) %collective-permute-start.24) | collective-permute-done | bytes 135200 | tf_op jit(solution)/shard_map/ppermute | solution.py:434
  79.8 2.3 %collective-permute-done.25.refs_7_ = bf16[528,128]{1,0:T(8,128)(2,1)S(1)} collective-permute-done((bf16[528,128]{1,0:T(8,128)(2,1)S(1)}, bf16[528,128]{1,0:T(8,128)(2,1)S(1)}, u32[]{:S(2)}, u32[]{:S(2)}) %collective-permute-start.25) | collective-permute-done | bytes 135200 | tf_op jit(solution)/shard_map/ppermute | solution.py:434
  82.1 1.9 %mix.2 = (bf16[2,192,512]{2,1,0:T(8,128)(2,1)S(1)}, bf16[2,192,512]{2,1,0:T(8,128)(2,1)S(1)}) custom-call(s32[3]{0:T(128)S(1)} %pad_add_fusion.pos_ref.refs_0_, f32[8,128,512]{2,1,0:T(8,128)S(1)} %get-tuple-element.62.refs_1_, f32[128,128]{1,0:T(8,128)S(1)} %get-tuple-element.63.refs_2_, bf16[528,128]{1,0:T(8,128)(2,1)S(1)} %collective-permute-done.21.refs_3_, ...), custom_call_target="tpu_custom_call" | custom-call | flops 2200000000 | tf_op jit(solution)/shard_map/mix/pallas_call | solution.py:39
  84.1 4.1 %collective-permute-start.20 = (bf16[528,128]{1,0:T(8,128)(2,1)S(1)}, bf16[528,128]{1,0:T(8,128)(2,1)S(1)}, u32[]{:S(2)}, u32[]{:S(2)}) collective-permute-start(bf16[528,128]{1,0:T(8,128)(2,1)S(1)} %get-tuple-element.65), channel_id=1, source_target_pairs={{0,28},{4,24},{8,20},{12,16},{16,12},{20,8},{24,4},{28,0},{1,29},{... | collective-permute-start | bytes 405512 | tf_op jit(solution)/shard_map/ppermute | solution.py:434
  90.1 2.3 %collective-permute-done.19.refs_3_ = bf16[528,128]{1,0:T(8,128)(2,1)S(1)} collective-permute-done((bf16[528,128]{1,0:T(8,128)(2,1)S(1)}, bf16[528,128]{1,0:T(8,128)(2,1)S(1)}, u32[]{:S(2)}, u32[]{:S(2)}) %collective-permute-start.19) | collective-permute-done | bytes 135200 | tf_op jit(solution)/shard_map/ppermute | solution.py:434
  92.4 2.7 %collective-permute-done.20.refs_4_ = bf16[528,128]{1,0:T(8,128)(2,1)S(1)} collective-permute-done((bf16[528,128]{1,0:T(8,128)(2,1)S(1)}, bf16[528,128]{1,0:T(8,128)(2,1)S(1)}, u32[]{:S(2)}, u32[]{:S(2)}) %collective-permute-start.20) | collective-permute-done | bytes 135200 | tf_op jit(solution)/shard_map/ppermute | solution.py:434
  101.0 9.3 %collective-permute-done.29.got = bf16[192,2048]{1,0:T(8,128)(2,1)S(1)} collective-permute-done((bf16[192,2048]{1,0:T(8,128)(2,1)S(1)}, bf16[192,2048]{1,0:T(8,128)(2,1)S(1)}, u32[]{:S(2)}, u32[]{:S(2)}) %collective-permute-start.29) | collective-permute-done | bytes 786464 | tf_op jit(solution)/shard_map/ppermute | solution.py:427
  112.0 2.8 %collective-permute-done.28.got = bf16[64,2048]{1,0:T(8,128)(2,1)S(1)} collective-permute-done((bf16[64,2048]{1,0:T(8,128)(2,1)S(1)}, bf16[64,2048]{1,0:T(8,128)(2,1)S(1)}, u32[]{:S(2)}, u32[]{:S(2)}) %collective-permute-start.28) | collective-permute-done | bytes 262176 | tf_op jit(solution)/shard_map/ppermute | solution.py:427
  (76 shorter events, 29.3 us)
Async XLA Ops:
  0.0 42.0 %collective-permute-start.8 = (bf16[1024,512]{1,0:T(8,128)(2,1)}, bf16[1024,512]{1,0:T(8,128)(2,1)S(1)}, u32[]{:S(2)}, u32[]{:S(2)}) collective-permute-start(bf16[1024,512]{1,0:T(8,128)(2,1)} %tok_hbm.1), channel_id=1, source_target_pairs={{0,2},{1,3},{2,0},{3,1},{4,6},{5,7},{6,4},{7,5},{8,10},{9,11},{10,... | collective-permute-start | bytes 3145736 | tf_op jit(solution)/shard_map/ppermute | solution.py:427
  5.1 23.3 %collective-permute-start.3 = (bf16[128,512]{1,0:T(8,128)(2,1)S(1)}, bf16[128,512]{1,0:T(8,128)(2,1)S(1)}, u32[]{:S(2)}, u32[]{:S(2)}) collective-permute-start(bf16[128,512]{1,0:T(8,128)(2,1)S(1)} %get-tuple-element.45), channel_id=1, source_target_pairs={{0,16},{4,20},{8,24},{12,28},{16,0},{20,4},{24,8},{28,12},{1,17},{... | collective-permute-start | bytes 393224 | tf_op jit(solution)/shard_map/ppermute | solution.py:434
  7.8 25.8 %collective-permute-start.4 = (bf16[128,512]{1,0:T(8,128)(2,1)S(1)}, bf16[128,512]{1,0:T(8,128)(2,1)S(1)}, u32[]{:S(2)}, u32[]{:S(2)}) collective-permute-start(bf16[128,512]{1,0:T(8,128)(2,1)S(1)} %get-tuple-element.46), channel_id=1, source_target_pairs={{0,20},{4,16},{8,28},{12,24},{16,4},{20,0},{24,12},{28,8},{1,21},{... | collective-permute-start | bytes 393224 | tf_op jit(solution)/shard_map/ppermute | solution.py:434
  9.1 5.0 %collective-permute-start = (bf16[128,512]{1,0:T(8,128)(2,1)S(1)}, bf16[128,512]{1,0:T(8,128)(2,1)S(1)}, u32[]{:S(2)}, u32[]{:S(2)}) collective-permute-start(bf16[128,512]{1,0:T(8,128)(2,1)S(1)} %get-tuple-element.42), channel_id=1, source_target_pairs={{0,4},{4,0},{8,12},{12,8},{16,20},{20,16},{24,28},{28,24},{1,5},{5... | collective-permute-start | bytes 393224 | tf_op jit(solution)/shard_map/ppermute | solution.py:434
  9.6 8.3 %collective-permute-start.1 = (bf16[128,512]{1,0:T(8,128)(2,1)S(1)}, bf16[128,512]{1,0:T(8,128)(2,1)S(1)}, u32[]{:S(2)}, u32[]{:S(2)}) collective-permute-start(bf16[128,512]{1,0:T(8,128)(2,1)S(1)} %get-tuple-element.43), channel_id=1, source_target_pairs={{0,8},{4,12},{8,0},{12,4},{16,24},{20,28},{24,16},{28,20},{1,9},{5... | collective-permute-start | bytes 393224 | tf_op jit(solution)/shard_map/ppermute | solution.py:434
  14.0 10.9 %collective-permute-start.2 = (bf16[128,512]{1,0:T(8,128)(2,1)S(1)}, bf16[128,512]{1,0:T(8,128)(2,1)S(1)}, u32[]{:S(2)}, u32[]{:S(2)}) collective-permute-start(bf16[128,512]{1,0:T(8,128)(2,1)S(1)} %get-tuple-element.44), channel_id=1, source_target_pairs={{0,12},{4,8},{8,4},{12,0},{16,28},{20,24},{24,20},{28,16},{1,13},{... | collective-permute-start | bytes 393224 | tf_op jit(solution)/shard_map/ppermute | solution.py:434
  17.9 15.8 %collective-permute-start.5 = (bf16[128,512]{1,0:T(8,128)(2,1)S(1)}, bf16[128,512]{1,0:T(8,128)(2,1)S(1)}, u32[]{:S(2)}, u32[]{:S(2)}) collective-permute-start(bf16[128,512]{1,0:T(8,128)(2,1)S(1)} %get-tuple-element.47), channel_id=1, source_target_pairs={{0,24},{4,28},{8,16},{12,20},{16,8},{20,12},{24,0},{28,4},{1,25},{... | collective-permute-start | bytes 393224 | tf_op jit(solution)/shard_map/ppermute | solution.py:434
  24.9 8.8 %collective-permute-start.6 = (bf16[128,512]{1,0:T(8,128)(2,1)S(1)}, bf16[128,512]{1,0:T(8,128)(2,1)S(1)}, u32[]{:S(2)}, u32[]{:S(2)}) collective-permute-start(bf16[128,512]{1,0:T(8,128)(2,1)S(1)} %get-tuple-element.48), channel_id=1, source_target_pairs={{0,28},{4,24},{8,20},{12,16},{16,12},{20,8},{24,4},{28,0},{1,29},{... | collective-permute-start | bytes 393224 | tf_op jit(solution)/shard_map/ppermute | solution.py:434
  28.4 13.5 %collective-permute-start.9 = (bf16[512,512]{1,0:T(8,128)(2,1)S(1)}, bf16[512,512]{1,0:T(8,128)(2,1)S(1)}, u32[]{:S(2)}, u32[]{:S(2)}) collective-permute-start(bf16[512,512]{1,0:T(8,128)(2,1)S(1)} %constant_dynamic-update-slice_fusion.refs_1_.refs_0_), channel_id=1, source_target_pairs={{0,2},{1,3},{2,0},{3,1},{4,6},{5,7},{6,4},{7,5},{8,10},{9,11},{10,... | collective-permute-start | bytes 1572872 | tf_op jit(solution)/shard_map/ppermute | solution.py:427
  33.6 25.7 %collective-permute-start.17 = (bf16[512,2048]{1,0:T(8,128)(2,1)S(1)}, bf16[512,2048]{1,0:T(8,128)(2,1)S(1)}, u32[]{:S(2)}, u32[]{:S(2)}) collective-permute-start(bf16[512,2048]{1,0:T(8,128)(2,1)S(1)} %get-tuple-element.58.refs_3_), channel_id=1, source_target_pairs={{0,1},{1,0},{2,3},{3,2},{4,5},{5,4},{6,7},{7,6},{8,9},{9,8},{10,11... | collective-permute-start | bytes 6291464 | tf_op jit(solution)/shard_map/ppermute | solution.py:427
  33.7 8.8 %collective-permute-start.7 = (bf16[1024,512]{1,0:T(8,128)(2,1)S(1)}, bf16[1024,512]{1,0:T(8,128)(2,1)S(1)}, u32[]{:S(2)}, u32[]{:S(2)}) collective-permute-start(bf16[1024,512]{1,0:T(8,128)(2,1)S(1)} %fence.3), channel_id=1, source_target_pairs={{0,1},{1,0},{2,3},{3,2},{4,5},{5,4},{6,7},{7,6},{8,9},{9,8},{10,11... | collective-permute-start | bytes 3145736 | tf_op jit(solution)/shard_map/ppermute | solution.py:427
  42.5 9.2 %collective-permute-start.13 = (bf16[512,512]{1,0:T(8,128)(2,1)S(1)}, bf16[512,512]{1,0:T(8,128)(2,1)S(1)}, u32[]{:S(2)}, u32[]{:S(2)}) collective-permute-start(bf16[512,512]{1,0:T(8,128)(2,1)S(1)} %collective-permute-done.9.refs_1_.refs_2_), channel_id=1, source_target_pairs={{0,1},{1,0},{2,3},{3,2},{4,5},{5,4},{6,7},{7,6},{8,9},{9,8},{10,11... | collective-permute-start | bytes 1572872 | tf_op jit(solution)/shard_map/ppermute | solution.py:427
  42.6 14.3 %collective-permute-start.11 = (bf16[512,512]{1,0:T(8,128)(2,1)S(1)}, bf16[512,512]{1,0:T(8,128)(2,1)S(1)}, u32[]{:S(2)}, u32[]{:S(2)}) collective-permute-start(bf16[512,512]{1,0:T(8,128)(2,1)S(1)} %constant_dynamic-update-slice_fusion.4.refs_2_.refs_5_.refs_0_), channel_id=1, source_target_pairs={{0,2},{1,3},{2,0},{3,1},{4,6},{5,7},{6,4},{7,5},{8,10},{9,11},{10,... | collective-permute-start | bytes 1572872 | tf_op jit(solution)/shard_map/ppermute | solution.py:427
  44.7 12.8 %collective-permute-start.16 = (bf16[512,512]{1,0:T(8,128)(2,1)S(1)}, bf16[512,512]{1,0:T(8,128)(2,1)S(1)}, u32[]{:S(2)}, u32[]{:S(2)}) collective-permute-start(bf16[512,512]{1,0:T(8,128)(2,1)S(1)} %constant_dynamic-update-slice_fusion.4.refs_2_.refs_5_.refs_0_), channel_id=1, source_target_pairs={{0,1},{1,0},{2,3},{3,2},{4,5},{5,4},{6,7},{7,6},{8,9},{9,8},{10,11... | collective-permute-start | bytes 1572872 | tf_op jit(solution)/shard_map/ppermute | solution.py:427
  46.1 22.2 %collective-permute-start.18 = (bf16[512,512]{1,0:T(8,128)(2,1)S(1)}, bf16[512,512]{1,0:T(8,128)(2,1)S(1)}, u32[]{:S(2)}, u32[]{:S(2)}) collective-permute-start(bf16[512,512]{1,0:T(8,128)(2,1)S(1)} %project_halo.1.refs_6_), channel_id=1, source_target_pairs={{0,4},{4,8},{8,12},{12,16},{16,20},{20,24},{24,28},{1,5},{5,9},{9,... | collective-permute-start | bytes 1572872 | tf_op jit(solution)/shard_map/ppermute | solution.py:462
  63.8 13.7 %collective-permute-start.21 = (bf16[528,128]{1,0:T(8,128)(2,1)S(1)}, bf16[528,128]{1,0:T(8,128)(2,1)S(1)}, u32[]{:S(2)}, u32[]{:S(2)}) collective-permute-start(bf16[528,128]{1,0:T(8,128)(2,1)S(1)} %get-tuple-element.66), channel_id=1, source_target_pairs={{0,16},{4,20},{8,24},{12,28},{16,0},{20,4},{24,8},{28,12},{1,17},{... | collective-permute-start | bytes 405512 | tf_op jit(solution)/shard_map/ppermute | solution.py:434
  63.8 13.7 %collective-permute-start.22 = (bf16[528,128]{1,0:T(8,128)(2,1)S(1)}, bf16[528,128]{1,0:T(8,128)(2,1)S(1)}, u32[]{:S(2)}, u32[]{:S(2)}) collective-permute-start(bf16[528,128]{1,0:T(8,128)(2,1)S(1)} %get-tuple-element.67), channel_id=1, source_target_pairs={{0,20},{4,16},{8,28},{12,24},{16,4},{20,0},{24,12},{28,8},{1,21},{... | collective-permute-start | bytes 405512 | tf_op jit(solution)/shard_map/ppermute | solution.py:434
  67.3 10.2 %collective-permute-start.23 = (bf16[528,128]{1,0:T(8,128)(2,1)S(1)}, bf16[528,128]{1,0:T(8,128)(2,1)S(1)}, u32[]{:S(2)}, u32[]{:S(2)}) collective-permute-start(bf16[528,128]{1,0:T(8,128)(2,1)S(1)} %get-tuple-element.68), channel_id=1, source_target_pairs={{0,4},{4,0},{8,12},{12,8},{16,20},{20,16},{24,28},{28,24},{1,5},{5... | collective-permute-start | bytes 405512 | tf_op jit(solution)/shard_map/ppermute | solution.py:434
  68.2 11.6 %collective-permute-start.24 = (bf16[528,128]{1,0:T(8,128)(2,1)S(1)}, bf16[528,128]{1,0:T(8,128)(2,1)S(1)}, u32[]{:S(2)}, u32[]{:S(2)}) collective-permute-start(bf16[528,128]{1,0:T(8,128)(2,1)S(1)} %get-tuple-element.69), channel_id=1, source_target_pairs={{0,8},{4,12},{8,0},{12,4},{16,24},{20,28},{24,16},{28,20},{1,9},{5... | collective-permute-start | bytes 405512 | tf_op jit(solution)/shard_map/ppermute | solution.py:434
  68.2 13.9 %collective-permute-start.25 = (bf16[528,128]{1,0:T(8,128)(2,1)S(1)}, bf16[528,128]{1,0:T(8,128)(2,1)S(1)}, u32[]{:S(2)}, u32[]{:S(2)}) collective-permute-start(bf16[528,128]{1,0:T(8,128)(2,1)S(1)} %get-tuple-element.70), channel_id=1, source_target_pairs={{0,12},{4,8},{8,4},{12,0},{16,28},{20,24},{24,20},{28,16},{1,13},{... | collective-permute-start | bytes 405512 | tf_op jit(solution)/shard_map/ppermute | solution.py:434
  84.1 8.4 %collective-permute-start.19 = (bf16[528,128]{1,0:T(8,128)(2,1)S(1)}, bf16[528,128]{1,0:T(8,128)(2,1)S(1)}, u32[]{:S(2)}, u32[]{:S(2)}) collective-permute-start(bf16[528,128]{1,0:T(8,128)(2,1)S(1)} %get-tuple-element.64), channel_id=1, source_target_pairs={{0,24},{4,28},{8,16},{12,20},{16,8},{20,12},{24,0},{28,4},{1,25},{... | collective-permute-start | bytes 405512 | tf_op jit(solution)/shard_map/ppermute | solution.py:434
  84.1 11.0 %collective-permute-start.20 = (bf16[528,128]{1,0:T(8,128)(2,1)S(1)}, bf16[528,128]{1,0:T(8,128)(2,1)S(1)}, u32[]{:S(2)}, u32[]{:S(2)}) collective-permute-start(bf16[528,128]{1,0:T(8,128)(2,1)S(1)} %get-tuple-element.65), channel_id=1, source_target_pairs={{0,28},{4,24},{8,20},{12,16},{16,12},{20,8},{24,4},{28,0},{1,29},{... | collective-permute-start | bytes 405512 | tf_op jit(solution)/shard_map/ppermute | solution.py:434
  89.8 20.5 %collective-permute-start.29 = (bf16[192,2048]{1,0:T(8,128)(2,1)S(1)}, bf16[192,2048]{1,0:T(8,128)(2,1)S(1)}, u32[]{:S(2)}, u32[]{:S(2)}) collective-permute-start(bf16[192,2048]{1,0:T(8,128)(2,1)S(1)} %out_project.4.refs_5_), channel_id=1, source_target_pairs={{0,2},{1,3},{2,0},{3,1},{4,6},{5,7},{6,4},{7,5},{8,10},{9,11},{10,... | collective-permute-start | bytes 2359304 | tf_op jit(solution)/shard_map/ppermute | solution.py:427
  99.3 15.6 %collective-permute-start.28 = (bf16[64,2048]{1,0:T(8,128)(2,1)S(1)}, bf16[64,2048]{1,0:T(8,128)(2,1)S(1)}, u32[]{:S(2)}, u32[]{:S(2)}) collective-permute-start(bf16[64,2048]{1,0:T(8,128)(2,1)S(1)} %out_project.6), channel_id=1, source_target_pairs={{0,2},{1,3},{2,0},{3,1},{4,6},{5,7},{6,4},{7,5},{8,10},{9,11},{10,... | collective-permute-start | bytes 786440 | tf_op jit(solution)/shard_map/ppermute | solution.py:427
  (10 other events, 72.6 us)

commit v18 on v17

--- a/solution.py
+++ b/solution.py
@@ -15,7 +15,7 @@
 CHUNKS = ((0, 1, 2, 3),)
 NEAR = 4
 PEERS = 8
-SHARES = ((4, 5, 1, 2, 3, 0), (6, 7))
+SHARES = ((4, 5, 1, 2, 0), (6, 7, 3))
 SCALE2 = DH ** (-0.5) * 1.4426950408889634
 FLOOR = -1e29
 MIB = 1024 * 1024

time: 116 us -> 123 us (1.060)
  waiting for transfers between devices: 35.6 us -> 44.2 us
  starting transfers between devices: 41.7 us -> 40.3 us
    ppermute x15, waiting for transfers between devices: 23.2 us -> 29.5 us  [swap(): return lax.ppermute(value, 'head', [(i, i ^ distance) for i in range(4)])]
    ppermute x14, waiting for transfers between devices: 12.4 us -> 14.7 us  [move(): lax.ppermute(value, 'seq', [(i, i ^ k) for i in range(peers)])]
    ppermute x14, starting transfers between devices: 31.6 us -> 29.5 us  [move(): lax.ppermute(value, 'seq', [(i, i ^ k) for i in range(peers)])]
  transfers between devices with their start and end apart: 30 -> 30, of which waited for: 10 -> 12; matrix products, arithmetic and copies ran while one was open for 0% -> 0% of each run, Pallas kernels for 27% -> 25%
where the time goes in v18:
time: 123 us
  waiting for transfers between devices  44.2 us (36%)
  starting transfers between devices  40.3 us (33%)
  Pallas kernels  34.5 us (28%)
  local copies, waits for them, and re-layouts  3.37 us (3%)
    ppermute x14, starting transfers between devices, move(): lax.ppermute(value, 'seq', [(i, i ^ k) for i in range(peers)])  29.5 us
    ppermute x15, waiting for transfers between devices, swap(): return lax.ppermute(value, 'head', [(i, i ^ distance) for i in range(4)])  29.5 us
    pallas_call x13, Pallas kernels, call(): pl.pallas_call(run, in_specs=specs + [ANYWHERE] * extra, out_specs=jax.tr...  28.2 us
    ppermute x14, waiting for transfers between devices, move(): lax.ppermute(value, 'seq', [(i, i ^ k) for i in range(peers)])  14.7 us
    ppermute x15, starting transfers between devices, swap(): return lax.ppermute(value, 'head', [(i, i ^ distance) for i in range(4)])  7.48 us
    unnamed x15, local copies, waits for them, and re-layouts  3.31 us
    ppermute x1, starting transfers between devices, chunked(): lax.ppermute(own_halo, 'seq', [(i, i + 1) for i in range(owners - 1)])  3.28 us
    pallas_call x2, Pallas kernels, join(): pl.pallas_call(functools.partial(join_kernel, share), in_specs=[IN_SMEM,...  2.93 us
  transfers between devices with their start and end apart: 30, of which 12 were waited for; matrix products, arithmetic and copies ran while one was open for 0% of the time, Pallas kernels for 25%

profile of v18, /device:TPU:0, one launch (start us, length us, event | category | flops | bytes accessed | tf_op | source)
XLA Modules:
  0.0 122.9 jit_solution(8438738845600018738)
XLA Ops:
  0.0 2.9 %collective-permute-start.8 = (bf16[1024,512]{1,0:T(8,128)(2,1)}, bf16[1024,512]{1,0:T(8,128)(2,1)S(1)}, u32[]{:S(2)}, u32[]{:S(2)}) collective-permute-start(bf16[1024,512]{1,0:T(8,128)(2,1)} %tok_hbm.1), channel_id=1, source_target_pairs={{0,2},{1,3},{2,0},{3,1},{4,6},{5,7},{6,4},{7,5},{8,10},{9,11},{10,... | collective-permute-start | bytes 3145736 | tf_op jit(solution)/shard_map/ppermute | solution.py:427
  3.0 2.1 %pack_tokens.1 = (bf16[1024,512]{1,0:T(8,128)(2,1)S(1)}, bf16[128,512]{1,0:T(8,128)(2,1)S(1)}, bf16[128,512]{1,0:T(8,128)(2,1)S(1)}, bf16[128,512]{1,0:T(8,128)(...) custom-call(s32[3]{0:T(128)S(1)} %pad_add_fusion.pos_ref.refs_0_, ...), custom_call_target="tpu_custom_call" | custom-call | bytes 2097152 | tf_op jit(solution)/shard_map/pack_tokens/pallas_call | solution.py:113
  5.1 2.7 %collective-permute-start.3 = (bf16[128,512]{1,0:T(8,128)(2,1)S(1)}, bf16[128,512]{1,0:T(8,128)(2,1)S(1)}, u32[]{:S(2)}, u32[]{:S(2)}) collective-permute-start(bf16[128,512]{1,0:T(8,128)(2,1)S(1)} %get-tuple-element.45), channel_id=1, source_target_pairs={{0,16},{4,20},{8,24},{12,28},{16,0},{20,4},{24,8},{28,12},{1,17},{... | collective-permute-start | bytes 393224 | tf_op jit(solution)/shard_map/ppermute | solution.py:434
  11.3 2.8 %collective-permute-done.after = bf16[128,512]{1,0:T(8,128)(2,1)S(1)} collective-permute-done((bf16[128,512]{1,0:T(8,128)(2,1)S(1)}, bf16[128,512]{1,0:T(8,128)(2,1)S(1)}, u32[]{:S(2)}, u32[]{:S(2)}) %collective-permute-start) | collective-permute-done | bytes 131104 | tf_op jit(solution)/shard_map/ppermute | solution.py:434
  14.0 3.8 %collective-permute-start.2 = (bf16[128,512]{1,0:T(8,128)(2,1)S(1)}, bf16[128,512]{1,0:T(8,128)(2,1)S(1)}, u32[]{:S(2)}, u32[]{:S(2)}) collective-permute-start(bf16[128,512]{1,0:T(8,128)(2,1)S(1)} %get-tuple-element.44), channel_id=1, source_target_pairs={{0,12},{4,8},{8,4},{12,0},{16,28},{20,24},{24,20},{28,16},{1,13},{... | collective-permute-start | bytes 393224 | tf_op jit(solution)/shard_map/ppermute | solution.py:434
  17.9 7.0 %collective-permute-start.5 = (bf16[128,512]{1,0:T(8,128)(2,1)S(1)}, bf16[128,512]{1,0:T(8,128)(2,1)S(1)}, u32[]{:S(2)}, u32[]{:S(2)}) collective-permute-start(bf16[128,512]{1,0:T(8,128)(2,1)S(1)} %get-tuple-element.47), channel_id=1, source_target_pairs={{0,24},{4,28},{8,16},{12,20},{16,8},{20,12},{24,0},{28,4},{1,25},{... | collective-permute-start | bytes 393224 | tf_op jit(solution)/shard_map/ppermute | solution.py:434
  24.9 3.5 %collective-permute-start.6 = (bf16[128,512]{1,0:T(8,128)(2,1)S(1)}, bf16[128,512]{1,0:T(8,128)(2,1)S(1)}, u32[]{:S(2)}, u32[]{:S(2)}) collective-permute-start(bf16[128,512]{1,0:T(8,128)(2,1)S(1)} %get-tuple-element.48), channel_id=1, source_target_pairs={{0,28},{4,24},{8,20},{12,16},{16,12},{20,8},{24,4},{28,0},{1,29},{... | collective-permute-start | bytes 393224 | tf_op jit(solution)/shard_map/ppermute | solution.py:434
  34.3 7.7 %collective-permute-done.9.refs_1_.refs_2_ = bf16[512,512]{1,0:T(8,128)(2,1)S(1)} collective-permute-done((bf16[512,512]{1,0:T(8,128)(2,1)S(1)}, bf16[512,512]{1,0:T(8,128)(2,1)S(1)}, u32[]{:S(2)}, u32[]{:S(2)}) %collective-permute-start.9) | collective-permute-done | bytes 524320 | tf_op jit(solution)/shard_map/ppermute | solution.py:427
  46.1 3.3 %collective-permute-start.18 = (bf16[512,512]{1,0:T(8,128)(2,1)S(1)}, bf16[512,512]{1,0:T(8,128)(2,1)S(1)}, u32[]{:S(2)}, u32[]{:S(2)}) collective-permute-start(bf16[512,512]{1,0:T(8,128)(2,1)S(1)} %project_halo.1.refs_6_), channel_id=1, source_target_pairs={{0,4},{4,8},{8,12},{12,16},{16,20},{20,24},{24,28},{1,5},{5,9},{9,... | collective-permute-start | bytes 1572872 | tf_op jit(solution)/shard_map/ppermute | solution.py:462
  49.3 2.3 %project_query.1.refs_7_.refs_1_ = bf16[1024,512]{1,0:T(8,128)(2,1)S(1)} custom-call(bf16[1024,512]{1,0:T(8,128)(2,1)S(1)} %get-tuple-element.40.refs_0_, bf16[1024,512]{1,0:T(8,128)(2,1)S(1)} %collective-permute-done.7.refs_1_, bf16[1024,512]{1,0:T(8,128)(2,1)S(1)} %fence.4.refs_2_, bf16[1024,512]{1,0:T(8,128)(2,1)S(1)} %collective-permute-done.10.refs_3_, ...), custom_call_target="tpu_custom_call" | custom-call | tf_op jit(solution)/shard_map/project_query/pallas_call | solution.py:39
  51.7 3.4 %project_near.1 = (bf16[512,512]{1,0:T(8,128)(2,1)S(1)}, bf16[512,512]{1,0:T(8,128)(2,1)S(1)}, bf16[512,512]{1,0:T(8,128)(2,1)S(1)}) custom-call(bf16[512,512]{1,0:T(8,128)(2,1)S(1)} %constant_dynamic-update-slice_fusion.refs_1_.refs_0_, bf16[512,512]{1,0:T(8,128)(2,1)S(1)} %collective-permute-done.12.refs_1_, ...), custom_call_target="tpu_custom_call" | custom-call | tf_op jit(solution)/shard_map/project_near/pallas_call | solution.py:39
  55.1 1.7 %collective-permute-done.11.refs_0_ = bf16[512,512]{1,0:T(8,128)(2,1)S(1)} collective-permute-done((bf16[512,512]{1,0:T(8,128)(2,1)S(1)}, bf16[512,512]{1,0:T(8,128)(2,1)S(1)}, u32[]{:S(2)}, u32[]{:S(2)}) %collective-permute-start.11) | collective-permute-done | bytes 524320 | tf_op jit(solution)/shard_map/ppermute | solution.py:427
  57.5 1.8 %half_sums.1 = (f32[512,512]{1,0:T(8,128)S(1)}, f32[512,512]{1,0:T(8,128)S(1)}, f32[512,512]{1,0:T(8,128)S(1)}) custom-call(bf16[512,512]{1,0:T(8,128)(2,1)S(1)} %constant_dynamic-update-slice_fusion.4.refs_2_.refs_5_.refs_0_, bf16[512,512]{1,0:T(8,128)(2,1)S(1)} %collective-permute-done.16.refs_1_, ...), custom_call_target="tpu_custom_call" | custom-call | tf_op jit(solution)/shard_map/half_sums/pallas_call | solution.py:39
  59.3 4.5 %column_part.1 = (bf16[528,128]{1,0:T(8,128)(2,1)S(1)}, bf16[528,128]{1,0:T(8,128)(2,1)S(1)}, bf16[528,128]{1,0:T(8,128)(2,1)S(1)}, bf16[528,128]{1,0:T(8,128)(2...) custom-call(s32[3]{0:T(128)S(1)} %pad_add_fusion.pos_ref.refs_0_, ...), custom_call_target="tpu_custom_call" | custom-call | tf_op jit(solution)/shard_map/column_part/pallas_call | solution.py:39
  63.8 3.5 %collective-permute-start.23 = (bf16[528,128]{1,0:T(8,128)(2,1)S(1)}, bf16[528,128]{1,0:T(8,128)(2,1)S(1)}, u32[]{:S(2)}, u32[]{:S(2)}) collective-permute-start(bf16[528,128]{1,0:T(8,128)(2,1)S(1)} %get-tuple-element.68), channel_id=1, source_target_pairs={{0,20},{4,16},{8,28},{12,24},{16,4},{20,0},{24,12},{28,8},{1,21},{... | collective-permute-start | bytes 405512 | tf_op jit(solution)/shard_map/ppermute | solution.py:434
  68.2 3.4 %project_key.1 = (bf16[1024,512]{1,0:T(8,128)(2,1)S(1)}, bf16[1024,512]{1,0:T(8,128)(2,1)S(1)}) custom-call(bf16[1024,512]{1,0:T(8,128)(2,1)S(1)} %get-tuple-element.40.refs_0_, bf16[1024,512]{1,0:T(8,128)(2,1)S(1)} %collective-permute-done.7.refs_1_, bf16[1024,512]{1,0:T(8,128)(2,1)S(1)} %fence.4.refs_2_, ...), custom_call_target="tpu_custom_call" | custom-call | tf_op jit(solution)/shard_map/project_key/pallas_call | solution.py:39
  71.6 3.3 %local_part.1 = (f32[8,128,512]{2,1,0:T(8,128)S(1)}, f32[128,128]{1,0:T(8,128)S(1)}) custom-call(s32[3]{0:T(128)S(1)} %pad_add_fusion.pos_ref.refs_0_, bf16[1024,512]{1,0:T(8,128)(2,1)S(1)} %project_query.1.refs_7_.refs_1_, bf16[1024,512]{1,0:T(8,128)(2,1)S(1)} %get-tuple-element.60.refs_2_, bf16[1024,512]{1,0:T(8,128)(2,1)S(1)} %get-tuple-element.61.refs_3_, ...), custom_call_target="tpu_custom_call" | custom-call | flops 5500000256 | tf_op jit(solution)/shard_map/local_part/pallas_call | solution.py:39
  74.9 2.3 %collective-permute-done.23.refs_4_ = bf16[528,128]{1,0:T(8,128)(2,1)S(1)} collective-permute-done((bf16[528,128]{1,0:T(8,128)(2,1)S(1)}, bf16[528,128]{1,0:T(8,128)(2,1)S(1)}, u32[]{:S(2)}, u32[]{:S(2)}) %collective-permute-start.23) | collective-permute-done | bytes 135200 | tf_op jit(solution)/shard_map/ppermute | solution.py:434
  81.2 3.7 %collective-permute-start.20 = (bf16[528,128]{1,0:T(8,128)(2,1)S(1)}, bf16[528,128]{1,0:T(8,128)(2,1)S(1)}, u32[]{:S(2)}, u32[]{:S(2)}) collective-permute-start(bf16[528,128]{1,0:T(8,128)(2,1)S(1)} %get-tuple-element.65), channel_id=1, source_target_pairs={{0,28},{4,24},{8,20},{12,16},{16,12},{20,8},{24,4},{28,0},{1,29},{... | collective-permute-start | bytes 405512 | tf_op jit(solution)/shard_map/ppermute | solution.py:434
  86.3 2.6 %collective-permute-done.19.refs_3_ = bf16[528,128]{1,0:T(8,128)(2,1)S(1)} collective-permute-done((bf16[528,128]{1,0:T(8,128)(2,1)S(1)}, bf16[528,128]{1,0:T(8,128)(2,1)S(1)}, u32[]{:S(2)}, u32[]{:S(2)}) %collective-permute-start.19) | collective-permute-done | bytes 135200 | tf_op jit(solution)/shard_map/ppermute | solution.py:434
  88.9 3.4 %collective-permute-done.20.refs_4_ = bf16[528,128]{1,0:T(8,128)(2,1)S(1)} collective-permute-done((bf16[528,128]{1,0:T(8,128)(2,1)S(1)}, bf16[528,128]{1,0:T(8,128)(2,1)S(1)}, u32[]{:S(2)}, u32[]{:S(2)}) %collective-permute-start.20) | collective-permute-done | bytes 135200 | tf_op jit(solution)/shard_map/ppermute | solution.py:434
  92.3 2.2 %collective-permute-done.21.refs_5_ = bf16[528,128]{1,0:T(8,128)(2,1)S(1)} collective-permute-done((bf16[528,128]{1,0:T(8,128)(2,1)S(1)}, bf16[528,128]{1,0:T(8,128)(2,1)S(1)}, u32[]{:S(2)}, u32[]{:S(2)}) %collective-permute-start.21) | collective-permute-done | bytes 135200 | tf_op jit(solution)/shard_map/ppermute | solution.py:434
  102.1 11.2 %collective-permute-done.29.got = bf16[160,2048]{1,0:T(8,128)(2,1)S(1)} collective-permute-done((bf16[160,2048]{1,0:T(8,128)(2,1)S(1)}, bf16[160,2048]{1,0:T(8,128)(2,1)S(1)}, u32[]{:S(2)}, u32[]{:S(2)}) %collective-permute-start.29) | collective-permute-done | bytes 655392 | tf_op jit(solution)/shard_map/ppermute | solution.py:427
  114.9 6.5 %collective-permute-done.28.got = bf16[96,2048]{1,0:T(8,128)(2,1)S(1)} collective-permute-done((bf16[96,2048]{1,0:T(8,128)(2,1)S(1)}, bf16[96,2048]{1,0:T(8,128)(2,1)S(1)}, u32[]{:S(2)}, u32[]{:S(2)}) %collective-permute-start.28) | collective-permute-done | bytes 393248 | tf_op jit(solution)/shard_map/ppermute | solution.py:427
  (76 shorter events, 30.9 us)
Async XLA Ops:
  0.0 42.0 %collective-permute-start.8 = (bf16[1024,512]{1,0:T(8,128)(2,1)}, bf16[1024,512]{1,0:T(8,128)(2,1)S(1)}, u32[]{:S(2)}, u32[]{:S(2)}) collective-permute-start(bf16[1024,512]{1,0:T(8,128)(2,1)} %tok_hbm.1), channel_id=1, source_target_pairs={{0,2},{1,3},{2,0},{3,1},{4,6},{5,7},{6,4},{7,5},{8,10},{9,11},{10,... | collective-permute-start | bytes 3145736 | tf_op jit(solution)/shard_map/ppermute | solution.py:427
  5.1 23.3 %collective-permute-start.3 = (bf16[128,512]{1,0:T(8,128)(2,1)S(1)}, bf16[128,512]{1,0:T(8,128)(2,1)S(1)}, u32[]{:S(2)}, u32[]{:S(2)}) collective-permute-start(bf16[128,512]{1,0:T(8,128)(2,1)S(1)} %get-tuple-element.45), channel_id=1, source_target_pairs={{0,16},{4,20},{8,24},{12,28},{16,0},{20,4},{24,8},{28,12},{1,17},{... | collective-permute-start | bytes 393224 | tf_op jit(solution)/shard_map/ppermute | solution.py:434
  7.8 25.8 %collective-permute-start.4 = (bf16[128,512]{1,0:T(8,128)(2,1)S(1)}, bf16[128,512]{1,0:T(8,128)(2,1)S(1)}, u32[]{:S(2)}, u32[]{:S(2)}) collective-permute-start(bf16[128,512]{1,0:T(8,128)(2,1)S(1)} %get-tuple-element.46), channel_id=1, source_target_pairs={{0,20},{4,16},{8,28},{12,24},{16,4},{20,0},{24,12},{28,8},{1,21},{... | collective-permute-start | bytes 393224 | tf_op jit(solution)/shard_map/ppermute | solution.py:434
  9.1 5.0 %collective-permute-start = (bf16[128,512]{1,0:T(8,128)(2,1)S(1)}, bf16[128,512]{1,0:T(8,128)(2,1)S(1)}, u32[]{:S(2)}, u32[]{:S(2)}) collective-permute-start(bf16[128,512]{1,0:T(8,128)(2,1)S(1)} %get-tuple-element.42), channel_id=1, source_target_pairs={{0,4},{4,0},{8,12},{12,8},{16,20},{20,16},{24,28},{28,24},{1,5},{5... | collective-permute-start | bytes 393224 | tf_op jit(solution)/shard_map/ppermute | solution.py:434
  9.6 8.3 %collective-permute-start.1 = (bf16[128,512]{1,0:T(8,128)(2,1)S(1)}, bf16[128,512]{1,0:T(8,128)(2,1)S(1)}, u32[]{:S(2)}, u32[]{:S(2)}) collective-permute-start(bf16[128,512]{1,0:T(8,128)(2,1)S(1)} %get-tuple-element.43), channel_id=1, source_target_pairs={{0,8},{4,12},{8,0},{12,4},{16,24},{20,28},{24,16},{28,20},{1,9},{5... | collective-permute-start | bytes 393224 | tf_op jit(solution)/shard_map/ppermute | solution.py:434
  14.0 10.9 %collective-permute-start.2 = (bf16[128,512]{1,0:T(8,128)(2,1)S(1)}, bf16[128,512]{1,0:T(8,128)(2,1)S(1)}, u32[]{:S(2)}, u32[]{:S(2)}) collective-permute-start(bf16[128,512]{1,0:T(8,128)(2,1)S(1)} %get-tuple-element.44), channel_id=1, source_target_pairs={{0,12},{4,8},{8,4},{12,0},{16,28},{20,24},{24,20},{28,16},{1,13},{... | collective-permute-start | bytes 393224 | tf_op jit(solution)/shard_map/ppermute | solution.py:434
  17.9 15.8 %collective-permute-start.5 = (bf16[128,512]{1,0:T(8,128)(2,1)S(1)}, bf16[128,512]{1,0:T(8,128)(2,1)S(1)}, u32[]{:S(2)}, u32[]{:S(2)}) collective-permute-start(bf16[128,512]{1,0:T(8,128)(2,1)S(1)} %get-tuple-element.47), channel_id=1, source_target_pairs={{0,24},{4,28},{8,16},{12,20},{16,8},{20,12},{24,0},{28,4},{1,25},{... | collective-permute-start | bytes 393224 | tf_op jit(solution)/shard_map/ppermute | solution.py:434
  24.9 8.8 %collective-permute-start.6 = (bf16[128,512]{1,0:T(8,128)(2,1)S(1)}, bf16[128,512]{1,0:T(8,128)(2,1)S(1)}, u32[]{:S(2)}, u32[]{:S(2)}) collective-permute-start(bf16[128,512]{1,0:T(8,128)(2,1)S(1)} %get-tuple-element.48), channel_id=1, source_target_pairs={{0,28},{4,24},{8,20},{12,16},{16,12},{20,8},{24,4},{28,0},{1,29},{... | collective-permute-start | bytes 393224 | tf_op jit(solution)/shard_map/ppermute | solution.py:434
  28.4 13.5 %collective-permute-start.9 = (bf16[512,512]{1,0:T(8,128)(2,1)S(1)}, bf16[512,512]{1,0:T(8,128)(2,1)S(1)}, u32[]{:S(2)}, u32[]{:S(2)}) collective-permute-start(bf16[512,512]{1,0:T(8,128)(2,1)S(1)} %constant_dynamic-update-slice_fusion.refs_1_.refs_0_), channel_id=1, source_target_pairs={{0,2},{1,3},{2,0},{3,1},{4,6},{5,7},{6,4},{7,5},{8,10},{9,11},{10,... | collective-permute-start | bytes 1572872 | tf_op jit(solution)/shard_map/ppermute | solution.py:427
  33.6 25.7 %collective-permute-start.17 = (bf16[512,2048]{1,0:T(8,128)(2,1)S(1)}, bf16[512,2048]{1,0:T(8,128)(2,1)S(1)}, u32[]{:S(2)}, u32[]{:S(2)}) collective-permute-start(bf16[512,2048]{1,0:T(8,128)(2,1)S(1)} %get-tuple-element.58.refs_3_), channel_id=1, source_target_pairs={{0,1},{1,0},{2,3},{3,2},{4,5},{5,4},{6,7},{7,6},{8,9},{9,8},{10,11... | collective-permute-start | bytes 6291464 | tf_op jit(solution)/shard_map/ppermute | solution.py:427
  33.7 8.8 %collective-permute-start.7 = (bf16[1024,512]{1,0:T(8,128)(2,1)S(1)}, bf16[1024,512]{1,0:T(8,128)(2,1)S(1)}, u32[]{:S(2)}, u32[]{:S(2)}) collective-permute-start(bf16[1024,512]{1,0:T(8,128)(2,1)S(1)} %fence.3), channel_id=1, source_target_pairs={{0,1},{1,0},{2,3},{3,2},{4,5},{5,4},{6,7},{7,6},{8,9},{9,8},{10,11... | collective-permute-start | bytes 3145736 | tf_op jit(solution)/shard_map/ppermute | solution.py:427
  42.5 9.2 %collective-permute-start.13 = (bf16[512,512]{1,0:T(8,128)(2,1)S(1)}, bf16[512,512]{1,0:T(8,128)(2,1)S(1)}, u32[]{:S(2)}, u32[]{:S(2)}) collective-permute-start(bf16[512,512]{1,0:T(8,128)(2,1)S(1)} %collective-permute-done.9.refs_1_.refs_2_), channel_id=1, source_target_pairs={{0,1},{1,0},{2,3},{3,2},{4,5},{5,4},{6,7},{7,6},{8,9},{9,8},{10,11... | collective-permute-start | bytes 1572872 | tf_op jit(solution)/shard_map/ppermute | solution.py:427
  42.6 14.3 %collective-permute-start.11 = (bf16[512,512]{1,0:T(8,128)(2,1)S(1)}, bf16[512,512]{1,0:T(8,128)(2,1)S(1)}, u32[]{:S(2)}, u32[]{:S(2)}) collective-permute-start(bf16[512,512]{1,0:T(8,128)(2,1)S(1)} %constant_dynamic-update-slice_fusion.4.refs_2_.refs_5_.refs_0_), channel_id=1, source_target_pairs={{0,2},{1,3},{2,0},{3,1},{4,6},{5,7},{6,4},{7,5},{8,10},{9,11},{10,... | collective-permute-start | bytes 1572872 | tf_op jit(solution)/shard_map/ppermute | solution.py:427
  44.7 12.8 %collective-permute-start.16 = (bf16[512,512]{1,0:T(8,128)(2,1)S(1)}, bf16[512,512]{1,0:T(8,128)(2,1)S(1)}, u32[]{:S(2)}, u32[]{:S(2)}) collective-permute-start(bf16[512,512]{1,0:T(8,128)(2,1)S(1)} %constant_dynamic-update-slice_fusion.4.refs_2_.refs_5_.refs_0_), channel_id=1, source_target_pairs={{0,1},{1,0},{2,3},{3,2},{4,5},{5,4},{6,7},{7,6},{8,9},{9,8},{10,11... | collective-permute-start | bytes 1572872 | tf_op jit(solution)/shard_map/ppermute | solution.py:427
  46.1 22.2 %collective-permute-start.18 = (bf16[512,512]{1,0:T(8,128)(2,1)S(1)}, bf16[512,512]{1,0:T(8,128)(2,1)S(1)}, u32[]{:S(2)}, u32[]{:S(2)}) collective-permute-start(bf16[512,512]{1,0:T(8,128)(2,1)S(1)} %project_halo.1.refs_6_), channel_id=1, source_target_pairs={{0,4},{4,8},{8,12},{12,16},{16,20},{20,24},{24,28},{1,5},{5,9},{9,... | collective-permute-start | bytes 1572872 | tf_op jit(solution)/shard_map/ppermute | solution.py:462
  63.8 11.1 %collective-permute-start.22 = (bf16[528,128]{1,0:T(8,128)(2,1)S(1)}, bf16[528,128]{1,0:T(8,128)(2,1)S(1)}, u32[]{:S(2)}, u32[]{:S(2)}) collective-permute-start(bf16[528,128]{1,0:T(8,128)(2,1)S(1)} %get-tuple-element.67), channel_id=1, source_target_pairs={{0,16},{4,20},{8,24},{12,28},{16,0},{20,4},{24,8},{28,12},{1,17},{... | collective-permute-start | bytes 405512 | tf_op jit(solution)/shard_map/ppermute | solution.py:434
  63.8 13.3 %collective-permute-start.23 = (bf16[528,128]{1,0:T(8,128)(2,1)S(1)}, bf16[528,128]{1,0:T(8,128)(2,1)S(1)}, u32[]{:S(2)}, u32[]{:S(2)}) collective-permute-start(bf16[528,128]{1,0:T(8,128)(2,1)S(1)} %get-tuple-element.68), channel_id=1, source_target_pairs={{0,20},{4,16},{8,28},{12,24},{16,4},{20,0},{24,12},{28,8},{1,21},{... | collective-permute-start | bytes 405512 | tf_op jit(solution)/shard_map/ppermute | solution.py:434
  67.3 9.8 %collective-permute-start.24 = (bf16[528,128]{1,0:T(8,128)(2,1)S(1)}, bf16[528,128]{1,0:T(8,128)(2,1)S(1)}, u32[]{:S(2)}, u32[]{:S(2)}) collective-permute-start(bf16[528,128]{1,0:T(8,128)(2,1)S(1)} %get-tuple-element.69), channel_id=1, source_target_pairs={{0,4},{4,0},{8,12},{12,8},{16,20},{20,16},{24,28},{28,24},{1,5},{5... | collective-permute-start | bytes 405512 | tf_op jit(solution)/shard_map/ppermute | solution.py:434
  68.2 10.4 %collective-permute-start.25 = (bf16[528,128]{1,0:T(8,128)(2,1)S(1)}, bf16[528,128]{1,0:T(8,128)(2,1)S(1)}, u32[]{:S(2)}, u32[]{:S(2)}) collective-permute-start(bf16[528,128]{1,0:T(8,128)(2,1)S(1)} %get-tuple-element.70), channel_id=1, source_target_pairs={{0,8},{4,12},{8,0},{12,4},{16,24},{20,28},{24,16},{28,20},{1,9},{5... | collective-permute-start | bytes 405512 | tf_op jit(solution)/shard_map/ppermute | solution.py:434
  80.2 8.7 %collective-permute-start.19 = (bf16[528,128]{1,0:T(8,128)(2,1)S(1)}, bf16[528,128]{1,0:T(8,128)(2,1)S(1)}, u32[]{:S(2)}, u32[]{:S(2)}) collective-permute-start(bf16[528,128]{1,0:T(8,128)(2,1)S(1)} %get-tuple-element.64), channel_id=1, source_target_pairs={{0,24},{4,28},{8,16},{12,20},{16,8},{20,12},{24,0},{28,4},{1,25},{... | collective-permute-start | bytes 405512 | tf_op jit(solution)/shard_map/ppermute | solution.py:434
  81.2 11.0 %collective-permute-start.20 = (bf16[528,128]{1,0:T(8,128)(2,1)S(1)}, bf16[528,128]{1,0:T(8,128)(2,1)S(1)}, u32[]{:S(2)}, u32[]{:S(2)}) collective-permute-start(bf16[528,128]{1,0:T(8,128)(2,1)S(1)} %get-tuple-element.65), channel_id=1, source_target_pairs={{0,28},{4,24},{8,20},{12,16},{16,12},{20,8},{24,4},{28,0},{1,29},{... | collective-permute-start | bytes 405512 | tf_op jit(solution)/shard_map/ppermute | solution.py:434
  84.9 9.6 %collective-permute-start.21 = (bf16[528,128]{1,0:T(8,128)(2,1)S(1)}, bf16[528,128]{1,0:T(8,128)(2,1)S(1)}, u32[]{:S(2)}, u32[]{:S(2)}) collective-permute-start(bf16[528,128]{1,0:T(8,128)(2,1)S(1)} %get-tuple-element.66), channel_id=1, source_target_pairs={{0,12},{4,8},{8,4},{12,0},{16,28},{20,24},{24,20},{28,16},{1,13},{... | collective-permute-start | bytes 405512 | tf_op jit(solution)/shard_map/ppermute | solution.py:434
  95.8 17.6 %collective-permute-start.29 = (bf16[160,2048]{1,0:T(8,128)(2,1)S(1)}, bf16[160,2048]{1,0:T(8,128)(2,1)S(1)}, u32[]{:S(2)}, u32[]{:S(2)}) collective-permute-start(bf16[160,2048]{1,0:T(8,128)(2,1)S(1)} %out_project.4.refs_6_), channel_id=1, source_target_pairs={{0,2},{1,3},{2,0},{3,1},{4,6},{5,7},{6,4},{7,5},{8,10},{9,11},{10,... | collective-permute-start | bytes 1966088 | tf_op jit(solution)/shard_map/ppermute | solution.py:427
  98.6 22.7 %collective-permute-start.28 = (bf16[96,2048]{1,0:T(8,128)(2,1)S(1)}, bf16[96,2048]{1,0:T(8,128)(2,1)S(1)}, u32[]{:S(2)}, u32[]{:S(2)}) collective-permute-start(bf16[96,2048]{1,0:T(8,128)(2,1)S(1)} %out_project.6), channel_id=1, source_target_pairs={{0,2},{1,3},{2,0},{3,1},{4,6},{5,7},{6,4},{7,5},{8,10},{9,11},{10,... | collective-permute-start | bytes 1179656 | tf_op jit(solution)/shard_map/ppermute | solution.py:427
  (10 other events, 73.0 us)

commit v19 on v18

--- a/solution.py
+++ b/solution.py
@@ -15,7 +15,7 @@
 CHUNKS = ((0, 1, 2, 3),)
 NEAR = 4
 PEERS = 8
-SHARES = ((4, 5, 1, 2, 0), (6, 7, 3))
+SHARES = ((4, 5, 3, 2, 1, 0), (6, 7))
 SCALE2 = DH ** (-0.5) * 1.4426950408889634
 FLOOR = -1e29
 MIB = 1024 * 1024

time: 123 us -> 116 us (0.943)
  waiting for transfers between devices: 44.2 us -> 34.3 us
  starting transfers between devices: 40.3 us -> 42.4 us
    ppermute x15, waiting for transfers between devices: 29.5 us -> 22.9 us  [swap(): return lax.ppermute(value, 'head', [(i, i ^ distance) for i in range(4)])]
    ppermute x14, waiting for transfers between devices: 14.7 us -> 11.4 us  [move(): lax.ppermute(value, 'seq', [(i, i ^ k) for i in range(peers)])]
    ppermute x14, starting transfers between devices: 29.5 us -> 31.9 us  [move(): lax.ppermute(value, 'seq', [(i, i ^ k) for i in range(peers)])]
  transfers between devices with their start and end apart: 30 -> 30, of which waited for: 12 -> 10; matrix products, arithmetic and copies ran while one was open for 0% -> 0% of each run, Pallas kernels for 25% -> 28%
where the time goes in v19:
time: 116 us
  starting transfers between devices  42.4 us (37%)
  Pallas kernels  35.1 us (30%)
  waiting for transfers between devices  34.3 us (30%)
  local copies, waits for them, and re-layouts  3.37 us (3%)
    ppermute x14, starting transfers between devices, move(): lax.ppermute(value, 'seq', [(i, i ^ k) for i in range(peers)])  31.9 us
    pallas_call x13, Pallas kernels, call(): pl.pallas_call(run, in_specs=specs + [ANYWHERE] * extra, out_specs=jax.tr...  28.7 us
    ppermute x15, waiting for transfers between devices, swap(): return lax.ppermute(value, 'head', [(i, i ^ distance) for i in range(4)])  22.9 us
    ppermute x14, waiting for transfers between devices, move(): lax.ppermute(value, 'seq', [(i, i ^ k) for i in range(peers)])  11.4 us
    ppermute x15, starting transfers between devices, swap(): return lax.ppermute(value, 'head', [(i, i ^ distance) for i in range(4)])  7.22 us
    unnamed x15, local copies, waits for them, and re-layouts  3.31 us
    ppermute x1, starting transfers between devices, chunked(): lax.ppermute(own_halo, 'seq', [(i, i + 1) for i in range(owners - 1)])  3.28 us
    pallas_call x2, Pallas kernels, join(): pl.pallas_call(functools.partial(join_kernel, share), in_specs=[IN_SMEM,...  2.98 us
  transfers between devices with their start and end apart: 30, of which 10 were waited for; matrix products, arithmetic and copies ran while one was open for 0% of the time, Pallas kernels for 28%

profile of v19, /device:TPU:0, one launch (start us, length us, event | category | flops | bytes accessed | tf_op | source)
XLA Modules:
  0.0 115.8 jit_solution(11008571878129291112)
XLA Ops:
  0.0 2.9 %collective-permute-start.8 = (bf16[1024,512]{1,0:T(8,128)(2,1)}, bf16[1024,512]{1,0:T(8,128)(2,1)S(1)}, u32[]{:S(2)}, u32[]{:S(2)}) collective-permute-start(bf16[1024,512]{1,0:T(8,128)(2,1)} %tok_hbm.1), channel_id=1, source_target_pairs={{0,2},{1,3},{2,0},{3,1},{4,6},{5,7},{6,4},{7,5},{8,10},{9,11},{10,... | collective-permute-start | bytes 3145736 | tf_op jit(solution)/shard_map/ppermute | solution.py:427
  3.0 2.1 %pack_tokens.1 = (bf16[1024,512]{1,0:T(8,128)(2,1)S(1)}, bf16[128,512]{1,0:T(8,128)(2,1)S(1)}, bf16[128,512]{1,0:T(8,128)(2,1)S(1)}, bf16[128,512]{1,0:T(8,128)(...) custom-call(s32[3]{0:T(128)S(1)} %pad_add_fusion.pos_ref.refs_0_, ...), custom_call_target="tpu_custom_call" | custom-call | bytes 2097152 | tf_op jit(solution)/shard_map/pack_tokens/pallas_call | solution.py:113
  5.1 2.7 %collective-permute-start.3 = (bf16[128,512]{1,0:T(8,128)(2,1)S(1)}, bf16[128,512]{1,0:T(8,128)(2,1)S(1)}, u32[]{:S(2)}, u32[]{:S(2)}) collective-permute-start(bf16[128,512]{1,0:T(8,128)(2,1)S(1)} %get-tuple-element.45), channel_id=1, source_target_pairs={{0,16},{4,20},{8,24},{12,28},{16,0},{20,4},{24,8},{28,12},{1,17},{... | collective-permute-start | bytes 393224 | tf_op jit(solution)/shard_map/ppermute | solution.py:434
  11.3 2.8 %collective-permute-done.after = bf16[128,512]{1,0:T(8,128)(2,1)S(1)} collective-permute-done((bf16[128,512]{1,0:T(8,128)(2,1)S(1)}, bf16[128,512]{1,0:T(8,128)(2,1)S(1)}, u32[]{:S(2)}, u32[]{:S(2)}) %collective-permute-start) | collective-permute-done | bytes 131104 | tf_op jit(solution)/shard_map/ppermute | solution.py:434
  14.0 3.8 %collective-permute-start.2 = (bf16[128,512]{1,0:T(8,128)(2,1)S(1)}, bf16[128,512]{1,0:T(8,128)(2,1)S(1)}, u32[]{:S(2)}, u32[]{:S(2)}) collective-permute-start(bf16[128,512]{1,0:T(8,128)(2,1)S(1)} %get-tuple-element.44), channel_id=1, source_target_pairs={{0,12},{4,8},{8,4},{12,0},{16,28},{20,24},{24,20},{28,16},{1,13},{... | collective-permute-start | bytes 393224 | tf_op jit(solution)/shard_map/ppermute | solution.py:434
  17.9 7.0 %collective-permute-start.5 = (bf16[128,512]{1,0:T(8,128)(2,1)S(1)}, bf16[128,512]{1,0:T(8,128)(2,1)S(1)}, u32[]{:S(2)}, u32[]{:S(2)}) collective-permute-start(bf16[128,512]{1,0:T(8,128)(2,1)S(1)} %get-tuple-element.47), channel_id=1, source_target_pairs={{0,24},{4,28},{8,16},{12,20},{16,8},{20,12},{24,0},{28,4},{1,25},{... | collective-permute-start | bytes 393224 | tf_op jit(solution)/shard_map/ppermute | solution.py:434
  24.9 3.5 %collective-permute-start.6 = (bf16[128,512]{1,0:T(8,128)(2,1)S(1)}, bf16[128,512]{1,0:T(8,128)(2,1)S(1)}, u32[]{:S(2)}, u32[]{:S(2)}) collective-permute-start(bf16[128,512]{1,0:T(8,128)(2,1)S(1)} %get-tuple-element.48), channel_id=1, source_target_pairs={{0,28},{4,24},{8,20},{12,16},{16,12},{20,8},{24,4},{28,0},{1,29},{... | collective-permute-start | bytes 393224 | tf_op jit(solution)/shard_map/ppermute | solution.py:434
  34.3 7.7 %collective-permute-done.9.refs_1_.refs_2_ = bf16[512,512]{1,0:T(8,128)(2,1)S(1)} collective-permute-done((bf16[512,512]{1,0:T(8,128)(2,1)S(1)}, bf16[512,512]{1,0:T(8,128)(2,1)S(1)}, u32[]{:S(2)}, u32[]{:S(2)}) %collective-permute-start.9) | collective-permute-done | bytes 524320 | tf_op jit(solution)/shard_map/ppermute | solution.py:427
  46.1 3.3 %collective-permute-start.18 = (bf16[512,512]{1,0:T(8,128)(2,1)S(1)}, bf16[512,512]{1,0:T(8,128)(2,1)S(1)}, u32[]{:S(2)}, u32[]{:S(2)}) collective-permute-start(bf16[512,512]{1,0:T(8,128)(2,1)S(1)} %project_halo.1.refs_6_), channel_id=1, source_target_pairs={{0,4},{4,8},{8,12},{12,16},{16,20},{20,24},{24,28},{1,5},{5,9},{9,... | collective-permute-start | bytes 1572872 | tf_op jit(solution)/shard_map/ppermute | solution.py:462
  49.3 2.3 %project_query.1.refs_7_.refs_1_ = bf16[1024,512]{1,0:T(8,128)(2,1)S(1)} custom-call(bf16[1024,512]{1,0:T(8,128)(2,1)S(1)} %get-tuple-element.40.refs_0_, bf16[1024,512]{1,0:T(8,128)(2,1)S(1)} %collective-permute-done.7.refs_1_, bf16[1024,512]{1,0:T(8,128)(2,1)S(1)} %fence.4.refs_2_, bf16[1024,512]{1,0:T(8,128)(2,1)S(1)} %collective-permute-done.10.refs_3_, ...), custom_call_target="tpu_custom_call" | custom-call | tf_op jit(solution)/shard_map/project_query/pallas_call | solution.py:39
  51.7 3.4 %project_near.1 = (bf16[512,512]{1,0:T(8,128)(2,1)S(1)}, bf16[512,512]{1,0:T(8,128)(2,1)S(1)}, bf16[512,512]{1,0:T(8,128)(2,1)S(1)}) custom-call(bf16[512,512]{1,0:T(8,128)(2,1)S(1)} %constant_dynamic-update-slice_fusion.refs_1_.refs_0_, bf16[512,512]{1,0:T(8,128)(2,1)S(1)} %collective-permute-done.12.refs_1_, ...), custom_call_target="tpu_custom_call" | custom-call | tf_op jit(solution)/shard_map/project_near/pallas_call | solution.py:39
  57.5 1.8 %half_sums.1 = (f32[512,512]{1,0:T(8,128)S(1)}, f32[512,512]{1,0:T(8,128)S(1)}, f32[512,512]{1,0:T(8,128)S(1)}) custom-call(bf16[512,512]{1,0:T(8,128)(2,1)S(1)} %constant_dynamic-update-slice_fusion.4.refs_2_.refs_5_.refs_0_, bf16[512,512]{1,0:T(8,128)(2,1)S(1)} %collective-permute-done.16.refs_1_, ...), custom_call_target="tpu_custom_call" | custom-call | tf_op jit(solution)/shard_map/half_sums/pallas_call | solution.py:39
  59.3 4.5 %column_part.1 = (bf16[528,128]{1,0:T(8,128)(2,1)S(1)}, bf16[528,128]{1,0:T(8,128)(2,1)S(1)}, bf16[528,128]{1,0:T(8,128)(2,1)S(1)}, bf16[528,128]{1,0:T(8,128)(2...) custom-call(s32[3]{0:T(128)S(1)} %pad_add_fusion.pos_ref.refs_0_, ...), custom_call_target="tpu_custom_call" | custom-call | tf_op jit(solution)/shard_map/column_part/pallas_call | solution.py:39
  63.8 3.5 %collective-permute-start.22 = (bf16[528,128]{1,0:T(8,128)(2,1)S(1)}, bf16[528,128]{1,0:T(8,128)(2,1)S(1)}, u32[]{:S(2)}, u32[]{:S(2)}) collective-permute-start(bf16[528,128]{1,0:T(8,128)(2,1)S(1)} %get-tuple-element.67), channel_id=1, source_target_pairs={{0,20},{4,16},{8,28},{12,24},{16,4},{20,0},{24,12},{28,8},{1,21},{... | collective-permute-start | bytes 405512 | tf_op jit(solution)/shard_map/ppermute | solution.py:434
  67.3 2.3 %collective-permute-start.24 = (bf16[528,128]{1,0:T(8,128)(2,1)S(1)}, bf16[528,128]{1,0:T(8,128)(2,1)S(1)}, u32[]{:S(2)}, u32[]{:S(2)}) collective-permute-start(bf16[528,128]{1,0:T(8,128)(2,1)S(1)} %get-tuple-element.69), channel_id=1, source_target_pairs={{0,8},{4,12},{8,0},{12,4},{16,24},{20,28},{24,16},{28,20},{1,9},{5... | collective-permute-start | bytes 405512 | tf_op jit(solution)/shard_map/ppermute | solution.py:434
  70.8 3.4 %project_key.1 = (bf16[1024,512]{1,0:T(8,128)(2,1)S(1)}, bf16[1024,512]{1,0:T(8,128)(2,1)S(1)}) custom-call(bf16[1024,512]{1,0:T(8,128)(2,1)S(1)} %get-tuple-element.40.refs_0_, bf16[1024,512]{1,0:T(8,128)(2,1)S(1)} %collective-permute-done.7.refs_1_, bf16[1024,512]{1,0:T(8,128)(2,1)S(1)} %fence.4.refs_2_, ...), custom_call_target="tpu_custom_call" | custom-call | tf_op jit(solution)/shard_map/project_key/pallas_call | solution.py:39
  74.2 3.2 %local_part.1 = (f32[8,128,512]{2,1,0:T(8,128)S(1)}, f32[128,128]{1,0:T(8,128)S(1)}) custom-call(s32[3]{0:T(128)S(1)} %pad_add_fusion.pos_ref.refs_0_, bf16[1024,512]{1,0:T(8,128)(2,1)S(1)} %project_query.1.refs_7_.refs_1_, bf16[1024,512]{1,0:T(8,128)(2,1)S(1)} %get-tuple-element.60.refs_2_, bf16[1024,512]{1,0:T(8,128)(2,1)S(1)} %get-tuple-element.61.refs_3_, ...), custom_call_target="tpu_custom_call" | custom-call | flops 5500000256 | tf_op jit(solution)/shard_map/local_part/pallas_call | solution.py:39
  77.5 2.4 %collective-permute-done.23.refs_5_ = bf16[528,128]{1,0:T(8,128)(2,1)S(1)} collective-permute-done((bf16[528,128]{1,0:T(8,128)(2,1)S(1)}, bf16[528,128]{1,0:T(8,128)(2,1)S(1)}, u32[]{:S(2)}, u32[]{:S(2)}) %collective-permute-start.23) | collective-permute-done | bytes 135200 | tf_op jit(solution)/shard_map/ppermute | solution.py:434
  81.3 1.9 %mix.2 = (bf16[2,192,512]{2,1,0:T(8,128)(2,1)S(1)}, bf16[2,192,512]{2,1,0:T(8,128)(2,1)S(1)}) custom-call(s32[3]{0:T(128)S(1)} %pad_add_fusion.pos_ref.refs_0_, f32[8,128,512]{2,1,0:T(8,128)S(1)} %get-tuple-element.62.refs_1_, f32[128,128]{1,0:T(8,128)S(1)} %get-tuple-element.63.refs_2_, bf16[528,128]{1,0:T(8,128)(2,1)S(1)} %collective-permute-done.21.refs_3_, ...), custom_call_target="tpu_custom_call" | custom-call | flops 2200000000 | tf_op jit(solution)/shard_map/mix/pallas_call | solution.py:39
  83.3 4.4 %collective-permute-start.20 = (bf16[528,128]{1,0:T(8,128)(2,1)S(1)}, bf16[528,128]{1,0:T(8,128)(2,1)S(1)}, u32[]{:S(2)}, u32[]{:S(2)}) collective-permute-start(bf16[528,128]{1,0:T(8,128)(2,1)S(1)} %get-tuple-element.65), channel_id=1, source_target_pairs={{0,28},{4,24},{8,20},{12,16},{16,12},{20,8},{24,4},{28,0},{1,29},{... | collective-permute-start | bytes 405512 | tf_op jit(solution)/shard_map/ppermute | solution.py:434
  89.8 1.8 %collective-permute-done.19.refs_3_ = bf16[528,128]{1,0:T(8,128)(2,1)S(1)} collective-permute-done((bf16[528,128]{1,0:T(8,128)(2,1)S(1)}, bf16[528,128]{1,0:T(8,128)(2,1)S(1)}, u32[]{:S(2)}, u32[]{:S(2)}) %collective-permute-start.19) | collective-permute-done | bytes 135200 | tf_op jit(solution)/shard_map/ppermute | solution.py:434
  91.6 3.0 %collective-permute-done.20.refs_4_ = bf16[528,128]{1,0:T(8,128)(2,1)S(1)} collective-permute-done((bf16[528,128]{1,0:T(8,128)(2,1)S(1)}, bf16[528,128]{1,0:T(8,128)(2,1)S(1)}, u32[]{:S(2)}, u32[]{:S(2)}) %collective-permute-start.20) | collective-permute-done | bytes 135200 | tf_op jit(solution)/shard_map/ppermute | solution.py:434
  100.7 9.1 %collective-permute-done.29.got = bf16[192,2048]{1,0:T(8,128)(2,1)S(1)} collective-permute-done((bf16[192,2048]{1,0:T(8,128)(2,1)S(1)}, bf16[192,2048]{1,0:T(8,128)(2,1)S(1)}, u32[]{:S(2)}, u32[]{:S(2)}) %collective-permute-start.29) | collective-permute-done | bytes 786464 | tf_op jit(solution)/shard_map/ppermute | solution.py:427
  111.5 2.8 %collective-permute-done.28.got = bf16[64,2048]{1,0:T(8,128)(2,1)S(1)} collective-permute-done((bf16[64,2048]{1,0:T(8,128)(2,1)S(1)}, bf16[64,2048]{1,0:T(8,128)(2,1)S(1)}, u32[]{:S(2)}, u32[]{:S(2)}) %collective-permute-start.28) | collective-permute-done | bytes 262176 | tf_op jit(solution)/shard_map/ppermute | solution.py:427
  (76 shorter events, 29.6 us)
Async XLA Ops:
  0.0 42.0 %collective-permute-start.8 = (bf16[1024,512]{1,0:T(8,128)(2,1)}, bf16[1024,512]{1,0:T(8,128)(2,1)S(1)}, u32[]{:S(2)}, u32[]{:S(2)}) collective-permute-start(bf16[1024,512]{1,0:T(8,128)(2,1)} %tok_hbm.1), channel_id=1, source_target_pairs={{0,2},{1,3},{2,0},{3,1},{4,6},{5,7},{6,4},{7,5},{8,10},{9,11},{10,... | collective-permute-start | bytes 3145736 | tf_op jit(solution)/shard_map/ppermute | solution.py:427
  5.1 23.3 %collective-permute-start.3 = (bf16[128,512]{1,0:T(8,128)(2,1)S(1)}, bf16[128,512]{1,0:T(8,128)(2,1)S(1)}, u32[]{:S(2)}, u32[]{:S(2)}) collective-permute-start(bf16[128,512]{1,0:T(8,128)(2,1)S(1)} %get-tuple-element.45), channel_id=1, source_target_pairs={{0,16},{4,20},{8,24},{12,28},{16,0},{20,4},{24,8},{28,12},{1,17},{... | collective-permute-start | bytes 393224 | tf_op jit(solution)/shard_map/ppermute | solution.py:434
  7.8 25.8 %collective-permute-start.4 = (bf16[128,512]{1,0:T(8,128)(2,1)S(1)}, bf16[128,512]{1,0:T(8,128)(2,1)S(1)}, u32[]{:S(2)}, u32[]{:S(2)}) collective-permute-start(bf16[128,512]{1,0:T(8,128)(2,1)S(1)} %get-tuple-element.46), channel_id=1, source_target_pairs={{0,20},{4,16},{8,28},{12,24},{16,4},{20,0},{24,12},{28,8},{1,21},{... | collective-permute-start | bytes 393224 | tf_op jit(solution)/shard_map/ppermute | solution.py:434
  9.1 5.0 %collective-permute-start = (bf16[128,512]{1,0:T(8,128)(2,1)S(1)}, bf16[128,512]{1,0:T(8,128)(2,1)S(1)}, u32[]{:S(2)}, u32[]{:S(2)}) collective-permute-start(bf16[128,512]{1,0:T(8,128)(2,1)S(1)} %get-tuple-element.42), channel_id=1, source_target_pairs={{0,4},{4,0},{8,12},{12,8},{16,20},{20,16},{24,28},{28,24},{1,5},{5... | collective-permute-start | bytes 393224 | tf_op jit(solution)/shard_map/ppermute | solution.py:434
  9.6 8.3 %collective-permute-start.1 = (bf16[128,512]{1,0:T(8,128)(2,1)S(1)}, bf16[128,512]{1,0:T(8,128)(2,1)S(1)}, u32[]{:S(2)}, u32[]{:S(2)}) collective-permute-start(bf16[128,512]{1,0:T(8,128)(2,1)S(1)} %get-tuple-element.43), channel_id=1, source_target_pairs={{0,8},{4,12},{8,0},{12,4},{16,24},{20,28},{24,16},{28,20},{1,9},{5... | collective-permute-start | bytes 393224 | tf_op jit(solution)/shard_map/ppermute | solution.py:434
  14.0 10.9 %collective-permute-start.2 = (bf16[128,512]{1,0:T(8,128)(2,1)S(1)}, bf16[128,512]{1,0:T(8,128)(2,1)S(1)}, u32[]{:S(2)}, u32[]{:S(2)}) collective-permute-start(bf16[128,512]{1,0:T(8,128)(2,1)S(1)} %get-tuple-element.44), channel_id=1, source_target_pairs={{0,12},{4,8},{8,4},{12,0},{16,28},{20,24},{24,20},{28,16},{1,13},{... | collective-permute-start | bytes 393224 | tf_op jit(solution)/shard_map/ppermute | solution.py:434
  17.9 15.8 %collective-permute-start.5 = (bf16[128,512]{1,0:T(8,128)(2,1)S(1)}, bf16[128,512]{1,0:T(8,128)(2,1)S(1)}, u32[]{:S(2)}, u32[]{:S(2)}) collective-permute-start(bf16[128,512]{1,0:T(8,128)(2,1)S(1)} %get-tuple-element.47), channel_id=1, source_target_pairs={{0,24},{4,28},{8,16},{12,20},{16,8},{20,12},{24,0},{28,4},{1,25},{... | collective-permute-start | bytes 393224 | tf_op jit(solution)/shard_map/ppermute | solution.py:434
  24.9 8.8 %collective-permute-start.6 = (bf16[128,512]{1,0:T(8,128)(2,1)S(1)}, bf16[128,512]{1,0:T(8,128)(2,1)S(1)}, u32[]{:S(2)}, u32[]{:S(2)}) collective-permute-start(bf16[128,512]{1,0:T(8,128)(2,1)S(1)} %get-tuple-element.48), channel_id=1, source_target_pairs={{0,28},{4,24},{8,20},{12,16},{16,12},{20,8},{24,4},{28,0},{1,29},{... | collective-permute-start | bytes 393224 | tf_op jit(solution)/shard_map/ppermute | solution.py:434
  28.4 13.5 %collective-permute-start.9 = (bf16[512,512]{1,0:T(8,128)(2,1)S(1)}, bf16[512,512]{1,0:T(8,128)(2,1)S(1)}, u32[]{:S(2)}, u32[]{:S(2)}) collective-permute-start(bf16[512,512]{1,0:T(8,128)(2,1)S(1)} %constant_dynamic-update-slice_fusion.refs_1_.refs_0_), channel_id=1, source_target_pairs={{0,2},{1,3},{2,0},{3,1},{4,6},{5,7},{6,4},{7,5},{8,10},{9,11},{10,... | collective-permute-start | bytes 1572872 | tf_op jit(solution)/shard_map/ppermute | solution.py:427
  33.6 25.7 %collective-permute-start.17 = (bf16[512,2048]{1,0:T(8,128)(2,1)S(1)}, bf16[512,2048]{1,0:T(8,128)(2,1)S(1)}, u32[]{:S(2)}, u32[]{:S(2)}) collective-permute-start(bf16[512,2048]{1,0:T(8,128)(2,1)S(1)} %get-tuple-element.58.refs_3_), channel_id=1, source_target_pairs={{0,1},{1,0},{2,3},{3,2},{4,5},{5,4},{6,7},{7,6},{8,9},{9,8},{10,11... | collective-permute-start | bytes 6291464 | tf_op jit(solution)/shard_map/ppermute | solution.py:427
  33.7 8.8 %collective-permute-start.7 = (bf16[1024,512]{1,0:T(8,128)(2,1)S(1)}, bf16[1024,512]{1,0:T(8,128)(2,1)S(1)}, u32[]{:S(2)}, u32[]{:S(2)}) collective-permute-start(bf16[1024,512]{1,0:T(8,128)(2,1)S(1)} %fence.3), channel_id=1, source_target_pairs={{0,1},{1,0},{2,3},{3,2},{4,5},{5,4},{6,7},{7,6},{8,9},{9,8},{10,11... | collective-permute-start | bytes 3145736 | tf_op jit(solution)/shard_map/ppermute | solution.py:427
  42.5 9.2 %collective-permute-start.13 = (bf16[512,512]{1,0:T(8,128)(2,1)S(1)}, bf16[512,512]{1,0:T(8,128)(2,1)S(1)}, u32[]{:S(2)}, u32[]{:S(2)}) collective-permute-start(bf16[512,512]{1,0:T(8,128)(2,1)S(1)} %collective-permute-done.9.refs_1_.refs_2_), channel_id=1, source_target_pairs={{0,1},{1,0},{2,3},{3,2},{4,5},{5,4},{6,7},{7,6},{8,9},{9,8},{10,11... | collective-permute-start | bytes 1572872 | tf_op jit(solution)/shard_map/ppermute | solution.py:427
  42.6 14.3 %collective-permute-start.11 = (bf16[512,512]{1,0:T(8,128)(2,1)S(1)}, bf16[512,512]{1,0:T(8,128)(2,1)S(1)}, u32[]{:S(2)}, u32[]{:S(2)}) collective-permute-start(bf16[512,512]{1,0:T(8,128)(2,1)S(1)} %constant_dynamic-update-slice_fusion.4.refs_2_.refs_5_.refs_0_), channel_id=1, source_target_pairs={{0,2},{1,3},{2,0},{3,1},{4,6},{5,7},{6,4},{7,5},{8,10},{9,11},{10,... | collective-permute-start | bytes 1572872 | tf_op jit(solution)/shard_map/ppermute | solution.py:427
  44.7 12.8 %collective-permute-start.16 = (bf16[512,512]{1,0:T(8,128)(2,1)S(1)}, bf16[512,512]{1,0:T(8,128)(2,1)S(1)}, u32[]{:S(2)}, u32[]{:S(2)}) collective-permute-start(bf16[512,512]{1,0:T(8,128)(2,1)S(1)} %constant_dynamic-update-slice_fusion.4.refs_2_.refs_5_.refs_0_), channel_id=1, source_target_pairs={{0,1},{1,0},{2,3},{3,2},{4,5},{5,4},{6,7},{7,6},{8,9},{9,8},{10,11... | collective-permute-start | bytes 1572872 | tf_op jit(solution)/shard_map/ppermute | solution.py:427
  46.1 23.6 %collective-permute-start.18 = (bf16[512,512]{1,0:T(8,128)(2,1)S(1)}, bf16[512,512]{1,0:T(8,128)(2,1)S(1)}, u32[]{:S(2)}, u32[]{:S(2)}) collective-permute-start(bf16[512,512]{1,0:T(8,128)(2,1)S(1)} %project_halo.1.refs_6_), channel_id=1, source_target_pairs={{0,4},{4,8},{8,12},{12,16},{16,20},{20,24},{24,28},{1,5},{5,9},{9,... | collective-permute-start | bytes 1572872 | tf_op jit(solution)/shard_map/ppermute | solution.py:462
  63.8 13.7 %collective-permute-start.21 = (bf16[528,128]{1,0:T(8,128)(2,1)S(1)}, bf16[528,128]{1,0:T(8,128)(2,1)S(1)}, u32[]{:S(2)}, u32[]{:S(2)}) collective-permute-start(bf16[528,128]{1,0:T(8,128)(2,1)S(1)} %get-tuple-element.66), channel_id=1, source_target_pairs={{0,16},{4,20},{8,24},{12,28},{16,0},{20,4},{24,8},{28,12},{1,17},{... | collective-permute-start | bytes 405512 | tf_op jit(solution)/shard_map/ppermute | solution.py:434
  63.8 13.7 %collective-permute-start.22 = (bf16[528,128]{1,0:T(8,128)(2,1)S(1)}, bf16[528,128]{1,0:T(8,128)(2,1)S(1)}, u32[]{:S(2)}, u32[]{:S(2)}) collective-permute-start(bf16[528,128]{1,0:T(8,128)(2,1)S(1)} %get-tuple-element.67), channel_id=1, source_target_pairs={{0,20},{4,16},{8,28},{12,24},{16,4},{20,0},{24,12},{28,8},{1,21},{... | collective-permute-start | bytes 405512 | tf_op jit(solution)/shard_map/ppermute | solution.py:434
  67.3 12.6 %collective-permute-start.23 = (bf16[528,128]{1,0:T(8,128)(2,1)S(1)}, bf16[528,128]{1,0:T(8,128)(2,1)S(1)}, u32[]{:S(2)}, u32[]{:S(2)}) collective-permute-start(bf16[528,128]{1,0:T(8,128)(2,1)S(1)} %get-tuple-element.68), channel_id=1, source_target_pairs={{0,12},{4,8},{8,4},{12,0},{16,28},{20,24},{24,20},{28,16},{1,13},{... | collective-permute-start | bytes 405512 | tf_op jit(solution)/shard_map/ppermute | solution.py:434
  67.3 14.0 %collective-permute-start.24 = (bf16[528,128]{1,0:T(8,128)(2,1)S(1)}, bf16[528,128]{1,0:T(8,128)(2,1)S(1)}, u32[]{:S(2)}, u32[]{:S(2)}) collective-permute-start(bf16[528,128]{1,0:T(8,128)(2,1)S(1)} %get-tuple-element.69), channel_id=1, source_target_pairs={{0,8},{4,12},{8,0},{12,4},{16,24},{20,28},{24,16},{28,20},{1,9},{5... | collective-permute-start | bytes 405512 | tf_op jit(solution)/shard_map/ppermute | solution.py:434
  69.7 11.6 %collective-permute-start.25 = (bf16[528,128]{1,0:T(8,128)(2,1)S(1)}, bf16[528,128]{1,0:T(8,128)(2,1)S(1)}, u32[]{:S(2)}, u32[]{:S(2)}) collective-permute-start(bf16[528,128]{1,0:T(8,128)(2,1)S(1)} %get-tuple-element.70), channel_id=1, source_target_pairs={{0,4},{4,0},{8,12},{12,8},{16,20},{20,16},{24,28},{28,24},{1,5},{5... | collective-permute-start | bytes 405512 | tf_op jit(solution)/shard_map/ppermute | solution.py:434
  83.3 8.3 %collective-permute-start.19 = (bf16[528,128]{1,0:T(8,128)(2,1)S(1)}, bf16[528,128]{1,0:T(8,128)(2,1)S(1)}, u32[]{:S(2)}, u32[]{:S(2)}) collective-permute-start(bf16[528,128]{1,0:T(8,128)(2,1)S(1)} %get-tuple-element.64), channel_id=1, source_target_pairs={{0,24},{4,28},{8,16},{12,20},{16,8},{20,12},{24,0},{28,4},{1,25},{... | collective-permute-start | bytes 405512 | tf_op jit(solution)/shard_map/ppermute | solution.py:434
  83.3 11.3 %collective-permute-start.20 = (bf16[528,128]{1,0:T(8,128)(2,1)S(1)}, bf16[528,128]{1,0:T(8,128)(2,1)S(1)}, u32[]{:S(2)}, u32[]{:S(2)}) collective-permute-start(bf16[528,128]{1,0:T(8,128)(2,1)S(1)} %get-tuple-element.65), channel_id=1, source_target_pairs={{0,28},{4,24},{8,20},{12,16},{16,12},{20,8},{24,4},{28,0},{1,29},{... | collective-permute-start | bytes 405512 | tf_op jit(solution)/shard_map/ppermute | solution.py:434
  89.3 20.5 %collective-permute-start.29 = (bf16[192,2048]{1,0:T(8,128)(2,1)S(1)}, bf16[192,2048]{1,0:T(8,128)(2,1)S(1)}, u32[]{:S(2)}, u32[]{:S(2)}) collective-permute-start(bf16[192,2048]{1,0:T(8,128)(2,1)S(1)} %out_project.4.refs_5_), channel_id=1, source_target_pairs={{0,2},{1,3},{2,0},{3,1},{4,6},{5,7},{6,4},{7,5},{8,10},{9,11},{10,... | collective-permute-start | bytes 2359304 | tf_op jit(solution)/shard_map/ppermute | solution.py:427
  98.8 15.6 %collective-permute-start.28 = (bf16[64,2048]{1,0:T(8,128)(2,1)S(1)}, bf16[64,2048]{1,0:T(8,128)(2,1)S(1)}, u32[]{:S(2)}, u32[]{:S(2)}) collective-permute-start(bf16[64,2048]{1,0:T(8,128)(2,1)S(1)} %out_project.6), channel_id=1, source_target_pairs={{0,2},{1,3},{2,0},{3,1},{4,6},{5,7},{6,4},{7,5},{8,10},{9,11},{10,... | collective-permute-start | bytes 786440 | tf_op jit(solution)/shard_map/ppermute | solution.py:427
  (10 other events, 72.9 us)

commit v20 on v19

--- a/solution.py
+++ b/solution.py
@@ -15,7 +15,7 @@
 CHUNKS = ((0, 1, 2, 3),)
 NEAR = 4
 PEERS = 8
-SHARES = ((4, 5, 3, 2, 1, 0), (6, 7))
+SHARES = ((1, 4, 5, 3, 2, 0), (6, 7))
 SCALE2 = DH ** (-0.5) * 1.4426950408889634
 FLOOR = -1e29
 MIB = 1024 * 1024

time: 116 us -> 117 us (level)
  waiting for transfers between devices: 34.3 us -> 35.6 us
  transfers between devices with their start and end apart: 30 -> 30, of which waited for: 10 -> 11; matrix products, arithmetic and copies ran while one was open for 0% -> 0% of each run, Pallas kernels for 28% -> 27%
where the time goes in v20:
time: 117 us; the launch traced here: 116 us
  starting transfers between devices  41.7 us (36%)
  waiting for transfers between devices  35.6 us (30%)
  Pallas kernels  35 us (30%)
  local copies, waits for them, and re-layouts  3.37 us (3%)
    ppermute x14, starting transfers between devices, move(): lax.ppermute(value, 'seq', [(i, i ^ k) for i in range(peers)])  31.6 us
    pallas_call x13, Pallas kernels, call(): pl.pallas_call(run, in_specs=specs + [ANYWHERE] * extra, out_specs=jax.tr...  28.6 us
    ppermute x15, waiting for transfers between devices, swap(): return lax.ppermute(value, 'head', [(i, i ^ distance) for i in range(4)])  23.2 us
    ppermute x14, waiting for transfers between devices, move(): lax.ppermute(value, 'seq', [(i, i ^ k) for i in range(peers)])  12.4 us
    ppermute x15, starting transfers between devices, swap(): return lax.ppermute(value, 'head', [(i, i ^ distance) for i in range(4)])  6.78 us
    unnamed x15, local copies, waits for them, and re-layouts  3.31 us
    ppermute x1, starting transfers between devices, chunked(): lax.ppermute(own_halo, 'seq', [(i, i + 1) for i in range(owners - 1)])  3.28 us
    pallas_call x2, Pallas kernels, join(): pl.pallas_call(functools.partial(join_kernel, share), in_specs=[IN_SMEM,...  2.98 us
  transfers between devices with their start and end apart: 30, of which 11 were waited for; matrix products, arithmetic and copies ran while one was open for 0% of the time, Pallas kernels for 27%

profile of v20, /device:TPU:0, one launch (start us, length us, event | category | flops | bytes accessed | tf_op | source)
XLA Modules:
  0.0 116.3 jit_solution(7255915690872641701)
XLA Ops:
  0.0 2.9 %collective-permute-start.8 = (bf16[1024,512]{1,0:T(8,128)(2,1)}, bf16[1024,512]{1,0:T(8,128)(2,1)S(1)}, u32[]{:S(2)}, u32[]{:S(2)}) collective-permute-start(bf16[1024,512]{1,0:T(8,128)(2,1)} %tok_hbm.1), channel_id=1, source_target_pairs={{0,2},{1,3},{2,0},{3,1},{4,6},{5,7},{6,4},{7,5},{8,10},{9,11},{10,... | collective-permute-start | bytes 3145736 | tf_op jit(solution)/shard_map/ppermute | solution.py:427
  3.0 2.1 %pack_tokens.1 = (bf16[1024,512]{1,0:T(8,128)(2,1)S(1)}, bf16[128,512]{1,0:T(8,128)(2,1)S(1)}, bf16[128,512]{1,0:T(8,128)(2,1)S(1)}, bf16[128,512]{1,0:T(8,128)(...) custom-call(s32[3]{0:T(128)S(1)} %pad_add_fusion.pos_ref.refs_0_, ...), custom_call_target="tpu_custom_call" | custom-call | bytes 2097152 | tf_op jit(solution)/shard_map/pack_tokens/pallas_call | solution.py:113
  5.1 2.7 %collective-permute-start.3 = (bf16[128,512]{1,0:T(8,128)(2,1)S(1)}, bf16[128,512]{1,0:T(8,128)(2,1)S(1)}, u32[]{:S(2)}, u32[]{:S(2)}) collective-permute-start(bf16[128,512]{1,0:T(8,128)(2,1)S(1)} %get-tuple-element.45), channel_id=1, source_target_pairs={{0,16},{4,20},{8,24},{12,28},{16,0},{20,4},{24,8},{28,12},{1,17},{... | collective-permute-start | bytes 393224 | tf_op jit(solution)/shard_map/ppermute | solution.py:434
  11.3 2.8 %collective-permute-done.after = bf16[128,512]{1,0:T(8,128)(2,1)S(1)} collective-permute-done((bf16[128,512]{1,0:T(8,128)(2,1)S(1)}, bf16[128,512]{1,0:T(8,128)(2,1)S(1)}, u32[]{:S(2)}, u32[]{:S(2)}) %collective-permute-start) | collective-permute-done | bytes 131104 | tf_op jit(solution)/shard_map/ppermute | solution.py:434
  14.0 3.8 %collective-permute-start.2 = (bf16[128,512]{1,0:T(8,128)(2,1)S(1)}, bf16[128,512]{1,0:T(8,128)(2,1)S(1)}, u32[]{:S(2)}, u32[]{:S(2)}) collective-permute-start(bf16[128,512]{1,0:T(8,128)(2,1)S(1)} %get-tuple-element.44), channel_id=1, source_target_pairs={{0,12},{4,8},{8,4},{12,0},{16,28},{20,24},{24,20},{28,16},{1,13},{... | collective-permute-start | bytes 393224 | tf_op jit(solution)/shard_map/ppermute | solution.py:434
  17.9 7.0 %collective-permute-start.5 = (bf16[128,512]{1,0:T(8,128)(2,1)S(1)}, bf16[128,512]{1,0:T(8,128)(2,1)S(1)}, u32[]{:S(2)}, u32[]{:S(2)}) collective-permute-start(bf16[128,512]{1,0:T(8,128)(2,1)S(1)} %get-tuple-element.47), channel_id=1, source_target_pairs={{0,24},{4,28},{8,16},{12,20},{16,8},{20,12},{24,0},{28,4},{1,25},{... | collective-permute-start | bytes 393224 | tf_op jit(solution)/shard_map/ppermute | solution.py:434
  24.9 3.5 %collective-permute-start.6 = (bf16[128,512]{1,0:T(8,128)(2,1)S(1)}, bf16[128,512]{1,0:T(8,128)(2,1)S(1)}, u32[]{:S(2)}, u32[]{:S(2)}) collective-permute-start(bf16[128,512]{1,0:T(8,128)(2,1)S(1)} %get-tuple-element.48), channel_id=1, source_target_pairs={{0,28},{4,24},{8,20},{12,16},{16,12},{20,8},{24,4},{28,0},{1,29},{... | collective-permute-start | bytes 393224 | tf_op jit(solution)/shard_map/ppermute | solution.py:434
  34.3 7.7 %collective-permute-done.9.refs_1_.refs_2_ = bf16[512,512]{1,0:T(8,128)(2,1)S(1)} collective-permute-done((bf16[512,512]{1,0:T(8,128)(2,1)S(1)}, bf16[512,512]{1,0:T(8,128)(2,1)S(1)}, u32[]{:S(2)}, u32[]{:S(2)}) %collective-permute-start.9) | collective-permute-done | bytes 524320 | tf_op jit(solution)/shard_map/ppermute | solution.py:427
  46.1 3.3 %collective-permute-start.18 = (bf16[512,512]{1,0:T(8,128)(2,1)S(1)}, bf16[512,512]{1,0:T(8,128)(2,1)S(1)}, u32[]{:S(2)}, u32[]{:S(2)}) collective-permute-start(bf16[512,512]{1,0:T(8,128)(2,1)S(1)} %project_halo.1.refs_6_), channel_id=1, source_target_pairs={{0,4},{4,8},{8,12},{12,16},{16,20},{20,24},{24,28},{1,5},{5,9},{9,... | collective-permute-start | bytes 1572872 | tf_op jit(solution)/shard_map/ppermute | solution.py:462
  49.3 2.3 %project_query.1.refs_7_.refs_1_ = bf16[1024,512]{1,0:T(8,128)(2,1)S(1)} custom-call(bf16[1024,512]{1,0:T(8,128)(2,1)S(1)} %get-tuple-element.40.refs_0_, bf16[1024,512]{1,0:T(8,128)(2,1)S(1)} %collective-permute-done.7.refs_1_, bf16[1024,512]{1,0:T(8,128)(2,1)S(1)} %fence.4.refs_2_, bf16[1024,512]{1,0:T(8,128)(2,1)S(1)} %collective-permute-done.10.refs_3_, ...), custom_call_target="tpu_custom_call" | custom-call | tf_op jit(solution)/shard_map/project_query/pallas_call | solution.py:39
  51.7 3.4 %project_near.1 = (bf16[512,512]{1,0:T(8,128)(2,1)S(1)}, bf16[512,512]{1,0:T(8,128)(2,1)S(1)}, bf16[512,512]{1,0:T(8,128)(2,1)S(1)}) custom-call(bf16[512,512]{1,0:T(8,128)(2,1)S(1)} %constant_dynamic-update-slice_fusion.refs_1_.refs_0_, bf16[512,512]{1,0:T(8,128)(2,1)S(1)} %collective-permute-done.12.refs_1_, ...), custom_call_target="tpu_custom_call" | custom-call | tf_op jit(solution)/shard_map/project_near/pallas_call | solution.py:39
  57.5 1.8 %half_sums.1 = (f32[512,512]{1,0:T(8,128)S(1)}, f32[512,512]{1,0:T(8,128)S(1)}, f32[512,512]{1,0:T(8,128)S(1)}) custom-call(bf16[512,512]{1,0:T(8,128)(2,1)S(1)} %constant_dynamic-update-slice_fusion.4.refs_2_.refs_5_.refs_0_, bf16[512,512]{1,0:T(8,128)(2,1)S(1)} %collective-permute-done.16.refs_1_, ...), custom_call_target="tpu_custom_call" | custom-call | tf_op jit(solution)/shard_map/half_sums/pallas_call | solution.py:39
  59.3 4.5 %column_part.1 = (bf16[528,128]{1,0:T(8,128)(2,1)S(1)}, bf16[528,128]{1,0:T(8,128)(2,1)S(1)}, bf16[528,128]{1,0:T(8,128)(2,1)S(1)}, bf16[528,128]{1,0:T(8,128)(2...) custom-call(s32[3]{0:T(128)S(1)} %pad_add_fusion.pos_ref.refs_0_, ...), custom_call_target="tpu_custom_call" | custom-call | tf_op jit(solution)/shard_map/column_part/pallas_call | solution.py:39
  65.0 3.2 %collective-permute-start.23 = (bf16[528,128]{1,0:T(8,128)(2,1)S(1)}, bf16[528,128]{1,0:T(8,128)(2,1)S(1)}, u32[]{:S(2)}, u32[]{:S(2)}) collective-permute-start(bf16[528,128]{1,0:T(8,128)(2,1)S(1)} %get-tuple-element.68), channel_id=1, source_target_pairs={{0,20},{4,16},{8,28},{12,24},{16,4},{20,0},{24,12},{28,8},{1,21},{... | collective-permute-start | bytes 405512 | tf_op jit(solution)/shard_map/ppermute | solution.py:434
  68.2 2.6 %collective-permute-start.25 = (bf16[528,128]{1,0:T(8,128)(2,1)S(1)}, bf16[528,128]{1,0:T(8,128)(2,1)S(1)}, u32[]{:S(2)}, u32[]{:S(2)}) collective-permute-start(bf16[528,128]{1,0:T(8,128)(2,1)S(1)} %get-tuple-element.70), channel_id=1, source_target_pairs={{0,8},{4,12},{8,0},{12,4},{16,24},{20,28},{24,16},{28,20},{1,9},{5... | collective-permute-start | bytes 405512 | tf_op jit(solution)/shard_map/ppermute | solution.py:434
  70.8 3.4 %project_key.1 = (bf16[1024,512]{1,0:T(8,128)(2,1)S(1)}, bf16[1024,512]{1,0:T(8,128)(2,1)S(1)}) custom-call(bf16[1024,512]{1,0:T(8,128)(2,1)S(1)} %get-tuple-element.40.refs_0_, bf16[1024,512]{1,0:T(8,128)(2,1)S(1)} %collective-permute-done.7.refs_1_, bf16[1024,512]{1,0:T(8,128)(2,1)S(1)} %fence.4.refs_2_, ...), custom_call_target="tpu_custom_call" | custom-call | tf_op jit(solution)/shard_map/project_key/pallas_call | solution.py:39
  74.2 3.2 %local_part.1 = (f32[8,128,512]{2,1,0:T(8,128)S(1)}, f32[128,128]{1,0:T(8,128)S(1)}) custom-call(s32[3]{0:T(128)S(1)} %pad_add_fusion.pos_ref.refs_0_, bf16[1024,512]{1,0:T(8,128)(2,1)S(1)} %project_query.1.refs_7_.refs_1_, bf16[1024,512]{1,0:T(8,128)(2,1)S(1)} %get-tuple-element.60.refs_2_, bf16[1024,512]{1,0:T(8,128)(2,1)S(1)} %get-tuple-element.61.refs_3_, ...), custom_call_target="tpu_custom_call" | custom-call | flops 5500000256 | tf_op jit(solution)/shard_map/local_part/pallas_call | solution.py:39
  78.0 2.6 %collective-permute-done.24.refs_6_ = bf16[528,128]{1,0:T(8,128)(2,1)S(1)} collective-permute-done((bf16[528,128]{1,0:T(8,128)(2,1)S(1)}, bf16[528,128]{1,0:T(8,128)(2,1)S(1)}, u32[]{:S(2)}, u32[]{:S(2)}) %collective-permute-start.24) | collective-permute-done | bytes 135200 | tf_op jit(solution)/shard_map/ppermute | solution.py:434
  82.1 1.9 %mix.2 = (bf16[2,192,512]{2,1,0:T(8,128)(2,1)S(1)}, bf16[2,192,512]{2,1,0:T(8,128)(2,1)S(1)}) custom-call(s32[3]{0:T(128)S(1)} %pad_add_fusion.pos_ref.refs_0_, f32[8,128,512]{2,1,0:T(8,128)S(1)} %get-tuple-element.62.refs_1_, f32[128,128]{1,0:T(8,128)S(1)} %get-tuple-element.63.refs_2_, bf16[528,128]{1,0:T(8,128)(2,1)S(1)} %collective-permute-done.21.refs_3_, ...), custom_call_target="tpu_custom_call" | custom-call | flops 2200000000 | tf_op jit(solution)/shard_map/mix/pallas_call | solution.py:39
  84.1 4.1 %collective-permute-start.20 = (bf16[528,128]{1,0:T(8,128)(2,1)S(1)}, bf16[528,128]{1,0:T(8,128)(2,1)S(1)}, u32[]{:S(2)}, u32[]{:S(2)}) collective-permute-start(bf16[528,128]{1,0:T(8,128)(2,1)S(1)} %get-tuple-element.65), channel_id=1, source_target_pairs={{0,28},{4,24},{8,20},{12,16},{16,12},{20,8},{24,4},{28,0},{1,29},{... | collective-permute-start | bytes 405512 | tf_op jit(solution)/shard_map/ppermute | solution.py:434
  90.1 2.3 %collective-permute-done.19.refs_3_ = bf16[528,128]{1,0:T(8,128)(2,1)S(1)} collective-permute-done((bf16[528,128]{1,0:T(8,128)(2,1)S(1)}, bf16[528,128]{1,0:T(8,128)(2,1)S(1)}, u32[]{:S(2)}, u32[]{:S(2)}) %collective-permute-start.19) | collective-permute-done | bytes 135200 | tf_op jit(solution)/shard_map/ppermute | solution.py:434
  92.4 2.8 %collective-permute-done.20.refs_4_ = bf16[528,128]{1,0:T(8,128)(2,1)S(1)} collective-permute-done((bf16[528,128]{1,0:T(8,128)(2,1)S(1)}, bf16[528,128]{1,0:T(8,128)(2,1)S(1)}, u32[]{:S(2)}, u32[]{:S(2)}) %collective-permute-start.20) | collective-permute-done | bytes 135200 | tf_op jit(solution)/shard_map/ppermute | solution.py:434
  101.0 9.3 %collective-permute-done.29.got = bf16[192,2048]{1,0:T(8,128)(2,1)S(1)} collective-permute-done((bf16[192,2048]{1,0:T(8,128)(2,1)S(1)}, bf16[192,2048]{1,0:T(8,128)(2,1)S(1)}, u32[]{:S(2)}, u32[]{:S(2)}) %collective-permute-start.29) | collective-permute-done | bytes 786464 | tf_op jit(solution)/shard_map/ppermute | solution.py:427
  112.0 2.8 %collective-permute-done.28.got = bf16[64,2048]{1,0:T(8,128)(2,1)S(1)} collective-permute-done((bf16[64,2048]{1,0:T(8,128)(2,1)S(1)}, bf16[64,2048]{1,0:T(8,128)(2,1)S(1)}, u32[]{:S(2)}, u32[]{:S(2)}) %collective-permute-start.28) | collective-permute-done | bytes 262176 | tf_op jit(solution)/shard_map/ppermute | solution.py:427
  (76 shorter events, 29.7 us)
Async XLA Ops:
  0.0 42.0 %collective-permute-start.8 = (bf16[1024,512]{1,0:T(8,128)(2,1)}, bf16[1024,512]{1,0:T(8,128)(2,1)S(1)}, u32[]{:S(2)}, u32[]{:S(2)}) collective-permute-start(bf16[1024,512]{1,0:T(8,128)(2,1)} %tok_hbm.1), channel_id=1, source_target_pairs={{0,2},{1,3},{2,0},{3,1},{4,6},{5,7},{6,4},{7,5},{8,10},{9,11},{10,... | collective-permute-start | bytes 3145736 | tf_op jit(solution)/shard_map/ppermute | solution.py:427
  5.1 23.3 %collective-permute-start.3 = (bf16[128,512]{1,0:T(8,128)(2,1)S(1)}, bf16[128,512]{1,0:T(8,128)(2,1)S(1)}, u32[]{:S(2)}, u32[]{:S(2)}) collective-permute-start(bf16[128,512]{1,0:T(8,128)(2,1)S(1)} %get-tuple-element.45), channel_id=1, source_target_pairs={{0,16},{4,20},{8,24},{12,28},{16,0},{20,4},{24,8},{28,12},{1,17},{... | collective-permute-start | bytes 393224 | tf_op jit(solution)/shard_map/ppermute | solution.py:434
  7.8 25.8 %collective-permute-start.4 = (bf16[128,512]{1,0:T(8,128)(2,1)S(1)}, bf16[128,512]{1,0:T(8,128)(2,1)S(1)}, u32[]{:S(2)}, u32[]{:S(2)}) collective-permute-start(bf16[128,512]{1,0:T(8,128)(2,1)S(1)} %get-tuple-element.46), channel_id=1, source_target_pairs={{0,20},{4,16},{8,28},{12,24},{16,4},{20,0},{24,12},{28,8},{1,21},{... | collective-permute-start | bytes 393224 | tf_op jit(solution)/shard_map/ppermute | solution.py:434
  9.1 5.0 %collective-permute-start = (bf16[128,512]{1,0:T(8,128)(2,1)S(1)}, bf16[128,512]{1,0:T(8,128)(2,1)S(1)}, u32[]{:S(2)}, u32[]{:S(2)}) collective-permute-start(bf16[128,512]{1,0:T(8,128)(2,1)S(1)} %get-tuple-element.42), channel_id=1, source_target_pairs={{0,4},{4,0},{8,12},{12,8},{16,20},{20,16},{24,28},{28,24},{1,5},{5... | collective-permute-start | bytes 393224 | tf_op jit(solution)/shard_map/ppermute | solution.py:434
  9.6 8.3 %collective-permute-start.1 = (bf16[128,512]{1,0:T(8,128)(2,1)S(1)}, bf16[128,512]{1,0:T(8,128)(2,1)S(1)}, u32[]{:S(2)}, u32[]{:S(2)}) collective-permute-start(bf16[128,512]{1,0:T(8,128)(2,1)S(1)} %get-tuple-element.43), channel_id=1, source_target_pairs={{0,8},{4,12},{8,0},{12,4},{16,24},{20,28},{24,16},{28,20},{1,9},{5... | collective-permute-start | bytes 393224 | tf_op jit(solution)/shard_map/ppermute | solution.py:434
  14.0 10.9 %collective-permute-start.2 = (bf16[128,512]{1,0:T(8,128)(2,1)S(1)}, bf16[128,512]{1,0:T(8,128)(2,1)S(1)}, u32[]{:S(2)}, u32[]{:S(2)}) collective-permute-start(bf16[128,512]{1,0:T(8,128)(2,1)S(1)} %get-tuple-element.44), channel_id=1, source_target_pairs={{0,12},{4,8},{8,4},{12,0},{16,28},{20,24},{24,20},{28,16},{1,13},{... | collective-permute-start | bytes 393224 | tf_op jit(solution)/shard_map/ppermute | solution.py:434
  17.9 15.8 %collective-permute-start.5 = (bf16[128,512]{1,0:T(8,128)(2,1)S(1)}, bf16[128,512]{1,0:T(8,128)(2,1)S(1)}, u32[]{:S(2)}, u32[]{:S(2)}) collective-permute-start(bf16[128,512]{1,0:T(8,128)(2,1)S(1)} %get-tuple-element.47), channel_id=1, source_target_pairs={{0,24},{4,28},{8,16},{12,20},{16,8},{20,12},{24,0},{28,4},{1,25},{... | collective-permute-start | bytes 393224 | tf_op jit(solution)/shard_map/ppermute | solution.py:434
  24.9 8.8 %collective-permute-start.6 = (bf16[128,512]{1,0:T(8,128)(2,1)S(1)}, bf16[128,512]{1,0:T(8,128)(2,1)S(1)}, u32[]{:S(2)}, u32[]{:S(2)}) collective-permute-start(bf16[128,512]{1,0:T(8,128)(2,1)S(1)} %get-tuple-element.48), channel_id=1, source_target_pairs={{0,28},{4,24},{8,20},{12,16},{16,12},{20,8},{24,4},{28,0},{1,29},{... | collective-permute-start | bytes 393224 | tf_op jit(solution)/shard_map/ppermute | solution.py:434
  28.4 13.5 %collective-permute-start.9 = (bf16[512,512]{1,0:T(8,128)(2,1)S(1)}, bf16[512,512]{1,0:T(8,128)(2,1)S(1)}, u32[]{:S(2)}, u32[]{:S(2)}) collective-permute-start(bf16[512,512]{1,0:T(8,128)(2,1)S(1)} %constant_dynamic-update-slice_fusion.refs_1_.refs_0_), channel_id=1, source_target_pairs={{0,2},{1,3},{2,0},{3,1},{4,6},{5,7},{6,4},{7,5},{8,10},{9,11},{10,... | collective-permute-start | bytes 1572872 | tf_op jit(solution)/shard_map/ppermute | solution.py:427
  33.6 25.7 %collective-permute-start.17 = (bf16[512,2048]{1,0:T(8,128)(2,1)S(1)}, bf16[512,2048]{1,0:T(8,128)(2,1)S(1)}, u32[]{:S(2)}, u32[]{:S(2)}) collective-permute-start(bf16[512,2048]{1,0:T(8,128)(2,1)S(1)} %get-tuple-element.58.refs_3_), channel_id=1, source_target_pairs={{0,1},{1,0},{2,3},{3,2},{4,5},{5,4},{6,7},{7,6},{8,9},{9,8},{10,11... | collective-permute-start | bytes 6291464 | tf_op jit(solution)/shard_map/ppermute | solution.py:427
  33.7 8.8 %collective-permute-start.7 = (bf16[1024,512]{1,0:T(8,128)(2,1)S(1)}, bf16[1024,512]{1,0:T(8,128)(2,1)S(1)}, u32[]{:S(2)}, u32[]{:S(2)}) collective-permute-start(bf16[1024,512]{1,0:T(8,128)(2,1)S(1)} %fence.3), channel_id=1, source_target_pairs={{0,1},{1,0},{2,3},{3,2},{4,5},{5,4},{6,7},{7,6},{8,9},{9,8},{10,11... | collective-permute-start | bytes 3145736 | tf_op jit(solution)/shard_map/ppermute | solution.py:427
  42.5 9.2 %collective-permute-start.13 = (bf16[512,512]{1,0:T(8,128)(2,1)S(1)}, bf16[512,512]{1,0:T(8,128)(2,1)S(1)}, u32[]{:S(2)}, u32[]{:S(2)}) collective-permute-start(bf16[512,512]{1,0:T(8,128)(2,1)S(1)} %collective-permute-done.9.refs_1_.refs_2_), channel_id=1, source_target_pairs={{0,1},{1,0},{2,3},{3,2},{4,5},{5,4},{6,7},{7,6},{8,9},{9,8},{10,11... | collective-permute-start | bytes 1572872 | tf_op jit(solution)/shard_map/ppermute | solution.py:427
  42.6 14.3 %collective-permute-start.11 = (bf16[512,512]{1,0:T(8,128)(2,1)S(1)}, bf16[512,512]{1,0:T(8,128)(2,1)S(1)}, u32[]{:S(2)}, u32[]{:S(2)}) collective-permute-start(bf16[512,512]{1,0:T(8,128)(2,1)S(1)} %constant_dynamic-update-slice_fusion.4.refs_2_.refs_5_.refs_0_), channel_id=1, source_target_pairs={{0,2},{1,3},{2,0},{3,1},{4,6},{5,7},{6,4},{7,5},{8,10},{9,11},{10,... | collective-permute-start | bytes 1572872 | tf_op jit(solution)/shard_map/ppermute | solution.py:427
  44.7 12.8 %collective-permute-start.16 = (bf16[512,512]{1,0:T(8,128)(2,1)S(1)}, bf16[512,512]{1,0:T(8,128)(2,1)S(1)}, u32[]{:S(2)}, u32[]{:S(2)}) collective-permute-start(bf16[512,512]{1,0:T(8,128)(2,1)S(1)} %constant_dynamic-update-slice_fusion.4.refs_2_.refs_5_.refs_0_), channel_id=1, source_target_pairs={{0,1},{1,0},{2,3},{3,2},{4,5},{5,4},{6,7},{7,6},{8,9},{9,8},{10,11... | collective-permute-start | bytes 1572872 | tf_op jit(solution)/shard_map/ppermute | solution.py:427
  46.1 22.2 %collective-permute-start.18 = (bf16[512,512]{1,0:T(8,128)(2,1)S(1)}, bf16[512,512]{1,0:T(8,128)(2,1)S(1)}, u32[]{:S(2)}, u32[]{:S(2)}) collective-permute-start(bf16[512,512]{1,0:T(8,128)(2,1)S(1)} %project_halo.1.refs_6_), channel_id=1, source_target_pairs={{0,4},{4,8},{8,12},{12,16},{16,20},{20,24},{24,28},{1,5},{5,9},{9,... | collective-permute-start | bytes 1572872 | tf_op jit(solution)/shard_map/ppermute | solution.py:462
  63.8 13.7 %collective-permute-start.21 = (bf16[528,128]{1,0:T(8,128)(2,1)S(1)}, bf16[528,128]{1,0:T(8,128)(2,1)S(1)}, u32[]{:S(2)}, u32[]{:S(2)}) collective-permute-start(bf16[528,128]{1,0:T(8,128)(2,1)S(1)} %get-tuple-element.66), channel_id=1, source_target_pairs={{0,4},{4,0},{8,12},{12,8},{16,20},{20,16},{24,28},{28,24},{1,5},{5... | collective-permute-start | bytes 405512 | tf_op jit(solution)/shard_map/ppermute | solution.py:434
  65.0 12.5 %collective-permute-start.22 = (bf16[528,128]{1,0:T(8,128)(2,1)S(1)}, bf16[528,128]{1,0:T(8,128)(2,1)S(1)}, u32[]{:S(2)}, u32[]{:S(2)}) collective-permute-start(bf16[528,128]{1,0:T(8,128)(2,1)S(1)} %get-tuple-element.67), channel_id=1, source_target_pairs={{0,16},{4,20},{8,24},{12,28},{16,0},{20,4},{24,8},{28,12},{1,17},{... | collective-permute-start | bytes 405512 | tf_op jit(solution)/shard_map/ppermute | solution.py:434
  65.0 13.1 %collective-permute-start.23 = (bf16[528,128]{1,0:T(8,128)(2,1)S(1)}, bf16[528,128]{1,0:T(8,128)(2,1)S(1)}, u32[]{:S(2)}, u32[]{:S(2)}) collective-permute-start(bf16[528,128]{1,0:T(8,128)(2,1)S(1)} %get-tuple-element.68), channel_id=1, source_target_pairs={{0,20},{4,16},{8,28},{12,24},{16,4},{20,0},{24,12},{28,8},{1,21},{... | collective-permute-start | bytes 405512 | tf_op jit(solution)/shard_map/ppermute | solution.py:434
  68.2 12.5 %collective-permute-start.24 = (bf16[528,128]{1,0:T(8,128)(2,1)S(1)}, bf16[528,128]{1,0:T(8,128)(2,1)S(1)}, u32[]{:S(2)}, u32[]{:S(2)}) collective-permute-start(bf16[528,128]{1,0:T(8,128)(2,1)S(1)} %get-tuple-element.69), channel_id=1, source_target_pairs={{0,12},{4,8},{8,4},{12,0},{16,28},{20,24},{24,20},{28,16},{1,13},{... | collective-permute-start | bytes 405512 | tf_op jit(solution)/shard_map/ppermute | solution.py:434
  68.2 13.9 %collective-permute-start.25 = (bf16[528,128]{1,0:T(8,128)(2,1)S(1)}, bf16[528,128]{1,0:T(8,128)(2,1)S(1)}, u32[]{:S(2)}, u32[]{:S(2)}) collective-permute-start(bf16[528,128]{1,0:T(8,128)(2,1)S(1)} %get-tuple-element.70), channel_id=1, source_target_pairs={{0,8},{4,12},{8,0},{12,4},{16,24},{20,28},{24,16},{28,20},{1,9},{5... | collective-permute-start | bytes 405512 | tf_op jit(solution)/shard_map/ppermute | solution.py:434
  84.1 8.3 %collective-permute-start.19 = (bf16[528,128]{1,0:T(8,128)(2,1)S(1)}, bf16[528,128]{1,0:T(8,128)(2,1)S(1)}, u32[]{:S(2)}, u32[]{:S(2)}) collective-permute-start(bf16[528,128]{1,0:T(8,128)(2,1)S(1)} %get-tuple-element.64), channel_id=1, source_target_pairs={{0,24},{4,28},{8,16},{12,20},{16,8},{20,12},{24,0},{28,4},{1,25},{... | collective-permute-start | bytes 405512 | tf_op jit(solution)/shard_map/ppermute | solution.py:434
  84.1 11.0 %collective-permute-start.20 = (bf16[528,128]{1,0:T(8,128)(2,1)S(1)}, bf16[528,128]{1,0:T(8,128)(2,1)S(1)}, u32[]{:S(2)}, u32[]{:S(2)}) collective-permute-start(bf16[528,128]{1,0:T(8,128)(2,1)S(1)} %get-tuple-element.65), channel_id=1, source_target_pairs={{0,28},{4,24},{8,20},{12,16},{16,12},{20,8},{24,4},{28,0},{1,29},{... | collective-permute-start | bytes 405512 | tf_op jit(solution)/shard_map/ppermute | solution.py:434
  89.8 20.5 %collective-permute-start.29 = (bf16[192,2048]{1,0:T(8,128)(2,1)S(1)}, bf16[192,2048]{1,0:T(8,128)(2,1)S(1)}, u32[]{:S(2)}, u32[]{:S(2)}) collective-permute-start(bf16[192,2048]{1,0:T(8,128)(2,1)S(1)} %out_project.4.refs_5_), channel_id=1, source_target_pairs={{0,2},{1,3},{2,0},{3,1},{4,6},{5,7},{6,4},{7,5},{8,10},{9,11},{10,... | collective-permute-start | bytes 2359304 | tf_op jit(solution)/shard_map/ppermute | solution.py:427
  99.3 15.6 %collective-permute-start.28 = (bf16[64,2048]{1,0:T(8,128)(2,1)S(1)}, bf16[64,2048]{1,0:T(8,128)(2,1)S(1)}, u32[]{:S(2)}, u32[]{:S(2)}) collective-permute-start(bf16[64,2048]{1,0:T(8,128)(2,1)S(1)} %out_project.6), channel_id=1, source_target_pairs={{0,2},{1,3},{2,0},{3,1},{4,6},{5,7},{6,4},{7,5},{8,10},{9,11},{10,... | collective-permute-start | bytes 786440 | tf_op jit(solution)/shard_map/ppermute | solution.py:427
  (10 other events, 72.6 us)

commit v21 on v19

--- a/solution.py
+++ b/solution.py
@@ -185,16 +185,13 @@
     out_ref[STRIDE:, :] = gathered((x0, x1, x2, x3), at, wv)
 
 
-def query_kernel(x0, x1, x2, x3, wq, q_ref):
-    q_ref[...] = gathered((x0, x1, x2, x3), slice(0, x0.shape[0]), wq)
-
-
-def key_kernel(x0, x1, x2, x3, wk, wv, halo, k_ref, v_ref):
-    upto = x0.shape[0] - STRIDE
+def project_kernel(x0, x1, x2, x3, wq, wk, wv, halo, q_ref, k_ref, v_ref):
+    rows = x0.shape[0]
+    upto = rows - STRIDE
     k_ref[upto:, :] = halo[:STRIDE, :]
     v_ref[upto:, :] = halo[STRIDE:, :]
-    for w, out in ((wk, k_ref), (wv, v_ref)):
-        out[:upto, :] = gathered((x0, x1, x2, x3), slice(0, upto), w)
+    for w, out, at in ((wq, q_ref, rows), (wk, k_ref, upto), (wv, v_ref, upto)):
+        out[:at, :] = gathered((x0, x1, x2, x3), slice(0, at), w)
 
 
 def softmax_columns(s):
@@ -460,31 +457,23 @@
         halo_kernel, "project_halo", 1.5, shape((2 * STRIDE, width)), (*pieces, *weights[1:])
     )
     halo = lax.ppermute(own_halo, "seq", [(i, i + 1) for i in range(owners - 1)])
-    q = call(
-        query_kernel,
-        "project_query",
-        0,
-        shape((rows, width)),
-        (*pieces, weights[0]),
-        (far_own,),
-    )
     near = call(
         near_kernel,
         "project_near",
         0,
         [shape(near_own.shape)] * 3,
         (near_own, near_core, near_across, swap(near_across, 1), *weights),
-        (q,),
+        (own_halo,),
     )
     far_half = half_sums(far_own, far_core, weights, (near[0],))
     far_across = fence(far_across, near[0])
     columns = column_part(pos, far_across, far_half, weights, near, owners, (w_other,))
-    k, v = call(
-        key_kernel,
-        "project_key",
+    q, k, v = call(
+        project_kernel,
+        "project_block",
         0,
-        [shape((rows, width))] * 2,
-        (*pieces, *weights[1:], own_halo),
+        [shape((rows, width))] * 3,
+        (*pieces, *weights, own_halo),
         (columns[0], halo),
     )
     locals_ = local_part(pos, q, k, v, halo, owners, (columns[0],))

time: 116 us -> 116 us (level)
    ppermute x15, waiting for transfers between devices: 22.9 us -> 25.4 us  [swap(): return lax.ppermute(value, 'head', [(i, i ^ distance) for i in range(4)])]
    ppermute x14, waiting for transfers between devices: 11.4 us -> 9.32 us  [move(): lax.ppermute(value, 'seq', [(i, i ^ k) for i in range(peers)])]
    pallas_call x13 -> x12, Pallas kernels: 28.7 us -> 28.4 us  [call(): pl.pallas_call(run, in_specs=specs + [ANYWHERE] * extra, out_specs=jax.tr...]
  transfers between devices with their start and end apart: 30 -> 30, of which waited for: 10 -> 10; matrix products, arithmetic and copies ran while one was open for 0% -> 0% of each run, Pallas kernels for 28% -> 27%
where the time goes in v21:
time: 116 us
  starting transfers between devices  42.4 us (37%)
  Pallas kernels  34.7 us (30%)
  waiting for transfers between devices  34.7 us (30%)
  local copies, waits for them, and re-layouts  3.37 us (3%)
    ppermute x14, starting transfers between devices, move(): lax.ppermute(value, 'seq', [(i, i ^ k) for i in range(peers)])  31.9 us
    pallas_call x12, Pallas kernels, call(): pl.pallas_call(run, in_specs=specs + [ANYWHERE] * extra, out_specs=jax.tr...  28.4 us
    ppermute x15, waiting for transfers between devices, swap(): return lax.ppermute(value, 'head', [(i, i ^ distance) for i in range(4)])  25.4 us
    ppermute x14, waiting for transfers between devices, move(): lax.ppermute(value, 'seq', [(i, i ^ k) for i in range(peers)])  9.32 us
    ppermute x15, starting transfers between devices, swap(): return lax.ppermute(value, 'head', [(i, i ^ distance) for i in range(4)])  7.23 us
    unnamed x15, local copies, waits for them, and re-layouts  3.31 us
    ppermute x1, starting transfers between devices, chunked(): lax.ppermute(own_halo, 'seq', [(i, i + 1) for i in range(owners - 1)])  3.28 us
    pallas_call x2, Pallas kernels, join(): pl.pallas_call(functools.partial(join_kernel, share), in_specs=[IN_SMEM,...  2.89 us
  transfers between devices with their start and end apart: 30, of which 10 were waited for; matrix products, arithmetic and copies ran while one was open for 0% of the time, Pallas kernels for 27%

profile of v21, /device:TPU:0, one launch (start us, length us, event | category | flops | bytes accessed | tf_op | source)
XLA Modules:
  0.0 115.8 jit_solution(16669799282989565471)
XLA Ops:
  0.0 2.9 %collective-permute-start.8 = (bf16[1024,512]{1,0:T(8,128)(2,1)}, bf16[1024,512]{1,0:T(8,128)(2,1)S(1)}, u32[]{:S(2)}, u32[]{:S(2)}) collective-permute-start(bf16[1024,512]{1,0:T(8,128)(2,1)} %tok_hbm.1), channel_id=1, source_target_pairs={{0,2},{1,3},{2,0},{3,1},{4,6},{5,7},{6,4},{7,5},{8,10},{9,11},{10,... | collective-permute-start | bytes 3145736 | tf_op jit(solution)/shard_map/ppermute | solution.py:424
  3.0 2.1 %pack_tokens.1 = (bf16[1024,512]{1,0:T(8,128)(2,1)S(1)}, bf16[128,512]{1,0:T(8,128)(2,1)S(1)}, bf16[128,512]{1,0:T(8,128)(2,1)S(1)}, bf16[128,512]{1,0:T(8,128)(...) custom-call(s32[3]{0:T(128)S(1)} %pad_add_fusion.pos_ref.refs_0_, ...), custom_call_target="tpu_custom_call" | custom-call | bytes 2097152 | tf_op jit(solution)/shard_map/pack_tokens/pallas_call | solution.py:113
  5.1 2.7 %collective-permute-start.3 = (bf16[128,512]{1,0:T(8,128)(2,1)S(1)}, bf16[128,512]{1,0:T(8,128)(2,1)S(1)}, u32[]{:S(2)}, u32[]{:S(2)}) collective-permute-start(bf16[128,512]{1,0:T(8,128)(2,1)S(1)} %get-tuple-element.46), channel_id=1, source_target_pairs={{0,16},{4,20},{8,24},{12,28},{16,0},{20,4},{24,8},{28,12},{1,17},{... | collective-permute-start | bytes 393224 | tf_op jit(solution)/shard_map/ppermute | solution.py:431
  11.3 2.8 %collective-permute-done.after = bf16[128,512]{1,0:T(8,128)(2,1)S(1)} collective-permute-done((bf16[128,512]{1,0:T(8,128)(2,1)S(1)}, bf16[128,512]{1,0:T(8,128)(2,1)S(1)}, u32[]{:S(2)}, u32[]{:S(2)}) %collective-permute-start) | collective-permute-done | bytes 131104 | tf_op jit(solution)/shard_map/ppermute | solution.py:431
  14.0 3.8 %collective-permute-start.2 = (bf16[128,512]{1,0:T(8,128)(2,1)S(1)}, bf16[128,512]{1,0:T(8,128)(2,1)S(1)}, u32[]{:S(2)}, u32[]{:S(2)}) collective-permute-start(bf16[128,512]{1,0:T(8,128)(2,1)S(1)} %get-tuple-element.45), channel_id=1, source_target_pairs={{0,12},{4,8},{8,4},{12,0},{16,28},{20,24},{24,20},{28,16},{1,13},{... | collective-permute-start | bytes 393224 | tf_op jit(solution)/shard_map/ppermute | solution.py:431
  17.9 7.0 %collective-permute-start.5 = (bf16[128,512]{1,0:T(8,128)(2,1)S(1)}, bf16[128,512]{1,0:T(8,128)(2,1)S(1)}, u32[]{:S(2)}, u32[]{:S(2)}) collective-permute-start(bf16[128,512]{1,0:T(8,128)(2,1)S(1)} %get-tuple-element.48), channel_id=1, source_target_pairs={{0,24},{4,28},{8,16},{12,20},{16,8},{20,12},{24,0},{28,4},{1,25},{... | collective-permute-start | bytes 393224 | tf_op jit(solution)/shard_map/ppermute | solution.py:431
  24.9 3.5 %collective-permute-start.6 = (bf16[128,512]{1,0:T(8,128)(2,1)S(1)}, bf16[128,512]{1,0:T(8,128)(2,1)S(1)}, u32[]{:S(2)}, u32[]{:S(2)}) collective-permute-start(bf16[128,512]{1,0:T(8,128)(2,1)S(1)} %get-tuple-element.49), channel_id=1, source_target_pairs={{0,28},{4,24},{8,20},{12,16},{16,12},{20,8},{24,4},{28,0},{1,29},{... | collective-permute-start | bytes 393224 | tf_op jit(solution)/shard_map/ppermute | solution.py:431
  34.3 7.7 %collective-permute-done.9.refs_1_.refs_2_ = bf16[512,512]{1,0:T(8,128)(2,1)S(1)} collective-permute-done((bf16[512,512]{1,0:T(8,128)(2,1)S(1)}, bf16[512,512]{1,0:T(8,128)(2,1)S(1)}, u32[]{:S(2)}, u32[]{:S(2)}) %collective-permute-start.9) | collective-permute-done | bytes 524320 | tf_op jit(solution)/shard_map/ppermute | solution.py:424
  46.1 3.3 %collective-permute-start.18 = (bf16[512,512]{1,0:T(8,128)(2,1)S(1)}, bf16[512,512]{1,0:T(8,128)(2,1)S(1)}, u32[]{:S(2)}, u32[]{:S(2)}) collective-permute-start(bf16[512,512]{1,0:T(8,128)(2,1)S(1)} %project_halo.1.refs_7_), channel_id=1, source_target_pairs={{0,4},{4,8},{8,12},{12,16},{16,20},{20,24},{24,28},{1,5},{5,9},{9,... | collective-permute-start | bytes 1572872 | tf_op jit(solution)/shard_map/ppermute | solution.py:459
  49.4 3.4 %project_near.1 = (bf16[512,512]{1,0:T(8,128)(2,1)S(1)}, bf16[512,512]{1,0:T(8,128)(2,1)S(1)}, bf16[512,512]{1,0:T(8,128)(2,1)S(1)}) custom-call(bf16[512,512]{1,0:T(8,128)(2,1)S(1)} %constant_dynamic-update-slice_fusion.refs_1_.refs_0_, bf16[512,512]{1,0:T(8,128)(2,1)S(1)} %collective-permute-done.12.refs_1_, ...), custom_call_target="tpu_custom_call" | custom-call | tf_op jit(solution)/shard_map/project_near/pallas_call | solution.py:39
  52.8 4.1 %collective-permute-done.11.refs_0_ = bf16[512,512]{1,0:T(8,128)(2,1)S(1)} collective-permute-done((bf16[512,512]{1,0:T(8,128)(2,1)S(1)}, bf16[512,512]{1,0:T(8,128)(2,1)S(1)}, u32[]{:S(2)}, u32[]{:S(2)}) %collective-permute-start.11) | collective-permute-done | bytes 524320 | tf_op jit(solution)/shard_map/ppermute | solution.py:424
  57.5 1.8 %half_sums.1 = (f32[512,512]{1,0:T(8,128)S(1)}, f32[512,512]{1,0:T(8,128)S(1)}, f32[512,512]{1,0:T(8,128)S(1)}) custom-call(bf16[512,512]{1,0:T(8,128)(2,1)S(1)} %constant_dynamic-update-slice_fusion.4.refs_2_.refs_0_, bf16[512,512]{1,0:T(8,128)(2,1)S(1)} %collective-permute-done.16.refs_1_, bf16[2048,512]{1,0:T(8,128)(2,1)S(1)} %get-tuple-element.50.refs_4_.refs_2_.refs_7_, ...), custom_call_target="tpu_custom_call" | custom-call | tf_op jit(solution)/shard_map/half_sums/pallas_call | solution.py:39
  59.3 4.4 %column_part.1 = (bf16[528,128]{1,0:T(8,128)(2,1)S(1)}, bf16[528,128]{1,0:T(8,128)(2,1)S(1)}, bf16[528,128]{1,0:T(8,128)(2,1)S(1)}, bf16[528,128]{1,0:T(8,128)(2...) custom-call(s32[3]{0:T(128)S(1)} %pad_add_fusion.pos_ref.refs_0_, ...), custom_call_target="tpu_custom_call" | custom-call | tf_op jit(solution)/shard_map/column_part/pallas_call | solution.py:39
  63.8 3.5 %collective-permute-start.22 = (bf16[528,128]{1,0:T(8,128)(2,1)S(1)}, bf16[528,128]{1,0:T(8,128)(2,1)S(1)}, u32[]{:S(2)}, u32[]{:S(2)}) collective-permute-start(bf16[528,128]{1,0:T(8,128)(2,1)S(1)} %get-tuple-element.69), channel_id=1, source_target_pairs={{0,20},{4,16},{8,28},{12,24},{16,4},{20,0},{24,12},{28,8},{1,21},{... | collective-permute-start | bytes 405512 | tf_op jit(solution)/shard_map/ppermute | solution.py:431
  67.3 2.3 %collective-permute-start.24 = (bf16[528,128]{1,0:T(8,128)(2,1)S(1)}, bf16[528,128]{1,0:T(8,128)(2,1)S(1)}, u32[]{:S(2)}, u32[]{:S(2)}) collective-permute-start(bf16[528,128]{1,0:T(8,128)(2,1)S(1)} %get-tuple-element.71), channel_id=1, source_target_pairs={{0,8},{4,12},{8,0},{12,4},{16,24},{20,28},{24,16},{28,20},{1,9},{5... | collective-permute-start | bytes 405512 | tf_op jit(solution)/shard_map/ppermute | solution.py:431
  70.8 5.6 %project_block.1 = (bf16[1024,512]{1,0:T(8,128)(2,1)S(1)}, bf16[1024,512]{1,0:T(8,128)(2,1)S(1)}, bf16[1024,512]{1,0:T(8,128)(2,1)S(1)}) custom-call(bf16[1024,512]{1,0:T(8,128)(2,1)S(1)} %get-tuple-element.41.refs_0_, bf16[1024,512]{1,0:T(8,128)(2,1)S(1)} %collective-permute-done.7.refs_1_, bf16[1024,512]{1,0:T(8,128)(2,1)S(1)} %fence.4.refs_2_, ...), custom_call_target="tpu_custom_call" | custom-call | tf_op jit(solution)/shard_map/project_block/pallas_call | solution.py:39
  76.4 3.1 %local_part.1 = (f32[8,128,512]{2,1,0:T(8,128)S(1)}, f32[128,128]{1,0:T(8,128)S(1)}) custom-call(s32[3]{0:T(128)S(1)} %pad_add_fusion.pos_ref.refs_0_, bf16[1024,512]{1,0:T(8,128)(2,1)S(1)} %get-tuple-element.61.refs_1_, bf16[1024,512]{1,0:T(8,128)(2,1)S(1)} %get-tuple-element.62.refs_2_, bf16[1024,512]{1,0:T(8,128)(2,1)S(1)} %get-tuple-element.63.refs_3_, ...), custom_call_target="tpu_custom_call" | custom-call | flops 5500000256 | tf_op jit(solution)/shard_map/local_part/pallas_call | solution.py:39
  81.3 1.9 %mix.2 = (bf16[2,192,512]{2,1,0:T(8,128)(2,1)S(1)}, bf16[2,192,512]{2,1,0:T(8,128)(2,1)S(1)}) custom-call(s32[3]{0:T(128)S(1)} %pad_add_fusion.pos_ref.refs_0_, f32[8,128,512]{2,1,0:T(8,128)S(1)} %get-tuple-element.64.refs_1_, f32[128,128]{1,0:T(8,128)S(1)} %get-tuple-element.65.refs_2_, bf16[528,128]{1,0:T(8,128)(2,1)S(1)} %collective-permute-done.21.refs_3_, ...), custom_call_target="tpu_custom_call" | custom-call | flops 2200000000 | tf_op jit(solution)/shard_map/mix/pallas_call | solution.py:39
  83.3 4.4 %collective-permute-start.20 = (bf16[528,128]{1,0:T(8,128)(2,1)S(1)}, bf16[528,128]{1,0:T(8,128)(2,1)S(1)}, u32[]{:S(2)}, u32[]{:S(2)}) collective-permute-start(bf16[528,128]{1,0:T(8,128)(2,1)S(1)} %get-tuple-element.67), channel_id=1, source_target_pairs={{0,28},{4,24},{8,20},{12,16},{16,12},{20,8},{24,4},{28,0},{1,29},{... | collective-permute-start | bytes 405512 | tf_op jit(solution)/shard_map/ppermute | solution.py:431
  89.8 1.8 %collective-permute-done.19.refs_3_ = bf16[528,128]{1,0:T(8,128)(2,1)S(1)} collective-permute-done((bf16[528,128]{1,0:T(8,128)(2,1)S(1)}, bf16[528,128]{1,0:T(8,128)(2,1)S(1)}, u32[]{:S(2)}, u32[]{:S(2)}) %collective-permute-start.19) | collective-permute-done | bytes 135200 | tf_op jit(solution)/shard_map/ppermute | solution.py:431
  91.6 3.0 %collective-permute-done.20.refs_4_ = bf16[528,128]{1,0:T(8,128)(2,1)S(1)} collective-permute-done((bf16[528,128]{1,0:T(8,128)(2,1)S(1)}, bf16[528,128]{1,0:T(8,128)(2,1)S(1)}, u32[]{:S(2)}, u32[]{:S(2)}) %collective-permute-start.20) | collective-permute-done | bytes 135200 | tf_op jit(solution)/shard_map/ppermute | solution.py:431
  100.7 9.1 %collective-permute-done.29.got = bf16[192,2048]{1,0:T(8,128)(2,1)S(1)} collective-permute-done((bf16[192,2048]{1,0:T(8,128)(2,1)S(1)}, bf16[192,2048]{1,0:T(8,128)(2,1)S(1)}, u32[]{:S(2)}, u32[]{:S(2)}) %collective-permute-start.29) | collective-permute-done | bytes 786464 | tf_op jit(solution)/shard_map/ppermute | solution.py:424
  109.8 1.6 %join.2.rest_0_ = bf16[256,2048]{1,0:T(8,128)(2,1)} custom-call(s32[3]{0:T(128)S(1)} %pad_add_fusion.pos_ref.refs_0_, f32[192,2048]{1,0:T(8,128)S(1)} %out_project.7.keep, bf16[192,2048]{1,0:T(8,128)(2,1)S(1)} %collective-permute-done.29.got), custom_call_target="tpu_custom_call" | custom-call | flops 1100000000 | tf_op jit(solution)/shard_map/join/pallas_call | solution.py:410
  111.4 2.9 %collective-permute-done.28.got = bf16[64,2048]{1,0:T(8,128)(2,1)S(1)} collective-permute-done((bf16[64,2048]{1,0:T(8,128)(2,1)S(1)}, bf16[64,2048]{1,0:T(8,128)(2,1)S(1)}, u32[]{:S(2)}, u32[]{:S(2)}) %collective-permute-start.28) | collective-permute-done | bytes 262176 | tf_op jit(solution)/shard_map/ppermute | solution.py:424
  (75 shorter events, 26.5 us)
Async XLA Ops:
  0.0 42.0 %collective-permute-start.8 = (bf16[1024,512]{1,0:T(8,128)(2,1)}, bf16[1024,512]{1,0:T(8,128)(2,1)S(1)}, u32[]{:S(2)}, u32[]{:S(2)}) collective-permute-start(bf16[1024,512]{1,0:T(8,128)(2,1)} %tok_hbm.1), channel_id=1, source_target_pairs={{0,2},{1,3},{2,0},{3,1},{4,6},{5,7},{6,4},{7,5},{8,10},{9,11},{10,... | collective-permute-start | bytes 3145736 | tf_op jit(solution)/shard_map/ppermute | solution.py:424
  5.1 23.3 %collective-permute-start.3 = (bf16[128,512]{1,0:T(8,128)(2,1)S(1)}, bf16[128,512]{1,0:T(8,128)(2,1)S(1)}, u32[]{:S(2)}, u32[]{:S(2)}) collective-permute-start(bf16[128,512]{1,0:T(8,128)(2,1)S(1)} %get-tuple-element.46), channel_id=1, source_target_pairs={{0,16},{4,20},{8,24},{12,28},{16,0},{20,4},{24,8},{28,12},{1,17},{... | collective-permute-start | bytes 393224 | tf_op jit(solution)/shard_map/ppermute | solution.py:431
  7.8 25.8 %collective-permute-start.4 = (bf16[128,512]{1,0:T(8,128)(2,1)S(1)}, bf16[128,512]{1,0:T(8,128)(2,1)S(1)}, u32[]{:S(2)}, u32[]{:S(2)}) collective-permute-start(bf16[128,512]{1,0:T(8,128)(2,1)S(1)} %get-tuple-element.47), channel_id=1, source_target_pairs={{0,20},{4,16},{8,28},{12,24},{16,4},{20,0},{24,12},{28,8},{1,21},{... | collective-permute-start | bytes 393224 | tf_op jit(solution)/shard_map/ppermute | solution.py:431
  9.1 5.0 %collective-permute-start = (bf16[128,512]{1,0:T(8,128)(2,1)S(1)}, bf16[128,512]{1,0:T(8,128)(2,1)S(1)}, u32[]{:S(2)}, u32[]{:S(2)}) collective-permute-start(bf16[128,512]{1,0:T(8,128)(2,1)S(1)} %get-tuple-element.43), channel_id=1, source_target_pairs={{0,4},{4,0},{8,12},{12,8},{16,20},{20,16},{24,28},{28,24},{1,5},{5... | collective-permute-start | bytes 393224 | tf_op jit(solution)/shard_map/ppermute | solution.py:431
  9.6 8.3 %collective-permute-start.1 = (bf16[128,512]{1,0:T(8,128)(2,1)S(1)}, bf16[128,512]{1,0:T(8,128)(2,1)S(1)}, u32[]{:S(2)}, u32[]{:S(2)}) collective-permute-start(bf16[128,512]{1,0:T(8,128)(2,1)S(1)} %get-tuple-element.44), channel_id=1, source_target_pairs={{0,8},{4,12},{8,0},{12,4},{16,24},{20,28},{24,16},{28,20},{1,9},{5... | collective-permute-start | bytes 393224 | tf_op jit(solution)/shard_map/ppermute | solution.py:431
  14.0 10.9 %collective-permute-start.2 = (bf16[128,512]{1,0:T(8,128)(2,1)S(1)}, bf16[128,512]{1,0:T(8,128)(2,1)S(1)}, u32[]{:S(2)}, u32[]{:S(2)}) collective-permute-start(bf16[128,512]{1,0:T(8,128)(2,1)S(1)} %get-tuple-element.45), channel_id=1, source_target_pairs={{0,12},{4,8},{8,4},{12,0},{16,28},{20,24},{24,20},{28,16},{1,13},{... | collective-permute-start | bytes 393224 | tf_op jit(solution)/shard_map/ppermute | solution.py:431
  17.9 15.8 %collective-permute-start.5 = (bf16[128,512]{1,0:T(8,128)(2,1)S(1)}, bf16[128,512]{1,0:T(8,128)(2,1)S(1)}, u32[]{:S(2)}, u32[]{:S(2)}) collective-permute-start(bf16[128,512]{1,0:T(8,128)(2,1)S(1)} %get-tuple-element.48), channel_id=1, source_target_pairs={{0,24},{4,28},{8,16},{12,20},{16,8},{20,12},{24,0},{28,4},{1,25},{... | collective-permute-start | bytes 393224 | tf_op jit(solution)/shard_map/ppermute | solution.py:431
  24.9 8.8 %collective-permute-start.6 = (bf16[128,512]{1,0:T(8,128)(2,1)S(1)}, bf16[128,512]{1,0:T(8,128)(2,1)S(1)}, u32[]{:S(2)}, u32[]{:S(2)}) collective-permute-start(bf16[128,512]{1,0:T(8,128)(2,1)S(1)} %get-tuple-element.49), channel_id=1, source_target_pairs={{0,28},{4,24},{8,20},{12,16},{16,12},{20,8},{24,4},{28,0},{1,29},{... | collective-permute-start | bytes 393224 | tf_op jit(solution)/shard_map/ppermute | solution.py:431
  28.4 13.5 %collective-permute-start.9 = (bf16[512,512]{1,0:T(8,128)(2,1)S(1)}, bf16[512,512]{1,0:T(8,128)(2,1)S(1)}, u32[]{:S(2)}, u32[]{:S(2)}) collective-permute-start(bf16[512,512]{1,0:T(8,128)(2,1)S(1)} %constant_dynamic-update-slice_fusion.refs_1_.refs_0_), channel_id=1, source_target_pairs={{0,2},{1,3},{2,0},{3,1},{4,6},{5,7},{6,4},{7,5},{8,10},{9,11},{10,... | collective-permute-start | bytes 1572872 | tf_op jit(solution)/shard_map/ppermute | solution.py:424
  33.6 25.7 %collective-permute-start.17 = (bf16[512,2048]{1,0:T(8,128)(2,1)S(1)}, bf16[512,2048]{1,0:T(8,128)(2,1)S(1)}, u32[]{:S(2)}, u32[]{:S(2)}) collective-permute-start(bf16[512,2048]{1,0:T(8,128)(2,1)S(1)} %get-tuple-element.59.refs_3_), channel_id=1, source_target_pairs={{0,1},{1,0},{2,3},{3,2},{4,5},{5,4},{6,7},{7,6},{8,9},{9,8},{10,11... | collective-permute-start | bytes 6291464 | tf_op jit(solution)/shard_map/ppermute | solution.py:424
  33.7 8.8 %collective-permute-start.7 = (bf16[1024,512]{1,0:T(8,128)(2,1)S(1)}, bf16[1024,512]{1,0:T(8,128)(2,1)S(1)}, u32[]{:S(2)}, u32[]{:S(2)}) collective-permute-start(bf16[1024,512]{1,0:T(8,128)(2,1)S(1)} %fence.3), channel_id=1, source_target_pairs={{0,1},{1,0},{2,3},{3,2},{4,5},{5,4},{6,7},{7,6},{8,9},{9,8},{10,11... | collective-permute-start | bytes 3145736 | tf_op jit(solution)/shard_map/ppermute | solution.py:424
  42.5 6.8 %collective-permute-start.13 = (bf16[512,512]{1,0:T(8,128)(2,1)S(1)}, bf16[512,512]{1,0:T(8,128)(2,1)S(1)}, u32[]{:S(2)}, u32[]{:S(2)}) collective-permute-start(bf16[512,512]{1,0:T(8,128)(2,1)S(1)} %collective-permute-done.9.refs_1_.refs_2_), channel_id=1, source_target_pairs={{0,1},{1,0},{2,3},{3,2},{4,5},{5,4},{6,7},{7,6},{8,9},{9,8},{10,11... | collective-permute-start | bytes 1572872 | tf_op jit(solution)/shard_map/ppermute | solution.py:424
  42.6 14.3 %collective-permute-start.11 = (bf16[512,512]{1,0:T(8,128)(2,1)S(1)}, bf16[512,512]{1,0:T(8,128)(2,1)S(1)}, u32[]{:S(2)}, u32[]{:S(2)}) collective-permute-start(bf16[512,512]{1,0:T(8,128)(2,1)S(1)} %constant_dynamic-update-slice_fusion.4.refs_2_.refs_0_), channel_id=1, source_target_pairs={{0,2},{1,3},{2,0},{3,1},{4,6},{5,7},{6,4},{7,5},{8,10},{9,11},{10,... | collective-permute-start | bytes 1572872 | tf_op jit(solution)/shard_map/ppermute | solution.py:424
  44.7 12.8 %collective-permute-start.16 = (bf16[512,512]{1,0:T(8,128)(2,1)S(1)}, bf16[512,512]{1,0:T(8,128)(2,1)S(1)}, u32[]{:S(2)}, u32[]{:S(2)}) collective-permute-start(bf16[512,512]{1,0:T(8,128)(2,1)S(1)} %constant_dynamic-update-slice_fusion.4.refs_2_.refs_0_), channel_id=1, source_target_pairs={{0,1},{1,0},{2,3},{3,2},{4,5},{5,4},{6,7},{7,6},{8,9},{9,8},{10,11... | collective-permute-start | bytes 1572872 | tf_op jit(solution)/shard_map/ppermute | solution.py:424
  46.1 23.6 %collective-permute-start.18 = (bf16[512,512]{1,0:T(8,128)(2,1)S(1)}, bf16[512,512]{1,0:T(8,128)(2,1)S(1)}, u32[]{:S(2)}, u32[]{:S(2)}) collective-permute-start(bf16[512,512]{1,0:T(8,128)(2,1)S(1)} %project_halo.1.refs_7_), channel_id=1, source_target_pairs={{0,4},{4,8},{8,12},{12,16},{16,20},{20,24},{24,28},{1,5},{5,9},{9,... | collective-permute-start | bytes 1572872 | tf_op jit(solution)/shard_map/ppermute | solution.py:459
  63.7 15.8 %collective-permute-start.21 = (bf16[528,128]{1,0:T(8,128)(2,1)S(1)}, bf16[528,128]{1,0:T(8,128)(2,1)S(1)}, u32[]{:S(2)}, u32[]{:S(2)}) collective-permute-start(bf16[528,128]{1,0:T(8,128)(2,1)S(1)} %get-tuple-element.68), channel_id=1, source_target_pairs={{0,16},{4,20},{8,24},{12,28},{16,0},{20,4},{24,8},{28,12},{1,17},{... | collective-permute-start | bytes 405512 | tf_op jit(solution)/shard_map/ppermute | solution.py:431
  63.8 15.7 %collective-permute-start.22 = (bf16[528,128]{1,0:T(8,128)(2,1)S(1)}, bf16[528,128]{1,0:T(8,128)(2,1)S(1)}, u32[]{:S(2)}, u32[]{:S(2)}) collective-permute-start(bf16[528,128]{1,0:T(8,128)(2,1)S(1)} %get-tuple-element.69), channel_id=1, source_target_pairs={{0,20},{4,16},{8,28},{12,24},{16,4},{20,0},{24,12},{28,8},{1,21},{... | collective-permute-start | bytes 405512 | tf_op jit(solution)/shard_map/ppermute | solution.py:431
  67.3 12.6 %collective-permute-start.23 = (bf16[528,128]{1,0:T(8,128)(2,1)S(1)}, bf16[528,128]{1,0:T(8,128)(2,1)S(1)}, u32[]{:S(2)}, u32[]{:S(2)}) collective-permute-start(bf16[528,128]{1,0:T(8,128)(2,1)S(1)} %get-tuple-element.70), channel_id=1, source_target_pairs={{0,12},{4,8},{8,4},{12,0},{16,28},{20,24},{24,20},{28,16},{1,13},{... | collective-permute-start | bytes 405512 | tf_op jit(solution)/shard_map/ppermute | solution.py:431
  67.3 14.0 %collective-permute-start.24 = (bf16[528,128]{1,0:T(8,128)(2,1)S(1)}, bf16[528,128]{1,0:T(8,128)(2,1)S(1)}, u32[]{:S(2)}, u32[]{:S(2)}) collective-permute-start(bf16[528,128]{1,0:T(8,128)(2,1)S(1)} %get-tuple-element.71), channel_id=1, source_target_pairs={{0,8},{4,12},{8,0},{12,4},{16,24},{20,28},{24,16},{28,20},{1,9},{5... | collective-permute-start | bytes 405512 | tf_op jit(solution)/shard_map/ppermute | solution.py:431
  69.7 11.6 %collective-permute-start.25 = (bf16[528,128]{1,0:T(8,128)(2,1)S(1)}, bf16[528,128]{1,0:T(8,128)(2,1)S(1)}, u32[]{:S(2)}, u32[]{:S(2)}) collective-permute-start(bf16[528,128]{1,0:T(8,128)(2,1)S(1)} %get-tuple-element.72), channel_id=1, source_target_pairs={{0,4},{4,0},{8,12},{12,8},{16,20},{20,16},{24,28},{28,24},{1,5},{5... | collective-permute-start | bytes 405512 | tf_op jit(solution)/shard_map/ppermute | solution.py:431
  83.2 8.3 %collective-permute-start.19 = (bf16[528,128]{1,0:T(8,128)(2,1)S(1)}, bf16[528,128]{1,0:T(8,128)(2,1)S(1)}, u32[]{:S(2)}, u32[]{:S(2)}) collective-permute-start(bf16[528,128]{1,0:T(8,128)(2,1)S(1)} %get-tuple-element.66), channel_id=1, source_target_pairs={{0,24},{4,28},{8,16},{12,20},{16,8},{20,12},{24,0},{28,4},{1,25},{... | collective-permute-start | bytes 405512 | tf_op jit(solution)/shard_map/ppermute | solution.py:431
  83.3 11.3 %collective-permute-start.20 = (bf16[528,128]{1,0:T(8,128)(2,1)S(1)}, bf16[528,128]{1,0:T(8,128)(2,1)S(1)}, u32[]{:S(2)}, u32[]{:S(2)}) collective-permute-start(bf16[528,128]{1,0:T(8,128)(2,1)S(1)} %get-tuple-element.67), channel_id=1, source_target_pairs={{0,28},{4,24},{8,20},{12,16},{16,12},{20,8},{24,4},{28,0},{1,29},{... | collective-permute-start | bytes 405512 | tf_op jit(solution)/shard_map/ppermute | solution.py:431
  89.3 20.5 %collective-permute-start.29 = (bf16[192,2048]{1,0:T(8,128)(2,1)S(1)}, bf16[192,2048]{1,0:T(8,128)(2,1)S(1)}, u32[]{:S(2)}, u32[]{:S(2)}) collective-permute-start(bf16[192,2048]{1,0:T(8,128)(2,1)S(1)} %out_project.4.refs_5_), channel_id=1, source_target_pairs={{0,2},{1,3},{2,0},{3,1},{4,6},{5,7},{6,4},{7,5},{8,10},{9,11},{10,... | collective-permute-start | bytes 2359304 | tf_op jit(solution)/shard_map/ppermute | solution.py:424
  98.7 15.6 %collective-permute-start.28 = (bf16[64,2048]{1,0:T(8,128)(2,1)S(1)}, bf16[64,2048]{1,0:T(8,128)(2,1)S(1)}, u32[]{:S(2)}, u32[]{:S(2)}) collective-permute-start(bf16[64,2048]{1,0:T(8,128)(2,1)S(1)} %out_project.6), channel_id=1, source_target_pairs={{0,2},{1,3},{2,0},{3,1},{4,6},{5,7},{6,4},{7,5},{8,10},{9,11},{10,... | collective-permute-start | bytes 786440 | tf_op jit(solution)/shard_map/ppermute | solution.py:424
  (10 other events, 72.9 us)
